TPU v7x, 32 devices: a whole 2x2x4 slice. The times are simulated.
32 devices in a mesh: space: 4 (over y, x), mode: 8 (over z, core).
Axes of the slice: x: 2, y: 2, z: 4, core: 2. Of those that a mesh axis runs over, the one named last changes fastest.
Arguments:
- distribution: float32 [8192, 1024], P('mode', 'space'), may hold values from -6 to 6
- scatter_matrix: bfloat16 [8192, 8192], P(None, 'mode'), as said below
- velocity: float32 [2, 8192], P(None, 'mode'), may hold values from -0.4 to 0.4
- capacity: float32 [8192], P('mode'), may hold values from 0.3 to 3
- cell_type: int32 [1024], P('space'), may hold values from 0 to 2
Outputs:
- updated: float32 [8192, 1024], P('mode', 'space')
- heat_flux: float32 [2, 1024], P(None, 'space')
Inputs may be any that keep to these rules, and one draw needn't show every extreme that they name: scatter_matrix is symmetric.
All inputs are finite; a program needn't handle non-finite values.
Results may differ from a plain program's by a relative error of at most 0.0003.
Values sent between devices are 32-bit elements; how exact they have to be, the bound alone decides.
No kernel may reach another device: no remote copies, remote signals or barrier semaphores. Data moves between devices by JAX's collectives and lax.ppermute only.
A program may use at most 64 MiB of HBM per device.

v0:
```python
import jax
import jax.numpy as jnp
from jax import lax
from jax.sharding import PartitionSpec as P

NY = 16


relax_rate = 0.5
time_step = 0.5


def padded_2(value, sides, width):
    for axis, dim in sides:
        count, length = (lax.axis_size(axis), value.shape[dim])
        up = [(i, (i + 1) % count) for i in range(count - 1)]
        down = [(j, i) for i, j in up]
        last = lax.slice_in_dim(value, length - width, length, axis=dim)
        leading = lax.slice_in_dim(value, 0, width, axis=dim)
        before = lax.ppermute(last, axis, up)
        after = lax.ppermute(leading, axis, down)
        value = jnp.concatenate([before, value, after], axis=dim)
    return value


def tendency(padded, collision, cell_kinds, velocity, capacity):
    padded_y = jnp.pad(padded, ((0, 0), (0, 0), (2, 2)))
    width = padded.shape[1] - 4
    centre = padded_y[:, 2 : width + 2, 2:-2]
    west_one = padded_y[:, 1 : width + 1, 2:-2]
    west_two = padded_y[:, 0:width, 2:-2]
    east_one = padded_y[:, 3 : width + 3, 2:-2]
    east_two = padded_y[:, 4 : width + 4, 2:-2]
    south_one = padded_y[:, 2 : width + 2, 1:-3]
    south_two = padded_y[:, 2 : width + 2, 0:-4]
    north_one = padded_y[:, 2 : width + 2, 3:-1]
    north_two = padded_y[:, 2 : width + 2, 4:]
    speed_x = velocity[0][:, None, None]
    speed_y = velocity[1][:, None, None]
    advection = jnp.maximum(speed_x, 0.0) * 0.5 * (3.0 * centre - 4.0 * west_one + west_two)
    advection = advection + jnp.minimum(speed_x, 0.0) * 0.5 * (
        -3.0 * centre + 4.0 * east_one - east_two
    )
    advection = advection + jnp.maximum(speed_y, 0.0) * 0.5 * (
        3.0 * centre - 4.0 * south_one + south_two
    )
    advection = advection + jnp.minimum(speed_y, 0.0) * 0.5 * (
        -3.0 * centre + 4.0 * north_one - north_two
    )
    contact = (cell_kinds > 0).astype(jnp.float32)
    reservoir = jnp.where(cell_kinds == 1, 1.0, -1.0).astype(jnp.float32)
    contact_term = relax_rate * contact[None] * (centre - reservoir[None] * capacity[:, None, None])
    return -advection - collision - contact_term


def on_device(distribution, scatter_matrix, velocity, capacity, cell_type):
    local_modes, local_cells = distribution.shape
    local_columns = local_cells // NY
    total_modes = scatter_matrix.shape[0]
    field_now = distribution.reshape(local_modes, local_columns, NY)
    cell_kinds = cell_type.reshape(local_columns, NY)

    def fold_term(block_piece):
        matrix_rows = scatter_matrix.astype(jnp.float32)
        return lax.dot_general(
            matrix_rows,
            block_piece,
            (((0,), (0,)), ((), ())),
            precision=lax.Precision.HIGHEST,
            preferred_element_type=jnp.float32,
        )

    def collide(values_in):
        flat_field = values_in.reshape(local_modes, -1)
        summed = fold_term(lax.all_gather(flat_field, "mode", axis=0, tiled=True))
        return summed.reshape(values_in.shape)

    def extend(values_in):
        return padded_2(values_in, (("space", 1),), 2)

    first_rate = tendency(extend(field_now), collide(field_now), cell_kinds, velocity, capacity)
    midpoint = field_now + time_step * first_rate
    second_rate = tendency(extend(midpoint), collide(midpoint), cell_kinds, velocity, capacity)
    updated = field_now + 0.5 * time_step * (first_rate + second_rate)
    updated = updated.reshape(local_modes, -1)
    weights = capacity[None, :] * velocity
    flux_part = jnp.dot(weights, updated, precision=lax.Precision.HIGHEST) / jnp.sqrt(
        jnp.float32(total_modes)
    )
    heat_flux = lax.psum(flux_part, "mode")
    return (updated, heat_flux)


def solution(mesh):
    return jax.shard_map(
        on_device,
        mesh=mesh,
        in_specs=(P("mode", "space"), P(None, "mode"), P(None, "mode"), P("mode"), P("space")),
        out_specs=(P("mode", "space"), P(None, "space")),
        check_vma=False,
    )
```

profile of v0, /device:TPU:0, one launch (start us, length us, event | category | flops | bytes accessed | tf_op | source)
XLA Modules:
  0.0 241.2 jit_solution(9601717022533052188)
XLA Ops:
  7.2 0.0 copy-start.5
  7.2 0.0 copy-start.4
  7.2 0.0 all-gather.3.cloned.1.call-start
  7.2 0.7 all-gather.3.cloned.1.call-update
  7.9 0.0 all-gather.5.cloned.1.call-start
  8.0 1.6 copy.18
  9.6 4.8 %collective-permute-start = (f32[1024,2,16]{0,2,1:T(8,128)S(1)}, f32[1024,2,16]{0,2,1:T(8,128)S(1)}, u32[]{:S(2)}, u32[]{:S(2)}) collective-permute-start(f32[1024,2,16]{0,2,1:T(8,128)S(1)} %get-tuple-element.8), channel_id=1, source_target_pairs={{0,8},{8,16},{16,24},{1,9},{9,17},{17,25},{2,10},{10,18},{18,26},{... | collective-permute-start | bytes 393224 | tf_op jit(solution)/shard_map/ppermute | solution.py:20
  14.4 1.3 collective-permute-start.1
  15.7 0.0 copy-done.5
  15.7 0.1 mul.229
  15.8 0.1 select_n.13
  15.9 0.0 copy-done.4
  15.9 1.2 collective-permute-done
  17.2 4.7 %collective-permute-done.1 = f32[1024,2,16]{0,2,1:T(8,128)S(1)} collective-permute-done((f32[1024,2,16]{0,2,1:T(8,128)S(1)}, f32[1024,2,16]{0,2,1:T(8,128)S(1)}, u32[]{:S(2)}, u32[]{:S(2)}) %collective-permute-start.1) | collective-permute-done | bytes 131104 | tf_op jit(solution)/shard_map/ppermute | solution.py:21
  21.9 0.3 select_maximum_fusion.2
  22.2 0.0 copy-start.3
  22.3 72.2 %all-gather.3.cloned.1.call-done = f32[8192,256]{1,0:T(8,128)} async-done(((f32[1024,256]{1,0:T(8,128)}), f32[8192,256]{1,0:T(8,128)}) %all-gather.3.cloned.1.call-update) | async-done | bytes 8388624 | tf_op jit(solution)/shard_map/all_gather | solution.py:75
  94.4 17.6 %fusion.51 = f32[1024,256]{0,1:T(8,128)S(1)} fusion(bf16[8192,1024]{1,0:T(8,128)(2,1)} %param.6, f32[8192,256]{1,0:T(8,128)} %all-gather.3.cloned.1.call-done), kind=kOutput, calls=%fused_computation.86 | convolution fusion | flops 25769803776 | bytes 26214400 | tf_op jit(solution)/shard_map/dot_general | solution.py:65
  112.0 0.0 copy-done.3
  112.0 2.8 %multiply_add_fusion = (f32[1024,16,16]{0,2,1:T(8,128)}, f32[1024,16,16]{0,2,1:T(8,128)}) fusion(f32[1024,16,16]{0,2,1:T(8,128)S(1)} %bitcast.18, f32[1024]{0:T(1024)S(1)} %copy-done.3, f32[16,16]{1,0:T(8,128)S(1)} %select_n.13, f32[16,16]{1,0:T(8,128)S(1)} %mul.229, f32[1024,16,16]{0,2,1:T(8,128)S(1)} %bitcast.24, ...), kind=kLoop, calls=%fused_computation.75 | loop fusion | flops 8650752 | bytes 8673280 | tf_op jit(solution)/shard_map/add | solution.py:82
  114.8 0.0 all-gather.5.cloned.1.call-update
  114.8 1.0 fusion.49
  115.8 3.4 %collective-permute-start.2 = (f32[1024,2,16]{0,2,1:T(8,128)S(1)}, f32[1024,2,16]{0,2,1:T(8,128)S(1)}, u32[]{:S(2)}, u32[]{:S(2)}) collective-permute-start(f32[1024,2,16]{0,2,1:T(8,128)S(1)} %get-tuple-element.6), channel_id=1, source_target_pairs={{0,8},{8,16},{16,24},{1,9},{9,17},{17,25},{2,10},{10,18},{18,26},{... | collective-permute-start | bytes 393224 | tf_op jit(solution)/shard_map/ppermute | solution.py:20
  119.2 1.5 collective-permute-start.3
  120.7 1.7 collective-permute-done.2
  122.4 4.7 %collective-permute-done.3 = f32[1024,2,16]{0,2,1:T(8,128)S(1)} collective-permute-done((f32[1024,2,16]{0,2,1:T(8,128)S(1)}, f32[1024,2,16]{0,2,1:T(8,128)S(1)}, u32[]{:S(2)}, u32[]{:S(2)}) %collective-permute-start.3) | collective-permute-done | bytes 131104 | tf_op jit(solution)/shard_map/ppermute | solution.py:21
  127.1 1.5 select_maximum_fusion
  128.6 66.9 %all-gather.5.cloned.1.call-done = f32[8192,256]{0,1:T(8,128)} async-done(((f32[1024,256]{0,1:T(8,128)}), f32[8192,256]{0,1:T(8,128)}) %all-gather.5.cloned.1.call-update) | async-done | bytes 8388624 | tf_op jit(solution)/shard_map/all_gather | solution.py:75
  195.5 0.0 copy-start
  195.5 0.0 copy-start.2
  195.5 17.8 %fusion.52 = f32[256,1024]{1,0:T(8,128)S(1)} fusion(f32[8192,256]{0,1:T(8,128)} %all-gather.5.cloned.1.call-done, bf16[8192,1024]{1,0:T(8,128)(2,1)} %param.6), kind=kOutput, calls=%fused_computation.87 | convolution fusion | flops 25769803776 | bytes 26214400 | tf_op jit(solution)/shard_map/dot_general | solution.py:65
  213.3 0.0 copy-done
  213.3 0.0 copy-done.2
  213.3 1.9 fusion.14
  215.3 0.0 copy-start.1
  215.3 1.0 copy-done.1
  216.3 0.9 convolution_multiply_fusion
  217.2 2.5 %copy.19 = f32[1024,256]{1,0:T(8,128)} copy(f32[1024,256]{0,1:T(8,128)} %bitcast.22) | data formatting | bytes 2097152
  219.7 14.6 %psum.7 = f32[2,256]{1,0:T(2,128)} all-reduce(f32[2,256]{1,0:T(2,128)S(1)} %convolution_multiply_fusion), channel_id=1, replica_groups=mesh['space'=4,'mode'=8] {'mode'}, use_global_device_ids=true, to_apply=%region_0.1 | all-reduce | flops 512 | bytes 4096 | tf_op jit(solution)/shard_map/psum | solution.py:90
  (3 shorter events, 0.0 us)
Async XLA Ops:
  7.2 8.6 %copy-start.5 = (s32[256]{0:T(256)S(1)}, s32[256]{0:T(256)}, u32[]{:S(2)}) copy-start(s32[256]{0:T(256)} %param.9) | copy-start | bytes 3076
  7.2 8.7 %copy-start.4 = (f32[2,1024]{1,0:T(2,128)S(1)}, f32[2,1024]{1,0:T(2,128)}, u32[]{:S(2)}) copy-start(f32[2,1024]{1,0:T(2,128)} %param.7) | copy-start | bytes 24580
  7.2 87.2 %all-gather.3.cloned.1.call-start = ((), (), s32[]{:S(2)}) async-start(), calls=%async_computation | async-start | bytes 9437184 | tf_op jit(solution)/shard_map/all_gather | solution.py:75
  7.9 187.6 %all-gather.5.cloned.1.call-start = ((), (), s32[]{:S(2)}) async-start(), calls=%async_computation.1 | async-start | bytes 9437184 | tf_op jit(solution)/shard_map/all_gather | solution.py:75
  9.6 7.6 %collective-permute-start = (f32[1024,2,16]{0,2,1:T(8,128)S(1)}, f32[1024,2,16]{0,2,1:T(8,128)S(1)}, u32[]{:S(2)}, u32[]{:S(2)}) collective-permute-start(f32[1024,2,16]{0,2,1:T(8,128)S(1)} %get-tuple-element.8), channel_id=1, source_target_pairs={{0,8},{8,16},{16,24},{1,9},{9,17},{17,25},{2,10},{10,18},{18,26},{... | collective-permute-start | bytes 393224 | tf_op jit(solution)/shard_map/ppermute | solution.py:20
  14.4 7.5 %collective-permute-start.1 = (f32[1024,2,16]{0,2,1:T(8,128)S(1)}, f32[1024,2,16]{0,2,1:T(8,128)S(1)}, u32[]{:S(2)}, u32[]{:S(2)}) collective-permute-start(f32[1024,2,16]{0,2,1:T(8,128)S(1)} %get-tuple-element.9), channel_id=1, source_target_pairs={{8,0},{16,8},{24,16},{9,1},{17,9},{25,17},{10,2},{18,10},{26,18},{... | collective-permute-start | bytes 393224 | tf_op jit(solution)/shard_map/ppermute | solution.py:21
  22.2 89.7 %copy-start.3 = (f32[1024]{0:T(1024)S(1)}, f32[1024]{0:T(1024)}, u32[]{:S(2)}) copy-start(f32[1024]{0:T(1024)} %param.8) | copy-start | bytes 12292
  115.8 6.6 %collective-permute-start.2 = (f32[1024,2,16]{0,2,1:T(8,128)S(1)}, f32[1024,2,16]{0,2,1:T(8,128)S(1)}, u32[]{:S(2)}, u32[]{:S(2)}) collective-permute-start(f32[1024,2,16]{0,2,1:T(8,128)S(1)} %get-tuple-element.6), channel_id=1, source_target_pairs={{0,8},{8,16},{16,24},{1,9},{9,17},{17,25},{2,10},{10,18},{18,26},{... | collective-permute-start | bytes 393224 | tf_op jit(solution)/shard_map/ppermute | solution.py:20
  119.2 7.9 %collective-permute-start.3 = (f32[1024,2,16]{0,2,1:T(8,128)S(1)}, f32[1024,2,16]{0,2,1:T(8,128)S(1)}, u32[]{:S(2)}, u32[]{:S(2)}) collective-permute-start(f32[1024,2,16]{0,2,1:T(8,128)S(1)} %get-tuple-element.7), channel_id=1, source_target_pairs={{8,0},{16,8},{24,16},{9,1},{17,9},{25,17},{10,2},{18,10},{26,18},{... | collective-permute-start | bytes 393224 | tf_op jit(solution)/shard_map/ppermute | solution.py:21
  195.5 17.8 %copy-start = (f32[1024,16,16]{0,2,1:T(8,128)S(1)}, f32[1024,16,16]{0,2,1:T(8,128)}, u32[]{:S(2)}) copy-start(f32[1024,16,16]{0,2,1:T(8,128)} %get-tuple-element.4) | copy-start | bytes 3145732
  195.5 17.8 %copy-start.2 = (f32[1024,16,16]{0,2,1:T(8,128)S(1)}, f32[1024,16,16]{0,2,1:T(8,128)}, u32[]{:S(2)}) copy-start(f32[1024,16,16]{0,2,1:T(8,128)} %get-tuple-element.5) | copy-start | bytes 3145732
  215.3 1.0 copy-start.1
Sparse Core Ops, SparseCore 0:
  9.6 84.7 all-gather.2
  114.9 80.5 all-gather.4
where the time goes:
time: 242 us; the launch traced here: 241 us
  waiting for transfers between devices  152 us (63%)
  matrix products  36.2 us (15%)
  blocking collectives  14.6 us (6%)
  between operations  14.2 us (6%)
  starting transfers between devices  11.1 us (5%)
  other arithmetic  6.61 us (3%)
  local copies, waits for them, and re-layouts  6.27 us (3%)
    all_gather x2, waiting for transfers between devices, collide(): summed = fold_term(lax.all_gather(flat_field, 'mode', axis=0, tiled=True))  139 us
    dot_general x2, matrix products, fold_term(): lax.dot_general(matrix_rows, block_piece, (((0,), (0,)), ((), ())), preci...  35.3 us
    psum x1, blocking collectives, on_device(): heat_flux = lax.psum(flux_part, 'mode')  14.6 us
    ppermute x2, waiting for transfers between devices, padded_2(): after = lax.ppermute(leading, axis, down)  9.49 us
    ppermute x2, starting transfers between devices, padded_2(): before = lax.ppermute(last, axis, up)  8.27 us
    unnamed x14, local copies, waits for them, and re-layouts  5.1 us
  transfers between devices with their start and end apart: 6, of which 6 were waited for; matrix products, arithmetic and copies ran while one was open for 2% of the time, Pallas kernels for 0%

commit v1 on v0

v1 whole, which is shorter than its diff:
```python
import jax
import jax.numpy as jnp
from jax import lax
from jax.sharding import PartitionSpec as P

NY = 16


relax_rate = 0.5
time_step = 0.5


def halo_x(value, width):
    count, length = (lax.axis_size("space"), value.shape[1])
    up = [(i, (i + 1) % count) for i in range(count - 1)]
    down = [(j, i) for i, j in up]
    before = lax.ppermute(value[:, length - width :], "space", up)
    after = lax.ppermute(value[:, :width], "space", down)
    return before, after


def split_two(value):
    high = lax.reduce_precision(value, 8, 7)
    return jnp.concatenate(
        [high.astype(jnp.bfloat16), (value - high).astype(jnp.bfloat16)], axis=-1
    )


def dot_halves(matrix, value, contract):
    width = value.shape[1]
    both = lax.dot_general(
        matrix,
        split_two(value),
        (((contract,), (0,)), ((), ())),
        preferred_element_type=jnp.float32,
    )
    return both[:, :width] + both[:, width:]


def local_rate(flat, before, after, cell_type, velocity, capacity):
    cells = flat.shape[1]
    wide = jnp.concatenate([before, flat, after], axis=1)
    two = 2 * NY
    y = lax.broadcasted_iota(jnp.int32, (1, cells), 1) % NY

    def shifted(offset):
        return wide[:, two + offset : two + offset + cells]

    def shifted_y(offset):
        inside = (y + offset >= 0) & (y + offset < NY)
        return jnp.where(inside, shifted(offset), 0.0)

    def one_axis(speed, back_one, back_two, ahead_one, ahead_two):
        return jnp.maximum(speed, 0.0) * 0.5 * (
            3.0 * flat - 4.0 * back_one + back_two
        ) + jnp.minimum(speed, 0.0) * 0.5 * (-3.0 * flat + 4.0 * ahead_one - ahead_two)

    advection = one_axis(
        velocity[0][:, None], shifted(-NY), shifted(-two), shifted(NY), shifted(two)
    ) + one_axis(
        velocity[1][:, None], shifted_y(-1), shifted_y(-2), shifted_y(1), shifted_y(2)
    )
    contact = (cell_type > 0).astype(jnp.float32)
    reservoir = jnp.where(cell_type == 1, 1.0, -1.0).astype(jnp.float32)
    contact_term = relax_rate * contact[None] * (flat - reservoir[None] * capacity[:, None])
    return -advection - contact_term


def on_device(distribution, scatter_matrix, velocity, capacity, cell_type):
    local_cells = distribution.shape[1]
    total_modes = scatter_matrix.shape[0]
    half = local_cells // 2

    def by_gather(value):
        whole = lax.all_gather(value, "mode", axis=0, tiled=True)
        return dot_halves(scatter_matrix, whole, 0)

    def by_scatter(value):
        terms = dot_halves(scatter_matrix, value, 1)
        return lax.psum_scatter(terms, "mode", scatter_dimension=0, tiled=True)

    weights = capacity[None, :] * velocity
    all_weights = lax.all_gather(weights, "mode", axis=1, tiled=True)
    weights_scattered = dot_halves(scatter_matrix, all_weights.T, 0).T

    first_a = by_gather(distribution[:, :half])
    first_b = by_scatter(distribution[:, half:])
    before, after = halo_x(distribution, 2 * NY)
    still = local_rate(distribution, before, after, cell_type, velocity, capacity)
    rate_a = still[:, :half] - first_a
    rate_b = still[:, half:] - first_b
    mid_a = distribution[:, :half] + time_step * rate_a
    mid_b = distribution[:, half:] + time_step * rate_b
    second_a = by_scatter(mid_a)
    second_b = by_gather(mid_b)
    midpoint = jnp.concatenate([mid_a, mid_b], axis=1)
    before, after = halo_x(midpoint, 2 * NY)
    still_mid = local_rate(midpoint, before, after, cell_type, velocity, capacity)
    step = 0.5 * time_step
    most = distribution + step * (jnp.concatenate([rate_a, rate_b], axis=1) + still_mid)
    flux_part = (
        jnp.dot(weights, most, precision=lax.Precision.HIGHEST)
        - step * jnp.dot(weights_scattered, midpoint, precision=lax.Precision.HIGHEST)
    ) / jnp.sqrt(jnp.float32(total_modes))
    heat_flux = lax.all_gather(flux_part, "mode", axis=0).sum(0)
    updated = most - step * jnp.concatenate([second_a, second_b], axis=1)
    return (updated, heat_flux)


def solution(mesh):
    return jax.shard_map(
        on_device,
        mesh=mesh,
        in_specs=(P("mode", "space"), P(None, "mode"), P(None, "mode"), P("mode"), P("space")),
        out_specs=(P("mode", "space"), P(None, "space")),
        check_vma=False,
    )
```

time: 242 us -> 243 us (level)
  the two profiles are of different devices: /device:TPU:0 before, /device:TPU:13 now
where the time goes in v1:
time: 243 us; the launch traced here: 238 us
  waiting for transfers between devices  83.8 us (34%)
  matrix products  67.9 us (28%)
  other arithmetic  30.5 us (13%)
  blocking collectives  25 us (10%)
  between operations  14 us (6%)
  starting transfers between devices  11.8 us (5%)
  local copies, waits for them, and re-layouts  5.06 us (2%)
    reduce_scatter x2, waiting for transfers between devices, by_scatter(): return lax.psum_scatter(terms, 'mode', scatter_dimension=0, tiled=True)  68.8 us
    dot_general x5, matrix products, dot_halves(): lax.dot_general(matrix, split_two(value), (((contract,), (0,)), ((), ()))...  63.6 us
    all_gather x1, blocking collectives, on_device(): all_weights = lax.all_gather(weights, 'mode', axis=1, tiled=True)  13.1 us
    add x3, other arithmetic, dot_halves(): return both[:, :width] + both[:, width:]  12.9 us
    all_gather x1, blocking collectives, on_device(): heat_flux = lax.all_gather(flux_part, 'mode', axis=0).sum(0)  11.9 us
    all_gather x2, waiting for transfers between devices, by_gather(): whole = lax.all_gather(value, 'mode', axis=0, tiled=True)  10.6 us
    convert_element_type x4, other arithmetic, split_two(): high.astype(jnp.bfloat16)  8.95 us
    ppermute x2, starting transfers between devices, halo_x(): after = lax.ppermute(value[:, :width], 'space', down)  6.15 us
  transfers between devices with their start and end apart: 8, of which 5 were waited for; matrix products, arithmetic and copies ran while one was open for 36% of the time, Pallas kernels for 0%

profile of v1, /device:TPU:13, one launch (start us, length us, event | category | flops | bytes accessed | tf_op | source)
XLA Modules:
  0.0 238.1 jit_solution(17580942267124802354)
XLA Ops:
  7.2 0.0 all-gather.5.cloned.1.call-start
  7.2 1.6 copy.27
  8.8 0.9 fusion.95
  9.7 0.0 all-gather.5.cloned.1.call-update
  9.7 0.0 reduce-scatter.3.cloned.1.call-start
  9.8 18.9 %convolution_bitcast_fusion.1 = f32[8192,256]{0,1:T(8,128)} fusion(bf16[8192,1024]{1,0:T(8,128)(2,1)} %param.6, bf16[1024,128]{0,1:T(8,128)(2,1)S(1)} %get-tuple-element.22, bf16[1024,128]{0,1:T(8,128)(2,1)S(1)} %get-tuple-element.23), kind=kOutput, calls=%fused_computation.1 | convolution fusion | flops 4296015872 | bytes 25690112 | tf_op jit(solution)/shard_map/dot_general | solution.py:31
  28.7 6.0 %slice_add_fusion.1 = f32[8192,128]{0,1:T(8,128)} fusion(f32[8192,256]{0,1:T(8,128)} %convolution_bitcast_fusion.1), kind=kLoop, calls=%fused_computation.9 | loop fusion | flops 1048576 | bytes 12582912 | tf_op jit(solution)/shard_map/add | solution.py:37
  34.7 0.0 copy-start.5
  34.7 0.0 copy-start.4
  34.7 0.0 copy-start.3
  34.7 0.0 reduce-scatter.3.cloned.1.call-update
  34.7 0.0 all-gather.7.cloned.1.call-start
  34.8 3.1 %collective-permute-start.1 = (f32[1024,32]{0,1:T(8,128)S(1)}, f32[1024,32]{0,1:T(8,128)S(1)}, u32[]{:S(2)}, u32[]{:S(2)}) collective-permute-start(f32[1024,32]{0,1:T(8,128)S(1)} %get-tuple-element.25), channel_id=1, source_target_pairs={{8,0},{16,8},{24,16},{9,1},{17,9},{25,17},{10,2},{18,10},{26,18},{... | collective-permute-start | bytes 393224 | tf_op jit(solution)/shard_map/ppermute | solution.py:18
  37.9 2.2 collective-permute-start
  40.1 0.0 copy-done.5
  40.1 0.0 copy-done.4
  40.2 1.0 collective-permute-done.1
  41.2 3.3 %collective-permute-done = f32[1024,32]{0,1:T(8,128)S(1)} collective-permute-done((f32[1024,32]{0,1:T(8,128)S(1)}, f32[1024,32]{0,1:T(8,128)S(1)}, u32[]{:S(2)}, u32[]{:S(2)}) %collective-permute-start) | collective-permute-done | bytes 131104 | tf_op jit(solution)/shard_map/ppermute | solution.py:17
  44.5 0.0 copy-done.3
  44.5 2.3 fusion.28
  46.8 10.6 %all-gather.5.cloned.1.call-done = f32[8192,128]{0,1:T(8,128)} async-done(((f32[1024,128]{0,1:T(8,128)}), f32[8192,128]{0,1:T(8,128)}) %all-gather.5.cloned.1.call-update) | async-done | bytes 4194320 | tf_op jit(solution)/shard_map/all_gather | solution.py:75
  57.4 2.9 %reduce-precision_convert_fusion.1 = (bf16[8192,128]{0,1:T(8,128)(2,1)S(1)}, bf16[8192,128]{0,1:T(8,128)(2,1)S(1)}) fusion(f32[8192,128]{0,1:T(8,128)} %all-gather.5.cloned.1.call-done), kind=kLoop, calls=%fused_computation.5 | loop fusion | flops 4194304 | bytes 8388608 | tf_op jit(solution)/shard_map/convert_element_type | solution.py:25
  60.2 9.2 %fusion.13 = f32[1024,256]{0,1:T(8,128)} fusion(bf16[8192,1024]{1,0:T(8,128)(2,1)} %param.6, bf16[8192,128]{0,1:T(8,128)(2,1)S(1)} %get-tuple-element.14, bf16[8192,128]{0,1:T(8,128)(2,1)S(1)} %get-tuple-element.13), kind=kOutput, calls=%fused_computation.27 | convolution fusion | flops 4303355904 | bytes 22020096 | tf_op jit(solution)/shard_map/dot_general | solution.py:31
  69.4 38.6 %reduce-scatter.3.cloned.1.call-done = f32[1024,128]{0,1:T(8,128)} async-done(((f32[8192,128]{0,1:T(8,128)}), f32[1024,128]{0,1:T(8,128)}) %reduce-scatter.3.cloned.1.call-update) | async-done | bytes 524304 | tf_op jit(solution)/shard_map/reduce_scatter | solution.py:80
  108.0 2.8 %reduce-precision_convert_fusion.2 = (bf16[1024,128]{0,1:T(8,128)(2,1)S(1)}, f32[1024,128]{0,1:T(8,128)S(1)}, f32[1024,128]{0,1:T(8,128)}, f32[1024,128]{0,1:T(8,128)}, f32[1024,128]{0,1:T(8,128)}) fusion(f32[1024,256]{0,1:T(8,128)S(1)} %copy.27, f32[1024,256]{0,1:T(8,128)} %fusion.13, f32[1024,256]{0,1:T(8,128)S(1)} %fusion.28, ...), kind=kLoop, calls=%fused_computation.108 | loop fusion | flops 1179648 | bytes 6029312 | tf_op jit(solution)/shard_map/convert_element_type | solution.py:25
  110.8 0.0 copy-start
  110.8 0.0 all-gather.7.cloned.1.call-update
  110.8 0.2 reduce-scatter.5.cloned.1.call-start
  111.1 18.9 %convolution_bitcast_fusion = f32[8192,256]{0,1:T(8,128)} fusion(bf16[8192,1024]{1,0:T(8,128)(2,1)} %param.6, bf16[1024,128]{0,1:T(8,128)(2,1)S(1)} %fusion.74, bf16[1024,128]{0,1:T(8,128)(2,1)S(1)} %get-tuple-element.8), kind=kOutput, calls=%fused_computation | convolution fusion | flops 4296015872 | bytes 25690112 | tf_op jit(solution)/shard_map/dot_general | solution.py:31
  130.0 6.0 %slice_add_fusion = f32[8192,128]{0,1:T(8,128)} fusion(f32[8192,256]{0,1:T(8,128)} %convolution_bitcast_fusion), kind=kLoop, calls=%fused_computation.8 | loop fusion | flops 1048576 | bytes 12582912 | tf_op jit(solution)/shard_map/add | solution.py:37
  136.0 0.0 reduce-scatter.5.cloned.1.call-update
  136.0 13.1 %all_gather.17 = f32[2,8192]{1,0:T(2,128)S(1)} all-gather(f32[2,1024]{1,0:T(2,128)S(1)} %broadcast_multiply_fusion), channel_id=1, replica_groups=mesh['space'=4,'mode'=8] {'mode'}, dimensions={1}, use_global_device_ids=true | all-gather | bytes 73728 | tf_op jit(solution)/shard_map/all_gather | solution.py:83
  149.1 0.9 slice.186
  150.1 0.0 copy-done
  150.1 3.1 %collective-permute-start.2 = (f32[1024,32]{0,1:T(8,128)S(1)}, f32[1024,32]{0,1:T(8,128)S(1)}, u32[]{:S(2)}, u32[]{:S(2)}) collective-permute-start(f32[1024,32]{0,1:T(8,128)S(1)} %slice.186), channel_id=1, source_target_pairs={{0,8},{8,16},{16,24},{1,9},{9,17},{17,25},{2,10},{10,18},{18,26},{... | collective-permute-start | bytes 393224 | tf_op jit(solution)/shard_map/ppermute | solution.py:17
  153.2 3.1 %collective-permute-start.3 = (f32[1024,32]{0,1:T(8,128)S(1)}, f32[1024,32]{0,1:T(8,128)S(1)}, u32[]{:S(2)}, u32[]{:S(2)}) collective-permute-start(f32[1024,32]{0,1:T(8,128)S(1)} %slice.189), channel_id=1, source_target_pairs={{8,0},{16,8},{24,16},{9,1},{17,9},{25,17},{10,2},{18,10},{26,18},{... | collective-permute-start | bytes 393224 | tf_op jit(solution)/shard_map/ppermute | solution.py:18
  156.3 0.0 copy-start.1
  156.3 0.0 copy-start.2
  156.3 8.1 %convolution_bitcast_fusion.2 = f32[1024,4]{0,1:T(4,128)S(1)} fusion(bf16[8192,1024]{1,0:T(8,128)(2,1)} %param.6, bf16[8192,2]{0,1:T(2,128)(2,1)S(1)} %get-tuple-element.27, bf16[8192,2]{0,1:T(2,128)(2,1)S(1)} %get-tuple-element.26), kind=kOutput, calls=%fused_computation.36 | convolution fusion | flops 67239936 | bytes 16859136 | tf_op jit(solution)/shard_map/dot_general | solution.py:31
  164.4 0.0 collective-permute-done.2
  164.4 0.0 collective-permute-done.3
  164.5 0.0 copy-done.1
  164.5 0.0 copy-done.2
  164.5 0.3 pad_maximum_fusion
  164.8 0.0 all-gather.7.cloned.1.call-done
  164.8 3.3 %reduce-precision_convert_fusion = (bf16[8192,128]{0,1:T(8,128)(2,1)S(1)}, bf16[8192,128]{0,1:T(8,128)(2,1)S(1)}) fusion(f32[8192,128]{0,1:T(8,128)} %all-gather.7.cloned.1.call-done), kind=kLoop, calls=%fused_computation.3 | loop fusion | flops 4194304 | bytes 8388608 | tf_op jit(solution)/shard_map/convert_element_type | solution.py:25
  168.1 8.5 %fusion.10 = f32[1024,256]{0,1:T(8,128)S(1)} fusion(bf16[8192,1024]{1,0:T(8,128)(2,1)} %param.6, bf16[8192,128]{0,1:T(8,128)(2,1)S(1)} %get-tuple-element.16, bf16[8192,128]{0,1:T(8,128)(2,1)S(1)} %get-tuple-element.15), kind=kOutput, calls=%fused_computation.26 | convolution fusion | flops 4303355904 | bytes 22020096 | tf_op jit(solution)/shard_map/dot_general | solution.py:31
  176.5 0.9 slice_add_fusion.3
  177.4 30.3 %reduce-scatter.5.cloned.1.call-done = f32[1024,128]{0,1:T(8,128)} async-done(((f32[8192,128]{0,1:T(8,128)}), f32[1024,128]{0,1:T(8,128)}) %reduce-scatter.5.cloned.1.call-update) | async-done | bytes 524304 | tf_op jit(solution)/shard_map/reduce_scatter | solution.py:80
  207.6 4.6 %fusion.72 = (f32[1024,256]{0,1:T(8,128)}, f32[1024,256]{0,1:T(8,128)}) fusion(f32[1024,128]{0,1:T(8,128)} %slice_add_fusion.3, f32[1024,128]{0,1:T(8,128)} %reduce-scatter.5.cloned.1.call-done, f32[1024,256]{0,1:T(8,128)S(1)} %copy.27, f32[1024]{0:T(1024)S(1)} %copy-done.3, f32[256]{0:T(256)S(1)} %get-tuple-element.33, f32[256]{0:T(256)S(1)} %get-tuple-element.32, ...), kind=kLoop, calls=%fused_computation.106 | loop fusion | flops 9961472 | bytes 14703616 | tf_op jit(solution)/shard_map/sub | solution.py:106
  212.2 2.5 %copy.28 = f32[1024,256]{1,0:T(8,128)} copy(f32[1024,256]{0,1:T(8,128)} %get-tuple-element.6) | data formatting | bytes 2097152
  214.7 2.1 fusion.97
  216.9 2.1 fusion.18
  219.0 11.9 %all-gather.1 = f32[8,2,256]{2,1,0:T(2,128)S(1)} all-gather(f32[1,2,256]{2,1,0:T(2,128)S(1)} %fusion.18), channel_id=2, replica_groups=mesh['space'=4,'mode'=8] {'mode'}, dimensions={0}, use_global_device_ids=true | all-gather | bytes 18432 | tf_op jit(solution)/shard_map/all_gather | solution.py:105
  230.9 0.6 reduce_sum.9
  (9 shorter events, 0.2 us)
Async XLA Ops:
  7.2 50.2 %all-gather.5.cloned.1.call-start = ((), (), s32[]{:S(2)}) async-start(), calls=%async_computation.2 | async-start | bytes 4718592 | tf_op jit(solution)/shard_map/all_gather | solution.py:75
  9.7 98.3 %reduce-scatter.3.cloned.1.call-start = ((), (), s32[]{:S(2)}) async-start(), calls=%async_computation.3 | async-start | bytes 4718592 | tf_op jit(solution)/shard_map/reduce_scatter | solution.py:80
  34.7 5.4 %copy-start.5 = (s32[256]{0:T(256)S(1)}, s32[256]{0:T(256)}, u32[]{:S(2)}) copy-start(s32[256]{0:T(256)} %param.9) | copy-start | bytes 3076
  34.7 5.4 %copy-start.4 = (f32[2,1024]{1,0:T(2,128)S(1)}, f32[2,1024]{1,0:T(2,128)}, u32[]{:S(2)}) copy-start(f32[2,1024]{1,0:T(2,128)} %param.7) | copy-start | bytes 24580
  34.7 9.8 %copy-start.3 = (f32[1024]{0:T(1024)S(1)}, f32[1024]{0:T(1024)}, u32[]{:S(2)}) copy-start(f32[1024]{0:T(1024)} %param.8) | copy-start | bytes 12292
  34.7 130.0 %all-gather.7.cloned.1.call-start = ((), (), s32[]{:S(2)}) async-start(), calls=%async_computation.5 | async-start | bytes 4718592 | tf_op jit(solution)/shard_map/all_gather | solution.py:75
  34.8 6.4 %collective-permute-start.1 = (f32[1024,32]{0,1:T(8,128)S(1)}, f32[1024,32]{0,1:T(8,128)S(1)}, u32[]{:S(2)}, u32[]{:S(2)}) collective-permute-start(f32[1024,32]{0,1:T(8,128)S(1)} %get-tuple-element.25), channel_id=1, source_target_pairs={{8,0},{16,8},{24,16},{9,1},{17,9},{25,17},{10,2},{18,10},{26,18},{... | collective-permute-start | bytes 393224 | tf_op jit(solution)/shard_map/ppermute | solution.py:18
  37.9 6.6 %collective-permute-start = (f32[1024,32]{0,1:T(8,128)S(1)}, f32[1024,32]{0,1:T(8,128)S(1)}, u32[]{:S(2)}, u32[]{:S(2)}) collective-permute-start(f32[1024,32]{0,1:T(8,128)S(1)} %get-tuple-element.24), channel_id=1, source_target_pairs={{0,8},{8,16},{16,24},{1,9},{9,17},{17,25},{2,10},{10,18},{18,26},{... | collective-permute-start | bytes 393224 | tf_op jit(solution)/shard_map/ppermute | solution.py:17
  110.8 39.3 %copy-start = (f32[1024,128]{0,1:T(8,128)}, f32[1024,128]{0,1:T(8,128)S(1)}, u32[]{:S(2)}) copy-start(f32[1024,128]{0,1:T(8,128)S(1)} %get-tuple-element.9) | copy-start | bytes 1572868
  110.8 96.8 %reduce-scatter.5.cloned.1.call-start = ((), (), s32[]{:S(2)}) async-start(), calls=%async_computation.4 | async-start | bytes 4718592 | tf_op jit(solution)/shard_map/reduce_scatter | solution.py:80
  150.1 14.4 %collective-permute-start.2 = (f32[1024,32]{0,1:T(8,128)S(1)}, f32[1024,32]{0,1:T(8,128)S(1)}, u32[]{:S(2)}, u32[]{:S(2)}) collective-permute-start(f32[1024,32]{0,1:T(8,128)S(1)} %slice.186), channel_id=1, source_target_pairs={{0,8},{8,16},{16,24},{1,9},{9,17},{17,25},{2,10},{10,18},{18,26},{... | collective-permute-start | bytes 393224 | tf_op jit(solution)/shard_map/ppermute | solution.py:17
  153.2 11.3 %collective-permute-start.3 = (f32[1024,32]{0,1:T(8,128)S(1)}, f32[1024,32]{0,1:T(8,128)S(1)}, u32[]{:S(2)}, u32[]{:S(2)}) collective-permute-start(f32[1024,32]{0,1:T(8,128)S(1)} %slice.189), channel_id=1, source_target_pairs={{8,0},{16,8},{24,16},{9,1},{17,9},{25,17},{10,2},{18,10},{26,18},{... | collective-permute-start | bytes 393224 | tf_op jit(solution)/shard_map/ppermute | solution.py:18
  156.3 8.2 %copy-start.1 = (f32[1024,128]{0,1:T(8,128)S(1)}, f32[1024,128]{0,1:T(8,128)}, u32[]{:S(2)}) copy-start(f32[1024,128]{0,1:T(8,128)} %copy-done) | copy-start | bytes 1572868
  156.3 8.2 %copy-start.2 = (f32[1024,128]{0,1:T(8,128)S(1)}, f32[1024,128]{0,1:T(8,128)}, u32[]{:S(2)}) copy-start(f32[1024,128]{0,1:T(8,128)} %get-tuple-element.17) | copy-start | bytes 1572868
Sparse Core Ops, SparseCore 0:
  10.2 47.1 all-gather.4
  59.6 48.3 reduce-scatter.2
  110.9 46.2 all-gather.6
  159.4 48.2 reduce-scatter.4

commit v2 on v1

v2 whole, which is shorter than its diff:
```python
import functools

import numpy as np

import jax
import jax.numpy as jnp
from jax import lax
from jax.experimental import pallas as pl
from jax.experimental.pallas import tpu as pltpu
from jax.sharding import PartitionSpec as P

NY = 16
HALO = 2 * NY


relax_rate = 0.5
time_step = 0.5
VMEM_BYTES = 48 * 1024 * 1024


def halves(value):
    high = value.astype(jnp.bfloat16)
    low = (value - high.astype(jnp.float32)).astype(jnp.bfloat16)
    return high, low


def scatter_kernel(core_ref, mine_rows, other_rows, field, mine, other, parts):
    cells = field.shape[1]

    @pl.when(pl.program_id(0) == 0)
    def _():
        parts[...] = jnp.concatenate(halves(field[...]), axis=1)

    for rows, out in ((mine_rows, mine), (other_rows, other)):
        both = jnp.dot(rows[...], parts[...], preferred_element_type=jnp.float32)
        out[0] = both[:, :cells] + both[:, cells:]


def partial_products(matrix, field, core):
    total, modes = matrix.shape
    cells = field.shape[1]
    chips = total // (2 * modes)
    out = jax.ShapeDtypeStruct((chips, modes, cells), jnp.float32)
    out_spec = pl.BlockSpec((1, modes, cells), lambda t, core: (t, 0, 0))
    return pl.pallas_call(
        scatter_kernel,
        out_shape=(out, out),
        grid_spec=pltpu.PrefetchScalarGridSpec(
            num_scalar_prefetch=1,
            grid=(chips,),
            in_specs=[
                pl.BlockSpec((modes, modes), lambda t, core: (2 * t + core[0], 0)),
                pl.BlockSpec((modes, modes), lambda t, core: (2 * t + 1 - core[0], 0)),
                pl.BlockSpec((modes, cells), lambda t, core: (0, 0)),
            ],
            out_specs=(out_spec, out_spec),
            scratch_shapes=[pltpu.VMEM((modes, 2 * cells), jnp.bfloat16)],
        ),
        compiler_params=pltpu.CompilerParams(vmem_limit_bytes=VMEM_BYTES),
        cost_estimate=pl.CostEstimate(
            flops=4 * total * modes * cells,
            bytes_accessed=2 * total * modes + 4 * total * cells,
            transcendentals=0,
        ),
        name="partial_products",
    )(core, matrix, matrix, field)


def gather_kernel(scale, slots, order_ref, rows, base, *refs):
    fields, refs = refs[:slots], refs[slots:]
    if len(refs) == 4:
        weights, out, weights_out, total = refs
    else:
        (out, total), weights = refs, None
    step = pl.program_id(0)
    cells = out.shape[1]

    @pl.when(step == 0)
    def _():
        total[...] = jnp.zeros_like(total)

    for slot in range(slots):

        @pl.when(step == slot)
        def _(slot=slot):
            pieces = list(halves(fields[slot][...].T))
            if weights is not None:
                pieces += halves(weights[...])
            left = jnp.concatenate(pieces, axis=0)
            total[...] += jnp.dot(left, rows[...], preferred_element_type=jnp.float32)

    @pl.when(step == slots - 1)
    def _():
        result = total[:cells] + total[cells : 2 * cells]
        out[...] = base[...] - scale * result.T
        if weights is not None:
            weights_out[...] = total[2 * cells : 2 * cells + 8] + total[2 * cells + 8 :]


def whole_product(matrix, fields, order, base, scale, weights=None):
    total, modes = matrix.shape
    cells = base.shape[1]
    slots = len(fields)
    whole = pl.BlockSpec((modes, cells), lambda s, order: (0, 0))
    in_specs = [pl.BlockSpec((modes, modes), lambda s, order: (order[s], 0)), whole]
    in_specs += [whole] * slots
    out_shape = [jax.ShapeDtypeStruct((modes, cells), jnp.float32)]
    out_specs = [whole]
    operands = [matrix, base, *fields]
    rows = 2 * cells
    if weights is not None:
        in_specs.append(pl.BlockSpec((8, modes), lambda s, order: (0, order[s])))
        operands.append(weights)
        out_shape.append(jax.ShapeDtypeStruct((8, modes), jnp.float32))
        out_specs.append(pl.BlockSpec((8, modes), lambda s, order: (0, 0)))
        rows += 16
    return pl.pallas_call(
        functools.partial(gather_kernel, scale, slots),
        out_shape=out_shape,
        grid_spec=pltpu.PrefetchScalarGridSpec(
            num_scalar_prefetch=1,
            grid=(slots,),
            in_specs=in_specs,
            out_specs=out_specs,
            scratch_shapes=[pltpu.VMEM((rows, modes), jnp.float32)],
        ),
        compiler_params=pltpu.CompilerParams(vmem_limit_bytes=VMEM_BYTES),
        cost_estimate=pl.CostEstimate(
            flops=4 * total * modes * cells,
            bytes_accessed=2 * total * modes + 4 * total * cells,
            transcendentals=0,
        ),
        name="whole_product",
    )(order, *operands)


def still_rate(field, before, after, columns, kinds):
    cells = field.shape[1]
    wide = jnp.concatenate([before, field, after], axis=1)
    edge = before.shape[1]
    y = lax.broadcasted_iota(jnp.int32, (1, cells), 1) % NY

    def shifted(offset):
        return wide[:, edge + offset : edge + offset + cells]

    def shifted_y(offset):
        inside = (y + offset >= 0) & (y + offset < NY)
        return jnp.where(inside, shifted(offset), 0.0)

    def one_axis(speed, back_one, back_two, ahead_one, ahead_two):
        return jnp.maximum(speed, 0.0) * 0.5 * (
            3.0 * field - 4.0 * back_one + back_two
        ) + jnp.minimum(speed, 0.0) * 0.5 * (-3.0 * field + 4.0 * ahead_one - ahead_two)

    advection = one_axis(
        columns[:, 0:1], shifted(-NY), shifted(-2 * NY), shifted(NY), shifted(2 * NY)
    ) + one_axis(
        columns[:, 1:2], shifted_y(-1), shifted_y(-2), shifted_y(1), shifted_y(2)
    )
    contact = (kinds > 0).astype(jnp.float32)
    reservoir = jnp.where(kinds == 1, 1.0, -1.0).astype(jnp.float32)
    return -advection - relax_rate * contact * (field - reservoir * columns[:, 2:3])


def strips(before, after):
    rows = before.shape[1]
    pad = jnp.zeros((rows, 128 - HALO), jnp.float32)
    return (
        jnp.concatenate([pad, before[...].T], axis=1),
        jnp.concatenate([after[...].T, pad], axis=1),
    )


def first_kernel(field, before, after, table, kinds, base_a, base_b):
    value = field[...]
    half = base_a.shape[1]
    rate = still_rate(value, *strips(before, after), table[...].T, kinds[...])
    base = value + time_step * rate
    base_a[...] = base[:, :half]
    base_b[...] = base[:, half:]


def second_kernel(
    field, mid_a, mid_b, before, after, table, kinds, scattered, end_a, end_b, flux
):
    half = end_a.shape[1]
    mid = jnp.concatenate([mid_a[...], mid_b[...]], axis=1)
    columns = table[...].T
    rate = still_rate(mid, *strips(before, after), columns, kinds[...])
    step = 0.5 * time_step
    end = 0.5 * (field[...] + mid) + step * rate
    end_a[...] = end[:, :half]
    end_b[...] = end[:, half:]
    taken = scattered[...].T

    @pl.when(pl.program_id(0) == 0)
    def _():
        flux[...] = jnp.zeros_like(flux)

    for d in range(2):
        weight = columns[:, 3 + d : 4 + d]
        terms = weight * end - (step * taken[:, d : d + 1]) * mid
        flux[d : d + 1, :] += jnp.sum(terms, axis=0, keepdims=True)


def stencil_call(kernel, modes, cells, arrays, kinds_of, outs):
    block = min(modes, 256)
    specs = {
        "rows": lambda a: pl.BlockSpec((block, a.shape[1]), lambda i: (i, 0)),
        "columns": lambda a: pl.BlockSpec((a.shape[0], block), lambda i: (0, i)),
        "whole": lambda a: pl.BlockSpec(a.shape, lambda i: (0, 0)),
    }
    return pl.pallas_call(
        kernel,
        out_shape=[shape for shape, _ in outs],
        grid=(modes // block,),
        in_specs=[specs[kind](a) for a, kind in zip(arrays, kinds_of)],
        out_specs=[specs[kind](shape) for shape, kind in outs],
        compiler_params=pltpu.CompilerParams(vmem_limit_bytes=VMEM_BYTES),
        cost_estimate=pl.CostEstimate(
            flops=40 * modes * cells, bytes_accessed=12 * modes * cells, transcendentals=0
        ),
        name="stencil",
    )(*arrays)


def halo(leading, last):
    count = lax.axis_size("space")
    up = [(i, i + 1) for i in range(count - 1)]
    down = [(j, i) for i, j in up]
    before = lax.ppermute(last, "space", up)
    after = lax.ppermute(leading, "space", down)
    return before, after


def slot_sources(chips, place):
    found = []
    for step in range(chips - 1):
        if place >= step + 1:
            found.append((0, step, place - 1 - step))
        if place <= chips - 2 - step:
            found.append((1, step, place + 1 + step))
    return found


def block_order(chips):
    orders = []
    for device in range(2 * chips):
        order = []
        for core in (device % 2, 1 - device % 2):
            chip = device // 2
            place = chip if core == 0 else chips - 1 - chip
            sources = [place] + [q for _, _, q in slot_sources(chips, place)]
            blocks = [2 * (q if core == 0 else chips - 1 - q) + core for q in sources]
            order.append(blocks)
        orders.append(order[0] + order[1])
    return np.array(orders, np.int32)


class Line:
    def __init__(self):
        devices = lax.axis_size("mode")
        self.chips = devices // 2
        me = lax.axis_index("mode")
        self.core = me % 2
        self.chip = me // 2
        self.place = jnp.where(self.core == 0, self.chip, self.chips - 1 - self.chip)
        right = [[(2 * z + c, 2 * z + 2 + c) for z in range(self.chips - 1)] for c in (0, 1)]
        left = [[(j, i) for i, j in pairs] for pairs in right]
        self.streams = (right[0] + left[1], right[1] + left[0])
        self.pairs = [(i, i ^ 1) for i in range(devices)]
        self.order = jnp.asarray(block_order(self.chips))[me]

    def exchange(self, value):
        return lax.ppermute(value, "mode", self.pairs)

    def along(self, stream, value):
        return lax.ppermute(value, "mode", self.streams[stream])

    def chip_at(self, stream, place):
        turned = self.core == stream
        chip = jnp.where(turned, place, self.chips - 1 - place)
        return jnp.clip(chip, 0, self.chips - 1)

    def place_in(self, stream):
        return self.place if stream == 0 else self.chips - 1 - self.place

    def pick(self, arrived, slot):
        chosen = None
        for place in range(self.chips):
            stream, step, _ = slot_sources(self.chips, place)[slot]
            value = arrived[stream][step]
            chosen = value if chosen is None else jnp.where(self.place == place, value, chosen)
        return chosen

    def run(self, own, mine, other):
        theirs = self.exchange(other)

        def term(chip):
            return lax.dynamic_index_in_dim(mine, chip, 0, False) + lax.dynamic_index_in_dim(
                theirs, chip, 0, False
            )

        here, there = [own], [self.exchange(own)]
        arrived = ([], [])
        for step in range(self.chips):
            for stream in (0, 1):
                if step == 0:
                    payload = own
                else:
                    place = self.place_in(stream)
                    added = term(self.chip_at(stream, place + self.chips - step))
                    payload = arrived[stream][-1] + jnp.where(place < step, added, 0.0)
                arrived[stream].append(self.along(stream, payload))
            if step < self.chips - 1:
                block = self.pick(arrived, step)
                here.append(block)
                there.append(self.exchange(block))
        total = arrived[0][-1] + arrived[1][-1] + term(self.chip)
        return here + there, total

    def gather_rows(self, value):
        me = lax.axis_index("mode")
        bit = 1
        while bit < 2 * self.chips:
            pairs = [(i, i ^ bit) for i in range(2 * self.chips)]
            other = lax.ppermute(value, "mode", pairs)
            later = (me // bit) % 2 == 1
            value = jnp.concatenate(
                [jnp.where(later, other, value), jnp.where(later, value, other)], axis=1
            )
            bit *= 2
        return value

    def add_up(self, value):
        bit = 1
        while bit < 2 * self.chips:
            pairs = [(i, i ^ bit) for i in range(2 * self.chips)]
            value = value + lax.ppermute(value, "mode", pairs)
            bit *= 2
        return value


def on_device(distribution, scatter_matrix, velocity, capacity, cell_type):
    modes, cells = distribution.shape
    total_modes = scatter_matrix.shape[0]
    half = cells // 2
    line = Line()
    core = jnp.reshape(line.core, (1,)).astype(jnp.int32)
    weights = capacity[None, :] * velocity
    table = jnp.concatenate(
        [velocity, capacity[None, :], weights, jnp.zeros((3, modes), jnp.float32)], axis=0
    )
    kinds = cell_type[None, :]
    part = jax.ShapeDtypeStruct((modes, half), jnp.float32)

    own_a = distribution[:, :half]
    own_b = distribution[:, half:]
    mine, other = partial_products(scatter_matrix, own_b, core)
    before, after = halo(distribution[:, :HALO].T, distribution[:, -HALO:].T)
    all_weights = jnp.pad(line.gather_rows(weights), ((0, 6), (0, 0)))
    base_a, base_b = stencil_call(
        first_kernel,
        modes,
        cells,
        [distribution, before, after, table, kinds],
        ["rows", "columns", "columns", "columns", "whole"],
        [(part, "rows"), (part, "rows")],
    )
    blocks, sum_b = line.run(own_a, mine, other)
    mid_b = base_b - time_step * sum_b
    mid_a, scattered = whole_product(
        scatter_matrix, blocks, line.order, base_a, time_step, all_weights
    )

    step = 0.5 * time_step
    mine, other = partial_products(scatter_matrix, mid_a, core)
    before, after = halo(mid_a[:, :HALO].T, mid_b[:, -HALO:].T)
    end_a, end_b, flux = stencil_call(
        second_kernel,
        modes,
        cells,
        [distribution, mid_a, mid_b, before, after, table, kinds, scattered],
        ["rows", "rows", "rows", "columns", "columns", "columns", "whole", "columns"],
        [(part, "rows"), (part, "rows"), (jax.ShapeDtypeStruct((8, cells), jnp.float32), "whole")],
    )
    heat_flux = line.add_up(flux[:2]) / jnp.sqrt(jnp.float32(total_modes))
    blocks, sum_a = line.run(mid_b, mine, other)
    (last_b,) = whole_product(scatter_matrix, blocks, line.order, end_b, step)
    updated = jnp.concatenate([end_a - step * sum_a, last_b], axis=1)
    return (updated, heat_flux)


def solution(mesh):
    return jax.shard_map(
        on_device,
        mesh=mesh,
        in_specs=(P("mode", "space"), P(None, "mode"), P(None, "mode"), P("mode"), P("space")),
        out_specs=(P("mode", "space"), P(None, "space")),
        check_vma=False,
    )
```

time: 243 us -> 224 us (0.922)
  matrix products: 67.9 us -> 0 us
  starting transfers between devices: 11.8 us -> 71.6 us
  Pallas kernels: 0 us -> 55.2 us
  blocking collectives: 25 us -> 0 us
  waiting for transfers between devices: 83.8 us -> 61.1 us
  between operations: 14 us -> 1.16 us
  other arithmetic: 30.5 us -> 18.5 us
  local copies, waits for them, and re-layouts: 5.06 us -> 13.9 us
    reduce_scatter x2 -> x0, waiting for transfers between devices: 68.8 us -> none  [by_scatter(): return lax.psum_scatter(terms, 'mode', scatter_dimension=0, tiled=True)]
    dot_general x7 -> x0, matrix products: 67.9 us -> none  [the longest x5 63.6 us: dot_halves(): lax.dot_general(matrix, split_two(value), (((contract,), (0,)), ((), ()))...]
    ppermute x4 -> x36, starting transfers between devices: 11.5 us -> 71.6 us  [the longest x16 44.6 us: along(): return lax.ppermute(value, 'mode', self.streams[stream])]
    ppermute x4 -> x36, waiting for transfers between devices: 4.3 us -> 61.1 us  [the longest x16 56.8 us: along(): return lax.ppermute(value, 'mode', self.streams[stream])]
    pallas_call x0 -> x6, Pallas kernels: none -> 55.2 us  [the longest x2 23.4 us: whole_product(): pl.pallas_call(functools.partial(gather_kernel, scale, slots), out_shape=...]
    all_gather x2 -> x0, blocking collectives: 25 us -> none  [the longest x1 13.1 us: on_device(): all_weights = lax.all_gather(weights, 'mode', axis=1, tiled=True)]
    all_gather x2 -> x0, waiting for transfers between devices: 10.6 us -> none  [by_gather(): whole = lax.all_gather(value, 'mode', axis=0, tiled=True)]
    convert_element_type x5 -> x0, other arithmetic: 9 us -> none  [the longest x4 8.95 us: split_two(): high.astype(jnp.bfloat16)]
  transfers between devices with their start and end apart: 8 -> 36, of which waited for: 5 -> 15; matrix products, arithmetic and copies ran while one was open for 36% -> 9% of each run, Pallas kernels for 0% -> 6%
where the time goes in v2:
time: 224 us; the launch traced here: 221 us
  starting transfers between devices  71.6 us (32%)
  waiting for transfers between devices  61.1 us (27%)
  Pallas kernels  55.2 us (25%)
  other arithmetic  18.5 us (8%)
  local copies, waits for them, and re-layouts  13.9 us (6%)
    ppermute x16, waiting for transfers between devices, along(): return lax.ppermute(value, 'mode', self.streams[stream])  56.8 us
    ppermute x16, starting transfers between devices, along(): return lax.ppermute(value, 'mode', self.streams[stream])  44.6 us
    pallas_call x2, Pallas kernels, whole_product(): pl.pallas_call(functools.partial(gather_kernel, scale, slots), out_shape=...  23.4 us
    pallas_call x2, Pallas kernels, partial_products(): pl.pallas_call(scatter_kernel, out_shape=(out, out), grid_spec=pltpu.Pref...  19.6 us
    add x6, other arithmetic, run(): payload = arrived[stream][-1] + jnp.where(place < step, added, 0.0)  13.5 us
    pallas_call x2, Pallas kernels, stencil_call(): pl.pallas_call(kernel, out_shape=[shape for shape, _ in outs], grid=(mode...  12.2 us
    ppermute x10, starting transfers between devices, exchange(): return lax.ppermute(value, 'mode', self.pairs)  11.8 us
    unnamed x34, local copies, waits for them, and re-layouts  6.46 us
  transfers between devices with their start and end apart: 36, of which 15 were waited for; matrix products, arithmetic and copies ran while one was open for 9% of the time, Pallas kernels for 6%

profile of v2, /device:TPU:13, one launch (start us, length us, event | category | flops | bytes accessed | tf_op | source)
XLA Modules:
  0.0 221.5 jit_solution(8525508977840616249)
XLA Ops:
  0.6 2.2 %fusion.7 = (f32[1024,128]{1,0:T(8,128)}, f32[1024,128]{1,0:T(8,128)}) fusion(f32[1024,256]{1,0:T(8,128)} %field.3), kind=kLoop, calls=%fused_computation.45 | loop fusion | bytes 2097152 | tf_op jit(solution)/shard_map/slice | solution.py:358
  2.9 1.0 copy-done.6
  3.9 9.8 %partial_products.2 = (f32[4,1024,128]{2,1,0:T(8,128)S(1)}, f32[4,1024,128]{2,1,0:T(8,128)}) custom-call(s32[1]{0:T(128)} %bitcast.5.core_ref, bf16[8192,1024]{1,0:T(8,128)(2,1)} %rows.3, bf16[8192,1024]{1,0:T(8,128)(2,1)} %rows.3, f32[1024,128]{1,0:T(8,128)S(1)} %copy-done.6), custom_call_target="tpu_custom_call" | custom-call | flops 4294967296 | bytes 20971520 | tf_op jit(solution)/shard_map/partial_products/pallas_call | solution.py:45
  14.3 3.2 %collective-permute-start.3 = (f32[1024,128]{1,0:T(8,128)}, f32[1024,128]{1,0:T(8,128)}, u32[]{:S(2)}, u32[]{:S(2)}) collective-permute-start(f32[1024,128]{1,0:T(8,128)} %get-tuple-element.43.refs_0_), channel_id=1, source_target_pairs={{1,3},{3,5},{5,7},{2,0},{4,2},{6,4},{9,11},{11,13},{13,15},{10,8},... | collective-permute-start | bytes 1572872 | tf_op jit(solution)/shard_map/ppermute | solution.py:278
  17.5 2.9 %collective-permute-start.2 = (f32[1024,128]{1,0:T(8,128)}, f32[1024,128]{1,0:T(8,128)}, u32[]{:S(2)}, u32[]{:S(2)}) collective-permute-start(f32[1024,128]{1,0:T(8,128)} %get-tuple-element.43.refs_0_), channel_id=1, source_target_pairs={{0,2},{2,4},{4,6},{3,1},{5,3},{7,5},{8,10},{10,12},{12,14},{11,9},... | collective-permute-start | bytes 1572872 | tf_op jit(solution)/shard_map/ppermute | solution.py:278
  21.2 1.1 fusion.8
  23.0 1.2 copy.12
  24.2 1.2 copy.13
  25.5 3.1 %collective-permute-start = (f32[32,1024]{1,0:T(8,128)S(1)}, f32[32,1024]{1,0:T(8,128)S(1)}, u32[]{:S(2)}, u32[]{:S(2)}) collective-permute-start(f32[32,1024]{1,0:T(8,128)S(1)} %bitcast.50), channel_id=1, source_target_pairs={{0,8},{8,16},{16,24},{1,9},{9,17},{17,25},{2,10},{10,18},{18,26},{... | collective-permute-start | bytes 393224 | tf_op jit(solution)/shard_map/ppermute | solution.py:231
  28.6 3.1 %collective-permute-start.1 = (f32[32,1024]{1,0:T(8,128)S(1)}, f32[32,1024]{1,0:T(8,128)S(1)}, u32[]{:S(2)}, u32[]{:S(2)}) collective-permute-start(f32[32,1024]{1,0:T(8,128)S(1)} %bitcast.49), channel_id=1, source_target_pairs={{8,0},{16,8},{24,16},{9,1},{17,9},{25,17},{10,2},{18,10},{26,18},{... | collective-permute-start | bytes 393224 | tf_op jit(solution)/shard_map/ppermute | solution.py:232
  32.0 1.7 bitcast_add_fusion.12
  33.7 3.2 %collective-permute-start.5 = (f32[1024,128]{1,0:T(8,128)S(1)}, f32[1024,128]{1,0:T(8,128)S(1)}, u32[]{:S(2)}, u32[]{:S(2)}) collective-permute-start(f32[1024,128]{1,0:T(8,128)S(1)} %get-tuple-element.35), channel_id=1, source_target_pairs={{0,2},{2,4},{4,6},{3,1},{5,3},{7,5},{8,10},{10,12},{12,14},{11,9},... | collective-permute-start | bytes 1572872 | tf_op jit(solution)/shard_map/ppermute | solution.py:278
  36.9 3.0 %collective-permute-start.6 = (f32[1024,128]{1,0:T(8,128)S(1)}, f32[1024,128]{1,0:T(8,128)S(1)}, u32[]{:S(2)}, u32[]{:S(2)}) collective-permute-start(f32[1024,128]{1,0:T(8,128)S(1)} %get-tuple-element.34), channel_id=1, source_target_pairs={{1,3},{3,5},{5,7},{2,0},{4,2},{6,4},{9,11},{11,13},{13,15},{10,8},... | collective-permute-start | bytes 1572872 | tf_op jit(solution)/shard_map/ppermute | solution.py:278
  39.9 5.4 %collective-permute-done.5 = f32[1024,128]{1,0:T(8,128)S(1)} collective-permute-done((f32[1024,128]{1,0:T(8,128)S(1)}, f32[1024,128]{1,0:T(8,128)S(1)}, u32[]{:S(2)}, u32[]{:S(2)}) %collective-permute-start.5) | collective-permute-done | bytes 524320 | tf_op jit(solution)/shard_map/ppermute | solution.py:278
  45.4 1.1 collective-permute-start.15
  46.5 4.9 %collective-permute-done.6 = f32[1024,128]{1,0:T(8,128)S(1)} collective-permute-done((f32[1024,128]{1,0:T(8,128)S(1)}, f32[1024,128]{1,0:T(8,128)S(1)}, u32[]{:S(2)}, u32[]{:S(2)}) %collective-permute-start.6) | collective-permute-done | bytes 524320 | tf_op jit(solution)/shard_map/ppermute | solution.py:278
  51.3 1.5 bitcast_add_fusion.10
  52.9 1.9 collective-permute-start.7
  54.8 3.8 %collective-permute-start.8 = (f32[1024,128]{1,0:T(8,128)S(1)}, f32[1024,128]{1,0:T(8,128)S(1)}, u32[]{:S(2)}, u32[]{:S(2)}) collective-permute-start(f32[1024,128]{1,0:T(8,128)S(1)} %get-tuple-element.32), channel_id=1, source_target_pairs={{1,3},{3,5},{5,7},{2,0},{4,2},{6,4},{9,11},{11,13},{13,15},{10,8},... | collective-permute-start | bytes 1572872 | tf_op jit(solution)/shard_map/ppermute | solution.py:278
  58.7 6.2 %collective-permute-done.7 = f32[1024,128]{1,0:T(8,128)S(1)} collective-permute-done((f32[1024,128]{1,0:T(8,128)S(1)}, f32[1024,128]{1,0:T(8,128)S(1)}, u32[]{:S(2)}, u32[]{:S(2)}) %collective-permute-start.7) | collective-permute-done | bytes 524320 | tf_op jit(solution)/shard_map/ppermute | solution.py:278
  64.9 6.2 %collective-permute-start.10 = (f32[1024,128]{1,0:T(8,128)S(1)}, f32[1024,128]{1,0:T(8,128)S(1)}, u32[]{:S(2)}, u32[]{:S(2)}) collective-permute-start(f32[1024,128]{1,0:T(8,128)S(1)} %get-tuple-element.36.refs_1_), channel_id=1, source_target_pairs={{0,1},{1,0},{2,3},{3,2},{4,5},{5,4},{6,7},{7,6},{8,9},{9,8},{10,11... | collective-permute-start | bytes 1572872 | tf_op jit(solution)/shard_map/ppermute | solution.py:275
  71.1 2.4 %bitcast_add_fusion.8 = (f32[1024,128]{1,0:T(8,128)}, f32[1024,128]{1,0:T(8,128)}, f32[1024,128]{1,0:T(8,128)S(1)}) fusion(f32[1024,128]{1,0:T(8,128)S(1)} %collective-permute-done.8, f32[4,1024,128]{2,1,0:T(8,128)} %collective-permute-done.4, s32[]{:T(128)S(6)} %min.30, f32[4,1024,128]{2,1,0:T(8,128)S(1)} %get-tuple-element.14, pred[]{:T(512)S(6)} %lt.81, ...), kind=kLoop, calls=%fused_computation.20 | loop fusion | flops 1179648 | bytes 5767181 | tf_op jit(solution)/shard_map/add | solution.py:313
  74.1 5.6 %stencil.2 = (f32[1024,128]{1,0:T(8,128)S(1)}, f32[1024,128]{1,0:T(8,128)S(1)}) custom-call(f32[1024,256]{1,0:T(8,128)S(1)} %copy-done, f32[32,1024]{1,0:T(8,128)S(1)} %collective-permute-done.before, f32[32,1024]{1,0:T(8,128)S(1)} %collective-permute-done.1.after, f32[8,1024]{1,0:T(8,128)S(1)} %maximum_maximum_fusion.table, s32[1,256]{1,0:T(1,128)S(1)} %bitcast.47), custom_call_target="tpu_custom_call" | custom-call | flops 10485760 | bytes 3145728 | tf_op jit(solution)/shard_map/stencil/pallas_call | solution.py:213
  80.5 11.9 %whole_product.2 = (f32[1024,128]{1,0:T(8,128)S(1)}, f32[8,1024]{1,0:T(8,128)S(1)}) custom-call(s32[8]{0:T(128)S(1)} %fusion.6.order_ref, bf16[8192,1024]{1,0:T(8,128)(2,1)} %rows.3, f32[1024,128]{1,0:T(8,128)S(1)} %get-tuple-element.13.base, f32[1024,128]{1,0:T(8,128)} %get-tuple-element.43.refs_0_, f32[1024,128]{1,0:T(8,128)S(1)} %get-tuple-element.36.refs_1_, ...), custom_call_target="tpu_custom_call" | custom-call | flops 4294967296 | bytes 20971520 | tf_op jit(solution)/shard_map/whole_product/pallas_call | solution.py:117
  92.5 9.9 %partial_products.3 = (f32[4,1024,128]{2,1,0:T(8,128)S(1)}, f32[4,1024,128]{2,1,0:T(8,128)}) custom-call(s32[1]{0:T(128)} %bitcast.5.core_ref, bf16[8192,1024]{1,0:T(8,128)(2,1)} %rows.3, bf16[8192,1024]{1,0:T(8,128)(2,1)} %rows.3, f32[1024,128]{1,0:T(8,128)S(1)} %get-tuple-element.16.mid_a.field), custom_call_target="tpu_custom_call" | custom-call | flops 4294967296 | bytes 20971520 | tf_op jit(solution)/shard_map/partial_products/pallas_call | solution.py:45
  102.3 1.3 copy-done.2
  103.7 1.9 collective-permute-start.16
  105.6 3.4 %collective-permute-start.17 = (f32[1024,128]{1,0:T(8,128)}, f32[1024,128]{1,0:T(8,128)S(1)}, u32[]{:S(2)}, u32[]{:S(2)}) collective-permute-start(f32[1024,128]{1,0:T(8,128)} %get-tuple-element.30), channel_id=1, source_target_pairs={{1,3},{3,5},{5,7},{2,0},{4,2},{6,4},{9,11},{11,13},{13,15},{10,8},... | collective-permute-start | bytes 1572872 | tf_op jit(solution)/shard_map/ppermute | solution.py:278
  109.0 7.7 %collective-permute-done.16 = f32[1024,128]{1,0:T(8,128)S(1)} collective-permute-done((f32[1024,128]{1,0:T(8,128)}, f32[1024,128]{1,0:T(8,128)S(1)}, u32[]{:S(2)}, u32[]{:S(2)}) %collective-permute-start.16) | collective-permute-done | bytes 524320 | tf_op jit(solution)/shard_map/ppermute | solution.py:278
  116.7 3.7 %collective-permute-done.17 = f32[1024,128]{1,0:T(8,128)S(1)} collective-permute-done((f32[1024,128]{1,0:T(8,128)}, f32[1024,128]{1,0:T(8,128)S(1)}, u32[]{:S(2)}, u32[]{:S(2)}) %collective-permute-start.17) | collective-permute-done | bytes 524320 | tf_op jit(solution)/shard_map/ppermute | solution.py:278
  121.2 1.5 fusion.5.mid_b.refs_0_
  122.7 1.9 collective-permute-start.20
  124.7 3.4 %collective-permute-start.25 = (f32[1024,128]{1,0:T(8,128)S(1)}, f32[1024,128]{1,0:T(8,128)S(1)}, u32[]{:S(2)}, u32[]{:S(2)}) collective-permute-start(f32[1024,128]{1,0:T(8,128)S(1)} %fusion.5.mid_b.refs_0_), channel_id=1, source_target_pairs={{1,3},{3,5},{5,7},{2,0},{4,2},{6,4},{9,11},{11,13},{13,15},{10,8},... | collective-permute-start | bytes 1572872 | tf_op jit(solution)/shard_map/ppermute | solution.py:278
  128.0 8.1 %collective-permute-done.20 = f32[1024,128]{1,0:T(8,128)S(1)} collective-permute-done((f32[1024,128]{1,0:T(8,128)S(1)}, f32[1024,128]{1,0:T(8,128)S(1)}, u32[]{:S(2)}, u32[]{:S(2)}) %collective-permute-start.20) | collective-permute-done | bytes 524320 | tf_op jit(solution)/shard_map/ppermute | solution.py:278
  136.1 2.4 %collective-permute-done.25 = f32[1024,128]{1,0:T(8,128)S(1)} collective-permute-done((f32[1024,128]{1,0:T(8,128)S(1)}, f32[1024,128]{1,0:T(8,128)S(1)}, u32[]{:S(2)}, u32[]{:S(2)}) %collective-permute-start.25) | collective-permute-done | bytes 524320 | tf_op jit(solution)/shard_map/ppermute | solution.py:278
  138.6 2.2 %bitcast_add_fusion.3 = (f32[1024,128]{1,0:T(8,128)S(1)}, f32[1024,128]{1,0:T(8,128)S(1)}, f32[1024,128]{1,0:T(8,128)}) fusion(f32[1024,128]{1,0:T(8,128)S(1)} %collective-permute-done.25, f32[4,1024,128]{2,1,0:T(8,128)} %collective-permute-done.21, s32[]{:T(128)S(6)} %min.26, f32[4,1024,128]{2,1,0:T(8,128)S(1)} %copy-done.3, pred[]{:T(512)S(6)} %lt.75, ...), kind=kLoop, calls=%fused_computation.13 | loop fusion | flops 1179648 | bytes 4718605 | tf_op jit(solution)/shard_map/add | solution.py:313
  140.8 1.9 collective-permute-start.22
  142.7 3.7 %collective-permute-start.26 = (f32[1024,128]{1,0:T(8,128)S(1)}, f32[1024,128]{1,0:T(8,128)S(1)}, u32[]{:S(2)}, u32[]{:S(2)}) collective-permute-start(f32[1024,128]{1,0:T(8,128)S(1)} %get-tuple-element.28), channel_id=1, source_target_pairs={{1,3},{3,5},{5,7},{2,0},{4,2},{6,4},{9,11},{11,13},{13,15},{10,8},... | collective-permute-start | bytes 1572872 | tf_op jit(solution)/shard_map/ppermute | solution.py:278
  146.4 7.1 %collective-permute-done.22 = f32[1024,128]{1,0:T(8,128)S(1)} collective-permute-done((f32[1024,128]{1,0:T(8,128)S(1)}, f32[1024,128]{1,0:T(8,128)S(1)}, u32[]{:S(2)}, u32[]{:S(2)}) %collective-permute-start.22) | collective-permute-done | bytes 524320 | tf_op jit(solution)/shard_map/ppermute | solution.py:278
  153.5 3.7 %collective-permute-done.26 = f32[1024,128]{1,0:T(8,128)S(1)} collective-permute-done((f32[1024,128]{1,0:T(8,128)S(1)}, f32[1024,128]{1,0:T(8,128)S(1)}, u32[]{:S(2)}, u32[]{:S(2)}) %collective-permute-start.26) | collective-permute-done | bytes 524320 | tf_op jit(solution)/shard_map/ppermute | solution.py:278
  157.2 2.5 %bitcast_add_fusion.2 = (f32[1024,128]{1,0:T(8,128)}, f32[1024,128]{1,0:T(8,128)}, f32[1024,128]{1,0:T(8,128)}) fusion(f32[1024,128]{1,0:T(8,128)S(1)} %collective-permute-done.26, f32[4,1024,128]{2,1,0:T(8,128)} %collective-permute-done.21, s32[]{:T(128)S(6)} %min.28, f32[4,1024,128]{2,1,0:T(8,128)S(1)} %copy-done.3, pred[]{:T(512)S(6)} %lt.77, ...), kind=kLoop, calls=%fused_computation.12 | loop fusion | flops 1179648 | bytes 5242893 | tf_op jit(solution)/shard_map/add | solution.py:313
  159.7 1.9 collective-permute-start.23
  161.6 3.4 %collective-permute-start.27 = (f32[1024,128]{1,0:T(8,128)}, f32[1024,128]{1,0:T(8,128)}, u32[]{:S(2)}, u32[]{:S(2)}) collective-permute-start(f32[1024,128]{1,0:T(8,128)} %get-tuple-element.26), channel_id=1, source_target_pairs={{1,3},{3,5},{5,7},{2,0},{4,2},{6,4},{9,11},{11,13},{13,15},{10,8},... | collective-permute-start | bytes 1572872 | tf_op jit(solution)/shard_map/ppermute | solution.py:278
  165.0 1.0 copy.10
  166.2 2.2 %collective-permute-start.18 = (f32[32,1024]{0,1:T(8,128)S(1)}, f32[32,1024]{0,1:T(8,128)}, u32[]{:S(2)}, u32[]{:S(2)}) collective-permute-start(f32[32,1024]{0,1:T(8,128)S(1)} %slice_bitcast_fusion), channel_id=1, source_target_pairs={{0,8},{8,16},{16,24},{1,9},{9,17},{17,25},{2,10},{10,18},{18,26},{... | collective-permute-start | bytes 393224 | tf_op jit(solution)/shard_map/ppermute | solution.py:231
  168.4 5.0 %collective-permute-done.23 = f32[1024,128]{1,0:T(8,128)} collective-permute-done((f32[1024,128]{1,0:T(8,128)}, f32[1024,128]{1,0:T(8,128)}, u32[]{:S(2)}, u32[]{:S(2)}) %collective-permute-start.23) | collective-permute-done | bytes 524320 | tf_op jit(solution)/shard_map/ppermute | solution.py:278
  173.4 2.7 %collective-permute-done.27 = f32[1024,128]{1,0:T(8,128)} collective-permute-done((f32[1024,128]{1,0:T(8,128)}, f32[1024,128]{1,0:T(8,128)}, u32[]{:S(2)}, u32[]{:S(2)}) %collective-permute-start.27) | collective-permute-done | bytes 524320 | tf_op jit(solution)/shard_map/ppermute | solution.py:278
  176.1 3.1 %bitcast_add_fusion.1 = (f32[1024,128]{1,0:T(8,128)}, f32[1024,128]{1,0:T(8,128)}, f32[1024,128]{1,0:T(8,128)}) fusion(f32[1024,128]{1,0:T(8,128)} %collective-permute-done.27, f32[4,1024,128]{2,1,0:T(8,128)} %collective-permute-done.21, s32[]{:T(128)S(6)} %min.30, f32[4,1024,128]{2,1,0:T(8,128)} %copy-done.2, pred[]{:T(512)S(6)} %lt.81, ...), kind=kLoop, calls=%fused_computation.11 | loop fusion | flops 1179648 | bytes 5767181 | tf_op jit(solution)/shard_map/add | solution.py:313
  179.3 1.9 collective-permute-start.24
  181.2 0.9 slice_bitcast_fusion.1
  182.1 2.2 collective-permute-start.19
  184.3 3.4 %collective-permute-start.28 = (f32[1024,128]{1,0:T(8,128)}, f32[1024,128]{1,0:T(8,128)}, u32[]{:S(2)}, u32[]{:S(2)}) collective-permute-start(f32[1024,128]{1,0:T(8,128)} %get-tuple-element.24), channel_id=1, source_target_pairs={{1,3},{3,5},{5,7},{2,0},{4,2},{6,4},{9,11},{11,13},{13,15},{10,8},... | collective-permute-start | bytes 1572872 | tf_op jit(solution)/shard_map/ppermute | solution.py:278
  187.7 1.2 copy.11.before
  189.0 6.6 %stencil.3 = (f32[1024,128]{1,0:T(8,128)S(1)}, f32[1024,128]{1,0:T(8,128)S(1)}, f32[8,256]{1,0:T(8,128)S(1)}) custom-call(f32[1024,256]{1,0:T(8,128)S(1)} %copy-done, f32[1024,128]{1,0:T(8,128)S(1)} %copy-done.5, f32[1024,128]{1,0:T(8,128)S(1)} %fusion.5.mid_b.refs_0_, f32[32,1024]{1,0:T(8,128)S(1)} %copy.11.before, ...), custom_call_target="tpu_custom_call" | custom-call | flops 10485760 | bytes 3145728 | tf_op jit(solution)/shard_map/stencil/pallas_call | solution.py:213
  195.6 1.8 collective-permute-start.33
  197.4 0.8 collective-permute-done.33
  198.2 0.9 collective-permute-start.34
  199.1 1.5 collective-permute-done.34
  200.6 1.5 collective-permute-start.29
  202.2 1.8 collective-permute-done.35
  204.0 2.6 %collective-permute-start.31 = (f32[1024,128]{1,0:T(8,128)}, f32[1024,128]{1,0:T(8,128)S(1)}, u32[]{:S(2)}, u32[]{:S(2)}) collective-permute-start(f32[1024,128]{1,0:T(8,128)} %get-tuple-element.40.refs_2_), channel_id=1, source_target_pairs={{0,1},{1,0},{2,3},{3,2},{4,5},{5,4},{6,7},{7,6},{8,9},{9,8},{10,11... | collective-permute-start | bytes 1572872 | tf_op jit(solution)/shard_map/ppermute | solution.py:275
  207.3 1.6 fusion.3
  209.0 11.5 %whole_product.3 = f32[1024,128]{1,0:T(8,128)S(1)} custom-call(s32[8]{0:T(128)S(1)} %fusion.6.order_ref, bf16[8192,1024]{1,0:T(8,128)(2,1)} %rows.3, f32[1024,128]{1,0:T(8,128)S(1)} %get-tuple-element.22.base, f32[1024,128]{1,0:T(8,128)S(1)} %fusion.5.mid_b.refs_0_, f32[1024,128]{1,0:T(8,128)S(1)} %copy-done.7, f32[1024,128]{1,0:T(8,128)S(1)} %copy-done.9, ...), custom_call_target="tpu_custom_call" | custom-call | flops 4294967296 | bytes 20971520 | tf_op jit(solution)/shard_map/whole_product/pallas_call | solution.py:117
  220.4 1.0 pad_maximum_fusion
  (78 shorter events, 5.8 us)
Async XLA Ops:
  2.9 1.0 copy-start.6
  3.9 16.6 %copy-start.14 = (f32[2,1024]{1,0:T(2,128)S(1)}, f32[2,1024]{1,0:T(2,128)}, u32[]{:S(2)}) copy-start(f32[2,1024]{1,0:T(2,128)} %param.8) | copy-start | bytes 24580
  3.9 16.6 %copy-start.15 = (f32[1024]{0:T(1024)S(1)}, f32[1024]{0:T(1024)}, u32[]{:S(2)}) copy-start(f32[1024]{0:T(1024)} %param.9) | copy-start | bytes 12292
  3.9 17.3 %copy-start = (f32[1024,256]{1,0:T(8,128)S(1)}, f32[1024,256]{1,0:T(8,128)}, u32[]{:S(2)}) copy-start(f32[1024,256]{1,0:T(8,128)} %field.3) | copy-start | bytes 3145732
  13.7 57.5 %copy-start.1 = (f32[4,1024,128]{2,1,0:T(8,128)}, f32[4,1024,128]{2,1,0:T(8,128)S(1)}, u32[]{:S(2)}) copy-start(f32[4,1024,128]{2,1,0:T(8,128)S(1)} %get-tuple-element.14) | copy-start | bytes 6291460
  13.7 18.3 %collective-permute-start.4 = (f32[4,1024,128]{2,1,0:T(8,128)}, f32[4,1024,128]{2,1,0:T(8,128)}, u32[]{:S(2)}, u32[]{:S(2)}) collective-permute-start(f32[4,1024,128]{2,1,0:T(8,128)} %get-tuple-element.15), channel_id=1, source_target_pairs={{0,1},{1,0},{2,3},{3,2},{4,5},{5,4},{6,7},{7,6},{8,9},{9,8},{10,11... | collective-permute-start | bytes 6291464 | tf_op jit(solution)/shard_map/ppermute | solution.py:275
  14.3 14.3 %collective-permute-start.3 = (f32[1024,128]{1,0:T(8,128)}, f32[1024,128]{1,0:T(8,128)}, u32[]{:S(2)}, u32[]{:S(2)}) collective-permute-start(f32[1024,128]{1,0:T(8,128)} %get-tuple-element.43.refs_0_), channel_id=1, source_target_pairs={{1,3},{3,5},{5,7},{2,0},{4,2},{6,4},{9,11},{11,13},{13,15},{10,8},... | collective-permute-start | bytes 1572872 | tf_op jit(solution)/shard_map/ppermute | solution.py:278
  17.5 14.2 %collective-permute-start.2 = (f32[1024,128]{1,0:T(8,128)}, f32[1024,128]{1,0:T(8,128)}, u32[]{:S(2)}, u32[]{:S(2)}) collective-permute-start(f32[1024,128]{1,0:T(8,128)} %get-tuple-element.43.refs_0_), channel_id=1, source_target_pairs={{0,2},{2,4},{4,6},{3,1},{5,3},{7,5},{8,10},{10,12},{12,14},{11,9},... | collective-permute-start | bytes 1572872 | tf_op jit(solution)/shard_map/ppermute | solution.py:278
  20.4 60.1 %collective-permute-start.9 = (f32[1024,128]{1,0:T(8,128)}, f32[1024,128]{1,0:T(8,128)}, u32[]{:S(2)}, u32[]{:S(2)}) collective-permute-start(f32[1024,128]{1,0:T(8,128)} %get-tuple-element.43.refs_0_), channel_id=1, source_target_pairs={{0,1},{1,0},{2,3},{3,2},{4,5},{5,4},{6,7},{7,6},{8,9},{9,8},{10,11... | collective-permute-start | bytes 1572872 | tf_op jit(solution)/shard_map/ppermute | solution.py:275
  20.5 4.9 %collective-permute-start.13 = (f32[2,1024]{1,0:T(2,128)S(1)}, f32[2,1024]{1,0:T(2,128)S(1)}, u32[]{:S(2)}, u32[]{:S(2)}) collective-permute-start(f32[2,1024]{1,0:T(2,128)S(1)} %broadcast_multiply_fusion), channel_id=1, source_target_pairs={{0,1},{1,0},{2,3},{3,2},{4,5},{5,4},{6,7},{7,6},{8,9},{9,8},{10,11... | collective-permute-start | bytes 24584 | tf_op jit(solution)/shard_map/ppermute | solution.py:327
  25.5 48.1 %collective-permute-start = (f32[32,1024]{1,0:T(8,128)S(1)}, f32[32,1024]{1,0:T(8,128)S(1)}, u32[]{:S(2)}, u32[]{:S(2)}) collective-permute-start(f32[32,1024]{1,0:T(8,128)S(1)} %bitcast.50), channel_id=1, source_target_pairs={{0,8},{8,16},{16,24},{1,9},{9,17},{17,25},{2,10},{10,18},{18,26},{... | collective-permute-start | bytes 393224 | tf_op jit(solution)/shard_map/ppermute | solution.py:231
  28.6 45.4 %collective-permute-start.1 = (f32[32,1024]{1,0:T(8,128)S(1)}, f32[32,1024]{1,0:T(8,128)S(1)}, u32[]{:S(2)}, u32[]{:S(2)}) collective-permute-start(f32[32,1024]{1,0:T(8,128)S(1)} %bitcast.49), channel_id=1, source_target_pairs={{8,0},{16,8},{24,16},{9,1},{17,9},{25,17},{10,2},{18,10},{26,18},{... | collective-permute-start | bytes 393224 | tf_op jit(solution)/shard_map/ppermute | solution.py:232
  31.7 5.1 %collective-permute-start.14 = (f32[2,2048]{1,0:T(2,128)S(1)}, f32[2,2048]{1,0:T(2,128)S(1)}, u32[]{:S(2)}, u32[]{:S(2)}) collective-permute-start(f32[2,2048]{1,0:T(2,128)S(1)} %pad_maximum_fusion.2), channel_id=1, source_target_pairs={{0,2},{1,3},{2,0},{3,1},{4,6},{5,7},{6,4},{7,5},{8,10},{9,11},{10,... | collective-permute-start | bytes 49160 | tf_op jit(solution)/shard_map/ppermute | solution.py:327
  33.7 11.7 %collective-permute-start.5 = (f32[1024,128]{1,0:T(8,128)S(1)}, f32[1024,128]{1,0:T(8,128)S(1)}, u32[]{:S(2)}, u32[]{:S(2)}) collective-permute-start(f32[1024,128]{1,0:T(8,128)S(1)} %get-tuple-element.35), channel_id=1, source_target_pairs={{0,2},{2,4},{4,6},{3,1},{5,3},{7,5},{8,10},{10,12},{12,14},{11,9},... | collective-permute-start | bytes 1572872 | tf_op jit(solution)/shard_map/ppermute | solution.py:278
  36.9 14.5 %collective-permute-start.6 = (f32[1024,128]{1,0:T(8,128)S(1)}, f32[1024,128]{1,0:T(8,128)S(1)}, u32[]{:S(2)}, u32[]{:S(2)}) collective-permute-start(f32[1024,128]{1,0:T(8,128)S(1)} %get-tuple-element.34), channel_id=1, source_target_pairs={{1,3},{3,5},{5,7},{2,0},{4,2},{6,4},{9,11},{11,13},{13,15},{10,8},... | collective-permute-start | bytes 1572872 | tf_op jit(solution)/shard_map/ppermute | solution.py:278
  45.4 9.4 %collective-permute-start.15 = (f32[2,4096]{1,0:T(2,128)S(1)}, f32[2,4096]{1,0:T(2,128)S(1)}, u32[]{:S(2)}, u32[]{:S(2)}) collective-permute-start(f32[2,4096]{1,0:T(2,128)S(1)} %pad_maximum_fusion.1), channel_id=1, source_target_pairs={{0,4},{1,5},{2,6},{3,7},{4,0},{5,1},{6,2},{7,3},{8,12},{9,13},{10,... | collective-permute-start | bytes 98312 | tf_op jit(solution)/shard_map/ppermute | solution.py:327
  52.9 12.0 %collective-permute-start.7 = (f32[1024,128]{1,0:T(8,128)S(1)}, f32[1024,128]{1,0:T(8,128)S(1)}, u32[]{:S(2)}, u32[]{:S(2)}) collective-permute-start(f32[1024,128]{1,0:T(8,128)S(1)} %get-tuple-element.33), channel_id=1, source_target_pairs={{0,2},{2,4},{4,6},{3,1},{5,3},{7,5},{8,10},{10,12},{12,14},{11,9},... | collective-permute-start | bytes 1572872 | tf_op jit(solution)/shard_map/ppermute | solution.py:278
  54.8 16.2 %collective-permute-start.8 = (f32[1024,128]{1,0:T(8,128)S(1)}, f32[1024,128]{1,0:T(8,128)S(1)}, u32[]{:S(2)}, u32[]{:S(2)}) collective-permute-start(f32[1024,128]{1,0:T(8,128)S(1)} %get-tuple-element.32), channel_id=1, source_target_pairs={{1,3},{3,5},{5,7},{2,0},{4,2},{6,4},{9,11},{11,13},{13,15},{10,8},... | collective-permute-start | bytes 1572872 | tf_op jit(solution)/shard_map/ppermute | solution.py:278
  64.9 15.7 %collective-permute-start.10 = (f32[1024,128]{1,0:T(8,128)S(1)}, f32[1024,128]{1,0:T(8,128)S(1)}, u32[]{:S(2)}, u32[]{:S(2)}) collective-permute-start(f32[1024,128]{1,0:T(8,128)S(1)} %get-tuple-element.36.refs_1_), channel_id=1, source_target_pairs={{0,1},{1,0},{2,3},{3,2},{4,5},{5,4},{6,7},{7,6},{8,9},{9,8},{10,11... | collective-permute-start | bytes 1572872 | tf_op jit(solution)/shard_map/ppermute | solution.py:275
  71.1 3.0 %copy-start.12 = (s32[256]{0:T(256)S(1)}, s32[256]{0:T(256)}, u32[]{:S(2)}) copy-start(s32[256]{0:T(256)} %param.10) | copy-start | bytes 3076
  71.1 9.5 %collective-permute-start.11 = (f32[1024,128]{1,0:T(8,128)S(1)}, f32[1024,128]{1,0:T(8,128)S(1)}, u32[]{:S(2)}, u32[]{:S(2)}) collective-permute-start(f32[1024,128]{1,0:T(8,128)S(1)} %get-tuple-element.37.refs_2_), channel_id=1, source_target_pairs={{0,1},{1,0},{2,3},{3,2},{4,5},{5,4},{6,7},{7,6},{8,9},{9,8},{10,11... | collective-permute-start | bytes 1572872 | tf_op jit(solution)/shard_map/ppermute | solution.py:275
  73.6 7.0 %collective-permute-start.12 = (f32[1024,128]{1,0:T(8,128)S(1)}, f32[1024,128]{1,0:T(8,128)S(1)}, u32[]{:S(2)}, u32[]{:S(2)}) collective-permute-start(f32[1024,128]{1,0:T(8,128)S(1)} %get-tuple-element.38.refs_3_), channel_id=1, source_target_pairs={{0,1},{1,0},{2,3},{3,2},{4,5},{5,4},{6,7},{7,6},{8,9},{9,8},{10,11... | collective-permute-start | bytes 1572872 | tf_op jit(solution)/shard_map/ppermute | solution.py:275
  79.7 0.8 copy-start.10
  92.4 9.9 %copy-start.4 = (f32[1024,128]{1,0:T(8,128)}, f32[1024,128]{1,0:T(8,128)S(1)}, u32[]{:S(2)}) copy-start(f32[1024,128]{1,0:T(8,128)S(1)} %get-tuple-element.16.mid_a.field) | copy-start | bytes 1572868
  92.4 28.7 %copy-start.11 = (f32[1024,128]{1,0:T(8,128)S(1)}, f32[1024,128]{1,0:T(8,128)}, u32[]{:S(2)}) copy-start(f32[1024,128]{1,0:T(8,128)} %copy-done.10) | copy-start | bytes 1572868
  102.3 1.4 copy-start.2
  103.7 34.9 %collective-permute-start.21 = (f32[4,1024,128]{2,1,0:T(8,128)}, f32[4,1024,128]{2,1,0:T(8,128)}, u32[]{:S(2)}, u32[]{:S(2)}) collective-permute-start(f32[4,1024,128]{2,1,0:T(8,128)} %get-tuple-element.21), channel_id=1, source_target_pairs={{0,1},{1,0},{2,3},{3,2},{4,5},{5,4},{6,7},{7,6},{8,9},{9,8},{10,11... | collective-permute-start | bytes 6291464 | tf_op jit(solution)/shard_map/ppermute | solution.py:275
  103.7 13.0 %collective-permute-start.16 = (f32[1024,128]{1,0:T(8,128)}, f32[1024,128]{1,0:T(8,128)S(1)}, u32[]{:S(2)}, u32[]{:S(2)}) collective-permute-start(f32[1024,128]{1,0:T(8,128)} %get-tuple-element.31), channel_id=1, source_target_pairs={{0,2},{2,4},{4,6},{3,1},{5,3},{7,5},{8,10},{10,12},{12,14},{11,9},... | collective-permute-start | bytes 1572872 | tf_op jit(solution)/shard_map/ppermute | solution.py:278
  105.6 14.7 %collective-permute-start.17 = (f32[1024,128]{1,0:T(8,128)}, f32[1024,128]{1,0:T(8,128)S(1)}, u32[]{:S(2)}, u32[]{:S(2)}) collective-permute-start(f32[1024,128]{1,0:T(8,128)} %get-tuple-element.30), channel_id=1, source_target_pairs={{1,3},{3,5},{5,7},{2,0},{4,2},{6,4},{9,11},{11,13},{13,15},{10,8},... | collective-permute-start | bytes 1572872 | tf_op jit(solution)/shard_map/ppermute | solution.py:278
  109.0 29.5 %copy-start.3 = (f32[4,1024,128]{2,1,0:T(8,128)S(1)}, f32[4,1024,128]{2,1,0:T(8,128)}, u32[]{:S(2)}) copy-start(f32[4,1024,128]{2,1,0:T(8,128)} %copy-done.2) | copy-start | bytes 6291460
  120.4 0.8 copy-start.13
  122.7 13.4 %collective-permute-start.20 = (f32[1024,128]{1,0:T(8,128)S(1)}, f32[1024,128]{1,0:T(8,128)S(1)}, u32[]{:S(2)}, u32[]{:S(2)}) collective-permute-start(f32[1024,128]{1,0:T(8,128)S(1)} %fusion.5.mid_b.refs_0_), channel_id=1, source_target_pairs={{0,2},{2,4},{4,6},{3,1},{5,3},{7,5},{8,10},{10,12},{12,14},{11,9},... | collective-permute-start | bytes 1572872 | tf_op jit(solution)/shard_map/ppermute | solution.py:278
  124.7 13.9 %collective-permute-start.25 = (f32[1024,128]{1,0:T(8,128)S(1)}, f32[1024,128]{1,0:T(8,128)S(1)}, u32[]{:S(2)}, u32[]{:S(2)}) collective-permute-start(f32[1024,128]{1,0:T(8,128)S(1)} %fusion.5.mid_b.refs_0_), channel_id=1, source_target_pairs={{1,3},{3,5},{5,7},{2,0},{4,2},{6,4},{9,11},{11,13},{13,15},{10,8},... | collective-permute-start | bytes 1572872 | tf_op jit(solution)/shard_map/ppermute | solution.py:278
  140.8 12.7 %collective-permute-start.22 = (f32[1024,128]{1,0:T(8,128)S(1)}, f32[1024,128]{1,0:T(8,128)S(1)}, u32[]{:S(2)}, u32[]{:S(2)}) collective-permute-start(f32[1024,128]{1,0:T(8,128)S(1)} %get-tuple-element.29), channel_id=1, source_target_pairs={{0,2},{2,4},{4,6},{3,1},{5,3},{7,5},{8,10},{10,12},{12,14},{11,9},... | collective-permute-start | bytes 1572872 | tf_op jit(solution)/shard_map/ppermute | solution.py:278
  142.7 22.3 %copy-start.5 = (f32[1024,128]{1,0:T(8,128)S(1)}, f32[1024,128]{1,0:T(8,128)}, u32[]{:S(2)}) copy-start(f32[1024,128]{1,0:T(8,128)} %copy-done.4) | copy-start | bytes 1572868
  142.7 14.5 %collective-permute-start.26 = (f32[1024,128]{1,0:T(8,128)S(1)}, f32[1024,128]{1,0:T(8,128)S(1)}, u32[]{:S(2)}, u32[]{:S(2)}) collective-permute-start(f32[1024,128]{1,0:T(8,128)S(1)} %get-tuple-element.28), channel_id=1, source_target_pairs={{1,3},{3,5},{5,7},{2,0},{4,2},{6,4},{9,11},{11,13},{13,15},{10,8},... | collective-permute-start | bytes 1572872 | tf_op jit(solution)/shard_map/ppermute | solution.py:278
  159.7 13.7 %collective-permute-start.23 = (f32[1024,128]{1,0:T(8,128)}, f32[1024,128]{1,0:T(8,128)}, u32[]{:S(2)}, u32[]{:S(2)}) collective-permute-start(f32[1024,128]{1,0:T(8,128)} %get-tuple-element.27), channel_id=1, source_target_pairs={{0,2},{2,4},{4,6},{3,1},{5,3},{7,5},{8,10},{10,12},{12,14},{11,9},... | collective-permute-start | bytes 1572872 | tf_op jit(solution)/shard_map/ppermute | solution.py:278
  161.6 14.5 %collective-permute-start.27 = (f32[1024,128]{1,0:T(8,128)}, f32[1024,128]{1,0:T(8,128)}, u32[]{:S(2)}, u32[]{:S(2)}) collective-permute-start(f32[1024,128]{1,0:T(8,128)} %get-tuple-element.26), channel_id=1, source_target_pairs={{1,3},{3,5},{5,7},{2,0},{4,2},{6,4},{9,11},{11,13},{13,15},{10,8},... | collective-permute-start | bytes 1572872 | tf_op jit(solution)/shard_map/ppermute | solution.py:278
  166.2 21.4 %collective-permute-start.18 = (f32[32,1024]{0,1:T(8,128)S(1)}, f32[32,1024]{0,1:T(8,128)}, u32[]{:S(2)}, u32[]{:S(2)}) collective-permute-start(f32[32,1024]{0,1:T(8,128)S(1)} %slice_bitcast_fusion), channel_id=1, source_target_pairs={{0,8},{8,16},{16,24},{1,9},{9,17},{17,25},{2,10},{10,18},{18,26},{... | collective-permute-start | bytes 393224 | tf_op jit(solution)/shard_map/ppermute | solution.py:231
  179.3 27.4 %collective-permute-start.24 = (f32[1024,128]{1,0:T(8,128)}, f32[1024,128]{1,0:T(8,128)}, u32[]{:S(2)}, u32[]{:S(2)}) collective-permute-start(f32[1024,128]{1,0:T(8,128)} %get-tuple-element.25), channel_id=1, source_target_pairs={{0,2},{2,4},{4,6},{3,1},{5,3},{7,5},{8,10},{10,12},{12,14},{11,9},... | collective-permute-start | bytes 1572872 | tf_op jit(solution)/shard_map/ppermute | solution.py:278
  182.1 6.9 %collective-permute-start.19 = (f32[32,1024]{1,0:T(8,128)S(1)}, f32[32,1024]{1,0:T(8,128)S(1)}, u32[]{:S(2)}, u32[]{:S(2)}) collective-permute-start(f32[32,1024]{1,0:T(8,128)S(1)} %slice_bitcast_fusion.1), channel_id=1, source_target_pairs={{8,0},{16,8},{24,16},{9,1},{17,9},{25,17},{10,2},{18,10},{26,18},{... | collective-permute-start | bytes 393224 | tf_op jit(solution)/shard_map/ppermute | solution.py:232
  184.3 23.0 %collective-permute-start.28 = (f32[1024,128]{1,0:T(8,128)}, f32[1024,128]{1,0:T(8,128)}, u32[]{:S(2)}, u32[]{:S(2)}) collective-permute-start(f32[1024,128]{1,0:T(8,128)} %get-tuple-element.24), channel_id=1, source_target_pairs={{1,3},{3,5},{5,7},{2,0},{4,2},{6,4},{9,11},{11,13},{13,15},{10,8},... | collective-permute-start | bytes 1572872 | tf_op jit(solution)/shard_map/ppermute | solution.py:278
  188.9 17.8 %copy-start.8 = (f32[1024,128]{1,0:T(8,128)S(1)}, f32[1024,128]{1,0:T(8,128)}, u32[]{:S(2)}) copy-start(f32[1024,128]{1,0:T(8,128)} %get-tuple-element.41.refs_3_) | copy-start | bytes 1572868
  195.6 13.4 %copy-start.7 = (f32[1024,128]{1,0:T(8,128)S(1)}, f32[1024,128]{1,0:T(8,128)}, u32[]{:S(2)}) copy-start(f32[1024,128]{1,0:T(8,128)} %get-tuple-element.39.refs_1_) | copy-start | bytes 1572868
  195.6 13.4 %copy-start.9 = (f32[1024,128]{1,0:T(8,128)S(1)}, f32[1024,128]{1,0:T(8,128)}, u32[]{:S(2)}) copy-start(f32[1024,128]{1,0:T(8,128)} %get-tuple-element.40.refs_2_) | copy-start | bytes 1572868
  195.6 2.6 %collective-permute-start.33 = (f32[2,256]{1,0:T(2,128)S(1)}, f32[2,256]{1,0:T(2,128)S(1)}, u32[]{:S(2)}, u32[]{:S(2)}) collective-permute-start(f32[2,256]{1,0:T(2,128)S(1)} %slice.27), channel_id=1, source_target_pairs={{0,1},{1,0},{2,3},{3,2},{4,5},{5,4},{6,7},{7,6},{8,9},{9,8},{10,11... | collective-permute-start | bytes 6152 | tf_op jit(solution)/shard_map/ppermute | solution.py:339
  198.2 2.4 %collective-permute-start.34 = (f32[2,256]{1,0:T(2,128)S(1)}, f32[2,256]{1,0:T(2,128)S(1)}, u32[]{:S(2)}, u32[]{:S(2)}) collective-permute-start(f32[2,256]{1,0:T(2,128)S(1)} %slice_add_fusion), channel_id=1, source_target_pairs={{0,2},{1,3},{2,0},{3,1},{4,6},{5,7},{6,4},{7,5},{8,10},{9,11},{10,... | collective-permute-start | bytes 6152 | tf_op jit(solution)/shard_map/ppermute | solution.py:339
  200.6 3.3 %collective-permute-start.35 = (f32[2,256]{1,0:T(2,128)S(1)}, f32[2,256]{1,0:T(2,128)S(1)}, u32[]{:S(2)}, u32[]{:S(2)}) collective-permute-start(f32[2,256]{1,0:T(2,128)S(1)} %add.233), channel_id=1, source_target_pairs={{0,4},{1,5},{2,6},{3,7},{4,0},{5,1},{6,2},{7,3},{8,12},{9,13},{10,... | collective-permute-start | bytes 6152 | tf_op jit(solution)/shard_map/ppermute | solution.py:339
  200.6 8.3 %collective-permute-start.29 = (f32[1024,128]{1,0:T(8,128)S(1)}, f32[1024,128]{1,0:T(8,128)S(1)}, u32[]{:S(2)}, u32[]{:S(2)}) collective-permute-start(f32[1024,128]{1,0:T(8,128)S(1)} %fusion.5.mid_b.refs_0_), channel_id=1, source_target_pairs={{0,1},{1,0},{2,3},{3,2},{4,5},{5,4},{6,7},{7,6},{8,9},{9,8},{10,11... | collective-permute-start | bytes 1572872 | tf_op jit(solution)/shard_map/ppermute | solution.py:275
  202.1 6.8 %collective-permute-start.30 = (f32[1024,128]{1,0:T(8,128)}, f32[1024,128]{1,0:T(8,128)S(1)}, u32[]{:S(2)}, u32[]{:S(2)}) collective-permute-start(f32[1024,128]{1,0:T(8,128)} %get-tuple-element.39.refs_1_), channel_id=1, source_target_pairs={{0,1},{1,0},{2,3},{3,2},{4,5},{5,4},{6,7},{7,6},{8,9},{9,8},{10,11... | collective-permute-start | bytes 1572872 | tf_op jit(solution)/shard_map/ppermute | solution.py:275
  204.0 5.0 %collective-permute-start.31 = (f32[1024,128]{1,0:T(8,128)}, f32[1024,128]{1,0:T(8,128)S(1)}, u32[]{:S(2)}, u32[]{:S(2)}) collective-permute-start(f32[1024,128]{1,0:T(8,128)} %get-tuple-element.40.refs_2_), channel_id=1, source_target_pairs={{0,1},{1,0},{2,3},{3,2},{4,5},{5,4},{6,7},{7,6},{8,9},{9,8},{10,11... | collective-permute-start | bytes 1572872 | tf_op jit(solution)/shard_map/ppermute | solution.py:275
  206.6 2.3 %collective-permute-start.32 = (f32[1024,128]{1,0:T(8,128)S(1)}, f32[1024,128]{1,0:T(8,128)S(1)}, u32[]{:S(2)}, u32[]{:S(2)}) collective-permute-start(f32[1024,128]{1,0:T(8,128)S(1)} %copy-done.8), channel_id=1, source_target_pairs={{0,1},{1,0},{2,3},{3,2},{4,5},{5,4},{6,7},{7,6},{8,9},{9,8},{10,11... | collective-permute-start | bytes 1572872 | tf_op jit(solution)/shard_map/ppermute | solution.py:275

commit v3 on v0

v3 whole, which is shorter than its diff:
```python
import functools

import numpy as np

import jax
import jax.numpy as jnp
from jax import lax
from jax.experimental import pallas as pl
from jax.experimental.pallas import tpu as pltpu
from jax.sharding import PartitionSpec as P

NY = 16
HALO = 2 * NY
LANES = 128


relax_rate = 0.5
time_step = 0.5

VMEM = pl.BlockSpec(memory_space=pltpu.VMEM)
SMEM = pl.BlockSpec(memory_space=pltpu.SMEM)
ANY = pl.BlockSpec(memory_space=pl.ANY)
HBM = pl.BlockSpec(memory_space=pltpu.HBM)


class Chain:
    def __init__(self):
        self.last = None

    def __call__(self, kernel, outs, arrays, info=None, places=None, scratch=(), out_specs=None):
        scalars = [] if info is None else [info]
        extra = [] if self.last is None else [self.last]
        skip = len(extra)
        first = len(scalars) + len(arrays)

        def body(*refs):
            kernel(*refs[:first], *refs[first + skip :])

        results = pl.pallas_call(
            body,
            out_shape=[jax.ShapeDtypeStruct(shape, jnp.float32) for shape in outs],
            in_specs=[SMEM] * len(scalars)
            + list(places or [VMEM] * len(arrays))
            + [ANY] * skip,
            out_specs=out_specs or [VMEM] * len(outs),
            scratch_shapes=list(scratch),
            compiler_params=pltpu.CompilerParams(vmem_limit_bytes=16 * 1024 * 1024),
            cost_estimate=pl.CostEstimate(flops=1024, bytes_accessed=1024, transcendentals=0),
            name=getattr(kernel, "func", kernel).__name__,
        )(*scalars, *arrays, *extra)
        self.last = results[0]
        return results


def halves(value):
    high = value.astype(jnp.bfloat16)
    low = (value - high.astype(jnp.float32)).astype(jnp.bfloat16)
    return high, low


def slot_products(at, column, info, matrix, field, mine, other):
    modes = matrix.shape[1]
    cells = mine.shape[1]
    parts = jnp.concatenate(halves(field[:, column : column + cells]), axis=1)
    for k, out in ((1, other), (0, mine)):
        start = pl.multiple_of(info[at + k] * modes, modes)
        both = jnp.dot(
            matrix[pl.ds(start, modes), :], parts, preferred_element_type=jnp.float32
        )
        out[...] = both[:, :cells] + both[:, cells:]


def two_blocks(at, first, last, scale, rows, info, matrix, *refs):
    modes = matrix.shape[1]
    blocks, refs = refs[:2], refs[2:]
    if not first:
        before, refs = refs[0], refs[1:]
    if last:
        base, refs = refs[0], refs[1:]
    total = None if first else before[...]
    for k, block in enumerate(blocks):
        pieces = list(halves(block[:modes].T))
        if rows:
            weights = [
                jnp.concatenate(
                    [
                        block[modes + i : modes + i + 1, :]
                        for i in range(d * modes // LANES, (d + 1) * modes // LANES)
                    ],
                    axis=1,
                )
                for d in range(2)
            ]
            weights.append(jnp.zeros((6, modes), jnp.float32))
            pieces += halves(jnp.concatenate(weights, axis=0))
        left = jnp.concatenate(pieces, axis=0)
        start = pl.multiple_of(info[at + k] * modes, modes)
        term = jnp.dot(left, matrix[pl.ds(start, modes), :], preferred_element_type=jnp.float32)
        total = term if total is None else total + term
    if not last:
        refs[0][...] = total
        return
    cells = base.shape[1]
    value = base[...] - scale * (total[:cells] + total[cells : 2 * cells]).T
    refs[0][...] = value
    if rows:
        refs[1][...] = value.T[:HALO]
        refs[2][...] = total[2 * cells : 2 * cells + 8] + total[2 * cells + 8 :]


def own_rows(distribution, velocity, capacity, out, sem):
    modes, cells = (velocity.shape[1], out.shape[1])
    copy = pltpu.make_async_copy(
        distribution.at[:, pl.ds(0, cells)], out.at[pl.ds(0, modes), :], sem
    )
    copy.start()
    per = modes // LANES
    for d in range(2):
        for i in range(per):
            lanes = slice(i * LANES, (i + 1) * LANES)
            out[modes + d * per + i : modes + d * per + i + 1, :] = (
                velocity[d : d + 1, lanes] * capacity[:, lanes]
            )
    for r in range(modes + 2 * per, out.shape[0]):
        out[r : r + 1, :] = jnp.zeros((1, LANES), jnp.float32)
    copy.wait()


def payload(at, slots, info, arrived, *refs):
    out = refs[-1]

    for k, slot in enumerate(slots):

        @pl.when(info[at] == slot)
        def _(k=k):
            mine, theirs = refs[2 * k], refs[2 * k + 1]
            modes = mine.shape[0]
            out[:modes] = arrived[:modes] + (mine[...] + theirs[...])
            if out.shape[0] > modes:
                out[modes:] = arrived[modes:]

    @pl.when(info[at] < 0)
    def _():
        out[...] = arrived[...]


def pick(at, info, *refs):
    out = refs[-1]
    for k, ref in enumerate(refs[:-1]):

        @pl.when(info[at] == k)
        def _(ref=ref):
            out[...] = ref[...]


def turn_sum(scale, one, two, mine, theirs, base, out, strip):
    modes = mine.shape[0]
    total = one[:modes] + two[:modes] + (mine[...] + theirs[...])
    value = base[...] - scale * total
    out[...] = value
    strip[...] = value.T[-HALO:]


def last_sum(scale, one, two, mine, theirs, base, other, out, value, sems):
    cells = base.shape[1]
    ahead = pltpu.make_async_copy(other, out.at[:, pl.ds(cells, cells)], sems.at[0])
    ahead.start()
    total = one[...] + two[...] + (mine[...] + theirs[...])
    value[...] = base[...] - scale * total
    copy = pltpu.make_async_copy(value, out.at[:, pl.ds(0, cells)], sems.at[1])
    copy.start()
    ahead.wait()
    copy.wait()


def strip_rows(distribution, leading, last):
    cells = distribution.shape[1]
    leading[...] = distribution[:, :LANES].T[:HALO]
    last[...] = distribution[:, cells - LANES :].T[-HALO:]


def still_rate(pieces, before, after, columns, kinds):
    lane = lax.broadcasted_iota(jnp.int32, (1, LANES), 1)
    y = lane % NY
    vx, vy, capacity = (columns[:, i : i + 1] for i in range(3))
    fore_x, back_x = 0.5 * jnp.maximum(vx, 0.0), 0.5 * jnp.minimum(vx, 0.0)
    fore_y, back_y = 0.5 * jnp.maximum(vy, 0.0), 0.5 * jnp.minimum(vy, 0.0)
    centre = 3.0 * (fore_x - back_x + fore_y - back_y)
    padded = [before, *pieces, after]
    rates = []
    for k, value in enumerate(pieces):
        def along_x(offset):
            near = pltpu.roll(value, -offset % LANES, 1)
            if offset < 0:
                return jnp.where(lane < -offset, pltpu.roll(padded[k], -offset, 1), near)
            return jnp.where(
                lane >= LANES - offset, pltpu.roll(padded[k + 2], LANES - offset, 1), near
            )

        def along_y(offset):
            inside = (y + offset >= 0) & (y + offset < NY)
            return jnp.where(inside, pltpu.roll(value, -offset % LANES, 1), 0.0)

        kind = kinds[:, k * LANES : (k + 1) * LANES]
        contact = jnp.where(kind > 0, relax_rate, 0.0)
        source = jnp.where(kind == 1, contact, -contact)
        rate = (
            source * capacity
            - (centre + contact) * value
            + fore_x * (4.0 * along_x(-NY) - along_x(-2 * NY))
            + back_x * (along_x(2 * NY) - 4.0 * along_x(NY))
            + fore_y * (4.0 * along_y(-1) - along_y(-2))
            + back_y * (along_y(2) - 4.0 * along_y(1))
        )
        rates.append(rate)
    return rates


def edges(before, after, rows):
    pad = jnp.zeros((rows.size, LANES - HALO), jnp.float32)
    return (
        jnp.concatenate([pad, before[:, rows].T], axis=1),
        jnp.concatenate([after[:, rows].T, pad], axis=1),
    )


def first_rest(field, before, after, table, kinds, base_a, base_b):
    modes, half = base_a.shape
    block = min(modes, LANES)

    def step(i, _):
        rows = pl.ds(pl.multiple_of(i * block, block), block)
        value = field[rows, :]
        pieces = [value[:, k : k + LANES] for k in range(0, 2 * half, LANES)]
        rates = still_rate(pieces, *edges(before, after, rows), table[:, rows].T, kinds[...])
        bases = [v + time_step * r for v, r in zip(pieces, rates)]
        middle = len(bases) // 2
        base_a[rows, :] = jnp.concatenate(bases[:middle], axis=1)
        base_b[rows, :] = jnp.concatenate(bases[middle:], axis=1)
        return 0

    lax.fori_loop(0, modes // block, step, 0)


def second_rest(
    field, mid_a, mid_b, before, after, table, kinds, scattered, end_a, end_b, flux
):
    modes, half = end_a.shape
    block = min(modes, LANES)
    step_size = 0.5 * time_step
    flux[...] = jnp.zeros_like(flux)

    def step(i, _):
        rows = pl.ds(pl.multiple_of(i * block, block), block)
        value = field[rows, :]
        mids = [
            mid[rows, k : k + LANES] for mid in (mid_a, mid_b) for k in range(0, half, LANES)
        ]
        columns = table[:, rows].T
        rates = still_rate(mids, *edges(before, after, rows), columns, kinds[...])
        taken = step_size * scattered[:, rows].T
        ends = []
        for k, (mid, rate) in enumerate(zip(mids, rates)):
            lanes = slice(k * LANES, (k + 1) * LANES)
            end = 0.5 * (value[:, lanes] + mid) + step_size * rate
            ends.append(end)
            for d in range(2):
                terms = columns[:, 3 + d : 4 + d] * end - taken[:, d : d + 1] * mid
                flux[d : d + 1, lanes] += jnp.sum(terms, axis=0, keepdims=True)
        middle = len(ends) // 2
        end_a[rows, :] = jnp.concatenate(ends[:middle], axis=1)
        end_b[rows, :] = jnp.concatenate(ends[middle:], axis=1)
        return 0

    lax.fori_loop(0, modes // block, step, 0)


def halo(leading, last):
    count = lax.axis_size("space")
    up = [(i, i + 1) for i in range(count - 1)]
    down = [(j, i) for i, j in up]
    before = lax.ppermute(last, "space", up)
    after = lax.ppermute(leading, "space", down)
    return before, after


def block_sources(chips, place):
    found = []
    for step in range(chips - 1):
        if place >= step + 1:
            found.append((0, step, place - 1 - step))
        if place <= chips - 2 - step:
            found.append((1, step, place + 1 + step))
    return found


def sum_targets(chips, chip):
    found = []
    for step in range(1, chips):
        far = chips - step
        found += [t for t in (chip + far, chip - far) if 0 <= t < chips]
    return found + [chip]


class Plan:
    def __init__(self, chips):
        rows = []
        self.choices = [
            sorted({block_sources(chips, p)[s][:2] for p in range(chips)})
            for s in range(chips - 1)
        ]
        self.slots = {}
        for device in range(2 * chips):
            chip, core = device // 2, device % 2
            place = chip if core == 0 else chips - 1 - chip
            blocks = []
            for c in (core, 1 - core):
                p = chip if c == 0 else chips - 1 - chip
                sources = [p] + [q for _, _, q in block_sources(chips, p)]
                blocks.append([2 * (q if c == 0 else chips - 1 - q) + c for q in sources])
            targets = sum_targets(chips, chip)
            row = [b for pair in zip(*blocks) for b in pair]
            row += [b for t in targets for b in (2 * t + core, 2 * t + 1 - core)]
            for stream in (0, 1):
                here = place if stream == 0 else chips - 1 - place
                for step in range(1, chips):
                    slot = -1
                    if here < step:
                        q = here + chips - step
                        slot = targets.index(q if core == stream else chips - 1 - q)
                        self.slots.setdefault((stream, step), set()).add(slot)
                    row.append(slot)
            own = [s[:2] for s in block_sources(chips, place)]
            row += [self.choices[s].index(own[s]) for s in range(chips - 1)]
            rows.append(row)
        self.table = np.array(rows, np.int32)
        self.block = lambda slot: 2 * slot
        self.target = lambda slot: 2 * chips + 2 * slot
        self.sent = lambda stream, step: 4 * chips + stream * (chips - 1) + step - 1
        self.picked = lambda slot: 4 * chips + 2 * (chips - 1) + slot


def on_device(distribution, scatter_matrix, velocity, capacity, cell_type):
    modes, cells = distribution.shape
    total_modes = scatter_matrix.shape[0]
    half = cells // 2
    extra = -(-2 * modes // LANES // 8) * 8
    step_size = 0.5 * time_step
    part = (modes, half)
    devices = lax.axis_size("mode")
    chips = devices // 2
    me = lax.axis_index("mode")
    plan = Plan(chips)
    info = jnp.asarray(plan.table)[me]
    call = Chain()
    right = [[(2 * z + c, 2 * z + 2 + c) for z in range(chips - 1)] for c in (0, 1)]
    left = [[(j, i) for i, j in pairs] for pairs in right]
    streams = (right[0] + left[1], right[1] + left[0])
    across = [(i, i ^ 1) for i in range(devices)]
    cap = capacity[None, :]
    table = jnp.concatenate(
        [velocity, cap, cap * velocity, jnp.zeros((3, modes), jnp.float32)], axis=0
    )
    kinds = cell_type[None, :]

    def exchange(value):
        return lax.ppermute(value, "mode", across)

    def along(stream, value):
        return lax.ppermute(value, "mode", streams[stream])

    class Round:
        def __init__(self, own, scale, rows):
            self.own, self.scale, self.rows = own, scale, rows
            self.arrived = [[along(stream, own)] for stream in (0, 1)]
            self.terms, self.blocks, self.total = [], [], None

        def add_terms(self, field, column):
            slot = len(self.terms)
            kernel = functools.partial(slot_products, plan.target(slot), column)
            mine, other = call(kernel, [part] * 2, [scatter_matrix, field], info)
            self.terms.append((mine, exchange(other)))

        def take_own(self):
            self.blocks.append((self.own, exchange(self.own)))

        def send(self, stream, step):
            slots = sorted(plan.slots[stream, step])
            arrived = self.arrived[stream][step - 1]
            kernel = functools.partial(payload, plan.sent(stream, step), slots)
            arrays = [arrived] + [a for s in slots for a in self.terms[s]]
            (value,) = call(kernel, [arrived.shape], arrays, info)
            self.arrived[stream].append(along(stream, value))

        def take(self, slot):
            arrays = [self.arrived[stream][step] for stream, step in plan.choices[slot - 1]]
            kernel = functools.partial(pick, plan.picked(slot - 1))
            (here,) = call(kernel, [arrays[0].shape], arrays, info)
            self.blocks.append((here, exchange(here)))

        def multiply(self, slot, base=None):
            first, last = slot == 0, base is not None
            kernel = functools.partial(
                two_blocks, plan.block(slot), first, last, self.scale, self.rows
            )
            arrays = [scatter_matrix, *self.blocks[slot]]
            arrays += [] if first else [self.total]
            arrays += [base] if last else []
            outs = [(2 * half + (16 if self.rows else 0), modes)]
            if last:
                outs = [part, (HALO, modes), (8, modes)] if self.rows else [part]
            results = call(kernel, outs, arrays, info)
            self.total = results[0]
            return results

        def ends(self):
            return [self.arrived[0][-1], self.arrived[1][-1], *self.terms[-1]]

    (own,) = call(
        own_rows,
        [(modes + extra, half)],
        [distribution, velocity, cap],
        places=[HBM, VMEM, VMEM],
        scratch=[pltpu.SemaphoreType.DMA(())],
    )
    one = Round(own, time_step, True)
    for slot in range(chips - 1):
        one.add_terms(distribution, half)
    one.take_own()
    for step in range(1, chips):
        if step == 1:
            one.take(step)
        for stream in (0, 1):
            one.send(stream, step)
        if step > 1:
            one.take(step)
        if step == 1:
            one.add_terms(distribution, half)
            strips = halo(*call(strip_rows, [(HALO, modes)] * 2, [distribution]))
        one.multiply(step - 1)
        if step == min(2, chips - 1):
            base_a, base_b = call(
                first_rest, [part] * 2, [distribution, *strips, table, kinds]
            )
    mid_a, leading, scattered = one.multiply(chips - 1, base_a)

    two = Round.__new__(Round)
    two.terms = []
    two.add_terms(mid_a, 0)
    mid_b, last = call(
        functools.partial(turn_sum, time_step), [part, (HALO, modes)], [*one.ends(), base_b]
    )
    terms = two.terms
    two = Round(mid_b, step_size, False)
    two.terms = terms
    for slot in range(1, chips - 1):
        two.add_terms(mid_a, 0)
    two.take_own()
    strips = halo(leading, last)
    for step in range(1, chips):
        if step == 1:
            two.take(step)
        for stream in (0, 1):
            two.send(stream, step)
        if step > 1:
            two.take(step)
        if step == 1:
            two.add_terms(mid_a, 0)
        two.multiply(step - 1)
        if step == min(2, chips - 1):
            end_a, end_b, flux = call(
                second_rest,
                [part, part, (8, cells)],
                [distribution, mid_a, mid_b, *strips, table, kinds, scattered],
            )
    flux = flux[:2]
    bit = 1
    while bit < devices:
        flux = flux + lax.ppermute(flux, "mode", [(i, i ^ bit) for i in range(devices)])
        bit *= 2
    heat_flux = flux / jnp.sqrt(jnp.float32(total_modes))
    (last_b,) = two.multiply(chips - 1, end_b)
    (updated,) = call(
        functools.partial(last_sum, step_size),
        [(modes, cells)],
        [*two.ends(), end_a, last_b],
        scratch=[pltpu.VMEM(part, jnp.float32), pltpu.SemaphoreType.DMA((2,))],
        out_specs=[HBM],
    )
    return (updated, heat_flux)


def solution(mesh):
    return jax.shard_map(
        on_device,
        mesh=mesh,
        in_specs=(P("mode", "space"), P(None, "mode"), P(None, "mode"), P("mode"), P("space")),
        out_specs=(P("mode", "space"), P(None, "space")),
        check_vma=False,
    )
```

time: 242 us -> 172 us (0.71)
  the two profiles are of different devices: /device:TPU:0 before, /device:TPU:13 now
where the time goes in v3:
time: 172 us; the launch traced here: 169 us
  starting transfers between devices  69.8 us (41%)
  Pallas kernels  55.8 us (32%)
  waiting for transfers between devices  29.9 us (17%)
  local copies, waits for them, and re-layouts  11.8 us (7%)
    pallas_call x40, Pallas kernels, __call__(): pl.pallas_call(body, out_shape=[jax.ShapeDtypeStruct(shape, jnp.float32)...  55.8 us
    ppermute x16, starting transfers between devices, along(): return lax.ppermute(value, 'mode', streams[stream])  42.1 us
    ppermute x16, waiting for transfers between devices, along(): return lax.ppermute(value, 'mode', streams[stream])  22.5 us
    ppermute x16, starting transfers between devices, exchange(): return lax.ppermute(value, 'mode', across)  13 us
    unnamed x18, local copies, waits for them, and re-layouts  11 us
    ppermute x2, starting transfers between devices, halo(): before = lax.ppermute(last, 'space', up)  5.59 us
    ppermute x2, starting transfers between devices, halo(): after = lax.ppermute(leading, 'space', down)  4.98 us
    ppermute x2, waiting for transfers between devices, halo(): before = lax.ppermute(last, 'space', up)  4.1 us
  transfers between devices with their start and end apart: 39, of which 13 were waited for; matrix products, arithmetic and copies ran while one was open for 1% of the time, Pallas kernels for 32%

profile of v3, /device:TPU:13, one launch (start us, length us, event | category | flops | bytes accessed | tf_op | source)
XLA Modules:
  0.0 169.4 jit_solution(799251201967599021)
XLA Ops:
  0.6 1.2 copy-done.2
  1.9 0.7 copy-done.4
  2.6 0.7 copy-done.6
  3.3 3.3 %collective-permute-start.2 = (f32[1040,128]{1,0:T(8,128)S(1)}, f32[1040,128]{1,0:T(8,128)S(1)}, u32[]{:S(2)}, u32[]{:S(2)}) collective-permute-start(f32[1040,128]{1,0:T(8,128)S(1)} %own_rows.1.refs_3_.refs_2_), channel_id=1, source_target_pairs={{1,3},{3,5},{5,7},{2,0},{4,2},{6,4},{9,11},{11,13},{13,15},{10,8},... | collective-permute-start | bytes 1597448 | tf_op jit(solution)/shard_map/ppermute | solution.py:370
  6.6 2.1 %collective-permute-start = (f32[1040,128]{1,0:T(8,128)S(1)}, f32[1040,128]{1,0:T(8,128)S(1)}, u32[]{:S(2)}, u32[]{:S(2)}) collective-permute-start(f32[1040,128]{1,0:T(8,128)S(1)} %own_rows.1.refs_3_.refs_2_), channel_id=1, source_target_pairs={{0,2},{2,4},{4,6},{3,1},{5,3},{7,5},{8,10},{10,12},{12,14},{11,9},... | collective-permute-start | bytes 1597448 | tf_op jit(solution)/shard_map/ppermute | solution.py:370
  8.8 0.7 dynamic-slice_bitcast_fusion.refs_0_
  9.5 5.8 %copy-done = bf16[8192,1024]{1,0:T(8,128)(2,1)S(1)} copy-done((bf16[8192,1024]{1,0:T(8,128)(2,1)S(1)}, bf16[8192,1024]{1,0:T(8,128)(2,1)}, u32[]{:S(2)}) %copy-start) | copy-done | bytes 16777240
  15.2 1.8 %slot_products.8 = (f32[1024,128]{1,0:T(8,128)S(1)}, f32[1024,128]{1,0:T(8,128)S(1)}) custom-call(s32[25]{0:T(128)S(1)} %dynamic-slice_bitcast_fusion.refs_0_, bf16[8192,1024]{1,0:T(8,128)(2,1)S(1)} %copy-done, f32[1024,256]{1,0:T(8,128)S(1)} %copy-done.3, f32[1040,128]{1,0:T(8,128)S(1)} %own_rows.1.refs_3_.refs_2_), custom_call_target="tpu_custom_call" | custom-call | flops 1024 | bytes 1024 | tf_op jit(solution)/shard_map/slot_products/pallas_call | solution.py:39
  17.0 1.3 collective-permute-start.1
  18.4 2.6 %copy-done.1 = bf16[8192,1024]{1,0:T(8,128)(2,1)S(1)} copy-done((bf16[8192,1024]{1,0:T(8,128)(2,1)S(1)}, bf16[8192,1024]{1,0:T(8,128)(2,1)}, u32[]{:S(2)}) %copy-start.1) | copy-done | bytes 16777240
  21.0 1.8 %slot_products.9 = (f32[1024,128]{1,0:T(8,128)S(1)}, f32[1024,128]{1,0:T(8,128)S(1)}) custom-call(s32[25]{0:T(128)S(1)} %dynamic-slice_bitcast_fusion.refs_0_, bf16[8192,1024]{1,0:T(8,128)(2,1)S(1)} %copy-done.1, f32[1024,256]{1,0:T(8,128)S(1)} %copy-done.3, f32[1024,128]{1,0:T(8,128)S(1)} %get-tuple-element.30.refs_3_.refs_2_), custom_call_target="tpu_custom_call" | custom-call | flops 1024 | bytes 1024 | tf_op jit(solution)/shard_map/slot_products/pallas_call | solution.py:39
  22.8 1.8 %slot_products.10 = (f32[1024,128]{1,0:T(8,128)S(1)}, f32[1024,128]{1,0:T(8,128)S(1)}) custom-call(s32[25]{0:T(128)S(1)} %dynamic-slice_bitcast_fusion.refs_0_, bf16[8192,1024]{1,0:T(8,128)(2,1)S(1)} %copy-done.1, f32[1024,256]{1,0:T(8,128)S(1)} %copy-done.3, f32[1024,128]{1,0:T(8,128)S(1)} %get-tuple-element.32.refs_3_.refs_4_.refs_2_), custom_call_target="tpu_custom_call" | custom-call | flops 1024 | bytes 1024 | tf_op jit(solution)/shard_map/slot_products/pallas_call | solution.py:39
  25.8 1.9 %collective-permute-start.3 = (f32[1040,128]{1,0:T(8,128)S(1)}, f32[1040,128]{1,0:T(8,128)S(1)}, u32[]{:S(2)}, u32[]{:S(2)}) collective-permute-start(f32[1040,128]{1,0:T(8,128)S(1)} %payload.12.refs_4_), channel_id=1, source_target_pairs={{0,2},{2,4},{4,6},{3,1},{5,3},{7,5},{8,10},{10,12},{12,14},{11,9},... | collective-permute-start | bytes 1597448 | tf_op jit(solution)/shard_map/ppermute | solution.py:370
  28.4 3.4 %collective-permute-start.11 = (f32[1040,128]{1,0:T(8,128)S(1)}, f32[1040,128]{1,0:T(8,128)S(1)}, u32[]{:S(2)}, u32[]{:S(2)}) collective-permute-start(f32[1040,128]{1,0:T(8,128)S(1)} %payload.13.refs_3_), channel_id=1, source_target_pairs={{1,3},{3,5},{5,7},{2,0},{4,2},{6,4},{9,11},{11,13},{13,15},{10,8},... | collective-permute-start | bytes 1597448 | tf_op jit(solution)/shard_map/ppermute | solution.py:370
  31.7 1.8 %collective-permute-start.4 = (f32[1024,128]{1,0:T(8,128)S(1)}, f32[1024,128]{1,0:T(8,128)S(1)}, u32[]{:S(2)}, u32[]{:S(2)}) collective-permute-start(f32[1024,128]{1,0:T(8,128)S(1)} %get-tuple-element.34), channel_id=1, source_target_pairs={{0,1},{1,0},{2,3},{3,2},{4,5},{5,4},{6,7},{7,6},{8,9},{9,8},{10,11... | collective-permute-start | bytes 1572872 | tf_op jit(solution)/shard_map/ppermute | solution.py:367
  33.7 1.8 %slot_products.11 = (f32[1024,128]{1,0:T(8,128)S(1)}, f32[1024,128]{1,0:T(8,128)S(1)}) custom-call(s32[25]{0:T(128)S(1)} %dynamic-slice_bitcast_fusion.refs_0_, bf16[8192,1024]{1,0:T(8,128)(2,1)S(1)} %copy-done.1, f32[1024,256]{1,0:T(8,128)S(1)} %copy-done.3, f32[1040,128]{1,0:T(8,128)S(1)} %payload.13.refs_3_), custom_call_target="tpu_custom_call" | custom-call | flops 1024 | bytes 1024 | tf_op jit(solution)/shard_map/slot_products/pallas_call | solution.py:39
  35.8 1.9 %two_blocks.8.refs_6_.refs_4_ = f32[272,1024]{1,0:T(8,128)S(1)} custom-call(s32[25]{0:T(128)S(1)} %dynamic-slice_bitcast_fusion.refs_0_, bf16[8192,1024]{1,0:T(8,128)(2,1)S(1)} %copy-done.1, f32[1040,128]{1,0:T(8,128)S(1)} %own_rows.1.refs_3_.refs_2_, f32[1040,128]{1,0:T(8,128)S(1)} %collective-permute-done.5.refs_3_, f32[32,1024]{1,0:T(8,128)S(1)} %get-tuple-element.36.refs_4_), custom_call_target="tpu_custom_call" | custom-call | flops 1024 | bytes 1024 | tf_op jit(solution)/shard_map/two_blocks/pallas_call | solution.py:39
  38.4 1.9 %collective-permute-start.6 = (f32[1040,128]{1,0:T(8,128)S(1)}, f32[1040,128]{1,0:T(8,128)S(1)}, u32[]{:S(2)}, u32[]{:S(2)}) collective-permute-start(f32[1040,128]{1,0:T(8,128)S(1)} %payload.14.refs_6_), channel_id=1, source_target_pairs={{0,2},{2,4},{4,6},{3,1},{5,3},{7,5},{8,10},{10,12},{12,14},{11,9},... | collective-permute-start | bytes 1597448 | tf_op jit(solution)/shard_map/ppermute | solution.py:370
  40.3 2.9 %collective-permute-done.11.refs_1_.refs_3_ = f32[1040,128]{1,0:T(8,128)S(1)} collective-permute-done((f32[1040,128]{1,0:T(8,128)S(1)}, f32[1040,128]{1,0:T(8,128)S(1)}, u32[]{:S(2)}, u32[]{:S(2)}) %collective-permute-start.11) | collective-permute-done | bytes 532512 | tf_op jit(solution)/shard_map/ppermute | solution.py:370
  43.9 3.2 %collective-permute-start.13 = (f32[1040,128]{1,0:T(8,128)S(1)}, f32[1040,128]{1,0:T(8,128)S(1)}, u32[]{:S(2)}, u32[]{:S(2)}) collective-permute-start(f32[1040,128]{1,0:T(8,128)S(1)} %payload.15.refs_4_), channel_id=1, source_target_pairs={{1,3},{3,5},{5,7},{2,0},{4,2},{6,4},{9,11},{11,13},{13,15},{10,8},... | collective-permute-start | bytes 1597448 | tf_op jit(solution)/shard_map/ppermute | solution.py:370
  47.1 3.3 %collective-permute-start.7 = (f32[1024,128]{1,0:T(8,128)S(1)}, f32[1024,128]{1,0:T(8,128)S(1)}, u32[]{:S(2)}, u32[]{:S(2)}) collective-permute-start(f32[1024,128]{1,0:T(8,128)S(1)} %get-tuple-element.37), channel_id=1, source_target_pairs={{0,1},{1,0},{2,3},{3,2},{4,5},{5,4},{6,7},{7,6},{8,9},{9,8},{10,11... | collective-permute-start | bytes 1572872 | tf_op jit(solution)/shard_map/ppermute | solution.py:367
  50.4 3.1 %collective-permute-start.9 = (f32[32,1024]{1,0:T(8,128)S(1)}, f32[32,1024]{1,0:T(8,128)S(1)}, u32[]{:S(2)}, u32[]{:S(2)}) collective-permute-start(f32[32,1024]{1,0:T(8,128)S(1)} %get-tuple-element.36.refs_4_), channel_id=1, source_target_pairs={{8,0},{16,8},{24,16},{9,1},{17,9},{25,17},{10,2},{18,10},{26,18},{... | collective-permute-start | bytes 393224 | tf_op jit(solution)/shard_map/ppermute | solution.py:283
  54.1 2.2 %collective-permute-start.8 = (f32[32,1024]{1,0:T(8,128)S(1)}, f32[32,1024]{1,0:T(8,128)S(1)}, u32[]{:S(2)}, u32[]{:S(2)}) collective-permute-start(f32[32,1024]{1,0:T(8,128)S(1)} %get-tuple-element.38), channel_id=1, source_target_pairs={{0,8},{8,16},{16,24},{1,9},{9,17},{17,25},{2,10},{10,18},{18,26},{... | collective-permute-start | bytes 393224 | tf_op jit(solution)/shard_map/ppermute | solution.py:282
  56.4 1.9 %two_blocks.9.refs_5_.refs_4_ = f32[272,1024]{1,0:T(8,128)S(1)} custom-call(s32[25]{0:T(128)S(1)} %dynamic-slice_bitcast_fusion.refs_0_, bf16[8192,1024]{1,0:T(8,128)(2,1)S(1)} %copy-done.1, f32[1040,128]{1,0:T(8,128)S(1)} %pick.6.refs_4_.refs_2_, f32[1040,128]{1,0:T(8,128)S(1)} %collective-permute-done.10.refs_3_, ...), custom_call_target="tpu_custom_call" | custom-call | flops 1024 | bytes 1024 | tf_op jit(solution)/shard_map/two_blocks/pallas_call | solution.py:39
  58.3 3.4 %collective-permute-done.8.refs_1_ = f32[32,1024]{1,0:T(8,128)S(1)} collective-permute-done((f32[32,1024]{1,0:T(8,128)S(1)}, f32[32,1024]{1,0:T(8,128)S(1)}, u32[]{:S(2)}, u32[]{:S(2)}) %collective-permute-start.8) | collective-permute-done | bytes 131104 | tf_op jit(solution)/shard_map/ppermute | solution.py:282
  61.7 1.1 collective-permute-start.17
  62.8 6.0 %first_rest.1 = (f32[1024,128]{1,0:T(8,128)S(1)}, f32[1024,128]{1,0:T(8,128)S(1)}) custom-call(f32[1024,256]{1,0:T(8,128)S(1)} %copy-done.3, f32[32,1024]{1,0:T(8,128)S(1)} %collective-permute-done.8.refs_1_, f32[32,1024]{1,0:T(8,128)S(1)} %collective-permute-done.9.refs_2_, f32[8,1024]{1,0:T(8,128)S(1)} %maximum_maximum_fusion.refs_3_.refs_5_, ...), custom_call_target="tpu_custom_call" | custom-call | flops 1024 | bytes 1024 | tf_op jit(solution)/shard_map/first_rest/pallas_call | solution.py:39
  70.8 3.0 %collective-permute-start.14 = (f32[1040,128]{1,0:T(8,128)S(1)}, f32[1040,128]{1,0:T(8,128)S(1)}, u32[]{:S(2)}, u32[]{:S(2)}) collective-permute-start(f32[1040,128]{1,0:T(8,128)S(1)} %payload.17.refs_5_), channel_id=1, source_target_pairs={{1,3},{3,5},{5,7},{2,0},{4,2},{6,4},{9,11},{11,13},{13,15},{10,8},... | collective-permute-start | bytes 1597448 | tf_op jit(solution)/shard_map/ppermute | solution.py:370
  73.9 2.5 %collective-permute-start.12 = (f32[1040,128]{1,0:T(8,128)S(1)}, f32[1040,128]{1,0:T(8,128)S(1)}, u32[]{:S(2)}, u32[]{:S(2)}) collective-permute-start(f32[1040,128]{1,0:T(8,128)S(1)} %payload.16.refs_6_), channel_id=1, source_target_pairs={{0,2},{2,4},{4,6},{3,1},{5,3},{7,5},{8,10},{10,12},{12,14},{11,9},... | collective-permute-start | bytes 1597448 | tf_op jit(solution)/shard_map/ppermute | solution.py:370
  76.3 1.1 collective-permute-start.15
  77.4 1.9 %two_blocks.10.refs_4_.refs_6_ = f32[272,1024]{1,0:T(8,128)S(1)} custom-call(s32[25]{0:T(128)S(1)} %dynamic-slice_bitcast_fusion.refs_0_, bf16[8192,1024]{1,0:T(8,128)(2,1)S(1)} %copy-done.1, f32[1040,128]{1,0:T(8,128)S(1)} %pick.7.refs_5_.refs_2_, f32[1040,128]{1,0:T(8,128)S(1)} %collective-permute-done.17.refs_3_, ...), custom_call_target="tpu_custom_call" | custom-call | flops 1024 | bytes 1024 | tf_op jit(solution)/shard_map/two_blocks/pallas_call | solution.py:39
  79.4 2.1 %two_blocks.11 = (f32[1024,128]{1,0:T(8,128)S(1)}, f32[32,1024]{1,0:T(8,128)S(1)}, f32[8,1024]{1,0:T(8,128)S(1)}) custom-call(s32[25]{0:T(128)S(1)} %dynamic-slice_bitcast_fusion.refs_0_, bf16[8192,1024]{1,0:T(8,128)(2,1)S(1)} %copy-done.1, f32[1040,128]{1,0:T(8,128)S(1)} %pick.8.refs_5_.refs_2_, f32[1040,128]{1,0:T(8,128)S(1)} %collective-permute-done.16.refs_3_, ...), custom_call_target="tpu_custom_call" | custom-call | flops 1024 | bytes 1024 | tf_op jit(solution)/shard_map/two_blocks/pallas_call | solution.py:39
  81.5 1.8 %slot_products.12 = (f32[1024,128]{1,0:T(8,128)S(1)}, f32[1024,128]{1,0:T(8,128)S(1)}) custom-call(s32[25]{0:T(128)S(1)} %dynamic-slice_bitcast_fusion.refs_0_, bf16[8192,1024]{1,0:T(8,128)(2,1)S(1)} %copy-done.1, f32[1024,128]{1,0:T(8,128)S(1)} %get-tuple-element.42.refs_2_.refs_3_.refs_1_, f32[1024,128]{1,0:T(8,128)S(1)} %get-tuple-element.42.refs_2_.refs_3_.refs_1_), custom_call_target="tpu_custom_call" | custom-call | flops 1024 | bytes 1024 | tf_op jit(solution)/shard_map/slot_products/pallas_call | solution.py:39
  83.9 3.6 %collective-permute-done.12.refs_0_ = f32[1040,128]{1,0:T(8,128)S(1)} collective-permute-done((f32[1040,128]{1,0:T(8,128)S(1)}, f32[1040,128]{1,0:T(8,128)S(1)}, u32[]{:S(2)}, u32[]{:S(2)}) %collective-permute-start.12) | collective-permute-done | bytes 532512 | tf_op jit(solution)/shard_map/ppermute | solution.py:370
  87.8 3.0 %collective-permute-start.20 = (f32[1024,128]{1,0:T(8,128)S(1)}, f32[1024,128]{1,0:T(8,128)S(1)}, u32[]{:S(2)}, u32[]{:S(2)}) collective-permute-start(f32[1024,128]{1,0:T(8,128)S(1)} %get-tuple-element.44.refs_3_.refs_2_), channel_id=1, source_target_pairs={{1,3},{3,5},{5,7},{2,0},{4,2},{6,4},{9,11},{11,13},{13,15},{10,8},... | collective-permute-start | bytes 1572872 | tf_op jit(solution)/shard_map/ppermute | solution.py:370
  90.8 2.3 %collective-permute-start.18 = (f32[1024,128]{1,0:T(8,128)S(1)}, f32[1024,128]{1,0:T(8,128)S(1)}, u32[]{:S(2)}, u32[]{:S(2)}) collective-permute-start(f32[1024,128]{1,0:T(8,128)S(1)} %get-tuple-element.44.refs_3_.refs_2_), channel_id=1, source_target_pairs={{0,2},{2,4},{4,6},{3,1},{5,3},{7,5},{8,10},{10,12},{12,14},{11,9},... | collective-permute-start | bytes 1572872 | tf_op jit(solution)/shard_map/ppermute | solution.py:370
  93.7 1.8 %slot_products.13 = (f32[1024,128]{1,0:T(8,128)S(1)}, f32[1024,128]{1,0:T(8,128)S(1)}) custom-call(s32[25]{0:T(128)S(1)} %dynamic-slice_bitcast_fusion.refs_0_, bf16[8192,1024]{1,0:T(8,128)(2,1)S(1)} %copy-done.1, f32[1024,128]{1,0:T(8,128)S(1)} %get-tuple-element.42.refs_2_.refs_3_.refs_1_, f32[1024,128]{1,0:T(8,128)S(1)} %get-tuple-element.44.refs_3_.refs_2_), custom_call_target="tpu_custom_call" | custom-call | flops 1024 | bytes 1024 | tf_op jit(solution)/shard_map/slot_products/pallas_call | solution.py:39
  95.9 1.8 %slot_products.14 = (f32[1024,128]{1,0:T(8,128)S(1)}, f32[1024,128]{1,0:T(8,128)S(1)}) custom-call(s32[25]{0:T(128)S(1)} %dynamic-slice_bitcast_fusion.refs_0_, bf16[8192,1024]{1,0:T(8,128)(2,1)S(1)} %copy-done.1, f32[1024,128]{1,0:T(8,128)S(1)} %get-tuple-element.42.refs_2_.refs_3_.refs_1_, f32[1024,128]{1,0:T(8,128)S(1)} %get-tuple-element.46.refs_3_.refs_4_.refs_2_), custom_call_target="tpu_custom_call" | custom-call | flops 1024 | bytes 1024 | tf_op jit(solution)/shard_map/slot_products/pallas_call | solution.py:39
  97.6 3.8 %collective-permute-done.20.refs_2_.refs_1_ = f32[1024,128]{1,0:T(8,128)S(1)} collective-permute-done((f32[1024,128]{1,0:T(8,128)S(1)}, f32[1024,128]{1,0:T(8,128)S(1)}, u32[]{:S(2)}, u32[]{:S(2)}) %collective-permute-start.20) | collective-permute-done | bytes 524320 | tf_op jit(solution)/shard_map/ppermute | solution.py:370
  101.4 2.2 %collective-permute-done.18.refs_1_ = f32[1024,128]{1,0:T(8,128)S(1)} collective-permute-done((f32[1024,128]{1,0:T(8,128)S(1)}, f32[1024,128]{1,0:T(8,128)S(1)}, u32[]{:S(2)}, u32[]{:S(2)}) %collective-permute-start.18) | collective-permute-done | bytes 524320 | tf_op jit(solution)/shard_map/ppermute | solution.py:370
  104.8 1.9 %collective-permute-start.21 = (f32[1024,128]{1,0:T(8,128)S(1)}, f32[1024,128]{1,0:T(8,128)S(1)}, u32[]{:S(2)}, u32[]{:S(2)}) collective-permute-start(f32[1024,128]{1,0:T(8,128)S(1)} %payload.18.refs_4_), channel_id=1, source_target_pairs={{0,2},{2,4},{4,6},{3,1},{5,3},{7,5},{8,10},{10,12},{12,14},{11,9},... | collective-permute-start | bytes 1572872 | tf_op jit(solution)/shard_map/ppermute | solution.py:370
  107.4 3.4 %collective-permute-start.29 = (f32[1024,128]{1,0:T(8,128)S(1)}, f32[1024,128]{1,0:T(8,128)S(1)}, u32[]{:S(2)}, u32[]{:S(2)}) collective-permute-start(f32[1024,128]{1,0:T(8,128)S(1)} %payload.19.refs_3_), channel_id=1, source_target_pairs={{1,3},{3,5},{5,7},{2,0},{4,2},{6,4},{9,11},{11,13},{13,15},{10,8},... | collective-permute-start | bytes 1572872 | tf_op jit(solution)/shard_map/ppermute | solution.py:370
  110.7 1.0 collective-permute-start.28
  111.8 1.8 %slot_products.15 = (f32[1024,128]{1,0:T(8,128)S(1)}, f32[1024,128]{1,0:T(8,128)S(1)}) custom-call(s32[25]{0:T(128)S(1)} %dynamic-slice_bitcast_fusion.refs_0_, bf16[8192,1024]{1,0:T(8,128)(2,1)S(1)} %copy-done.1, f32[1024,128]{1,0:T(8,128)S(1)} %get-tuple-element.42.refs_2_.refs_3_.refs_1_, f32[1024,128]{1,0:T(8,128)S(1)} %payload.19.refs_3_), custom_call_target="tpu_custom_call" | custom-call | flops 1024 | bytes 1024 | tf_op jit(solution)/shard_map/slot_products/pallas_call | solution.py:39
  113.7 1.9 %two_blocks.12.refs_6_.refs_4_ = f32[256,1024]{1,0:T(8,128)S(1)} custom-call(s32[25]{0:T(128)S(1)} %dynamic-slice_bitcast_fusion.refs_0_, bf16[8192,1024]{1,0:T(8,128)(2,1)S(1)} %copy-done.1, f32[1024,128]{1,0:T(8,128)S(1)} %get-tuple-element.44.refs_3_.refs_2_, f32[1024,128]{1,0:T(8,128)S(1)} %collective-permute-done.23.refs_3_, ...), custom_call_target="tpu_custom_call" | custom-call | flops 1024 | bytes 1024 | tf_op jit(solution)/shard_map/two_blocks/pallas_call | solution.py:39
  116.5 1.9 %collective-permute-start.24 = (f32[1024,128]{1,0:T(8,128)S(1)}, f32[1024,128]{1,0:T(8,128)S(1)}, u32[]{:S(2)}, u32[]{:S(2)}) collective-permute-start(f32[1024,128]{1,0:T(8,128)S(1)} %payload.20.refs_6_), channel_id=1, source_target_pairs={{0,2},{2,4},{4,6},{3,1},{5,3},{7,5},{8,10},{10,12},{12,14},{11,9},... | collective-permute-start | bytes 1572872 | tf_op jit(solution)/shard_map/ppermute | solution.py:370
  118.4 2.8 %collective-permute-done.29.refs_1_.refs_3_ = f32[1024,128]{1,0:T(8,128)S(1)} collective-permute-done((f32[1024,128]{1,0:T(8,128)S(1)}, f32[1024,128]{1,0:T(8,128)S(1)}, u32[]{:S(2)}, u32[]{:S(2)}) %collective-permute-start.29) | collective-permute-done | bytes 524320 | tf_op jit(solution)/shard_map/ppermute | solution.py:370
  121.9 3.0 %collective-permute-start.31 = (f32[1024,128]{1,0:T(8,128)S(1)}, f32[1024,128]{1,0:T(8,128)S(1)}, u32[]{:S(2)}, u32[]{:S(2)}) collective-permute-start(f32[1024,128]{1,0:T(8,128)S(1)} %payload.21.refs_4_), channel_id=1, source_target_pairs={{1,3},{3,5},{5,7},{2,0},{4,2},{6,4},{9,11},{11,13},{13,15},{10,8},... | collective-permute-start | bytes 1572872 | tf_op jit(solution)/shard_map/ppermute | solution.py:370
  124.8 1.9 %collective-permute-start.27 = (f32[32,1024]{1,0:T(8,128)S(1)}, f32[32,1024]{1,0:T(8,128)S(1)}, u32[]{:S(2)}, u32[]{:S(2)}) collective-permute-start(f32[32,1024]{1,0:T(8,128)S(1)} %get-tuple-element.52), channel_id=1, source_target_pairs={{8,0},{16,8},{24,16},{9,1},{17,9},{25,17},{10,2},{18,10},{26,18},{... | collective-permute-start | bytes 393224 | tf_op jit(solution)/shard_map/ppermute | solution.py:283
  126.8 3.4 %collective-permute-start.26 = (f32[32,1024]{1,0:T(8,128)S(1)}, f32[32,1024]{1,0:T(8,128)S(1)}, u32[]{:S(2)}, u32[]{:S(2)}) collective-permute-start(f32[32,1024]{1,0:T(8,128)S(1)} %get-tuple-element.51), channel_id=1, source_target_pairs={{0,8},{8,16},{16,24},{1,9},{9,17},{17,25},{2,10},{10,18},{18,26},{... | collective-permute-start | bytes 393224 | tf_op jit(solution)/shard_map/ppermute | solution.py:282
  130.8 1.9 %two_blocks.13.refs_8_.refs_4_ = f32[256,1024]{1,0:T(8,128)S(1)} custom-call(s32[25]{0:T(128)S(1)} %dynamic-slice_bitcast_fusion.refs_0_, bf16[8192,1024]{1,0:T(8,128)(2,1)S(1)} %copy-done.1, f32[1024,128]{1,0:T(8,128)S(1)} %pick.9.refs_4_.refs_2_, f32[1024,128]{1,0:T(8,128)S(1)} %collective-permute-done.28.refs_3_, ...), custom_call_target="tpu_custom_call" | custom-call | flops 1024 | bytes 1024 | tf_op jit(solution)/shard_map/two_blocks/pallas_call | solution.py:39
  132.6 0.8 collective-permute-done.26.refs_3_
  133.4 7.3 %second_rest.1 = (f32[1024,128]{1,0:T(8,128)S(1)}, f32[1024,128]{1,0:T(8,128)S(1)}, f32[8,256]{1,0:T(8,128)S(1)}) custom-call(f32[1024,256]{1,0:T(8,128)S(1)} %copy-done.3, f32[1024,128]{1,0:T(8,128)S(1)} %get-tuple-element.42.refs_2_.refs_3_.refs_1_, f32[1024,128]{1,0:T(8,128)S(1)} %get-tuple-element.44.refs_3_.refs_2_, ...), custom_call_target="tpu_custom_call" | custom-call | flops 1024 | bytes 1024 | tf_op jit(solution)/shard_map/second_rest/pallas_call | solution.py:39
  140.7 3.7 %collective-permute-start.36 = (f32[2,256]{1,0:T(2,128)S(1)}, f32[2,256]{1,0:T(2,128)S(1)}, u32[]{:S(2)}, u32[]{:S(2)}) collective-permute-start(f32[2,256]{1,0:T(2,128)S(1)} %slice.3), channel_id=1, source_target_pairs={{0,1},{1,0},{2,3},{3,2},{4,5},{5,4},{6,7},{7,6},{8,9},{9,8},{10,11... | collective-permute-start | bytes 6152 | tf_op jit(solution)/shard_map/ppermute | solution.py:479
  144.4 0.8 collective-permute-done.36
  145.3 2.4 %collective-permute-done.37 = f32[2,256]{1,0:T(2,128)S(1)} collective-permute-done((f32[2,256]{1,0:T(2,128)S(1)}, f32[2,256]{1,0:T(2,128)S(1)}, u32[]{:S(2)}, u32[]{:S(2)}) %collective-permute-start.37) | collective-permute-done | bytes 2080 | tf_op jit(solution)/shard_map/ppermute | solution.py:479
  148.1 1.6 collective-permute-start.35
  152.2 2.6 %collective-permute-start.32 = (f32[1024,128]{1,0:T(8,128)S(1)}, f32[1024,128]{1,0:T(8,128)S(1)}, u32[]{:S(2)}, u32[]{:S(2)}) collective-permute-start(f32[1024,128]{1,0:T(8,128)S(1)} %payload.23.refs_5_), channel_id=1, source_target_pairs={{1,3},{3,5},{5,7},{2,0},{4,2},{6,4},{9,11},{11,13},{13,15},{10,8},... | collective-permute-start | bytes 1572872 | tf_op jit(solution)/shard_map/ppermute | solution.py:370
  154.8 2.7 %collective-permute-start.30 = (f32[1024,128]{1,0:T(8,128)S(1)}, f32[1024,128]{1,0:T(8,128)S(1)}, u32[]{:S(2)}, u32[]{:S(2)}) collective-permute-start(f32[1024,128]{1,0:T(8,128)S(1)} %payload.22.refs_6_), channel_id=1, source_target_pairs={{0,2},{2,4},{4,6},{3,1},{5,3},{7,5},{8,10},{10,12},{12,14},{11,9},... | collective-permute-start | bytes 1572872 | tf_op jit(solution)/shard_map/ppermute | solution.py:370
  158.1 1.9 %two_blocks.14.refs_4_.refs_6_ = f32[256,1024]{1,0:T(8,128)S(1)} custom-call(s32[25]{0:T(128)S(1)} %dynamic-slice_bitcast_fusion.refs_0_, bf16[8192,1024]{1,0:T(8,128)(2,1)S(1)} %copy-done.1, f32[1024,128]{1,0:T(8,128)S(1)} %pick.10.refs_5_.refs_2_, f32[1024,128]{1,0:T(8,128)S(1)} %collective-permute-done.35.refs_3_, ...), custom_call_target="tpu_custom_call" | custom-call | flops 1024 | bytes 1024 | tf_op jit(solution)/shard_map/two_blocks/pallas_call | solution.py:39
  160.0 2.0 %two_blocks.15.refs_5_.refs_6_ = f32[1024,128]{1,0:T(8,128)S(1)} custom-call(s32[25]{0:T(128)S(1)} %dynamic-slice_bitcast_fusion.refs_0_, bf16[8192,1024]{1,0:T(8,128)(2,1)S(1)} %copy-done.1, f32[1024,128]{1,0:T(8,128)S(1)} %pick.11.refs_5_.refs_2_, f32[1024,128]{1,0:T(8,128)S(1)} %collective-permute-done.34.refs_3_, ...), custom_call_target="tpu_custom_call" | custom-call | flops 1024 | bytes 1024 | tf_op jit(solution)/shard_map/two_blocks/pallas_call | solution.py:39
  162.0 1.6 collective-permute-done.32.refs_1_
  163.6 4.6 %collective-permute-done.30.refs_0_ = f32[1024,128]{1,0:T(8,128)S(1)} collective-permute-done((f32[1024,128]{1,0:T(8,128)S(1)}, f32[1024,128]{1,0:T(8,128)S(1)}, u32[]{:S(2)}, u32[]{:S(2)}) %collective-permute-start.30) | collective-permute-done | bytes 524320 | tf_op jit(solution)/shard_map/ppermute | solution.py:370
  168.2 1.0 last_sum.1
  (81 shorter events, 15.6 us)
Async XLA Ops:
  0.6 1.2 copy-start.2
  1.9 0.7 copy-start.4
  2.6 0.7 copy-start.6
  3.2 6.2 %copy-start.3 = (f32[1024,256]{1,0:T(8,128)S(1)}, f32[1024,256]{1,0:T(8,128)}, u32[]{:S(2)}) copy-start(f32[1024,256]{1,0:T(8,128)} %refs_0_.7) | copy-start | bytes 3145732
  3.3 21.3 %collective-permute-start.2 = (f32[1040,128]{1,0:T(8,128)S(1)}, f32[1040,128]{1,0:T(8,128)S(1)}, u32[]{:S(2)}, u32[]{:S(2)}) collective-permute-start(f32[1040,128]{1,0:T(8,128)S(1)} %own_rows.1.refs_3_.refs_2_), channel_id=1, source_target_pairs={{1,3},{3,5},{5,7},{2,0},{4,2},{6,4},{9,11},{11,13},{13,15},{10,8},... | collective-permute-start | bytes 1597448 | tf_op jit(solution)/shard_map/ppermute | solution.py:370
  6.6 18.0 %collective-permute-start = (f32[1040,128]{1,0:T(8,128)S(1)}, f32[1040,128]{1,0:T(8,128)S(1)}, u32[]{:S(2)}, u32[]{:S(2)}) collective-permute-start(f32[1040,128]{1,0:T(8,128)S(1)} %own_rows.1.refs_3_.refs_2_), channel_id=1, source_target_pairs={{0,2},{2,4},{4,6},{3,1},{5,3},{7,5},{8,10},{10,12},{12,14},{11,9},... | collective-permute-start | bytes 1597448 | tf_op jit(solution)/shard_map/ppermute | solution.py:370
  9.5 5.8 %copy-start = (bf16[8192,1024]{1,0:T(8,128)(2,1)S(1)}, bf16[8192,1024]{1,0:T(8,128)(2,1)}, u32[]{:S(2)}) copy-start(bf16[8192,1024]{1,0:T(8,128)(2,1)} %refs_1_.33) | copy-start | bytes 50331652
  15.2 5.8 %copy-start.1 = (bf16[8192,1024]{1,0:T(8,128)(2,1)S(1)}, bf16[8192,1024]{1,0:T(8,128)(2,1)}, u32[]{:S(2)}) copy-start(bf16[8192,1024]{1,0:T(8,128)(2,1)} %refs_1_.33) | copy-start | bytes 50331652
  17.0 8.2 %collective-permute-start.1 = (f32[1024,128]{1,0:T(8,128)S(1)}, f32[1024,128]{1,0:T(8,128)S(1)}, u32[]{:S(2)}, u32[]{:S(2)}) collective-permute-start(f32[1024,128]{1,0:T(8,128)S(1)} %get-tuple-element.31), channel_id=1, source_target_pairs={{0,1},{1,0},{2,3},{3,2},{4,5},{5,4},{6,7},{7,6},{8,9},{9,8},{10,11... | collective-permute-start | bytes 1572872 | tf_op jit(solution)/shard_map/ppermute | solution.py:367
  18.3 17.5 %collective-permute-start.5 = (f32[1040,128]{1,0:T(8,128)S(1)}, f32[1040,128]{1,0:T(8,128)S(1)}, u32[]{:S(2)}, u32[]{:S(2)}) collective-permute-start(f32[1040,128]{1,0:T(8,128)S(1)} %own_rows.1.refs_3_.refs_2_), channel_id=1, source_target_pairs={{0,1},{1,0},{2,3},{3,2},{4,5},{5,4},{6,7},{7,6},{8,9},{9,8},{10,11... | collective-permute-start | bytes 1597448 | tf_op jit(solution)/shard_map/ppermute | solution.py:367
  25.8 11.9 %collective-permute-start.3 = (f32[1040,128]{1,0:T(8,128)S(1)}, f32[1040,128]{1,0:T(8,128)S(1)}, u32[]{:S(2)}, u32[]{:S(2)}) collective-permute-start(f32[1040,128]{1,0:T(8,128)S(1)} %payload.12.refs_4_), channel_id=1, source_target_pairs={{0,2},{2,4},{4,6},{3,1},{5,3},{7,5},{8,10},{10,12},{12,14},{11,9},... | collective-permute-start | bytes 1597448 | tf_op jit(solution)/shard_map/ppermute | solution.py:370
  28.4 14.8 %collective-permute-start.11 = (f32[1040,128]{1,0:T(8,128)S(1)}, f32[1040,128]{1,0:T(8,128)S(1)}, u32[]{:S(2)}, u32[]{:S(2)}) collective-permute-start(f32[1040,128]{1,0:T(8,128)S(1)} %payload.13.refs_3_), channel_id=1, source_target_pairs={{1,3},{3,5},{5,7},{2,0},{4,2},{6,4},{9,11},{11,13},{13,15},{10,8},... | collective-permute-start | bytes 1597448 | tf_op jit(solution)/shard_map/ppermute | solution.py:370
  31.7 6.0 %collective-permute-start.4 = (f32[1024,128]{1,0:T(8,128)S(1)}, f32[1024,128]{1,0:T(8,128)S(1)}, u32[]{:S(2)}, u32[]{:S(2)}) collective-permute-start(f32[1024,128]{1,0:T(8,128)S(1)} %get-tuple-element.34), channel_id=1, source_target_pairs={{0,1},{1,0},{2,3},{3,2},{4,5},{5,4},{6,7},{7,6},{8,9},{9,8},{10,11... | collective-permute-start | bytes 1572872 | tf_op jit(solution)/shard_map/ppermute | solution.py:367
  33.6 20.5 %collective-permute-start.10 = (f32[1040,128]{1,0:T(8,128)S(1)}, f32[1040,128]{1,0:T(8,128)S(1)}, u32[]{:S(2)}, u32[]{:S(2)}) collective-permute-start(f32[1040,128]{1,0:T(8,128)S(1)} %pick.6.refs_4_.refs_2_), channel_id=1, source_target_pairs={{0,1},{1,0},{2,3},{3,2},{4,5},{5,4},{6,7},{7,6},{8,9},{9,8},{10,11... | collective-permute-start | bytes 1597448 | tf_op jit(solution)/shard_map/ppermute | solution.py:367
  38.4 12.0 %copy-start.5 = (f32[2,1024]{1,0:T(2,128)S(1)}, f32[2,1024]{1,0:T(2,128)}, u32[]{:S(2)}) copy-start(f32[2,1024]{1,0:T(2,128)} %refs_1_.17) | copy-start | bytes 24580
  38.4 12.0 %copy-start.7 = (f32[1024]{0:T(1024)S(1)}, f32[1024]{0:T(1024)}, u32[]{:S(2)}) copy-start(f32[1024]{0:T(1024)} %param.9) | copy-start | bytes 12292
  38.4 30.4 %collective-permute-start.6 = (f32[1040,128]{1,0:T(8,128)S(1)}, f32[1040,128]{1,0:T(8,128)S(1)}, u32[]{:S(2)}, u32[]{:S(2)}) collective-permute-start(f32[1040,128]{1,0:T(8,128)S(1)} %payload.14.refs_6_), channel_id=1, source_target_pairs={{0,2},{2,4},{4,6},{3,1},{5,3},{7,5},{8,10},{10,12},{12,14},{11,9},... | collective-permute-start | bytes 1597448 | tf_op jit(solution)/shard_map/ppermute | solution.py:370
  43.9 25.6 %collective-permute-start.13 = (f32[1040,128]{1,0:T(8,128)S(1)}, f32[1040,128]{1,0:T(8,128)S(1)}, u32[]{:S(2)}, u32[]{:S(2)}) collective-permute-start(f32[1040,128]{1,0:T(8,128)S(1)} %payload.15.refs_4_), channel_id=1, source_target_pairs={{1,3},{3,5},{5,7},{2,0},{4,2},{6,4},{9,11},{11,13},{13,15},{10,8},... | collective-permute-start | bytes 1597448 | tf_op jit(solution)/shard_map/ppermute | solution.py:370
  47.1 21.7 %collective-permute-start.7 = (f32[1024,128]{1,0:T(8,128)S(1)}, f32[1024,128]{1,0:T(8,128)S(1)}, u32[]{:S(2)}, u32[]{:S(2)}) collective-permute-start(f32[1024,128]{1,0:T(8,128)S(1)} %get-tuple-element.37), channel_id=1, source_target_pairs={{0,1},{1,0},{2,3},{3,2},{4,5},{5,4},{6,7},{7,6},{8,9},{9,8},{10,11... | collective-permute-start | bytes 1572872 | tf_op jit(solution)/shard_map/ppermute | solution.py:367
  50.4 12.4 %collective-permute-start.9 = (f32[32,1024]{1,0:T(8,128)S(1)}, f32[32,1024]{1,0:T(8,128)S(1)}, u32[]{:S(2)}, u32[]{:S(2)}) collective-permute-start(f32[32,1024]{1,0:T(8,128)S(1)} %get-tuple-element.36.refs_4_), channel_id=1, source_target_pairs={{8,0},{16,8},{24,16},{9,1},{17,9},{25,17},{10,2},{18,10},{26,18},{... | collective-permute-start | bytes 393224 | tf_op jit(solution)/shard_map/ppermute | solution.py:283
  54.1 7.6 %collective-permute-start.8 = (f32[32,1024]{1,0:T(8,128)S(1)}, f32[32,1024]{1,0:T(8,128)S(1)}, u32[]{:S(2)}, u32[]{:S(2)}) collective-permute-start(f32[32,1024]{1,0:T(8,128)S(1)} %get-tuple-element.38), channel_id=1, source_target_pairs={{0,8},{8,16},{16,24},{1,9},{9,17},{17,25},{2,10},{10,18},{18,26},{... | collective-permute-start | bytes 393224 | tf_op jit(solution)/shard_map/ppermute | solution.py:282
  56.4 6.4 %copy-start.8 = (s32[256]{0:T(256)S(1)}, s32[256]{0:T(256)}, u32[]{:S(2)}) copy-start(s32[256]{0:T(256)} %param.10) | copy-start | bytes 3076
  61.7 15.7 %collective-permute-start.17 = (f32[1040,128]{1,0:T(8,128)S(1)}, f32[1040,128]{1,0:T(8,128)S(1)}, u32[]{:S(2)}, u32[]{:S(2)}) collective-permute-start(f32[1040,128]{1,0:T(8,128)S(1)} %pick.7.refs_5_.refs_2_), channel_id=1, source_target_pairs={{0,1},{1,0},{2,3},{3,2},{4,5},{5,4},{6,7},{7,6},{8,9},{9,8},{10,11... | collective-permute-start | bytes 1597448 | tf_op jit(solution)/shard_map/ppermute | solution.py:367
  70.8 8.6 %collective-permute-start.16 = (f32[1040,128]{1,0:T(8,128)S(1)}, f32[1040,128]{1,0:T(8,128)S(1)}, u32[]{:S(2)}, u32[]{:S(2)}) collective-permute-start(f32[1040,128]{1,0:T(8,128)S(1)} %pick.8.refs_5_.refs_2_), channel_id=1, source_target_pairs={{0,1},{1,0},{2,3},{3,2},{4,5},{5,4},{6,7},{7,6},{8,9},{9,8},{10,11... | collective-permute-start | bytes 1597448 | tf_op jit(solution)/shard_map/ppermute | solution.py:367
  70.8 13.1 %collective-permute-start.14 = (f32[1040,128]{1,0:T(8,128)S(1)}, f32[1040,128]{1,0:T(8,128)S(1)}, u32[]{:S(2)}, u32[]{:S(2)}) collective-permute-start(f32[1040,128]{1,0:T(8,128)S(1)} %payload.17.refs_5_), channel_id=1, source_target_pairs={{1,3},{3,5},{5,7},{2,0},{4,2},{6,4},{9,11},{11,13},{13,15},{10,8},... | collective-permute-start | bytes 1597448 | tf_op jit(solution)/shard_map/ppermute | solution.py:370
  73.9 13.6 %collective-permute-start.12 = (f32[1040,128]{1,0:T(8,128)S(1)}, f32[1040,128]{1,0:T(8,128)S(1)}, u32[]{:S(2)}, u32[]{:S(2)}) collective-permute-start(f32[1040,128]{1,0:T(8,128)S(1)} %payload.16.refs_6_), channel_id=1, source_target_pairs={{0,2},{2,4},{4,6},{3,1},{5,3},{7,5},{8,10},{10,12},{12,14},{11,9},... | collective-permute-start | bytes 1597448 | tf_op jit(solution)/shard_map/ppermute | solution.py:370
  76.3 6.9 %collective-permute-start.15 = (f32[1024,128]{1,0:T(8,128)S(1)}, f32[1024,128]{1,0:T(8,128)S(1)}, u32[]{:S(2)}, u32[]{:S(2)}) collective-permute-start(f32[1024,128]{1,0:T(8,128)S(1)} %get-tuple-element.40), channel_id=1, source_target_pairs={{0,1},{1,0},{2,3},{3,2},{4,5},{5,4},{6,7},{7,6},{8,9},{9,8},{10,11... | collective-permute-start | bytes 1572872 | tf_op jit(solution)/shard_map/ppermute | solution.py:367
  87.8 13.6 %collective-permute-start.20 = (f32[1024,128]{1,0:T(8,128)S(1)}, f32[1024,128]{1,0:T(8,128)S(1)}, u32[]{:S(2)}, u32[]{:S(2)}) collective-permute-start(f32[1024,128]{1,0:T(8,128)S(1)} %get-tuple-element.44.refs_3_.refs_2_), channel_id=1, source_target_pairs={{1,3},{3,5},{5,7},{2,0},{4,2},{6,4},{9,11},{11,13},{13,15},{10,8},... | collective-permute-start | bytes 1572872 | tf_op jit(solution)/shard_map/ppermute | solution.py:370
  90.8 12.8 %collective-permute-start.18 = (f32[1024,128]{1,0:T(8,128)S(1)}, f32[1024,128]{1,0:T(8,128)S(1)}, u32[]{:S(2)}, u32[]{:S(2)}) collective-permute-start(f32[1024,128]{1,0:T(8,128)S(1)} %get-tuple-element.44.refs_3_.refs_2_), channel_id=1, source_target_pairs={{0,2},{2,4},{4,6},{3,1},{5,3},{7,5},{8,10},{10,12},{12,14},{11,9},... | collective-permute-start | bytes 1572872 | tf_op jit(solution)/shard_map/ppermute | solution.py:370
  93.1 11.1 %collective-permute-start.19 = (f32[1024,128]{1,0:T(8,128)S(1)}, f32[1024,128]{1,0:T(8,128)S(1)}, u32[]{:S(2)}, u32[]{:S(2)}) collective-permute-start(f32[1024,128]{1,0:T(8,128)S(1)} %get-tuple-element.45), channel_id=1, source_target_pairs={{0,1},{1,0},{2,3},{3,2},{4,5},{5,4},{6,7},{7,6},{8,9},{9,8},{10,11... | collective-permute-start | bytes 1572872 | tf_op jit(solution)/shard_map/ppermute | solution.py:367
  93.5 20.1 %collective-permute-start.23 = (f32[1024,128]{1,0:T(8,128)S(1)}, f32[1024,128]{1,0:T(8,128)S(1)}, u32[]{:S(2)}, u32[]{:S(2)}) collective-permute-start(f32[1024,128]{1,0:T(8,128)S(1)} %get-tuple-element.44.refs_3_.refs_2_), channel_id=1, source_target_pairs={{0,1},{1,0},{2,3},{3,2},{4,5},{5,4},{6,7},{7,6},{8,9},{9,8},{10,11... | collective-permute-start | bytes 1572872 | tf_op jit(solution)/shard_map/ppermute | solution.py:367
  95.5 20.0 %collective-permute-start.22 = (f32[1024,128]{1,0:T(8,128)S(1)}, f32[1024,128]{1,0:T(8,128)S(1)}, u32[]{:S(2)}, u32[]{:S(2)}) collective-permute-start(f32[1024,128]{1,0:T(8,128)S(1)} %get-tuple-element.48), channel_id=1, source_target_pairs={{0,1},{1,0},{2,3},{3,2},{4,5},{5,4},{6,7},{7,6},{8,9},{9,8},{10,11... | collective-permute-start | bytes 1572872 | tf_op jit(solution)/shard_map/ppermute | solution.py:367
  104.8 11.0 %collective-permute-start.21 = (f32[1024,128]{1,0:T(8,128)S(1)}, f32[1024,128]{1,0:T(8,128)S(1)}, u32[]{:S(2)}, u32[]{:S(2)}) collective-permute-start(f32[1024,128]{1,0:T(8,128)S(1)} %payload.18.refs_4_), channel_id=1, source_target_pairs={{0,2},{2,4},{4,6},{3,1},{5,3},{7,5},{8,10},{10,12},{12,14},{11,9},... | collective-permute-start | bytes 1572872 | tf_op jit(solution)/shard_map/ppermute | solution.py:370
  107.4 13.9 %collective-permute-start.29 = (f32[1024,128]{1,0:T(8,128)S(1)}, f32[1024,128]{1,0:T(8,128)S(1)}, u32[]{:S(2)}, u32[]{:S(2)}) collective-permute-start(f32[1024,128]{1,0:T(8,128)S(1)} %payload.19.refs_3_), channel_id=1, source_target_pairs={{1,3},{3,5},{5,7},{2,0},{4,2},{6,4},{9,11},{11,13},{13,15},{10,8},... | collective-permute-start | bytes 1572872 | tf_op jit(solution)/shard_map/ppermute | solution.py:370
  110.7 16.1 %collective-permute-start.28 = (f32[1024,128]{1,0:T(8,128)S(1)}, f32[1024,128]{1,0:T(8,128)S(1)}, u32[]{:S(2)}, u32[]{:S(2)}) collective-permute-start(f32[1024,128]{1,0:T(8,128)S(1)} %pick.9.refs_4_.refs_2_), channel_id=1, source_target_pairs={{0,1},{1,0},{2,3},{3,2},{4,5},{5,4},{6,7},{7,6},{8,9},{9,8},{10,11... | collective-permute-start | bytes 1572872 | tf_op jit(solution)/shard_map/ppermute | solution.py:367
  113.6 36.0 %collective-permute-start.25 = (f32[1024,128]{1,0:T(8,128)S(1)}, f32[1024,128]{1,0:T(8,128)S(1)}, u32[]{:S(2)}, u32[]{:S(2)}) collective-permute-start(f32[1024,128]{1,0:T(8,128)S(1)} %get-tuple-element.50), channel_id=1, source_target_pairs={{0,1},{1,0},{2,3},{3,2},{4,5},{5,4},{6,7},{7,6},{8,9},{9,8},{10,11... | collective-permute-start | bytes 1572872 | tf_op jit(solution)/shard_map/ppermute | solution.py:367
  116.5 33.2 %collective-permute-start.24 = (f32[1024,128]{1,0:T(8,128)S(1)}, f32[1024,128]{1,0:T(8,128)S(1)}, u32[]{:S(2)}, u32[]{:S(2)}) collective-permute-start(f32[1024,128]{1,0:T(8,128)S(1)} %payload.20.refs_6_), channel_id=1, source_target_pairs={{0,2},{2,4},{4,6},{3,1},{5,3},{7,5},{8,10},{10,12},{12,14},{11,9},... | collective-permute-start | bytes 1572872 | tf_op jit(solution)/shard_map/ppermute | solution.py:370
  121.9 28.5 %collective-permute-start.31 = (f32[1024,128]{1,0:T(8,128)S(1)}, f32[1024,128]{1,0:T(8,128)S(1)}, u32[]{:S(2)}, u32[]{:S(2)}) collective-permute-start(f32[1024,128]{1,0:T(8,128)S(1)} %payload.21.refs_4_), channel_id=1, source_target_pairs={{1,3},{3,5},{5,7},{2,0},{4,2},{6,4},{9,11},{11,13},{13,15},{10,8},... | collective-permute-start | bytes 1572872 | tf_op jit(solution)/shard_map/ppermute | solution.py:370
  124.8 7.8 %collective-permute-start.27 = (f32[32,1024]{1,0:T(8,128)S(1)}, f32[32,1024]{1,0:T(8,128)S(1)}, u32[]{:S(2)}, u32[]{:S(2)}) collective-permute-start(f32[32,1024]{1,0:T(8,128)S(1)} %get-tuple-element.52), channel_id=1, source_target_pairs={{8,0},{16,8},{24,16},{9,1},{17,9},{25,17},{10,2},{18,10},{26,18},{... | collective-permute-start | bytes 393224 | tf_op jit(solution)/shard_map/ppermute | solution.py:283
  126.8 6.6 %collective-permute-start.26 = (f32[32,1024]{1,0:T(8,128)S(1)}, f32[32,1024]{1,0:T(8,128)S(1)}, u32[]{:S(2)}, u32[]{:S(2)}) collective-permute-start(f32[32,1024]{1,0:T(8,128)S(1)} %get-tuple-element.51), channel_id=1, source_target_pairs={{0,8},{8,16},{16,24},{1,9},{9,17},{17,25},{2,10},{10,18},{18,26},{... | collective-permute-start | bytes 393224 | tf_op jit(solution)/shard_map/ppermute | solution.py:282
  140.7 4.5 %collective-permute-start.36 = (f32[2,256]{1,0:T(2,128)S(1)}, f32[2,256]{1,0:T(2,128)S(1)}, u32[]{:S(2)}, u32[]{:S(2)}) collective-permute-start(f32[2,256]{1,0:T(2,128)S(1)} %slice.3), channel_id=1, source_target_pairs={{0,1},{1,0},{2,3},{3,2},{4,5},{5,4},{6,7},{7,6},{8,9},{9,8},{10,11... | collective-permute-start | bytes 6152 | tf_op jit(solution)/shard_map/ppermute | solution.py:479
  145.3 2.4 %collective-permute-start.37 = (f32[2,256]{1,0:T(2,128)S(1)}, f32[2,256]{1,0:T(2,128)S(1)}, u32[]{:S(2)}, u32[]{:S(2)}) collective-permute-start(f32[2,256]{1,0:T(2,128)S(1)} %slice_add_fusion), channel_id=1, source_target_pairs={{0,2},{1,3},{2,0},{3,1},{4,6},{5,7},{6,4},{7,5},{8,10},{9,11},{10,... | collective-permute-start | bytes 6152 | tf_op jit(solution)/shard_map/ppermute | solution.py:479
  147.7 7.1 %collective-permute-start.38 = (f32[2,256]{1,0:T(2,128)S(1)}, f32[2,256]{1,0:T(2,128)S(1)}, u32[]{:S(2)}, u32[]{:S(2)}) collective-permute-start(f32[2,256]{1,0:T(2,128)S(1)} %add.14), channel_id=1, source_target_pairs={{0,4},{1,5},{2,6},{3,7},{4,0},{5,1},{6,2},{7,3},{8,12},{9,13},{10,... | collective-permute-start | bytes 6152 | tf_op jit(solution)/shard_map/ppermute | solution.py:479
  148.1 10.0 %collective-permute-start.35 = (f32[1024,128]{1,0:T(8,128)S(1)}, f32[1024,128]{1,0:T(8,128)S(1)}, u32[]{:S(2)}, u32[]{:S(2)}) collective-permute-start(f32[1024,128]{1,0:T(8,128)S(1)} %pick.10.refs_5_.refs_2_), channel_id=1, source_target_pairs={{0,1},{1,0},{2,3},{3,2},{4,5},{5,4},{6,7},{7,6},{8,9},{9,8},{10,11... | collective-permute-start | bytes 1572872 | tf_op jit(solution)/shard_map/ppermute | solution.py:367
  151.6 8.4 %collective-permute-start.34 = (f32[1024,128]{1,0:T(8,128)S(1)}, f32[1024,128]{1,0:T(8,128)S(1)}, u32[]{:S(2)}, u32[]{:S(2)}) collective-permute-start(f32[1024,128]{1,0:T(8,128)S(1)} %pick.11.refs_5_.refs_2_), channel_id=1, source_target_pairs={{0,1},{1,0},{2,3},{3,2},{4,5},{5,4},{6,7},{7,6},{8,9},{9,8},{10,11... | collective-permute-start | bytes 1572872 | tf_op jit(solution)/shard_map/ppermute | solution.py:367
  151.7 10.3 %collective-permute-start.33 = (f32[1024,128]{1,0:T(8,128)S(1)}, f32[1024,128]{1,0:T(8,128)S(1)}, u32[]{:S(2)}, u32[]{:S(2)}) collective-permute-start(f32[1024,128]{1,0:T(8,128)S(1)} %get-tuple-element.55), channel_id=1, source_target_pairs={{0,1},{1,0},{2,3},{3,2},{4,5},{5,4},{6,7},{7,6},{8,9},{9,8},{10,11... | collective-permute-start | bytes 1572872 | tf_op jit(solution)/shard_map/ppermute | solution.py:367
  152.2 11.4 %collective-permute-start.32 = (f32[1024,128]{1,0:T(8,128)S(1)}, f32[1024,128]{1,0:T(8,128)S(1)}, u32[]{:S(2)}, u32[]{:S(2)}) collective-permute-start(f32[1024,128]{1,0:T(8,128)S(1)} %payload.23.refs_5_), channel_id=1, source_target_pairs={{1,3},{3,5},{5,7},{2,0},{4,2},{6,4},{9,11},{11,13},{13,15},{10,8},... | collective-permute-start | bytes 1572872 | tf_op jit(solution)/shard_map/ppermute | solution.py:370
  154.8 13.4 %collective-permute-start.30 = (f32[1024,128]{1,0:T(8,128)S(1)}, f32[1024,128]{1,0:T(8,128)S(1)}, u32[]{:S(2)}, u32[]{:S(2)}) collective-permute-start(f32[1024,128]{1,0:T(8,128)S(1)} %payload.22.refs_6_), channel_id=1, source_target_pairs={{0,2},{2,4},{4,6},{3,1},{5,3},{7,5},{8,10},{10,12},{12,14},{11,9},... | collective-permute-start | bytes 1572872 | tf_op jit(solution)/shard_map/ppermute | solution.py:370

commit v4 on v3

v4 whole, which is shorter than its diff:
```python
import functools

import numpy as np

import jax
import jax.numpy as jnp
from jax import lax
from jax.experimental import pallas as pl
from jax.experimental.pallas import tpu as pltpu
from jax.sharding import PartitionSpec as P

NY = 16
HALO = 2 * NY
LANES = 128
SMALL = 32


relax_rate = 0.5
time_step = 0.5

VMEM = pl.BlockSpec(memory_space=pltpu.VMEM)
ANY = pl.BlockSpec(memory_space=pl.ANY)
HBM = pl.BlockSpec(memory_space=pltpu.HBM)


class Chain:
    def __init__(self):
        self.last = None

    def __call__(self, kernel, outs, arrays, places=None, scratch=(), out_specs=None, room=16):
        extra = [] if self.last is None else [self.last]
        skip = len(extra)
        first = len(arrays)

        def body(*refs):
            kernel(*refs[:first], *refs[first + skip :])

        results = pl.pallas_call(
            body,
            out_shape=[
                jax.ShapeDtypeStruct(shape, jnp.float32) if isinstance(shape, tuple) else shape
                for shape in outs
            ],
            in_specs=list(places or [VMEM] * len(arrays)) + [ANY] * skip,
            out_specs=out_specs or [VMEM] * len(outs),
            scratch_shapes=list(scratch),
            compiler_params=pltpu.CompilerParams(vmem_limit_bytes=room * 1024 * 1024),
            cost_estimate=pl.CostEstimate(flops=1024, bytes_accessed=1024, transcendentals=0),
            name=getattr(kernel, "func", kernel).__name__,
        )(*arrays, *extra)
        self.last = results[0]
        return results


def halves(value):
    high = value.astype(jnp.bfloat16)
    low = (value - high.astype(jnp.float32)).astype(jnp.bfloat16)
    return high, low


def for_device(numbers):
    if len(set(numbers)) == 1:
        return numbers[0]
    me = lax.axis_index("mode")
    chosen = jnp.int32(numbers[0])
    for device, number in enumerate(numbers[1:], 1):
        chosen = jnp.where(me == device, jnp.int32(number), chosen)
    return chosen


def rows_of(matrix, block):
    modes = matrix.shape[1]
    return pl.ds(pl.multiple_of(block * modes, modes), modes)


def one_slot(blocks, matrix, parts, mine, other):
    cells = mine.shape[1]
    for block, out in zip(blocks, (mine, other)):
        both = jnp.dot(matrix[rows_of(matrix, block), :], parts, preferred_element_type=jnp.float32)
        out[...] = both[:, :cells] + both[:, cells:]


def slot_products(blocks, matrix, field, mine, other):
    blocks = [for_device(numbers) for numbers in blocks]
    parts = jnp.concatenate(halves(field[...]), axis=1)
    one_slot(blocks, matrix, parts, mine, other)


def load_and_products(blocks, column, matrix, distribution, *refs):
    slots = len(blocks)
    outs, (held, field, sems) = refs[: 2 * slots], refs[2 * slots :]
    cells = field.shape[1]
    start = pltpu.make_async_copy(
        distribution.at[:, pl.ds(column, cells)], field, sems.at[2 * slots]
    )
    start.start()
    blocks = [[for_device(numbers) for numbers in pair] for pair in blocks]
    copies = []
    for slot, pair in enumerate(blocks):
        for k, block in enumerate(pair):
            rows = rows_of(held, block)
            copies.append(
                pltpu.make_async_copy(
                    matrix.at[rows, :], held.at[rows, :], sems.at[2 * slot + k]
                )
            )
            copies[-1].start()
    start.wait()
    parts = jnp.concatenate(halves(field[...]), axis=1)
    for slot, pair in enumerate(blocks):
        for k in range(2):
            copies[2 * slot + k].wait()
        one_slot(pair, held, parts, outs[2 * slot], outs[2 * slot + 1])


def two_blocks(numbers, first, last, scale, rows, matrix, *refs):
    modes = matrix.shape[1]
    blocks, refs = refs[:2], refs[2:]
    if not first:
        before, refs = refs[0], refs[1:]
    if last:
        base, refs = refs[0], refs[1:]
    total = None if first else before[...]
    for k, block in enumerate(blocks):
        pieces = list(halves(block[:modes].T))
        if rows:
            weights = [
                jnp.concatenate(
                    [
                        block[modes + i : modes + i + 1, :]
                        for i in range(d * modes // LANES, (d + 1) * modes // LANES)
                    ],
                    axis=1,
                )
                for d in range(2)
            ]
            weights.append(jnp.zeros((6, modes), jnp.float32))
            pieces += halves(jnp.concatenate(weights, axis=0))
        left = jnp.concatenate(pieces, axis=0)
        there = rows_of(matrix, for_device(numbers[k]))
        term = jnp.dot(left, matrix[there, :], preferred_element_type=jnp.float32)
        total = term if total is None else total + term
    if not last:
        refs[0][...] = total
        return
    cells = base.shape[1]
    value = base[...] - scale * (total[:cells] + total[cells : 2 * cells]).T
    refs[0][...] = value
    if rows:
        refs[1][...] = value.T[:HALO]
        refs[2][...] = total[2 * cells : 2 * cells + 8] + total[2 * cells + 8 :]


def own_rows(distribution, velocity, capacity, out, speeds, weight, sems):
    modes, cells = (velocity.shape[1], out.shape[1])
    copies = [
        pltpu.make_async_copy(velocity, speeds, sems.at[0]),
        pltpu.make_async_copy(capacity, weight, sems.at[1]),
        pltpu.make_async_copy(
            distribution.at[:, pl.ds(0, cells)], out.at[pl.ds(0, modes), :], sems.at[2]
        ),
    ]
    for copy in copies:
        copy.start()
    for copy in copies[:2]:
        copy.wait()
    per = modes // LANES
    out[modes:] = jnp.zeros((out.shape[0] - modes, LANES), jnp.float32)
    for d in range(2):
        for i in range(per):
            lanes = slice(i * LANES, (i + 1) * LANES)
            out[modes + d * per + i : modes + d * per + i + 1, :] = (
                speeds[d : d + 1, lanes] * weight[:, lanes]
            )
    copies[2].wait()


def payload(numbers, slots, arrived, *refs):
    out = refs[-1]
    slot_here = for_device(numbers)

    for k, slot in enumerate(slots):

        @pl.when(slot_here == slot)
        def _(k=k):
            mine, theirs = refs[2 * k], refs[2 * k + 1]
            modes = mine.shape[0]
            out[:modes] = arrived[:modes] + (mine[...] + theirs[...])
            if out.shape[0] > modes:
                out[modes:] = arrived[modes:]

    @pl.when(slot_here < 0)
    def _():
        out[...] = arrived[...]


def pick(numbers, *refs):
    out = refs[-1]
    choice = for_device(numbers)
    for k, ref in enumerate(refs[:-1]):

        @pl.when(choice == k)
        def _(ref=ref):
            out[...] = ref[...]


def add(one, two, out):
    out[...] = one[...] + two[...]


def turn_sum(scale, one, two, mine, theirs, base, out, strip):
    modes = mine.shape[0]
    total = one[:modes] + two[:modes] + (mine[...] + theirs[...])
    value = base[...] - scale * total
    out[...] = value
    strip[...] = value.T[-HALO:]


def last_sum(scale, one, two, mine, theirs, base, other, out, value, sems):
    cells = base.shape[1]
    ahead = pltpu.make_async_copy(other, out.at[:, pl.ds(cells, cells)], sems.at[0])
    ahead.start()
    total = one[...] + two[...] + (mine[...] + theirs[...])
    value[...] = base[...] - scale * total
    copy = pltpu.make_async_copy(value, out.at[:, pl.ds(0, cells)], sems.at[1])
    copy.start()
    ahead.wait()
    copy.wait()


def strip_rows(distribution, leading, last):
    cells = distribution.shape[1]
    leading[...] = distribution[:, :LANES].T[:HALO]
    last[...] = distribution[:, cells - LANES :].T[-HALO:]


def strip_pairs(leading, last, out_even, out_odd):
    even = lax.axis_index("space") % 2 == 0

    @pl.when(even)
    def _():
        out_even[...] = last[...]
        out_odd[...] = leading[...]

    @pl.when(jnp.logical_not(even))
    def _():
        out_even[...] = leading[...]
        out_odd[...] = last[...]


def still_rate(pieces, before, after, columns, kinds):
    lane = lax.broadcasted_iota(jnp.int32, (1, LANES), 1)
    y = lane % NY
    vx, vy, capacity = (columns[:, i : i + 1] for i in range(3))
    fore_x, back_x = 0.5 * jnp.maximum(vx, 0.0), 0.5 * jnp.minimum(vx, 0.0)
    fore_y, back_y = 0.5 * jnp.maximum(vy, 0.0), 0.5 * jnp.minimum(vy, 0.0)
    centre = 3.0 * (fore_x - back_x + fore_y - back_y)
    padded = [before, *pieces, after]
    rates = []
    for k, value in enumerate(pieces):
        def along_x(offset):
            near = pltpu.roll(value, -offset % LANES, 1)
            if offset < 0:
                return jnp.where(lane < -offset, pltpu.roll(padded[k], -offset, 1), near)
            return jnp.where(
                lane >= LANES - offset, pltpu.roll(padded[k + 2], LANES - offset, 1), near
            )

        def along_y(offset):
            inside = (y + offset >= 0) & (y + offset < NY)
            return jnp.where(inside, pltpu.roll(value, -offset % LANES, 1), 0.0)

        kind = kinds[:, k * LANES : (k + 1) * LANES]
        contact = jnp.where(kind > 0, relax_rate, 0.0)
        source = jnp.where(kind == 1, contact, -contact)
        rate = (
            source * capacity
            - (centre + contact) * value
            + fore_x * (4.0 * along_x(-NY) - along_x(-2 * NY))
            + back_x * (along_x(2 * NY) - 4.0 * along_x(NY))
            + fore_y * (4.0 * along_y(-1) - along_y(-2))
            + back_y * (along_y(2) - 4.0 * along_y(1))
        )
        rates.append(rate)
    return rates


def edges(came_even, came_odd, rows):
    even = lax.axis_index("space") % 2 == 0
    from_even, from_odd = came_even[:, rows].T, came_odd[:, rows].T
    before = jnp.where(even, from_odd, from_even)
    after = jnp.where(even, from_even, from_odd)
    pad = jnp.zeros((before.shape[0], LANES - HALO), jnp.float32)
    return (
        jnp.concatenate([pad, before], axis=1),
        jnp.concatenate([after, pad], axis=1),
    )


def pieces_of(value):
    return [value[:, k : k + LANES] for k in range(0, value.shape[1], LANES)]


def first_rest(field, came_even, came_odd, table, kinds, base_a, base_b):
    modes, half = base_a.shape
    block = min(modes, LANES)
    small = min(block, SMALL)

    def step(i, _):
        start = pl.multiple_of(i * block, block)
        before, after = edges(came_even, came_odd, pl.ds(start, block))
        columns = table[:, pl.ds(start, block)].T
        for k in range(0, block, small):
            rows = pl.ds(pl.multiple_of(start + k, small), small)
            here = slice(k, k + small)
            pieces = pieces_of(field[rows, :])
            rates = still_rate(pieces, before[here], after[here], columns[here], kinds[...])
            middle = len(pieces) // 2
            for j, (piece, rate) in enumerate(zip(pieces, rates)):
                out, at = (base_a, j) if j < middle else (base_b, j - middle)
                out[rows, at * LANES : (at + 1) * LANES] = piece + time_step * rate
        return 0

    lax.fori_loop(0, modes // block, step, 0)


def second_rest(
    field, mid_a, mid_b, came_even, came_odd, table, kinds, scattered, end_a, end_b, flux
):
    modes, half = end_a.shape
    cells = field.shape[1]
    block = min(modes, LANES)
    small = min(block, SMALL)
    step_size = 0.5 * time_step

    def step(i, sums):
        start = pl.multiple_of(i * block, block)
        before, after = edges(came_even, came_odd, pl.ds(start, block))
        columns = table[:, pl.ds(start, block)].T
        taken = step_size * scattered[:, pl.ds(start, block)].T
        sums = list(sums)
        for k in range(0, block, small):
            rows = pl.ds(pl.multiple_of(start + k, small), small)
            here = slice(k, k + small)
            values = pieces_of(field[rows, :])
            mids = pieces_of(mid_a[rows, :]) + pieces_of(mid_b[rows, :])
            rates = still_rate(mids, before[here], after[here], columns[here], kinds[...])
            middle = len(mids) // 2
            for j, (value, mid, rate) in enumerate(zip(values, mids, rates)):
                out, at = (end_a, j) if j < middle else (end_b, j - middle)
                end = 0.5 * (value + mid) + step_size * rate
                out[rows, at * LANES : (at + 1) * LANES] = end
                for d in range(2):
                    terms = columns[here, 3 + d : 4 + d] * end - taken[here, d : d + 1] * mid
                    folded = sum(terms[r : r + 8] for r in range(0, small, 8))
                    sums[2 * j + d] = sums[2 * j + d] + folded
        return tuple(sums)

    zero = jnp.zeros((8, LANES), jnp.float32)
    sums = lax.fori_loop(0, modes // block, step, (zero,) * (2 * cells // LANES))
    for j in range(cells // LANES):
        for d in range(2):
            flux[d : d + 1, j * LANES : (j + 1) * LANES] = jnp.sum(
                sums[2 * j + d], axis=0, keepdims=True
            )


def paired(to_even, to_odd):
    count = lax.axis_size("space")
    came = []
    for first, value in enumerate((to_even, to_odd)):
        pairs = [(i, i + 1) for i in range(first, count - 1, 2)]
        came.append(lax.ppermute(value, "space", pairs + [(j, i) for i, j in pairs]))
    return came


class Plan:
    def __init__(self, chips):
        self.chips = chips
        self.devices = range(2 * chips)
        sources = [self.sources(d) for d in self.devices]
        targets = [self.targets(d // 2) for d in self.devices]
        self.blocks = [
            [
                [2 * sources[e][slot][2] + e % 2 for e in (d ^ other for d in self.devices)]
                for other in (0, 1)
            ]
            for slot in range(chips)
        ]
        self.rows = [
            [[2 * targets[d][slot] + (d % 2 ^ other) for d in self.devices] for other in (0, 1)]
            for slot in range(chips)
        ]
        self.choices = [
            sorted({sources[d][slot][:2] for d in self.devices}) for slot in range(chips)
        ]
        self.picked = [
            [self.choices[slot].index(sources[d][slot][:2]) for d in self.devices]
            for slot in range(chips)
        ]
        self.sent = {}
        for stream in (0, 1):
            for step in range(1, chips):
                numbers = []
                for d in self.devices:
                    way = self.way(d, stream)
                    place = d // 2 if way > 0 else chips - 1 - d // 2
                    target = d // 2 + way * (chips - step)
                    numbers.append(targets[d].index(target) if place < step else -1)
                self.sent[stream, step] = numbers
        self.pairs = []
        for stream in (0, 1):
            up = [
                (d, d + 2) for d in self.devices[:-2] if self.way(d, stream) > 0
            ]
            self.pairs.append(up + [(j, i) for i, j in up])

    def way(self, device, stream):
        return 1 if (device // 2 + device % 2 + stream) % 2 == 0 else -1

    def sources(self, device):
        found = [(-1, -1, device // 2)]
        for step in range(self.chips - 1):
            for stream in (step % 2, 1 - step % 2):
                chip = device // 2 + self.way(device, stream) * (step + 1)
                if 0 <= chip < self.chips:
                    found.append((stream, step, chip))
        return found

    def targets(self, chip):
        found = []
        for step in range(1, self.chips):
            far = self.chips - step
            found += [t for t in (chip + far, chip - far) if 0 <= t < self.chips]
        return found + [chip]


def on_device(distribution, scatter_matrix, velocity, capacity, cell_type):
    modes, cells = distribution.shape
    total_modes = scatter_matrix.shape[0]
    half = cells // 2
    extra = -(-2 * modes // LANES // 8) * 8
    step_size = 0.5 * time_step
    part = (modes, half)
    devices = lax.axis_size("mode")
    chips = devices // 2
    plan = Plan(chips)
    call = Chain()
    across = [(i, i ^ 1) for i in range(devices)]
    cap = capacity[None, :]
    table = jnp.concatenate(
        [velocity, cap, cap * velocity, jnp.zeros((3, modes), jnp.float32)], axis=0
    )
    kinds = cell_type[None, :]

    def exchange(value):
        return lax.ppermute(value, "mode", across)

    def along(stream, value):
        return lax.ppermute(value, "mode", plan.pairs[stream])

    class Round:
        def __init__(self, matrix, scale, rows):
            self.matrix, self.scale, self.rows = matrix, scale, rows
            self.terms, self.total = [], None

        def begin(self, own):
            self.own = own
            self.arrived = [[along(0, own)], [along(1, own)]]
            self.blocks = []

        def add_terms(self, field):
            kernel = functools.partial(slot_products, plan.rows[len(self.terms)])
            mine, other = call(kernel, [part] * 2, [self.matrix, field])
            self.terms.append((mine, exchange(other)))

        def take_own(self):
            self.blocks.append((self.own, exchange(self.own)))

        def send(self, step):
            sent = {}
            for stream in (step % 2, 1 - step % 2):
                numbers = plan.sent[stream, step]
                slots = sorted({n for n in numbers if n >= 0})
                arrived = self.arrived[1 - stream][step - 1]
                kernel = functools.partial(payload, numbers, slots)
                arrays = [arrived] + [a for s in slots for a in self.terms[s]]
                (value,) = call(kernel, [arrived.shape], arrays)
                sent[stream] = along(stream, value)
            for stream in (0, 1):
                self.arrived[stream].append(sent[stream])

        def take(self, slot):
            arrays = [self.arrived[stream][step] for stream, step in plan.choices[slot]]
            kernel = functools.partial(pick, plan.picked[slot])
            (here,) = call(kernel, [arrays[0].shape], arrays)
            self.blocks.append((here, exchange(here)))

        def multiply(self, slot, base=None):
            first, last = slot == 0, base is not None
            kernel = functools.partial(
                two_blocks, plan.blocks[slot], first, last, self.scale, self.rows
            )
            arrays = [self.matrix, *self.blocks[slot]]
            arrays += [] if first else [self.total]
            arrays += [base] if last else []
            outs = [(2 * half + (16 if self.rows else 0), modes)]
            if last:
                outs = [part, (HALO, modes), (8, modes)] if self.rows else [part]
            results = call(kernel, outs, arrays)
            self.total = results[0]
            return results

        def ends(self):
            return [self.arrived[0][-1], self.arrived[1][-1], *self.terms[-1]]

    (own,) = call(
        own_rows,
        [(modes + extra, half)],
        [distribution, velocity, cap],
        places=[HBM] * 3,
        scratch=[
            pltpu.VMEM((2, modes), jnp.float32),
            pltpu.VMEM((1, modes), jnp.float32),
            pltpu.SemaphoreType.DMA((3,)),
        ],
        room=56,
    )
    one = Round(None, time_step, True)
    one.begin(own)
    *terms, matrix = call(
        functools.partial(load_and_products, plan.rows, half),
        [part] * (2 * chips) + [jax.ShapeDtypeStruct(scatter_matrix.shape, jnp.bfloat16)],
        [scatter_matrix, distribution],
        places=[HBM] * 2,
        scratch=[
            pltpu.VMEM(part, jnp.float32),
            pltpu.SemaphoreType.DMA((2 * chips + 1,)),
        ],
        room=28,
    )
    one.matrix = matrix
    one.terms = [(terms[2 * s], exchange(terms[2 * s + 1])) for s in range(chips)]
    one.take_own()
    for step in range(1, chips):
        if step in (1, chips - 1):
            one.take(step)
        one.send(step)
        if step not in (1, chips - 1):
            one.take(step)
        if step == 1:
            strips = call(strip_rows, [(HALO, modes)] * 2, [distribution])
            strips = paired(*call(strip_pairs, [(HALO, modes)] * 2, strips))
        one.multiply(step - 1)
        if step == min(2, chips - 1):
            base_a, base_b = call(
                first_rest, [part] * 2, [distribution, *strips, table, kinds]
            )
    mid_a, leading, scattered = one.multiply(chips - 1, base_a)

    two = Round(matrix, step_size, False)
    two.add_terms(mid_a)
    mid_b, last = call(
        functools.partial(turn_sum, time_step), [part, (HALO, modes)], [*one.ends(), base_b]
    )
    two.begin(mid_b)
    for slot in range(1, chips - 1):
        two.add_terms(mid_a)
    two.take_own()
    strips = paired(*call(strip_pairs, [(HALO, modes)] * 2, [leading, last]))
    for step in range(1, chips):
        if step in (1, chips - 1):
            two.take(step)
        two.send(step)
        if step not in (1, chips - 1):
            two.take(step)
        if step == 1:
            two.add_terms(mid_a)
        two.multiply(step - 1)
        if step == 1:
            end_a, end_b, flux = call(
                second_rest,
                [part, part, (2, cells)],
                [distribution, mid_a, mid_b, *strips, table, kinds, scattered],
            )
        else:
            flux = sum_pairs(call, flux, devices, step - 1, chips - 1)
    heat_flux = flux / jnp.sqrt(jnp.float32(total_modes))
    (last_b,) = two.multiply(chips - 1, end_b)
    (updated,) = call(
        functools.partial(last_sum, step_size),
        [(modes, cells)],
        [*two.ends(), end_a, last_b],
        scratch=[pltpu.VMEM(part, jnp.float32), pltpu.SemaphoreType.DMA((2,))],
        out_specs=[HBM],
    )
    return (updated, heat_flux)


def sum_pairs(call, value, devices, turn, turns):
    bits = [1 << k for k in range(devices.bit_length() - 1)]
    share = -(-len(bits) // (turns - 1))
    for bit in bits[(turn - 1) * share : turn * share]:
        came = lax.ppermute(value, "mode", [(i, i ^ bit) for i in range(devices)])
        (value,) = call(add, [value.shape], [value, came])
    return value


def solution(mesh):
    return jax.shard_map(
        on_device,
        mesh=mesh,
        in_specs=(P("mode", "space"), P(None, "mode"), P(None, "mode"), P("mode"), P("space")),
        out_specs=(P("mode", "space"), P(None, "space")),
        check_vma=False,
    )
```

time: 172 us -> 157 us (0.913); the launches traced: 169 us -> 156 us
  waiting for transfers between devices: 29.9 us -> 46.3 us
  Pallas kernels: 55.8 us -> 44.2 us
  local copies, waits for them, and re-layouts: 11.8 us -> 1.14 us
  starting transfers between devices: 69.8 us -> 62.6 us
    ppermute x23, waiting for transfers between devices: 29.9 us -> 46.2 us  [the longest x16 27.9 us: along(): return lax.ppermute(value, 'mode', plan.pairs[stream])]
    pallas_call x40 -> x42, Pallas kernels: 55.8 us -> 44.2 us  [__call__(): pl.pallas_call(body, out_shape=[jax.ShapeDtypeStruct(shape, jnp.float32)...]
    unnamed x18 -> x10, local copies, waits for them, and re-layouts: 11 us -> 1.06 us
    ppermute x23, starting transfers between devices: 56.8 us -> 52.3 us  [the longest x16 42.4 us: along(): return lax.ppermute(value, 'mode', plan.pairs[stream])]
    ppermute x16, starting transfers between devices: 13 us -> 10.3 us  [exchange(): return lax.ppermute(value, 'mode', across)]
  transfers between devices with their start and end apart: 39 -> 39, of which waited for: 13 -> 14; matrix products, arithmetic and copies ran while one was open for 1% -> 0% of each run, Pallas kernels for 32% -> 26%
where the time goes in v4:
time: 157 us; the launch traced here: 156 us
  starting transfers between devices  62.6 us (40%)
  waiting for transfers between devices  46.3 us (29%)
  Pallas kernels  44.2 us (28%)
    pallas_call x42, Pallas kernels, __call__(): pl.pallas_call(body, out_shape=[jax.ShapeDtypeStruct(shape, jnp.float32)...  44.2 us
    ppermute x16, starting transfers between devices, along(): return lax.ppermute(value, 'mode', plan.pairs[stream])  42.4 us
    ppermute x16, waiting for transfers between devices, along(): return lax.ppermute(value, 'mode', plan.pairs[stream])  27.9 us
    ppermute x3, waiting for transfers between devices, sum_pairs(): came = lax.ppermute(value, 'mode', [(i, i ^ bit) for i in range(devices)])  10.9 us
    ppermute x16, starting transfers between devices, exchange(): return lax.ppermute(value, 'mode', across)  10.3 us
    ppermute x4, waiting for transfers between devices, paired(): lax.ppermute(value, 'space', pairs + [(j, i) for i, j in pairs])  7.48 us
    ppermute x4, starting transfers between devices, paired(): lax.ppermute(value, 'space', pairs + [(j, i) for i, j in pairs])  6.2 us
    ppermute x3, starting transfers between devices, sum_pairs(): came = lax.ppermute(value, 'mode', [(i, i ^ bit) for i in range(devices)])  3.63 us
  transfers between devices with their start and end apart: 39, of which 14 were waited for; matrix products, arithmetic and copies ran while one was open for 0% of the time, Pallas kernels for 26%

profile of v4, /device:TPU:13, one launch (start us, length us, event | category | flops | bytes accessed | tf_op | source)
XLA Modules:
  0.0 156.3 jit_solution(6647627951941173958)
XLA Ops:
  0.6 2.0 %own_rows.1.refs_2_.refs_1_ = f32[1040,128]{1,0:T(8,128)} custom-call(f32[1024,256]{1,0:T(8,128)} %refs_0_.9, f32[2,1024]{1,0:T(2,128)} %refs_1_.2, f32[1,1024]{1,0:T(1,128)} %bitcast.4), custom_call_target="tpu_custom_call" | custom-call | flops 1024 | bytes 1024 | tf_op jit(solution)/shard_map/own_rows/pallas_call | solution.py:38
  2.6 2.1 %collective-permute-start = (f32[1040,128]{1,0:T(8,128)}, f32[1040,128]{1,0:T(8,128)S(1)}, u32[]{:S(2)}, u32[]{:S(2)}) collective-permute-start(f32[1040,128]{1,0:T(8,128)} %own_rows.1.refs_2_.refs_1_), channel_id=1, source_target_pairs={{1,3},{2,4},{5,7},{3,1},{4,2},{7,5},{9,11},{10,12},{13,15},{11,9},... | collective-permute-start | bytes 1597448 | tf_op jit(solution)/shard_map/ppermute | solution.py:460
  4.7 4.3 %collective-permute-start.2 = (f32[1040,128]{1,0:T(8,128)}, f32[1040,128]{1,0:T(8,128)S(1)}, u32[]{:S(2)}, u32[]{:S(2)}) collective-permute-start(f32[1040,128]{1,0:T(8,128)} %own_rows.1.refs_2_.refs_1_), channel_id=1, source_target_pairs={{0,2},{3,5},{4,6},{2,0},{5,3},{6,4},{8,10},{11,13},{12,14},{10,8},... | collective-permute-start | bytes 1597448 | tf_op jit(solution)/shard_map/ppermute | solution.py:460
  9.1 1.0 copy-done.1
  10.1 7.4 %load_and_products.1 = (f32[1024,128]{1,0:T(8,128)S(1)}, f32[1024,128]{1,0:T(8,128)S(1)}, f32[1024,128]{1,0:T(8,128)S(1)}, f32[1024,128]{1,0:T(8,128)S(1)}, f32[...) custom-call(bf16[8192,1024]{1,0:T(8,128)(2,1)} %refs_0_.6, ...), custom_call_target="tpu_custom_call" | custom-call | flops 1024 | bytes 1024 | tf_op jit(solution)/shard_map/load_and_products/pallas_call | solution.py:38
  17.6 0.5 collective-permute-start.6
  18.1 1.6 %collective-permute-done.2.refs_0_ = f32[1040,128]{1,0:T(8,128)S(1)} collective-permute-done((f32[1040,128]{1,0:T(8,128)}, f32[1040,128]{1,0:T(8,128)S(1)}, u32[]{:S(2)}, u32[]{:S(2)}) %collective-permute-start.2) | collective-permute-done | bytes 532512 | tf_op jit(solution)/shard_map/ppermute | solution.py:460
  19.8 2.7 %collective-permute-start.5 = (f32[1040,128]{1,0:T(8,128)S(1)}, f32[1040,128]{1,0:T(8,128)S(1)}, u32[]{:S(2)}, u32[]{:S(2)}) collective-permute-start(f32[1040,128]{1,0:T(8,128)S(1)} %payload.12.refs_3_), channel_id=1, source_target_pairs={{1,3},{2,4},{5,7},{3,1},{4,2},{7,5},{9,11},{10,12},{13,15},{11,9},... | collective-permute-start | bytes 1597448 | tf_op jit(solution)/shard_map/ppermute | solution.py:460
  22.6 2.5 %collective-permute-start.3 = (f32[1040,128]{1,0:T(8,128)S(1)}, f32[1040,128]{1,0:T(8,128)S(1)}, u32[]{:S(2)}, u32[]{:S(2)}) collective-permute-start(f32[1040,128]{1,0:T(8,128)S(1)} %payload.13.refs_1_), channel_id=1, source_target_pairs={{0,2},{3,5},{4,6},{2,0},{5,3},{6,4},{8,10},{11,13},{12,14},{10,8},... | collective-permute-start | bytes 1597448 | tf_op jit(solution)/shard_map/ppermute | solution.py:460
  25.1 0.5 collective-permute-start.12
  26.0 1.4 two_blocks.8.refs_5_.refs_3_
  27.4 4.8 %collective-permute-done.5.refs_0_.refs_2_ = f32[1040,128]{1,0:T(8,128)S(1)} collective-permute-done((f32[1040,128]{1,0:T(8,128)S(1)}, f32[1040,128]{1,0:T(8,128)S(1)}, u32[]{:S(2)}, u32[]{:S(2)}) %collective-permute-start.5) | collective-permute-done | bytes 532512 | tf_op jit(solution)/shard_map/ppermute | solution.py:460
  32.3 3.5 %collective-permute-done.3.refs_0_ = f32[1040,128]{1,0:T(8,128)S(1)} collective-permute-done((f32[1040,128]{1,0:T(8,128)S(1)}, f32[1040,128]{1,0:T(8,128)S(1)}, u32[]{:S(2)}, u32[]{:S(2)}) %collective-permute-start.3) | collective-permute-done | bytes 532512 | tf_op jit(solution)/shard_map/ppermute | solution.py:460
  35.9 1.9 %collective-permute-start.7 = (f32[1040,128]{1,0:T(8,128)S(1)}, f32[1040,128]{1,0:T(8,128)S(1)}, u32[]{:S(2)}, u32[]{:S(2)}) collective-permute-start(f32[1040,128]{1,0:T(8,128)S(1)} %payload.15.refs_3_), channel_id=1, source_target_pairs={{1,3},{2,4},{5,7},{3,1},{4,2},{7,5},{9,11},{10,12},{13,15},{11,9},... | collective-permute-start | bytes 1597448 | tf_op jit(solution)/shard_map/ppermute | solution.py:460
  37.8 3.2 %collective-permute-start.9 = (f32[1040,128]{1,0:T(8,128)S(1)}, f32[1040,128]{1,0:T(8,128)S(1)}, u32[]{:S(2)}, u32[]{:S(2)}) collective-permute-start(f32[1040,128]{1,0:T(8,128)S(1)} %payload.14.refs_5_), channel_id=1, source_target_pairs={{0,2},{3,5},{4,6},{2,0},{5,3},{6,4},{8,10},{11,13},{12,14},{10,8},... | collective-permute-start | bytes 1597448 | tf_op jit(solution)/shard_map/ppermute | solution.py:460
  41.0 0.8 collective-permute-start.8
  41.9 1.3 collective-permute-start.10
  43.2 2.1 %collective-permute-start.11 = (f32[32,1024]{1,0:T(8,128)S(1)}, f32[32,1024]{1,0:T(8,128)S(1)}, u32[]{:S(2)}, u32[]{:S(2)}) collective-permute-start(f32[32,1024]{1,0:T(8,128)S(1)} %get-tuple-element.45), channel_id=1, source_target_pairs={{8,16},{16,8},{9,17},{17,9},{10,18},{18,10},{11,19},{19,11},{12,20... | collective-permute-start | bytes 393224 | tf_op jit(solution)/shard_map/ppermute | solution.py:373
  45.4 1.4 two_blocks.9.refs_5_.refs_3_
  47.1 0.8 collective-permute-start.17
  47.9 2.9 %collective-permute-done.11.refs_2_ = f32[32,1024]{1,0:T(8,128)S(1)} collective-permute-done((f32[32,1024]{1,0:T(8,128)S(1)}, f32[32,1024]{1,0:T(8,128)S(1)}, u32[]{:S(2)}, u32[]{:S(2)}) %collective-permute-start.11) | collective-permute-done | bytes 131104 | tf_op jit(solution)/shard_map/ppermute | solution.py:373
  50.8 7.3 %first_rest.1 = (f32[1024,128]{1,0:T(8,128)S(1)}, f32[1024,128]{1,0:T(8,128)S(1)}) custom-call(f32[1024,256]{1,0:T(8,128)S(1)} %copy-done, f32[32,1024]{1,0:T(8,128)S(1)} %collective-permute-done.10.refs_1_, f32[32,1024]{1,0:T(8,128)S(1)} %collective-permute-done.11.refs_2_, f32[8,1024]{1,0:T(8,128)S(1)} %maximum_maximum_fusion.refs_3_.refs_5_, ...), custom_call_target="tpu_custom_call" | custom-call | flops 1024 | bytes 1024 | tf_op jit(solution)/shard_map/first_rest/pallas_call | solution.py:38
  58.2 1.2 collective-permute-start.16
  59.6 2.1 %collective-permute-start.13 = (f32[1040,128]{1,0:T(8,128)S(1)}, f32[1040,128]{1,0:T(8,128)S(1)}, u32[]{:S(2)}, u32[]{:S(2)}) collective-permute-start(f32[1040,128]{1,0:T(8,128)S(1)} %payload.17.refs_4_), channel_id=1, source_target_pairs={{0,2},{3,5},{4,6},{2,0},{5,3},{6,4},{8,10},{11,13},{12,14},{10,8},... | collective-permute-start | bytes 1597448 | tf_op jit(solution)/shard_map/ppermute | solution.py:460
  61.7 2.4 %collective-permute-start.14 = (f32[1040,128]{1,0:T(8,128)S(1)}, f32[1040,128]{1,0:T(8,128)S(1)}, u32[]{:S(2)}, u32[]{:S(2)}) collective-permute-start(f32[1040,128]{1,0:T(8,128)S(1)} %payload.16.refs_5_), channel_id=1, source_target_pairs={{1,3},{2,4},{5,7},{3,1},{4,2},{7,5},{9,11},{10,12},{13,15},{11,9},... | collective-permute-start | bytes 1597448 | tf_op jit(solution)/shard_map/ppermute | solution.py:460
  64.1 2.0 %collective-permute-start.15 = (f32[1024,128]{1,0:T(8,128)S(1)}, f32[1024,128]{1,0:T(8,128)S(1)}, u32[]{:S(2)}, u32[]{:S(2)}) collective-permute-start(f32[1024,128]{1,0:T(8,128)S(1)} %get-tuple-element.48), channel_id=1, source_target_pairs={{0,1},{1,0},{2,3},{3,2},{4,5},{5,4},{6,7},{7,6},{8,9},{9,8},{10,11... | collective-permute-start | bytes 1572872 | tf_op jit(solution)/shard_map/ppermute | solution.py:457
  66.1 1.4 two_blocks.10.refs_3_.refs_5_
  67.5 1.5 two_blocks.11
  69.1 1.3 slot_products.4
  70.3 0.8 collective-permute-done.13.refs_0_
  71.2 4.6 %collective-permute-done.14.refs_1_ = f32[1040,128]{1,0:T(8,128)S(1)} collective-permute-done((f32[1040,128]{1,0:T(8,128)S(1)}, f32[1040,128]{1,0:T(8,128)S(1)}, u32[]{:S(2)}, u32[]{:S(2)}) %collective-permute-start.14) | collective-permute-done | bytes 532512 | tf_op jit(solution)/shard_map/ppermute | solution.py:460
  76.1 3.7 %collective-permute-start.18 = (f32[1024,128]{1,0:T(8,128)S(1)}, f32[1024,128]{1,0:T(8,128)S(1)}, u32[]{:S(2)}, u32[]{:S(2)}) collective-permute-start(f32[1024,128]{1,0:T(8,128)S(1)} %get-tuple-element.52.refs_2_.refs_1_), channel_id=1, source_target_pairs={{1,3},{2,4},{5,7},{3,1},{4,2},{7,5},{9,11},{10,12},{13,15},{11,9},... | collective-permute-start | bytes 1572872 | tf_op jit(solution)/shard_map/ppermute | solution.py:460
  79.8 2.0 %collective-permute-start.20 = (f32[1024,128]{1,0:T(8,128)S(1)}, f32[1024,128]{1,0:T(8,128)S(1)}, u32[]{:S(2)}, u32[]{:S(2)}) collective-permute-start(f32[1024,128]{1,0:T(8,128)S(1)} %get-tuple-element.52.refs_2_.refs_1_), channel_id=1, source_target_pairs={{0,2},{3,5},{4,6},{2,0},{5,3},{6,4},{8,10},{11,13},{12,14},{10,8},... | collective-permute-start | bytes 1572872 | tf_op jit(solution)/shard_map/ppermute | solution.py:460
  81.8 0.5 collective-permute-start.26
  82.3 1.3 slot_products.5
  83.6 1.3 slot_products.6
  85.0 4.8 %collective-permute-done.18.refs_1_.refs_0_ = f32[1024,128]{1,0:T(8,128)S(1)} collective-permute-done((f32[1024,128]{1,0:T(8,128)S(1)}, f32[1024,128]{1,0:T(8,128)S(1)}, u32[]{:S(2)}, u32[]{:S(2)}) %collective-permute-start.18) | collective-permute-done | bytes 524320 | tf_op jit(solution)/shard_map/ppermute | solution.py:460
  89.9 2.4 %collective-permute-done.20.refs_0_ = f32[1024,128]{1,0:T(8,128)S(1)} collective-permute-done((f32[1024,128]{1,0:T(8,128)S(1)}, f32[1024,128]{1,0:T(8,128)S(1)}, u32[]{:S(2)}, u32[]{:S(2)}) %collective-permute-start.20) | collective-permute-done | bytes 524320 | tf_op jit(solution)/shard_map/ppermute | solution.py:460
  92.4 1.9 %collective-permute-start.23 = (f32[1024,128]{1,0:T(8,128)S(1)}, f32[1024,128]{1,0:T(8,128)S(1)}, u32[]{:S(2)}, u32[]{:S(2)}) collective-permute-start(f32[1024,128]{1,0:T(8,128)S(1)} %payload.18.refs_3_), channel_id=1, source_target_pairs={{1,3},{2,4},{5,7},{3,1},{4,2},{7,5},{9,11},{10,12},{13,15},{11,9},... | collective-permute-start | bytes 1572872 | tf_op jit(solution)/shard_map/ppermute | solution.py:460
  94.4 2.1 %collective-permute-start.21 = (f32[1024,128]{1,0:T(8,128)S(1)}, f32[1024,128]{1,0:T(8,128)S(1)}, u32[]{:S(2)}, u32[]{:S(2)}) collective-permute-start(f32[1024,128]{1,0:T(8,128)S(1)} %payload.19.refs_2_), channel_id=1, source_target_pairs={{0,2},{3,5},{4,6},{2,0},{5,3},{6,4},{8,10},{11,13},{12,14},{10,8},... | collective-permute-start | bytes 1572872 | tf_op jit(solution)/shard_map/ppermute | solution.py:460
  96.6 4.3 %collective-permute-done.24.refs_3_ = f32[32,1024]{1,0:T(8,128)S(1)} collective-permute-done((f32[32,1024]{1,0:T(8,128)S(1)}, f32[32,1024]{1,0:T(8,128)S(1)}, u32[]{:S(2)}, u32[]{:S(2)}) %collective-permute-start.24) | collective-permute-done | bytes 131104 | tf_op jit(solution)/shard_map/ppermute | solution.py:373
  100.8 2.8 %collective-permute-start.25 = (f32[32,1024]{1,0:T(8,128)S(1)}, f32[32,1024]{1,0:T(8,128)S(1)}, u32[]{:S(2)}, u32[]{:S(2)}) collective-permute-start(f32[32,1024]{1,0:T(8,128)S(1)} %get-tuple-element.60), channel_id=1, source_target_pairs={{8,16},{16,8},{9,17},{17,9},{10,18},{18,10},{11,19},{19,11},{12,20... | collective-permute-start | bytes 393224 | tf_op jit(solution)/shard_map/ppermute | solution.py:373
  103.6 2.0 %collective-permute-start.31 = (f32[1024,128]{1,0:T(8,128)S(1)}, f32[1024,128]{1,0:T(8,128)S(1)}, u32[]{:S(2)}, u32[]{:S(2)}) collective-permute-start(f32[1024,128]{1,0:T(8,128)S(1)} %pick.9.refs_3_.refs_1_), channel_id=1, source_target_pairs={{0,1},{1,0},{2,3},{3,2},{4,5},{5,4},{6,7},{7,6},{8,9},{9,8},{10,11... | collective-permute-start | bytes 1572872 | tf_op jit(solution)/shard_map/ppermute | solution.py:457
  105.6 1.3 slot_products.7
  106.9 1.3 two_blocks.12.refs_8_.refs_3_
  108.2 8.7 %second_rest.1 = (f32[1024,128]{1,0:T(8,128)S(1)}, f32[1024,128]{1,0:T(8,128)S(1)}, f32[2,256]{1,0:T(2,128)S(1)}) custom-call(f32[1024,256]{1,0:T(8,128)S(1)} %copy-done, f32[1024,128]{1,0:T(8,128)S(1)} %get-tuple-element.50.refs_1_.refs_2_, f32[1024,128]{1,0:T(8,128)S(1)} %get-tuple-element.52.refs_2_.refs_1_, ...), custom_call_target="tpu_custom_call" | custom-call | flops 1024 | bytes 1024 | tf_op jit(solution)/shard_map/second_rest/pallas_call | solution.py:38
  117.1 3.3 %collective-permute-start.27 = (f32[1024,128]{1,0:T(8,128)S(1)}, f32[1024,128]{1,0:T(8,128)S(1)}, u32[]{:S(2)}, u32[]{:S(2)}) collective-permute-start(f32[1024,128]{1,0:T(8,128)S(1)} %payload.21.refs_3_), channel_id=1, source_target_pairs={{1,3},{2,4},{5,7},{3,1},{4,2},{7,5},{9,11},{10,12},{13,15},{11,9},... | collective-permute-start | bytes 1572872 | tf_op jit(solution)/shard_map/ppermute | solution.py:460
  120.3 3.3 %collective-permute-start.29 = (f32[1024,128]{1,0:T(8,128)S(1)}, f32[1024,128]{1,0:T(8,128)S(1)}, u32[]{:S(2)}, u32[]{:S(2)}) collective-permute-start(f32[1024,128]{1,0:T(8,128)S(1)} %payload.20.refs_5_), channel_id=1, source_target_pairs={{0,2},{3,5},{4,6},{2,0},{5,3},{6,4},{8,10},{11,13},{12,14},{10,8},... | collective-permute-start | bytes 1572872 | tf_op jit(solution)/shard_map/ppermute | solution.py:460
  123.6 0.9 collective-permute-start.28
  124.7 0.5 collective-permute-start.30
  125.2 1.3 two_blocks.13.refs_2_.refs_3_
  126.5 0.3 collective-permute-done.30.refs_1_
  126.9 1.7 %collective-permute-start.32 = (f32[2,256]{1,0:T(2,128)S(1)}, f32[2,256]{1,0:T(2,128)S(1)}, u32[]{:S(2)}, u32[]{:S(2)}) collective-permute-start(f32[2,256]{1,0:T(2,128)S(1)} %add.3.refs_0_.refs_2_), channel_id=1, source_target_pairs={{0,2},{1,3},{2,0},{3,1},{4,6},{5,7},{6,4},{7,5},{8,10},{9,11},{10,... | collective-permute-start | bytes 6152 | tf_op jit(solution)/shard_map/ppermute | solution.py:604
  128.6 1.4 collective-permute-done.32.refs_1_
  129.9 5.1 %collective-permute-done.29.refs_1_.refs_0_ = f32[1024,128]{1,0:T(8,128)S(1)} collective-permute-done((f32[1024,128]{1,0:T(8,128)S(1)}, f32[1024,128]{1,0:T(8,128)S(1)}, u32[]{:S(2)}, u32[]{:S(2)}) %collective-permute-start.29) | collective-permute-done | bytes 524320 | tf_op jit(solution)/shard_map/ppermute | solution.py:460
  135.4 0.5 collective-permute-start.35
  136.0 3.2 %collective-permute-start.33 = (f32[1024,128]{1,0:T(8,128)S(1)}, f32[1024,128]{1,0:T(8,128)S(1)}, u32[]{:S(2)}, u32[]{:S(2)}) collective-permute-start(f32[1024,128]{1,0:T(8,128)S(1)} %payload.23.refs_4_), channel_id=1, source_target_pairs={{0,2},{3,5},{4,6},{2,0},{5,3},{6,4},{8,10},{11,13},{12,14},{10,8},... | collective-permute-start | bytes 1572872 | tf_op jit(solution)/shard_map/ppermute | solution.py:460
  139.2 1.9 %collective-permute-start.34 = (f32[1024,128]{1,0:T(8,128)S(1)}, f32[1024,128]{1,0:T(8,128)S(1)}, u32[]{:S(2)}, u32[]{:S(2)}) collective-permute-start(f32[1024,128]{1,0:T(8,128)S(1)} %payload.22.refs_5_), channel_id=1, source_target_pairs={{1,3},{2,4},{5,7},{3,1},{4,2},{7,5},{9,11},{10,12},{13,15},{11,9},... | collective-permute-start | bytes 1572872 | tf_op jit(solution)/shard_map/ppermute | solution.py:460
  141.2 1.4 collective-permute-start.38
  142.6 1.3 two_blocks.14.refs_2_.refs_3_
  143.9 9.2 %collective-permute-done.38.refs_1_ = f32[2,256]{1,0:T(2,128)S(1)} collective-permute-done((f32[2,256]{1,0:T(2,128)S(1)}, f32[2,256]{1,0:T(2,128)S(1)}, u32[]{:S(2)}, u32[]{:S(2)}) %collective-permute-start.38) | collective-permute-done | bytes 2080 | tf_op jit(solution)/shard_map/ppermute | solution.py:604
  153.1 0.6 broadcast_multiply_fusion.1
  153.7 1.4 two_blocks.15.refs_5_.refs_6_
  155.2 1.0 last_sum.1
  (71 shorter events, 3.0 us)
Async XLA Ops:
  0.6 8.4 %copy-start = (f32[1024,256]{1,0:T(8,128)S(1)}, f32[1024,256]{1,0:T(8,128)}, u32[]{:S(2)}) copy-start(f32[1024,256]{1,0:T(8,128)} %refs_0_.9) | copy-start | bytes 3145732
  2.6 15.4 %collective-permute-start = (f32[1040,128]{1,0:T(8,128)}, f32[1040,128]{1,0:T(8,128)S(1)}, u32[]{:S(2)}, u32[]{:S(2)}) collective-permute-start(f32[1040,128]{1,0:T(8,128)} %own_rows.1.refs_2_.refs_1_), channel_id=1, source_target_pairs={{1,3},{2,4},{5,7},{3,1},{4,2},{7,5},{9,11},{10,12},{13,15},{11,9},... | collective-permute-start | bytes 1597448 | tf_op jit(solution)/shard_map/ppermute | solution.py:460
  4.7 15.0 %collective-permute-start.2 = (f32[1040,128]{1,0:T(8,128)}, f32[1040,128]{1,0:T(8,128)S(1)}, u32[]{:S(2)}, u32[]{:S(2)}) collective-permute-start(f32[1040,128]{1,0:T(8,128)} %own_rows.1.refs_2_.refs_1_), channel_id=1, source_target_pairs={{0,2},{3,5},{4,6},{2,0},{5,3},{6,4},{8,10},{11,13},{12,14},{10,8},... | collective-permute-start | bytes 1597448 | tf_op jit(solution)/shard_map/ppermute | solution.py:460
  9.1 1.0 copy-start.1
  17.5 2.3 %collective-permute-start.1 = (f32[1024,128]{1,0:T(8,128)S(1)}, f32[1024,128]{1,0:T(8,128)S(1)}, u32[]{:S(2)}, u32[]{:S(2)}) collective-permute-start(f32[1024,128]{1,0:T(8,128)S(1)} %get-tuple-element.36), channel_id=1, source_target_pairs={{0,1},{1,0},{2,3},{3,2},{4,5},{5,4},{6,7},{7,6},{8,9},{9,8},{10,11... | collective-permute-start | bytes 1572872 | tf_op jit(solution)/shard_map/ppermute | solution.py:457
  17.6 8.4 %collective-permute-start.6 = (f32[1040,128]{1,0:T(8,128)S(1)}, f32[1040,128]{1,0:T(8,128)S(1)}, u32[]{:S(2)}, u32[]{:S(2)}) collective-permute-start(f32[1040,128]{1,0:T(8,128)S(1)} %copy-done.1), channel_id=1, source_target_pairs={{0,1},{1,0},{2,3},{3,2},{4,5},{5,4},{6,7},{7,6},{8,9},{9,8},{10,11... | collective-permute-start | bytes 1597448 | tf_op jit(solution)/shard_map/ppermute | solution.py:457
  19.8 12.4 %collective-permute-start.5 = (f32[1040,128]{1,0:T(8,128)S(1)}, f32[1040,128]{1,0:T(8,128)S(1)}, u32[]{:S(2)}, u32[]{:S(2)}) collective-permute-start(f32[1040,128]{1,0:T(8,128)S(1)} %payload.12.refs_3_), channel_id=1, source_target_pairs={{1,3},{2,4},{5,7},{3,1},{4,2},{7,5},{9,11},{10,12},{13,15},{11,9},... | collective-permute-start | bytes 1597448 | tf_op jit(solution)/shard_map/ppermute | solution.py:460
  22.6 13.3 %collective-permute-start.3 = (f32[1040,128]{1,0:T(8,128)S(1)}, f32[1040,128]{1,0:T(8,128)S(1)}, u32[]{:S(2)}, u32[]{:S(2)}) collective-permute-start(f32[1040,128]{1,0:T(8,128)S(1)} %payload.13.refs_1_), channel_id=1, source_target_pairs={{0,2},{3,5},{4,6},{2,0},{5,3},{6,4},{8,10},{11,13},{12,14},{10,8},... | collective-permute-start | bytes 1597448 | tf_op jit(solution)/shard_map/ppermute | solution.py:460
  25.0 2.3 %collective-permute-start.4 = (f32[1024,128]{1,0:T(8,128)S(1)}, f32[1024,128]{1,0:T(8,128)S(1)}, u32[]{:S(2)}, u32[]{:S(2)}) collective-permute-start(f32[1024,128]{1,0:T(8,128)S(1)} %get-tuple-element.38), channel_id=1, source_target_pairs={{0,1},{1,0},{2,3},{3,2},{4,5},{5,4},{6,7},{7,6},{8,9},{9,8},{10,11... | collective-permute-start | bytes 1572872 | tf_op jit(solution)/shard_map/ppermute | solution.py:457
  25.1 18.1 %collective-permute-start.12 = (f32[1040,128]{1,0:T(8,128)S(1)}, f32[1040,128]{1,0:T(8,128)S(1)}, u32[]{:S(2)}, u32[]{:S(2)}) collective-permute-start(f32[1040,128]{1,0:T(8,128)S(1)} %pick.6.refs_3_.refs_1_), channel_id=1, source_target_pairs={{0,1},{1,0},{2,3},{3,2},{4,5},{5,4},{6,7},{7,6},{8,9},{9,8},{10,11... | collective-permute-start | bytes 1597448 | tf_op jit(solution)/shard_map/ppermute | solution.py:457
  32.3 9.6 %copy-start.3 = (f32[2,1024]{1,0:T(2,128)S(1)}, f32[2,1024]{1,0:T(2,128)}, u32[]{:S(2)}) copy-start(f32[2,1024]{1,0:T(2,128)} %refs_1_.2) | copy-start | bytes 24580
  32.3 9.6 %copy-start.4 = (f32[1024]{0:T(1024)S(1)}, f32[1024]{0:T(1024)}, u32[]{:S(2)}) copy-start(f32[1024]{0:T(1024)} %param.8) | copy-start | bytes 12292
  35.9 22.2 %collective-permute-start.7 = (f32[1040,128]{1,0:T(8,128)S(1)}, f32[1040,128]{1,0:T(8,128)S(1)}, u32[]{:S(2)}, u32[]{:S(2)}) collective-permute-start(f32[1040,128]{1,0:T(8,128)S(1)} %payload.15.refs_3_), channel_id=1, source_target_pairs={{1,3},{2,4},{5,7},{3,1},{4,2},{7,5},{9,11},{10,12},{13,15},{11,9},... | collective-permute-start | bytes 1597448 | tf_op jit(solution)/shard_map/ppermute | solution.py:460
  37.8 20.3 %collective-permute-start.9 = (f32[1040,128]{1,0:T(8,128)S(1)}, f32[1040,128]{1,0:T(8,128)S(1)}, u32[]{:S(2)}, u32[]{:S(2)}) collective-permute-start(f32[1040,128]{1,0:T(8,128)S(1)} %payload.14.refs_5_), channel_id=1, source_target_pairs={{0,2},{3,5},{4,6},{2,0},{5,3},{6,4},{8,10},{11,13},{12,14},{10,8},... | collective-permute-start | bytes 1597448 | tf_op jit(solution)/shard_map/ppermute | solution.py:460
  41.0 18.4 %collective-permute-start.8 = (f32[1024,128]{1,0:T(8,128)S(1)}, f32[1024,128]{1,0:T(8,128)S(1)}, u32[]{:S(2)}, u32[]{:S(2)}) collective-permute-start(f32[1024,128]{1,0:T(8,128)S(1)} %get-tuple-element.44), channel_id=1, source_target_pairs={{0,1},{1,0},{2,3},{3,2},{4,5},{5,4},{6,7},{7,6},{8,9},{9,8},{10,11... | collective-permute-start | bytes 1572872 | tf_op jit(solution)/shard_map/ppermute | solution.py:457
  41.9 5.2 %collective-permute-start.10 = (f32[32,1024]{1,0:T(8,128)S(1)}, f32[32,1024]{1,0:T(8,128)S(1)}, u32[]{:S(2)}, u32[]{:S(2)}) collective-permute-start(f32[32,1024]{1,0:T(8,128)S(1)} %get-tuple-element.42.refs_3_), channel_id=1, source_target_pairs={{0,8},{16,24},{8,0},{24,16},{1,9},{17,25},{9,1},{25,17},{2,10},{18... | collective-permute-start | bytes 393224 | tf_op jit(solution)/shard_map/ppermute | solution.py:373
  43.2 7.6 %collective-permute-start.11 = (f32[32,1024]{1,0:T(8,128)S(1)}, f32[32,1024]{1,0:T(8,128)S(1)}, u32[]{:S(2)}, u32[]{:S(2)}) collective-permute-start(f32[32,1024]{1,0:T(8,128)S(1)} %get-tuple-element.45), channel_id=1, source_target_pairs={{8,16},{16,8},{9,17},{17,9},{10,18},{18,10},{11,19},{19,11},{12,20... | collective-permute-start | bytes 393224 | tf_op jit(solution)/shard_map/ppermute | solution.py:373
  45.4 5.4 %copy-start.2 = (s32[256]{0:T(256)S(1)}, s32[256]{0:T(256)}, u32[]{:S(2)}) copy-start(s32[256]{0:T(256)} %param.9) | copy-start | bytes 3076
  47.1 19.1 %collective-permute-start.17 = (f32[1040,128]{1,0:T(8,128)S(1)}, f32[1040,128]{1,0:T(8,128)S(1)}, u32[]{:S(2)}, u32[]{:S(2)}) collective-permute-start(f32[1040,128]{1,0:T(8,128)S(1)} %pick.7.refs_4_.refs_1_), channel_id=1, source_target_pairs={{0,1},{1,0},{2,3},{3,2},{4,5},{5,4},{6,7},{7,6},{8,9},{9,8},{10,11... | collective-permute-start | bytes 1597448 | tf_op jit(solution)/shard_map/ppermute | solution.py:457
  58.2 9.3 %collective-permute-start.16 = (f32[1040,128]{1,0:T(8,128)S(1)}, f32[1040,128]{1,0:T(8,128)S(1)}, u32[]{:S(2)}, u32[]{:S(2)}) collective-permute-start(f32[1040,128]{1,0:T(8,128)S(1)} %pick.8.refs_5_.refs_1_), channel_id=1, source_target_pairs={{0,1},{1,0},{2,3},{3,2},{4,5},{5,4},{6,7},{7,6},{8,9},{9,8},{10,11... | collective-permute-start | bytes 1597448 | tf_op jit(solution)/shard_map/ppermute | solution.py:457
  59.6 11.6 %collective-permute-start.13 = (f32[1040,128]{1,0:T(8,128)S(1)}, f32[1040,128]{1,0:T(8,128)S(1)}, u32[]{:S(2)}, u32[]{:S(2)}) collective-permute-start(f32[1040,128]{1,0:T(8,128)S(1)} %payload.17.refs_4_), channel_id=1, source_target_pairs={{0,2},{3,5},{4,6},{2,0},{5,3},{6,4},{8,10},{11,13},{12,14},{10,8},... | collective-permute-start | bytes 1597448 | tf_op jit(solution)/shard_map/ppermute | solution.py:460
  61.7 14.1 %collective-permute-start.14 = (f32[1040,128]{1,0:T(8,128)S(1)}, f32[1040,128]{1,0:T(8,128)S(1)}, u32[]{:S(2)}, u32[]{:S(2)}) collective-permute-start(f32[1040,128]{1,0:T(8,128)S(1)} %payload.16.refs_5_), channel_id=1, source_target_pairs={{1,3},{2,4},{5,7},{3,1},{4,2},{7,5},{9,11},{10,12},{13,15},{11,9},... | collective-permute-start | bytes 1597448 | tf_op jit(solution)/shard_map/ppermute | solution.py:460
  64.1 6.3 %collective-permute-start.15 = (f32[1024,128]{1,0:T(8,128)S(1)}, f32[1024,128]{1,0:T(8,128)S(1)}, u32[]{:S(2)}, u32[]{:S(2)}) collective-permute-start(f32[1024,128]{1,0:T(8,128)S(1)} %get-tuple-element.48), channel_id=1, source_target_pairs={{0,1},{1,0},{2,3},{3,2},{4,5},{5,4},{6,7},{7,6},{8,9},{9,8},{10,11... | collective-permute-start | bytes 1572872 | tf_op jit(solution)/shard_map/ppermute | solution.py:457
  76.1 13.8 %collective-permute-start.18 = (f32[1024,128]{1,0:T(8,128)S(1)}, f32[1024,128]{1,0:T(8,128)S(1)}, u32[]{:S(2)}, u32[]{:S(2)}) collective-permute-start(f32[1024,128]{1,0:T(8,128)S(1)} %get-tuple-element.52.refs_2_.refs_1_), channel_id=1, source_target_pairs={{1,3},{2,4},{5,7},{3,1},{4,2},{7,5},{9,11},{10,12},{13,15},{11,9},... | collective-permute-start | bytes 1572872 | tf_op jit(solution)/shard_map/ppermute | solution.py:460
  79.8 12.5 %collective-permute-start.20 = (f32[1024,128]{1,0:T(8,128)S(1)}, f32[1024,128]{1,0:T(8,128)S(1)}, u32[]{:S(2)}, u32[]{:S(2)}) collective-permute-start(f32[1024,128]{1,0:T(8,128)S(1)} %get-tuple-element.52.refs_2_.refs_1_), channel_id=1, source_target_pairs={{0,2},{3,5},{4,6},{2,0},{5,3},{6,4},{8,10},{11,13},{12,14},{10,8},... | collective-permute-start | bytes 1572872 | tf_op jit(solution)/shard_map/ppermute | solution.py:460
  81.8 10.6 %collective-permute-start.19 = (f32[1024,128]{1,0:T(8,128)S(1)}, f32[1024,128]{1,0:T(8,128)S(1)}, u32[]{:S(2)}, u32[]{:S(2)}) collective-permute-start(f32[1024,128]{1,0:T(8,128)S(1)} %get-tuple-element.53), channel_id=1, source_target_pairs={{0,1},{1,0},{2,3},{3,2},{4,5},{5,4},{6,7},{7,6},{8,9},{9,8},{10,11... | collective-permute-start | bytes 1572872 | tf_op jit(solution)/shard_map/ppermute | solution.py:457
  81.8 21.7 %collective-permute-start.26 = (f32[1024,128]{1,0:T(8,128)S(1)}, f32[1024,128]{1,0:T(8,128)S(1)}, u32[]{:S(2)}, u32[]{:S(2)}) collective-permute-start(f32[1024,128]{1,0:T(8,128)S(1)} %get-tuple-element.52.refs_2_.refs_1_), channel_id=1, source_target_pairs={{0,1},{1,0},{2,3},{3,2},{4,5},{5,4},{6,7},{7,6},{8,9},{9,8},{10,11... | collective-permute-start | bytes 1572872 | tf_op jit(solution)/shard_map/ppermute | solution.py:457
  84.9 32.0 %collective-permute-start.22 = (f32[1024,128]{1,0:T(8,128)S(1)}, f32[1024,128]{1,0:T(8,128)S(1)}, u32[]{:S(2)}, u32[]{:S(2)}) collective-permute-start(f32[1024,128]{1,0:T(8,128)S(1)} %get-tuple-element.59), channel_id=1, source_target_pairs={{0,1},{1,0},{2,3},{3,2},{4,5},{5,4},{6,7},{7,6},{8,9},{9,8},{10,11... | collective-permute-start | bytes 1572872 | tf_op jit(solution)/shard_map/ppermute | solution.py:457
  92.4 24.5 %collective-permute-start.23 = (f32[1024,128]{1,0:T(8,128)S(1)}, f32[1024,128]{1,0:T(8,128)S(1)}, u32[]{:S(2)}, u32[]{:S(2)}) collective-permute-start(f32[1024,128]{1,0:T(8,128)S(1)} %payload.18.refs_3_), channel_id=1, source_target_pairs={{1,3},{2,4},{5,7},{3,1},{4,2},{7,5},{9,11},{10,12},{13,15},{11,9},... | collective-permute-start | bytes 1572872 | tf_op jit(solution)/shard_map/ppermute | solution.py:460
  94.4 22.6 %collective-permute-start.21 = (f32[1024,128]{1,0:T(8,128)S(1)}, f32[1024,128]{1,0:T(8,128)S(1)}, u32[]{:S(2)}, u32[]{:S(2)}) collective-permute-start(f32[1024,128]{1,0:T(8,128)S(1)} %payload.19.refs_2_), channel_id=1, source_target_pairs={{0,2},{3,5},{4,6},{2,0},{5,3},{6,4},{8,10},{11,13},{12,14},{10,8},... | collective-permute-start | bytes 1572872 | tf_op jit(solution)/shard_map/ppermute | solution.py:460
  96.5 4.3 %collective-permute-start.24 = (f32[32,1024]{1,0:T(8,128)S(1)}, f32[32,1024]{1,0:T(8,128)S(1)}, u32[]{:S(2)}, u32[]{:S(2)}) collective-permute-start(f32[32,1024]{1,0:T(8,128)S(1)} %get-tuple-element.58.refs_2_), channel_id=1, source_target_pairs={{0,8},{16,24},{8,0},{24,16},{1,9},{17,25},{9,1},{25,17},{2,10},{18... | collective-permute-start | bytes 393224 | tf_op jit(solution)/shard_map/ppermute | solution.py:373
  100.8 7.3 %collective-permute-start.25 = (f32[32,1024]{1,0:T(8,128)S(1)}, f32[32,1024]{1,0:T(8,128)S(1)}, u32[]{:S(2)}, u32[]{:S(2)}) collective-permute-start(f32[32,1024]{1,0:T(8,128)S(1)} %get-tuple-element.60), channel_id=1, source_target_pairs={{8,16},{16,8},{9,17},{17,9},{10,18},{18,10},{11,19},{19,11},{12,20... | collective-permute-start | bytes 393224 | tf_op jit(solution)/shard_map/ppermute | solution.py:373
  103.6 21.1 %collective-permute-start.31 = (f32[1024,128]{1,0:T(8,128)S(1)}, f32[1024,128]{1,0:T(8,128)S(1)}, u32[]{:S(2)}, u32[]{:S(2)}) collective-permute-start(f32[1024,128]{1,0:T(8,128)S(1)} %pick.9.refs_3_.refs_1_), channel_id=1, source_target_pairs={{0,1},{1,0},{2,3},{3,2},{4,5},{5,4},{6,7},{7,6},{8,9},{9,8},{10,11... | collective-permute-start | bytes 1572872 | tf_op jit(solution)/shard_map/ppermute | solution.py:457
  117.1 12.9 %collective-permute-start.27 = (f32[1024,128]{1,0:T(8,128)S(1)}, f32[1024,128]{1,0:T(8,128)S(1)}, u32[]{:S(2)}, u32[]{:S(2)}) collective-permute-start(f32[1024,128]{1,0:T(8,128)S(1)} %payload.21.refs_3_), channel_id=1, source_target_pairs={{1,3},{2,4},{5,7},{3,1},{4,2},{7,5},{9,11},{10,12},{13,15},{11,9},... | collective-permute-start | bytes 1572872 | tf_op jit(solution)/shard_map/ppermute | solution.py:460
  120.3 14.8 %collective-permute-start.29 = (f32[1024,128]{1,0:T(8,128)S(1)}, f32[1024,128]{1,0:T(8,128)S(1)}, u32[]{:S(2)}, u32[]{:S(2)}) collective-permute-start(f32[1024,128]{1,0:T(8,128)S(1)} %payload.20.refs_5_), channel_id=1, source_target_pairs={{0,2},{3,5},{4,6},{2,0},{5,3},{6,4},{8,10},{11,13},{12,14},{10,8},... | collective-permute-start | bytes 1572872 | tf_op jit(solution)/shard_map/ppermute | solution.py:460
  123.6 11.6 %collective-permute-start.28 = (f32[1024,128]{1,0:T(8,128)S(1)}, f32[1024,128]{1,0:T(8,128)S(1)}, u32[]{:S(2)}, u32[]{:S(2)}) collective-permute-start(f32[1024,128]{1,0:T(8,128)S(1)} %get-tuple-element.64), channel_id=1, source_target_pairs={{0,1},{1,0},{2,3},{3,2},{4,5},{5,4},{6,7},{7,6},{8,9},{9,8},{10,11... | collective-permute-start | bytes 1572872 | tf_op jit(solution)/shard_map/ppermute | solution.py:457
  124.6 16.6 %collective-permute-start.37 = (f32[1024,128]{1,0:T(8,128)S(1)}, f32[1024,128]{1,0:T(8,128)S(1)}, u32[]{:S(2)}, u32[]{:S(2)}) collective-permute-start(f32[1024,128]{1,0:T(8,128)S(1)} %pick.10.refs_4_.refs_1_), channel_id=1, source_target_pairs={{0,1},{1,0},{2,3},{3,2},{4,5},{5,4},{6,7},{7,6},{8,9},{9,8},{10,11... | collective-permute-start | bytes 1572872 | tf_op jit(solution)/shard_map/ppermute | solution.py:457
  124.7 2.1 %collective-permute-start.30 = (f32[2,256]{1,0:T(2,128)S(1)}, f32[2,256]{1,0:T(2,128)S(1)}, u32[]{:S(2)}, u32[]{:S(2)}) collective-permute-start(f32[2,256]{1,0:T(2,128)S(1)} %get-tuple-element.65.refs_0_), channel_id=1, source_target_pairs={{0,1},{1,0},{2,3},{3,2},{4,5},{5,4},{6,7},{7,6},{8,9},{9,8},{10,11... | collective-permute-start | bytes 6152 | tf_op jit(solution)/shard_map/ppermute | solution.py:604
  126.9 3.1 %collective-permute-start.32 = (f32[2,256]{1,0:T(2,128)S(1)}, f32[2,256]{1,0:T(2,128)S(1)}, u32[]{:S(2)}, u32[]{:S(2)}) collective-permute-start(f32[2,256]{1,0:T(2,128)S(1)} %add.3.refs_0_.refs_2_), channel_id=1, source_target_pairs={{0,2},{1,3},{2,0},{3,1},{4,6},{5,7},{6,4},{7,5},{8,10},{9,11},{10,... | collective-permute-start | bytes 6152 | tf_op jit(solution)/shard_map/ppermute | solution.py:604
  135.1 18.6 %collective-permute-start.36 = (f32[1024,128]{1,0:T(8,128)S(1)}, f32[1024,128]{1,0:T(8,128)S(1)}, u32[]{:S(2)}, u32[]{:S(2)}) collective-permute-start(f32[1024,128]{1,0:T(8,128)S(1)} %pick.11.refs_5_.refs_1_), channel_id=1, source_target_pairs={{0,1},{1,0},{2,3},{3,2},{4,5},{5,4},{6,7},{7,6},{8,9},{9,8},{10,11... | collective-permute-start | bytes 1572872 | tf_op jit(solution)/shard_map/ppermute | solution.py:457
  135.4 19.8 %collective-permute-start.35 = (f32[1024,128]{1,0:T(8,128)S(1)}, f32[1024,128]{1,0:T(8,128)S(1)}, u32[]{:S(2)}, u32[]{:S(2)}) collective-permute-start(f32[1024,128]{1,0:T(8,128)S(1)} %get-tuple-element.66), channel_id=1, source_target_pairs={{0,1},{1,0},{2,3},{3,2},{4,5},{5,4},{6,7},{7,6},{8,9},{9,8},{10,11... | collective-permute-start | bytes 1572872 | tf_op jit(solution)/shard_map/ppermute | solution.py:457
  136.0 19.1 %collective-permute-start.33 = (f32[1024,128]{1,0:T(8,128)S(1)}, f32[1024,128]{1,0:T(8,128)S(1)}, u32[]{:S(2)}, u32[]{:S(2)}) collective-permute-start(f32[1024,128]{1,0:T(8,128)S(1)} %payload.23.refs_4_), channel_id=1, source_target_pairs={{0,2},{3,5},{4,6},{2,0},{5,3},{6,4},{8,10},{11,13},{12,14},{10,8},... | collective-permute-start | bytes 1572872 | tf_op jit(solution)/shard_map/ppermute | solution.py:460
  139.2 15.9 %collective-permute-start.34 = (f32[1024,128]{1,0:T(8,128)S(1)}, f32[1024,128]{1,0:T(8,128)S(1)}, u32[]{:S(2)}, u32[]{:S(2)}) collective-permute-start(f32[1024,128]{1,0:T(8,128)S(1)} %payload.22.refs_5_), channel_id=1, source_target_pairs={{1,3},{2,4},{5,7},{3,1},{4,2},{7,5},{9,11},{10,12},{13,15},{11,9},... | collective-permute-start | bytes 1572872 | tf_op jit(solution)/shard_map/ppermute | solution.py:460
  141.2 12.0 %collective-permute-start.38 = (f32[2,256]{1,0:T(2,128)S(1)}, f32[2,256]{1,0:T(2,128)S(1)}, u32[]{:S(2)}, u32[]{:S(2)}) collective-permute-start(f32[2,256]{1,0:T(2,128)S(1)} %add.4.refs_4_.refs_0_), channel_id=1, source_target_pairs={{0,4},{1,5},{2,6},{3,7},{4,0},{5,1},{6,2},{7,3},{8,12},{9,13},{10,... | collective-permute-start | bytes 6152 | tf_op jit(solution)/shard_map/ppermute | solution.py:604

commit v5 on v4

--- a/solution.py
+++ b/solution.py
@@ -12,7 +12,7 @@
 NY = 16
 HALO = 2 * NY
 LANES = 128
-SMALL = 32
+BLOCK = 512
 
 
 relax_rate = 0.5
@@ -113,15 +113,16 @@
         one_slot(pair, held, parts, outs[2 * slot], outs[2 * slot + 1])
 
 
-def two_blocks(numbers, first, last, scale, rows, matrix, *refs):
+def two_blocks(numbers, parts, first, last, scale, rows, matrix, *refs):
     modes = matrix.shape[1]
-    blocks, refs = refs[:2], refs[2:]
+    blocks, refs = [[refs[0]], refs[1 : 1 + parts]], refs[1 + parts :]
     if not first:
         before, refs = refs[0], refs[1:]
     if last:
         base, refs = refs[0], refs[1:]
     total = None if first else before[...]
-    for k, block in enumerate(blocks):
+    for k, pieces in enumerate(blocks):
+        block = jnp.concatenate([piece[...] for piece in pieces], axis=0)
         pieces = list(halves(block[:modes].T))
         if rows:
             weights = [
@@ -183,9 +184,9 @@
 
         @pl.when(slot_here == slot)
         def _(k=k):
-            mine, theirs = refs[2 * k], refs[2 * k + 1]
-            modes = mine.shape[0]
-            out[:modes] = arrived[:modes] + (mine[...] + theirs[...])
+            terms = refs[k]
+            modes = terms.shape[0]
+            out[:modes] = arrived[:modes] + terms[...]
             if out.shape[0] > modes:
                 out[modes:] = arrived[modes:]
 
@@ -208,19 +209,19 @@
     out[...] = one[...] + two[...]
 
 
-def turn_sum(scale, one, two, mine, theirs, base, out, strip):
-    modes = mine.shape[0]
-    total = one[:modes] + two[:modes] + (mine[...] + theirs[...])
+def turn_sum(scale, one, two, terms, base, out, strip):
+    modes = terms.shape[0]
+    total = one[:modes] + two[:modes] + terms[...]
     value = base[...] - scale * total
     out[...] = value
     strip[...] = value.T[-HALO:]
 
 
-def last_sum(scale, one, two, mine, theirs, base, other, out, value, sems):
+def last_sum(scale, one, two, terms, base, other, out, value, sems):
     cells = base.shape[1]
     ahead = pltpu.make_async_copy(other, out.at[:, pl.ds(cells, cells)], sems.at[0])
     ahead.start()
-    total = one[...] + two[...] + (mine[...] + theirs[...])
+    total = one[...] + two[...] + terms[...]
     value[...] = base[...] - scale * total
     copy = pltpu.make_async_copy(value, out.at[:, pl.ds(0, cells)], sems.at[1])
     copy.start()
@@ -248,121 +249,104 @@
         out_odd[...] = last[...]
 
 
-def still_rate(pieces, before, after, columns, kinds):
-    lane = lax.broadcasted_iota(jnp.int32, (1, LANES), 1)
-    y = lane % NY
+def differences(cells):
+    columns = cells // NY
+    own, strip = np.zeros((cells, 4 * cells)), np.zeros((2 * HALO, 4 * cells))
+    for x in range(columns):
+        for y in range(NY):
+            cell = x * NY + y
+            for way in (-1, 1):
+                for far, factor in enumerate((3.0, -4.0, 1.0)):
+                    at_x, at_y = x + way * far, y + way * far
+                    first = cell + (0 if way < 0 else cells)
+                    factor = -way * factor
+                    if at_x < 0:
+                        strip[(at_x + 2) * NY + y, first] = factor
+                    elif at_x >= columns:
+                        strip[HALO + (at_x - columns) * NY + y, first] = factor
+                    else:
+                        own[at_x * NY + y, first] = factor
+                    if 0 <= at_y < NY:
+                        own[x * NY + at_y, first + 2 * cells] = factor
+    return np.concatenate([own, own, strip, strip]).astype(jnp.bfloat16)
+
+
+def strip_columns(came_even, came_odd):
+    even = lax.axis_index("space") % 2 == 0
+    before = jnp.where(even, came_odd[...], came_even[...])
+    after = jnp.where(even, came_even[...], came_odd[...])
+    parts = halves(jnp.concatenate([before, after], axis=0))
+    return jnp.concatenate([p.astype(jnp.float32) for p in parts], axis=0).T.astype(jnp.bfloat16)
+
+
+def still_rate(field, strip, operators, columns, kinds):
+    cells = field.shape[1]
+    left = jnp.concatenate([*halves(field), strip], axis=1)
+    steps = jnp.dot(left, operators[...], preferred_element_type=jnp.float32)
     vx, vy, capacity = (columns[:, i : i + 1] for i in range(3))
-    fore_x, back_x = 0.5 * jnp.maximum(vx, 0.0), 0.5 * jnp.minimum(vx, 0.0)
-    fore_y, back_y = 0.5 * jnp.maximum(vy, 0.0), 0.5 * jnp.minimum(vy, 0.0)
-    centre = 3.0 * (fore_x - back_x + fore_y - back_y)
-    padded = [before, *pieces, after]
-    rates = []
-    for k, value in enumerate(pieces):
-        def along_x(offset):
-            near = pltpu.roll(value, -offset % LANES, 1)
-            if offset < 0:
-                return jnp.where(lane < -offset, pltpu.roll(padded[k], -offset, 1), near)
-            return jnp.where(
-                lane >= LANES - offset, pltpu.roll(padded[k + 2], LANES - offset, 1), near
-            )
-
-        def along_y(offset):
-            inside = (y + offset >= 0) & (y + offset < NY)
-            return jnp.where(inside, pltpu.roll(value, -offset % LANES, 1), 0.0)
-
-        kind = kinds[:, k * LANES : (k + 1) * LANES]
-        contact = jnp.where(kind > 0, relax_rate, 0.0)
-        source = jnp.where(kind == 1, contact, -contact)
-        rate = (
-            source * capacity
-            - (centre + contact) * value
-            + fore_x * (4.0 * along_x(-NY) - along_x(-2 * NY))
-            + back_x * (along_x(2 * NY) - 4.0 * along_x(NY))
-            + fore_y * (4.0 * along_y(-1) - along_y(-2))
-            + back_y * (along_y(2) - 4.0 * along_y(1))
-        )
-        rates.append(rate)
-    return rates
-
-
-def edges(came_even, came_odd, rows):
-    even = lax.axis_index("space") % 2 == 0
-    from_even, from_odd = came_even[:, rows].T, came_odd[:, rows].T
-    before = jnp.where(even, from_odd, from_even)
-    after = jnp.where(even, from_even, from_odd)
-    pad = jnp.zeros((before.shape[0], LANES - HALO), jnp.float32)
-    return (
-        jnp.concatenate([pad, before], axis=1),
-        jnp.concatenate([after, pad], axis=1),
-    )
-
-
-def pieces_of(value):
-    return [value[:, k : k + LANES] for k in range(0, value.shape[1], LANES)]
-
-
-def first_rest(field, came_even, came_odd, table, kinds, base_a, base_b):
+    speeds = (jnp.maximum(vx, 0.0), jnp.minimum(vx, 0.0))
+    speeds += (jnp.maximum(vy, 0.0), jnp.minimum(vy, 0.0))
+    contact = jnp.where(kinds > 0, relax_rate, 0.0)
+    source = jnp.where(kinds == 1, contact, -contact)
+    rate = source * capacity - contact * field
+    for k, speed in enumerate(speeds):
+        rate = rate - (0.5 * speed) * steps[:, k * cells : (k + 1) * cells]
+    return rate
+
+
+def first_rest(field, came_even, came_odd, operators, table, kinds, base_a, base_b, strips):
     modes, half = base_a.shape
-    block = min(modes, LANES)
-    small = min(block, SMALL)
+    block = min(modes, BLOCK)
+    strips[...] = strip_columns(came_even, came_odd)
 
     def step(i, _):
-        start = pl.multiple_of(i * block, block)
-        before, after = edges(came_even, came_odd, pl.ds(start, block))
-        columns = table[:, pl.ds(start, block)].T
-        for k in range(0, block, small):
-            rows = pl.ds(pl.multiple_of(start + k, small), small)
-            here = slice(k, k + small)
-            pieces = pieces_of(field[rows, :])
-            rates = still_rate(pieces, before[here], after[here], columns[here], kinds[...])
-            middle = len(pieces) // 2
-            for j, (piece, rate) in enumerate(zip(pieces, rates)):
-                out, at = (base_a, j) if j < middle else (base_b, j - middle)
-                out[rows, at * LANES : (at + 1) * LANES] = piece + time_step * rate
+        rows = pl.ds(pl.multiple_of(i * block, block), block)
+        value = field[rows, :]
+        rate = still_rate(value, strips[rows, :], operators, table[:, rows].T, kinds[...])
+        base = value + time_step * rate
+        base_a[rows, :] = base[:, :half]
+        base_b[rows, :] = base[:, half:]
         return 0
 
     lax.fori_loop(0, modes // block, step, 0)
 
 
 def second_rest(
-    field, mid_a, mid_b, came_even, came_odd, table, kinds, scattered, end_a, end_b, flux
+    field,
+    mid_a,
+    mid_b,
+    came_even,
+    came_odd,
+    operators,
+    table,
+    kinds,
+    scattered,
+    end_a,
+    end_b,
+    flux,
+    strips,
 ):
     modes, half = end_a.shape
-    cells = field.shape[1]
-    block = min(modes, LANES)
-    small = min(block, SMALL)
+    block = min(modes, BLOCK)
     step_size = 0.5 * time_step
-
-    def step(i, sums):
-        start = pl.multiple_of(i * block, block)
-        before, after = edges(came_even, came_odd, pl.ds(start, block))
-        columns = table[:, pl.ds(start, block)].T
-        taken = step_size * scattered[:, pl.ds(start, block)].T
-        sums = list(sums)
-        for k in range(0, block, small):
-            rows = pl.ds(pl.multiple_of(start + k, small), small)
-            here = slice(k, k + small)
-            values = pieces_of(field[rows, :])
-            mids = pieces_of(mid_a[rows, :]) + pieces_of(mid_b[rows, :])
-            rates = still_rate(mids, before[here], after[here], columns[here], kinds[...])
-            middle = len(mids) // 2
-            for j, (value, mid, rate) in enumerate(zip(values, mids, rates)):
-                out, at = (end_a, j) if j < middle else (end_b, j - middle)
-                end = 0.5 * (value + mid) + step_size * rate
-                out[rows, at * LANES : (at + 1) * LANES] = end
-                for d in range(2):
-                    terms = columns[here, 3 + d : 4 + d] * end - taken[here, d : d + 1] * mid
-                    folded = sum(terms[r : r + 8] for r in range(0, small, 8))
-                    sums[2 * j + d] = sums[2 * j + d] + folded
-        return tuple(sums)
-
-    zero = jnp.zeros((8, LANES), jnp.float32)
-    sums = lax.fori_loop(0, modes // block, step, (zero,) * (2 * cells // LANES))
-    for j in range(cells // LANES):
+    strips[...] = strip_columns(came_even, came_odd)
+    flux[...] = jnp.zeros_like(flux)
+
+    def step(i, _):
+        rows = pl.ds(pl.multiple_of(i * block, block), block)
+        mid = jnp.concatenate([mid_a[rows, :], mid_b[rows, :]], axis=1)
+        columns = table[:, rows].T
+        taken = step_size * scattered[:, rows].T
+        rate = still_rate(mid, strips[rows, :], operators, columns, kinds[...])
+        end = 0.5 * (field[rows, :] + mid) + step_size * rate
+        end_a[rows, :] = end[:, :half]
+        end_b[rows, :] = end[:, half:]
         for d in range(2):
-            flux[d : d + 1, j * LANES : (j + 1) * LANES] = jnp.sum(
-                sums[2 * j + d], axis=0, keepdims=True
-            )
+            terms = columns[:, 3 + d : 4 + d] * end - taken[:, d : d + 1] * mid
+            flux[d : d + 1, :] += jnp.sum(terms, axis=0, keepdims=True)
+        return 0
+
+    lax.fori_loop(0, modes // block, step, 0)
 
 
 def paired(to_even, to_odd):
@@ -474,6 +458,10 @@
             mine, other = call(kernel, [part] * 2, [self.matrix, field])
             self.terms.append((mine, exchange(other)))
 
+        def join_terms(self, *slots):
+            for slot in slots:
+                (self.terms[slot],) = call(add, [part], self.terms[slot])
+
         def take_own(self):
             self.blocks.append((self.own, exchange(self.own)))
 
@@ -482,26 +470,33 @@
             for stream in (step % 2, 1 - step % 2):
                 numbers = plan.sent[stream, step]
                 slots = sorted({n for n in numbers if n >= 0})
+                for slot in slots:
+                    if isinstance(self.terms[slot], tuple):
+                        self.join_terms(slot)
                 arrived = self.arrived[1 - stream][step - 1]
                 kernel = functools.partial(payload, numbers, slots)
-                arrays = [arrived] + [a for s in slots for a in self.terms[s]]
+                arrays = [arrived] + [self.terms[s] for s in slots]
                 (value,) = call(kernel, [arrived.shape], arrays)
                 sent[stream] = along(stream, value)
             for stream in (0, 1):
                 self.arrived[stream].append(sent[stream])
 
-        def take(self, slot):
+        def take(self, slot, parts=1):
             arrays = [self.arrived[stream][step] for stream, step in plan.choices[slot]]
             kernel = functools.partial(pick, plan.picked[slot])
             (here,) = call(kernel, [arrays[0].shape], arrays)
-            self.blocks.append((here, exchange(here)))
+            cut = here.shape[0] // parts // 8 * 8
+            ends = [cut * k for k in range(parts)] + [here.shape[0]]
+            there = [exchange(here[i:j]) for i, j in zip(ends, ends[1:])]
+            self.blocks.append((here, *there))
 
         def multiply(self, slot, base=None):
             first, last = slot == 0, base is not None
+            blocks = self.blocks[slot]
             kernel = functools.partial(
-                two_blocks, plan.blocks[slot], first, last, self.scale, self.rows
+                two_blocks, plan.blocks[slot], len(blocks) - 1, first, last, self.scale, self.rows
             )
-            arrays = [self.matrix, *self.blocks[slot]]
+            arrays = [self.matrix, *blocks]
             arrays += [] if first else [self.total]
             arrays += [base] if last else []
             outs = [(2 * half + (16 if self.rows else 0), modes)]
@@ -512,7 +507,7 @@
             return results
 
         def ends(self):
-            return [self.arrived[0][-1], self.arrived[1][-1], *self.terms[-1]]
+            return [self.arrived[0][-1], self.arrived[1][-1], self.terms[-1]]
 
     (own,) = call(
         own_rows,
@@ -542,19 +537,26 @@
     one.matrix = matrix
     one.terms = [(terms[2 * s], exchange(terms[2 * s + 1])) for s in range(chips)]
     one.take_own()
+    operators = jnp.asarray(differences(cells))
+    aside = [pltpu.VMEM((modes, 4 * HALO), jnp.bfloat16)]
+    strips = None
     for step in range(1, chips):
-        if step in (1, chips - 1):
-            one.take(step)
+        if step == 1:
+            one.take(1)
         one.send(step)
-        if step not in (1, chips - 1):
-            one.take(step)
         if step == 1:
+            one.join_terms(*(s for s in range(chips) if isinstance(one.terms[s], tuple)))
             strips = call(strip_rows, [(HALO, modes)] * 2, [distribution])
             strips = paired(*call(strip_pairs, [(HALO, modes)] * 2, strips))
+        else:
+            one.take(step, 2 if step == chips - 1 else 1)
         one.multiply(step - 1)
         if step == min(2, chips - 1):
             base_a, base_b = call(
-                first_rest, [part] * 2, [distribution, *strips, table, kinds]
+                first_rest,
+                [part] * 2,
+                [distribution, *strips, operators, table, kinds],
+                scratch=aside,
             )
     mid_a, leading, scattered = one.multiply(chips - 1, base_a)
 
@@ -564,16 +566,20 @@
         functools.partial(turn_sum, time_step), [part, (HALO, modes)], [*one.ends(), base_b]
     )
     two.begin(mid_b)
+    two.join_terms(0)
     for slot in range(1, chips - 1):
         two.add_terms(mid_a)
     two.take_own()
-    strips = paired(*call(strip_pairs, [(HALO, modes)] * 2, [leading, last]))
+    strips = call(strip_pairs, [(HALO, modes)] * 2, [leading, last])
+    strips = paired(*strips)
+    adding = None
     for step in range(1, chips):
-        if step in (1, chips - 1):
-            two.take(step)
+        if adding is not None:
+            adding.next()
         two.send(step)
-        if step not in (1, chips - 1):
-            two.take(step)
+        if step == 1:
+            two.join_terms(*(s for s in range(1, chips - 1) if isinstance(two.terms[s], tuple)))
+        two.take(step, 2 if step == chips - 1 else 1)
         if step == 1:
             two.add_terms(mid_a)
         two.multiply(step - 1)
@@ -581,12 +587,14 @@
             end_a, end_b, flux = call(
                 second_rest,
                 [part, part, (2, cells)],
-                [distribution, mid_a, mid_b, *strips, table, kinds, scattered],
+                [distribution, mid_a, mid_b, *strips, operators, table, kinds, scattered],
+                scratch=aside,
             )
-        else:
-            flux = sum_pairs(call, flux, devices, step - 1, chips - 1)
-    heat_flux = flux / jnp.sqrt(jnp.float32(total_modes))
+            adding = Adding(call, flux, devices)
     (last_b,) = two.multiply(chips - 1, end_b)
+    heat_flux = adding.finish() / jnp.sqrt(jnp.float32(total_modes))
+    if isinstance(two.terms[-1], tuple):
+        two.join_terms(chips - 1)
     (updated,) = call(
         functools.partial(last_sum, step_size),
         [(modes, cells)],
@@ -597,13 +605,21 @@
     return (updated, heat_flux)
 
 
-def sum_pairs(call, value, devices, turn, turns):
-    bits = [1 << k for k in range(devices.bit_length() - 1)]
-    share = -(-len(bits) // (turns - 1))
-    for bit in bits[(turn - 1) * share : turn * share]:
-        came = lax.ppermute(value, "mode", [(i, i ^ bit) for i in range(devices)])
-        (value,) = call(add, [value.shape], [value, came])
-    return value
+class Adding:
+    def __init__(self, call, value, devices):
+        self.call, self.value, self.devices, self.bit = call, value, devices, 1
+
+    def next(self):
+        if self.bit < self.devices:
+            pairs = [(i, i ^ self.bit) for i in range(self.devices)]
+            came = lax.ppermute(self.value, "mode", pairs)
+            (self.value,) = self.call(add, [self.value.shape], [self.value, came])
+            self.bit *= 2
+
+    def finish(self):
+        while self.bit < self.devices:
+            self.next()
+        return self.value
 
 
 def solution(mesh):

time: 157 us -> 138 us (0.88); the launches traced: 156 us -> 135 us
  waiting for transfers between devices: 46.3 us -> 33.9 us
  Pallas kernels: 44.2 us -> 33.8 us
  starting transfers between devices: 62.6 us -> 64.2 us
    ppermute x16, waiting for transfers between devices: 27.9 us -> 17.4 us  [along(): return lax.ppermute(value, 'mode', plan.pairs[stream])]
    pallas_call x42 -> x50, Pallas kernels: 44.2 us -> 33.8 us  [__call__(): pl.pallas_call(body, out_shape=[jax.ShapeDtypeStruct(shape, jnp.float32)...]
    ppermute x4, waiting for transfers between devices: 7.48 us -> 2.57 us  [paired(): lax.ppermute(value, 'space', pairs + [(j, i) for i, j in pairs])]
    ppermute x16 -> x18, waiting for transfers between devices: 0.04 us -> 2.34 us  [exchange(): return lax.ppermute(value, 'mode', across)]
    ppermute x16 -> x18, starting transfers between devices: 10.3 us -> 9.18 us  [exchange(): return lax.ppermute(value, 'mode', across)]
  transfers between devices with their start and end apart: 39 -> 41, of which waited for: 14 -> 13; matrix products, arithmetic and copies ran while one was open for 0% -> 1% of each run, Pallas kernels for 26% -> 23%
where the time goes in v5:
time: 138 us; the launch traced here: 135 us
  starting transfers between devices  64.2 us (47%)
  waiting for transfers between devices  33.9 us (25%)
  Pallas kernels  33.8 us (24%)
  between operations  1.53 us (1%)
    ppermute x16, starting transfers between devices, along(): return lax.ppermute(value, 'mode', plan.pairs[stream])  43.3 us
    pallas_call x50, Pallas kernels, __call__(): pl.pallas_call(body, out_shape=[jax.ShapeDtypeStruct(shape, jnp.float32)...  33.8 us
    ppermute x16, waiting for transfers between devices, along(): return lax.ppermute(value, 'mode', plan.pairs[stream])  17.4 us
    ppermute x3, waiting for transfers between devices, next(): came = lax.ppermute(self.value, 'mode', pairs)  11.6 us
    ppermute x18, starting transfers between devices, exchange(): return lax.ppermute(value, 'mode', across)  9.18 us
    ppermute x4, starting transfers between devices, paired(): lax.ppermute(value, 'space', pairs + [(j, i) for i, j in pairs])  7.32 us
    ppermute x3, starting transfers between devices, next(): came = lax.ppermute(self.value, 'mode', pairs)  4.43 us
  transfers between devices with their start and end apart: 41, of which 13 were waited for; matrix products, arithmetic and copies ran while one was open for 1% of the time, Pallas kernels for 23%

profile of v5, /device:TPU:13, one launch (start us, length us, event | category | flops | bytes accessed | tf_op | source)
XLA Modules:
  0.0 135.3 jit_solution(15532896687965840348)
XLA Ops:
  0.6 2.0 %own_rows.1.refs_2_.refs_1_ = f32[1040,128]{1,0:T(8,128)} custom-call(f32[1024,256]{1,0:T(8,128)} %refs_0_.9, f32[2,1024]{1,0:T(2,128)} %refs_1_.2, f32[1,1024]{1,0:T(1,128)} %bitcast.4), custom_call_target="tpu_custom_call" | custom-call | flops 1024 | bytes 1024 | tf_op jit(solution)/shard_map/own_rows/pallas_call | solution.py:38
  2.6 2.1 %collective-permute-start = (f32[1040,128]{1,0:T(8,128)}, f32[1040,128]{1,0:T(8,128)S(1)}, u32[]{:S(2)}, u32[]{:S(2)}) collective-permute-start(f32[1040,128]{1,0:T(8,128)} %own_rows.1.refs_2_.refs_1_), channel_id=1, source_target_pairs={{1,3},{2,4},{5,7},{3,1},{4,2},{7,5},{9,11},{10,12},{13,15},{11,9},... | collective-permute-start | bytes 1597448 | tf_op jit(solution)/shard_map/ppermute | solution.py:444
  4.7 4.3 %collective-permute-start.2 = (f32[1040,128]{1,0:T(8,128)}, f32[1040,128]{1,0:T(8,128)S(1)}, u32[]{:S(2)}, u32[]{:S(2)}) collective-permute-start(f32[1040,128]{1,0:T(8,128)} %own_rows.1.refs_2_.refs_1_), channel_id=1, source_target_pairs={{0,2},{3,5},{4,6},{2,0},{5,3},{6,4},{8,10},{11,13},{12,14},{10,8},... | collective-permute-start | bytes 1597448 | tf_op jit(solution)/shard_map/ppermute | solution.py:444
  9.1 1.0 copy-done.2
  10.1 7.4 %load_and_products.1 = (f32[1024,128]{1,0:T(8,128)S(1)}, f32[1024,128]{1,0:T(8,128)S(1)}, f32[1024,128]{1,0:T(8,128)S(1)}, f32[1024,128]{1,0:T(8,128)S(1)}, f32[...) custom-call(bf16[8192,1024]{1,0:T(8,128)(2,1)} %refs_0_.6, ...), custom_call_target="tpu_custom_call" | custom-call | flops 1024 | bytes 1024 | tf_op jit(solution)/shard_map/load_and_products/pallas_call | solution.py:38
  17.6 0.5 collective-permute-start.4
  18.1 0.4 collective-permute-start.6
  18.6 1.1 collective-permute-done.2.refs_0_
  19.9 2.7 %collective-permute-start.5 = (f32[1040,128]{1,0:T(8,128)S(1)}, f32[1040,128]{1,0:T(8,128)S(1)}, u32[]{:S(2)}, u32[]{:S(2)}) collective-permute-start(f32[1040,128]{1,0:T(8,128)S(1)} %payload.12.refs_2_), channel_id=1, source_target_pairs={{1,3},{2,4},{5,7},{3,1},{4,2},{7,5},{9,11},{10,12},{13,15},{11,9},... | collective-permute-start | bytes 1597448 | tf_op jit(solution)/shard_map/ppermute | solution.py:444
  22.6 2.5 %collective-permute-start.3 = (f32[1040,128]{1,0:T(8,128)S(1)}, f32[1040,128]{1,0:T(8,128)S(1)}, u32[]{:S(2)}, u32[]{:S(2)}) collective-permute-start(f32[1040,128]{1,0:T(8,128)S(1)} %payload.13.refs_2_), channel_id=1, source_target_pairs={{0,2},{3,5},{4,6},{2,0},{5,3},{6,4},{8,10},{11,13},{12,14},{10,8},... | collective-permute-start | bytes 1597448 | tf_op jit(solution)/shard_map/ppermute | solution.py:444
  25.2 0.5 collective-permute-start.13
  25.8 1.3 collective-permute-done.7.refs_1_
  27.1 0.3 strip_rows.1
  27.5 1.4 %two_blocks.8.refs_3_ = f32[272,1024]{1,0:T(8,128)S(1)} custom-call(bf16[8192,1024]{1,0:T(8,128)(2,1)S(1)} %get-tuple-element.39.refs_0_, f32[1040,128]{1,0:T(8,128)S(1)} %copy-done.2, f32[1040,128]{1,0:T(8,128)S(1)} %collective-permute-done.6.refs_2_, f32[32,1024]{1,0:T(8,128)S(1)} %get-tuple-element.46.refs_3_), custom_call_target="tpu_custom_call" | custom-call | flops 1024 | bytes 1024 | tf_op jit(solution)/shard_map/two_blocks/pallas_call | solution.py:38
  28.9 3.3 %collective-permute-done.5.refs_0_.refs_2_ = f32[1040,128]{1,0:T(8,128)S(1)} collective-permute-done((f32[1040,128]{1,0:T(8,128)S(1)}, f32[1040,128]{1,0:T(8,128)S(1)}, u32[]{:S(2)}, u32[]{:S(2)}) %collective-permute-start.5) | collective-permute-done | bytes 532512 | tf_op jit(solution)/shard_map/ppermute | solution.py:444
  32.4 4.0 %collective-permute-start.10 = (f32[1040,128]{1,0:T(8,128)S(1)}, f32[1040,128]{1,0:T(8,128)S(1)}, u32[]{:S(2)}, u32[]{:S(2)}) collective-permute-start(f32[1040,128]{1,0:T(8,128)S(1)} %payload.14.refs_3_), channel_id=1, source_target_pairs={{0,2},{3,5},{4,6},{2,0},{5,3},{6,4},{8,10},{11,13},{12,14},{10,8},... | collective-permute-start | bytes 1597448 | tf_op jit(solution)/shard_map/ppermute | solution.py:444
  36.5 1.9 %collective-permute-start.9 = (f32[1040,128]{1,0:T(8,128)S(1)}, f32[1040,128]{1,0:T(8,128)S(1)}, u32[]{:S(2)}, u32[]{:S(2)}) collective-permute-start(f32[1040,128]{1,0:T(8,128)S(1)} %payload.15.refs_3_), channel_id=1, source_target_pairs={{1,3},{2,4},{5,7},{3,1},{4,2},{7,5},{9,11},{10,12},{13,15},{11,9},... | collective-permute-start | bytes 1597448 | tf_op jit(solution)/shard_map/ppermute | solution.py:444
  38.5 1.3 collective-permute-start.11
  39.8 2.1 %collective-permute-start.12 = (f32[32,1024]{1,0:T(8,128)S(1)}, f32[32,1024]{1,0:T(8,128)S(1)}, u32[]{:S(2)}, u32[]{:S(2)}) collective-permute-start(f32[32,1024]{1,0:T(8,128)S(1)} %get-tuple-element.47), channel_id=1, source_target_pairs={{8,16},{16,8},{9,17},{17,9},{10,18},{18,10},{11,19},{19,11},{12,20... | collective-permute-start | bytes 393224 | tf_op jit(solution)/shard_map/ppermute | solution.py:357
  42.0 2.1 %collective-permute-start.18 = (f32[1040,128]{1,0:T(8,128)S(1)}, f32[1040,128]{1,0:T(8,128)S(1)}, u32[]{:S(2)}, u32[]{:S(2)}) collective-permute-start(f32[1040,128]{1,0:T(8,128)S(1)} %pick.7.refs_4_.refs_1_), channel_id=1, source_target_pairs={{0,1},{1,0},{2,3},{3,2},{4,5},{5,4},{6,7},{7,6},{8,9},{9,8},{10,11... | collective-permute-start | bytes 1597448 | tf_op jit(solution)/shard_map/ppermute | solution.py:441
  44.1 1.4 %two_blocks.9.refs_6_.refs_3_ = f32[272,1024]{1,0:T(8,128)S(1)} custom-call(bf16[8192,1024]{1,0:T(8,128)(2,1)S(1)} %get-tuple-element.39.refs_0_, f32[1040,128]{1,0:T(8,128)S(1)} %pick.6.refs_2_.refs_1_, f32[1040,128]{1,0:T(8,128)S(1)} %collective-permute-done.13.refs_2_, f32[272,1024]{1,0:T(8,128)S(1)} %two_blocks.8.refs_3_, ...), custom_call_target="tpu_custom_call" | custom-call | flops 1024 | bytes 1024 | tf_op jit(solution)/shard_map/two_blocks/pallas_call | solution.py:38
  45.5 0.9 collective-permute-done.12.refs_2_
  46.4 2.2 %first_rest.1 = (f32[1024,128]{1,0:T(8,128)S(1)}, f32[1024,128]{1,0:T(8,128)S(1)}) custom-call(f32[1024,256]{1,0:T(8,128)S(1)} %copy-done, f32[32,1024]{1,0:T(8,128)S(1)} %collective-permute-done.11.refs_1_, f32[32,1024]{1,0:T(8,128)S(1)} %collective-permute-done.12.refs_2_, bf16[640,1024]{1,0:T(8,128)(2,1)S(1)} %copy-done.1, ...), custom_call_target="tpu_custom_call" | custom-call | flops 1024 | bytes 1024 | tf_op jit(solution)/shard_map/first_rest/pallas_call | solution.py:38
  48.7 4.3 %collective-permute-start.15 = (f32[1040,128]{1,0:T(8,128)S(1)}, f32[1040,128]{1,0:T(8,128)S(1)}, u32[]{:S(2)}, u32[]{:S(2)}) collective-permute-start(f32[1040,128]{1,0:T(8,128)S(1)} %payload.16.refs_3_), channel_id=1, source_target_pairs={{1,3},{2,4},{5,7},{3,1},{4,2},{7,5},{9,11},{10,12},{13,15},{11,9},... | collective-permute-start | bytes 1597448 | tf_op jit(solution)/shard_map/ppermute | solution.py:444
  53.1 3.3 %collective-permute-start.14 = (f32[1040,128]{1,0:T(8,128)S(1)}, f32[1040,128]{1,0:T(8,128)S(1)}, u32[]{:S(2)}, u32[]{:S(2)}) collective-permute-start(f32[1040,128]{1,0:T(8,128)S(1)} %payload.17.refs_4_), channel_id=1, source_target_pairs={{0,2},{3,5},{4,6},{2,0},{5,3},{6,4},{8,10},{11,13},{12,14},{10,8},... | collective-permute-start | bytes 1597448 | tf_op jit(solution)/shard_map/ppermute | solution.py:444
  56.7 0.5 collective-permute-start.17
  57.2 1.4 %two_blocks.10.refs_4_.refs_6_ = f32[272,1024]{1,0:T(8,128)S(1)} custom-call(bf16[8192,1024]{1,0:T(8,128)(2,1)S(1)} %get-tuple-element.39.refs_0_, f32[1040,128]{1,0:T(8,128)S(1)} %pick.7.refs_4_.refs_1_, f32[1040,128]{1,0:T(8,128)S(1)} %collective-permute-done.18.refs_2_, f32[272,1024]{1,0:T(8,128)S(1)} %two_blocks.9.refs_6_.refs_3_, ...), custom_call_target="tpu_custom_call" | custom-call | flops 1024 | bytes 1024 | tf_op jit(solution)/shard_map/two_blocks/pallas_call | solution.py:38
  58.6 1.5 %two_blocks.11 = (f32[1024,128]{1,0:T(8,128)S(1)}, f32[32,1024]{1,0:T(8,128)S(1)}, f32[8,1024]{1,0:T(8,128)S(1)}) custom-call(bf16[8192,1024]{1,0:T(8,128)(2,1)S(1)} %get-tuple-element.39.refs_0_, f32[1040,128]{1,0:T(8,128)S(1)} %pick.8.refs_4_.refs_1_, f32[520,128]{1,0:T(8,128)S(1)} %collective-permute-done.16.refs_2_, ...), custom_call_target="tpu_custom_call" | custom-call | flops 1024 | bytes 1024 | tf_op jit(solution)/shard_map/two_blocks/pallas_call | solution.py:38
  60.2 1.3 slot_products.4
  61.6 6.1 %collective-permute-done.14.refs_0_ = f32[1040,128]{1,0:T(8,128)S(1)} collective-permute-done((f32[1040,128]{1,0:T(8,128)S(1)}, f32[1040,128]{1,0:T(8,128)S(1)}, u32[]{:S(2)}, u32[]{:S(2)}) %collective-permute-start.14) | collective-permute-done | bytes 532512 | tf_op jit(solution)/shard_map/ppermute | solution.py:444
  68.0 2.1 %collective-permute-start.21 = (f32[1024,128]{1,0:T(8,128)S(1)}, f32[1024,128]{1,0:T(8,128)S(1)}, u32[]{:S(2)}, u32[]{:S(2)}) collective-permute-start(f32[1024,128]{1,0:T(8,128)S(1)} %get-tuple-element.52.refs_2_.refs_1_), channel_id=1, source_target_pairs={{0,2},{3,5},{4,6},{2,0},{5,3},{6,4},{8,10},{11,13},{12,14},{10,8},... | collective-permute-start | bytes 1572872 | tf_op jit(solution)/shard_map/ppermute | solution.py:444
  70.0 1.9 %collective-permute-start.19 = (f32[1024,128]{1,0:T(8,128)S(1)}, f32[1024,128]{1,0:T(8,128)S(1)}, u32[]{:S(2)}, u32[]{:S(2)}) collective-permute-start(f32[1024,128]{1,0:T(8,128)S(1)} %get-tuple-element.52.refs_2_.refs_1_), channel_id=1, source_target_pairs={{1,3},{2,4},{5,7},{3,1},{4,2},{7,5},{9,11},{10,12},{13,15},{11,9},... | collective-permute-start | bytes 1572872 | tf_op jit(solution)/shard_map/ppermute | solution.py:444
  72.0 1.3 slot_products.5
  73.3 1.5 %collective-permute-start.23 = (f32[1024,128]{1,0:T(8,128)S(1)}, f32[1024,128]{1,0:T(8,128)S(1)}, u32[]{:S(2)}, u32[]{:S(2)}) collective-permute-start(f32[1024,128]{1,0:T(8,128)S(1)} %get-tuple-element.59), channel_id=1, source_target_pairs={{0,1},{1,0},{2,3},{3,2},{4,5},{5,4},{6,7},{7,6},{8,9},{9,8},{10,11... | collective-permute-start | bytes 1572872 | tf_op jit(solution)/shard_map/ppermute | solution.py:441
  74.8 1.3 slot_products.6
  76.2 0.5 collective-permute-start.27
  76.7 4.7 %collective-permute-done.21.refs_0_ = f32[1024,128]{1,0:T(8,128)S(1)} collective-permute-done((f32[1024,128]{1,0:T(8,128)S(1)}, f32[1024,128]{1,0:T(8,128)S(1)}, u32[]{:S(2)}, u32[]{:S(2)}) %collective-permute-start.21) | collective-permute-done | bytes 524320 | tf_op jit(solution)/shard_map/ppermute | solution.py:444
  81.4 1.9 %collective-permute-start.24 = (f32[1024,128]{1,0:T(8,128)S(1)}, f32[1024,128]{1,0:T(8,128)S(1)}, u32[]{:S(2)}, u32[]{:S(2)}) collective-permute-start(f32[1024,128]{1,0:T(8,128)S(1)} %payload.18.refs_2_), channel_id=1, source_target_pairs={{1,3},{2,4},{5,7},{3,1},{4,2},{7,5},{9,11},{10,12},{13,15},{11,9},... | collective-permute-start | bytes 1572872 | tf_op jit(solution)/shard_map/ppermute | solution.py:444
  83.3 0.5 collective-permute-done.19.refs_0_.refs_1_
  83.8 2.0 %collective-permute-start.22 = (f32[1024,128]{1,0:T(8,128)S(1)}, f32[1024,128]{1,0:T(8,128)S(1)}, u32[]{:S(2)}, u32[]{:S(2)}) collective-permute-start(f32[1024,128]{1,0:T(8,128)S(1)} %payload.19.refs_2_), channel_id=1, source_target_pairs={{0,2},{3,5},{4,6},{2,0},{5,3},{6,4},{8,10},{11,13},{12,14},{10,8},... | collective-permute-start | bytes 1572872 | tf_op jit(solution)/shard_map/ppermute | solution.py:444
  85.8 1.9 %collective-permute-start.25 = (f32[32,1024]{1,0:T(8,128)S(1)}, f32[32,1024]{1,0:T(8,128)S(1)}, u32[]{:S(2)}, u32[]{:S(2)}) collective-permute-start(f32[32,1024]{1,0:T(8,128)S(1)} %get-tuple-element.58.refs_2_), channel_id=1, source_target_pairs={{0,8},{16,24},{8,0},{24,16},{1,9},{17,25},{9,1},{25,17},{2,10},{18... | collective-permute-start | bytes 393224 | tf_op jit(solution)/shard_map/ppermute | solution.py:357
  87.7 2.1 %collective-permute-start.26 = (f32[32,1024]{1,0:T(8,128)S(1)}, f32[32,1024]{1,0:T(8,128)S(1)}, u32[]{:S(2)}, u32[]{:S(2)}) collective-permute-start(f32[32,1024]{1,0:T(8,128)S(1)} %get-tuple-element.60), channel_id=1, source_target_pairs={{8,16},{16,8},{9,17},{17,9},{10,18},{18,10},{11,19},{19,11},{12,20... | collective-permute-start | bytes 393224 | tf_op jit(solution)/shard_map/ppermute | solution.py:357
  90.0 1.3 slot_products.7
  91.3 1.3 two_blocks.12.refs_9_.refs_3_
  92.6 1.7 %collective-permute-done.26.refs_4_ = f32[32,1024]{1,0:T(8,128)S(1)} collective-permute-done((f32[32,1024]{1,0:T(8,128)S(1)}, f32[32,1024]{1,0:T(8,128)S(1)}, u32[]{:S(2)}, u32[]{:S(2)}) %collective-permute-start.26) | collective-permute-done | bytes 131104 | tf_op jit(solution)/shard_map/ppermute | solution.py:357
  94.3 2.8 %second_rest.1 = (f32[1024,128]{1,0:T(8,128)S(1)}, f32[1024,128]{1,0:T(8,128)S(1)}, f32[2,256]{1,0:T(2,128)S(1)}) custom-call(f32[1024,256]{1,0:T(8,128)S(1)} %copy-done, f32[1024,128]{1,0:T(8,128)S(1)} %get-tuple-element.50.refs_1_.refs_2_, f32[1024,128]{1,0:T(8,128)S(1)} %get-tuple-element.52.refs_2_.refs_1_, ...), custom_call_target="tpu_custom_call" | custom-call | flops 1024 | bytes 1024 | tf_op jit(solution)/shard_map/second_rest/pallas_call | solution.py:38
  97.1 3.4 %collective-permute-start.29 = (f32[2,256]{1,0:T(2,128)S(1)}, f32[2,256]{1,0:T(2,128)S(1)}, u32[]{:S(2)}, u32[]{:S(2)}) collective-permute-start(f32[2,256]{1,0:T(2,128)S(1)} %get-tuple-element.64.refs_0_), channel_id=1, source_target_pairs={{0,1},{1,0},{2,3},{3,2},{4,5},{5,4},{6,7},{7,6},{8,9},{9,8},{10,11... | collective-permute-start | bytes 6152 | tf_op jit(solution)/shard_map/ppermute | solution.py:615
  100.5 0.7 collective-permute-done.29.refs_1_
  101.3 1.9 %collective-permute-start.31 = (f32[1024,128]{1,0:T(8,128)S(1)}, f32[1024,128]{1,0:T(8,128)S(1)}, u32[]{:S(2)}, u32[]{:S(2)}) collective-permute-start(f32[1024,128]{1,0:T(8,128)S(1)} %payload.20.refs_3_), channel_id=1, source_target_pairs={{0,2},{3,5},{4,6},{2,0},{5,3},{6,4},{8,10},{11,13},{12,14},{10,8},... | collective-permute-start | bytes 1572872 | tf_op jit(solution)/shard_map/ppermute | solution.py:444
  103.3 2.4 %collective-permute-start.30 = (f32[1024,128]{1,0:T(8,128)S(1)}, f32[1024,128]{1,0:T(8,128)S(1)}, u32[]{:S(2)}, u32[]{:S(2)}) collective-permute-start(f32[1024,128]{1,0:T(8,128)S(1)} %payload.21.refs_3_), channel_id=1, source_target_pairs={{1,3},{2,4},{5,7},{3,1},{4,2},{7,5},{9,11},{10,12},{13,15},{11,9},... | collective-permute-start | bytes 1572872 | tf_op jit(solution)/shard_map/ppermute | solution.py:444
  105.8 1.9 %collective-permute-start.40 = (f32[1024,128]{1,0:T(8,128)S(1)}, f32[1024,128]{1,0:T(8,128)S(1)}, u32[]{:S(2)}, u32[]{:S(2)}) collective-permute-start(f32[1024,128]{1,0:T(8,128)S(1)} %pick.10.refs_4_.refs_1_), channel_id=1, source_target_pairs={{0,1},{1,0},{2,3},{3,2},{4,5},{5,4},{6,7},{7,6},{8,9},{9,8},{10,11... | collective-permute-start | bytes 1572872 | tf_op jit(solution)/shard_map/ppermute | solution.py:441
  107.8 1.3 two_blocks.13.refs_2_.refs_3_
  109.2 8.5 %collective-permute-done.32.refs_1_ = f32[2,256]{1,0:T(2,128)S(1)} collective-permute-done((f32[2,256]{1,0:T(2,128)S(1)}, f32[2,256]{1,0:T(2,128)S(1)}, u32[]{:S(2)}, u32[]{:S(2)}) %collective-permute-start.32) | collective-permute-done | bytes 2080 | tf_op jit(solution)/shard_map/ppermute | solution.py:615
  117.8 4.1 %collective-permute-start.35 = (f32[1024,128]{1,0:T(8,128)S(1)}, f32[1024,128]{1,0:T(8,128)S(1)}, u32[]{:S(2)}, u32[]{:S(2)}) collective-permute-start(f32[1024,128]{1,0:T(8,128)S(1)} %payload.22.refs_3_), channel_id=1, source_target_pairs={{1,3},{2,4},{5,7},{3,1},{4,2},{7,5},{9,11},{10,12},{13,15},{11,9},... | collective-permute-start | bytes 1572872 | tf_op jit(solution)/shard_map/ppermute | solution.py:444
  122.0 1.9 %collective-permute-start.34 = (f32[1024,128]{1,0:T(8,128)S(1)}, f32[1024,128]{1,0:T(8,128)S(1)}, u32[]{:S(2)}, u32[]{:S(2)}) collective-permute-start(f32[1024,128]{1,0:T(8,128)S(1)} %payload.23.refs_4_), channel_id=1, source_target_pairs={{0,2},{3,5},{4,6},{2,0},{5,3},{6,4},{8,10},{11,13},{12,14},{10,8},... | collective-permute-start | bytes 1572872 | tf_op jit(solution)/shard_map/ppermute | solution.py:444
  124.2 0.5 collective-permute-start.39
  124.6 1.0 collective-permute-done.38.refs_2_
  125.7 1.1 collective-permute-start.37
  126.7 1.3 two_blocks.14.refs_4_.refs_6_
  128.1 1.4 %two_blocks.15.refs_2_.refs_4_ = f32[1024,128]{1,0:T(8,128)S(1)} custom-call(bf16[8192,1024]{1,0:T(8,128)(2,1)S(1)} %get-tuple-element.39.refs_0_, f32[1024,128]{1,0:T(8,128)S(1)} %pick.11.refs_4_.refs_1_, f32[512,128]{1,0:T(8,128)S(1)} %collective-permute-done.38.refs_2_, f32[512,128]{1,0:T(8,128)S(1)} %collective-permute-done.39.refs_3_, ...), custom_call_target="tpu_custom_call" | custom-call | flops 1024 | bytes 1024 | tf_op jit(solution)/shard_map/two_blocks/pallas_call | solution.py:38
  129.5 2.4 %collective-permute-done.37.refs_1_ = f32[2,256]{1,0:T(2,128)S(1)} collective-permute-done((f32[2,256]{1,0:T(2,128)S(1)}, f32[2,256]{1,0:T(2,128)S(1)}, u32[]{:S(2)}, u32[]{:S(2)}) %collective-permute-start.37) | collective-permute-done | bytes 2080 | tf_op jit(solution)/shard_map/ppermute | solution.py:615
  132.0 0.6 broadcast_multiply_fusion.1
  132.5 1.6 %collective-permute-done.34.refs_0_ = f32[1024,128]{1,0:T(8,128)S(1)} collective-permute-done((f32[1024,128]{1,0:T(8,128)S(1)}, f32[1024,128]{1,0:T(8,128)S(1)}, u32[]{:S(2)}, u32[]{:S(2)}) %collective-permute-start.34) | collective-permute-done | bytes 524320 | tf_op jit(solution)/shard_map/ppermute | solution.py:444
  134.2 1.0 last_sum.1
  (87 shorter events, 3.2 us)
Async XLA Ops:
  0.6 8.4 %copy-start = (f32[1024,256]{1,0:T(8,128)S(1)}, f32[1024,256]{1,0:T(8,128)}, u32[]{:S(2)}) copy-start(f32[1024,256]{1,0:T(8,128)} %refs_0_.9) | copy-start | bytes 3145732
  2.6 15.5 %collective-permute-start = (f32[1040,128]{1,0:T(8,128)}, f32[1040,128]{1,0:T(8,128)S(1)}, u32[]{:S(2)}, u32[]{:S(2)}) collective-permute-start(f32[1040,128]{1,0:T(8,128)} %own_rows.1.refs_2_.refs_1_), channel_id=1, source_target_pairs={{1,3},{2,4},{5,7},{3,1},{4,2},{7,5},{9,11},{10,12},{13,15},{11,9},... | collective-permute-start | bytes 1597448 | tf_op jit(solution)/shard_map/ppermute | solution.py:444
  4.7 15.0 %collective-permute-start.2 = (f32[1040,128]{1,0:T(8,128)}, f32[1040,128]{1,0:T(8,128)S(1)}, u32[]{:S(2)}, u32[]{:S(2)}) collective-permute-start(f32[1040,128]{1,0:T(8,128)} %own_rows.1.refs_2_.refs_1_), channel_id=1, source_target_pairs={{0,2},{3,5},{4,6},{2,0},{5,3},{6,4},{8,10},{11,13},{12,14},{10,8},... | collective-permute-start | bytes 1597448 | tf_op jit(solution)/shard_map/ppermute | solution.py:444
  9.1 1.0 copy-start.2
  17.5 2.3 %collective-permute-start.1 = (f32[1024,128]{1,0:T(8,128)S(1)}, f32[1024,128]{1,0:T(8,128)S(1)}, u32[]{:S(2)}, u32[]{:S(2)}) collective-permute-start(f32[1024,128]{1,0:T(8,128)S(1)} %get-tuple-element.36), channel_id=1, source_target_pairs={{0,1},{1,0},{2,3},{3,2},{4,5},{5,4},{6,7},{7,6},{8,9},{9,8},{10,11... | collective-permute-start | bytes 1572872 | tf_op jit(solution)/shard_map/ppermute | solution.py:441
  17.6 7.5 %collective-permute-start.4 = (f32[1024,128]{1,0:T(8,128)S(1)}, f32[1024,128]{1,0:T(8,128)S(1)}, u32[]{:S(2)}, u32[]{:S(2)}) collective-permute-start(f32[1024,128]{1,0:T(8,128)S(1)} %get-tuple-element.38), channel_id=1, source_target_pairs={{0,1},{1,0},{2,3},{3,2},{4,5},{5,4},{6,7},{7,6},{8,9},{9,8},{10,11... | collective-permute-start | bytes 1572872 | tf_op jit(solution)/shard_map/ppermute | solution.py:441
  18.1 7.1 %collective-permute-start.8 = (f32[1024,128]{1,0:T(8,128)S(1)}, f32[1024,128]{1,0:T(8,128)S(1)}, u32[]{:S(2)}, u32[]{:S(2)}) collective-permute-start(f32[1024,128]{1,0:T(8,128)S(1)} %get-tuple-element.43), channel_id=1, source_target_pairs={{0,1},{1,0},{2,3},{3,2},{4,5},{5,4},{6,7},{7,6},{8,9},{9,8},{10,11... | collective-permute-start | bytes 1572872 | tf_op jit(solution)/shard_map/ppermute | solution.py:441
  18.1 9.4 %collective-permute-start.6 = (f32[1040,128]{1,0:T(8,128)S(1)}, f32[1040,128]{1,0:T(8,128)S(1)}, u32[]{:S(2)}, u32[]{:S(2)}) collective-permute-start(f32[1040,128]{1,0:T(8,128)S(1)} %copy-done.2), channel_id=1, source_target_pairs={{0,1},{1,0},{2,3},{3,2},{4,5},{5,4},{6,7},{7,6},{8,9},{9,8},{10,11... | collective-permute-start | bytes 1597448 | tf_op jit(solution)/shard_map/ppermute | solution.py:441
  19.9 12.4 %collective-permute-start.5 = (f32[1040,128]{1,0:T(8,128)S(1)}, f32[1040,128]{1,0:T(8,128)S(1)}, u32[]{:S(2)}, u32[]{:S(2)}) collective-permute-start(f32[1040,128]{1,0:T(8,128)S(1)} %payload.12.refs_2_), channel_id=1, source_target_pairs={{1,3},{2,4},{5,7},{3,1},{4,2},{7,5},{9,11},{10,12},{13,15},{11,9},... | collective-permute-start | bytes 1597448 | tf_op jit(solution)/shard_map/ppermute | solution.py:444
  22.6 13.8 %collective-permute-start.3 = (f32[1040,128]{1,0:T(8,128)S(1)}, f32[1040,128]{1,0:T(8,128)S(1)}, u32[]{:S(2)}, u32[]{:S(2)}) collective-permute-start(f32[1040,128]{1,0:T(8,128)S(1)} %payload.13.refs_2_), channel_id=1, source_target_pairs={{0,2},{3,5},{4,6},{2,0},{5,3},{6,4},{8,10},{11,13},{12,14},{10,8},... | collective-permute-start | bytes 1597448 | tf_op jit(solution)/shard_map/ppermute | solution.py:444
  25.1 2.0 %collective-permute-start.7 = (f32[1024,128]{1,0:T(8,128)S(1)}, f32[1024,128]{1,0:T(8,128)S(1)}, u32[]{:S(2)}, u32[]{:S(2)}) collective-permute-start(f32[1024,128]{1,0:T(8,128)S(1)} %get-tuple-element.41), channel_id=1, source_target_pairs={{0,1},{1,0},{2,3},{3,2},{4,5},{5,4},{6,7},{7,6},{8,9},{9,8},{10,11... | collective-permute-start | bytes 1572872 | tf_op jit(solution)/shard_map/ppermute | solution.py:441
  25.2 16.8 %collective-permute-start.13 = (f32[1040,128]{1,0:T(8,128)S(1)}, f32[1040,128]{1,0:T(8,128)S(1)}, u32[]{:S(2)}, u32[]{:S(2)}) collective-permute-start(f32[1040,128]{1,0:T(8,128)S(1)} %pick.6.refs_2_.refs_1_), channel_id=1, source_target_pairs={{0,1},{1,0},{2,3},{3,2},{4,5},{5,4},{6,7},{7,6},{8,9},{9,8},{10,11... | collective-permute-start | bytes 1597448 | tf_op jit(solution)/shard_map/ppermute | solution.py:441
  32.3 6.2 %copy-start.4 = (f32[2,1024]{1,0:T(2,128)S(1)}, f32[2,1024]{1,0:T(2,128)}, u32[]{:S(2)}) copy-start(f32[2,1024]{1,0:T(2,128)} %refs_1_.2) | copy-start | bytes 24580
  32.4 6.2 %copy-start.5 = (f32[1024]{0:T(1024)S(1)}, f32[1024]{0:T(1024)}, u32[]{:S(2)}) copy-start(f32[1024]{0:T(1024)} %param.9) | copy-start | bytes 12292
  32.4 16.2 %collective-permute-start.10 = (f32[1040,128]{1,0:T(8,128)S(1)}, f32[1040,128]{1,0:T(8,128)S(1)}, u32[]{:S(2)}, u32[]{:S(2)}) collective-permute-start(f32[1040,128]{1,0:T(8,128)S(1)} %payload.14.refs_3_), channel_id=1, source_target_pairs={{0,2},{3,5},{4,6},{2,0},{5,3},{6,4},{8,10},{11,13},{12,14},{10,8},... | collective-permute-start | bytes 1597448 | tf_op jit(solution)/shard_map/ppermute | solution.py:444
  36.5 16.5 %collective-permute-start.9 = (f32[1040,128]{1,0:T(8,128)S(1)}, f32[1040,128]{1,0:T(8,128)S(1)}, u32[]{:S(2)}, u32[]{:S(2)}) collective-permute-start(f32[1040,128]{1,0:T(8,128)S(1)} %payload.15.refs_3_), channel_id=1, source_target_pairs={{1,3},{2,4},{5,7},{3,1},{4,2},{7,5},{9,11},{10,12},{13,15},{11,9},... | collective-permute-start | bytes 1597448 | tf_op jit(solution)/shard_map/ppermute | solution.py:444
  38.5 7.0 %collective-permute-start.11 = (f32[32,1024]{1,0:T(8,128)S(1)}, f32[32,1024]{1,0:T(8,128)S(1)}, u32[]{:S(2)}, u32[]{:S(2)}) collective-permute-start(f32[32,1024]{1,0:T(8,128)S(1)} %get-tuple-element.46.refs_3_), channel_id=1, source_target_pairs={{0,8},{16,24},{8,0},{24,16},{1,9},{17,25},{9,1},{25,17},{2,10},{18... | collective-permute-start | bytes 393224 | tf_op jit(solution)/shard_map/ppermute | solution.py:357
  39.8 6.6 %collective-permute-start.12 = (f32[32,1024]{1,0:T(8,128)S(1)}, f32[32,1024]{1,0:T(8,128)S(1)}, u32[]{:S(2)}, u32[]{:S(2)}) collective-permute-start(f32[32,1024]{1,0:T(8,128)S(1)} %get-tuple-element.47), channel_id=1, source_target_pairs={{8,16},{16,8},{9,17},{17,9},{10,18},{18,10},{11,19},{19,11},{12,20... | collective-permute-start | bytes 393224 | tf_op jit(solution)/shard_map/ppermute | solution.py:357
  42.0 15.2 %collective-permute-start.18 = (f32[1040,128]{1,0:T(8,128)S(1)}, f32[1040,128]{1,0:T(8,128)S(1)}, u32[]{:S(2)}, u32[]{:S(2)}) collective-permute-start(f32[1040,128]{1,0:T(8,128)S(1)} %pick.7.refs_4_.refs_1_), channel_id=1, source_target_pairs={{0,1},{1,0},{2,3},{3,2},{4,5},{5,4},{6,7},{7,6},{8,9},{9,8},{10,11... | collective-permute-start | bytes 1597448 | tf_op jit(solution)/shard_map/ppermute | solution.py:441
  44.1 2.3 %copy-start.1 = (bf16[640,1024]{1,0:T(8,128)(2,1)S(1)}, bf16[640,1024]{1,0:T(8,128)(2,1)}, u32[]{:S(2)}) copy-start(bf16[640,1024]{1,0:T(8,128)(2,1)} %constant.7.clone.refs_3_.refs_5_) | copy-start | bytes 3932164
  44.1 2.3 %copy-start.3 = (s32[256]{0:T(256)S(1)}, s32[256]{0:T(256)}, u32[]{:S(2)}) copy-start(s32[256]{0:T(256)} %param.10) | copy-start | bytes 3076
  48.7 19.1 %collective-permute-start.15 = (f32[1040,128]{1,0:T(8,128)S(1)}, f32[1040,128]{1,0:T(8,128)S(1)}, u32[]{:S(2)}, u32[]{:S(2)}) collective-permute-start(f32[1040,128]{1,0:T(8,128)S(1)} %payload.16.refs_3_), channel_id=1, source_target_pairs={{1,3},{2,4},{5,7},{3,1},{4,2},{7,5},{9,11},{10,12},{13,15},{11,9},... | collective-permute-start | bytes 1597448 | tf_op jit(solution)/shard_map/ppermute | solution.py:444
  53.1 14.7 %collective-permute-start.14 = (f32[1040,128]{1,0:T(8,128)S(1)}, f32[1040,128]{1,0:T(8,128)S(1)}, u32[]{:S(2)}, u32[]{:S(2)}) collective-permute-start(f32[1040,128]{1,0:T(8,128)S(1)} %payload.17.refs_4_), channel_id=1, source_target_pairs={{0,2},{3,5},{4,6},{2,0},{5,3},{6,4},{8,10},{11,13},{12,14},{10,8},... | collective-permute-start | bytes 1597448 | tf_op jit(solution)/shard_map/ppermute | solution.py:444
  56.6 2.0 %collective-permute-start.16 = (f32[520,128]{1,0:T(8,128)S(1)}, f32[520,128]{1,0:T(8,128)S(1)}, u32[]{:S(2)}, u32[]{:S(2)}) collective-permute-start(f32[520,128]{1,0:T(8,128)S(1)} %get-tuple-element.69), channel_id=1, source_target_pairs={{0,1},{1,0},{2,3},{3,2},{4,5},{5,4},{6,7},{7,6},{8,9},{9,8},{10,11... | collective-permute-start | bytes 798728 | tf_op jit(solution)/shard_map/ppermute | solution.py:441
  56.7 1.9 %collective-permute-start.17 = (f32[520,128]{1,0:T(8,128)S(1)}, f32[520,128]{1,0:T(8,128)S(1)}, u32[]{:S(2)}, u32[]{:S(2)}) collective-permute-start(f32[520,128]{1,0:T(8,128)S(1)} %get-tuple-element.68), channel_id=1, source_target_pairs={{0,1},{1,0},{2,3},{3,2},{4,5},{5,4},{6,7},{7,6},{8,9},{9,8},{10,11... | collective-permute-start | bytes 798728 | tf_op jit(solution)/shard_map/ppermute | solution.py:441
  61.4 10.5 %collective-permute-start.20 = (f32[1024,128]{1,0:T(8,128)S(1)}, f32[1024,128]{1,0:T(8,128)S(1)}, u32[]{:S(2)}, u32[]{:S(2)}) collective-permute-start(f32[1024,128]{1,0:T(8,128)S(1)} %get-tuple-element.53), channel_id=1, source_target_pairs={{0,1},{1,0},{2,3},{3,2},{4,5},{5,4},{6,7},{7,6},{8,9},{9,8},{10,11... | collective-permute-start | bytes 1572872 | tf_op jit(solution)/shard_map/ppermute | solution.py:441
  68.0 13.4 %collective-permute-start.21 = (f32[1024,128]{1,0:T(8,128)S(1)}, f32[1024,128]{1,0:T(8,128)S(1)}, u32[]{:S(2)}, u32[]{:S(2)}) collective-permute-start(f32[1024,128]{1,0:T(8,128)S(1)} %get-tuple-element.52.refs_2_.refs_1_), channel_id=1, source_target_pairs={{0,2},{3,5},{4,6},{2,0},{5,3},{6,4},{8,10},{11,13},{12,14},{10,8},... | collective-permute-start | bytes 1572872 | tf_op jit(solution)/shard_map/ppermute | solution.py:444
  70.0 13.8 %collective-permute-start.19 = (f32[1024,128]{1,0:T(8,128)S(1)}, f32[1024,128]{1,0:T(8,128)S(1)}, u32[]{:S(2)}, u32[]{:S(2)}) collective-permute-start(f32[1024,128]{1,0:T(8,128)S(1)} %get-tuple-element.52.refs_2_.refs_1_), channel_id=1, source_target_pairs={{1,3},{2,4},{5,7},{3,1},{4,2},{7,5},{9,11},{10,12},{13,15},{11,9},... | collective-permute-start | bytes 1572872 | tf_op jit(solution)/shard_map/ppermute | solution.py:444
  73.3 12.5 %collective-permute-start.23 = (f32[1024,128]{1,0:T(8,128)S(1)}, f32[1024,128]{1,0:T(8,128)S(1)}, u32[]{:S(2)}, u32[]{:S(2)}) collective-permute-start(f32[1024,128]{1,0:T(8,128)S(1)} %get-tuple-element.59), channel_id=1, source_target_pairs={{0,1},{1,0},{2,3},{3,2},{4,5},{5,4},{6,7},{7,6},{8,9},{9,8},{10,11... | collective-permute-start | bytes 1572872 | tf_op jit(solution)/shard_map/ppermute | solution.py:441
  76.1 11.6 %collective-permute-start.28 = (f32[1024,128]{1,0:T(8,128)S(1)}, f32[1024,128]{1,0:T(8,128)S(1)}, u32[]{:S(2)}, u32[]{:S(2)}) collective-permute-start(f32[1024,128]{1,0:T(8,128)S(1)} %get-tuple-element.62), channel_id=1, source_target_pairs={{0,1},{1,0},{2,3},{3,2},{4,5},{5,4},{6,7},{7,6},{8,9},{9,8},{10,11... | collective-permute-start | bytes 1572872 | tf_op jit(solution)/shard_map/ppermute | solution.py:441
  76.2 15.1 %collective-permute-start.27 = (f32[1024,128]{1,0:T(8,128)S(1)}, f32[1024,128]{1,0:T(8,128)S(1)}, u32[]{:S(2)}, u32[]{:S(2)}) collective-permute-start(f32[1024,128]{1,0:T(8,128)S(1)} %get-tuple-element.52.refs_2_.refs_1_), channel_id=1, source_target_pairs={{0,1},{1,0},{2,3},{3,2},{4,5},{5,4},{6,7},{7,6},{8,9},{9,8},{10,11... | collective-permute-start | bytes 1572872 | tf_op jit(solution)/shard_map/ppermute | solution.py:441
  81.4 19.9 %collective-permute-start.24 = (f32[1024,128]{1,0:T(8,128)S(1)}, f32[1024,128]{1,0:T(8,128)S(1)}, u32[]{:S(2)}, u32[]{:S(2)}) collective-permute-start(f32[1024,128]{1,0:T(8,128)S(1)} %payload.18.refs_2_), channel_id=1, source_target_pairs={{1,3},{2,4},{5,7},{3,1},{4,2},{7,5},{9,11},{10,12},{13,15},{11,9},... | collective-permute-start | bytes 1572872 | tf_op jit(solution)/shard_map/ppermute | solution.py:444
  83.8 19.4 %collective-permute-start.22 = (f32[1024,128]{1,0:T(8,128)S(1)}, f32[1024,128]{1,0:T(8,128)S(1)}, u32[]{:S(2)}, u32[]{:S(2)}) collective-permute-start(f32[1024,128]{1,0:T(8,128)S(1)} %payload.19.refs_2_), channel_id=1, source_target_pairs={{0,2},{3,5},{4,6},{2,0},{5,3},{6,4},{8,10},{11,13},{12,14},{10,8},... | collective-permute-start | bytes 1572872 | tf_op jit(solution)/shard_map/ppermute | solution.py:444
  85.8 6.8 %collective-permute-start.25 = (f32[32,1024]{1,0:T(8,128)S(1)}, f32[32,1024]{1,0:T(8,128)S(1)}, u32[]{:S(2)}, u32[]{:S(2)}) collective-permute-start(f32[32,1024]{1,0:T(8,128)S(1)} %get-tuple-element.58.refs_2_), channel_id=1, source_target_pairs={{0,8},{16,24},{8,0},{24,16},{1,9},{17,25},{9,1},{25,17},{2,10},{18... | collective-permute-start | bytes 393224 | tf_op jit(solution)/shard_map/ppermute | solution.py:357
  87.7 6.6 %collective-permute-start.26 = (f32[32,1024]{1,0:T(8,128)S(1)}, f32[32,1024]{1,0:T(8,128)S(1)}, u32[]{:S(2)}, u32[]{:S(2)}) collective-permute-start(f32[32,1024]{1,0:T(8,128)S(1)} %get-tuple-element.60), channel_id=1, source_target_pairs={{8,16},{16,8},{9,17},{17,9},{10,18},{18,10},{11,19},{19,11},{12,20... | collective-permute-start | bytes 393224 | tf_op jit(solution)/shard_map/ppermute | solution.py:357
  97.1 4.2 %collective-permute-start.29 = (f32[2,256]{1,0:T(2,128)S(1)}, f32[2,256]{1,0:T(2,128)S(1)}, u32[]{:S(2)}, u32[]{:S(2)}) collective-permute-start(f32[2,256]{1,0:T(2,128)S(1)} %get-tuple-element.64.refs_0_), channel_id=1, source_target_pairs={{0,1},{1,0},{2,3},{3,2},{4,5},{5,4},{6,7},{7,6},{8,9},{9,8},{10,11... | collective-permute-start | bytes 6152 | tf_op jit(solution)/shard_map/ppermute | solution.py:615
  100.4 7.4 %collective-permute-start.33 = (f32[1024,128]{1,0:T(8,128)S(1)}, f32[1024,128]{1,0:T(8,128)S(1)}, u32[]{:S(2)}, u32[]{:S(2)}) collective-permute-start(f32[1024,128]{1,0:T(8,128)S(1)} %pick.9.refs_2_.refs_1_), channel_id=1, source_target_pairs={{0,1},{1,0},{2,3},{3,2},{4,5},{5,4},{6,7},{7,6},{8,9},{9,8},{10,11... | collective-permute-start | bytes 1572872 | tf_op jit(solution)/shard_map/ppermute | solution.py:441
  101.3 16.4 %collective-permute-start.31 = (f32[1024,128]{1,0:T(8,128)S(1)}, f32[1024,128]{1,0:T(8,128)S(1)}, u32[]{:S(2)}, u32[]{:S(2)}) collective-permute-start(f32[1024,128]{1,0:T(8,128)S(1)} %payload.20.refs_3_), channel_id=1, source_target_pairs={{0,2},{3,5},{4,6},{2,0},{5,3},{6,4},{8,10},{11,13},{12,14},{10,8},... | collective-permute-start | bytes 1572872 | tf_op jit(solution)/shard_map/ppermute | solution.py:444
  103.3 18.6 %collective-permute-start.30 = (f32[1024,128]{1,0:T(8,128)S(1)}, f32[1024,128]{1,0:T(8,128)S(1)}, u32[]{:S(2)}, u32[]{:S(2)}) collective-permute-start(f32[1024,128]{1,0:T(8,128)S(1)} %payload.21.refs_3_), channel_id=1, source_target_pairs={{1,3},{2,4},{5,7},{3,1},{4,2},{7,5},{9,11},{10,12},{13,15},{11,9},... | collective-permute-start | bytes 1572872 | tf_op jit(solution)/shard_map/ppermute | solution.py:444
  105.8 18.3 %collective-permute-start.40 = (f32[1024,128]{1,0:T(8,128)S(1)}, f32[1024,128]{1,0:T(8,128)S(1)}, u32[]{:S(2)}, u32[]{:S(2)}) collective-permute-start(f32[1024,128]{1,0:T(8,128)S(1)} %pick.10.refs_4_.refs_1_), channel_id=1, source_target_pairs={{0,1},{1,0},{2,3},{3,2},{4,5},{5,4},{6,7},{7,6},{8,9},{9,8},{10,11... | collective-permute-start | bytes 1572872 | tf_op jit(solution)/shard_map/ppermute | solution.py:441
  107.8 24.2 %collective-permute-start.36 = (f32[1024,128]{1,0:T(8,128)S(1)}, f32[1024,128]{1,0:T(8,128)S(1)}, u32[]{:S(2)}, u32[]{:S(2)}) collective-permute-start(f32[1024,128]{1,0:T(8,128)S(1)} %get-tuple-element.66), channel_id=1, source_target_pairs={{0,1},{1,0},{2,3},{3,2},{4,5},{5,4},{6,7},{7,6},{8,9},{9,8},{10,11... | collective-permute-start | bytes 1572872 | tf_op jit(solution)/shard_map/ppermute | solution.py:441
  107.8 9.9 %collective-permute-start.32 = (f32[2,256]{1,0:T(2,128)S(1)}, f32[2,256]{1,0:T(2,128)S(1)}, u32[]{:S(2)}, u32[]{:S(2)}) collective-permute-start(f32[2,256]{1,0:T(2,128)S(1)} %add.18.refs_3_.refs_0_), channel_id=1, source_target_pairs={{0,2},{1,3},{2,0},{3,1},{4,6},{5,7},{6,4},{7,5},{8,10},{9,11},{10,... | collective-permute-start | bytes 6152 | tf_op jit(solution)/shard_map/ppermute | solution.py:615
  117.8 16.4 %collective-permute-start.35 = (f32[1024,128]{1,0:T(8,128)S(1)}, f32[1024,128]{1,0:T(8,128)S(1)}, u32[]{:S(2)}, u32[]{:S(2)}) collective-permute-start(f32[1024,128]{1,0:T(8,128)S(1)} %payload.22.refs_3_), channel_id=1, source_target_pairs={{1,3},{2,4},{5,7},{3,1},{4,2},{7,5},{9,11},{10,12},{13,15},{11,9},... | collective-permute-start | bytes 1572872 | tf_op jit(solution)/shard_map/ppermute | solution.py:444
  122.0 12.2 %collective-permute-start.34 = (f32[1024,128]{1,0:T(8,128)S(1)}, f32[1024,128]{1,0:T(8,128)S(1)}, u32[]{:S(2)}, u32[]{:S(2)}) collective-permute-start(f32[1024,128]{1,0:T(8,128)S(1)} %payload.23.refs_4_), channel_id=1, source_target_pairs={{0,2},{3,5},{4,6},{2,0},{5,3},{6,4},{8,10},{11,13},{12,14},{10,8},... | collective-permute-start | bytes 1572872 | tf_op jit(solution)/shard_map/ppermute | solution.py:444
  124.1 1.6 %collective-permute-start.38 = (f32[512,128]{1,0:T(8,128)S(1)}, f32[512,128]{1,0:T(8,128)S(1)}, u32[]{:S(2)}, u32[]{:S(2)}) collective-permute-start(f32[512,128]{1,0:T(8,128)S(1)} %get-tuple-element.71), channel_id=1, source_target_pairs={{0,1},{1,0},{2,3},{3,2},{4,5},{5,4},{6,7},{7,6},{8,9},{9,8},{10,11... | collective-permute-start | bytes 786440 | tf_op jit(solution)/shard_map/ppermute | solution.py:441
  124.2 3.9 %collective-permute-start.39 = (f32[512,128]{1,0:T(8,128)S(1)}, f32[512,128]{1,0:T(8,128)S(1)}, u32[]{:S(2)}, u32[]{:S(2)}) collective-permute-start(f32[512,128]{1,0:T(8,128)S(1)} %get-tuple-element.70), channel_id=1, source_target_pairs={{0,1},{1,0},{2,3},{3,2},{4,5},{5,4},{6,7},{7,6},{8,9},{9,8},{10,11... | collective-permute-start | bytes 786440 | tf_op jit(solution)/shard_map/ppermute | solution.py:441
  125.7 6.2 %collective-permute-start.37 = (f32[2,256]{1,0:T(2,128)S(1)}, f32[2,256]{1,0:T(2,128)S(1)}, u32[]{:S(2)}, u32[]{:S(2)}) collective-permute-start(f32[2,256]{1,0:T(2,128)S(1)} %add.19.refs_3_.refs_0_), channel_id=1, source_target_pairs={{0,4},{1,5},{2,6},{3,7},{4,0},{5,1},{6,2},{7,3},{8,12},{9,13},{10,... | collective-permute-start | bytes 6152 | tf_op jit(solution)/shard_map/ppermute | solution.py:615

commit v6 on v5

--- a/solution.py
+++ b/solution.py
@@ -1,4 +1,5 @@
 import functools
+import math
 
 import numpy as np
 
@@ -48,7 +49,7 @@
             cost_estimate=pl.CostEstimate(flops=1024, bytes_accessed=1024, transcendentals=0),
             name=getattr(kernel, "func", kernel).__name__,
         )(*arrays, *extra)
-        self.last = results[0]
+        self.last = results[-1]
         return results
 
 
@@ -152,28 +153,33 @@
         refs[2][...] = total[2 * cells : 2 * cells + 8] + total[2 * cells + 8 :]
 
 
-def own_rows(distribution, velocity, capacity, out, speeds, weight, sems):
-    modes, cells = (velocity.shape[1], out.shape[1])
+def own_rows(distribution, velocity, capacity, out, token, speeds, weight, rows, sems):
+    modes, cells = velocity.shape[1], out.shape[1]
+    field = pltpu.make_async_copy(
+        distribution.at[:, pl.ds(0, cells)], out.at[pl.ds(0, modes), :], sems.at[0]
+    )
+    field.start()
     copies = [
-        pltpu.make_async_copy(velocity, speeds, sems.at[0]),
-        pltpu.make_async_copy(capacity, weight, sems.at[1]),
-        pltpu.make_async_copy(
-            distribution.at[:, pl.ds(0, cells)], out.at[pl.ds(0, modes), :], sems.at[2]
-        ),
+        pltpu.make_async_copy(velocity, speeds, sems.at[1]),
+        pltpu.make_async_copy(capacity, weight, sems.at[2]),
     ]
     for copy in copies:
         copy.start()
-    for copy in copies[:2]:
+    token[...] = jnp.zeros_like(token)
+    rows[...] = jnp.zeros_like(rows)
+    for copy in copies:
         copy.wait()
     per = modes // LANES
-    out[modes:] = jnp.zeros((out.shape[0] - modes, LANES), jnp.float32)
     for d in range(2):
         for i in range(per):
             lanes = slice(i * LANES, (i + 1) * LANES)
-            out[modes + d * per + i : modes + d * per + i + 1, :] = (
-                speeds[d : d + 1, lanes] * weight[:, lanes]
-            )
-    copies[2].wait()
+            rows[d * per + i : d * per + i + 1, :] = speeds[d : d + 1, lanes] * weight[:, lanes]
+    extra = pltpu.make_async_copy(
+        rows, out.at[pl.ds(modes, rows.shape[0]), :], sems.at[3]
+    )
+    extra.start()
+    field.wait()
+    extra.wait()
 
 
 def payload(numbers, slots, arrived, *refs):
@@ -209,20 +215,32 @@
     out[...] = one[...] + two[...]
 
 
-def turn_sum(scale, one, two, terms, base, out, strip):
+def add_all(*refs):
+    out, token = refs[-2:]
+    total = refs[0][...]
+    for ref in refs[1:-2]:
+        total = total + ref[...]
+    out[...] = total
+    token[...] = jnp.zeros_like(token)
+
+
+def take_off(scale, arrived, terms, base, out):
     modes = terms.shape[0]
-    total = one[:modes] + two[:modes] + terms[...]
-    value = base[...] - scale * total
+    out[...] = base[...] - scale * (arrived[:modes] + terms[...])
+
+
+def turn_sum(scale, arrived, base, out, strip):
+    modes = base.shape[0]
+    value = base[...] - scale * arrived[:modes]
     out[...] = value
     strip[...] = value.T[-HALO:]
 
 
-def last_sum(scale, one, two, terms, base, other, out, value, sems):
+def last_sum(scale, arrived, base, other, out, value, sems):
     cells = base.shape[1]
     ahead = pltpu.make_async_copy(other, out.at[:, pl.ds(cells, cells)], sems.at[0])
     ahead.start()
-    total = one[...] + two[...] + terms[...]
-    value[...] = base[...] - scale * total
+    value[...] = base[...] - scale * arrived[...]
     copy = pltpu.make_async_copy(value, out.at[:, pl.ds(0, cells)], sems.at[1])
     copy.start()
     ahead.wait()
@@ -312,6 +330,7 @@
 
 
 def second_rest(
+    flux_scale,
     field,
     mid_a,
     mid_b,
@@ -343,7 +362,7 @@
         end_b[rows, :] = end[:, half:]
         for d in range(2):
             terms = columns[:, 3 + d : 4 + d] * end - taken[:, d : d + 1] * mid
-            flux[d : d + 1, :] += jnp.sum(terms, axis=0, keepdims=True)
+            flux[d : d + 1, :] += flux_scale * jnp.sum(terms, axis=0, keepdims=True)
         return 0
 
     lax.fori_loop(0, modes // block, step, 0)
@@ -465,9 +484,11 @@
         def take_own(self):
             self.blocks.append((self.own, exchange(self.own)))
 
-        def send(self, step):
+        def send(self, step, between=None):
             sent = {}
             for stream in (step % 2, 1 - step % 2):
+                if between is not None and sent:
+                    between()
                 numbers = plan.sent[stream, step]
                 slots = sorted({n for n in numbers if n >= 0})
                 for slot in slots:
@@ -506,19 +527,24 @@
             self.total = results[0]
             return results
 
-        def ends(self):
-            return [self.arrived[0][-1], self.arrived[1][-1], self.terms[-1]]
-
-    (own,) = call(
+        def ends(self, base):
+            first = (chips - 1) % 2
+            kernel = functools.partial(take_off, self.scale)
+            (rest,) = call(kernel, [part], [self.arrived[first][-1], self.terms[-1], base])
+            return [self.arrived[1 - first][-1], rest]
+
+    own, _ = call(
         own_rows,
-        [(modes + extra, half)],
+        [(modes + extra, half), (8, LANES)],
         [distribution, velocity, cap],
         places=[HBM] * 3,
         scratch=[
             pltpu.VMEM((2, modes), jnp.float32),
             pltpu.VMEM((1, modes), jnp.float32),
-            pltpu.SemaphoreType.DMA((3,)),
+            pltpu.VMEM((extra, LANES), jnp.float32),
+            pltpu.SemaphoreType.DMA((4,)),
         ],
+        out_specs=[HBM, VMEM],
         room=56,
     )
     one = Round(None, time_step, True)
@@ -563,7 +589,7 @@
     two = Round(matrix, step_size, False)
     two.add_terms(mid_a)
     mid_b, last = call(
-        functools.partial(turn_sum, time_step), [part, (HALO, modes)], [*one.ends(), base_b]
+        functools.partial(turn_sum, time_step), [part, (HALO, modes)], one.ends(base_b)
     )
     two.begin(mid_b)
     two.join_terms(0)
@@ -572,54 +598,58 @@
     two.take_own()
     strips = call(strip_pairs, [(HALO, modes)] * 2, [leading, last])
     strips = paired(*strips)
-    adding = None
+    flux = None
     for step in range(1, chips):
-        if adding is not None:
-            adding.next()
-        two.send(step)
         if step == 1:
+            two.send(step)
             two.join_terms(*(s for s in range(1, chips - 1) if isinstance(two.terms[s], tuple)))
-        two.take(step, 2 if step == chips - 1 else 1)
+        elif step == 2:
+            two.send(step, lambda: flux.over(1))
+        elif step == chips - 1:
+            two.send(step, lambda: flux.over(*range(2, devices, 2)))
+        else:
+            two.send(step)
+        if step == 2 and isinstance(two.terms[-1], tuple):
+            two.join_terms(chips - 1)
+        two.take(step, 2 if step >= chips - 2 else 1)
         if step == 1:
             two.add_terms(mid_a)
-        two.multiply(step - 1)
+        if step < chips - 1:
+            two.multiply(step - 1)
+        if step == chips - 2:
+            two.multiply(step)
         if step == 1:
-            end_a, end_b, flux = call(
-                second_rest,
+            end_a, end_b, part_flux = call(
+                functools.partial(second_rest, 1.0 / math.sqrt(total_modes)),
                 [part, part, (2, cells)],
                 [distribution, mid_a, mid_b, *strips, operators, table, kinds, scattered],
                 scratch=aside,
             )
-            adding = Adding(call, flux, devices)
+            flux = Flux(call, part_flux, devices)
     (last_b,) = two.multiply(chips - 1, end_b)
-    heat_flux = adding.finish() / jnp.sqrt(jnp.float32(total_modes))
+    heat_flux = flux.value
     if isinstance(two.terms[-1], tuple):
         two.join_terms(chips - 1)
     (updated,) = call(
         functools.partial(last_sum, step_size),
         [(modes, cells)],
-        [*two.ends(), end_a, last_b],
+        [*two.ends(end_a), last_b],
         scratch=[pltpu.VMEM(part, jnp.float32), pltpu.SemaphoreType.DMA((2,))],
         out_specs=[HBM],
     )
     return (updated, heat_flux)
 
 
-class Adding:
+class Flux:
     def __init__(self, call, value, devices):
-        self.call, self.value, self.devices, self.bit = call, value, devices, 1
-
-    def next(self):
-        if self.bit < self.devices:
-            pairs = [(i, i ^ self.bit) for i in range(self.devices)]
-            came = lax.ppermute(self.value, "mode", pairs)
-            (self.value,) = self.call(add, [self.value.shape], [self.value, came])
-            self.bit *= 2
-
-    def finish(self):
-        while self.bit < self.devices:
-            self.next()
-        return self.value
+        self.call, self.value, self.devices = call, value, devices
+
+    def over(self, *bits):
+        came = [
+            lax.ppermute(self.value, "mode", [(i, i ^ bit) for i in range(self.devices)])
+            for bit in bits
+        ]
+        self.value, _ = self.call(add_all, [self.value.shape, (8, LANES)], [self.value, *came])
 
 
 def solution(mesh):

time: 138 us -> 151 us (1.094); the launches traced: 135 us -> 150 us
  Pallas kernels: 33.8 us -> 50.3 us
  waiting for transfers between devices: 33.9 us -> 31.8 us
    pallas_call x50 -> x51, Pallas kernels: 33.8 us -> 50.3 us  [__call__(): pl.pallas_call(body, out_shape=[jax.ShapeDtypeStruct(shape, jnp.float32)...]
    ppermute x3 -> x4, waiting for transfers between devices: 11.6 us -> 0.01 us  [over(): lax.ppermute(self.value, 'mode', [(i, i ^ bit) for i in range(self.device...]
    ppermute x16, waiting for transfers between devices: 17.4 us -> 24.2 us  [along(): return lax.ppermute(value, 'mode', plan.pairs[stream])]
    ppermute x18 -> x19, starting transfers between devices: 9.18 us -> 12.3 us  [exchange(): return lax.ppermute(value, 'mode', across)]
    ppermute x3 -> x4, starting transfers between devices: 4.43 us -> 2.73 us  [over(): lax.ppermute(self.value, 'mode', [(i, i ^ bit) for i in range(self.device...]
    ppermute x18 -> x19, waiting for transfers between devices: 2.34 us -> 3.92 us  [exchange(): return lax.ppermute(value, 'mode', across)]
  transfers between devices with their start and end apart: 41 -> 43, of which waited for: 13 -> 15; matrix products, arithmetic and copies ran while one was open for 1% -> 0% of each run, Pallas kernels for 23% -> 21%
where the time goes in v6:
time: 151 us; the launch traced here: 150 us
  starting transfers between devices  65.6 us (43%)
  Pallas kernels  50.3 us (33%)
  waiting for transfers between devices  31.8 us (21%)
  between operations  1.58 us (1%)
    pallas_call x51, Pallas kernels, __call__(): pl.pallas_call(body, out_shape=[jax.ShapeDtypeStruct(shape, jnp.float32)...  50.3 us
    ppermute x16, starting transfers between devices, along(): return lax.ppermute(value, 'mode', plan.pairs[stream])  43.4 us
    ppermute x16, waiting for transfers between devices, along(): return lax.ppermute(value, 'mode', plan.pairs[stream])  24.2 us
    ppermute x19, starting transfers between devices, exchange(): return lax.ppermute(value, 'mode', across)  12.3 us
    ppermute x4, starting transfers between devices, paired(): lax.ppermute(value, 'space', pairs + [(j, i) for i, j in pairs])  7.17 us
    ppermute x19, waiting for transfers between devices, exchange(): return lax.ppermute(value, 'mode', across)  3.92 us
    ppermute x4, waiting for transfers between devices, paired(): lax.ppermute(value, 'space', pairs + [(j, i) for i, j in pairs])  3.7 us
  transfers between devices with their start and end apart: 43, of which 15 were waited for; matrix products, arithmetic and copies ran while one was open for 0% of the time, Pallas kernels for 21%

profile of v6, /device:TPU:13, one launch (start us, length us, event | category | flops | bytes accessed | tf_op | source)
XLA Modules:
  0.0 150.3 jit_solution(3893249416413846620)
XLA Ops:
  0.6 17.6 %own_rows.1 = (f32[1040,128]{1,0:T(8,128)}, f32[8,128]{1,0:T(8,128)}) custom-call(f32[1024,256]{1,0:T(8,128)} %refs_0_.9, f32[2,1024]{1,0:T(2,128)} %refs_1_.2, f32[1,1024]{1,0:T(1,128)} %bitcast.4), custom_call_target="tpu_custom_call" | custom-call | flops 1024 | bytes 1024 | tf_op jit(solution)/shard_map/own_rows/pallas_call | solution.py:39
  18.3 2.1 %collective-permute-start = (f32[1040,128]{1,0:T(8,128)}, f32[1040,128]{1,0:T(8,128)S(1)}, u32[]{:S(2)}, u32[]{:S(2)}) collective-permute-start(f32[1040,128]{1,0:T(8,128)} %get-tuple-element.41.refs_1_), channel_id=1, source_target_pairs={{1,3},{2,4},{5,7},{3,1},{4,2},{7,5},{9,11},{10,12},{13,15},{11,9},... | collective-permute-start | bytes 1597448 | tf_op jit(solution)/shard_map/ppermute | solution.py:463
  20.3 4.3 %collective-permute-start.2 = (f32[1040,128]{1,0:T(8,128)}, f32[1040,128]{1,0:T(8,128)S(1)}, u32[]{:S(2)}, u32[]{:S(2)}) collective-permute-start(f32[1040,128]{1,0:T(8,128)} %get-tuple-element.41.refs_1_), channel_id=1, source_target_pairs={{0,2},{3,5},{4,6},{2,0},{5,3},{6,4},{8,10},{11,13},{12,14},{10,8},... | collective-permute-start | bytes 1597448 | tf_op jit(solution)/shard_map/ppermute | solution.py:463
  24.7 0.7 copy-done.3
  25.4 7.4 %load_and_products.1 = (f32[1024,128]{1,0:T(8,128)S(1)}, f32[1024,128]{1,0:T(8,128)S(1)}, f32[1024,128]{1,0:T(8,128)S(1)}, f32[1024,128]{1,0:T(8,128)S(1)}, f32[...) custom-call(bf16[8192,1024]{1,0:T(8,128)(2,1)} %refs_0_.6, ...), custom_call_target="tpu_custom_call" | custom-call | flops 1024 | bytes 1024 | tf_op jit(solution)/shard_map/load_and_products/pallas_call | solution.py:39
  32.9 0.5 collective-permute-start.4
  33.5 0.6 collective-permute-start.6
  34.0 1.3 collective-permute-done.2.refs_0_
  35.5 2.3 %collective-permute-start.5 = (f32[1040,128]{1,0:T(8,128)S(1)}, f32[1040,128]{1,0:T(8,128)S(1)}, u32[]{:S(2)}, u32[]{:S(2)}) collective-permute-start(f32[1040,128]{1,0:T(8,128)S(1)} %payload.12.refs_2_), channel_id=1, source_target_pairs={{1,3},{2,4},{5,7},{3,1},{4,2},{7,5},{9,11},{10,12},{13,15},{11,9},... | collective-permute-start | bytes 1597448 | tf_op jit(solution)/shard_map/ppermute | solution.py:463
  37.9 2.8 %collective-permute-start.3 = (f32[1040,128]{1,0:T(8,128)S(1)}, f32[1040,128]{1,0:T(8,128)S(1)}, u32[]{:S(2)}, u32[]{:S(2)}) collective-permute-start(f32[1040,128]{1,0:T(8,128)S(1)} %payload.13.refs_2_), channel_id=1, source_target_pairs={{0,2},{3,5},{4,6},{2,0},{5,3},{6,4},{8,10},{11,13},{12,14},{10,8},... | collective-permute-start | bytes 1597448 | tf_op jit(solution)/shard_map/ppermute | solution.py:463
  40.8 0.5 collective-permute-start.13
  41.4 1.3 collective-permute-done.7.refs_1_
  43.1 1.4 two_blocks.8.refs_3_
  44.5 3.4 %collective-permute-done.5.refs_0_.refs_2_ = f32[1040,128]{1,0:T(8,128)S(1)} collective-permute-done((f32[1040,128]{1,0:T(8,128)S(1)}, f32[1040,128]{1,0:T(8,128)S(1)}, u32[]{:S(2)}, u32[]{:S(2)}) %collective-permute-start.5) | collective-permute-done | bytes 532512 | tf_op jit(solution)/shard_map/ppermute | solution.py:463
  48.0 4.3 %collective-permute-start.10 = (f32[1040,128]{1,0:T(8,128)S(1)}, f32[1040,128]{1,0:T(8,128)S(1)}, u32[]{:S(2)}, u32[]{:S(2)}) collective-permute-start(f32[1040,128]{1,0:T(8,128)S(1)} %payload.14.refs_3_), channel_id=1, source_target_pairs={{0,2},{3,5},{4,6},{2,0},{5,3},{6,4},{8,10},{11,13},{12,14},{10,8},... | collective-permute-start | bytes 1597448 | tf_op jit(solution)/shard_map/ppermute | solution.py:463
  52.4 1.9 %collective-permute-start.9 = (f32[1040,128]{1,0:T(8,128)S(1)}, f32[1040,128]{1,0:T(8,128)S(1)}, u32[]{:S(2)}, u32[]{:S(2)}) collective-permute-start(f32[1040,128]{1,0:T(8,128)S(1)} %payload.15.refs_3_), channel_id=1, source_target_pairs={{1,3},{2,4},{5,7},{3,1},{4,2},{7,5},{9,11},{10,12},{13,15},{11,9},... | collective-permute-start | bytes 1597448 | tf_op jit(solution)/shard_map/ppermute | solution.py:463
  54.4 3.1 %collective-permute-start.12 = (f32[32,1024]{1,0:T(8,128)S(1)}, f32[32,1024]{1,0:T(8,128)S(1)}, u32[]{:S(2)}, u32[]{:S(2)}) collective-permute-start(f32[32,1024]{1,0:T(8,128)S(1)} %get-tuple-element.54.refs_3_), channel_id=1, source_target_pairs={{8,16},{16,8},{9,17},{17,9},{10,18},{18,10},{11,19},{19,11},{12,20... | collective-permute-start | bytes 393224 | tf_op jit(solution)/shard_map/ppermute | solution.py:376
  57.7 1.5 collective-permute-start.18
  59.2 1.4 two_blocks.9.refs_6_.refs_3_
  60.6 1.3 collective-permute-done.11.refs_1_
  61.9 2.2 %first_rest.1 = (f32[1024,128]{1,0:T(8,128)S(1)}, f32[1024,128]{1,0:T(8,128)S(1)}) custom-call(f32[1024,256]{1,0:T(8,128)S(1)} %copy-done, f32[32,1024]{1,0:T(8,128)S(1)} %collective-permute-done.11.refs_1_, f32[32,1024]{1,0:T(8,128)S(1)} %collective-permute-done.12.refs_2_, bf16[640,1024]{1,0:T(8,128)(2,1)S(1)} %copy-done.1, ...), custom_call_target="tpu_custom_call" | custom-call | flops 1024 | bytes 1024 | tf_op jit(solution)/shard_map/first_rest/pallas_call | solution.py:39
  64.2 1.5 collective-permute-done.9.refs_0_.refs_3_
  65.9 1.2 collective-permute-start.16
  67.2 1.9 %collective-permute-start.15 = (f32[1040,128]{1,0:T(8,128)S(1)}, f32[1040,128]{1,0:T(8,128)S(1)}, u32[]{:S(2)}, u32[]{:S(2)}) collective-permute-start(f32[1040,128]{1,0:T(8,128)S(1)} %payload.16.refs_3_), channel_id=1, source_target_pairs={{1,3},{2,4},{5,7},{3,1},{4,2},{7,5},{9,11},{10,12},{13,15},{11,9},... | collective-permute-start | bytes 1597448 | tf_op jit(solution)/shard_map/ppermute | solution.py:463
  69.1 3.4 %collective-permute-start.14 = (f32[1040,128]{1,0:T(8,128)S(1)}, f32[1040,128]{1,0:T(8,128)S(1)}, u32[]{:S(2)}, u32[]{:S(2)}) collective-permute-start(f32[1040,128]{1,0:T(8,128)S(1)} %payload.17.refs_4_), channel_id=1, source_target_pairs={{0,2},{3,5},{4,6},{2,0},{5,3},{6,4},{8,10},{11,13},{12,14},{10,8},... | collective-permute-start | bytes 1597448 | tf_op jit(solution)/shard_map/ppermute | solution.py:463
  72.6 1.4 two_blocks.10.refs_4_.refs_6_
  74.0 1.5 %two_blocks.11 = (f32[1024,128]{1,0:T(8,128)S(1)}, f32[32,1024]{1,0:T(8,128)S(1)}, f32[8,1024]{1,0:T(8,128)S(1)}) custom-call(bf16[8192,1024]{1,0:T(8,128)(2,1)S(1)} %get-tuple-element.45.refs_2_.refs_0_, f32[1040,128]{1,0:T(8,128)S(1)} %pick.8.refs_4_.refs_1_, f32[520,128]{1,0:T(8,128)S(1)} %collective-permute-done.16.refs_2_, ...), custom_call_target="tpu_custom_call" | custom-call | flops 1024 | bytes 1024 | tf_op jit(solution)/shard_map/two_blocks/pallas_call | solution.py:39
  75.5 1.3 slot_products.4
  76.9 2.6 %collective-permute-done.15.refs_0_ = f32[1040,128]{1,0:T(8,128)S(1)} collective-permute-done((f32[1040,128]{1,0:T(8,128)S(1)}, f32[1040,128]{1,0:T(8,128)S(1)}, u32[]{:S(2)}, u32[]{:S(2)}) %collective-permute-start.15) | collective-permute-done | bytes 532512 | tf_op jit(solution)/shard_map/ppermute | solution.py:463
  79.6 4.3 %collective-permute-done.14.refs_0_ = f32[1040,128]{1,0:T(8,128)S(1)} collective-permute-done((f32[1040,128]{1,0:T(8,128)S(1)}, f32[1040,128]{1,0:T(8,128)S(1)}, u32[]{:S(2)}, u32[]{:S(2)}) %collective-permute-start.14) | collective-permute-done | bytes 532512 | tf_op jit(solution)/shard_map/ppermute | solution.py:463
  84.0 2.5 %collective-permute-start.21 = (f32[1024,128]{1,0:T(8,128)S(1)}, f32[1024,128]{1,0:T(8,128)S(1)}, u32[]{:S(2)}, u32[]{:S(2)}) collective-permute-start(f32[1024,128]{1,0:T(8,128)S(1)} %get-tuple-element.61.refs_1_.refs_2_), channel_id=1, source_target_pairs={{0,2},{3,5},{4,6},{2,0},{5,3},{6,4},{8,10},{11,13},{12,14},{10,8},... | collective-permute-start | bytes 1572872 | tf_op jit(solution)/shard_map/ppermute | solution.py:463
  86.6 1.9 %collective-permute-start.19 = (f32[1024,128]{1,0:T(8,128)S(1)}, f32[1024,128]{1,0:T(8,128)S(1)}, u32[]{:S(2)}, u32[]{:S(2)}) collective-permute-start(f32[1024,128]{1,0:T(8,128)S(1)} %get-tuple-element.61.refs_1_.refs_2_), channel_id=1, source_target_pairs={{1,3},{2,4},{5,7},{3,1},{4,2},{7,5},{9,11},{10,12},{13,15},{11,9},... | collective-permute-start | bytes 1572872 | tf_op jit(solution)/shard_map/ppermute | solution.py:463
  88.6 1.3 slot_products.5
  89.8 1.1 collective-permute-start.23
  91.0 1.3 slot_products.6
  92.3 0.5 collective-permute-start.26
  92.8 4.5 %collective-permute-done.21.refs_0_ = f32[1024,128]{1,0:T(8,128)S(1)} collective-permute-done((f32[1024,128]{1,0:T(8,128)S(1)}, f32[1024,128]{1,0:T(8,128)S(1)}, u32[]{:S(2)}, u32[]{:S(2)}) %collective-permute-start.21) | collective-permute-done | bytes 524320 | tf_op jit(solution)/shard_map/ppermute | solution.py:463
  97.4 1.9 %collective-permute-start.29 = (f32[1024,128]{1,0:T(8,128)S(1)}, f32[1024,128]{1,0:T(8,128)S(1)}, u32[]{:S(2)}, u32[]{:S(2)}) collective-permute-start(f32[1024,128]{1,0:T(8,128)S(1)} %payload.18.refs_2_), channel_id=1, source_target_pairs={{1,3},{2,4},{5,7},{3,1},{4,2},{7,5},{9,11},{10,12},{13,15},{11,9},... | collective-permute-start | bytes 1572872 | tf_op jit(solution)/shard_map/ppermute | solution.py:463
  99.3 0.6 collective-permute-done.19.refs_0_.refs_1_
  99.9 2.9 %collective-permute-start.22 = (f32[1024,128]{1,0:T(8,128)S(1)}, f32[1024,128]{1,0:T(8,128)S(1)}, u32[]{:S(2)}, u32[]{:S(2)}) collective-permute-start(f32[1024,128]{1,0:T(8,128)S(1)} %payload.19.refs_2_), channel_id=1, source_target_pairs={{0,2},{3,5},{4,6},{2,0},{5,3},{6,4},{8,10},{11,13},{12,14},{10,8},... | collective-permute-start | bytes 1572872 | tf_op jit(solution)/shard_map/ppermute | solution.py:463
  103.0 1.3 slot_products.7
  104.2 0.8 collective-permute-start.35
  105.1 0.9 collective-permute-start.24
  106.0 3.1 %collective-permute-start.25 = (f32[32,1024]{1,0:T(8,128)S(1)}, f32[32,1024]{1,0:T(8,128)S(1)}, u32[]{:S(2)}, u32[]{:S(2)}) collective-permute-start(f32[32,1024]{1,0:T(8,128)S(1)} %get-tuple-element.67.refs_2_), channel_id=1, source_target_pairs={{8,16},{16,8},{9,17},{17,9},{10,18},{18,10},{11,19},{19,11},{12,20... | collective-permute-start | bytes 393224 | tf_op jit(solution)/shard_map/ppermute | solution.py:376
  109.1 1.3 two_blocks.12.refs_9_.refs_3_
  110.5 0.7 collective-permute-start.38
  111.1 2.4 %collective-permute-done.25.refs_4_ = f32[32,1024]{1,0:T(8,128)S(1)} collective-permute-done((f32[32,1024]{1,0:T(8,128)S(1)}, f32[32,1024]{1,0:T(8,128)S(1)}, u32[]{:S(2)}, u32[]{:S(2)}) %collective-permute-start.25) | collective-permute-done | bytes 131104 | tf_op jit(solution)/shard_map/ppermute | solution.py:376
  113.5 2.8 %second_rest.1 = (f32[1024,128]{1,0:T(8,128)S(1)}, f32[1024,128]{1,0:T(8,128)S(1)}, f32[2,256]{1,0:T(2,128)S(1)}) custom-call(f32[1024,256]{1,0:T(8,128)S(1)} %copy-done, f32[1024,128]{1,0:T(8,128)S(1)} %get-tuple-element.58.refs_1_, f32[1024,128]{1,0:T(8,128)S(1)} %get-tuple-element.61.refs_1_.refs_2_, f32[32,1024]{1,0:T(8,128)S(1)} %collective-permute-done.24.refs_3_, ...), custom_call_target="tpu_custom_call" | custom-call | flops 1024 | bytes 1024 | tf_op jit(solution)/shard_map/second_rest/pallas_call | solution.py:39
  116.3 1.2 collective-permute-start.28
  117.7 3.2 %collective-permute-start.34 = (f32[1024,128]{1,0:T(8,128)S(1)}, f32[1024,128]{1,0:T(8,128)S(1)}, u32[]{:S(2)}, u32[]{:S(2)}) collective-permute-start(f32[1024,128]{1,0:T(8,128)S(1)} %payload.20.refs_2_), channel_id=1, source_target_pairs={{0,2},{3,5},{4,6},{2,0},{5,3},{6,4},{8,10},{11,13},{12,14},{10,8},... | collective-permute-start | bytes 1572872 | tf_op jit(solution)/shard_map/ppermute | solution.py:463
  121.0 1.9 %collective-permute-start.30 = (f32[1024,128]{1,0:T(8,128)S(1)}, f32[1024,128]{1,0:T(8,128)S(1)}, u32[]{:S(2)}, u32[]{:S(2)}) collective-permute-start(f32[1024,128]{1,0:T(8,128)S(1)} %payload.21.refs_2_), channel_id=1, source_target_pairs={{1,3},{2,4},{5,7},{3,1},{4,2},{7,5},{9,11},{10,12},{13,15},{11,9},... | collective-permute-start | bytes 1572872 | tf_op jit(solution)/shard_map/ppermute | solution.py:463
  123.3 2.4 %collective-permute-start.36 = (f32[512,128]{1,0:T(8,128)S(1)}, f32[512,128]{1,0:T(8,128)S(1)}, u32[]{:S(2)}, u32[]{:S(2)}) collective-permute-start(f32[512,128]{1,0:T(8,128)S(1)} %get-tuple-element.85), channel_id=1, source_target_pairs={{0,1},{1,0},{2,3},{3,2},{4,5},{5,4},{6,7},{7,6},{8,9},{9,8},{10,11... | collective-permute-start | bytes 786440 | tf_op jit(solution)/shard_map/ppermute | solution.py:460
  125.8 1.1 collective-permute-done.36.refs_2_
  127.2 1.2 collective-permute-start.33
  128.4 1.3 two_blocks.13.refs_4_.refs_5_
  129.8 1.3 two_blocks.14.refs_3_.refs_4_
  131.2 3.9 %collective-permute-start.40 = (f32[1024,128]{1,0:T(8,128)S(1)}, f32[1024,128]{1,0:T(8,128)S(1)}, u32[]{:S(2)}, u32[]{:S(2)}) collective-permute-start(f32[1024,128]{1,0:T(8,128)S(1)} %payload.22.refs_4_), channel_id=1, source_target_pairs={{1,3},{2,4},{5,7},{3,1},{4,2},{7,5},{9,11},{10,12},{13,15},{11,9},... | collective-permute-start | bytes 1572872 | tf_op jit(solution)/shard_map/ppermute | solution.py:463
  135.1 0.6 add_all.3
  135.8 2.1 %collective-permute-start.39 = (f32[1024,128]{1,0:T(8,128)S(1)}, f32[1024,128]{1,0:T(8,128)S(1)}, u32[]{:S(2)}, u32[]{:S(2)}) collective-permute-start(f32[1024,128]{1,0:T(8,128)S(1)} %payload.23.refs_4_), channel_id=1, source_target_pairs={{0,2},{3,5},{4,6},{2,0},{5,3},{6,4},{8,10},{11,13},{12,14},{10,8},... | collective-permute-start | bytes 1572872 | tf_op jit(solution)/shard_map/ppermute | solution.py:463
  138.0 1.8 %collective-permute-start.41 = (f32[512,128]{1,0:T(8,128)S(1)}, f32[512,128]{1,0:T(8,128)S(1)}, u32[]{:S(2)}, u32[]{:S(2)}) collective-permute-start(f32[512,128]{1,0:T(8,128)S(1)} %get-tuple-element.83), channel_id=1, source_target_pairs={{0,1},{1,0},{2,3},{3,2},{4,5},{5,4},{6,7},{7,6},{8,9},{9,8},{10,11... | collective-permute-start | bytes 786440 | tf_op jit(solution)/shard_map/ppermute | solution.py:460
  139.9 1.1 collective-permute-done.41.refs_2_
  141.4 1.4 two_blocks.15.refs_3_.refs_2_
  142.9 6.2 %collective-permute-done.39.refs_0_ = f32[1024,128]{1,0:T(8,128)S(1)} collective-permute-done((f32[1024,128]{1,0:T(8,128)S(1)}, f32[1024,128]{1,0:T(8,128)S(1)}, u32[]{:S(2)}, u32[]{:S(2)}) %collective-permute-start.39) | collective-permute-done | bytes 524320 | tf_op jit(solution)/shard_map/ppermute | solution.py:463
  149.1 1.0 last_sum.1
  (94 shorter events, 4.4 us)
Async XLA Ops:
  0.6 24.1 %copy-start = (f32[1024,256]{1,0:T(8,128)S(1)}, f32[1024,256]{1,0:T(8,128)}, u32[]{:S(2)}) copy-start(f32[1024,256]{1,0:T(8,128)} %refs_0_.9) | copy-start | bytes 3145732
  18.3 15.2 %collective-permute-start = (f32[1040,128]{1,0:T(8,128)}, f32[1040,128]{1,0:T(8,128)S(1)}, u32[]{:S(2)}, u32[]{:S(2)}) collective-permute-start(f32[1040,128]{1,0:T(8,128)} %get-tuple-element.41.refs_1_), channel_id=1, source_target_pairs={{1,3},{2,4},{5,7},{3,1},{4,2},{7,5},{9,11},{10,12},{13,15},{11,9},... | collective-permute-start | bytes 1597448 | tf_op jit(solution)/shard_map/ppermute | solution.py:463
  20.3 15.0 %collective-permute-start.2 = (f32[1040,128]{1,0:T(8,128)}, f32[1040,128]{1,0:T(8,128)S(1)}, u32[]{:S(2)}, u32[]{:S(2)}) collective-permute-start(f32[1040,128]{1,0:T(8,128)} %get-tuple-element.41.refs_1_), channel_id=1, source_target_pairs={{0,2},{3,5},{4,6},{2,0},{5,3},{6,4},{8,10},{11,13},{12,14},{10,8},... | collective-permute-start | bytes 1597448 | tf_op jit(solution)/shard_map/ppermute | solution.py:463
  24.7 0.7 copy-start.3
  25.4 8.1 %copy-start.2 = (f32[1040,128]{1,0:T(8,128)S(1)}, f32[1040,128]{1,0:T(8,128)}, u32[]{:S(2)}) copy-start(f32[1040,128]{1,0:T(8,128)} %get-tuple-element.41.refs_1_) | copy-start | bytes 1597444
  32.8 2.6 %collective-permute-start.1 = (f32[1024,128]{1,0:T(8,128)S(1)}, f32[1024,128]{1,0:T(8,128)S(1)}, u32[]{:S(2)}, u32[]{:S(2)}) collective-permute-start(f32[1024,128]{1,0:T(8,128)S(1)} %get-tuple-element.44), channel_id=1, source_target_pairs={{0,1},{1,0},{2,3},{3,2},{4,5},{5,4},{6,7},{7,6},{8,9},{9,8},{10,11... | collective-permute-start | bytes 1572872 | tf_op jit(solution)/shard_map/ppermute | solution.py:460
  32.9 7.8 %collective-permute-start.4 = (f32[1024,128]{1,0:T(8,128)S(1)}, f32[1024,128]{1,0:T(8,128)S(1)}, u32[]{:S(2)}, u32[]{:S(2)}) collective-permute-start(f32[1024,128]{1,0:T(8,128)S(1)} %get-tuple-element.47), channel_id=1, source_target_pairs={{0,1},{1,0},{2,3},{3,2},{4,5},{5,4},{6,7},{7,6},{8,9},{9,8},{10,11... | collective-permute-start | bytes 1572872 | tf_op jit(solution)/shard_map/ppermute | solution.py:460
  33.4 7.4 %collective-permute-start.8 = (f32[1024,128]{1,0:T(8,128)S(1)}, f32[1024,128]{1,0:T(8,128)S(1)}, u32[]{:S(2)}, u32[]{:S(2)}) collective-permute-start(f32[1024,128]{1,0:T(8,128)S(1)} %get-tuple-element.51), channel_id=1, source_target_pairs={{0,1},{1,0},{2,3},{3,2},{4,5},{5,4},{6,7},{7,6},{8,9},{9,8},{10,11... | collective-permute-start | bytes 1572872 | tf_op jit(solution)/shard_map/ppermute | solution.py:460
  33.5 9.7 %collective-permute-start.6 = (f32[1040,128]{1,0:T(8,128)S(1)}, f32[1040,128]{1,0:T(8,128)S(1)}, u32[]{:S(2)}, u32[]{:S(2)}) collective-permute-start(f32[1040,128]{1,0:T(8,128)S(1)} %copy-done.2), channel_id=1, source_target_pairs={{0,1},{1,0},{2,3},{3,2},{4,5},{5,4},{6,7},{7,6},{8,9},{9,8},{10,11... | collective-permute-start | bytes 1597448 | tf_op jit(solution)/shard_map/ppermute | solution.py:460
  35.5 12.4 %collective-permute-start.5 = (f32[1040,128]{1,0:T(8,128)S(1)}, f32[1040,128]{1,0:T(8,128)S(1)}, u32[]{:S(2)}, u32[]{:S(2)}) collective-permute-start(f32[1040,128]{1,0:T(8,128)S(1)} %payload.12.refs_2_), channel_id=1, source_target_pairs={{1,3},{2,4},{5,7},{3,1},{4,2},{7,5},{9,11},{10,12},{13,15},{11,9},... | collective-permute-start | bytes 1597448 | tf_op jit(solution)/shard_map/ppermute | solution.py:463
  37.9 14.4 %collective-permute-start.3 = (f32[1040,128]{1,0:T(8,128)S(1)}, f32[1040,128]{1,0:T(8,128)S(1)}, u32[]{:S(2)}, u32[]{:S(2)}) collective-permute-start(f32[1040,128]{1,0:T(8,128)S(1)} %payload.13.refs_2_), channel_id=1, source_target_pairs={{0,2},{3,5},{4,6},{2,0},{5,3},{6,4},{8,10},{11,13},{12,14},{10,8},... | collective-permute-start | bytes 1597448 | tf_op jit(solution)/shard_map/ppermute | solution.py:463
  40.7 2.0 %collective-permute-start.7 = (f32[1024,128]{1,0:T(8,128)S(1)}, f32[1024,128]{1,0:T(8,128)S(1)}, u32[]{:S(2)}, u32[]{:S(2)}) collective-permute-start(f32[1024,128]{1,0:T(8,128)S(1)} %get-tuple-element.49), channel_id=1, source_target_pairs={{0,1},{1,0},{2,3},{3,2},{4,5},{5,4},{6,7},{7,6},{8,9},{9,8},{10,11... | collective-permute-start | bytes 1572872 | tf_op jit(solution)/shard_map/ppermute | solution.py:460
  40.8 16.8 %collective-permute-start.13 = (f32[1040,128]{1,0:T(8,128)S(1)}, f32[1040,128]{1,0:T(8,128)S(1)}, u32[]{:S(2)}, u32[]{:S(2)}) collective-permute-start(f32[1040,128]{1,0:T(8,128)S(1)} %pick.6.refs_2_.refs_1_), channel_id=1, source_target_pairs={{0,1},{1,0},{2,3},{3,2},{4,5},{5,4},{6,7},{7,6},{8,9},{9,8},{10,11... | collective-permute-start | bytes 1597448 | tf_op jit(solution)/shard_map/ppermute | solution.py:460
  48.0 6.5 %copy-start.5 = (f32[2,1024]{1,0:T(2,128)S(1)}, f32[2,1024]{1,0:T(2,128)}, u32[]{:S(2)}) copy-start(f32[2,1024]{1,0:T(2,128)} %refs_1_.2) | copy-start | bytes 24580
  48.0 6.4 %copy-start.6 = (f32[1024]{0:T(1024)S(1)}, f32[1024]{0:T(1024)}, u32[]{:S(2)}) copy-start(f32[1024]{0:T(1024)} %param.9) | copy-start | bytes 12292
  48.0 16.1 %collective-permute-start.10 = (f32[1040,128]{1,0:T(8,128)S(1)}, f32[1040,128]{1,0:T(8,128)S(1)}, u32[]{:S(2)}, u32[]{:S(2)}) collective-permute-start(f32[1040,128]{1,0:T(8,128)S(1)} %payload.14.refs_3_), channel_id=1, source_target_pairs={{0,2},{3,5},{4,6},{2,0},{5,3},{6,4},{8,10},{11,13},{12,14},{10,8},... | collective-permute-start | bytes 1597448 | tf_op jit(solution)/shard_map/ppermute | solution.py:463
  52.4 13.3 %collective-permute-start.9 = (f32[1040,128]{1,0:T(8,128)S(1)}, f32[1040,128]{1,0:T(8,128)S(1)}, u32[]{:S(2)}, u32[]{:S(2)}) collective-permute-start(f32[1040,128]{1,0:T(8,128)S(1)} %payload.15.refs_3_), channel_id=1, source_target_pairs={{1,3},{2,4},{5,7},{3,1},{4,2},{7,5},{9,11},{10,12},{13,15},{11,9},... | collective-permute-start | bytes 1597448 | tf_op jit(solution)/shard_map/ppermute | solution.py:463
  54.4 7.5 %collective-permute-start.12 = (f32[32,1024]{1,0:T(8,128)S(1)}, f32[32,1024]{1,0:T(8,128)S(1)}, u32[]{:S(2)}, u32[]{:S(2)}) collective-permute-start(f32[32,1024]{1,0:T(8,128)S(1)} %get-tuple-element.54.refs_3_), channel_id=1, source_target_pairs={{8,16},{16,8},{9,17},{17,9},{10,18},{18,10},{11,19},{19,11},{12,20... | collective-permute-start | bytes 393224 | tf_op jit(solution)/shard_map/ppermute | solution.py:376
  57.5 4.4 %collective-permute-start.11 = (f32[32,1024]{1,0:T(8,128)S(1)}, f32[32,1024]{1,0:T(8,128)S(1)}, u32[]{:S(2)}, u32[]{:S(2)}) collective-permute-start(f32[32,1024]{1,0:T(8,128)S(1)} %get-tuple-element.55), channel_id=1, source_target_pairs={{0,8},{16,24},{8,0},{24,16},{1,9},{17,25},{9,1},{25,17},{2,10},{18... | collective-permute-start | bytes 393224 | tf_op jit(solution)/shard_map/ppermute | solution.py:376
  57.7 14.9 %collective-permute-start.18 = (f32[1040,128]{1,0:T(8,128)S(1)}, f32[1040,128]{1,0:T(8,128)S(1)}, u32[]{:S(2)}, u32[]{:S(2)}) collective-permute-start(f32[1040,128]{1,0:T(8,128)S(1)} %pick.7.refs_4_.refs_1_), channel_id=1, source_target_pairs={{0,1},{1,0},{2,3},{3,2},{4,5},{5,4},{6,7},{7,6},{8,9},{9,8},{10,11... | collective-permute-start | bytes 1597448 | tf_op jit(solution)/shard_map/ppermute | solution.py:460
  59.2 2.7 %copy-start.1 = (bf16[640,1024]{1,0:T(8,128)(2,1)S(1)}, bf16[640,1024]{1,0:T(8,128)(2,1)}, u32[]{:S(2)}) copy-start(bf16[640,1024]{1,0:T(8,128)(2,1)} %constant.4.clone.refs_3_.refs_5_) | copy-start | bytes 3932164
  59.2 2.7 %copy-start.4 = (s32[256]{0:T(256)S(1)}, s32[256]{0:T(256)}, u32[]{:S(2)}) copy-start(s32[256]{0:T(256)} %param.10) | copy-start | bytes 3076
  65.9 8.1 %collective-permute-start.16 = (f32[520,128]{1,0:T(8,128)S(1)}, f32[520,128]{1,0:T(8,128)S(1)}, u32[]{:S(2)}, u32[]{:S(2)}) collective-permute-start(f32[520,128]{1,0:T(8,128)S(1)} %get-tuple-element.81), channel_id=1, source_target_pairs={{0,1},{1,0},{2,3},{3,2},{4,5},{5,4},{6,7},{7,6},{8,9},{9,8},{10,11... | collective-permute-start | bytes 798728 | tf_op jit(solution)/shard_map/ppermute | solution.py:460
  67.1 6.8 %collective-permute-start.17 = (f32[520,128]{1,0:T(8,128)S(1)}, f32[520,128]{1,0:T(8,128)S(1)}, u32[]{:S(2)}, u32[]{:S(2)}) collective-permute-start(f32[520,128]{1,0:T(8,128)S(1)} %get-tuple-element.80), channel_id=1, source_target_pairs={{0,1},{1,0},{2,3},{3,2},{4,5},{5,4},{6,7},{7,6},{8,9},{9,8},{10,11... | collective-permute-start | bytes 798728 | tf_op jit(solution)/shard_map/ppermute | solution.py:460
  67.2 12.2 %collective-permute-start.15 = (f32[1040,128]{1,0:T(8,128)S(1)}, f32[1040,128]{1,0:T(8,128)S(1)}, u32[]{:S(2)}, u32[]{:S(2)}) collective-permute-start(f32[1040,128]{1,0:T(8,128)S(1)} %payload.16.refs_3_), channel_id=1, source_target_pairs={{1,3},{2,4},{5,7},{3,1},{4,2},{7,5},{9,11},{10,12},{13,15},{11,9},... | collective-permute-start | bytes 1597448 | tf_op jit(solution)/shard_map/ppermute | solution.py:463
  69.1 14.7 %collective-permute-start.14 = (f32[1040,128]{1,0:T(8,128)S(1)}, f32[1040,128]{1,0:T(8,128)S(1)}, u32[]{:S(2)}, u32[]{:S(2)}) collective-permute-start(f32[1040,128]{1,0:T(8,128)S(1)} %payload.17.refs_4_), channel_id=1, source_target_pairs={{0,2},{3,5},{4,6},{2,0},{5,3},{6,4},{8,10},{11,13},{12,14},{10,8},... | collective-permute-start | bytes 1597448 | tf_op jit(solution)/shard_map/ppermute | solution.py:463
  76.8 11.7 %collective-permute-start.20 = (f32[1024,128]{1,0:T(8,128)S(1)}, f32[1024,128]{1,0:T(8,128)S(1)}, u32[]{:S(2)}, u32[]{:S(2)}) collective-permute-start(f32[1024,128]{1,0:T(8,128)S(1)} %get-tuple-element.60.refs_3_), channel_id=1, source_target_pairs={{0,1},{1,0},{2,3},{3,2},{4,5},{5,4},{6,7},{7,6},{8,9},{9,8},{10,11... | collective-permute-start | bytes 1572872 | tf_op jit(solution)/shard_map/ppermute | solution.py:460
  84.0 13.3 %collective-permute-start.21 = (f32[1024,128]{1,0:T(8,128)S(1)}, f32[1024,128]{1,0:T(8,128)S(1)}, u32[]{:S(2)}, u32[]{:S(2)}) collective-permute-start(f32[1024,128]{1,0:T(8,128)S(1)} %get-tuple-element.61.refs_1_.refs_2_), channel_id=1, source_target_pairs={{0,2},{3,5},{4,6},{2,0},{5,3},{6,4},{8,10},{11,13},{12,14},{10,8},... | collective-permute-start | bytes 1572872 | tf_op jit(solution)/shard_map/ppermute | solution.py:463
  86.6 13.3 %collective-permute-start.19 = (f32[1024,128]{1,0:T(8,128)S(1)}, f32[1024,128]{1,0:T(8,128)S(1)}, u32[]{:S(2)}, u32[]{:S(2)}) collective-permute-start(f32[1024,128]{1,0:T(8,128)S(1)} %get-tuple-element.61.refs_1_.refs_2_), channel_id=1, source_target_pairs={{1,3},{2,4},{5,7},{3,1},{4,2},{7,5},{9,11},{10,12},{13,15},{11,9},... | collective-permute-start | bytes 1572872 | tf_op jit(solution)/shard_map/ppermute | solution.py:463
  89.8 12.9 %collective-permute-start.23 = (f32[1024,128]{1,0:T(8,128)S(1)}, f32[1024,128]{1,0:T(8,128)S(1)}, u32[]{:S(2)}, u32[]{:S(2)}) collective-permute-start(f32[1024,128]{1,0:T(8,128)S(1)} %get-tuple-element.65.refs_2_), channel_id=1, source_target_pairs={{0,1},{1,0},{2,3},{3,2},{4,5},{5,4},{6,7},{7,6},{8,9},{9,8},{10,11... | collective-permute-start | bytes 1572872 | tf_op jit(solution)/shard_map/ppermute | solution.py:460
  92.2 10.6 %collective-permute-start.27 = (f32[1024,128]{1,0:T(8,128)S(1)}, f32[1024,128]{1,0:T(8,128)S(1)}, u32[]{:S(2)}, u32[]{:S(2)}) collective-permute-start(f32[1024,128]{1,0:T(8,128)S(1)} %get-tuple-element.66.refs_2_), channel_id=1, source_target_pairs={{0,1},{1,0},{2,3},{3,2},{4,5},{5,4},{6,7},{7,6},{8,9},{9,8},{10,11... | collective-permute-start | bytes 1572872 | tf_op jit(solution)/shard_map/ppermute | solution.py:460
  92.3 13.7 %collective-permute-start.26 = (f32[1024,128]{1,0:T(8,128)S(1)}, f32[1024,128]{1,0:T(8,128)S(1)}, u32[]{:S(2)}, u32[]{:S(2)}) collective-permute-start(f32[1024,128]{1,0:T(8,128)S(1)} %get-tuple-element.61.refs_1_.refs_2_), channel_id=1, source_target_pairs={{0,1},{1,0},{2,3},{3,2},{4,5},{5,4},{6,7},{7,6},{8,9},{9,8},{10,11... | collective-permute-start | bytes 1572872 | tf_op jit(solution)/shard_map/ppermute | solution.py:460
  97.4 20.2 %collective-permute-start.29 = (f32[1024,128]{1,0:T(8,128)S(1)}, f32[1024,128]{1,0:T(8,128)S(1)}, u32[]{:S(2)}, u32[]{:S(2)}) collective-permute-start(f32[1024,128]{1,0:T(8,128)S(1)} %payload.18.refs_2_), channel_id=1, source_target_pairs={{1,3},{2,4},{5,7},{3,1},{4,2},{7,5},{9,11},{10,12},{13,15},{11,9},... | collective-permute-start | bytes 1572872 | tf_op jit(solution)/shard_map/ppermute | solution.py:463
  99.9 21.0 %collective-permute-start.22 = (f32[1024,128]{1,0:T(8,128)S(1)}, f32[1024,128]{1,0:T(8,128)S(1)}, u32[]{:S(2)}, u32[]{:S(2)}) collective-permute-start(f32[1024,128]{1,0:T(8,128)S(1)} %payload.19.refs_2_), channel_id=1, source_target_pairs={{0,2},{3,5},{4,6},{2,0},{5,3},{6,4},{8,10},{11,13},{12,14},{10,8},... | collective-permute-start | bytes 1572872 | tf_op jit(solution)/shard_map/ppermute | solution.py:463
  104.2 18.7 %collective-permute-start.35 = (f32[1024,128]{1,0:T(8,128)S(1)}, f32[1024,128]{1,0:T(8,128)S(1)}, u32[]{:S(2)}, u32[]{:S(2)}) collective-permute-start(f32[1024,128]{1,0:T(8,128)S(1)} %get-tuple-element.71.refs_3_), channel_id=1, source_target_pairs={{0,1},{1,0},{2,3},{3,2},{4,5},{5,4},{6,7},{7,6},{8,9},{9,8},{10,11... | collective-permute-start | bytes 1572872 | tf_op jit(solution)/shard_map/ppermute | solution.py:460
  105.1 5.4 %collective-permute-start.24 = (f32[32,1024]{1,0:T(8,128)S(1)}, f32[32,1024]{1,0:T(8,128)S(1)}, u32[]{:S(2)}, u32[]{:S(2)}) collective-permute-start(f32[32,1024]{1,0:T(8,128)S(1)} %get-tuple-element.69), channel_id=1, source_target_pairs={{0,8},{16,24},{8,0},{24,16},{1,9},{17,25},{9,1},{25,17},{2,10},{18... | collective-permute-start | bytes 393224 | tf_op jit(solution)/shard_map/ppermute | solution.py:376
  106.0 7.5 %collective-permute-start.25 = (f32[32,1024]{1,0:T(8,128)S(1)}, f32[32,1024]{1,0:T(8,128)S(1)}, u32[]{:S(2)}, u32[]{:S(2)}) collective-permute-start(f32[32,1024]{1,0:T(8,128)S(1)} %get-tuple-element.67.refs_2_), channel_id=1, source_target_pairs={{8,16},{16,8},{9,17},{17,9},{10,18},{18,10},{11,19},{19,11},{12,20... | collective-permute-start | bytes 393224 | tf_op jit(solution)/shard_map/ppermute | solution.py:376
  110.5 15.3 %collective-permute-start.38 = (f32[1024,128]{1,0:T(8,128)S(1)}, f32[1024,128]{1,0:T(8,128)S(1)}, u32[]{:S(2)}, u32[]{:S(2)}) collective-permute-start(f32[1024,128]{1,0:T(8,128)S(1)} %pick.9.refs_2_.refs_1_), channel_id=1, source_target_pairs={{0,1},{1,0},{2,3},{3,2},{4,5},{5,4},{6,7},{7,6},{8,9},{9,8},{10,11... | collective-permute-start | bytes 1572872 | tf_op jit(solution)/shard_map/ppermute | solution.py:460
  116.3 4.5 %collective-permute-start.28 = (f32[2,256]{1,0:T(2,128)S(1)}, f32[2,256]{1,0:T(2,128)S(1)}, u32[]{:S(2)}, u32[]{:S(2)}) collective-permute-start(f32[2,256]{1,0:T(2,128)S(1)} %get-tuple-element.72.refs_3_.refs_0_), channel_id=1, source_target_pairs={{0,1},{1,0},{2,3},{3,2},{4,5},{5,4},{6,7},{7,6},{8,9},{9,8},{10,11... | collective-permute-start | bytes 6152 | tf_op jit(solution)/shard_map/ppermute | solution.py:649
  117.7 13.4 %collective-permute-start.34 = (f32[1024,128]{1,0:T(8,128)S(1)}, f32[1024,128]{1,0:T(8,128)S(1)}, u32[]{:S(2)}, u32[]{:S(2)}) collective-permute-start(f32[1024,128]{1,0:T(8,128)S(1)} %payload.20.refs_2_), channel_id=1, source_target_pairs={{0,2},{3,5},{4,6},{2,0},{5,3},{6,4},{8,10},{11,13},{12,14},{10,8},... | collective-permute-start | bytes 1572872 | tf_op jit(solution)/shard_map/ppermute | solution.py:463
  121.0 14.8 %collective-permute-start.30 = (f32[1024,128]{1,0:T(8,128)S(1)}, f32[1024,128]{1,0:T(8,128)S(1)}, u32[]{:S(2)}, u32[]{:S(2)}) collective-permute-start(f32[1024,128]{1,0:T(8,128)S(1)} %payload.21.refs_2_), channel_id=1, source_target_pairs={{1,3},{2,4},{5,7},{3,1},{4,2},{7,5},{9,11},{10,12},{13,15},{11,9},... | collective-permute-start | bytes 1572872 | tf_op jit(solution)/shard_map/ppermute | solution.py:463
  123.3 3.5 %collective-permute-start.36 = (f32[512,128]{1,0:T(8,128)S(1)}, f32[512,128]{1,0:T(8,128)S(1)}, u32[]{:S(2)}, u32[]{:S(2)}) collective-permute-start(f32[512,128]{1,0:T(8,128)S(1)} %get-tuple-element.85), channel_id=1, source_target_pairs={{0,1},{1,0},{2,3},{3,2},{4,5},{5,4},{6,7},{7,6},{8,9},{9,8},{10,11... | collective-permute-start | bytes 786440 | tf_op jit(solution)/shard_map/ppermute | solution.py:460
  125.7 1.5 %collective-permute-start.37 = (f32[512,128]{1,0:T(8,128)S(1)}, f32[512,128]{1,0:T(8,128)S(1)}, u32[]{:S(2)}, u32[]{:S(2)}) collective-permute-start(f32[512,128]{1,0:T(8,128)S(1)} %get-tuple-element.84), channel_id=1, source_target_pairs={{0,1},{1,0},{2,3},{3,2},{4,5},{5,4},{6,7},{7,6},{8,9},{9,8},{10,11... | collective-permute-start | bytes 786440 | tf_op jit(solution)/shard_map/ppermute | solution.py:460
  125.8 9.3 %collective-permute-start.31 = (f32[2,256]{1,0:T(2,128)S(1)}, f32[2,256]{1,0:T(2,128)S(1)}, u32[]{:S(2)}, u32[]{:S(2)}) collective-permute-start(f32[2,256]{1,0:T(2,128)S(1)} %get-tuple-element.74.refs_0_), channel_id=1, source_target_pairs={{0,2},{1,3},{2,0},{3,1},{4,6},{5,7},{6,4},{7,5},{8,10},{9,11},{10,... | collective-permute-start | bytes 6152 | tf_op jit(solution)/shard_map/ppermute | solution.py:649
  126.9 8.3 %collective-permute-start.32 = (f32[2,256]{1,0:T(2,128)S(1)}, f32[2,256]{1,0:T(2,128)S(1)}, u32[]{:S(2)}, u32[]{:S(2)}) collective-permute-start(f32[2,256]{1,0:T(2,128)S(1)} %get-tuple-element.74.refs_0_), channel_id=1, source_target_pairs={{0,4},{1,5},{2,6},{3,7},{4,0},{5,1},{6,2},{7,3},{8,12},{9,13},{10,... | collective-permute-start | bytes 6152 | tf_op jit(solution)/shard_map/ppermute | solution.py:649
  127.2 7.9 %collective-permute-start.33 = (f32[2,256]{1,0:T(2,128)S(1)}, f32[2,256]{1,0:T(2,128)S(1)}, u32[]{:S(2)}, u32[]{:S(2)}) collective-permute-start(f32[2,256]{1,0:T(2,128)S(1)} %get-tuple-element.74.refs_0_), channel_id=1, source_target_pairs={{0,6},{1,7},{2,4},{3,5},{4,2},{5,3},{6,0},{7,1},{8,14},{9,15},{10,... | collective-permute-start | bytes 6152 | tf_op jit(solution)/shard_map/ppermute | solution.py:649
  131.2 11.6 %collective-permute-start.40 = (f32[1024,128]{1,0:T(8,128)S(1)}, f32[1024,128]{1,0:T(8,128)S(1)}, u32[]{:S(2)}, u32[]{:S(2)}) collective-permute-start(f32[1024,128]{1,0:T(8,128)S(1)} %payload.22.refs_4_), channel_id=1, source_target_pairs={{1,3},{2,4},{5,7},{3,1},{4,2},{7,5},{9,11},{10,12},{13,15},{11,9},... | collective-permute-start | bytes 1572872 | tf_op jit(solution)/shard_map/ppermute | solution.py:463
  135.8 13.3 %collective-permute-start.39 = (f32[1024,128]{1,0:T(8,128)S(1)}, f32[1024,128]{1,0:T(8,128)S(1)}, u32[]{:S(2)}, u32[]{:S(2)}) collective-permute-start(f32[1024,128]{1,0:T(8,128)S(1)} %payload.23.refs_4_), channel_id=1, source_target_pairs={{0,2},{3,5},{4,6},{2,0},{5,3},{6,4},{8,10},{11,13},{12,14},{10,8},... | collective-permute-start | bytes 1572872 | tf_op jit(solution)/shard_map/ppermute | solution.py:463
  138.0 3.0 %collective-permute-start.41 = (f32[512,128]{1,0:T(8,128)S(1)}, f32[512,128]{1,0:T(8,128)S(1)}, u32[]{:S(2)}, u32[]{:S(2)}) collective-permute-start(f32[512,128]{1,0:T(8,128)S(1)} %get-tuple-element.83), channel_id=1, source_target_pairs={{0,1},{1,0},{2,3},{3,2},{4,5},{5,4},{6,7},{7,6},{8,9},{9,8},{10,11... | collective-permute-start | bytes 786440 | tf_op jit(solution)/shard_map/ppermute | solution.py:460
  139.8 1.5 %collective-permute-start.42 = (f32[512,128]{1,0:T(8,128)S(1)}, f32[512,128]{1,0:T(8,128)S(1)}, u32[]{:S(2)}, u32[]{:S(2)}) collective-permute-start(f32[512,128]{1,0:T(8,128)S(1)} %get-tuple-element.82), channel_id=1, source_target_pairs={{0,1},{1,0},{2,3},{3,2},{4,5},{5,4},{6,7},{7,6},{8,9},{9,8},{10,11... | collective-permute-start | bytes 786440 | tf_op jit(solution)/shard_map/ppermute | solution.py:460

commit v7 on v6

--- a/solution.py
+++ b/solution.py
@@ -153,33 +153,29 @@
         refs[2][...] = total[2 * cells : 2 * cells + 8] + total[2 * cells + 8 :]
 
 
-def own_rows(distribution, velocity, capacity, out, token, speeds, weight, rows, sems):
+def own_rows(distribution, velocity, capacity, out, token, speeds, weight, sems):
     modes, cells = velocity.shape[1], out.shape[1]
-    field = pltpu.make_async_copy(
-        distribution.at[:, pl.ds(0, cells)], out.at[pl.ds(0, modes), :], sems.at[0]
-    )
-    field.start()
     copies = [
-        pltpu.make_async_copy(velocity, speeds, sems.at[1]),
-        pltpu.make_async_copy(capacity, weight, sems.at[2]),
+        pltpu.make_async_copy(velocity, speeds, sems.at[0]),
+        pltpu.make_async_copy(capacity, weight, sems.at[1]),
+        pltpu.make_async_copy(
+            distribution.at[:, pl.ds(0, cells)], out.at[pl.ds(0, modes), :], sems.at[2]
+        ),
     ]
     for copy in copies:
         copy.start()
     token[...] = jnp.zeros_like(token)
-    rows[...] = jnp.zeros_like(rows)
-    for copy in copies:
+    for copy in copies[:2]:
         copy.wait()
     per = modes // LANES
+    out[modes:] = jnp.zeros((out.shape[0] - modes, LANES), jnp.float32)
     for d in range(2):
         for i in range(per):
             lanes = slice(i * LANES, (i + 1) * LANES)
-            rows[d * per + i : d * per + i + 1, :] = speeds[d : d + 1, lanes] * weight[:, lanes]
-    extra = pltpu.make_async_copy(
-        rows, out.at[pl.ds(modes, rows.shape[0]), :], sems.at[3]
-    )
-    extra.start()
-    field.wait()
-    extra.wait()
+            out[modes + d * per + i : modes + d * per + i + 1, :] = (
+                speeds[d : d + 1, lanes] * weight[:, lanes]
+            )
+    copies[2].wait()
 
 
 def payload(numbers, slots, arrived, *refs):
@@ -211,8 +207,12 @@
             out[...] = ref[...]
 
 
-def add(one, two, out):
-    out[...] = one[...] + two[...]
+def add(one, *refs):
+    out, first = refs[-1], 0
+    for piece in refs[:-1]:
+        rows = slice(first, first + piece.shape[0])
+        out[rows] = one[rows] + piece[...]
+        first += piece.shape[0]
 
 
 def add_all(*refs):
@@ -456,8 +456,10 @@
     )
     kinds = cell_type[None, :]
 
-    def exchange(value):
-        return lax.ppermute(value, "mode", across)
+    def exchange(value, parts=1):
+        cut = value.shape[0] // parts // 8 * 8
+        ends = [cut * k for k in range(parts)] + [value.shape[0]]
+        return [lax.ppermute(value[i:j], "mode", across) for i, j in zip(ends, ends[1:])]
 
     def along(stream, value):
         return lax.ppermute(value, "mode", plan.pairs[stream])
@@ -472,17 +474,17 @@
             self.arrived = [[along(0, own)], [along(1, own)]]
             self.blocks = []
 
-        def add_terms(self, field):
+        def add_terms(self, field, parts=1):
             kernel = functools.partial(slot_products, plan.rows[len(self.terms)])
             mine, other = call(kernel, [part] * 2, [self.matrix, field])
-            self.terms.append((mine, exchange(other)))
+            self.terms.append((mine, *exchange(other, parts)))
 
         def join_terms(self, *slots):
             for slot in slots:
                 (self.terms[slot],) = call(add, [part], self.terms[slot])
 
         def take_own(self):
-            self.blocks.append((self.own, exchange(self.own)))
+            self.blocks.append((self.own, *exchange(self.own)))
 
         def send(self, step, between=None):
             sent = {}
@@ -506,10 +508,7 @@
             arrays = [self.arrived[stream][step] for stream, step in plan.choices[slot]]
             kernel = functools.partial(pick, plan.picked[slot])
             (here,) = call(kernel, [arrays[0].shape], arrays)
-            cut = here.shape[0] // parts // 8 * 8
-            ends = [cut * k for k in range(parts)] + [here.shape[0]]
-            there = [exchange(here[i:j]) for i, j in zip(ends, ends[1:])]
-            self.blocks.append((here, *there))
+            self.blocks.append((here, *exchange(here, parts)))
 
         def multiply(self, slot, base=None):
             first, last = slot == 0, base is not None
@@ -527,11 +526,13 @@
             self.total = results[0]
             return results
 
-        def ends(self, base):
-            first = (chips - 1) % 2
+        def first_end(self, base):
             kernel = functools.partial(take_off, self.scale)
-            (rest,) = call(kernel, [part], [self.arrived[first][-1], self.terms[-1], base])
-            return [self.arrived[1 - first][-1], rest]
+            arrived = self.arrived[(chips - 1) % 2][-1]
+            (self.rest,) = call(kernel, [part], [arrived, self.terms[-1], base])
+
+        def ends(self):
+            return [self.arrived[chips % 2][-1], self.rest]
 
     own, _ = call(
         own_rows,
@@ -541,10 +542,8 @@
         scratch=[
             pltpu.VMEM((2, modes), jnp.float32),
             pltpu.VMEM((1, modes), jnp.float32),
-            pltpu.VMEM((extra, LANES), jnp.float32),
-            pltpu.SemaphoreType.DMA((4,)),
+            pltpu.SemaphoreType.DMA((3,)),
         ],
-        out_specs=[HBM, VMEM],
         room=56,
     )
     one = Round(None, time_step, True)
@@ -561,7 +560,7 @@
         room=28,
     )
     one.matrix = matrix
-    one.terms = [(terms[2 * s], exchange(terms[2 * s + 1])) for s in range(chips)]
+    one.terms = [(terms[2 * s], *exchange(terms[2 * s + 1])) for s in range(chips)]
     one.take_own()
     operators = jnp.asarray(differences(cells))
     aside = [pltpu.VMEM((modes, 4 * HALO), jnp.bfloat16)]
@@ -587,14 +586,15 @@
     mid_a, leading, scattered = one.multiply(chips - 1, base_a)
 
     two = Round(matrix, step_size, False)
-    two.add_terms(mid_a)
+    one.first_end(base_b)
+    two.add_terms(mid_a, 1)
     mid_b, last = call(
-        functools.partial(turn_sum, time_step), [part, (HALO, modes)], one.ends(base_b)
+        functools.partial(turn_sum, time_step), [part, (HALO, modes)], one.ends()
     )
     two.begin(mid_b)
-    two.join_terms(0)
     for slot in range(1, chips - 1):
         two.add_terms(mid_a)
+    two.join_terms(0)
     two.take_own()
     strips = call(strip_pairs, [(HALO, modes)] * 2, [leading, last])
     strips = paired(*strips)
@@ -630,10 +630,11 @@
     heat_flux = flux.value
     if isinstance(two.terms[-1], tuple):
         two.join_terms(chips - 1)
+    two.first_end(end_a)
     (updated,) = call(
         functools.partial(last_sum, step_size),
         [(modes, cells)],
-        [*two.ends(end_a), last_b],
+        [*two.ends(), last_b],
         scratch=[pltpu.VMEM(part, jnp.float32), pltpu.SemaphoreType.DMA((2,))],
         out_specs=[HBM],
     )

time: 151 us -> 135 us (0.89)
  Pallas kernels: 50.3 us -> 34.9 us
  waiting for transfers between devices: 31.8 us -> 23.6 us
  starting transfers between devices: 65.6 us -> 73.7 us
    pallas_call x51, Pallas kernels: 50.3 us -> 34.9 us  [__call__(): pl.pallas_call(body, out_shape=[jax.ShapeDtypeStruct(shape, jnp.float32)...]
    ppermute x16, waiting for transfers between devices: 24.2 us -> 18.2 us  [along(): return lax.ppermute(value, 'mode', plan.pairs[stream])]
    ppermute x19, starting transfers between devices: 12.3 us -> 18.2 us  [exchange(): lax.ppermute(value[i:j], 'mode', across)]
  transfers between devices with their start and end apart: 43 -> 43, of which waited for: 15 -> 10; matrix products, arithmetic and copies ran while one was open for 0% -> 0% of each run, Pallas kernels for 21% -> 24%
where the time goes in v7:
time: 135 us
  starting transfers between devices  73.7 us (55%)
  Pallas kernels  34.9 us (26%)
  waiting for transfers between devices  23.6 us (17%)
  between operations  1.58 us (1%)
    ppermute x16, starting transfers between devices, along(): return lax.ppermute(value, 'mode', plan.pairs[stream])  44.7 us
    pallas_call x51, Pallas kernels, __call__(): pl.pallas_call(body, out_shape=[jax.ShapeDtypeStruct(shape, jnp.float32)...  34.9 us
    ppermute x19, starting transfers between devices, exchange(): lax.ppermute(value[i:j], 'mode', across)  18.2 us
    ppermute x16, waiting for transfers between devices, along(): return lax.ppermute(value, 'mode', plan.pairs[stream])  18.2 us
    ppermute x4, starting transfers between devices, paired(): lax.ppermute(value, 'space', pairs + [(j, i) for i, j in pairs])  8.01 us
    ppermute x4, starting transfers between devices, over(): lax.ppermute(self.value, 'mode', [(i, i ^ bit) for i in range(self.device...  2.8 us
    ppermute x4, waiting for transfers between devices, paired(): lax.ppermute(value, 'space', pairs + [(j, i) for i, j in pairs])  2.8 us
  transfers between devices with their start and end apart: 43, of which 10 were waited for; matrix products, arithmetic and copies ran while one was open for 0% of the time, Pallas kernels for 24%

profile of v7, /device:TPU:13, one launch (start us, length us, event | category | flops | bytes accessed | tf_op | source)
XLA Modules:
  0.0 134.7 jit_solution(12367801405935086115)
XLA Ops:
  0.6 2.0 %own_rows.1 = (f32[1040,128]{1,0:T(8,128)}, f32[8,128]{1,0:T(8,128)}) custom-call(f32[1024,256]{1,0:T(8,128)} %refs_0_.9, f32[2,1024]{1,0:T(2,128)} %refs_1_.2, f32[1,1024]{1,0:T(1,128)} %bitcast.4), custom_call_target="tpu_custom_call" | custom-call | flops 1024 | bytes 1024 | tf_op jit(solution)/shard_map/own_rows/pallas_call | solution.py:39
  2.6 2.1 %collective-permute-start = (f32[1040,128]{1,0:T(8,128)}, f32[1040,128]{1,0:T(8,128)S(1)}, u32[]{:S(2)}, u32[]{:S(2)}) collective-permute-start(f32[1040,128]{1,0:T(8,128)} %get-tuple-element.41.refs_1_), channel_id=1, source_target_pairs={{1,3},{2,4},{5,7},{3,1},{4,2},{7,5},{9,11},{10,12},{13,15},{11,9},... | collective-permute-start | bytes 1597448 | tf_op jit(solution)/shard_map/ppermute | solution.py:465
  4.7 4.3 %collective-permute-start.2 = (f32[1040,128]{1,0:T(8,128)}, f32[1040,128]{1,0:T(8,128)S(1)}, u32[]{:S(2)}, u32[]{:S(2)}) collective-permute-start(f32[1040,128]{1,0:T(8,128)} %get-tuple-element.41.refs_1_), channel_id=1, source_target_pairs={{0,2},{3,5},{4,6},{2,0},{5,3},{6,4},{8,10},{11,13},{12,14},{10,8},... | collective-permute-start | bytes 1597448 | tf_op jit(solution)/shard_map/ppermute | solution.py:465
  9.1 0.7 copy-done.3
  9.7 7.4 %load_and_products.1 = (f32[1024,128]{1,0:T(8,128)S(1)}, f32[1024,128]{1,0:T(8,128)S(1)}, f32[1024,128]{1,0:T(8,128)S(1)}, f32[1024,128]{1,0:T(8,128)S(1)}, f32[...) custom-call(bf16[8192,1024]{1,0:T(8,128)(2,1)} %refs_0_.6, ...), custom_call_target="tpu_custom_call" | custom-call | flops 1024 | bytes 1024 | tf_op jit(solution)/shard_map/load_and_products/pallas_call | solution.py:39
  17.3 0.5 collective-permute-start.4
  17.8 1.9 %collective-permute-done.2.refs_0_ = f32[1040,128]{1,0:T(8,128)S(1)} collective-permute-done((f32[1040,128]{1,0:T(8,128)}, f32[1040,128]{1,0:T(8,128)S(1)}, u32[]{:S(2)}, u32[]{:S(2)}) %collective-permute-start.2) | collective-permute-done | bytes 532512 | tf_op jit(solution)/shard_map/ppermute | solution.py:465
  19.9 2.3 %collective-permute-start.5 = (f32[1040,128]{1,0:T(8,128)S(1)}, f32[1040,128]{1,0:T(8,128)S(1)}, u32[]{:S(2)}, u32[]{:S(2)}) collective-permute-start(f32[1040,128]{1,0:T(8,128)S(1)} %payload.12.refs_2_), channel_id=1, source_target_pairs={{1,3},{2,4},{5,7},{3,1},{4,2},{7,5},{9,11},{10,12},{13,15},{11,9},... | collective-permute-start | bytes 1597448 | tf_op jit(solution)/shard_map/ppermute | solution.py:465
  22.2 0.8 collective-permute-start.8
  23.1 2.5 %collective-permute-start.3 = (f32[1040,128]{1,0:T(8,128)S(1)}, f32[1040,128]{1,0:T(8,128)S(1)}, u32[]{:S(2)}, u32[]{:S(2)}) collective-permute-start(f32[1040,128]{1,0:T(8,128)S(1)} %payload.13.refs_2_), channel_id=1, source_target_pairs={{0,2},{3,5},{4,6},{2,0},{5,3},{6,4},{8,10},{11,13},{12,14},{10,8},... | collective-permute-start | bytes 1597448 | tf_op jit(solution)/shard_map/ppermute | solution.py:465
  25.9 0.6 collective-permute-start.13
  26.5 0.3 strip_rows.1
  26.9 1.4 %two_blocks.8.refs_3_ = f32[272,1024]{1,0:T(8,128)S(1)} custom-call(bf16[8192,1024]{1,0:T(8,128)(2,1)S(1)} %get-tuple-element.45.refs_2_.refs_0_, f32[1040,128]{1,0:T(8,128)S(1)} %copy-done.2, f32[1040,128]{1,0:T(8,128)S(1)} %collective-permute-done.6.refs_2_, f32[32,1024]{1,0:T(8,128)S(1)} %get-tuple-element.54.refs_3_), custom_call_target="tpu_custom_call" | custom-call | flops 1024 | bytes 1024 | tf_op jit(solution)/shard_map/two_blocks/pallas_call | solution.py:39
  28.2 3.5 %collective-permute-done.5.refs_0_.refs_2_ = f32[1040,128]{1,0:T(8,128)S(1)} collective-permute-done((f32[1040,128]{1,0:T(8,128)S(1)}, f32[1040,128]{1,0:T(8,128)S(1)}, u32[]{:S(2)}, u32[]{:S(2)}) %collective-permute-start.5) | collective-permute-done | bytes 532512 | tf_op jit(solution)/shard_map/ppermute | solution.py:465
  31.8 4.2 %collective-permute-start.10 = (f32[1040,128]{1,0:T(8,128)S(1)}, f32[1040,128]{1,0:T(8,128)S(1)}, u32[]{:S(2)}, u32[]{:S(2)}) collective-permute-start(f32[1040,128]{1,0:T(8,128)S(1)} %payload.14.refs_3_), channel_id=1, source_target_pairs={{0,2},{3,5},{4,6},{2,0},{5,3},{6,4},{8,10},{11,13},{12,14},{10,8},... | collective-permute-start | bytes 1597448 | tf_op jit(solution)/shard_map/ppermute | solution.py:465
  36.1 1.9 %collective-permute-start.9 = (f32[1040,128]{1,0:T(8,128)S(1)}, f32[1040,128]{1,0:T(8,128)S(1)}, u32[]{:S(2)}, u32[]{:S(2)}) collective-permute-start(f32[1040,128]{1,0:T(8,128)S(1)} %payload.15.refs_3_), channel_id=1, source_target_pairs={{1,3},{2,4},{5,7},{3,1},{4,2},{7,5},{9,11},{10,12},{13,15},{11,9},... | collective-permute-start | bytes 1597448 | tf_op jit(solution)/shard_map/ppermute | solution.py:465
  38.2 3.1 %collective-permute-start.12 = (f32[32,1024]{1,0:T(8,128)S(1)}, f32[32,1024]{1,0:T(8,128)S(1)}, u32[]{:S(2)}, u32[]{:S(2)}) collective-permute-start(f32[32,1024]{1,0:T(8,128)S(1)} %get-tuple-element.54.refs_3_), channel_id=1, source_target_pairs={{8,16},{16,8},{9,17},{17,9},{10,18},{18,10},{11,19},{19,11},{12,20... | collective-permute-start | bytes 393224 | tf_op jit(solution)/shard_map/ppermute | solution.py:376
  41.5 2.1 %collective-permute-start.18 = (f32[1040,128]{1,0:T(8,128)S(1)}, f32[1040,128]{1,0:T(8,128)S(1)}, u32[]{:S(2)}, u32[]{:S(2)}) collective-permute-start(f32[1040,128]{1,0:T(8,128)S(1)} %pick.7.refs_4_.refs_1_), channel_id=1, source_target_pairs={{0,1},{1,0},{2,3},{3,2},{4,5},{5,4},{6,7},{7,6},{8,9},{9,8},{10,11... | collective-permute-start | bytes 1597448 | tf_op jit(solution)/shard_map/ppermute | solution.py:462
  43.6 1.4 %two_blocks.9.refs_6_.refs_3_ = f32[272,1024]{1,0:T(8,128)S(1)} custom-call(bf16[8192,1024]{1,0:T(8,128)(2,1)S(1)} %get-tuple-element.45.refs_2_.refs_0_, f32[1040,128]{1,0:T(8,128)S(1)} %pick.6.refs_2_.refs_1_, f32[1040,128]{1,0:T(8,128)S(1)} %collective-permute-done.13.refs_2_, f32[272,1024]{1,0:T(8,128)S(1)} %two_blocks.8.refs_3_, ...), custom_call_target="tpu_custom_call" | custom-call | flops 1024 | bytes 1024 | tf_op jit(solution)/shard_map/two_blocks/pallas_call | solution.py:39
  45.0 0.4 collective-permute-done.11.refs_1_
  45.4 2.2 %first_rest.1 = (f32[1024,128]{1,0:T(8,128)S(1)}, f32[1024,128]{1,0:T(8,128)S(1)}) custom-call(f32[1024,256]{1,0:T(8,128)S(1)} %copy-done, f32[32,1024]{1,0:T(8,128)S(1)} %collective-permute-done.11.refs_1_, f32[32,1024]{1,0:T(8,128)S(1)} %collective-permute-done.12.refs_2_, bf16[640,1024]{1,0:T(8,128)(2,1)S(1)} %copy-done.1, ...), custom_call_target="tpu_custom_call" | custom-call | flops 1024 | bytes 1024 | tf_op jit(solution)/shard_map/first_rest/pallas_call | solution.py:39
  47.7 4.0 %collective-permute-start.15 = (f32[1040,128]{1,0:T(8,128)S(1)}, f32[1040,128]{1,0:T(8,128)S(1)}, u32[]{:S(2)}, u32[]{:S(2)}) collective-permute-start(f32[1040,128]{1,0:T(8,128)S(1)} %payload.16.refs_3_), channel_id=1, source_target_pairs={{1,3},{2,4},{5,7},{3,1},{4,2},{7,5},{9,11},{10,12},{13,15},{11,9},... | collective-permute-start | bytes 1597448 | tf_op jit(solution)/shard_map/ppermute | solution.py:465
  51.8 3.7 %collective-permute-start.14 = (f32[1040,128]{1,0:T(8,128)S(1)}, f32[1040,128]{1,0:T(8,128)S(1)}, u32[]{:S(2)}, u32[]{:S(2)}) collective-permute-start(f32[1040,128]{1,0:T(8,128)S(1)} %payload.17.refs_4_), channel_id=1, source_target_pairs={{0,2},{3,5},{4,6},{2,0},{5,3},{6,4},{8,10},{11,13},{12,14},{10,8},... | collective-permute-start | bytes 1597448 | tf_op jit(solution)/shard_map/ppermute | solution.py:465
  55.8 0.4 collective-permute-start.16
  56.4 1.4 %two_blocks.10.refs_4_.refs_6_ = f32[272,1024]{1,0:T(8,128)S(1)} custom-call(bf16[8192,1024]{1,0:T(8,128)(2,1)S(1)} %get-tuple-element.45.refs_2_.refs_0_, f32[1040,128]{1,0:T(8,128)S(1)} %pick.7.refs_4_.refs_1_, f32[1040,128]{1,0:T(8,128)S(1)} %collective-permute-done.18.refs_2_, f32[272,1024]{1,0:T(8,128)S(1)} %two_blocks.9.refs_6_.refs_3_, ...), custom_call_target="tpu_custom_call" | custom-call | flops 1024 | bytes 1024 | tf_op jit(solution)/shard_map/two_blocks/pallas_call | solution.py:39
  57.8 1.5 %two_blocks.11 = (f32[1024,128]{1,0:T(8,128)S(1)}, f32[32,1024]{1,0:T(8,128)S(1)}, f32[8,1024]{1,0:T(8,128)S(1)}) custom-call(bf16[8192,1024]{1,0:T(8,128)(2,1)S(1)} %get-tuple-element.45.refs_2_.refs_0_, f32[1040,128]{1,0:T(8,128)S(1)} %pick.8.refs_4_.refs_1_, f32[520,128]{1,0:T(8,128)S(1)} %collective-permute-done.16.refs_2_, ...), custom_call_target="tpu_custom_call" | custom-call | flops 1024 | bytes 1024 | tf_op jit(solution)/shard_map/two_blocks/pallas_call | solution.py:39
  59.4 1.3 slot_products.4
  60.7 7.3 %collective-permute-start.20 = (f32[1024,128]{1,0:T(8,128)S(1)}, f32[1024,128]{1,0:T(8,128)S(1)}, u32[]{:S(2)}, u32[]{:S(2)}) collective-permute-start(f32[1024,128]{1,0:T(8,128)S(1)} %get-tuple-element.60.refs_2_), channel_id=1, source_target_pairs={{0,1},{1,0},{2,3},{3,2},{4,5},{5,4},{6,7},{7,6},{8,9},{9,8},{10,11... | collective-permute-start | bytes 1572872 | tf_op jit(solution)/shard_map/ppermute | solution.py:462
  68.2 2.3 %collective-permute-start.21 = (f32[1024,128]{1,0:T(8,128)S(1)}, f32[1024,128]{1,0:T(8,128)S(1)}, u32[]{:S(2)}, u32[]{:S(2)}) collective-permute-start(f32[1024,128]{1,0:T(8,128)S(1)} %get-tuple-element.61.refs_1_.refs_2_), channel_id=1, source_target_pairs={{0,2},{3,5},{4,6},{2,0},{5,3},{6,4},{8,10},{11,13},{12,14},{10,8},... | collective-permute-start | bytes 1572872 | tf_op jit(solution)/shard_map/ppermute | solution.py:465
  70.5 1.9 %collective-permute-start.19 = (f32[1024,128]{1,0:T(8,128)S(1)}, f32[1024,128]{1,0:T(8,128)S(1)}, u32[]{:S(2)}, u32[]{:S(2)}) collective-permute-start(f32[1024,128]{1,0:T(8,128)S(1)} %get-tuple-element.61.refs_1_.refs_2_), channel_id=1, source_target_pairs={{1,3},{2,4},{5,7},{3,1},{4,2},{7,5},{9,11},{10,12},{13,15},{11,9},... | collective-permute-start | bytes 1572872 | tf_op jit(solution)/shard_map/ppermute | solution.py:465
  72.4 1.3 slot_products.5
  73.7 0.4 collective-permute-start.23
  74.1 1.3 slot_products.6
  75.6 0.3 collective-permute-start.26
  76.0 5.5 %collective-permute-done.21.refs_0_ = f32[1024,128]{1,0:T(8,128)S(1)} collective-permute-done((f32[1024,128]{1,0:T(8,128)S(1)}, f32[1024,128]{1,0:T(8,128)S(1)}, u32[]{:S(2)}, u32[]{:S(2)}) %collective-permute-start.21) | collective-permute-done | bytes 524320 | tf_op jit(solution)/shard_map/ppermute | solution.py:465
  81.6 1.9 %collective-permute-start.29 = (f32[1024,128]{1,0:T(8,128)S(1)}, f32[1024,128]{1,0:T(8,128)S(1)}, u32[]{:S(2)}, u32[]{:S(2)}) collective-permute-start(f32[1024,128]{1,0:T(8,128)S(1)} %payload.18.refs_2_), channel_id=1, source_target_pairs={{1,3},{2,4},{5,7},{3,1},{4,2},{7,5},{9,11},{10,12},{13,15},{11,9},... | collective-permute-start | bytes 1572872 | tf_op jit(solution)/shard_map/ppermute | solution.py:465
  83.5 0.7 collective-permute-done.19.refs_0_.refs_1_
  84.2 2.3 %collective-permute-start.22 = (f32[1024,128]{1,0:T(8,128)S(1)}, f32[1024,128]{1,0:T(8,128)S(1)}, u32[]{:S(2)}, u32[]{:S(2)}) collective-permute-start(f32[1024,128]{1,0:T(8,128)S(1)} %payload.19.refs_2_), channel_id=1, source_target_pairs={{0,2},{3,5},{4,6},{2,0},{5,3},{6,4},{8,10},{11,13},{12,14},{10,8},... | collective-permute-start | bytes 1572872 | tf_op jit(solution)/shard_map/ppermute | solution.py:465
  86.8 1.3 slot_products.7
  88.0 0.5 collective-permute-start.35
  88.5 1.8 %collective-permute-start.24 = (f32[32,1024]{1,0:T(8,128)S(1)}, f32[32,1024]{1,0:T(8,128)S(1)}, u32[]{:S(2)}, u32[]{:S(2)}) collective-permute-start(f32[32,1024]{1,0:T(8,128)S(1)} %get-tuple-element.69), channel_id=1, source_target_pairs={{0,8},{16,24},{8,0},{24,16},{1,9},{17,25},{9,1},{25,17},{2,10},{18... | collective-permute-start | bytes 393224 | tf_op jit(solution)/shard_map/ppermute | solution.py:376
  90.3 3.1 %collective-permute-start.25 = (f32[32,1024]{1,0:T(8,128)S(1)}, f32[32,1024]{1,0:T(8,128)S(1)}, u32[]{:S(2)}, u32[]{:S(2)}) collective-permute-start(f32[32,1024]{1,0:T(8,128)S(1)} %get-tuple-element.67.refs_2_), channel_id=1, source_target_pairs={{8,16},{16,8},{9,17},{17,9},{10,18},{18,10},{11,19},{19,11},{12,20... | collective-permute-start | bytes 393224 | tf_op jit(solution)/shard_map/ppermute | solution.py:376
  93.4 1.3 two_blocks.12.refs_9_.refs_3_
  94.8 0.7 collective-permute-start.38
  95.4 2.4 %collective-permute-done.25.refs_4_ = f32[32,1024]{1,0:T(8,128)S(1)} collective-permute-done((f32[32,1024]{1,0:T(8,128)S(1)}, f32[32,1024]{1,0:T(8,128)S(1)}, u32[]{:S(2)}, u32[]{:S(2)}) %collective-permute-start.25) | collective-permute-done | bytes 131104 | tf_op jit(solution)/shard_map/ppermute | solution.py:376
  97.8 2.8 %second_rest.1 = (f32[1024,128]{1,0:T(8,128)S(1)}, f32[1024,128]{1,0:T(8,128)S(1)}, f32[2,256]{1,0:T(2,128)S(1)}) custom-call(f32[1024,256]{1,0:T(8,128)S(1)} %copy-done, f32[1024,128]{1,0:T(8,128)S(1)} %get-tuple-element.59.refs_1_, f32[1024,128]{1,0:T(8,128)S(1)} %get-tuple-element.61.refs_1_.refs_2_, f32[32,1024]{1,0:T(8,128)S(1)} %collective-permute-done.24.refs_3_, ...), custom_call_target="tpu_custom_call" | custom-call | flops 1024 | bytes 1024 | tf_op jit(solution)/shard_map/second_rest/pallas_call | solution.py:39
  100.7 1.2 collective-permute-start.28
  102.0 2.8 %collective-permute-start.34 = (f32[1024,128]{1,0:T(8,128)S(1)}, f32[1024,128]{1,0:T(8,128)S(1)}, u32[]{:S(2)}, u32[]{:S(2)}) collective-permute-start(f32[1024,128]{1,0:T(8,128)S(1)} %payload.20.refs_2_), channel_id=1, source_target_pairs={{0,2},{3,5},{4,6},{2,0},{5,3},{6,4},{8,10},{11,13},{12,14},{10,8},... | collective-permute-start | bytes 1572872 | tf_op jit(solution)/shard_map/ppermute | solution.py:465
  104.9 1.9 %collective-permute-start.30 = (f32[1024,128]{1,0:T(8,128)S(1)}, f32[1024,128]{1,0:T(8,128)S(1)}, u32[]{:S(2)}, u32[]{:S(2)}) collective-permute-start(f32[1024,128]{1,0:T(8,128)S(1)} %payload.21.refs_2_), channel_id=1, source_target_pairs={{1,3},{2,4},{5,7},{3,1},{4,2},{7,5},{9,11},{10,12},{13,15},{11,9},... | collective-permute-start | bytes 1572872 | tf_op jit(solution)/shard_map/ppermute | solution.py:465
  107.2 2.4 %collective-permute-start.36 = (f32[512,128]{1,0:T(8,128)S(1)}, f32[512,128]{1,0:T(8,128)S(1)}, u32[]{:S(2)}, u32[]{:S(2)}) collective-permute-start(f32[512,128]{1,0:T(8,128)S(1)} %get-tuple-element.85), channel_id=1, source_target_pairs={{0,1},{1,0},{2,3},{3,2},{4,5},{5,4},{6,7},{7,6},{8,9},{9,8},{10,11... | collective-permute-start | bytes 786440 | tf_op jit(solution)/shard_map/ppermute | solution.py:462
  109.7 1.1 collective-permute-done.36.refs_2_
  110.8 0.7 collective-permute-start.32
  111.5 0.9 collective-permute-start.33
  112.4 1.3 two_blocks.13.refs_4_.refs_5_
  113.7 1.3 two_blocks.14.refs_3_.refs_4_
  115.1 3.9 %collective-permute-start.40 = (f32[1024,128]{1,0:T(8,128)S(1)}, f32[1024,128]{1,0:T(8,128)S(1)}, u32[]{:S(2)}, u32[]{:S(2)}) collective-permute-start(f32[1024,128]{1,0:T(8,128)S(1)} %payload.22.refs_4_), channel_id=1, source_target_pairs={{1,3},{2,4},{5,7},{3,1},{4,2},{7,5},{9,11},{10,12},{13,15},{11,9},... | collective-permute-start | bytes 1572872 | tf_op jit(solution)/shard_map/ppermute | solution.py:465
  119.1 0.6 add_all.3
  119.7 2.5 %collective-permute-start.39 = (f32[1024,128]{1,0:T(8,128)S(1)}, f32[1024,128]{1,0:T(8,128)S(1)}, u32[]{:S(2)}, u32[]{:S(2)}) collective-permute-start(f32[1024,128]{1,0:T(8,128)S(1)} %payload.23.refs_4_), channel_id=1, source_target_pairs={{0,2},{3,5},{4,6},{2,0},{5,3},{6,4},{8,10},{11,13},{12,14},{10,8},... | collective-permute-start | bytes 1572872 | tf_op jit(solution)/shard_map/ppermute | solution.py:465
  122.3 1.5 %collective-permute-start.41 = (f32[512,128]{1,0:T(8,128)S(1)}, f32[512,128]{1,0:T(8,128)S(1)}, u32[]{:S(2)}, u32[]{:S(2)}) collective-permute-start(f32[512,128]{1,0:T(8,128)S(1)} %get-tuple-element.83), channel_id=1, source_target_pairs={{0,1},{1,0},{2,3},{3,2},{4,5},{5,4},{6,7},{7,6},{8,9},{9,8},{10,11... | collective-permute-start | bytes 786440 | tf_op jit(solution)/shard_map/ppermute | solution.py:462
  123.9 1.1 collective-permute-done.41.refs_2_
  125.0 0.4 collective-permute-done.42.refs_3_
  125.3 1.4 %two_blocks.15.refs_3_.refs_2_ = f32[1024,128]{1,0:T(8,128)S(1)} custom-call(bf16[8192,1024]{1,0:T(8,128)(2,1)S(1)} %get-tuple-element.45.refs_2_.refs_0_, f32[1024,128]{1,0:T(8,128)S(1)} %pick.11.refs_1_.refs_6_, f32[512,128]{1,0:T(8,128)S(1)} %collective-permute-done.41.refs_2_, f32[512,128]{1,0:T(8,128)S(1)} %collective-permute-done.42.refs_3_, ...), custom_call_target="tpu_custom_call" | custom-call | flops 1024 | bytes 1024 | tf_op jit(solution)/shard_map/two_blocks/pallas_call | solution.py:39
  126.9 6.7 %collective-permute-done.39.refs_0_ = f32[1024,128]{1,0:T(8,128)S(1)} collective-permute-done((f32[1024,128]{1,0:T(8,128)S(1)}, f32[1024,128]{1,0:T(8,128)S(1)}, u32[]{:S(2)}, u32[]{:S(2)}) %collective-permute-start.39) | collective-permute-done | bytes 524320 | tf_op jit(solution)/shard_map/ppermute | solution.py:465
  133.6 1.0 last_sum.1
  (94 shorter events, 3.7 us)
Async XLA Ops:
  0.6 8.4 %copy-start = (f32[1024,256]{1,0:T(8,128)S(1)}, f32[1024,256]{1,0:T(8,128)}, u32[]{:S(2)}) copy-start(f32[1024,256]{1,0:T(8,128)} %refs_0_.9) | copy-start | bytes 3145732
  2.6 15.2 %collective-permute-start = (f32[1040,128]{1,0:T(8,128)}, f32[1040,128]{1,0:T(8,128)S(1)}, u32[]{:S(2)}, u32[]{:S(2)}) collective-permute-start(f32[1040,128]{1,0:T(8,128)} %get-tuple-element.41.refs_1_), channel_id=1, source_target_pairs={{1,3},{2,4},{5,7},{3,1},{4,2},{7,5},{9,11},{10,12},{13,15},{11,9},... | collective-permute-start | bytes 1597448 | tf_op jit(solution)/shard_map/ppermute | solution.py:465
  4.7 15.0 %collective-permute-start.2 = (f32[1040,128]{1,0:T(8,128)}, f32[1040,128]{1,0:T(8,128)S(1)}, u32[]{:S(2)}, u32[]{:S(2)}) collective-permute-start(f32[1040,128]{1,0:T(8,128)} %get-tuple-element.41.refs_1_), channel_id=1, source_target_pairs={{0,2},{3,5},{4,6},{2,0},{5,3},{6,4},{8,10},{11,13},{12,14},{10,8},... | collective-permute-start | bytes 1597448 | tf_op jit(solution)/shard_map/ppermute | solution.py:465
  9.1 0.7 copy-start.3
  9.7 8.0 %copy-start.2 = (f32[1040,128]{1,0:T(8,128)S(1)}, f32[1040,128]{1,0:T(8,128)}, u32[]{:S(2)}) copy-start(f32[1040,128]{1,0:T(8,128)} %get-tuple-element.41.refs_1_) | copy-start | bytes 1597444
  17.2 2.6 %collective-permute-start.1 = (f32[1024,128]{1,0:T(8,128)S(1)}, f32[1024,128]{1,0:T(8,128)S(1)}, u32[]{:S(2)}, u32[]{:S(2)}) collective-permute-start(f32[1024,128]{1,0:T(8,128)S(1)} %get-tuple-element.44), channel_id=1, source_target_pairs={{0,1},{1,0},{2,3},{3,2},{4,5},{5,4},{6,7},{7,6},{8,9},{9,8},{10,11... | collective-permute-start | bytes 1572872 | tf_op jit(solution)/shard_map/ppermute | solution.py:462
  17.3 5.9 %collective-permute-start.4 = (f32[1024,128]{1,0:T(8,128)S(1)}, f32[1024,128]{1,0:T(8,128)S(1)}, u32[]{:S(2)}, u32[]{:S(2)}) collective-permute-start(f32[1024,128]{1,0:T(8,128)S(1)} %get-tuple-element.47), channel_id=1, source_target_pairs={{0,1},{1,0},{2,3},{3,2},{4,5},{5,4},{6,7},{7,6},{8,9},{9,8},{10,11... | collective-permute-start | bytes 1572872 | tf_op jit(solution)/shard_map/ppermute | solution.py:462
  17.8 9.1 %collective-permute-start.6 = (f32[1040,128]{1,0:T(8,128)S(1)}, f32[1040,128]{1,0:T(8,128)S(1)}, u32[]{:S(2)}, u32[]{:S(2)}) collective-permute-start(f32[1040,128]{1,0:T(8,128)S(1)} %copy-done.2), channel_id=1, source_target_pairs={{0,1},{1,0},{2,3},{3,2},{4,5},{5,4},{6,7},{7,6},{8,9},{9,8},{10,11... | collective-permute-start | bytes 1597448 | tf_op jit(solution)/shard_map/ppermute | solution.py:462
  19.9 11.8 %collective-permute-start.5 = (f32[1040,128]{1,0:T(8,128)S(1)}, f32[1040,128]{1,0:T(8,128)S(1)}, u32[]{:S(2)}, u32[]{:S(2)}) collective-permute-start(f32[1040,128]{1,0:T(8,128)S(1)} %payload.12.refs_2_), channel_id=1, source_target_pairs={{1,3},{2,4},{5,7},{3,1},{4,2},{7,5},{9,11},{10,12},{13,15},{11,9},... | collective-permute-start | bytes 1597448 | tf_op jit(solution)/shard_map/ppermute | solution.py:465
  22.2 3.5 %collective-permute-start.8 = (f32[1024,128]{1,0:T(8,128)S(1)}, f32[1024,128]{1,0:T(8,128)S(1)}, u32[]{:S(2)}, u32[]{:S(2)}) collective-permute-start(f32[1024,128]{1,0:T(8,128)S(1)} %get-tuple-element.51), channel_id=1, source_target_pairs={{0,1},{1,0},{2,3},{3,2},{4,5},{5,4},{6,7},{7,6},{8,9},{9,8},{10,11... | collective-permute-start | bytes 1572872 | tf_op jit(solution)/shard_map/ppermute | solution.py:462
  23.0 2.8 %collective-permute-start.7 = (f32[1024,128]{1,0:T(8,128)S(1)}, f32[1024,128]{1,0:T(8,128)S(1)}, u32[]{:S(2)}, u32[]{:S(2)}) collective-permute-start(f32[1024,128]{1,0:T(8,128)S(1)} %get-tuple-element.49), channel_id=1, source_target_pairs={{0,1},{1,0},{2,3},{3,2},{4,5},{5,4},{6,7},{7,6},{8,9},{9,8},{10,11... | collective-permute-start | bytes 1572872 | tf_op jit(solution)/shard_map/ppermute | solution.py:462
  23.1 12.9 %collective-permute-start.3 = (f32[1040,128]{1,0:T(8,128)S(1)}, f32[1040,128]{1,0:T(8,128)S(1)}, u32[]{:S(2)}, u32[]{:S(2)}) collective-permute-start(f32[1040,128]{1,0:T(8,128)S(1)} %payload.13.refs_2_), channel_id=1, source_target_pairs={{0,2},{3,5},{4,6},{2,0},{5,3},{6,4},{8,10},{11,13},{12,14},{10,8},... | collective-permute-start | bytes 1597448 | tf_op jit(solution)/shard_map/ppermute | solution.py:465
  25.9 15.6 %collective-permute-start.13 = (f32[1040,128]{1,0:T(8,128)S(1)}, f32[1040,128]{1,0:T(8,128)S(1)}, u32[]{:S(2)}, u32[]{:S(2)}) collective-permute-start(f32[1040,128]{1,0:T(8,128)S(1)} %pick.6.refs_2_.refs_1_), channel_id=1, source_target_pairs={{0,1},{1,0},{2,3},{3,2},{4,5},{5,4},{6,7},{7,6},{8,9},{9,8},{10,11... | collective-permute-start | bytes 1597448 | tf_op jit(solution)/shard_map/ppermute | solution.py:462
  31.8 6.4 %copy-start.5 = (f32[2,1024]{1,0:T(2,128)S(1)}, f32[2,1024]{1,0:T(2,128)}, u32[]{:S(2)}) copy-start(f32[2,1024]{1,0:T(2,128)} %refs_1_.2) | copy-start | bytes 24580
  31.8 6.4 %copy-start.6 = (f32[1024]{0:T(1024)S(1)}, f32[1024]{0:T(1024)}, u32[]{:S(2)}) copy-start(f32[1024]{0:T(1024)} %param.9) | copy-start | bytes 12292
  31.8 15.8 %collective-permute-start.10 = (f32[1040,128]{1,0:T(8,128)S(1)}, f32[1040,128]{1,0:T(8,128)S(1)}, u32[]{:S(2)}, u32[]{:S(2)}) collective-permute-start(f32[1040,128]{1,0:T(8,128)S(1)} %payload.14.refs_3_), channel_id=1, source_target_pairs={{0,2},{3,5},{4,6},{2,0},{5,3},{6,4},{8,10},{11,13},{12,14},{10,8},... | collective-permute-start | bytes 1597448 | tf_op jit(solution)/shard_map/ppermute | solution.py:465
  36.1 15.6 %collective-permute-start.9 = (f32[1040,128]{1,0:T(8,128)S(1)}, f32[1040,128]{1,0:T(8,128)S(1)}, u32[]{:S(2)}, u32[]{:S(2)}) collective-permute-start(f32[1040,128]{1,0:T(8,128)S(1)} %payload.15.refs_3_), channel_id=1, source_target_pairs={{1,3},{2,4},{5,7},{3,1},{4,2},{7,5},{9,11},{10,12},{13,15},{11,9},... | collective-permute-start | bytes 1597448 | tf_op jit(solution)/shard_map/ppermute | solution.py:465
  38.2 7.3 %collective-permute-start.12 = (f32[32,1024]{1,0:T(8,128)S(1)}, f32[32,1024]{1,0:T(8,128)S(1)}, u32[]{:S(2)}, u32[]{:S(2)}) collective-permute-start(f32[32,1024]{1,0:T(8,128)S(1)} %get-tuple-element.54.refs_3_), channel_id=1, source_target_pairs={{8,16},{16,8},{9,17},{17,9},{10,18},{18,10},{11,19},{19,11},{12,20... | collective-permute-start | bytes 393224 | tf_op jit(solution)/shard_map/ppermute | solution.py:376
  41.2 4.2 %collective-permute-start.11 = (f32[32,1024]{1,0:T(8,128)S(1)}, f32[32,1024]{1,0:T(8,128)S(1)}, u32[]{:S(2)}, u32[]{:S(2)}) collective-permute-start(f32[32,1024]{1,0:T(8,128)S(1)} %get-tuple-element.55), channel_id=1, source_target_pairs={{0,8},{16,24},{8,0},{24,16},{1,9},{17,25},{9,1},{25,17},{2,10},{18... | collective-permute-start | bytes 393224 | tf_op jit(solution)/shard_map/ppermute | solution.py:376
  41.4 4.0 %copy-start.1 = (bf16[640,1024]{1,0:T(8,128)(2,1)S(1)}, bf16[640,1024]{1,0:T(8,128)(2,1)}, u32[]{:S(2)}) copy-start(bf16[640,1024]{1,0:T(8,128)(2,1)} %constant.4.clone.refs_3_.refs_5_) | copy-start | bytes 3932164
  41.4 4.0 %copy-start.4 = (s32[256]{0:T(256)S(1)}, s32[256]{0:T(256)}, u32[]{:S(2)}) copy-start(s32[256]{0:T(256)} %param.10) | copy-start | bytes 3076
  41.5 14.9 %collective-permute-start.18 = (f32[1040,128]{1,0:T(8,128)S(1)}, f32[1040,128]{1,0:T(8,128)S(1)}, u32[]{:S(2)}, u32[]{:S(2)}) collective-permute-start(f32[1040,128]{1,0:T(8,128)S(1)} %pick.7.refs_4_.refs_1_), channel_id=1, source_target_pairs={{0,1},{1,0},{2,3},{3,2},{4,5},{5,4},{6,7},{7,6},{8,9},{9,8},{10,11... | collective-permute-start | bytes 1597448 | tf_op jit(solution)/shard_map/ppermute | solution.py:462
  47.7 11.6 %collective-permute-start.15 = (f32[1040,128]{1,0:T(8,128)S(1)}, f32[1040,128]{1,0:T(8,128)S(1)}, u32[]{:S(2)}, u32[]{:S(2)}) collective-permute-start(f32[1040,128]{1,0:T(8,128)S(1)} %payload.16.refs_3_), channel_id=1, source_target_pairs={{1,3},{2,4},{5,7},{3,1},{4,2},{7,5},{9,11},{10,12},{13,15},{11,9},... | collective-permute-start | bytes 1597448 | tf_op jit(solution)/shard_map/ppermute | solution.py:465
  51.8 16.1 %collective-permute-start.14 = (f32[1040,128]{1,0:T(8,128)S(1)}, f32[1040,128]{1,0:T(8,128)S(1)}, u32[]{:S(2)}, u32[]{:S(2)}) collective-permute-start(f32[1040,128]{1,0:T(8,128)S(1)} %payload.17.refs_4_), channel_id=1, source_target_pairs={{0,2},{3,5},{4,6},{2,0},{5,3},{6,4},{8,10},{11,13},{12,14},{10,8},... | collective-permute-start | bytes 1597448 | tf_op jit(solution)/shard_map/ppermute | solution.py:465
  55.8 2.0 %collective-permute-start.16 = (f32[520,128]{1,0:T(8,128)S(1)}, f32[520,128]{1,0:T(8,128)S(1)}, u32[]{:S(2)}, u32[]{:S(2)}) collective-permute-start(f32[520,128]{1,0:T(8,128)S(1)} %get-tuple-element.81), channel_id=1, source_target_pairs={{0,1},{1,0},{2,3},{3,2},{4,5},{5,4},{6,7},{7,6},{8,9},{9,8},{10,11... | collective-permute-start | bytes 798728 | tf_op jit(solution)/shard_map/ppermute | solution.py:462
  56.2 1.5 %collective-permute-start.17 = (f32[520,128]{1,0:T(8,128)S(1)}, f32[520,128]{1,0:T(8,128)S(1)}, u32[]{:S(2)}, u32[]{:S(2)}) collective-permute-start(f32[520,128]{1,0:T(8,128)S(1)} %get-tuple-element.80), channel_id=1, source_target_pairs={{0,1},{1,0},{2,3},{3,2},{4,5},{5,4},{6,7},{7,6},{8,9},{9,8},{10,11... | collective-permute-start | bytes 798728 | tf_op jit(solution)/shard_map/ppermute | solution.py:462
  60.7 14.9 %collective-permute-start.20 = (f32[1024,128]{1,0:T(8,128)S(1)}, f32[1024,128]{1,0:T(8,128)S(1)}, u32[]{:S(2)}, u32[]{:S(2)}) collective-permute-start(f32[1024,128]{1,0:T(8,128)S(1)} %get-tuple-element.60.refs_2_), channel_id=1, source_target_pairs={{0,1},{1,0},{2,3},{3,2},{4,5},{5,4},{6,7},{7,6},{8,9},{9,8},{10,11... | collective-permute-start | bytes 1572872 | tf_op jit(solution)/shard_map/ppermute | solution.py:462
  68.2 13.4 %collective-permute-start.21 = (f32[1024,128]{1,0:T(8,128)S(1)}, f32[1024,128]{1,0:T(8,128)S(1)}, u32[]{:S(2)}, u32[]{:S(2)}) collective-permute-start(f32[1024,128]{1,0:T(8,128)S(1)} %get-tuple-element.61.refs_1_.refs_2_), channel_id=1, source_target_pairs={{0,2},{3,5},{4,6},{2,0},{5,3},{6,4},{8,10},{11,13},{12,14},{10,8},... | collective-permute-start | bytes 1572872 | tf_op jit(solution)/shard_map/ppermute | solution.py:465
  70.5 13.7 %collective-permute-start.19 = (f32[1024,128]{1,0:T(8,128)S(1)}, f32[1024,128]{1,0:T(8,128)S(1)}, u32[]{:S(2)}, u32[]{:S(2)}) collective-permute-start(f32[1024,128]{1,0:T(8,128)S(1)} %get-tuple-element.61.refs_1_.refs_2_), channel_id=1, source_target_pairs={{1,3},{2,4},{5,7},{3,1},{4,2},{7,5},{9,11},{10,12},{13,15},{11,9},... | collective-permute-start | bytes 1572872 | tf_op jit(solution)/shard_map/ppermute | solution.py:465
  73.7 12.9 %collective-permute-start.23 = (f32[1024,128]{1,0:T(8,128)S(1)}, f32[1024,128]{1,0:T(8,128)S(1)}, u32[]{:S(2)}, u32[]{:S(2)}) collective-permute-start(f32[1024,128]{1,0:T(8,128)S(1)} %get-tuple-element.64.refs_2_), channel_id=1, source_target_pairs={{0,1},{1,0},{2,3},{3,2},{4,5},{5,4},{6,7},{7,6},{8,9},{9,8},{10,11... | collective-permute-start | bytes 1572872 | tf_op jit(solution)/shard_map/ppermute | solution.py:462
  75.3 11.3 %collective-permute-start.27 = (f32[1024,128]{1,0:T(8,128)S(1)}, f32[1024,128]{1,0:T(8,128)S(1)}, u32[]{:S(2)}, u32[]{:S(2)}) collective-permute-start(f32[1024,128]{1,0:T(8,128)S(1)} %get-tuple-element.65.refs_2_), channel_id=1, source_target_pairs={{0,1},{1,0},{2,3},{3,2},{4,5},{5,4},{6,7},{7,6},{8,9},{9,8},{10,11... | collective-permute-start | bytes 1572872 | tf_op jit(solution)/shard_map/ppermute | solution.py:462
  75.6 14.7 %collective-permute-start.26 = (f32[1024,128]{1,0:T(8,128)S(1)}, f32[1024,128]{1,0:T(8,128)S(1)}, u32[]{:S(2)}, u32[]{:S(2)}) collective-permute-start(f32[1024,128]{1,0:T(8,128)S(1)} %get-tuple-element.61.refs_1_.refs_2_), channel_id=1, source_target_pairs={{0,1},{1,0},{2,3},{3,2},{4,5},{5,4},{6,7},{7,6},{8,9},{9,8},{10,11... | collective-permute-start | bytes 1572872 | tf_op jit(solution)/shard_map/ppermute | solution.py:462
  81.6 20.3 %collective-permute-start.29 = (f32[1024,128]{1,0:T(8,128)S(1)}, f32[1024,128]{1,0:T(8,128)S(1)}, u32[]{:S(2)}, u32[]{:S(2)}) collective-permute-start(f32[1024,128]{1,0:T(8,128)S(1)} %payload.18.refs_2_), channel_id=1, source_target_pairs={{1,3},{2,4},{5,7},{3,1},{4,2},{7,5},{9,11},{10,12},{13,15},{11,9},... | collective-permute-start | bytes 1572872 | tf_op jit(solution)/shard_map/ppermute | solution.py:465
  84.2 20.6 %collective-permute-start.22 = (f32[1024,128]{1,0:T(8,128)S(1)}, f32[1024,128]{1,0:T(8,128)S(1)}, u32[]{:S(2)}, u32[]{:S(2)}) collective-permute-start(f32[1024,128]{1,0:T(8,128)S(1)} %payload.19.refs_2_), channel_id=1, source_target_pairs={{0,2},{3,5},{4,6},{2,0},{5,3},{6,4},{8,10},{11,13},{12,14},{10,8},... | collective-permute-start | bytes 1572872 | tf_op jit(solution)/shard_map/ppermute | solution.py:465
  88.0 18.8 %collective-permute-start.35 = (f32[1024,128]{1,0:T(8,128)S(1)}, f32[1024,128]{1,0:T(8,128)S(1)}, u32[]{:S(2)}, u32[]{:S(2)}) collective-permute-start(f32[1024,128]{1,0:T(8,128)S(1)} %get-tuple-element.71.refs_3_), channel_id=1, source_target_pairs={{0,1},{1,0},{2,3},{3,2},{4,5},{5,4},{6,7},{7,6},{8,9},{9,8},{10,11... | collective-permute-start | bytes 1572872 | tf_op jit(solution)/shard_map/ppermute | solution.py:462
  88.5 6.2 %collective-permute-start.24 = (f32[32,1024]{1,0:T(8,128)S(1)}, f32[32,1024]{1,0:T(8,128)S(1)}, u32[]{:S(2)}, u32[]{:S(2)}) collective-permute-start(f32[32,1024]{1,0:T(8,128)S(1)} %get-tuple-element.69), channel_id=1, source_target_pairs={{0,8},{16,24},{8,0},{24,16},{1,9},{17,25},{9,1},{25,17},{2,10},{18... | collective-permute-start | bytes 393224 | tf_op jit(solution)/shard_map/ppermute | solution.py:376
  90.3 7.5 %collective-permute-start.25 = (f32[32,1024]{1,0:T(8,128)S(1)}, f32[32,1024]{1,0:T(8,128)S(1)}, u32[]{:S(2)}, u32[]{:S(2)}) collective-permute-start(f32[32,1024]{1,0:T(8,128)S(1)} %get-tuple-element.67.refs_2_), channel_id=1, source_target_pairs={{8,16},{16,8},{9,17},{17,9},{10,18},{18,10},{11,19},{19,11},{12,20... | collective-permute-start | bytes 393224 | tf_op jit(solution)/shard_map/ppermute | solution.py:376
  94.8 14.9 %collective-permute-start.38 = (f32[1024,128]{1,0:T(8,128)S(1)}, f32[1024,128]{1,0:T(8,128)S(1)}, u32[]{:S(2)}, u32[]{:S(2)}) collective-permute-start(f32[1024,128]{1,0:T(8,128)S(1)} %pick.9.refs_2_.refs_1_), channel_id=1, source_target_pairs={{0,1},{1,0},{2,3},{3,2},{4,5},{5,4},{6,7},{7,6},{8,9},{9,8},{10,11... | collective-permute-start | bytes 1572872 | tf_op jit(solution)/shard_map/ppermute | solution.py:462
  100.7 4.1 %collective-permute-start.28 = (f32[2,256]{1,0:T(2,128)S(1)}, f32[2,256]{1,0:T(2,128)S(1)}, u32[]{:S(2)}, u32[]{:S(2)}) collective-permute-start(f32[2,256]{1,0:T(2,128)S(1)} %get-tuple-element.72.refs_3_.refs_0_), channel_id=1, source_target_pairs={{0,1},{1,0},{2,3},{3,2},{4,5},{5,4},{6,7},{7,6},{8,9},{9,8},{10,11... | collective-permute-start | bytes 6152 | tf_op jit(solution)/shard_map/ppermute | solution.py:650
  102.0 13.1 %collective-permute-start.34 = (f32[1024,128]{1,0:T(8,128)S(1)}, f32[1024,128]{1,0:T(8,128)S(1)}, u32[]{:S(2)}, u32[]{:S(2)}) collective-permute-start(f32[1024,128]{1,0:T(8,128)S(1)} %payload.20.refs_2_), channel_id=1, source_target_pairs={{0,2},{3,5},{4,6},{2,0},{5,3},{6,4},{8,10},{11,13},{12,14},{10,8},... | collective-permute-start | bytes 1572872 | tf_op jit(solution)/shard_map/ppermute | solution.py:465
  104.9 14.8 %collective-permute-start.30 = (f32[1024,128]{1,0:T(8,128)S(1)}, f32[1024,128]{1,0:T(8,128)S(1)}, u32[]{:S(2)}, u32[]{:S(2)}) collective-permute-start(f32[1024,128]{1,0:T(8,128)S(1)} %payload.21.refs_2_), channel_id=1, source_target_pairs={{1,3},{2,4},{5,7},{3,1},{4,2},{7,5},{9,11},{10,12},{13,15},{11,9},... | collective-permute-start | bytes 1572872 | tf_op jit(solution)/shard_map/ppermute | solution.py:465
  107.2 3.6 %collective-permute-start.36 = (f32[512,128]{1,0:T(8,128)S(1)}, f32[512,128]{1,0:T(8,128)S(1)}, u32[]{:S(2)}, u32[]{:S(2)}) collective-permute-start(f32[512,128]{1,0:T(8,128)S(1)} %get-tuple-element.85), channel_id=1, source_target_pairs={{0,1},{1,0},{2,3},{3,2},{4,5},{5,4},{6,7},{7,6},{8,9},{9,8},{10,11... | collective-permute-start | bytes 786440 | tf_op jit(solution)/shard_map/ppermute | solution.py:462
  109.6 1.9 %collective-permute-start.37 = (f32[512,128]{1,0:T(8,128)S(1)}, f32[512,128]{1,0:T(8,128)S(1)}, u32[]{:S(2)}, u32[]{:S(2)}) collective-permute-start(f32[512,128]{1,0:T(8,128)S(1)} %get-tuple-element.84), channel_id=1, source_target_pairs={{0,1},{1,0},{2,3},{3,2},{4,5},{5,4},{6,7},{7,6},{8,9},{9,8},{10,11... | collective-permute-start | bytes 786440 | tf_op jit(solution)/shard_map/ppermute | solution.py:462
  109.7 9.3 %collective-permute-start.31 = (f32[2,256]{1,0:T(2,128)S(1)}, f32[2,256]{1,0:T(2,128)S(1)}, u32[]{:S(2)}, u32[]{:S(2)}) collective-permute-start(f32[2,256]{1,0:T(2,128)S(1)} %get-tuple-element.74.refs_0_), channel_id=1, source_target_pairs={{0,2},{1,3},{2,0},{3,1},{4,6},{5,7},{6,4},{7,5},{8,10},{9,11},{10,... | collective-permute-start | bytes 6152 | tf_op jit(solution)/shard_map/ppermute | solution.py:650
  110.8 8.3 %collective-permute-start.32 = (f32[2,256]{1,0:T(2,128)S(1)}, f32[2,256]{1,0:T(2,128)S(1)}, u32[]{:S(2)}, u32[]{:S(2)}) collective-permute-start(f32[2,256]{1,0:T(2,128)S(1)} %get-tuple-element.74.refs_0_), channel_id=1, source_target_pairs={{0,4},{1,5},{2,6},{3,7},{4,0},{5,1},{6,2},{7,3},{8,12},{9,13},{10,... | collective-permute-start | bytes 6152 | tf_op jit(solution)/shard_map/ppermute | solution.py:650
  111.5 7.6 %collective-permute-start.33 = (f32[2,256]{1,0:T(2,128)S(1)}, f32[2,256]{1,0:T(2,128)S(1)}, u32[]{:S(2)}, u32[]{:S(2)}) collective-permute-start(f32[2,256]{1,0:T(2,128)S(1)} %get-tuple-element.74.refs_0_), channel_id=1, source_target_pairs={{0,6},{1,7},{2,4},{3,5},{4,2},{5,3},{6,0},{7,1},{8,14},{9,15},{10,... | collective-permute-start | bytes 6152 | tf_op jit(solution)/shard_map/ppermute | solution.py:650
  115.1 11.7 %collective-permute-start.40 = (f32[1024,128]{1,0:T(8,128)S(1)}, f32[1024,128]{1,0:T(8,128)S(1)}, u32[]{:S(2)}, u32[]{:S(2)}) collective-permute-start(f32[1024,128]{1,0:T(8,128)S(1)} %payload.22.refs_4_), channel_id=1, source_target_pairs={{1,3},{2,4},{5,7},{3,1},{4,2},{7,5},{9,11},{10,12},{13,15},{11,9},... | collective-permute-start | bytes 1572872 | tf_op jit(solution)/shard_map/ppermute | solution.py:465
  119.7 13.9 %collective-permute-start.39 = (f32[1024,128]{1,0:T(8,128)S(1)}, f32[1024,128]{1,0:T(8,128)S(1)}, u32[]{:S(2)}, u32[]{:S(2)}) collective-permute-start(f32[1024,128]{1,0:T(8,128)S(1)} %payload.23.refs_4_), channel_id=1, source_target_pairs={{0,2},{3,5},{4,6},{2,0},{5,3},{6,4},{8,10},{11,13},{12,14},{10,8},... | collective-permute-start | bytes 1572872 | tf_op jit(solution)/shard_map/ppermute | solution.py:465
  122.3 2.6 %collective-permute-start.41 = (f32[512,128]{1,0:T(8,128)S(1)}, f32[512,128]{1,0:T(8,128)S(1)}, u32[]{:S(2)}, u32[]{:S(2)}) collective-permute-start(f32[512,128]{1,0:T(8,128)S(1)} %get-tuple-element.83), channel_id=1, source_target_pairs={{0,1},{1,0},{2,3},{3,2},{4,5},{5,4},{6,7},{7,6},{8,9},{9,8},{10,11... | collective-permute-start | bytes 786440 | tf_op jit(solution)/shard_map/ppermute | solution.py:462
  123.8 1.5 %collective-permute-start.42 = (f32[512,128]{1,0:T(8,128)S(1)}, f32[512,128]{1,0:T(8,128)S(1)}, u32[]{:S(2)}, u32[]{:S(2)}) collective-permute-start(f32[512,128]{1,0:T(8,128)S(1)} %get-tuple-element.82), channel_id=1, source_target_pairs={{0,1},{1,0},{2,3},{3,2},{4,5},{5,4},{6,7},{7,6},{8,9},{9,8},{10,11... | collective-permute-start | bytes 786440 | tf_op jit(solution)/shard_map/ppermute | solution.py:462

commit v8 on v7

--- a/solution.py
+++ b/solution.py
@@ -289,12 +289,13 @@
     return np.concatenate([own, own, strip, strip]).astype(jnp.bfloat16)
 
 
-def strip_columns(came_even, came_odd):
+def strip_columns(came_even, came_odd, out):
     even = lax.axis_index("space") % 2 == 0
     before = jnp.where(even, came_odd[...], came_even[...])
     after = jnp.where(even, came_even[...], came_odd[...])
     parts = halves(jnp.concatenate([before, after], axis=0))
-    return jnp.concatenate([p.astype(jnp.float32) for p in parts], axis=0).T.astype(jnp.bfloat16)
+    rows = jnp.concatenate([p.astype(jnp.float32) for p in parts], axis=0)
+    out[...] = rows.T.astype(jnp.bfloat16)
 
 
 def still_rate(field, strip, operators, columns, kinds):
@@ -312,10 +313,9 @@
     return rate
 
 
-def first_rest(field, came_even, came_odd, operators, table, kinds, base_a, base_b, strips):
+def first_rest(field, strips, operators, table, kinds, base_a, base_b):
     modes, half = base_a.shape
     block = min(modes, BLOCK)
-    strips[...] = strip_columns(came_even, came_odd)
 
     def step(i, _):
         rows = pl.ds(pl.multiple_of(i * block, block), block)
@@ -334,8 +334,7 @@
     field,
     mid_a,
     mid_b,
-    came_even,
-    came_odd,
+    strips,
     operators,
     table,
     kinds,
@@ -343,12 +342,10 @@
     end_a,
     end_b,
     flux,
-    strips,
 ):
     modes, half = end_a.shape
     block = min(modes, BLOCK)
     step_size = 0.5 * time_step
-    strips[...] = strip_columns(came_even, came_odd)
     flux[...] = jnp.zeros_like(flux)
 
     def step(i, _):
@@ -563,12 +560,17 @@
     one.terms = [(terms[2 * s], *exchange(terms[2 * s + 1])) for s in range(chips)]
     one.take_own()
     operators = jnp.asarray(differences(cells))
-    aside = [pltpu.VMEM((modes, 4 * HALO), jnp.bfloat16)]
     strips = None
+
+    def unpack():
+        nonlocal strips
+        shape = jax.ShapeDtypeStruct((modes, 4 * HALO), jnp.bfloat16)
+        (strips,) = call(strip_columns, [shape], strips)
+
     for step in range(1, chips):
         if step == 1:
             one.take(1)
-        one.send(step)
+        one.send(step, unpack if step == 2 else None)
         if step == 1:
             one.join_terms(*(s for s in range(chips) if isinstance(one.terms[s], tuple)))
             strips = call(strip_rows, [(HALO, modes)] * 2, [distribution])
@@ -580,40 +582,38 @@
             base_a, base_b = call(
                 first_rest,
                 [part] * 2,
-                [distribution, *strips, operators, table, kinds],
-                scratch=aside,
+                [distribution, strips, operators, table, kinds],
             )
     mid_a, leading, scattered = one.multiply(chips - 1, base_a)
 
     two = Round(matrix, step_size, False)
+    two.add_terms(mid_a, 1)
     one.first_end(base_b)
-    two.add_terms(mid_a, 1)
     mid_b, last = call(
         functools.partial(turn_sum, time_step), [part, (HALO, modes)], one.ends()
     )
     two.begin(mid_b)
-    for slot in range(1, chips - 1):
-        two.add_terms(mid_a)
+    two.add_terms(mid_a)
+    two.add_terms(mid_a)
     two.join_terms(0)
-    two.take_own()
-    strips = call(strip_pairs, [(HALO, modes)] * 2, [leading, last])
-    strips = paired(*strips)
+    strips = paired(*call(strip_pairs, [(HALO, modes)] * 2, [leading, last]))
     flux = None
     for step in range(1, chips):
         if step == 1:
-            two.send(step)
-            two.join_terms(*(s for s in range(1, chips - 1) if isinstance(two.terms[s], tuple)))
+            two.send(step, unpack)
+            two.take_own()
+            two.join_terms(1, 2)
         elif step == 2:
             two.send(step, lambda: flux.over(1))
+            two.join_terms(*range(3, chips))
         elif step == chips - 1:
             two.send(step, lambda: flux.over(*range(2, devices, 2)))
         else:
             two.send(step)
-        if step == 2 and isinstance(two.terms[-1], tuple):
-            two.join_terms(chips - 1)
         two.take(step, 2 if step >= chips - 2 else 1)
         if step == 1:
-            two.add_terms(mid_a)
+            for slot in range(3, chips):
+                two.add_terms(mid_a)
         if step < chips - 1:
             two.multiply(step - 1)
         if step == chips - 2:
@@ -622,14 +622,11 @@
             end_a, end_b, part_flux = call(
                 functools.partial(second_rest, 1.0 / math.sqrt(total_modes)),
                 [part, part, (2, cells)],
-                [distribution, mid_a, mid_b, *strips, operators, table, kinds, scattered],
-                scratch=aside,
+                [distribution, mid_a, mid_b, strips, operators, table, kinds, scattered],
             )
             flux = Flux(call, part_flux, devices)
     (last_b,) = two.multiply(chips - 1, end_b)
     heat_flux = flux.value
-    if isinstance(two.terms[-1], tuple):
-        two.join_terms(chips - 1)
     two.first_end(end_a)
     (updated,) = call(
         functools.partial(last_sum, step_size),

time: 135 us -> 140 us (1.037)
  waiting for transfers between devices: 23.6 us -> 30.2 us
  starting transfers between devices: 73.7 us -> 71.8 us
    ppermute x16, waiting for transfers between devices: 18.2 us -> 20.9 us  [along(): return lax.ppermute(value, 'mode', plan.pairs[stream])]
    ppermute x4, waiting for transfers between devices: 2.8 us -> 5.21 us  [paired(): lax.ppermute(value, 'space', pairs + [(j, i) for i, j in pairs])]
    ppermute x19, starting transfers between devices: 18.2 us -> 16.5 us  [exchange(): lax.ppermute(value[i:j], 'mode', across)]
    ppermute x4, waiting for transfers between devices: 0.01 us -> 1.43 us  [over(): lax.ppermute(self.value, 'mode', [(i, i ^ bit) for i in range(self.device...]
    pallas_call x51 -> x53, Pallas kernels: 34.9 us -> 34.8 us  [__call__(): pl.pallas_call(body, out_shape=[jax.ShapeDtypeStruct(shape, jnp.float32)...]
  transfers between devices with their start and end apart: 43 -> 43, of which waited for: 10 -> 13; matrix products, arithmetic and copies ran while one was open for 0% -> 0% of each run, Pallas kernels for 24% -> 23%
where the time goes in v8:
time: 140 us; the launch traced here: 139 us
  starting transfers between devices  71.8 us (51%)
  Pallas kernels  34.8 us (25%)
  waiting for transfers between devices  30.2 us (22%)
  between operations  1.57 us (1%)
    ppermute x16, starting transfers between devices, along(): return lax.ppermute(value, 'mode', plan.pairs[stream])  45.6 us
    pallas_call x53, Pallas kernels, __call__(): pl.pallas_call(body, out_shape=[jax.ShapeDtypeStruct(shape, jnp.float32)...  34.8 us
    ppermute x16, waiting for transfers between devices, along(): return lax.ppermute(value, 'mode', plan.pairs[stream])  20.9 us
    ppermute x19, starting transfers between devices, exchange(): lax.ppermute(value[i:j], 'mode', across)  16.5 us
    ppermute x4, starting transfers between devices, paired(): lax.ppermute(value, 'space', pairs + [(j, i) for i, j in pairs])  7.68 us
    ppermute x4, waiting for transfers between devices, paired(): lax.ppermute(value, 'space', pairs + [(j, i) for i, j in pairs])  5.21 us
  transfers between devices with their start and end apart: 43, of which 13 were waited for; matrix products, arithmetic and copies ran while one was open for 0% of the time, Pallas kernels for 23%

profile of v8, /device:TPU:13, one launch (start us, length us, event | category | flops | bytes accessed | tf_op | source)
XLA Modules:
  0.0 139.4 jit_solution(562587572804280187)
XLA Ops:
  0.6 2.0 %own_rows.1 = (f32[1040,128]{1,0:T(8,128)}, f32[8,128]{1,0:T(8,128)}) custom-call(f32[1024,256]{1,0:T(8,128)} %refs_0_.9, f32[2,1024]{1,0:T(2,128)} %refs_1_.2, f32[1,1024]{1,0:T(1,128)} %bitcast.4), custom_call_target="tpu_custom_call" | custom-call | flops 1024 | bytes 1024 | tf_op jit(solution)/shard_map/own_rows/pallas_call | solution.py:39
  2.6 2.1 %collective-permute-start = (f32[1040,128]{1,0:T(8,128)}, f32[1040,128]{1,0:T(8,128)S(1)}, u32[]{:S(2)}, u32[]{:S(2)}) collective-permute-start(f32[1040,128]{1,0:T(8,128)} %get-tuple-element.41.refs_1_), channel_id=1, source_target_pairs={{1,3},{2,4},{5,7},{3,1},{4,2},{7,5},{9,11},{10,12},{13,15},{11,9},... | collective-permute-start | bytes 1597448 | tf_op jit(solution)/shard_map/ppermute | solution.py:462
  4.7 4.3 %collective-permute-start.2 = (f32[1040,128]{1,0:T(8,128)}, f32[1040,128]{1,0:T(8,128)S(1)}, u32[]{:S(2)}, u32[]{:S(2)}) collective-permute-start(f32[1040,128]{1,0:T(8,128)} %get-tuple-element.41.refs_1_), channel_id=1, source_target_pairs={{0,2},{3,5},{4,6},{2,0},{5,3},{6,4},{8,10},{11,13},{12,14},{10,8},... | collective-permute-start | bytes 1597448 | tf_op jit(solution)/shard_map/ppermute | solution.py:462
  9.1 0.7 copy-done.3
  9.7 7.4 %load_and_products.1 = (f32[1024,128]{1,0:T(8,128)S(1)}, f32[1024,128]{1,0:T(8,128)S(1)}, f32[1024,128]{1,0:T(8,128)S(1)}, f32[1024,128]{1,0:T(8,128)S(1)}, f32[...) custom-call(bf16[8192,1024]{1,0:T(8,128)(2,1)} %refs_0_.6, ...), custom_call_target="tpu_custom_call" | custom-call | flops 1024 | bytes 1024 | tf_op jit(solution)/shard_map/load_and_products/pallas_call | solution.py:39
  17.3 0.5 collective-permute-start.4
  17.8 0.6 collective-permute-start.5
  18.4 1.3 collective-permute-done.2.refs_0_
  19.9 2.3 %collective-permute-start.9 = (f32[1040,128]{1,0:T(8,128)S(1)}, f32[1040,128]{1,0:T(8,128)S(1)}, u32[]{:S(2)}, u32[]{:S(2)}) collective-permute-start(f32[1040,128]{1,0:T(8,128)S(1)} %payload.12.refs_2_), channel_id=1, source_target_pairs={{1,3},{2,4},{5,7},{3,1},{4,2},{7,5},{9,11},{10,12},{13,15},{11,9},... | collective-permute-start | bytes 1597448 | tf_op jit(solution)/shard_map/ppermute | solution.py:462
  22.3 3.6 %collective-permute-start.3 = (f32[1040,128]{1,0:T(8,128)S(1)}, f32[1040,128]{1,0:T(8,128)S(1)}, u32[]{:S(2)}, u32[]{:S(2)}) collective-permute-start(f32[1040,128]{1,0:T(8,128)S(1)} %payload.13.refs_2_), channel_id=1, source_target_pairs={{0,2},{3,5},{4,6},{2,0},{5,3},{6,4},{8,10},{11,13},{12,14},{10,8},... | collective-permute-start | bytes 1597448 | tf_op jit(solution)/shard_map/ppermute | solution.py:462
  26.5 1.3 collective-permute-start.7
  27.8 2.1 %collective-permute-start.8 = (f32[32,1024]{1,0:T(8,128)S(1)}, f32[32,1024]{1,0:T(8,128)S(1)}, u32[]{:S(2)}, u32[]{:S(2)}) collective-permute-start(f32[32,1024]{1,0:T(8,128)S(1)} %get-tuple-element.55.refs_3_), channel_id=1, source_target_pairs={{8,16},{16,8},{9,17},{17,9},{10,18},{18,10},{11,19},{19,11},{12,20... | collective-permute-start | bytes 393224 | tf_op jit(solution)/shard_map/ppermute | solution.py:373
  29.9 0.6 collective-permute-start.13
  30.5 1.4 two_blocks.8.refs_3_
  32.0 3.7 %collective-permute-start.12 = (f32[1040,128]{1,0:T(8,128)S(1)}, f32[1040,128]{1,0:T(8,128)S(1)}, u32[]{:S(2)}, u32[]{:S(2)}) collective-permute-start(f32[1040,128]{1,0:T(8,128)S(1)} %payload.14.refs_2_), channel_id=1, source_target_pairs={{0,2},{3,5},{4,6},{2,0},{5,3},{6,4},{8,10},{11,13},{12,14},{10,8},... | collective-permute-start | bytes 1597448 | tf_op jit(solution)/shard_map/ppermute | solution.py:462
  35.9 0.6 collective-permute-done.3.refs_0_
  36.6 1.9 %collective-permute-start.11 = (f32[1040,128]{1,0:T(8,128)S(1)}, f32[1040,128]{1,0:T(8,128)S(1)}, u32[]{:S(2)}, u32[]{:S(2)}) collective-permute-start(f32[1040,128]{1,0:T(8,128)S(1)} %payload.15.refs_3_), channel_id=1, source_target_pairs={{1,3},{2,4},{5,7},{3,1},{4,2},{7,5},{9,11},{10,12},{13,15},{11,9},... | collective-permute-start | bytes 1597448 | tf_op jit(solution)/shard_map/ppermute | solution.py:462
  38.7 2.6 %collective-permute-start.18 = (f32[1040,128]{1,0:T(8,128)S(1)}, f32[1040,128]{1,0:T(8,128)S(1)}, u32[]{:S(2)}, u32[]{:S(2)}) collective-permute-start(f32[1040,128]{1,0:T(8,128)S(1)} %pick.7.refs_4_.refs_1_), channel_id=1, source_target_pairs={{0,1},{1,0},{2,3},{3,2},{4,5},{5,4},{6,7},{7,6},{8,9},{9,8},{10,11... | collective-permute-start | bytes 1597448 | tf_op jit(solution)/shard_map/ppermute | solution.py:459
  41.4 1.4 two_blocks.9.refs_5_.refs_3_
  42.8 2.0 %first_rest.1 = (f32[1024,128]{1,0:T(8,128)S(1)}, f32[1024,128]{1,0:T(8,128)S(1)}) custom-call(f32[1024,256]{1,0:T(8,128)S(1)} %copy-done, bf16[1024,128]{1,0:T(8,128)(2,1)S(1)} %strip_columns.2.refs_3_.refs_1_, bf16[640,1024]{1,0:T(8,128)(2,1)S(1)} %copy-done.1, f32[8,1024]{1,0:T(8,128)S(1)} %maximum_maximum_fusion.refs_3_.refs_5_, s32[1,256]{1,0:T(1,128)S(1)} %bitcast.2, ...), custom_call_target="tpu_custom_call" | custom-call | flops 1024 | bytes 1024 | tf_op jit(solution)/shard_map/first_rest/pallas_call | solution.py:39
  44.9 1.9 %collective-permute-start.15 = (f32[1040,128]{1,0:T(8,128)S(1)}, f32[1040,128]{1,0:T(8,128)S(1)}, u32[]{:S(2)}, u32[]{:S(2)}) collective-permute-start(f32[1040,128]{1,0:T(8,128)S(1)} %payload.16.refs_3_), channel_id=1, source_target_pairs={{1,3},{2,4},{5,7},{3,1},{4,2},{7,5},{9,11},{10,12},{13,15},{11,9},... | collective-permute-start | bytes 1597448 | tf_op jit(solution)/shard_map/ppermute | solution.py:462
  46.9 4.8 %collective-permute-done.11.refs_0_.refs_3_ = f32[1040,128]{1,0:T(8,128)S(1)} collective-permute-done((f32[1040,128]{1,0:T(8,128)S(1)}, f32[1040,128]{1,0:T(8,128)S(1)}, u32[]{:S(2)}, u32[]{:S(2)}) %collective-permute-start.11) | collective-permute-done | bytes 532512 | tf_op jit(solution)/shard_map/ppermute | solution.py:462
  51.8 3.0 %collective-permute-start.14 = (f32[1040,128]{1,0:T(8,128)S(1)}, f32[1040,128]{1,0:T(8,128)S(1)}, u32[]{:S(2)}, u32[]{:S(2)}) collective-permute-start(f32[1040,128]{1,0:T(8,128)S(1)} %payload.17.refs_4_), channel_id=1, source_target_pairs={{0,2},{3,5},{4,6},{2,0},{5,3},{6,4},{8,10},{11,13},{12,14},{10,8},... | collective-permute-start | bytes 1597448 | tf_op jit(solution)/shard_map/ppermute | solution.py:462
  55.1 2.3 %collective-permute-start.16 = (f32[520,128]{1,0:T(8,128)S(1)}, f32[520,128]{1,0:T(8,128)S(1)}, u32[]{:S(2)}, u32[]{:S(2)}) collective-permute-start(f32[520,128]{1,0:T(8,128)S(1)} %get-tuple-element.81), channel_id=1, source_target_pairs={{0,1},{1,0},{2,3},{3,2},{4,5},{5,4},{6,7},{7,6},{8,9},{9,8},{10,11... | collective-permute-start | bytes 798728 | tf_op jit(solution)/shard_map/ppermute | solution.py:459
  57.5 1.4 two_blocks.10.refs_4_.refs_6_
  59.0 1.5 %two_blocks.11 = (f32[1024,128]{1,0:T(8,128)S(1)}, f32[32,1024]{1,0:T(8,128)S(1)}, f32[8,1024]{1,0:T(8,128)S(1)}) custom-call(bf16[8192,1024]{1,0:T(8,128)(2,1)S(1)} %get-tuple-element.45.refs_2_.refs_0_, f32[1040,128]{1,0:T(8,128)S(1)} %pick.8.refs_4_.refs_1_, f32[520,128]{1,0:T(8,128)S(1)} %collective-permute-done.16.refs_2_, ...), custom_call_target="tpu_custom_call" | custom-call | flops 1024 | bytes 1024 | tf_op jit(solution)/shard_map/two_blocks/pallas_call | solution.py:39
  60.5 1.3 slot_products.4
  61.7 0.5 collective-permute-start.20
  62.3 5.0 %collective-permute-done.14.refs_0_ = f32[1040,128]{1,0:T(8,128)S(1)} collective-permute-done((f32[1040,128]{1,0:T(8,128)S(1)}, f32[1040,128]{1,0:T(8,128)S(1)}, u32[]{:S(2)}, u32[]{:S(2)}) %collective-permute-start.14) | collective-permute-done | bytes 532512 | tf_op jit(solution)/shard_map/ppermute | solution.py:462
  67.5 3.2 %collective-permute-start.23 = (f32[1024,128]{1,0:T(8,128)S(1)}, f32[1024,128]{1,0:T(8,128)S(1)}, u32[]{:S(2)}, u32[]{:S(2)}) collective-permute-start(f32[1024,128]{1,0:T(8,128)S(1)} %get-tuple-element.61.refs_1_.refs_2_), channel_id=1, source_target_pairs={{0,2},{3,5},{4,6},{2,0},{5,3},{6,4},{8,10},{11,13},{12,14},{10,8},... | collective-permute-start | bytes 1572872 | tf_op jit(solution)/shard_map/ppermute | solution.py:462
  70.8 1.9 %collective-permute-start.19 = (f32[1024,128]{1,0:T(8,128)S(1)}, f32[1024,128]{1,0:T(8,128)S(1)}, u32[]{:S(2)}, u32[]{:S(2)}) collective-permute-start(f32[1024,128]{1,0:T(8,128)S(1)} %get-tuple-element.61.refs_1_.refs_2_), channel_id=1, source_target_pairs={{1,3},{2,4},{5,7},{3,1},{4,2},{7,5},{9,11},{10,12},{13,15},{11,9},... | collective-permute-start | bytes 1572872 | tf_op jit(solution)/shard_map/ppermute | solution.py:462
  72.7 1.3 slot_products.5
  73.9 1.1 collective-permute-start.25
  75.1 1.2 slot_products.6
  76.5 1.3 collective-permute-start.21
  77.8 3.4 %collective-permute-done.21.refs_0_ = f32[32,1024]{1,0:T(8,128)S(1)} collective-permute-done((f32[32,1024]{1,0:T(8,128)S(1)}, f32[32,1024]{1,0:T(8,128)S(1)}, u32[]{:S(2)}, u32[]{:S(2)}) %collective-permute-start.21) | collective-permute-done | bytes 131104 | tf_op jit(solution)/shard_map/ppermute | solution.py:373
  81.2 3.0 %collective-permute-start.22 = (f32[32,1024]{1,0:T(8,128)S(1)}, f32[32,1024]{1,0:T(8,128)S(1)}, u32[]{:S(2)}, u32[]{:S(2)}) collective-permute-start(f32[32,1024]{1,0:T(8,128)S(1)} %get-tuple-element.68.refs_2_), channel_id=1, source_target_pairs={{8,16},{16,8},{9,17},{17,9},{10,18},{18,10},{11,19},{19,11},{12,20... | collective-permute-start | bytes 393224 | tf_op jit(solution)/shard_map/ppermute | solution.py:373
  84.2 1.7 %collective-permute-start.26 = (f32[1024,128]{1,0:T(8,128)S(1)}, f32[1024,128]{1,0:T(8,128)S(1)}, u32[]{:S(2)}, u32[]{:S(2)}) collective-permute-start(f32[1024,128]{1,0:T(8,128)S(1)} %get-tuple-element.61.refs_1_.refs_2_), channel_id=1, source_target_pairs={{0,1},{1,0},{2,3},{3,2},{4,5},{5,4},{6,7},{7,6},{8,9},{9,8},{10,11... | collective-permute-start | bytes 1572872 | tf_op jit(solution)/shard_map/ppermute | solution.py:459
  86.0 1.8 %collective-permute-done.22.refs_1_ = f32[32,1024]{1,0:T(8,128)S(1)} collective-permute-done((f32[32,1024]{1,0:T(8,128)S(1)}, f32[32,1024]{1,0:T(8,128)S(1)}, u32[]{:S(2)}, u32[]{:S(2)}) %collective-permute-start.22) | collective-permute-done | bytes 131104 | tf_op jit(solution)/shard_map/ppermute | solution.py:373
  87.8 3.7 %collective-permute-start.29 = (f32[1024,128]{1,0:T(8,128)S(1)}, f32[1024,128]{1,0:T(8,128)S(1)}, u32[]{:S(2)}, u32[]{:S(2)}) collective-permute-start(f32[1024,128]{1,0:T(8,128)S(1)} %payload.18.refs_2_), channel_id=1, source_target_pairs={{1,3},{2,4},{5,7},{3,1},{4,2},{7,5},{9,11},{10,12},{13,15},{11,9},... | collective-permute-start | bytes 1572872 | tf_op jit(solution)/shard_map/ppermute | solution.py:462
  91.8 2.1 %collective-permute-start.24 = (f32[1024,128]{1,0:T(8,128)S(1)}, f32[1024,128]{1,0:T(8,128)S(1)}, u32[]{:S(2)}, u32[]{:S(2)}) collective-permute-start(f32[1024,128]{1,0:T(8,128)S(1)} %payload.19.refs_2_), channel_id=1, source_target_pairs={{0,2},{3,5},{4,6},{2,0},{5,3},{6,4},{8,10},{11,13},{12,14},{10,8},... | collective-permute-start | bytes 1572872 | tf_op jit(solution)/shard_map/ppermute | solution.py:462
  94.0 1.3 slot_products.7
  95.3 1.2 collective-permute-start.35
  96.6 1.3 two_blocks.12.refs_8_.refs_3_
  97.9 2.7 %second_rest.1 = (f32[1024,128]{1,0:T(8,128)S(1)}, f32[1024,128]{1,0:T(8,128)S(1)}, f32[2,256]{1,0:T(2,128)S(1)}) custom-call(f32[1024,256]{1,0:T(8,128)S(1)} %copy-done, f32[1024,128]{1,0:T(8,128)S(1)} %get-tuple-element.58.refs_1_, f32[1024,128]{1,0:T(8,128)S(1)} %get-tuple-element.61.refs_1_.refs_2_, bf16[1024,128]{1,0:T(8,128)(2,1)S(1)} %strip_columns.3.refs_2_.refs_3_, ...), custom_call_target="tpu_custom_call" | custom-call | flops 1024 | bytes 1024 | tf_op jit(solution)/shard_map/second_rest/pallas_call | solution.py:39
  100.6 0.5 collective-permute-start.28
  101.2 3.0 %collective-permute-start.34 = (f32[1024,128]{1,0:T(8,128)S(1)}, f32[1024,128]{1,0:T(8,128)S(1)}, u32[]{:S(2)}, u32[]{:S(2)}) collective-permute-start(f32[1024,128]{1,0:T(8,128)S(1)} %payload.20.refs_2_), channel_id=1, source_target_pairs={{0,2},{3,5},{4,6},{2,0},{5,3},{6,4},{8,10},{11,13},{12,14},{10,8},... | collective-permute-start | bytes 1572872 | tf_op jit(solution)/shard_map/ppermute | solution.py:462
  104.3 2.0 %collective-permute-done.24.refs_0_ = f32[1024,128]{1,0:T(8,128)S(1)} collective-permute-done((f32[1024,128]{1,0:T(8,128)S(1)}, f32[1024,128]{1,0:T(8,128)S(1)}, u32[]{:S(2)}, u32[]{:S(2)}) %collective-permute-start.24) | collective-permute-done | bytes 524320 | tf_op jit(solution)/shard_map/ppermute | solution.py:462
  106.3 1.9 %collective-permute-start.30 = (f32[1024,128]{1,0:T(8,128)S(1)}, f32[1024,128]{1,0:T(8,128)S(1)}, u32[]{:S(2)}, u32[]{:S(2)}) collective-permute-start(f32[1024,128]{1,0:T(8,128)S(1)} %payload.21.refs_2_), channel_id=1, source_target_pairs={{1,3},{2,4},{5,7},{3,1},{4,2},{7,5},{9,11},{10,12},{13,15},{11,9},... | collective-permute-start | bytes 1572872 | tf_op jit(solution)/shard_map/ppermute | solution.py:462
  108.6 2.6 %collective-permute-start.36 = (f32[512,128]{1,0:T(8,128)S(1)}, f32[512,128]{1,0:T(8,128)S(1)}, u32[]{:S(2)}, u32[]{:S(2)}) collective-permute-start(f32[512,128]{1,0:T(8,128)S(1)} %get-tuple-element.85), channel_id=1, source_target_pairs={{0,1},{1,0},{2,3},{3,2},{4,5},{5,4},{6,7},{7,6},{8,9},{9,8},{10,11... | collective-permute-start | bytes 786440 | tf_op jit(solution)/shard_map/ppermute | solution.py:459
  111.3 1.1 collective-permute-done.36.refs_2_
  112.4 1.0 collective-permute-start.32
  113.4 0.6 collective-permute-start.33
  114.0 1.3 two_blocks.13.refs_4_.refs_5_
  115.3 1.3 two_blocks.14.refs_3_.refs_4_
  116.8 3.9 %collective-permute-start.40 = (f32[1024,128]{1,0:T(8,128)S(1)}, f32[1024,128]{1,0:T(8,128)S(1)}, u32[]{:S(2)}, u32[]{:S(2)}) collective-permute-start(f32[1024,128]{1,0:T(8,128)S(1)} %payload.22.refs_4_), channel_id=1, source_target_pairs={{1,3},{2,4},{5,7},{3,1},{4,2},{7,5},{9,11},{10,12},{13,15},{11,9},... | collective-permute-start | bytes 1572872 | tf_op jit(solution)/shard_map/ppermute | solution.py:462
  120.6 1.4 %collective-permute-done.31.refs_1_ = f32[2,256]{1,0:T(2,128)S(1)} collective-permute-done((f32[2,256]{1,0:T(2,128)S(1)}, f32[2,256]{1,0:T(2,128)S(1)}, u32[]{:S(2)}, u32[]{:S(2)}) %collective-permute-start.31) | collective-permute-done | bytes 2080 | tf_op jit(solution)/shard_map/ppermute | solution.py:647
  122.1 0.6 add_all.3
  122.7 2.8 %collective-permute-start.39 = (f32[1024,128]{1,0:T(8,128)S(1)}, f32[1024,128]{1,0:T(8,128)S(1)}, u32[]{:S(2)}, u32[]{:S(2)}) collective-permute-start(f32[1024,128]{1,0:T(8,128)S(1)} %payload.23.refs_4_), channel_id=1, source_target_pairs={{0,2},{3,5},{4,6},{2,0},{5,3},{6,4},{8,10},{11,13},{12,14},{10,8},... | collective-permute-start | bytes 1572872 | tf_op jit(solution)/shard_map/ppermute | solution.py:462
  125.7 2.3 %collective-permute-start.41 = (f32[512,128]{1,0:T(8,128)S(1)}, f32[512,128]{1,0:T(8,128)S(1)}, u32[]{:S(2)}, u32[]{:S(2)}) collective-permute-start(f32[512,128]{1,0:T(8,128)S(1)} %get-tuple-element.83), channel_id=1, source_target_pairs={{0,1},{1,0},{2,3},{3,2},{4,5},{5,4},{6,7},{7,6},{8,9},{9,8},{10,11... | collective-permute-start | bytes 786440 | tf_op jit(solution)/shard_map/ppermute | solution.py:459
  128.1 1.1 collective-permute-done.41.refs_2_
  129.5 1.4 %two_blocks.15.refs_3_.refs_2_ = f32[1024,128]{1,0:T(8,128)S(1)} custom-call(bf16[8192,1024]{1,0:T(8,128)(2,1)S(1)} %get-tuple-element.45.refs_2_.refs_0_, f32[1024,128]{1,0:T(8,128)S(1)} %pick.11.refs_1_.refs_6_, f32[512,128]{1,0:T(8,128)S(1)} %collective-permute-done.41.refs_2_, f32[512,128]{1,0:T(8,128)S(1)} %collective-permute-done.42.refs_3_, ...), custom_call_target="tpu_custom_call" | custom-call | flops 1024 | bytes 1024 | tf_op jit(solution)/shard_map/two_blocks/pallas_call | solution.py:39
  131.1 7.1 %collective-permute-done.39.refs_0_ = f32[1024,128]{1,0:T(8,128)S(1)} collective-permute-done((f32[1024,128]{1,0:T(8,128)S(1)}, f32[1024,128]{1,0:T(8,128)S(1)}, u32[]{:S(2)}, u32[]{:S(2)}) %collective-permute-start.39) | collective-permute-done | bytes 524320 | tf_op jit(solution)/shard_map/ppermute | solution.py:462
  138.2 1.0 last_sum.1
  (96 shorter events, 4.4 us)
Async XLA Ops:
  0.6 8.4 %copy-start = (f32[1024,256]{1,0:T(8,128)S(1)}, f32[1024,256]{1,0:T(8,128)}, u32[]{:S(2)}) copy-start(f32[1024,256]{1,0:T(8,128)} %refs_0_.9) | copy-start | bytes 3145732
  2.6 15.2 %collective-permute-start = (f32[1040,128]{1,0:T(8,128)}, f32[1040,128]{1,0:T(8,128)S(1)}, u32[]{:S(2)}, u32[]{:S(2)}) collective-permute-start(f32[1040,128]{1,0:T(8,128)} %get-tuple-element.41.refs_1_), channel_id=1, source_target_pairs={{1,3},{2,4},{5,7},{3,1},{4,2},{7,5},{9,11},{10,12},{13,15},{11,9},... | collective-permute-start | bytes 1597448 | tf_op jit(solution)/shard_map/ppermute | solution.py:462
  4.7 15.0 %collective-permute-start.2 = (f32[1040,128]{1,0:T(8,128)}, f32[1040,128]{1,0:T(8,128)S(1)}, u32[]{:S(2)}, u32[]{:S(2)}) collective-permute-start(f32[1040,128]{1,0:T(8,128)} %get-tuple-element.41.refs_1_), channel_id=1, source_target_pairs={{0,2},{3,5},{4,6},{2,0},{5,3},{6,4},{8,10},{11,13},{12,14},{10,8},... | collective-permute-start | bytes 1597448 | tf_op jit(solution)/shard_map/ppermute | solution.py:462
  9.1 0.7 copy-start.3
  9.7 10.0 %copy-start.2 = (f32[1040,128]{1,0:T(8,128)S(1)}, f32[1040,128]{1,0:T(8,128)}, u32[]{:S(2)}) copy-start(f32[1040,128]{1,0:T(8,128)} %get-tuple-element.41.refs_1_) | copy-start | bytes 1597444
  17.2 2.6 %collective-permute-start.1 = (f32[1024,128]{1,0:T(8,128)S(1)}, f32[1024,128]{1,0:T(8,128)S(1)}, u32[]{:S(2)}, u32[]{:S(2)}) collective-permute-start(f32[1024,128]{1,0:T(8,128)S(1)} %get-tuple-element.44), channel_id=1, source_target_pairs={{0,1},{1,0},{2,3},{3,2},{4,5},{5,4},{6,7},{7,6},{8,9},{9,8},{10,11... | collective-permute-start | bytes 1572872 | tf_op jit(solution)/shard_map/ppermute | solution.py:459
  17.3 5.0 %collective-permute-start.4 = (f32[1024,128]{1,0:T(8,128)S(1)}, f32[1024,128]{1,0:T(8,128)S(1)}, u32[]{:S(2)}, u32[]{:S(2)}) collective-permute-start(f32[1024,128]{1,0:T(8,128)S(1)} %get-tuple-element.47), channel_id=1, source_target_pairs={{0,1},{1,0},{2,3},{3,2},{4,5},{5,4},{6,7},{7,6},{8,9},{9,8},{10,11... | collective-permute-start | bytes 1572872 | tf_op jit(solution)/shard_map/ppermute | solution.py:459
  17.7 8.3 %collective-permute-start.6 = (f32[1024,128]{1,0:T(8,128)S(1)}, f32[1024,128]{1,0:T(8,128)S(1)}, u32[]{:S(2)}, u32[]{:S(2)}) collective-permute-start(f32[1024,128]{1,0:T(8,128)S(1)} %get-tuple-element.51), channel_id=1, source_target_pairs={{0,1},{1,0},{2,3},{3,2},{4,5},{5,4},{6,7},{7,6},{8,9},{9,8},{10,11... | collective-permute-start | bytes 1572872 | tf_op jit(solution)/shard_map/ppermute | solution.py:459
  17.8 8.3 %collective-permute-start.5 = (f32[1024,128]{1,0:T(8,128)S(1)}, f32[1024,128]{1,0:T(8,128)S(1)}, u32[]{:S(2)}, u32[]{:S(2)}) collective-permute-start(f32[1024,128]{1,0:T(8,128)S(1)} %get-tuple-element.49), channel_id=1, source_target_pairs={{0,1},{1,0},{2,3},{3,2},{4,5},{5,4},{6,7},{7,6},{8,9},{9,8},{10,11... | collective-permute-start | bytes 1572872 | tf_op jit(solution)/shard_map/ppermute | solution.py:459
  19.7 10.2 %collective-permute-start.10 = (f32[1040,128]{1,0:T(8,128)S(1)}, f32[1040,128]{1,0:T(8,128)S(1)}, u32[]{:S(2)}, u32[]{:S(2)}) collective-permute-start(f32[1040,128]{1,0:T(8,128)S(1)} %copy-done.2), channel_id=1, source_target_pairs={{0,1},{1,0},{2,3},{3,2},{4,5},{5,4},{6,7},{7,6},{8,9},{9,8},{10,11... | collective-permute-start | bytes 1597448 | tf_op jit(solution)/shard_map/ppermute | solution.py:459
  19.9 12.0 %collective-permute-start.9 = (f32[1040,128]{1,0:T(8,128)S(1)}, f32[1040,128]{1,0:T(8,128)S(1)}, u32[]{:S(2)}, u32[]{:S(2)}) collective-permute-start(f32[1040,128]{1,0:T(8,128)S(1)} %payload.12.refs_2_), channel_id=1, source_target_pairs={{1,3},{2,4},{5,7},{3,1},{4,2},{7,5},{9,11},{10,12},{13,15},{11,9},... | collective-permute-start | bytes 1597448 | tf_op jit(solution)/shard_map/ppermute | solution.py:462
  22.3 14.3 %collective-permute-start.3 = (f32[1040,128]{1,0:T(8,128)S(1)}, f32[1040,128]{1,0:T(8,128)S(1)}, u32[]{:S(2)}, u32[]{:S(2)}) collective-permute-start(f32[1040,128]{1,0:T(8,128)S(1)} %payload.13.refs_2_), channel_id=1, source_target_pairs={{0,2},{3,5},{4,6},{2,0},{5,3},{6,4},{8,10},{11,13},{12,14},{10,8},... | collective-permute-start | bytes 1597448 | tf_op jit(solution)/shard_map/ppermute | solution.py:462
  26.5 9.2 %collective-permute-start.7 = (f32[32,1024]{1,0:T(8,128)S(1)}, f32[32,1024]{1,0:T(8,128)S(1)}, u32[]{:S(2)}, u32[]{:S(2)}) collective-permute-start(f32[32,1024]{1,0:T(8,128)S(1)} %get-tuple-element.54), channel_id=1, source_target_pairs={{0,8},{16,24},{8,0},{24,16},{1,9},{17,25},{9,1},{25,17},{2,10},{18... | collective-permute-start | bytes 393224 | tf_op jit(solution)/shard_map/ppermute | solution.py:373
  27.8 7.9 %collective-permute-start.8 = (f32[32,1024]{1,0:T(8,128)S(1)}, f32[32,1024]{1,0:T(8,128)S(1)}, u32[]{:S(2)}, u32[]{:S(2)}) collective-permute-start(f32[32,1024]{1,0:T(8,128)S(1)} %get-tuple-element.55.refs_3_), channel_id=1, source_target_pairs={{8,16},{16,8},{9,17},{17,9},{10,18},{18,10},{11,19},{19,11},{12,20... | collective-permute-start | bytes 393224 | tf_op jit(solution)/shard_map/ppermute | solution.py:373
  29.9 11.5 %collective-permute-start.13 = (f32[1040,128]{1,0:T(8,128)S(1)}, f32[1040,128]{1,0:T(8,128)S(1)}, u32[]{:S(2)}, u32[]{:S(2)}) collective-permute-start(f32[1040,128]{1,0:T(8,128)S(1)} %pick.6.refs_2_.refs_1_), channel_id=1, source_target_pairs={{0,1},{1,0},{2,3},{3,2},{4,5},{5,4},{6,7},{7,6},{8,9},{9,8},{10,11... | collective-permute-start | bytes 1597448 | tf_op jit(solution)/shard_map/ppermute | solution.py:459
  32.0 12.8 %collective-permute-start.12 = (f32[1040,128]{1,0:T(8,128)S(1)}, f32[1040,128]{1,0:T(8,128)S(1)}, u32[]{:S(2)}, u32[]{:S(2)}) collective-permute-start(f32[1040,128]{1,0:T(8,128)S(1)} %payload.14.refs_2_), channel_id=1, source_target_pairs={{0,2},{3,5},{4,6},{2,0},{5,3},{6,4},{8,10},{11,13},{12,14},{10,8},... | collective-permute-start | bytes 1597448 | tf_op jit(solution)/shard_map/ppermute | solution.py:462
  35.9 2.7 %copy-start.5 = (f32[2,1024]{1,0:T(2,128)S(1)}, f32[2,1024]{1,0:T(2,128)}, u32[]{:S(2)}) copy-start(f32[2,1024]{1,0:T(2,128)} %refs_1_.2) | copy-start | bytes 24580
  35.9 2.7 %copy-start.6 = (f32[1024]{0:T(1024)S(1)}, f32[1024]{0:T(1024)}, u32[]{:S(2)}) copy-start(f32[1024]{0:T(1024)} %param.9) | copy-start | bytes 12292
  36.6 15.1 %collective-permute-start.11 = (f32[1040,128]{1,0:T(8,128)S(1)}, f32[1040,128]{1,0:T(8,128)S(1)}, u32[]{:S(2)}, u32[]{:S(2)}) collective-permute-start(f32[1040,128]{1,0:T(8,128)S(1)} %payload.15.refs_3_), channel_id=1, source_target_pairs={{1,3},{2,4},{5,7},{3,1},{4,2},{7,5},{9,11},{10,12},{13,15},{11,9},... | collective-permute-start | bytes 1597448 | tf_op jit(solution)/shard_map/ppermute | solution.py:462
  38.7 18.8 %collective-permute-start.18 = (f32[1040,128]{1,0:T(8,128)S(1)}, f32[1040,128]{1,0:T(8,128)S(1)}, u32[]{:S(2)}, u32[]{:S(2)}) collective-permute-start(f32[1040,128]{1,0:T(8,128)S(1)} %pick.7.refs_4_.refs_1_), channel_id=1, source_target_pairs={{0,1},{1,0},{2,3},{3,2},{4,5},{5,4},{6,7},{7,6},{8,9},{9,8},{10,11... | collective-permute-start | bytes 1597448 | tf_op jit(solution)/shard_map/ppermute | solution.py:459
  41.4 1.4 %copy-start.1 = (bf16[640,1024]{1,0:T(8,128)(2,1)S(1)}, bf16[640,1024]{1,0:T(8,128)(2,1)}, u32[]{:S(2)}) copy-start(bf16[640,1024]{1,0:T(8,128)(2,1)} %constant.4.clone.refs_2_.refs_4_) | copy-start | bytes 3932164
  41.4 1.4 %copy-start.4 = (s32[256]{0:T(256)S(1)}, s32[256]{0:T(256)}, u32[]{:S(2)}) copy-start(s32[256]{0:T(256)} %param.10) | copy-start | bytes 3076
  44.9 17.3 %collective-permute-start.15 = (f32[1040,128]{1,0:T(8,128)S(1)}, f32[1040,128]{1,0:T(8,128)S(1)}, u32[]{:S(2)}, u32[]{:S(2)}) collective-permute-start(f32[1040,128]{1,0:T(8,128)S(1)} %payload.16.refs_3_), channel_id=1, source_target_pairs={{1,3},{2,4},{5,7},{3,1},{4,2},{7,5},{9,11},{10,12},{13,15},{11,9},... | collective-permute-start | bytes 1597448 | tf_op jit(solution)/shard_map/ppermute | solution.py:462
  51.8 15.6 %collective-permute-start.14 = (f32[1040,128]{1,0:T(8,128)S(1)}, f32[1040,128]{1,0:T(8,128)S(1)}, u32[]{:S(2)}, u32[]{:S(2)}) collective-permute-start(f32[1040,128]{1,0:T(8,128)S(1)} %payload.17.refs_4_), channel_id=1, source_target_pairs={{0,2},{3,5},{4,6},{2,0},{5,3},{6,4},{8,10},{11,13},{12,14},{10,8},... | collective-permute-start | bytes 1597448 | tf_op jit(solution)/shard_map/ppermute | solution.py:462
  55.1 3.8 %collective-permute-start.16 = (f32[520,128]{1,0:T(8,128)S(1)}, f32[520,128]{1,0:T(8,128)S(1)}, u32[]{:S(2)}, u32[]{:S(2)}) collective-permute-start(f32[520,128]{1,0:T(8,128)S(1)} %get-tuple-element.81), channel_id=1, source_target_pairs={{0,1},{1,0},{2,3},{3,2},{4,5},{5,4},{6,7},{7,6},{8,9},{9,8},{10,11... | collective-permute-start | bytes 798728 | tf_op jit(solution)/shard_map/ppermute | solution.py:459
  57.4 1.5 %collective-permute-start.17 = (f32[520,128]{1,0:T(8,128)S(1)}, f32[520,128]{1,0:T(8,128)S(1)}, u32[]{:S(2)}, u32[]{:S(2)}) collective-permute-start(f32[520,128]{1,0:T(8,128)S(1)} %get-tuple-element.80), channel_id=1, source_target_pairs={{0,1},{1,0},{2,3},{3,2},{4,5},{5,4},{6,7},{7,6},{8,9},{9,8},{10,11... | collective-permute-start | bytes 798728 | tf_op jit(solution)/shard_map/ppermute | solution.py:459
  61.7 14.7 %collective-permute-start.20 = (f32[1024,128]{1,0:T(8,128)S(1)}, f32[1024,128]{1,0:T(8,128)S(1)}, u32[]{:S(2)}, u32[]{:S(2)}) collective-permute-start(f32[1024,128]{1,0:T(8,128)S(1)} %get-tuple-element.60.refs_3_), channel_id=1, source_target_pairs={{0,1},{1,0},{2,3},{3,2},{4,5},{5,4},{6,7},{7,6},{8,9},{9,8},{10,11... | collective-permute-start | bytes 1572872 | tf_op jit(solution)/shard_map/ppermute | solution.py:459
  67.5 16.7 %collective-permute-start.23 = (f32[1024,128]{1,0:T(8,128)S(1)}, f32[1024,128]{1,0:T(8,128)S(1)}, u32[]{:S(2)}, u32[]{:S(2)}) collective-permute-start(f32[1024,128]{1,0:T(8,128)S(1)} %get-tuple-element.61.refs_1_.refs_2_), channel_id=1, source_target_pairs={{0,2},{3,5},{4,6},{2,0},{5,3},{6,4},{8,10},{11,13},{12,14},{10,8},... | collective-permute-start | bytes 1572872 | tf_op jit(solution)/shard_map/ppermute | solution.py:462
  70.8 20.9 %collective-permute-start.19 = (f32[1024,128]{1,0:T(8,128)S(1)}, f32[1024,128]{1,0:T(8,128)S(1)}, u32[]{:S(2)}, u32[]{:S(2)}) collective-permute-start(f32[1024,128]{1,0:T(8,128)S(1)} %get-tuple-element.61.refs_1_.refs_2_), channel_id=1, source_target_pairs={{1,3},{2,4},{5,7},{3,1},{4,2},{7,5},{9,11},{10,12},{13,15},{11,9},... | collective-permute-start | bytes 1572872 | tf_op jit(solution)/shard_map/ppermute | solution.py:462
  73.9 19.9 %collective-permute-start.25 = (f32[1024,128]{1,0:T(8,128)S(1)}, f32[1024,128]{1,0:T(8,128)S(1)}, u32[]{:S(2)}, u32[]{:S(2)}) collective-permute-start(f32[1024,128]{1,0:T(8,128)S(1)} %get-tuple-element.64.refs_2_), channel_id=1, source_target_pairs={{0,1},{1,0},{2,3},{3,2},{4,5},{5,4},{6,7},{7,6},{8,9},{9,8},{10,11... | collective-permute-start | bytes 1572872 | tf_op jit(solution)/shard_map/ppermute | solution.py:459
  76.3 17.6 %collective-permute-start.27 = (f32[1024,128]{1,0:T(8,128)S(1)}, f32[1024,128]{1,0:T(8,128)S(1)}, u32[]{:S(2)}, u32[]{:S(2)}) collective-permute-start(f32[1024,128]{1,0:T(8,128)S(1)} %get-tuple-element.65.refs_2_), channel_id=1, source_target_pairs={{0,1},{1,0},{2,3},{3,2},{4,5},{5,4},{6,7},{7,6},{8,9},{9,8},{10,11... | collective-permute-start | bytes 1572872 | tf_op jit(solution)/shard_map/ppermute | solution.py:459
  76.5 4.6 %collective-permute-start.21 = (f32[32,1024]{1,0:T(8,128)S(1)}, f32[32,1024]{1,0:T(8,128)S(1)}, u32[]{:S(2)}, u32[]{:S(2)}) collective-permute-start(f32[32,1024]{1,0:T(8,128)S(1)} %get-tuple-element.67), channel_id=1, source_target_pairs={{0,8},{16,24},{8,0},{24,16},{1,9},{17,25},{9,1},{25,17},{2,10},{18... | collective-permute-start | bytes 393224 | tf_op jit(solution)/shard_map/ppermute | solution.py:373
  81.2 6.6 %collective-permute-start.22 = (f32[32,1024]{1,0:T(8,128)S(1)}, f32[32,1024]{1,0:T(8,128)S(1)}, u32[]{:S(2)}, u32[]{:S(2)}) collective-permute-start(f32[32,1024]{1,0:T(8,128)S(1)} %get-tuple-element.68.refs_2_), channel_id=1, source_target_pairs={{8,16},{16,8},{9,17},{17,9},{10,18},{18,10},{11,19},{19,11},{12,20... | collective-permute-start | bytes 393224 | tf_op jit(solution)/shard_map/ppermute | solution.py:373
  84.2 12.3 %collective-permute-start.26 = (f32[1024,128]{1,0:T(8,128)S(1)}, f32[1024,128]{1,0:T(8,128)S(1)}, u32[]{:S(2)}, u32[]{:S(2)}) collective-permute-start(f32[1024,128]{1,0:T(8,128)S(1)} %get-tuple-element.61.refs_1_.refs_2_), channel_id=1, source_target_pairs={{0,1},{1,0},{2,3},{3,2},{4,5},{5,4},{6,7},{7,6},{8,9},{9,8},{10,11... | collective-permute-start | bytes 1572872 | tf_op jit(solution)/shard_map/ppermute | solution.py:459
  87.8 13.3 %collective-permute-start.29 = (f32[1024,128]{1,0:T(8,128)S(1)}, f32[1024,128]{1,0:T(8,128)S(1)}, u32[]{:S(2)}, u32[]{:S(2)}) collective-permute-start(f32[1024,128]{1,0:T(8,128)S(1)} %payload.18.refs_2_), channel_id=1, source_target_pairs={{1,3},{2,4},{5,7},{3,1},{4,2},{7,5},{9,11},{10,12},{13,15},{11,9},... | collective-permute-start | bytes 1572872 | tf_op jit(solution)/shard_map/ppermute | solution.py:462
  91.8 14.5 %collective-permute-start.24 = (f32[1024,128]{1,0:T(8,128)S(1)}, f32[1024,128]{1,0:T(8,128)S(1)}, u32[]{:S(2)}, u32[]{:S(2)}) collective-permute-start(f32[1024,128]{1,0:T(8,128)S(1)} %payload.19.refs_2_), channel_id=1, source_target_pairs={{0,2},{3,5},{4,6},{2,0},{5,3},{6,4},{8,10},{11,13},{12,14},{10,8},... | collective-permute-start | bytes 1572872 | tf_op jit(solution)/shard_map/ppermute | solution.py:462
  95.3 12.9 %collective-permute-start.35 = (f32[1024,128]{1,0:T(8,128)S(1)}, f32[1024,128]{1,0:T(8,128)S(1)}, u32[]{:S(2)}, u32[]{:S(2)}) collective-permute-start(f32[1024,128]{1,0:T(8,128)S(1)} %get-tuple-element.71.refs_3_), channel_id=1, source_target_pairs={{0,1},{1,0},{2,3},{3,2},{4,5},{5,4},{6,7},{7,6},{8,9},{9,8},{10,11... | collective-permute-start | bytes 1572872 | tf_op jit(solution)/shard_map/ppermute | solution.py:459
  96.5 14.8 %collective-permute-start.38 = (f32[1024,128]{1,0:T(8,128)S(1)}, f32[1024,128]{1,0:T(8,128)S(1)}, u32[]{:S(2)}, u32[]{:S(2)}) collective-permute-start(f32[1024,128]{1,0:T(8,128)S(1)} %pick.9.refs_2_.refs_1_), channel_id=1, source_target_pairs={{0,1},{1,0},{2,3},{3,2},{4,5},{5,4},{6,7},{7,6},{8,9},{9,8},{10,11... | collective-permute-start | bytes 1572872 | tf_op jit(solution)/shard_map/ppermute | solution.py:459
  100.6 3.6 %collective-permute-start.28 = (f32[2,256]{1,0:T(2,128)S(1)}, f32[2,256]{1,0:T(2,128)S(1)}, u32[]{:S(2)}, u32[]{:S(2)}) collective-permute-start(f32[2,256]{1,0:T(2,128)S(1)} %get-tuple-element.72.refs_3_.refs_0_), channel_id=1, source_target_pairs={{0,1},{1,0},{2,3},{3,2},{4,5},{5,4},{6,7},{7,6},{8,9},{9,8},{10,11... | collective-permute-start | bytes 6152 | tf_op jit(solution)/shard_map/ppermute | solution.py:647
  101.2 15.5 %collective-permute-start.34 = (f32[1024,128]{1,0:T(8,128)S(1)}, f32[1024,128]{1,0:T(8,128)S(1)}, u32[]{:S(2)}, u32[]{:S(2)}) collective-permute-start(f32[1024,128]{1,0:T(8,128)S(1)} %payload.20.refs_2_), channel_id=1, source_target_pairs={{0,2},{3,5},{4,6},{2,0},{5,3},{6,4},{8,10},{11,13},{12,14},{10,8},... | collective-permute-start | bytes 1572872 | tf_op jit(solution)/shard_map/ppermute | solution.py:462
  106.3 16.4 %collective-permute-start.30 = (f32[1024,128]{1,0:T(8,128)S(1)}, f32[1024,128]{1,0:T(8,128)S(1)}, u32[]{:S(2)}, u32[]{:S(2)}) collective-permute-start(f32[1024,128]{1,0:T(8,128)S(1)} %payload.21.refs_2_), channel_id=1, source_target_pairs={{1,3},{2,4},{5,7},{3,1},{4,2},{7,5},{9,11},{10,12},{13,15},{11,9},... | collective-permute-start | bytes 1572872 | tf_op jit(solution)/shard_map/ppermute | solution.py:462
  108.6 3.8 %collective-permute-start.36 = (f32[512,128]{1,0:T(8,128)S(1)}, f32[512,128]{1,0:T(8,128)S(1)}, u32[]{:S(2)}, u32[]{:S(2)}) collective-permute-start(f32[512,128]{1,0:T(8,128)S(1)} %get-tuple-element.85), channel_id=1, source_target_pairs={{0,1},{1,0},{2,3},{3,2},{4,5},{5,4},{6,7},{7,6},{8,9},{9,8},{10,11... | collective-permute-start | bytes 786440 | tf_op jit(solution)/shard_map/ppermute | solution.py:459
  111.2 2.2 %collective-permute-start.37 = (f32[512,128]{1,0:T(8,128)S(1)}, f32[512,128]{1,0:T(8,128)S(1)}, u32[]{:S(2)}, u32[]{:S(2)}) collective-permute-start(f32[512,128]{1,0:T(8,128)S(1)} %get-tuple-element.84), channel_id=1, source_target_pairs={{0,1},{1,0},{2,3},{3,2},{4,5},{5,4},{6,7},{7,6},{8,9},{9,8},{10,11... | collective-permute-start | bytes 786440 | tf_op jit(solution)/shard_map/ppermute | solution.py:459
  111.3 10.7 %collective-permute-start.31 = (f32[2,256]{1,0:T(2,128)S(1)}, f32[2,256]{1,0:T(2,128)S(1)}, u32[]{:S(2)}, u32[]{:S(2)}) collective-permute-start(f32[2,256]{1,0:T(2,128)S(1)} %get-tuple-element.74.refs_0_), channel_id=1, source_target_pairs={{0,2},{1,3},{2,0},{3,1},{4,6},{5,7},{6,4},{7,5},{8,10},{9,11},{10,... | collective-permute-start | bytes 6152 | tf_op jit(solution)/shard_map/ppermute | solution.py:647
  112.4 9.7 %collective-permute-start.32 = (f32[2,256]{1,0:T(2,128)S(1)}, f32[2,256]{1,0:T(2,128)S(1)}, u32[]{:S(2)}, u32[]{:S(2)}) collective-permute-start(f32[2,256]{1,0:T(2,128)S(1)} %get-tuple-element.74.refs_0_), channel_id=1, source_target_pairs={{0,4},{1,5},{2,6},{3,7},{4,0},{5,1},{6,2},{7,3},{8,12},{9,13},{10,... | collective-permute-start | bytes 6152 | tf_op jit(solution)/shard_map/ppermute | solution.py:647
  113.4 8.6 %collective-permute-start.33 = (f32[2,256]{1,0:T(2,128)S(1)}, f32[2,256]{1,0:T(2,128)S(1)}, u32[]{:S(2)}, u32[]{:S(2)}) collective-permute-start(f32[2,256]{1,0:T(2,128)S(1)} %get-tuple-element.74.refs_0_), channel_id=1, source_target_pairs={{0,6},{1,7},{2,4},{3,5},{4,2},{5,3},{6,0},{7,1},{8,14},{9,15},{10,... | collective-permute-start | bytes 6152 | tf_op jit(solution)/shard_map/ppermute | solution.py:647
  116.8 14.2 %collective-permute-start.40 = (f32[1024,128]{1,0:T(8,128)S(1)}, f32[1024,128]{1,0:T(8,128)S(1)}, u32[]{:S(2)}, u32[]{:S(2)}) collective-permute-start(f32[1024,128]{1,0:T(8,128)S(1)} %payload.22.refs_4_), channel_id=1, source_target_pairs={{1,3},{2,4},{5,7},{3,1},{4,2},{7,5},{9,11},{10,12},{13,15},{11,9},... | collective-permute-start | bytes 1572872 | tf_op jit(solution)/shard_map/ppermute | solution.py:462
  122.7 15.5 %collective-permute-start.39 = (f32[1024,128]{1,0:T(8,128)S(1)}, f32[1024,128]{1,0:T(8,128)S(1)}, u32[]{:S(2)}, u32[]{:S(2)}) collective-permute-start(f32[1024,128]{1,0:T(8,128)S(1)} %payload.23.refs_4_), channel_id=1, source_target_pairs={{0,2},{3,5},{4,6},{2,0},{5,3},{6,4},{8,10},{11,13},{12,14},{10,8},... | collective-permute-start | bytes 1572872 | tf_op jit(solution)/shard_map/ppermute | solution.py:462
  125.7 3.5 %collective-permute-start.41 = (f32[512,128]{1,0:T(8,128)S(1)}, f32[512,128]{1,0:T(8,128)S(1)}, u32[]{:S(2)}, u32[]{:S(2)}) collective-permute-start(f32[512,128]{1,0:T(8,128)S(1)} %get-tuple-element.83), channel_id=1, source_target_pairs={{0,1},{1,0},{2,3},{3,2},{4,5},{5,4},{6,7},{7,6},{8,9},{9,8},{10,11... | collective-permute-start | bytes 786440 | tf_op jit(solution)/shard_map/ppermute | solution.py:459
  128.0 1.5 %collective-permute-start.42 = (f32[512,128]{1,0:T(8,128)S(1)}, f32[512,128]{1,0:T(8,128)S(1)}, u32[]{:S(2)}, u32[]{:S(2)}) collective-permute-start(f32[512,128]{1,0:T(8,128)S(1)} %get-tuple-element.82), channel_id=1, source_target_pairs={{0,1},{1,0},{2,3},{3,2},{4,5},{5,4},{6,7},{7,6},{8,9},{9,8},{10,11... | collective-permute-start | bytes 786440 | tf_op jit(solution)/shard_map/ppermute | solution.py:459

commit v9 on v8

--- a/solution.py
+++ b/solution.py
@@ -213,6 +213,10 @@
         rows = slice(first, first + piece.shape[0])
         out[rows] = one[rows] + piece[...]
         first += piece.shape[0]
+
+
+def pass_on(value, out):
+    out[...] = value[...]
 
 
 def add_all(*refs):
@@ -480,8 +484,9 @@
             for slot in slots:
                 (self.terms[slot],) = call(add, [part], self.terms[slot])
 
-        def take_own(self):
-            self.blocks.append((self.own, *exchange(self.own)))
+        def take_own(self, later=False):
+            own = call(pass_on, [self.own.shape], [self.own])[0] if later else self.own
+            self.blocks.append((self.own, *exchange(own)))
 
         def send(self, step, between=None):
             sent = {}
@@ -594,7 +599,6 @@
     )
     two.begin(mid_b)
     two.add_terms(mid_a)
-    two.add_terms(mid_a)
     two.join_terms(0)
     strips = paired(*call(strip_pairs, [(HALO, modes)] * 2, [leading, last]))
     flux = None
@@ -602,19 +606,21 @@
         if step == 1:
             two.send(step, unpack)
             two.take_own()
-            two.join_terms(1, 2)
+            two.join_terms(1)
         elif step == 2:
             two.send(step, lambda: flux.over(1))
-            two.join_terms(*range(3, chips))
+            two.join_terms(*range(2, chips))
         elif step == chips - 1:
             two.send(step, lambda: flux.over(*range(2, devices, 2)))
         else:
             two.send(step)
         two.take(step, 2 if step >= chips - 2 else 1)
         if step == 1:
-            for slot in range(3, chips):
+            for slot in range(2, chips):
                 two.add_terms(mid_a)
-        if step < chips - 1:
+        if step == 2:
+            two.multiply(0)
+        if 1 < step < chips - 1:
             two.multiply(step - 1)
         if step == chips - 2:
             two.multiply(step)

time: 140 us -> 135 us (0.964); the launches traced: 139 us -> 133 us
  waiting for transfers between devices: 30.2 us -> 24.6 us
    ppermute x4, waiting for transfers between devices: 5.21 us -> 2.11 us  [paired(): lax.ppermute(value, 'space', pairs + [(j, i) for i, j in pairs])]
    ppermute x4, starting transfers between devices: 2.08 us -> 4.21 us  [over(): lax.ppermute(self.value, 'mode', [(i, i ^ bit) for i in range(self.device...]
    ppermute x16, starting transfers between devices: 45.6 us -> 43.9 us  [along(): return lax.ppermute(value, 'mode', plan.pairs[stream])]
  transfers between devices with their start and end apart: 43 -> 43, of which waited for: 13 -> 13; matrix products, arithmetic and copies ran while one was open for 0% -> 0% of each run, Pallas kernels for 23% -> 24%
where the time goes in v9:
time: 135 us; the launch traced here: 133 us
  starting transfers between devices  70.6 us (52%)
  Pallas kernels  34.9 us (26%)
  waiting for transfers between devices  24.6 us (18%)
  between operations  1.58 us (1%)
    ppermute x16, starting transfers between devices, along(): return lax.ppermute(value, 'mode', plan.pairs[stream])  43.9 us
    pallas_call x53, Pallas kernels, __call__(): pl.pallas_call(body, out_shape=[jax.ShapeDtypeStruct(shape, jnp.float32)...  34.9 us
    ppermute x16, waiting for transfers between devices, along(): return lax.ppermute(value, 'mode', plan.pairs[stream])  20.1 us
    ppermute x19, starting transfers between devices, exchange(): lax.ppermute(value[i:j], 'mode', across)  15.7 us
    ppermute x4, starting transfers between devices, paired(): lax.ppermute(value, 'space', pairs + [(j, i) for i, j in pairs])  6.75 us
    ppermute x4, starting transfers between devices, over(): lax.ppermute(self.value, 'mode', [(i, i ^ bit) for i in range(self.device...  4.21 us
  transfers between devices with their start and end apart: 43, of which 13 were waited for; matrix products, arithmetic and copies ran while one was open for 0% of the time, Pallas kernels for 24%

profile of v9, /device:TPU:13, one launch (start us, length us, event | category | flops | bytes accessed | tf_op | source)
XLA Modules:
  0.0 132.6 jit_solution(3440127914332733377)
XLA Ops:
  0.6 2.0 %own_rows.1 = (f32[1040,128]{1,0:T(8,128)}, f32[8,128]{1,0:T(8,128)}) custom-call(f32[1024,256]{1,0:T(8,128)} %refs_0_.9, f32[2,1024]{1,0:T(2,128)} %refs_1_.2, f32[1,1024]{1,0:T(1,128)} %bitcast.4), custom_call_target="tpu_custom_call" | custom-call | flops 1024 | bytes 1024 | tf_op jit(solution)/shard_map/own_rows/pallas_call | solution.py:39
  2.6 2.1 %collective-permute-start = (f32[1040,128]{1,0:T(8,128)}, f32[1040,128]{1,0:T(8,128)S(1)}, u32[]{:S(2)}, u32[]{:S(2)}) collective-permute-start(f32[1040,128]{1,0:T(8,128)} %get-tuple-element.41.refs_1_), channel_id=1, source_target_pairs={{1,3},{2,4},{5,7},{3,1},{4,2},{7,5},{9,11},{10,12},{13,15},{11,9},... | collective-permute-start | bytes 1597448 | tf_op jit(solution)/shard_map/ppermute | solution.py:466
  4.7 4.3 %collective-permute-start.2 = (f32[1040,128]{1,0:T(8,128)}, f32[1040,128]{1,0:T(8,128)S(1)}, u32[]{:S(2)}, u32[]{:S(2)}) collective-permute-start(f32[1040,128]{1,0:T(8,128)} %get-tuple-element.41.refs_1_), channel_id=1, source_target_pairs={{0,2},{3,5},{4,6},{2,0},{5,3},{6,4},{8,10},{11,13},{12,14},{10,8},... | collective-permute-start | bytes 1597448 | tf_op jit(solution)/shard_map/ppermute | solution.py:466
  9.1 0.7 copy-done.3
  9.7 7.4 %load_and_products.1 = (f32[1024,128]{1,0:T(8,128)S(1)}, f32[1024,128]{1,0:T(8,128)S(1)}, f32[1024,128]{1,0:T(8,128)S(1)}, f32[1024,128]{1,0:T(8,128)S(1)}, f32[...) custom-call(bf16[8192,1024]{1,0:T(8,128)(2,1)} %refs_0_.6, ...), custom_call_target="tpu_custom_call" | custom-call | flops 1024 | bytes 1024 | tf_op jit(solution)/shard_map/load_and_products/pallas_call | solution.py:39
  17.3 0.5 collective-permute-start.4
  17.8 0.6 collective-permute-start.5
  18.4 1.3 collective-permute-done.2.refs_0_
  19.9 2.3 %collective-permute-start.9 = (f32[1040,128]{1,0:T(8,128)S(1)}, f32[1040,128]{1,0:T(8,128)S(1)}, u32[]{:S(2)}, u32[]{:S(2)}) collective-permute-start(f32[1040,128]{1,0:T(8,128)S(1)} %payload.12.refs_2_), channel_id=1, source_target_pairs={{1,3},{2,4},{5,7},{3,1},{4,2},{7,5},{9,11},{10,12},{13,15},{11,9},... | collective-permute-start | bytes 1597448 | tf_op jit(solution)/shard_map/ppermute | solution.py:466
  22.3 3.6 %collective-permute-start.3 = (f32[1040,128]{1,0:T(8,128)S(1)}, f32[1040,128]{1,0:T(8,128)S(1)}, u32[]{:S(2)}, u32[]{:S(2)}) collective-permute-start(f32[1040,128]{1,0:T(8,128)S(1)} %payload.13.refs_2_), channel_id=1, source_target_pairs={{0,2},{3,5},{4,6},{2,0},{5,3},{6,4},{8,10},{11,13},{12,14},{10,8},... | collective-permute-start | bytes 1597448 | tf_op jit(solution)/shard_map/ppermute | solution.py:466
  26.5 1.3 collective-permute-start.7
  27.8 2.1 %collective-permute-start.8 = (f32[32,1024]{1,0:T(8,128)S(1)}, f32[32,1024]{1,0:T(8,128)S(1)}, u32[]{:S(2)}, u32[]{:S(2)}) collective-permute-start(f32[32,1024]{1,0:T(8,128)S(1)} %get-tuple-element.55.refs_3_), channel_id=1, source_target_pairs={{8,16},{16,8},{9,17},{17,9},{10,18},{18,10},{11,19},{19,11},{12,20... | collective-permute-start | bytes 393224 | tf_op jit(solution)/shard_map/ppermute | solution.py:377
  29.9 0.6 collective-permute-start.13
  30.5 1.4 %two_blocks.8.refs_3_ = f32[272,1024]{1,0:T(8,128)S(1)} custom-call(bf16[8192,1024]{1,0:T(8,128)(2,1)S(1)} %get-tuple-element.45.refs_2_.refs_0_, f32[1040,128]{1,0:T(8,128)S(1)} %copy-done.2, f32[1040,128]{1,0:T(8,128)S(1)} %collective-permute-done.10.refs_2_, f32[32,1024]{1,0:T(8,128)S(1)} %get-tuple-element.55.refs_3_), custom_call_target="tpu_custom_call" | custom-call | flops 1024 | bytes 1024 | tf_op jit(solution)/shard_map/two_blocks/pallas_call | solution.py:39
  32.0 3.7 %collective-permute-start.12 = (f32[1040,128]{1,0:T(8,128)S(1)}, f32[1040,128]{1,0:T(8,128)S(1)}, u32[]{:S(2)}, u32[]{:S(2)}) collective-permute-start(f32[1040,128]{1,0:T(8,128)S(1)} %payload.14.refs_2_), channel_id=1, source_target_pairs={{0,2},{3,5},{4,6},{2,0},{5,3},{6,4},{8,10},{11,13},{12,14},{10,8},... | collective-permute-start | bytes 1597448 | tf_op jit(solution)/shard_map/ppermute | solution.py:466
  35.9 0.6 collective-permute-done.3.refs_0_
  36.6 1.9 %collective-permute-start.11 = (f32[1040,128]{1,0:T(8,128)S(1)}, f32[1040,128]{1,0:T(8,128)S(1)}, u32[]{:S(2)}, u32[]{:S(2)}) collective-permute-start(f32[1040,128]{1,0:T(8,128)S(1)} %payload.15.refs_3_), channel_id=1, source_target_pairs={{1,3},{2,4},{5,7},{3,1},{4,2},{7,5},{9,11},{10,12},{13,15},{11,9},... | collective-permute-start | bytes 1597448 | tf_op jit(solution)/shard_map/ppermute | solution.py:466
  38.7 2.6 %collective-permute-start.18 = (f32[1040,128]{1,0:T(8,128)S(1)}, f32[1040,128]{1,0:T(8,128)S(1)}, u32[]{:S(2)}, u32[]{:S(2)}) collective-permute-start(f32[1040,128]{1,0:T(8,128)S(1)} %pick.7.refs_4_.refs_1_), channel_id=1, source_target_pairs={{0,1},{1,0},{2,3},{3,2},{4,5},{5,4},{6,7},{7,6},{8,9},{9,8},{10,11... | collective-permute-start | bytes 1597448 | tf_op jit(solution)/shard_map/ppermute | solution.py:463
  41.4 1.4 %two_blocks.9.refs_5_.refs_3_ = f32[272,1024]{1,0:T(8,128)S(1)} custom-call(bf16[8192,1024]{1,0:T(8,128)(2,1)S(1)} %get-tuple-element.45.refs_2_.refs_0_, f32[1040,128]{1,0:T(8,128)S(1)} %pick.6.refs_2_.refs_1_, f32[1040,128]{1,0:T(8,128)S(1)} %collective-permute-done.13.refs_2_, f32[272,1024]{1,0:T(8,128)S(1)} %two_blocks.8.refs_3_, ...), custom_call_target="tpu_custom_call" | custom-call | flops 1024 | bytes 1024 | tf_op jit(solution)/shard_map/two_blocks/pallas_call | solution.py:39
  42.8 2.0 %first_rest.1 = (f32[1024,128]{1,0:T(8,128)S(1)}, f32[1024,128]{1,0:T(8,128)S(1)}) custom-call(f32[1024,256]{1,0:T(8,128)S(1)} %copy-done, bf16[1024,128]{1,0:T(8,128)(2,1)S(1)} %strip_columns.2.refs_3_.refs_1_, bf16[640,1024]{1,0:T(8,128)(2,1)S(1)} %copy-done.1, f32[8,1024]{1,0:T(8,128)S(1)} %maximum_maximum_fusion.refs_3_.refs_5_, s32[1,256]{1,0:T(1,128)S(1)} %bitcast.2, ...), custom_call_target="tpu_custom_call" | custom-call | flops 1024 | bytes 1024 | tf_op jit(solution)/shard_map/first_rest/pallas_call | solution.py:39
  44.9 1.9 %collective-permute-start.15 = (f32[1040,128]{1,0:T(8,128)S(1)}, f32[1040,128]{1,0:T(8,128)S(1)}, u32[]{:S(2)}, u32[]{:S(2)}) collective-permute-start(f32[1040,128]{1,0:T(8,128)S(1)} %payload.16.refs_3_), channel_id=1, source_target_pairs={{1,3},{2,4},{5,7},{3,1},{4,2},{7,5},{9,11},{10,12},{13,15},{11,9},... | collective-permute-start | bytes 1597448 | tf_op jit(solution)/shard_map/ppermute | solution.py:466
  46.9 4.8 %collective-permute-done.11.refs_0_.refs_3_ = f32[1040,128]{1,0:T(8,128)S(1)} collective-permute-done((f32[1040,128]{1,0:T(8,128)S(1)}, f32[1040,128]{1,0:T(8,128)S(1)}, u32[]{:S(2)}, u32[]{:S(2)}) %collective-permute-start.11) | collective-permute-done | bytes 532512 | tf_op jit(solution)/shard_map/ppermute | solution.py:466
  51.8 3.0 %collective-permute-start.14 = (f32[1040,128]{1,0:T(8,128)S(1)}, f32[1040,128]{1,0:T(8,128)S(1)}, u32[]{:S(2)}, u32[]{:S(2)}) collective-permute-start(f32[1040,128]{1,0:T(8,128)S(1)} %payload.17.refs_4_), channel_id=1, source_target_pairs={{0,2},{3,5},{4,6},{2,0},{5,3},{6,4},{8,10},{11,13},{12,14},{10,8},... | collective-permute-start | bytes 1597448 | tf_op jit(solution)/shard_map/ppermute | solution.py:466
  55.1 2.3 %collective-permute-start.16 = (f32[520,128]{1,0:T(8,128)S(1)}, f32[520,128]{1,0:T(8,128)S(1)}, u32[]{:S(2)}, u32[]{:S(2)}) collective-permute-start(f32[520,128]{1,0:T(8,128)S(1)} %get-tuple-element.81), channel_id=1, source_target_pairs={{0,1},{1,0},{2,3},{3,2},{4,5},{5,4},{6,7},{7,6},{8,9},{9,8},{10,11... | collective-permute-start | bytes 798728 | tf_op jit(solution)/shard_map/ppermute | solution.py:463
  57.5 1.4 %two_blocks.10.refs_4_.refs_6_ = f32[272,1024]{1,0:T(8,128)S(1)} custom-call(bf16[8192,1024]{1,0:T(8,128)(2,1)S(1)} %get-tuple-element.45.refs_2_.refs_0_, f32[1040,128]{1,0:T(8,128)S(1)} %pick.7.refs_4_.refs_1_, f32[1040,128]{1,0:T(8,128)S(1)} %collective-permute-done.18.refs_2_, f32[272,1024]{1,0:T(8,128)S(1)} %two_blocks.9.refs_5_.refs_3_, ...), custom_call_target="tpu_custom_call" | custom-call | flops 1024 | bytes 1024 | tf_op jit(solution)/shard_map/two_blocks/pallas_call | solution.py:39
  59.0 1.5 %two_blocks.11 = (f32[1024,128]{1,0:T(8,128)S(1)}, f32[32,1024]{1,0:T(8,128)S(1)}, f32[8,1024]{1,0:T(8,128)S(1)}) custom-call(bf16[8192,1024]{1,0:T(8,128)(2,1)S(1)} %get-tuple-element.45.refs_2_.refs_0_, f32[1040,128]{1,0:T(8,128)S(1)} %pick.8.refs_4_.refs_1_, f32[520,128]{1,0:T(8,128)S(1)} %collective-permute-done.16.refs_2_, ...), custom_call_target="tpu_custom_call" | custom-call | flops 1024 | bytes 1024 | tf_op jit(solution)/shard_map/two_blocks/pallas_call | solution.py:39
  60.5 1.3 slot_products.4
  61.8 0.4 collective-permute-start.20
  62.3 5.1 %collective-permute-done.14.refs_0_ = f32[1040,128]{1,0:T(8,128)S(1)} collective-permute-done((f32[1040,128]{1,0:T(8,128)S(1)}, f32[1040,128]{1,0:T(8,128)S(1)}, u32[]{:S(2)}, u32[]{:S(2)}) %collective-permute-start.14) | collective-permute-done | bytes 532512 | tf_op jit(solution)/shard_map/ppermute | solution.py:466
  67.6 3.2 %collective-permute-start.23 = (f32[1024,128]{1,0:T(8,128)S(1)}, f32[1024,128]{1,0:T(8,128)S(1)}, u32[]{:S(2)}, u32[]{:S(2)}) collective-permute-start(f32[1024,128]{1,0:T(8,128)S(1)} %get-tuple-element.61.refs_2_.refs_1_), channel_id=1, source_target_pairs={{0,2},{3,5},{4,6},{2,0},{5,3},{6,4},{8,10},{11,13},{12,14},{10,8},... | collective-permute-start | bytes 1572872 | tf_op jit(solution)/shard_map/ppermute | solution.py:466
  70.8 1.9 %collective-permute-start.19 = (f32[1024,128]{1,0:T(8,128)S(1)}, f32[1024,128]{1,0:T(8,128)S(1)}, u32[]{:S(2)}, u32[]{:S(2)}) collective-permute-start(f32[1024,128]{1,0:T(8,128)S(1)} %get-tuple-element.61.refs_2_.refs_1_), channel_id=1, source_target_pairs={{1,3},{2,4},{5,7},{3,1},{4,2},{7,5},{9,11},{10,12},{13,15},{11,9},... | collective-permute-start | bytes 1572872 | tf_op jit(solution)/shard_map/ppermute | solution.py:466
  72.7 1.3 slot_products.5
  74.0 1.1 collective-permute-start.25
  75.2 1.3 collective-permute-start.21
  76.5 2.1 %collective-permute-start.22 = (f32[32,1024]{1,0:T(8,128)S(1)}, f32[32,1024]{1,0:T(8,128)S(1)}, u32[]{:S(2)}, u32[]{:S(2)}) collective-permute-start(f32[32,1024]{1,0:T(8,128)S(1)} %get-tuple-element.67.refs_2_), channel_id=1, source_target_pairs={{8,16},{16,8},{9,17},{17,9},{10,18},{18,10},{11,19},{19,11},{12,20... | collective-permute-start | bytes 393224 | tf_op jit(solution)/shard_map/ppermute | solution.py:377
  78.6 1.4 %collective-permute-done.23.refs_0_ = f32[1024,128]{1,0:T(8,128)S(1)} collective-permute-done((f32[1024,128]{1,0:T(8,128)S(1)}, f32[1024,128]{1,0:T(8,128)S(1)}, u32[]{:S(2)}, u32[]{:S(2)}) %collective-permute-start.23) | collective-permute-done | bytes 524320 | tf_op jit(solution)/shard_map/ppermute | solution.py:466
  80.0 1.9 %collective-permute-start.27 = (f32[1024,128]{1,0:T(8,128)S(1)}, f32[1024,128]{1,0:T(8,128)S(1)}, u32[]{:S(2)}, u32[]{:S(2)}) collective-permute-start(f32[1024,128]{1,0:T(8,128)S(1)} %payload.18.refs_2_), channel_id=1, source_target_pairs={{1,3},{2,4},{5,7},{3,1},{4,2},{7,5},{9,11},{10,12},{13,15},{11,9},... | collective-permute-start | bytes 1572872 | tf_op jit(solution)/shard_map/ppermute | solution.py:466
  82.0 2.1 %collective-permute-done.22.refs_1_ = f32[32,1024]{1,0:T(8,128)S(1)} collective-permute-done((f32[32,1024]{1,0:T(8,128)S(1)}, f32[32,1024]{1,0:T(8,128)S(1)}, u32[]{:S(2)}, u32[]{:S(2)}) %collective-permute-start.22) | collective-permute-done | bytes 131104 | tf_op jit(solution)/shard_map/ppermute | solution.py:377
  84.2 0.6 collective-permute-done.19.refs_0_.refs_1_
  84.8 2.8 %collective-permute-start.24 = (f32[1024,128]{1,0:T(8,128)S(1)}, f32[1024,128]{1,0:T(8,128)S(1)}, u32[]{:S(2)}, u32[]{:S(2)}) collective-permute-start(f32[1024,128]{1,0:T(8,128)S(1)} %payload.19.refs_2_), channel_id=1, source_target_pairs={{0,2},{3,5},{4,6},{2,0},{5,3},{6,4},{8,10},{11,13},{12,14},{10,8},... | collective-permute-start | bytes 1572872 | tf_op jit(solution)/shard_map/ppermute | solution.py:466
  87.7 1.3 slot_products.6
  89.0 2.4 %collective-permute-start.29 = (f32[1024,128]{1,0:T(8,128)S(1)}, f32[1024,128]{1,0:T(8,128)S(1)}, u32[]{:S(2)}, u32[]{:S(2)}) collective-permute-start(f32[1024,128]{1,0:T(8,128)S(1)} %get-tuple-element.69.refs_2_), channel_id=1, source_target_pairs={{0,1},{1,0},{2,3},{3,2},{4,5},{5,4},{6,7},{7,6},{8,9},{9,8},{10,11... | collective-permute-start | bytes 1572872 | tf_op jit(solution)/shard_map/ppermute | solution.py:463
  91.4 1.3 slot_products.7
  92.7 2.7 %second_rest.1 = (f32[1024,128]{1,0:T(8,128)S(1)}, f32[1024,128]{1,0:T(8,128)S(1)}, f32[2,256]{1,0:T(2,128)S(1)}) custom-call(f32[1024,256]{1,0:T(8,128)S(1)} %copy-done, f32[1024,128]{1,0:T(8,128)S(1)} %get-tuple-element.58.refs_1_, f32[1024,128]{1,0:T(8,128)S(1)} %get-tuple-element.61.refs_2_.refs_1_, bf16[1024,128]{1,0:T(8,128)(2,1)S(1)} %strip_columns.3.refs_2_.refs_3_, ...), custom_call_target="tpu_custom_call" | custom-call | flops 1024 | bytes 1024 | tf_op jit(solution)/shard_map/second_rest/pallas_call | solution.py:39
  95.4 0.6 collective-permute-start.26
  96.0 0.8 collective-permute-done.26.refs_1_
  97.2 2.8 %collective-permute-start.37 = (f32[1024,128]{1,0:T(8,128)S(1)}, f32[1024,128]{1,0:T(8,128)S(1)}, u32[]{:S(2)}, u32[]{:S(2)}) collective-permute-start(f32[1024,128]{1,0:T(8,128)S(1)} %pick.9.refs_2_.refs_1_), channel_id=1, source_target_pairs={{0,1},{1,0},{2,3},{3,2},{4,5},{5,4},{6,7},{7,6},{8,9},{9,8},{10,11... | collective-permute-start | bytes 1572872 | tf_op jit(solution)/shard_map/ppermute | solution.py:463
  100.1 3.8 %collective-permute-start.33 = (f32[1024,128]{1,0:T(8,128)S(1)}, f32[1024,128]{1,0:T(8,128)S(1)}, u32[]{:S(2)}, u32[]{:S(2)}) collective-permute-start(f32[1024,128]{1,0:T(8,128)S(1)} %payload.20.refs_2_), channel_id=1, source_target_pairs={{0,2},{3,5},{4,6},{2,0},{5,3},{6,4},{8,10},{11,13},{12,14},{10,8},... | collective-permute-start | bytes 1572872 | tf_op jit(solution)/shard_map/ppermute | solution.py:466
  104.0 1.9 %collective-permute-start.28 = (f32[1024,128]{1,0:T(8,128)S(1)}, f32[1024,128]{1,0:T(8,128)S(1)}, u32[]{:S(2)}, u32[]{:S(2)}) collective-permute-start(f32[1024,128]{1,0:T(8,128)S(1)} %payload.21.refs_2_), channel_id=1, source_target_pairs={{1,3},{2,4},{5,7},{3,1},{4,2},{7,5},{9,11},{10,12},{13,15},{11,9},... | collective-permute-start | bytes 1572872 | tf_op jit(solution)/shard_map/ppermute | solution.py:466
  107.0 1.5 %collective-permute-start.30 = (f32[2,256]{1,0:T(2,128)S(1)}, f32[2,256]{1,0:T(2,128)S(1)}, u32[]{:S(2)}, u32[]{:S(2)}) collective-permute-start(f32[2,256]{1,0:T(2,128)S(1)} %get-tuple-element.74.refs_0_), channel_id=1, source_target_pairs={{0,2},{1,3},{2,0},{3,1},{4,6},{5,7},{6,4},{7,5},{8,10},{9,11},{10,... | collective-permute-start | bytes 6152 | tf_op jit(solution)/shard_map/ppermute | solution.py:653
  108.5 0.7 collective-permute-start.31
  109.2 1.5 %collective-permute-start.32 = (f32[2,256]{1,0:T(2,128)S(1)}, f32[2,256]{1,0:T(2,128)S(1)}, u32[]{:S(2)}, u32[]{:S(2)}) collective-permute-start(f32[2,256]{1,0:T(2,128)S(1)} %get-tuple-element.74.refs_0_), channel_id=1, source_target_pairs={{0,6},{1,7},{2,4},{3,5},{4,2},{5,3},{6,0},{7,1},{8,14},{9,15},{10,... | collective-permute-start | bytes 6152 | tf_op jit(solution)/shard_map/ppermute | solution.py:653
  110.7 1.3 two_blocks.12.refs_3_.refs_4_
  112.0 1.3 two_blocks.13.refs_4_.refs_5_
  113.3 1.3 %two_blocks.14.refs_3_.refs_4_ = f32[256,1024]{1,0:T(8,128)S(1)} custom-call(bf16[8192,1024]{1,0:T(8,128)(2,1)S(1)} %get-tuple-element.45.refs_2_.refs_0_, f32[1024,128]{1,0:T(8,128)S(1)} %pick.10.refs_3_.refs_1_, f32[512,128]{1,0:T(8,128)S(1)} %collective-permute-done.35.refs_2_, f32[512,128]{1,0:T(8,128)S(1)} %collective-permute-done.36.refs_3_, ...), custom_call_target="tpu_custom_call" | custom-call | flops 1024 | bytes 1024 | tf_op jit(solution)/shard_map/two_blocks/pallas_call | solution.py:39
  114.8 3.3 %collective-permute-start.40 = (f32[1024,128]{1,0:T(8,128)S(1)}, f32[1024,128]{1,0:T(8,128)S(1)}, u32[]{:S(2)}, u32[]{:S(2)}) collective-permute-start(f32[1024,128]{1,0:T(8,128)S(1)} %payload.22.refs_4_), channel_id=1, source_target_pairs={{1,3},{2,4},{5,7},{3,1},{4,2},{7,5},{9,11},{10,12},{13,15},{11,9},... | collective-permute-start | bytes 1572872 | tf_op jit(solution)/shard_map/ppermute | solution.py:466
  118.1 0.6 add_all.3
  118.7 2.1 %collective-permute-start.39 = (f32[1024,128]{1,0:T(8,128)S(1)}, f32[1024,128]{1,0:T(8,128)S(1)}, u32[]{:S(2)}, u32[]{:S(2)}) collective-permute-start(f32[1024,128]{1,0:T(8,128)S(1)} %payload.23.refs_4_), channel_id=1, source_target_pairs={{0,2},{3,5},{4,6},{2,0},{5,3},{6,4},{8,10},{11,13},{12,14},{10,8},... | collective-permute-start | bytes 1572872 | tf_op jit(solution)/shard_map/ppermute | solution.py:466
  121.0 1.1 collective-permute-start.41
  122.1 1.1 collective-permute-done.41.refs_2_
  123.6 1.4 %two_blocks.15.refs_3_.refs_2_ = f32[1024,128]{1,0:T(8,128)S(1)} custom-call(bf16[8192,1024]{1,0:T(8,128)(2,1)S(1)} %get-tuple-element.45.refs_2_.refs_0_, f32[1024,128]{1,0:T(8,128)S(1)} %pick.11.refs_1_.refs_6_, f32[512,128]{1,0:T(8,128)S(1)} %collective-permute-done.41.refs_2_, f32[512,128]{1,0:T(8,128)S(1)} %collective-permute-done.42.refs_3_, ...), custom_call_target="tpu_custom_call" | custom-call | flops 1024 | bytes 1024 | tf_op jit(solution)/shard_map/two_blocks/pallas_call | solution.py:39
  125.1 0.6 collective-permute-done.40.refs_0_
  125.8 5.7 %collective-permute-done.39.refs_0_ = f32[1024,128]{1,0:T(8,128)S(1)} collective-permute-done((f32[1024,128]{1,0:T(8,128)S(1)}, f32[1024,128]{1,0:T(8,128)S(1)}, u32[]{:S(2)}, u32[]{:S(2)}) %collective-permute-start.39) | collective-permute-done | bytes 524320 | tf_op jit(solution)/shard_map/ppermute | solution.py:466
  131.5 1.0 last_sum.1
  (96 shorter events, 5.2 us)
Async XLA Ops:
  0.6 8.4 %copy-start = (f32[1024,256]{1,0:T(8,128)S(1)}, f32[1024,256]{1,0:T(8,128)}, u32[]{:S(2)}) copy-start(f32[1024,256]{1,0:T(8,128)} %refs_0_.9) | copy-start | bytes 3145732
  2.6 15.2 %collective-permute-start = (f32[1040,128]{1,0:T(8,128)}, f32[1040,128]{1,0:T(8,128)S(1)}, u32[]{:S(2)}, u32[]{:S(2)}) collective-permute-start(f32[1040,128]{1,0:T(8,128)} %get-tuple-element.41.refs_1_), channel_id=1, source_target_pairs={{1,3},{2,4},{5,7},{3,1},{4,2},{7,5},{9,11},{10,12},{13,15},{11,9},... | collective-permute-start | bytes 1597448 | tf_op jit(solution)/shard_map/ppermute | solution.py:466
  4.7 15.0 %collective-permute-start.2 = (f32[1040,128]{1,0:T(8,128)}, f32[1040,128]{1,0:T(8,128)S(1)}, u32[]{:S(2)}, u32[]{:S(2)}) collective-permute-start(f32[1040,128]{1,0:T(8,128)} %get-tuple-element.41.refs_1_), channel_id=1, source_target_pairs={{0,2},{3,5},{4,6},{2,0},{5,3},{6,4},{8,10},{11,13},{12,14},{10,8},... | collective-permute-start | bytes 1597448 | tf_op jit(solution)/shard_map/ppermute | solution.py:466
  9.1 0.7 copy-start.3
  9.7 10.0 %copy-start.2 = (f32[1040,128]{1,0:T(8,128)S(1)}, f32[1040,128]{1,0:T(8,128)}, u32[]{:S(2)}) copy-start(f32[1040,128]{1,0:T(8,128)} %get-tuple-element.41.refs_1_) | copy-start | bytes 1597444
  17.2 2.6 %collective-permute-start.1 = (f32[1024,128]{1,0:T(8,128)S(1)}, f32[1024,128]{1,0:T(8,128)S(1)}, u32[]{:S(2)}, u32[]{:S(2)}) collective-permute-start(f32[1024,128]{1,0:T(8,128)S(1)} %get-tuple-element.44), channel_id=1, source_target_pairs={{0,1},{1,0},{2,3},{3,2},{4,5},{5,4},{6,7},{7,6},{8,9},{9,8},{10,11... | collective-permute-start | bytes 1572872 | tf_op jit(solution)/shard_map/ppermute | solution.py:463
  17.3 5.0 %collective-permute-start.4 = (f32[1024,128]{1,0:T(8,128)S(1)}, f32[1024,128]{1,0:T(8,128)S(1)}, u32[]{:S(2)}, u32[]{:S(2)}) collective-permute-start(f32[1024,128]{1,0:T(8,128)S(1)} %get-tuple-element.47), channel_id=1, source_target_pairs={{0,1},{1,0},{2,3},{3,2},{4,5},{5,4},{6,7},{7,6},{8,9},{9,8},{10,11... | collective-permute-start | bytes 1572872 | tf_op jit(solution)/shard_map/ppermute | solution.py:463
  17.7 8.3 %collective-permute-start.6 = (f32[1024,128]{1,0:T(8,128)S(1)}, f32[1024,128]{1,0:T(8,128)S(1)}, u32[]{:S(2)}, u32[]{:S(2)}) collective-permute-start(f32[1024,128]{1,0:T(8,128)S(1)} %get-tuple-element.51), channel_id=1, source_target_pairs={{0,1},{1,0},{2,3},{3,2},{4,5},{5,4},{6,7},{7,6},{8,9},{9,8},{10,11... | collective-permute-start | bytes 1572872 | tf_op jit(solution)/shard_map/ppermute | solution.py:463
  17.8 8.3 %collective-permute-start.5 = (f32[1024,128]{1,0:T(8,128)S(1)}, f32[1024,128]{1,0:T(8,128)S(1)}, u32[]{:S(2)}, u32[]{:S(2)}) collective-permute-start(f32[1024,128]{1,0:T(8,128)S(1)} %get-tuple-element.49), channel_id=1, source_target_pairs={{0,1},{1,0},{2,3},{3,2},{4,5},{5,4},{6,7},{7,6},{8,9},{9,8},{10,11... | collective-permute-start | bytes 1572872 | tf_op jit(solution)/shard_map/ppermute | solution.py:463
  19.7 10.2 %collective-permute-start.10 = (f32[1040,128]{1,0:T(8,128)S(1)}, f32[1040,128]{1,0:T(8,128)S(1)}, u32[]{:S(2)}, u32[]{:S(2)}) collective-permute-start(f32[1040,128]{1,0:T(8,128)S(1)} %copy-done.2), channel_id=1, source_target_pairs={{0,1},{1,0},{2,3},{3,2},{4,5},{5,4},{6,7},{7,6},{8,9},{9,8},{10,11... | collective-permute-start | bytes 1597448 | tf_op jit(solution)/shard_map/ppermute | solution.py:463
  19.9 12.0 %collective-permute-start.9 = (f32[1040,128]{1,0:T(8,128)S(1)}, f32[1040,128]{1,0:T(8,128)S(1)}, u32[]{:S(2)}, u32[]{:S(2)}) collective-permute-start(f32[1040,128]{1,0:T(8,128)S(1)} %payload.12.refs_2_), channel_id=1, source_target_pairs={{1,3},{2,4},{5,7},{3,1},{4,2},{7,5},{9,11},{10,12},{13,15},{11,9},... | collective-permute-start | bytes 1597448 | tf_op jit(solution)/shard_map/ppermute | solution.py:466
  22.3 14.3 %collective-permute-start.3 = (f32[1040,128]{1,0:T(8,128)S(1)}, f32[1040,128]{1,0:T(8,128)S(1)}, u32[]{:S(2)}, u32[]{:S(2)}) collective-permute-start(f32[1040,128]{1,0:T(8,128)S(1)} %payload.13.refs_2_), channel_id=1, source_target_pairs={{0,2},{3,5},{4,6},{2,0},{5,3},{6,4},{8,10},{11,13},{12,14},{10,8},... | collective-permute-start | bytes 1597448 | tf_op jit(solution)/shard_map/ppermute | solution.py:466
  26.5 9.2 %collective-permute-start.7 = (f32[32,1024]{1,0:T(8,128)S(1)}, f32[32,1024]{1,0:T(8,128)S(1)}, u32[]{:S(2)}, u32[]{:S(2)}) collective-permute-start(f32[32,1024]{1,0:T(8,128)S(1)} %get-tuple-element.54), channel_id=1, source_target_pairs={{0,8},{16,24},{8,0},{24,16},{1,9},{17,25},{9,1},{25,17},{2,10},{18... | collective-permute-start | bytes 393224 | tf_op jit(solution)/shard_map/ppermute | solution.py:377
  27.8 7.9 %collective-permute-start.8 = (f32[32,1024]{1,0:T(8,128)S(1)}, f32[32,1024]{1,0:T(8,128)S(1)}, u32[]{:S(2)}, u32[]{:S(2)}) collective-permute-start(f32[32,1024]{1,0:T(8,128)S(1)} %get-tuple-element.55.refs_3_), channel_id=1, source_target_pairs={{8,16},{16,8},{9,17},{17,9},{10,18},{18,10},{11,19},{19,11},{12,20... | collective-permute-start | bytes 393224 | tf_op jit(solution)/shard_map/ppermute | solution.py:377
  29.9 11.5 %collective-permute-start.13 = (f32[1040,128]{1,0:T(8,128)S(1)}, f32[1040,128]{1,0:T(8,128)S(1)}, u32[]{:S(2)}, u32[]{:S(2)}) collective-permute-start(f32[1040,128]{1,0:T(8,128)S(1)} %pick.6.refs_2_.refs_1_), channel_id=1, source_target_pairs={{0,1},{1,0},{2,3},{3,2},{4,5},{5,4},{6,7},{7,6},{8,9},{9,8},{10,11... | collective-permute-start | bytes 1597448 | tf_op jit(solution)/shard_map/ppermute | solution.py:463
  32.0 12.8 %collective-permute-start.12 = (f32[1040,128]{1,0:T(8,128)S(1)}, f32[1040,128]{1,0:T(8,128)S(1)}, u32[]{:S(2)}, u32[]{:S(2)}) collective-permute-start(f32[1040,128]{1,0:T(8,128)S(1)} %payload.14.refs_2_), channel_id=1, source_target_pairs={{0,2},{3,5},{4,6},{2,0},{5,3},{6,4},{8,10},{11,13},{12,14},{10,8},... | collective-permute-start | bytes 1597448 | tf_op jit(solution)/shard_map/ppermute | solution.py:466
  35.9 2.7 %copy-start.5 = (f32[2,1024]{1,0:T(2,128)S(1)}, f32[2,1024]{1,0:T(2,128)}, u32[]{:S(2)}) copy-start(f32[2,1024]{1,0:T(2,128)} %refs_1_.2) | copy-start | bytes 24580
  35.9 2.7 %copy-start.6 = (f32[1024]{0:T(1024)S(1)}, f32[1024]{0:T(1024)}, u32[]{:S(2)}) copy-start(f32[1024]{0:T(1024)} %param.9) | copy-start | bytes 12292
  36.6 15.1 %collective-permute-start.11 = (f32[1040,128]{1,0:T(8,128)S(1)}, f32[1040,128]{1,0:T(8,128)S(1)}, u32[]{:S(2)}, u32[]{:S(2)}) collective-permute-start(f32[1040,128]{1,0:T(8,128)S(1)} %payload.15.refs_3_), channel_id=1, source_target_pairs={{1,3},{2,4},{5,7},{3,1},{4,2},{7,5},{9,11},{10,12},{13,15},{11,9},... | collective-permute-start | bytes 1597448 | tf_op jit(solution)/shard_map/ppermute | solution.py:466
  38.7 18.8 %collective-permute-start.18 = (f32[1040,128]{1,0:T(8,128)S(1)}, f32[1040,128]{1,0:T(8,128)S(1)}, u32[]{:S(2)}, u32[]{:S(2)}) collective-permute-start(f32[1040,128]{1,0:T(8,128)S(1)} %pick.7.refs_4_.refs_1_), channel_id=1, source_target_pairs={{0,1},{1,0},{2,3},{3,2},{4,5},{5,4},{6,7},{7,6},{8,9},{9,8},{10,11... | collective-permute-start | bytes 1597448 | tf_op jit(solution)/shard_map/ppermute | solution.py:463
  41.4 1.4 %copy-start.1 = (bf16[640,1024]{1,0:T(8,128)(2,1)S(1)}, bf16[640,1024]{1,0:T(8,128)(2,1)}, u32[]{:S(2)}) copy-start(bf16[640,1024]{1,0:T(8,128)(2,1)} %constant.4.clone.refs_2_.refs_4_) | copy-start | bytes 3932164
  41.4 1.4 %copy-start.4 = (s32[256]{0:T(256)S(1)}, s32[256]{0:T(256)}, u32[]{:S(2)}) copy-start(s32[256]{0:T(256)} %param.10) | copy-start | bytes 3076
  44.9 17.3 %collective-permute-start.15 = (f32[1040,128]{1,0:T(8,128)S(1)}, f32[1040,128]{1,0:T(8,128)S(1)}, u32[]{:S(2)}, u32[]{:S(2)}) collective-permute-start(f32[1040,128]{1,0:T(8,128)S(1)} %payload.16.refs_3_), channel_id=1, source_target_pairs={{1,3},{2,4},{5,7},{3,1},{4,2},{7,5},{9,11},{10,12},{13,15},{11,9},... | collective-permute-start | bytes 1597448 | tf_op jit(solution)/shard_map/ppermute | solution.py:466
  51.8 15.6 %collective-permute-start.14 = (f32[1040,128]{1,0:T(8,128)S(1)}, f32[1040,128]{1,0:T(8,128)S(1)}, u32[]{:S(2)}, u32[]{:S(2)}) collective-permute-start(f32[1040,128]{1,0:T(8,128)S(1)} %payload.17.refs_4_), channel_id=1, source_target_pairs={{0,2},{3,5},{4,6},{2,0},{5,3},{6,4},{8,10},{11,13},{12,14},{10,8},... | collective-permute-start | bytes 1597448 | tf_op jit(solution)/shard_map/ppermute | solution.py:466
  55.1 3.8 %collective-permute-start.16 = (f32[520,128]{1,0:T(8,128)S(1)}, f32[520,128]{1,0:T(8,128)S(1)}, u32[]{:S(2)}, u32[]{:S(2)}) collective-permute-start(f32[520,128]{1,0:T(8,128)S(1)} %get-tuple-element.81), channel_id=1, source_target_pairs={{0,1},{1,0},{2,3},{3,2},{4,5},{5,4},{6,7},{7,6},{8,9},{9,8},{10,11... | collective-permute-start | bytes 798728 | tf_op jit(solution)/shard_map/ppermute | solution.py:463
  57.4 1.5 %collective-permute-start.17 = (f32[520,128]{1,0:T(8,128)S(1)}, f32[520,128]{1,0:T(8,128)S(1)}, u32[]{:S(2)}, u32[]{:S(2)}) collective-permute-start(f32[520,128]{1,0:T(8,128)S(1)} %get-tuple-element.80), channel_id=1, source_target_pairs={{0,1},{1,0},{2,3},{3,2},{4,5},{5,4},{6,7},{7,6},{8,9},{9,8},{10,11... | collective-permute-start | bytes 798728 | tf_op jit(solution)/shard_map/ppermute | solution.py:463
  61.8 13.3 %collective-permute-start.20 = (f32[1024,128]{1,0:T(8,128)S(1)}, f32[1024,128]{1,0:T(8,128)S(1)}, u32[]{:S(2)}, u32[]{:S(2)}) collective-permute-start(f32[1024,128]{1,0:T(8,128)S(1)} %get-tuple-element.60.refs_3_), channel_id=1, source_target_pairs={{0,1},{1,0},{2,3},{3,2},{4,5},{5,4},{6,7},{7,6},{8,9},{9,8},{10,11... | collective-permute-start | bytes 1572872 | tf_op jit(solution)/shard_map/ppermute | solution.py:463
  67.6 12.4 %collective-permute-start.23 = (f32[1024,128]{1,0:T(8,128)S(1)}, f32[1024,128]{1,0:T(8,128)S(1)}, u32[]{:S(2)}, u32[]{:S(2)}) collective-permute-start(f32[1024,128]{1,0:T(8,128)S(1)} %get-tuple-element.61.refs_2_.refs_1_), channel_id=1, source_target_pairs={{0,2},{3,5},{4,6},{2,0},{5,3},{6,4},{8,10},{11,13},{12,14},{10,8},... | collective-permute-start | bytes 1572872 | tf_op jit(solution)/shard_map/ppermute | solution.py:466
  70.8 14.0 %collective-permute-start.19 = (f32[1024,128]{1,0:T(8,128)S(1)}, f32[1024,128]{1,0:T(8,128)S(1)}, u32[]{:S(2)}, u32[]{:S(2)}) collective-permute-start(f32[1024,128]{1,0:T(8,128)S(1)} %get-tuple-element.61.refs_2_.refs_1_), channel_id=1, source_target_pairs={{1,3},{2,4},{5,7},{3,1},{4,2},{7,5},{9,11},{10,12},{13,15},{11,9},... | collective-permute-start | bytes 1572872 | tf_op jit(solution)/shard_map/ppermute | solution.py:466
  74.0 13.6 %collective-permute-start.25 = (f32[1024,128]{1,0:T(8,128)S(1)}, f32[1024,128]{1,0:T(8,128)S(1)}, u32[]{:S(2)}, u32[]{:S(2)}) collective-permute-start(f32[1024,128]{1,0:T(8,128)S(1)} %get-tuple-element.64.refs_2_), channel_id=1, source_target_pairs={{0,1},{1,0},{2,3},{3,2},{4,5},{5,4},{6,7},{7,6},{8,9},{9,8},{10,11... | collective-permute-start | bytes 1572872 | tf_op jit(solution)/shard_map/ppermute | solution.py:463
  75.2 6.7 %collective-permute-start.21 = (f32[32,1024]{1,0:T(8,128)S(1)}, f32[32,1024]{1,0:T(8,128)S(1)}, u32[]{:S(2)}, u32[]{:S(2)}) collective-permute-start(f32[32,1024]{1,0:T(8,128)S(1)} %get-tuple-element.66), channel_id=1, source_target_pairs={{0,8},{16,24},{8,0},{24,16},{1,9},{17,25},{9,1},{25,17},{2,10},{18... | collective-permute-start | bytes 393224 | tf_op jit(solution)/shard_map/ppermute | solution.py:377
  76.5 7.6 %collective-permute-start.22 = (f32[32,1024]{1,0:T(8,128)S(1)}, f32[32,1024]{1,0:T(8,128)S(1)}, u32[]{:S(2)}, u32[]{:S(2)}) collective-permute-start(f32[32,1024]{1,0:T(8,128)S(1)} %get-tuple-element.67.refs_2_), channel_id=1, source_target_pairs={{8,16},{16,8},{9,17},{17,9},{10,18},{18,10},{11,19},{19,11},{12,20... | collective-permute-start | bytes 393224 | tf_op jit(solution)/shard_map/ppermute | solution.py:377
  80.0 17.1 %collective-permute-start.27 = (f32[1024,128]{1,0:T(8,128)S(1)}, f32[1024,128]{1,0:T(8,128)S(1)}, u32[]{:S(2)}, u32[]{:S(2)}) collective-permute-start(f32[1024,128]{1,0:T(8,128)S(1)} %payload.18.refs_2_), channel_id=1, source_target_pairs={{1,3},{2,4},{5,7},{3,1},{4,2},{7,5},{9,11},{10,12},{13,15},{11,9},... | collective-permute-start | bytes 1572872 | tf_op jit(solution)/shard_map/ppermute | solution.py:466
  84.8 15.3 %collective-permute-start.24 = (f32[1024,128]{1,0:T(8,128)S(1)}, f32[1024,128]{1,0:T(8,128)S(1)}, u32[]{:S(2)}, u32[]{:S(2)}) collective-permute-start(f32[1024,128]{1,0:T(8,128)S(1)} %payload.19.refs_2_), channel_id=1, source_target_pairs={{0,2},{3,5},{4,6},{2,0},{5,3},{6,4},{8,10},{11,13},{12,14},{10,8},... | collective-permute-start | bytes 1572872 | tf_op jit(solution)/shard_map/ppermute | solution.py:466
  89.0 15.0 %collective-permute-start.29 = (f32[1024,128]{1,0:T(8,128)S(1)}, f32[1024,128]{1,0:T(8,128)S(1)}, u32[]{:S(2)}, u32[]{:S(2)}) collective-permute-start(f32[1024,128]{1,0:T(8,128)S(1)} %get-tuple-element.69.refs_2_), channel_id=1, source_target_pairs={{0,1},{1,0},{2,3},{3,2},{4,5},{5,4},{6,7},{7,6},{8,9},{9,8},{10,11... | collective-permute-start | bytes 1572872 | tf_op jit(solution)/shard_map/ppermute | solution.py:463
  92.7 13.4 %collective-permute-start.34 = (f32[1024,128]{1,0:T(8,128)S(1)}, f32[1024,128]{1,0:T(8,128)S(1)}, u32[]{:S(2)}, u32[]{:S(2)}) collective-permute-start(f32[1024,128]{1,0:T(8,128)S(1)} %get-tuple-element.70.refs_8_), channel_id=1, source_target_pairs={{0,1},{1,0},{2,3},{3,2},{4,5},{5,4},{6,7},{7,6},{8,9},{9,8},{10,11... | collective-permute-start | bytes 1572872 | tf_op jit(solution)/shard_map/ppermute | solution.py:463
  95.4 1.4 %collective-permute-start.26 = (f32[2,256]{1,0:T(2,128)S(1)}, f32[2,256]{1,0:T(2,128)S(1)}, u32[]{:S(2)}, u32[]{:S(2)}) collective-permute-start(f32[2,256]{1,0:T(2,128)S(1)} %get-tuple-element.71.refs_3_.refs_0_), channel_id=1, source_target_pairs={{0,1},{1,0},{2,3},{3,2},{4,5},{5,4},{6,7},{7,6},{8,9},{9,8},{10,11... | collective-permute-start | bytes 6152 | tf_op jit(solution)/shard_map/ppermute | solution.py:653
  96.8 9.9 %collective-permute-start.38 = (f32[1024,128]{1,0:T(8,128)S(1)}, f32[1024,128]{1,0:T(8,128)S(1)}, u32[]{:S(2)}, u32[]{:S(2)}) collective-permute-start(f32[1024,128]{1,0:T(8,128)S(1)} %get-tuple-element.61.refs_2_.refs_1_), channel_id=1, source_target_pairs={{0,1},{1,0},{2,3},{3,2},{4,5},{5,4},{6,7},{7,6},{8,9},{9,8},{10,11... | collective-permute-start | bytes 1572872 | tf_op jit(solution)/shard_map/ppermute | solution.py:463
  97.2 9.8 %collective-permute-start.37 = (f32[1024,128]{1,0:T(8,128)S(1)}, f32[1024,128]{1,0:T(8,128)S(1)}, u32[]{:S(2)}, u32[]{:S(2)}) collective-permute-start(f32[1024,128]{1,0:T(8,128)S(1)} %pick.9.refs_2_.refs_1_), channel_id=1, source_target_pairs={{0,1},{1,0},{2,3},{3,2},{4,5},{5,4},{6,7},{7,6},{8,9},{9,8},{10,11... | collective-permute-start | bytes 1572872 | tf_op jit(solution)/shard_map/ppermute | solution.py:463
  100.1 14.6 %collective-permute-start.33 = (f32[1024,128]{1,0:T(8,128)S(1)}, f32[1024,128]{1,0:T(8,128)S(1)}, u32[]{:S(2)}, u32[]{:S(2)}) collective-permute-start(f32[1024,128]{1,0:T(8,128)S(1)} %payload.20.refs_2_), channel_id=1, source_target_pairs={{0,2},{3,5},{4,6},{2,0},{5,3},{6,4},{8,10},{11,13},{12,14},{10,8},... | collective-permute-start | bytes 1572872 | tf_op jit(solution)/shard_map/ppermute | solution.py:466
  104.0 14.7 %collective-permute-start.28 = (f32[1024,128]{1,0:T(8,128)S(1)}, f32[1024,128]{1,0:T(8,128)S(1)}, u32[]{:S(2)}, u32[]{:S(2)}) collective-permute-start(f32[1024,128]{1,0:T(8,128)S(1)} %payload.21.refs_2_), channel_id=1, source_target_pairs={{1,3},{2,4},{5,7},{3,1},{4,2},{7,5},{9,11},{10,12},{13,15},{11,9},... | collective-permute-start | bytes 1572872 | tf_op jit(solution)/shard_map/ppermute | solution.py:466
  106.4 2.1 %collective-permute-start.35 = (f32[512,128]{1,0:T(8,128)S(1)}, f32[512,128]{1,0:T(8,128)S(1)}, u32[]{:S(2)}, u32[]{:S(2)}) collective-permute-start(f32[512,128]{1,0:T(8,128)S(1)} %get-tuple-element.85), channel_id=1, source_target_pairs={{0,1},{1,0},{2,3},{3,2},{4,5},{5,4},{6,7},{7,6},{8,9},{9,8},{10,11... | collective-permute-start | bytes 786440 | tf_op jit(solution)/shard_map/ppermute | solution.py:463
  106.8 2.4 %collective-permute-start.36 = (f32[512,128]{1,0:T(8,128)S(1)}, f32[512,128]{1,0:T(8,128)S(1)}, u32[]{:S(2)}, u32[]{:S(2)}) collective-permute-start(f32[512,128]{1,0:T(8,128)S(1)} %get-tuple-element.84), channel_id=1, source_target_pairs={{0,1},{1,0},{2,3},{3,2},{4,5},{5,4},{6,7},{7,6},{8,9},{9,8},{10,11... | collective-permute-start | bytes 786440 | tf_op jit(solution)/shard_map/ppermute | solution.py:463
  107.0 11.0 %collective-permute-start.30 = (f32[2,256]{1,0:T(2,128)S(1)}, f32[2,256]{1,0:T(2,128)S(1)}, u32[]{:S(2)}, u32[]{:S(2)}) collective-permute-start(f32[2,256]{1,0:T(2,128)S(1)} %get-tuple-element.74.refs_0_), channel_id=1, source_target_pairs={{0,2},{1,3},{2,0},{3,1},{4,6},{5,7},{6,4},{7,5},{8,10},{9,11},{10,... | collective-permute-start | bytes 6152 | tf_op jit(solution)/shard_map/ppermute | solution.py:653
  108.5 9.6 %collective-permute-start.31 = (f32[2,256]{1,0:T(2,128)S(1)}, f32[2,256]{1,0:T(2,128)S(1)}, u32[]{:S(2)}, u32[]{:S(2)}) collective-permute-start(f32[2,256]{1,0:T(2,128)S(1)} %get-tuple-element.74.refs_0_), channel_id=1, source_target_pairs={{0,4},{1,5},{2,6},{3,7},{4,0},{5,1},{6,2},{7,3},{8,12},{9,13},{10,... | collective-permute-start | bytes 6152 | tf_op jit(solution)/shard_map/ppermute | solution.py:653
  109.2 8.9 %collective-permute-start.32 = (f32[2,256]{1,0:T(2,128)S(1)}, f32[2,256]{1,0:T(2,128)S(1)}, u32[]{:S(2)}, u32[]{:S(2)}) collective-permute-start(f32[2,256]{1,0:T(2,128)S(1)} %get-tuple-element.74.refs_0_), channel_id=1, source_target_pairs={{0,6},{1,7},{2,4},{3,5},{4,2},{5,3},{6,0},{7,1},{8,14},{9,15},{10,... | collective-permute-start | bytes 6152 | tf_op jit(solution)/shard_map/ppermute | solution.py:653
  114.8 10.9 %collective-permute-start.40 = (f32[1024,128]{1,0:T(8,128)S(1)}, f32[1024,128]{1,0:T(8,128)S(1)}, u32[]{:S(2)}, u32[]{:S(2)}) collective-permute-start(f32[1024,128]{1,0:T(8,128)S(1)} %payload.22.refs_4_), channel_id=1, source_target_pairs={{1,3},{2,4},{5,7},{3,1},{4,2},{7,5},{9,11},{10,12},{13,15},{11,9},... | collective-permute-start | bytes 1572872 | tf_op jit(solution)/shard_map/ppermute | solution.py:466
  118.7 12.7 %collective-permute-start.39 = (f32[1024,128]{1,0:T(8,128)S(1)}, f32[1024,128]{1,0:T(8,128)S(1)}, u32[]{:S(2)}, u32[]{:S(2)}) collective-permute-start(f32[1024,128]{1,0:T(8,128)S(1)} %payload.23.refs_4_), channel_id=1, source_target_pairs={{0,2},{3,5},{4,6},{2,0},{5,3},{6,4},{8,10},{11,13},{12,14},{10,8},... | collective-permute-start | bytes 1572872 | tf_op jit(solution)/shard_map/ppermute | solution.py:466
  121.0 2.3 %collective-permute-start.41 = (f32[512,128]{1,0:T(8,128)S(1)}, f32[512,128]{1,0:T(8,128)S(1)}, u32[]{:S(2)}, u32[]{:S(2)}) collective-permute-start(f32[512,128]{1,0:T(8,128)S(1)} %get-tuple-element.83), channel_id=1, source_target_pairs={{0,1},{1,0},{2,3},{3,2},{4,5},{5,4},{6,7},{7,6},{8,9},{9,8},{10,11... | collective-permute-start | bytes 786440 | tf_op jit(solution)/shard_map/ppermute | solution.py:463
  122.1 1.5 %collective-permute-start.42 = (f32[512,128]{1,0:T(8,128)S(1)}, f32[512,128]{1,0:T(8,128)S(1)}, u32[]{:S(2)}, u32[]{:S(2)}) collective-permute-start(f32[512,128]{1,0:T(8,128)S(1)} %get-tuple-element.82), channel_id=1, source_target_pairs={{0,1},{1,0},{2,3},{3,2},{4,5},{5,4},{6,7},{7,6},{8,9},{9,8},{10,11... | collective-permute-start | bytes 786440 | tf_op jit(solution)/shard_map/ppermute | solution.py:463

commit v10 on v9

--- a/solution.py
+++ b/solution.py
@@ -512,8 +512,14 @@
             (here,) = call(kernel, [arrays[0].shape], arrays)
             self.blocks.append((here, *exchange(here, parts)))
 
-        def multiply(self, slot, base=None):
-            first, last = slot == 0, base is not None
+        def hold(self, *slots):
+            for slot in slots:
+                here, there = self.blocks[slot]
+                (there,) = call(pass_on, [there.shape], [there])
+                self.blocks[slot] = (here, there)
+
+        def multiply(self, slot, base=None, first=None):
+            first, last = slot == 0 if first is None else first, base is not None
             blocks = self.blocks[slot]
             kernel = functools.partial(
                 two_blocks, plan.blocks[slot], len(blocks) - 1, first, last, self.scale, self.rows
@@ -618,12 +624,13 @@
         if step == 1:
             for slot in range(2, chips):
                 two.add_terms(mid_a)
-        if step == 2:
-            two.multiply(0)
         if 1 < step < chips - 1:
-            two.multiply(step - 1)
+            two.hold(*range(step) if step == 2 else (step - 1,))
         if step == chips - 2:
-            two.multiply(step)
+            two.multiply(step, first=True)
+        if step == chips - 1:
+            for slot in range(chips - 2):
+                two.multiply(slot, first=False)
         if step == 1:
             end_a, end_b, part_flux = call(
                 functools.partial(second_rest, 1.0 / math.sqrt(total_modes)),

time: 135 us -> 131 us (0.970)
  starting transfers between devices: 70.6 us -> 66.4 us
    ppermute x19, starting transfers between devices: 15.7 us -> 13.3 us  [exchange(): lax.ppermute(value[i:j], 'mode', across)]
    ppermute x4, waiting for transfers between devices: 2.11 us -> 0.43 us  [paired(): lax.ppermute(value, 'space', pairs + [(j, i) for i, j in pairs])]
    ppermute x4, waiting for transfers between devices: 0.83 us -> 2.47 us  [over(): lax.ppermute(self.value, 'mode', [(i, i ^ bit) for i in range(self.device...]
    ppermute x16, waiting for transfers between devices: 20.1 us -> 21.5 us  [along(): return lax.ppermute(value, 'mode', plan.pairs[stream])]
    pallas_call x53 -> x55, Pallas kernels: 34.9 us -> 35 us  [__call__(): pl.pallas_call(body, out_shape=[jax.ShapeDtypeStruct(shape, jnp.float32)...]
  transfers between devices with their start and end apart: 43 -> 43, of which waited for: 13 -> 14; matrix products, arithmetic and copies ran while one was open for 0% -> 0% of each run, Pallas kernels for 24% -> 25%
where the time goes in v10:
time: 131 us; the launch traced here: 130 us
  starting transfers between devices  66.4 us (51%)
  Pallas kernels  35 us (27%)
  waiting for transfers between devices  25.8 us (20%)
  between operations  1.57 us (1%)
    ppermute x16, starting transfers between devices, along(): return lax.ppermute(value, 'mode', plan.pairs[stream])  43.3 us
    pallas_call x55, Pallas kernels, __call__(): pl.pallas_call(body, out_shape=[jax.ShapeDtypeStruct(shape, jnp.float32)...  35 us
    ppermute x16, waiting for transfers between devices, along(): return lax.ppermute(value, 'mode', plan.pairs[stream])  21.5 us
    ppermute x19, starting transfers between devices, exchange(): lax.ppermute(value[i:j], 'mode', across)  13.3 us
    ppermute x4, starting transfers between devices, paired(): lax.ppermute(value, 'space', pairs + [(j, i) for i, j in pairs])  6.74 us
    ppermute x4, starting transfers between devices, over(): lax.ppermute(self.value, 'mode', [(i, i ^ bit) for i in range(self.device...  3.13 us
  transfers between devices with their start and end apart: 43, of which 14 were waited for; matrix products, arithmetic and copies ran while one was open for 0% of the time, Pallas kernels for 25%

profile of v10, /device:TPU:13, one launch (start us, length us, event | category | flops | bytes accessed | tf_op | source)
XLA Modules:
  0.0 129.8 jit_solution(10360087940402887988)
XLA Ops:
  0.6 2.0 %own_rows.1 = (f32[1040,128]{1,0:T(8,128)}, f32[8,128]{1,0:T(8,128)}) custom-call(f32[1024,256]{1,0:T(8,128)} %refs_0_.9, f32[2,1024]{1,0:T(2,128)} %refs_1_.2, f32[1,1024]{1,0:T(1,128)} %bitcast.4), custom_call_target="tpu_custom_call" | custom-call | flops 1024 | bytes 1024 | tf_op jit(solution)/shard_map/own_rows/pallas_call | solution.py:39
  2.6 3.2 %collective-permute-start.2 = (f32[1040,128]{1,0:T(8,128)}, f32[1040,128]{1,0:T(8,128)S(1)}, u32[]{:S(2)}, u32[]{:S(2)}) collective-permute-start(f32[1040,128]{1,0:T(8,128)} %get-tuple-element.41.refs_1_), channel_id=1, source_target_pairs={{0,2},{3,5},{4,6},{2,0},{5,3},{6,4},{8,10},{11,13},{12,14},{10,8},... | collective-permute-start | bytes 1597448 | tf_op jit(solution)/shard_map/ppermute | solution.py:466
  5.8 1.9 %collective-permute-start = (f32[1040,128]{1,0:T(8,128)}, f32[1040,128]{1,0:T(8,128)S(1)}, u32[]{:S(2)}, u32[]{:S(2)}) collective-permute-start(f32[1040,128]{1,0:T(8,128)} %get-tuple-element.41.refs_1_), channel_id=1, source_target_pairs={{1,3},{2,4},{5,7},{3,1},{4,2},{7,5},{9,11},{10,12},{13,15},{11,9},... | collective-permute-start | bytes 1597448 | tf_op jit(solution)/shard_map/ppermute | solution.py:466
  7.8 0.7 copy-done.3
  8.5 7.4 %load_and_products.1 = (f32[1024,128]{1,0:T(8,128)S(1)}, f32[1024,128]{1,0:T(8,128)S(1)}, f32[1024,128]{1,0:T(8,128)S(1)}, f32[1024,128]{1,0:T(8,128)S(1)}, f32[...) custom-call(bf16[8192,1024]{1,0:T(8,128)(2,1)} %refs_0_.6, ...), custom_call_target="tpu_custom_call" | custom-call | flops 1024 | bytes 1024 | tf_op jit(solution)/shard_map/load_and_products/pallas_call | solution.py:39
  15.9 2.6 %collective-permute-start.1 = (f32[1024,128]{1,0:T(8,128)S(1)}, f32[1024,128]{1,0:T(8,128)S(1)}, u32[]{:S(2)}, u32[]{:S(2)}) collective-permute-start(f32[1024,128]{1,0:T(8,128)S(1)} %get-tuple-element.44), channel_id=1, source_target_pairs={{0,1},{1,0},{2,3},{3,2},{4,5},{5,4},{6,7},{7,6},{8,9},{9,8},{10,11... | collective-permute-start | bytes 1572872 | tf_op jit(solution)/shard_map/ppermute | solution.py:463
  18.5 0.4 collective-permute-start.6
  19.1 0.6 collective-permute-done.refs_1_.refs_0_
  20.1 1.9 %collective-permute-start.9 = (f32[1040,128]{1,0:T(8,128)S(1)}, f32[1040,128]{1,0:T(8,128)S(1)}, u32[]{:S(2)}, u32[]{:S(2)}) collective-permute-start(f32[1040,128]{1,0:T(8,128)S(1)} %payload.12.refs_2_), channel_id=1, source_target_pairs={{1,3},{2,4},{5,7},{3,1},{4,2},{7,5},{9,11},{10,12},{13,15},{11,9},... | collective-permute-start | bytes 1597448 | tf_op jit(solution)/shard_map/ppermute | solution.py:466
  22.1 4.7 %collective-permute-start.3 = (f32[1040,128]{1,0:T(8,128)S(1)}, f32[1040,128]{1,0:T(8,128)S(1)}, u32[]{:S(2)}, u32[]{:S(2)}) collective-permute-start(f32[1040,128]{1,0:T(8,128)S(1)} %payload.13.refs_2_), channel_id=1, source_target_pairs={{0,2},{3,5},{4,6},{2,0},{5,3},{6,4},{8,10},{11,13},{12,14},{10,8},... | collective-permute-start | bytes 1597448 | tf_op jit(solution)/shard_map/ppermute | solution.py:466
  27.0 0.3 strip_rows.1
  27.4 1.3 collective-permute-start.7
  28.7 2.1 %collective-permute-start.8 = (f32[32,1024]{1,0:T(8,128)S(1)}, f32[32,1024]{1,0:T(8,128)S(1)}, u32[]{:S(2)}, u32[]{:S(2)}) collective-permute-start(f32[32,1024]{1,0:T(8,128)S(1)} %get-tuple-element.55.refs_3_), channel_id=1, source_target_pairs={{8,16},{16,8},{9,17},{17,9},{10,18},{18,10},{11,19},{19,11},{12,20... | collective-permute-start | bytes 393224 | tf_op jit(solution)/shard_map/ppermute | solution.py:377
  30.9 1.4 %two_blocks.8.refs_3_ = f32[272,1024]{1,0:T(8,128)S(1)} custom-call(bf16[8192,1024]{1,0:T(8,128)(2,1)S(1)} %get-tuple-element.45.refs_2_.refs_0_, f32[1040,128]{1,0:T(8,128)S(1)} %copy-done.2, f32[1040,128]{1,0:T(8,128)S(1)} %collective-permute-done.10.refs_2_, f32[32,1024]{1,0:T(8,128)S(1)} %get-tuple-element.55.refs_3_), custom_call_target="tpu_custom_call" | custom-call | flops 1024 | bytes 1024 | tf_op jit(solution)/shard_map/two_blocks/pallas_call | solution.py:39
  32.4 4.6 %collective-permute-start.12 = (f32[1040,128]{1,0:T(8,128)S(1)}, f32[1040,128]{1,0:T(8,128)S(1)}, u32[]{:S(2)}, u32[]{:S(2)}) collective-permute-start(f32[1040,128]{1,0:T(8,128)S(1)} %payload.14.refs_2_), channel_id=1, source_target_pairs={{0,2},{3,5},{4,6},{2,0},{5,3},{6,4},{8,10},{11,13},{12,14},{10,8},... | collective-permute-start | bytes 1597448 | tf_op jit(solution)/shard_map/ppermute | solution.py:466
  37.3 1.9 %collective-permute-start.11 = (f32[1040,128]{1,0:T(8,128)S(1)}, f32[1040,128]{1,0:T(8,128)S(1)}, u32[]{:S(2)}, u32[]{:S(2)}) collective-permute-start(f32[1040,128]{1,0:T(8,128)S(1)} %payload.15.refs_3_), channel_id=1, source_target_pairs={{1,3},{2,4},{5,7},{3,1},{4,2},{7,5},{9,11},{10,12},{13,15},{11,9},... | collective-permute-start | bytes 1597448 | tf_op jit(solution)/shard_map/ppermute | solution.py:466
  39.4 1.1 collective-permute-start.18
  40.5 1.4 %two_blocks.9.refs_5_.refs_3_ = f32[272,1024]{1,0:T(8,128)S(1)} custom-call(bf16[8192,1024]{1,0:T(8,128)(2,1)S(1)} %get-tuple-element.45.refs_2_.refs_0_, f32[1040,128]{1,0:T(8,128)S(1)} %pick.6.refs_2_.refs_1_, f32[1040,128]{1,0:T(8,128)S(1)} %collective-permute-done.13.refs_2_, f32[272,1024]{1,0:T(8,128)S(1)} %two_blocks.8.refs_3_, ...), custom_call_target="tpu_custom_call" | custom-call | flops 1024 | bytes 1024 | tf_op jit(solution)/shard_map/two_blocks/pallas_call | solution.py:39
  41.9 2.0 %first_rest.1 = (f32[1024,128]{1,0:T(8,128)S(1)}, f32[1024,128]{1,0:T(8,128)S(1)}) custom-call(f32[1024,256]{1,0:T(8,128)S(1)} %copy-done, bf16[1024,128]{1,0:T(8,128)(2,1)S(1)} %strip_columns.2.refs_3_.refs_1_, bf16[640,1024]{1,0:T(8,128)(2,1)S(1)} %copy-done.1, f32[8,1024]{1,0:T(8,128)S(1)} %maximum_maximum_fusion.refs_3_.refs_5_, s32[1,256]{1,0:T(1,128)S(1)} %bitcast.2, ...), custom_call_target="tpu_custom_call" | custom-call | flops 1024 | bytes 1024 | tf_op jit(solution)/shard_map/first_rest/pallas_call | solution.py:39
  43.9 1.5 %collective-permute-done.12.refs_0_.refs_1_ = f32[1040,128]{1,0:T(8,128)S(1)} collective-permute-done((f32[1040,128]{1,0:T(8,128)S(1)}, f32[1040,128]{1,0:T(8,128)S(1)}, u32[]{:S(2)}, u32[]{:S(2)}) %collective-permute-start.12) | collective-permute-done | bytes 532512 | tf_op jit(solution)/shard_map/ppermute | solution.py:466
  45.5 1.9 %collective-permute-start.15 = (f32[1040,128]{1,0:T(8,128)S(1)}, f32[1040,128]{1,0:T(8,128)S(1)}, u32[]{:S(2)}, u32[]{:S(2)}) collective-permute-start(f32[1040,128]{1,0:T(8,128)S(1)} %payload.16.refs_3_), channel_id=1, source_target_pairs={{1,3},{2,4},{5,7},{3,1},{4,2},{7,5},{9,11},{10,12},{13,15},{11,9},... | collective-permute-start | bytes 1597448 | tf_op jit(solution)/shard_map/ppermute | solution.py:466
  47.4 3.6 %collective-permute-done.11.refs_0_.refs_3_ = f32[1040,128]{1,0:T(8,128)S(1)} collective-permute-done((f32[1040,128]{1,0:T(8,128)S(1)}, f32[1040,128]{1,0:T(8,128)S(1)}, u32[]{:S(2)}, u32[]{:S(2)}) %collective-permute-start.11) | collective-permute-done | bytes 532512 | tf_op jit(solution)/shard_map/ppermute | solution.py:466
  51.1 2.8 %collective-permute-start.14 = (f32[1040,128]{1,0:T(8,128)S(1)}, f32[1040,128]{1,0:T(8,128)S(1)}, u32[]{:S(2)}, u32[]{:S(2)}) collective-permute-start(f32[1040,128]{1,0:T(8,128)S(1)} %payload.17.refs_4_), channel_id=1, source_target_pairs={{0,2},{3,5},{4,6},{2,0},{5,3},{6,4},{8,10},{11,13},{12,14},{10,8},... | collective-permute-start | bytes 1597448 | tf_op jit(solution)/shard_map/ppermute | solution.py:466
  54.2 1.3 %collective-permute-start.17 = (f32[520,128]{1,0:T(8,128)S(1)}, f32[520,128]{1,0:T(8,128)S(1)}, u32[]{:S(2)}, u32[]{:S(2)}) collective-permute-start(f32[520,128]{1,0:T(8,128)S(1)} %get-tuple-element.80), channel_id=1, source_target_pairs={{0,1},{1,0},{2,3},{3,2},{4,5},{5,4},{6,7},{7,6},{8,9},{9,8},{10,11... | collective-permute-start | bytes 798728 | tf_op jit(solution)/shard_map/ppermute | solution.py:463
  55.6 1.4 %two_blocks.10.refs_4_.refs_6_ = f32[272,1024]{1,0:T(8,128)S(1)} custom-call(bf16[8192,1024]{1,0:T(8,128)(2,1)S(1)} %get-tuple-element.45.refs_2_.refs_0_, f32[1040,128]{1,0:T(8,128)S(1)} %pick.7.refs_4_.refs_1_, f32[1040,128]{1,0:T(8,128)S(1)} %collective-permute-done.18.refs_2_, f32[272,1024]{1,0:T(8,128)S(1)} %two_blocks.9.refs_5_.refs_3_, ...), custom_call_target="tpu_custom_call" | custom-call | flops 1024 | bytes 1024 | tf_op jit(solution)/shard_map/two_blocks/pallas_call | solution.py:39
  57.1 1.5 %two_blocks.11 = (f32[1024,128]{1,0:T(8,128)S(1)}, f32[32,1024]{1,0:T(8,128)S(1)}, f32[8,1024]{1,0:T(8,128)S(1)}) custom-call(bf16[8192,1024]{1,0:T(8,128)(2,1)S(1)} %get-tuple-element.45.refs_2_.refs_0_, f32[1040,128]{1,0:T(8,128)S(1)} %pick.8.refs_4_.refs_1_, f32[520,128]{1,0:T(8,128)S(1)} %collective-permute-done.16.refs_2_, ...), custom_call_target="tpu_custom_call" | custom-call | flops 1024 | bytes 1024 | tf_op jit(solution)/shard_map/two_blocks/pallas_call | solution.py:39
  58.6 1.3 slot_products.4
  59.9 0.4 collective-permute-start.20
  60.4 5.5 %collective-permute-done.14.refs_0_ = f32[1040,128]{1,0:T(8,128)S(1)} collective-permute-done((f32[1040,128]{1,0:T(8,128)S(1)}, f32[1040,128]{1,0:T(8,128)S(1)}, u32[]{:S(2)}, u32[]{:S(2)}) %collective-permute-start.14) | collective-permute-done | bytes 532512 | tf_op jit(solution)/shard_map/ppermute | solution.py:466
  66.2 3.1 %collective-permute-start.23 = (f32[1024,128]{1,0:T(8,128)S(1)}, f32[1024,128]{1,0:T(8,128)S(1)}, u32[]{:S(2)}, u32[]{:S(2)}) collective-permute-start(f32[1024,128]{1,0:T(8,128)S(1)} %get-tuple-element.61.refs_2_.refs_1_), channel_id=1, source_target_pairs={{0,2},{3,5},{4,6},{2,0},{5,3},{6,4},{8,10},{11,13},{12,14},{10,8},... | collective-permute-start | bytes 1572872 | tf_op jit(solution)/shard_map/ppermute | solution.py:466
  69.3 1.9 %collective-permute-start.19 = (f32[1024,128]{1,0:T(8,128)S(1)}, f32[1024,128]{1,0:T(8,128)S(1)}, u32[]{:S(2)}, u32[]{:S(2)}) collective-permute-start(f32[1024,128]{1,0:T(8,128)S(1)} %get-tuple-element.61.refs_2_.refs_1_), channel_id=1, source_target_pairs={{1,3},{2,4},{5,7},{3,1},{4,2},{7,5},{9,11},{10,12},{13,15},{11,9},... | collective-permute-start | bytes 1572872 | tf_op jit(solution)/shard_map/ppermute | solution.py:466
  71.2 1.3 slot_products.5
  72.5 0.6 collective-permute-start.25
  73.2 1.3 collective-permute-start.21
  74.5 2.1 %collective-permute-start.22 = (f32[32,1024]{1,0:T(8,128)S(1)}, f32[32,1024]{1,0:T(8,128)S(1)}, u32[]{:S(2)}, u32[]{:S(2)}) collective-permute-start(f32[32,1024]{1,0:T(8,128)S(1)} %get-tuple-element.67.refs_2_), channel_id=1, source_target_pairs={{8,16},{16,8},{9,17},{17,9},{10,18},{18,10},{11,19},{19,11},{12,20... | collective-permute-start | bytes 393224 | tf_op jit(solution)/shard_map/ppermute | solution.py:377
  76.6 3.1 %collective-permute-done.23.refs_0_ = f32[1024,128]{1,0:T(8,128)S(1)} collective-permute-done((f32[1024,128]{1,0:T(8,128)S(1)}, f32[1024,128]{1,0:T(8,128)S(1)}, u32[]{:S(2)}, u32[]{:S(2)}) %collective-permute-start.23) | collective-permute-done | bytes 524320 | tf_op jit(solution)/shard_map/ppermute | solution.py:466
  79.7 1.9 %collective-permute-start.27 = (f32[1024,128]{1,0:T(8,128)S(1)}, f32[1024,128]{1,0:T(8,128)S(1)}, u32[]{:S(2)}, u32[]{:S(2)}) collective-permute-start(f32[1024,128]{1,0:T(8,128)S(1)} %payload.18.refs_2_), channel_id=1, source_target_pairs={{1,3},{2,4},{5,7},{3,1},{4,2},{7,5},{9,11},{10,12},{13,15},{11,9},... | collective-permute-start | bytes 1572872 | tf_op jit(solution)/shard_map/ppermute | solution.py:466
  81.6 0.4 collective-permute-done.22.refs_1_
  82.4 3.2 %collective-permute-start.24 = (f32[1024,128]{1,0:T(8,128)S(1)}, f32[1024,128]{1,0:T(8,128)S(1)}, u32[]{:S(2)}, u32[]{:S(2)}) collective-permute-start(f32[1024,128]{1,0:T(8,128)S(1)} %payload.19.refs_2_), channel_id=1, source_target_pairs={{0,2},{3,5},{4,6},{2,0},{5,3},{6,4},{8,10},{11,13},{12,14},{10,8},... | collective-permute-start | bytes 1572872 | tf_op jit(solution)/shard_map/ppermute | solution.py:466
  85.7 1.3 slot_products.6
  87.0 1.7 %collective-permute-start.29 = (f32[1024,128]{1,0:T(8,128)S(1)}, f32[1024,128]{1,0:T(8,128)S(1)}, u32[]{:S(2)}, u32[]{:S(2)}) collective-permute-start(f32[1024,128]{1,0:T(8,128)S(1)} %get-tuple-element.69.refs_2_), channel_id=1, source_target_pairs={{0,1},{1,0},{2,3},{3,2},{4,5},{5,4},{6,7},{7,6},{8,9},{9,8},{10,11... | collective-permute-start | bytes 1572872 | tf_op jit(solution)/shard_map/ppermute | solution.py:463
  88.6 1.2 slot_products.7
  90.0 2.7 %second_rest.1 = (f32[1024,128]{1,0:T(8,128)S(1)}, f32[1024,128]{1,0:T(8,128)S(1)}, f32[2,256]{1,0:T(2,128)S(1)}) custom-call(f32[1024,256]{1,0:T(8,128)S(1)} %copy-done, f32[1024,128]{1,0:T(8,128)S(1)} %get-tuple-element.58.refs_1_, f32[1024,128]{1,0:T(8,128)S(1)} %get-tuple-element.61.refs_2_.refs_1_, bf16[1024,128]{1,0:T(8,128)(2,1)S(1)} %strip_columns.3.refs_2_.refs_3_, ...), custom_call_target="tpu_custom_call" | custom-call | flops 1024 | bytes 1024 | tf_op jit(solution)/shard_map/second_rest/pallas_call | solution.py:39
  92.7 0.6 collective-permute-start.26
  93.2 0.8 collective-permute-done.26.refs_1_
  94.1 0.3 collective-permute-start.38
  94.4 2.6 %collective-permute-start.37 = (f32[1024,128]{1,0:T(8,128)S(1)}, f32[1024,128]{1,0:T(8,128)S(1)}, u32[]{:S(2)}, u32[]{:S(2)}) collective-permute-start(f32[1024,128]{1,0:T(8,128)S(1)} %pick.9.refs_2_.refs_1_), channel_id=1, source_target_pairs={{0,1},{1,0},{2,3},{3,2},{4,5},{5,4},{6,7},{7,6},{8,9},{9,8},{10,11... | collective-permute-start | bytes 1572872 | tf_op jit(solution)/shard_map/ppermute | solution.py:463
  97.1 4.1 %collective-permute-start.33 = (f32[1024,128]{1,0:T(8,128)S(1)}, f32[1024,128]{1,0:T(8,128)S(1)}, u32[]{:S(2)}, u32[]{:S(2)}) collective-permute-start(f32[1024,128]{1,0:T(8,128)S(1)} %payload.20.refs_2_), channel_id=1, source_target_pairs={{0,2},{3,5},{4,6},{2,0},{5,3},{6,4},{8,10},{11,13},{12,14},{10,8},... | collective-permute-start | bytes 1572872 | tf_op jit(solution)/shard_map/ppermute | solution.py:466
  101.3 1.9 %collective-permute-start.28 = (f32[1024,128]{1,0:T(8,128)S(1)}, f32[1024,128]{1,0:T(8,128)S(1)}, u32[]{:S(2)}, u32[]{:S(2)}) collective-permute-start(f32[1024,128]{1,0:T(8,128)S(1)} %payload.21.refs_2_), channel_id=1, source_target_pairs={{1,3},{2,4},{5,7},{3,1},{4,2},{7,5},{9,11},{10,12},{13,15},{11,9},... | collective-permute-start | bytes 1572872 | tf_op jit(solution)/shard_map/ppermute | solution.py:466
  103.5 0.3 collective-permute-start.36
  104.1 1.0 collective-permute-done.36.refs_3_
  105.1 2.5 %collective-permute-start.31 = (f32[2,256]{1,0:T(2,128)S(1)}, f32[2,256]{1,0:T(2,128)S(1)}, u32[]{:S(2)}, u32[]{:S(2)}) collective-permute-start(f32[2,256]{1,0:T(2,128)S(1)} %get-tuple-element.74.refs_0_), channel_id=1, source_target_pairs={{0,4},{1,5},{2,6},{3,7},{4,0},{5,1},{6,2},{7,3},{8,12},{9,13},{10,... | collective-permute-start | bytes 6152 | tf_op jit(solution)/shard_map/ppermute | solution.py:660
  107.7 1.3 %two_blocks.12.refs_3_ = f32[256,1024]{1,0:T(8,128)S(1)} custom-call(bf16[8192,1024]{1,0:T(8,128)(2,1)S(1)} %get-tuple-element.45.refs_2_.refs_0_, f32[1024,128]{1,0:T(8,128)S(1)} %pick.10.refs_1_, f32[512,128]{1,0:T(8,128)S(1)} %collective-permute-done.35.refs_2_, f32[512,128]{1,0:T(8,128)S(1)} %collective-permute-done.36.refs_3_, ...), custom_call_target="tpu_custom_call" | custom-call | flops 1024 | bytes 1024 | tf_op jit(solution)/shard_map/two_blocks/pallas_call | solution.py:39
  109.1 2.4 %collective-permute-done.33.refs_0_.refs_1_ = f32[1024,128]{1,0:T(8,128)S(1)} collective-permute-done((f32[1024,128]{1,0:T(8,128)S(1)}, f32[1024,128]{1,0:T(8,128)S(1)}, u32[]{:S(2)}, u32[]{:S(2)}) %collective-permute-start.33) | collective-permute-done | bytes 524320 | tf_op jit(solution)/shard_map/ppermute | solution.py:466
  111.5 1.9 %collective-permute-start.40 = (f32[1024,128]{1,0:T(8,128)S(1)}, f32[1024,128]{1,0:T(8,128)S(1)}, u32[]{:S(2)}, u32[]{:S(2)}) collective-permute-start(f32[1024,128]{1,0:T(8,128)S(1)} %payload.22.refs_4_), channel_id=1, source_target_pairs={{1,3},{2,4},{5,7},{3,1},{4,2},{7,5},{9,11},{10,12},{13,15},{11,9},... | collective-permute-start | bytes 1572872 | tf_op jit(solution)/shard_map/ppermute | solution.py:466
  113.4 1.6 %collective-permute-done.31.refs_2_ = f32[2,256]{1,0:T(2,128)S(1)} collective-permute-done((f32[2,256]{1,0:T(2,128)S(1)}, f32[2,256]{1,0:T(2,128)S(1)}, u32[]{:S(2)}, u32[]{:S(2)}) %collective-permute-start.31) | collective-permute-done | bytes 2080 | tf_op jit(solution)/shard_map/ppermute | solution.py:660
  115.1 0.6 add_all.3
  115.7 2.2 %collective-permute-start.39 = (f32[1024,128]{1,0:T(8,128)S(1)}, f32[1024,128]{1,0:T(8,128)S(1)}, u32[]{:S(2)}, u32[]{:S(2)}) collective-permute-start(f32[1024,128]{1,0:T(8,128)S(1)} %payload.23.refs_4_), channel_id=1, source_target_pairs={{0,2},{3,5},{4,6},{2,0},{5,3},{6,4},{8,10},{11,13},{12,14},{10,8},... | collective-permute-start | bytes 1572872 | tf_op jit(solution)/shard_map/ppermute | solution.py:466
  118.3 1.3 collective-permute-start.42
  119.6 1.3 %two_blocks.13.refs_3_.refs_4_ = f32[256,1024]{1,0:T(8,128)S(1)} custom-call(bf16[8192,1024]{1,0:T(8,128)(2,1)S(1)} %get-tuple-element.45.refs_2_.refs_0_, f32[1024,128]{1,0:T(8,128)S(1)} %get-tuple-element.61.refs_2_.refs_1_, f32[1024,128]{1,0:T(8,128)S(1)} %pass_on.2.refs_1_.refs_2_, f32[256,1024]{1,0:T(8,128)S(1)} %two_blocks.12.refs_3_, ...), custom_call_target="tpu_custom_call" | custom-call | flops 1024 | bytes 1024 | tf_op jit(solution)/shard_map/two_blocks/pallas_call | solution.py:39
  121.0 1.3 %two_blocks.14.refs_4_.refs_6_ = f32[256,1024]{1,0:T(8,128)S(1)} custom-call(bf16[8192,1024]{1,0:T(8,128)(2,1)S(1)} %get-tuple-element.45.refs_2_.refs_0_, f32[1024,128]{1,0:T(8,128)S(1)} %pick.9.refs_2_.refs_1_, f32[1024,128]{1,0:T(8,128)S(1)} %pass_on.3.refs_4_.refs_2_, f32[256,1024]{1,0:T(8,128)S(1)} %two_blocks.13.refs_3_.refs_4_, ...), custom_call_target="tpu_custom_call" | custom-call | flops 1024 | bytes 1024 | tf_op jit(solution)/shard_map/two_blocks/pallas_call | solution.py:39
  122.3 1.4 %two_blocks.15.refs_3_.refs_2_ = f32[1024,128]{1,0:T(8,128)S(1)} custom-call(bf16[8192,1024]{1,0:T(8,128)(2,1)S(1)} %get-tuple-element.45.refs_2_.refs_0_, f32[1024,128]{1,0:T(8,128)S(1)} %pick.11.refs_4_.refs_1_, f32[512,128]{1,0:T(8,128)S(1)} %collective-permute-done.41.refs_2_, f32[512,128]{1,0:T(8,128)S(1)} %collective-permute-done.42.refs_3_, ...), custom_call_target="tpu_custom_call" | custom-call | flops 1024 | bytes 1024 | tf_op jit(solution)/shard_map/two_blocks/pallas_call | solution.py:39
  123.9 4.7 %collective-permute-done.39.refs_0_ = f32[1024,128]{1,0:T(8,128)S(1)} collective-permute-done((f32[1024,128]{1,0:T(8,128)S(1)}, f32[1024,128]{1,0:T(8,128)S(1)}, u32[]{:S(2)}, u32[]{:S(2)}) %collective-permute-start.39) | collective-permute-done | bytes 524320 | tf_op jit(solution)/shard_map/ppermute | solution.py:466
  128.6 1.0 last_sum.1
  (98 shorter events, 4.5 us)
Async XLA Ops:
  0.6 7.1 %copy-start = (f32[1024,256]{1,0:T(8,128)S(1)}, f32[1024,256]{1,0:T(8,128)}, u32[]{:S(2)}) copy-start(f32[1024,256]{1,0:T(8,128)} %refs_0_.9) | copy-start | bytes 3145732
  2.6 16.3 %collective-permute-start.2 = (f32[1040,128]{1,0:T(8,128)}, f32[1040,128]{1,0:T(8,128)S(1)}, u32[]{:S(2)}, u32[]{:S(2)}) collective-permute-start(f32[1040,128]{1,0:T(8,128)} %get-tuple-element.41.refs_1_), channel_id=1, source_target_pairs={{0,2},{3,5},{4,6},{2,0},{5,3},{6,4},{8,10},{11,13},{12,14},{10,8},... | collective-permute-start | bytes 1597448 | tf_op jit(solution)/shard_map/ppermute | solution.py:466
  5.8 13.9 %collective-permute-start = (f32[1040,128]{1,0:T(8,128)}, f32[1040,128]{1,0:T(8,128)S(1)}, u32[]{:S(2)}, u32[]{:S(2)}) collective-permute-start(f32[1040,128]{1,0:T(8,128)} %get-tuple-element.41.refs_1_), channel_id=1, source_target_pairs={{1,3},{2,4},{5,7},{3,1},{4,2},{7,5},{9,11},{10,12},{13,15},{11,9},... | collective-permute-start | bytes 1597448 | tf_op jit(solution)/shard_map/ppermute | solution.py:466
  7.8 0.7 copy-start.3
  8.5 11.2 %copy-start.2 = (f32[1040,128]{1,0:T(8,128)S(1)}, f32[1040,128]{1,0:T(8,128)}, u32[]{:S(2)}) copy-start(f32[1040,128]{1,0:T(8,128)} %get-tuple-element.41.refs_1_) | copy-start | bytes 1597444
  15.9 4.1 %collective-permute-start.1 = (f32[1024,128]{1,0:T(8,128)S(1)}, f32[1024,128]{1,0:T(8,128)S(1)}, u32[]{:S(2)}, u32[]{:S(2)}) collective-permute-start(f32[1024,128]{1,0:T(8,128)S(1)} %get-tuple-element.44), channel_id=1, source_target_pairs={{0,1},{1,0},{2,3},{3,2},{4,5},{5,4},{6,7},{7,6},{8,9},{9,8},{10,11... | collective-permute-start | bytes 1572872 | tf_op jit(solution)/shard_map/ppermute | solution.py:463
  18.5 3.7 %collective-permute-start.4 = (f32[1024,128]{1,0:T(8,128)S(1)}, f32[1024,128]{1,0:T(8,128)S(1)}, u32[]{:S(2)}, u32[]{:S(2)}) collective-permute-start(f32[1024,128]{1,0:T(8,128)S(1)} %get-tuple-element.47), channel_id=1, source_target_pairs={{0,1},{1,0},{2,3},{3,2},{4,5},{5,4},{6,7},{7,6},{8,9},{9,8},{10,11... | collective-permute-start | bytes 1572872 | tf_op jit(solution)/shard_map/ppermute | solution.py:463
  18.5 8.3 %collective-permute-start.6 = (f32[1024,128]{1,0:T(8,128)S(1)}, f32[1024,128]{1,0:T(8,128)S(1)}, u32[]{:S(2)}, u32[]{:S(2)}) collective-permute-start(f32[1024,128]{1,0:T(8,128)S(1)} %get-tuple-element.51), channel_id=1, source_target_pairs={{0,1},{1,0},{2,3},{3,2},{4,5},{5,4},{6,7},{7,6},{8,9},{9,8},{10,11... | collective-permute-start | bytes 1572872 | tf_op jit(solution)/shard_map/ppermute | solution.py:463
  19.0 8.0 %collective-permute-start.5 = (f32[1024,128]{1,0:T(8,128)S(1)}, f32[1024,128]{1,0:T(8,128)S(1)}, u32[]{:S(2)}, u32[]{:S(2)}) collective-permute-start(f32[1024,128]{1,0:T(8,128)S(1)} %get-tuple-element.49), channel_id=1, source_target_pairs={{0,1},{1,0},{2,3},{3,2},{4,5},{5,4},{6,7},{7,6},{8,9},{9,8},{10,11... | collective-permute-start | bytes 1572872 | tf_op jit(solution)/shard_map/ppermute | solution.py:463
  19.7 11.1 %collective-permute-start.10 = (f32[1040,128]{1,0:T(8,128)S(1)}, f32[1040,128]{1,0:T(8,128)S(1)}, u32[]{:S(2)}, u32[]{:S(2)}) collective-permute-start(f32[1040,128]{1,0:T(8,128)S(1)} %copy-done.2), channel_id=1, source_target_pairs={{0,1},{1,0},{2,3},{3,2},{4,5},{5,4},{6,7},{7,6},{8,9},{9,8},{10,11... | collective-permute-start | bytes 1597448 | tf_op jit(solution)/shard_map/ppermute | solution.py:463
  20.1 12.2 %collective-permute-start.9 = (f32[1040,128]{1,0:T(8,128)S(1)}, f32[1040,128]{1,0:T(8,128)S(1)}, u32[]{:S(2)}, u32[]{:S(2)}) collective-permute-start(f32[1040,128]{1,0:T(8,128)S(1)} %payload.12.refs_2_), channel_id=1, source_target_pairs={{1,3},{2,4},{5,7},{3,1},{4,2},{7,5},{9,11},{10,12},{13,15},{11,9},... | collective-permute-start | bytes 1597448 | tf_op jit(solution)/shard_map/ppermute | solution.py:466
  22.1 15.1 %collective-permute-start.3 = (f32[1040,128]{1,0:T(8,128)S(1)}, f32[1040,128]{1,0:T(8,128)S(1)}, u32[]{:S(2)}, u32[]{:S(2)}) collective-permute-start(f32[1040,128]{1,0:T(8,128)S(1)} %payload.13.refs_2_), channel_id=1, source_target_pairs={{0,2},{3,5},{4,6},{2,0},{5,3},{6,4},{8,10},{11,13},{12,14},{10,8},... | collective-permute-start | bytes 1597448 | tf_op jit(solution)/shard_map/ppermute | solution.py:466
  27.4 9.6 %collective-permute-start.7 = (f32[32,1024]{1,0:T(8,128)S(1)}, f32[32,1024]{1,0:T(8,128)S(1)}, u32[]{:S(2)}, u32[]{:S(2)}) collective-permute-start(f32[32,1024]{1,0:T(8,128)S(1)} %get-tuple-element.54), channel_id=1, source_target_pairs={{0,8},{16,24},{8,0},{24,16},{1,9},{17,25},{9,1},{25,17},{2,10},{18... | collective-permute-start | bytes 393224 | tf_op jit(solution)/shard_map/ppermute | solution.py:377
  28.7 8.3 %collective-permute-start.8 = (f32[32,1024]{1,0:T(8,128)S(1)}, f32[32,1024]{1,0:T(8,128)S(1)}, u32[]{:S(2)}, u32[]{:S(2)}) collective-permute-start(f32[32,1024]{1,0:T(8,128)S(1)} %get-tuple-element.55.refs_3_), channel_id=1, source_target_pairs={{8,16},{16,8},{9,17},{17,9},{10,18},{18,10},{11,19},{19,11},{12,20... | collective-permute-start | bytes 393224 | tf_op jit(solution)/shard_map/ppermute | solution.py:377
  30.8 9.7 %collective-permute-start.13 = (f32[1040,128]{1,0:T(8,128)S(1)}, f32[1040,128]{1,0:T(8,128)S(1)}, u32[]{:S(2)}, u32[]{:S(2)}) collective-permute-start(f32[1040,128]{1,0:T(8,128)S(1)} %pick.6.refs_2_.refs_1_), channel_id=1, source_target_pairs={{0,1},{1,0},{2,3},{3,2},{4,5},{5,4},{6,7},{7,6},{8,9},{9,8},{10,11... | collective-permute-start | bytes 1597448 | tf_op jit(solution)/shard_map/ppermute | solution.py:463
  32.4 13.1 %collective-permute-start.12 = (f32[1040,128]{1,0:T(8,128)S(1)}, f32[1040,128]{1,0:T(8,128)S(1)}, u32[]{:S(2)}, u32[]{:S(2)}) collective-permute-start(f32[1040,128]{1,0:T(8,128)S(1)} %payload.14.refs_2_), channel_id=1, source_target_pairs={{0,2},{3,5},{4,6},{2,0},{5,3},{6,4},{8,10},{11,13},{12,14},{10,8},... | collective-permute-start | bytes 1597448 | tf_op jit(solution)/shard_map/ppermute | solution.py:466
  37.2 2.1 %copy-start.5 = (f32[2,1024]{1,0:T(2,128)S(1)}, f32[2,1024]{1,0:T(2,128)}, u32[]{:S(2)}) copy-start(f32[2,1024]{1,0:T(2,128)} %refs_1_.2) | copy-start | bytes 24580
  37.2 2.1 %copy-start.6 = (f32[1024]{0:T(1024)S(1)}, f32[1024]{0:T(1024)}, u32[]{:S(2)}) copy-start(f32[1024]{0:T(1024)} %param.9) | copy-start | bytes 12292
  37.3 13.8 %collective-permute-start.11 = (f32[1040,128]{1,0:T(8,128)S(1)}, f32[1040,128]{1,0:T(8,128)S(1)}, u32[]{:S(2)}, u32[]{:S(2)}) collective-permute-start(f32[1040,128]{1,0:T(8,128)S(1)} %payload.15.refs_3_), channel_id=1, source_target_pairs={{1,3},{2,4},{5,7},{3,1},{4,2},{7,5},{9,11},{10,12},{13,15},{11,9},... | collective-permute-start | bytes 1597448 | tf_op jit(solution)/shard_map/ppermute | solution.py:466
  39.4 16.3 %collective-permute-start.18 = (f32[1040,128]{1,0:T(8,128)S(1)}, f32[1040,128]{1,0:T(8,128)S(1)}, u32[]{:S(2)}, u32[]{:S(2)}) collective-permute-start(f32[1040,128]{1,0:T(8,128)S(1)} %pick.7.refs_4_.refs_1_), channel_id=1, source_target_pairs={{0,1},{1,0},{2,3},{3,2},{4,5},{5,4},{6,7},{7,6},{8,9},{9,8},{10,11... | collective-permute-start | bytes 1597448 | tf_op jit(solution)/shard_map/ppermute | solution.py:463
  40.5 1.4 %copy-start.1 = (bf16[640,1024]{1,0:T(8,128)(2,1)S(1)}, bf16[640,1024]{1,0:T(8,128)(2,1)}, u32[]{:S(2)}) copy-start(bf16[640,1024]{1,0:T(8,128)(2,1)} %constant.4.clone.refs_2_.refs_4_) | copy-start | bytes 3932164
  40.5 1.4 %copy-start.4 = (s32[256]{0:T(256)S(1)}, s32[256]{0:T(256)}, u32[]{:S(2)}) copy-start(s32[256]{0:T(256)} %param.10) | copy-start | bytes 3076
  45.5 14.8 %collective-permute-start.15 = (f32[1040,128]{1,0:T(8,128)S(1)}, f32[1040,128]{1,0:T(8,128)S(1)}, u32[]{:S(2)}, u32[]{:S(2)}) collective-permute-start(f32[1040,128]{1,0:T(8,128)S(1)} %payload.16.refs_3_), channel_id=1, source_target_pairs={{1,3},{2,4},{5,7},{3,1},{4,2},{7,5},{9,11},{10,12},{13,15},{11,9},... | collective-permute-start | bytes 1597448 | tf_op jit(solution)/shard_map/ppermute | solution.py:466
  51.1 14.8 %collective-permute-start.14 = (f32[1040,128]{1,0:T(8,128)S(1)}, f32[1040,128]{1,0:T(8,128)S(1)}, u32[]{:S(2)}, u32[]{:S(2)}) collective-permute-start(f32[1040,128]{1,0:T(8,128)S(1)} %payload.17.refs_4_), channel_id=1, source_target_pairs={{0,2},{3,5},{4,6},{2,0},{5,3},{6,4},{8,10},{11,13},{12,14},{10,8},... | collective-permute-start | bytes 1597448 | tf_op jit(solution)/shard_map/ppermute | solution.py:466
  54.2 2.8 %collective-permute-start.17 = (f32[520,128]{1,0:T(8,128)S(1)}, f32[520,128]{1,0:T(8,128)S(1)}, u32[]{:S(2)}, u32[]{:S(2)}) collective-permute-start(f32[520,128]{1,0:T(8,128)S(1)} %get-tuple-element.80), channel_id=1, source_target_pairs={{0,1},{1,0},{2,3},{3,2},{4,5},{5,4},{6,7},{7,6},{8,9},{9,8},{10,11... | collective-permute-start | bytes 798728 | tf_op jit(solution)/shard_map/ppermute | solution.py:463
  55.6 1.5 %collective-permute-start.16 = (f32[520,128]{1,0:T(8,128)S(1)}, f32[520,128]{1,0:T(8,128)S(1)}, u32[]{:S(2)}, u32[]{:S(2)}) collective-permute-start(f32[520,128]{1,0:T(8,128)S(1)} %get-tuple-element.81), channel_id=1, source_target_pairs={{0,1},{1,0},{2,3},{3,2},{4,5},{5,4},{6,7},{7,6},{8,9},{9,8},{10,11... | collective-permute-start | bytes 798728 | tf_op jit(solution)/shard_map/ppermute | solution.py:463
  59.9 13.2 %collective-permute-start.20 = (f32[1024,128]{1,0:T(8,128)S(1)}, f32[1024,128]{1,0:T(8,128)S(1)}, u32[]{:S(2)}, u32[]{:S(2)}) collective-permute-start(f32[1024,128]{1,0:T(8,128)S(1)} %get-tuple-element.60.refs_3_), channel_id=1, source_target_pairs={{0,1},{1,0},{2,3},{3,2},{4,5},{5,4},{6,7},{7,6},{8,9},{9,8},{10,11... | collective-permute-start | bytes 1572872 | tf_op jit(solution)/shard_map/ppermute | solution.py:463
  66.2 13.5 %collective-permute-start.23 = (f32[1024,128]{1,0:T(8,128)S(1)}, f32[1024,128]{1,0:T(8,128)S(1)}, u32[]{:S(2)}, u32[]{:S(2)}) collective-permute-start(f32[1024,128]{1,0:T(8,128)S(1)} %get-tuple-element.61.refs_2_.refs_1_), channel_id=1, source_target_pairs={{0,2},{3,5},{4,6},{2,0},{5,3},{6,4},{8,10},{11,13},{12,14},{10,8},... | collective-permute-start | bytes 1572872 | tf_op jit(solution)/shard_map/ppermute | solution.py:466
  69.3 13.1 %collective-permute-start.19 = (f32[1024,128]{1,0:T(8,128)S(1)}, f32[1024,128]{1,0:T(8,128)S(1)}, u32[]{:S(2)}, u32[]{:S(2)}) collective-permute-start(f32[1024,128]{1,0:T(8,128)S(1)} %get-tuple-element.61.refs_2_.refs_1_), channel_id=1, source_target_pairs={{1,3},{2,4},{5,7},{3,1},{4,2},{7,5},{9,11},{10,12},{13,15},{11,9},... | collective-permute-start | bytes 1572872 | tf_op jit(solution)/shard_map/ppermute | solution.py:466
  72.5 13.1 %collective-permute-start.25 = (f32[1024,128]{1,0:T(8,128)S(1)}, f32[1024,128]{1,0:T(8,128)S(1)}, u32[]{:S(2)}, u32[]{:S(2)}) collective-permute-start(f32[1024,128]{1,0:T(8,128)S(1)} %get-tuple-element.64.refs_2_), channel_id=1, source_target_pairs={{0,1},{1,0},{2,3},{3,2},{4,5},{5,4},{6,7},{7,6},{8,9},{9,8},{10,11... | collective-permute-start | bytes 1572872 | tf_op jit(solution)/shard_map/ppermute | solution.py:463
  73.2 8.4 %collective-permute-start.21 = (f32[32,1024]{1,0:T(8,128)S(1)}, f32[32,1024]{1,0:T(8,128)S(1)}, u32[]{:S(2)}, u32[]{:S(2)}) collective-permute-start(f32[32,1024]{1,0:T(8,128)S(1)} %get-tuple-element.66), channel_id=1, source_target_pairs={{0,8},{16,24},{8,0},{24,16},{1,9},{17,25},{9,1},{25,17},{2,10},{18... | collective-permute-start | bytes 393224 | tf_op jit(solution)/shard_map/ppermute | solution.py:377
  74.5 7.6 %collective-permute-start.22 = (f32[32,1024]{1,0:T(8,128)S(1)}, f32[32,1024]{1,0:T(8,128)S(1)}, u32[]{:S(2)}, u32[]{:S(2)}) collective-permute-start(f32[32,1024]{1,0:T(8,128)S(1)} %get-tuple-element.67.refs_2_), channel_id=1, source_target_pairs={{8,16},{16,8},{9,17},{17,9},{10,18},{18,10},{11,19},{19,11},{12,20... | collective-permute-start | bytes 393224 | tf_op jit(solution)/shard_map/ppermute | solution.py:377
  79.7 14.7 %collective-permute-start.27 = (f32[1024,128]{1,0:T(8,128)S(1)}, f32[1024,128]{1,0:T(8,128)S(1)}, u32[]{:S(2)}, u32[]{:S(2)}) collective-permute-start(f32[1024,128]{1,0:T(8,128)S(1)} %payload.18.refs_2_), channel_id=1, source_target_pairs={{1,3},{2,4},{5,7},{3,1},{4,2},{7,5},{9,11},{10,12},{13,15},{11,9},... | collective-permute-start | bytes 1572872 | tf_op jit(solution)/shard_map/ppermute | solution.py:466
  82.4 14.7 %collective-permute-start.24 = (f32[1024,128]{1,0:T(8,128)S(1)}, f32[1024,128]{1,0:T(8,128)S(1)}, u32[]{:S(2)}, u32[]{:S(2)}) collective-permute-start(f32[1024,128]{1,0:T(8,128)S(1)} %payload.19.refs_2_), channel_id=1, source_target_pairs={{0,2},{3,5},{4,6},{2,0},{5,3},{6,4},{8,10},{11,13},{12,14},{10,8},... | collective-permute-start | bytes 1572872 | tf_op jit(solution)/shard_map/ppermute | solution.py:466
  87.0 14.3 %collective-permute-start.29 = (f32[1024,128]{1,0:T(8,128)S(1)}, f32[1024,128]{1,0:T(8,128)S(1)}, u32[]{:S(2)}, u32[]{:S(2)}) collective-permute-start(f32[1024,128]{1,0:T(8,128)S(1)} %get-tuple-element.69.refs_2_), channel_id=1, source_target_pairs={{0,1},{1,0},{2,3},{3,2},{4,5},{5,4},{6,7},{7,6},{8,9},{9,8},{10,11... | collective-permute-start | bytes 1572872 | tf_op jit(solution)/shard_map/ppermute | solution.py:463
  89.9 13.4 %collective-permute-start.34 = (f32[1024,128]{1,0:T(8,128)S(1)}, f32[1024,128]{1,0:T(8,128)S(1)}, u32[]{:S(2)}, u32[]{:S(2)}) collective-permute-start(f32[1024,128]{1,0:T(8,128)S(1)} %get-tuple-element.70.refs_8_), channel_id=1, source_target_pairs={{0,1},{1,0},{2,3},{3,2},{4,5},{5,4},{6,7},{7,6},{8,9},{9,8},{10,11... | collective-permute-start | bytes 1572872 | tf_op jit(solution)/shard_map/ppermute | solution.py:463
  92.7 1.4 %collective-permute-start.26 = (f32[2,256]{1,0:T(2,128)S(1)}, f32[2,256]{1,0:T(2,128)S(1)}, u32[]{:S(2)}, u32[]{:S(2)}) collective-permute-start(f32[2,256]{1,0:T(2,128)S(1)} %get-tuple-element.71.refs_3_.refs_0_), channel_id=1, source_target_pairs={{0,1},{1,0},{2,3},{3,2},{4,5},{5,4},{6,7},{7,6},{8,9},{9,8},{10,11... | collective-permute-start | bytes 6152 | tf_op jit(solution)/shard_map/ppermute | solution.py:660
  94.1 9.8 %collective-permute-start.38 = (f32[1024,128]{1,0:T(8,128)S(1)}, f32[1024,128]{1,0:T(8,128)S(1)}, u32[]{:S(2)}, u32[]{:S(2)}) collective-permute-start(f32[1024,128]{1,0:T(8,128)S(1)} %get-tuple-element.61.refs_2_.refs_1_), channel_id=1, source_target_pairs={{0,1},{1,0},{2,3},{3,2},{4,5},{5,4},{6,7},{7,6},{8,9},{9,8},{10,11... | collective-permute-start | bytes 1572872 | tf_op jit(solution)/shard_map/ppermute | solution.py:463
  94.4 9.7 %collective-permute-start.37 = (f32[1024,128]{1,0:T(8,128)S(1)}, f32[1024,128]{1,0:T(8,128)S(1)}, u32[]{:S(2)}, u32[]{:S(2)}) collective-permute-start(f32[1024,128]{1,0:T(8,128)S(1)} %pick.9.refs_2_.refs_1_), channel_id=1, source_target_pairs={{0,1},{1,0},{2,3},{3,2},{4,5},{5,4},{6,7},{7,6},{8,9},{9,8},{10,11... | collective-permute-start | bytes 1572872 | tf_op jit(solution)/shard_map/ppermute | solution.py:463
  97.1 14.3 %collective-permute-start.33 = (f32[1024,128]{1,0:T(8,128)S(1)}, f32[1024,128]{1,0:T(8,128)S(1)}, u32[]{:S(2)}, u32[]{:S(2)}) collective-permute-start(f32[1024,128]{1,0:T(8,128)S(1)} %payload.20.refs_2_), channel_id=1, source_target_pairs={{0,2},{3,5},{4,6},{2,0},{5,3},{6,4},{8,10},{11,13},{12,14},{10,8},... | collective-permute-start | bytes 1572872 | tf_op jit(solution)/shard_map/ppermute | solution.py:466
  101.3 14.4 %collective-permute-start.28 = (f32[1024,128]{1,0:T(8,128)S(1)}, f32[1024,128]{1,0:T(8,128)S(1)}, u32[]{:S(2)}, u32[]{:S(2)}) collective-permute-start(f32[1024,128]{1,0:T(8,128)S(1)} %payload.21.refs_2_), channel_id=1, source_target_pairs={{1,3},{2,4},{5,7},{3,1},{4,2},{7,5},{9,11},{10,12},{13,15},{11,9},... | collective-permute-start | bytes 1572872 | tf_op jit(solution)/shard_map/ppermute | solution.py:466
  103.5 1.6 %collective-permute-start.36 = (f32[512,128]{1,0:T(8,128)S(1)}, f32[512,128]{1,0:T(8,128)S(1)}, u32[]{:S(2)}, u32[]{:S(2)}) collective-permute-start(f32[512,128]{1,0:T(8,128)S(1)} %get-tuple-element.84), channel_id=1, source_target_pairs={{0,1},{1,0},{2,3},{3,2},{4,5},{5,4},{6,7},{7,6},{8,9},{9,8},{10,11... | collective-permute-start | bytes 786440 | tf_op jit(solution)/shard_map/ppermute | solution.py:463
  103.8 3.8 %collective-permute-start.35 = (f32[512,128]{1,0:T(8,128)S(1)}, f32[512,128]{1,0:T(8,128)S(1)}, u32[]{:S(2)}, u32[]{:S(2)}) collective-permute-start(f32[512,128]{1,0:T(8,128)S(1)} %get-tuple-element.85), channel_id=1, source_target_pairs={{0,1},{1,0},{2,3},{3,2},{4,5},{5,4},{6,7},{7,6},{8,9},{9,8},{10,11... | collective-permute-start | bytes 786440 | tf_op jit(solution)/shard_map/ppermute | solution.py:463
  104.1 9.3 %collective-permute-start.32 = (f32[2,256]{1,0:T(2,128)S(1)}, f32[2,256]{1,0:T(2,128)S(1)}, u32[]{:S(2)}, u32[]{:S(2)}) collective-permute-start(f32[2,256]{1,0:T(2,128)S(1)} %get-tuple-element.74.refs_0_), channel_id=1, source_target_pairs={{0,6},{1,7},{2,4},{3,5},{4,2},{5,3},{6,0},{7,1},{8,14},{9,15},{10,... | collective-permute-start | bytes 6152 | tf_op jit(solution)/shard_map/ppermute | solution.py:660
  105.1 10.0 %collective-permute-start.31 = (f32[2,256]{1,0:T(2,128)S(1)}, f32[2,256]{1,0:T(2,128)S(1)}, u32[]{:S(2)}, u32[]{:S(2)}) collective-permute-start(f32[2,256]{1,0:T(2,128)S(1)} %get-tuple-element.74.refs_0_), channel_id=1, source_target_pairs={{0,4},{1,5},{2,6},{3,7},{4,0},{5,1},{6,2},{7,3},{8,12},{9,13},{10,... | collective-permute-start | bytes 6152 | tf_op jit(solution)/shard_map/ppermute | solution.py:660
  107.6 7.4 %collective-permute-start.30 = (f32[2,256]{1,0:T(2,128)S(1)}, f32[2,256]{1,0:T(2,128)S(1)}, u32[]{:S(2)}, u32[]{:S(2)}) collective-permute-start(f32[2,256]{1,0:T(2,128)S(1)} %get-tuple-element.74.refs_0_), channel_id=1, source_target_pairs={{0,2},{1,3},{2,0},{3,1},{4,6},{5,7},{6,4},{7,5},{8,10},{9,11},{10,... | collective-permute-start | bytes 6152 | tf_op jit(solution)/shard_map/ppermute | solution.py:660
  111.5 12.3 %collective-permute-start.40 = (f32[1024,128]{1,0:T(8,128)S(1)}, f32[1024,128]{1,0:T(8,128)S(1)}, u32[]{:S(2)}, u32[]{:S(2)}) collective-permute-start(f32[1024,128]{1,0:T(8,128)S(1)} %payload.22.refs_4_), channel_id=1, source_target_pairs={{1,3},{2,4},{5,7},{3,1},{4,2},{7,5},{9,11},{10,12},{13,15},{11,9},... | collective-permute-start | bytes 1572872 | tf_op jit(solution)/shard_map/ppermute | solution.py:466
  115.7 12.9 %collective-permute-start.39 = (f32[1024,128]{1,0:T(8,128)S(1)}, f32[1024,128]{1,0:T(8,128)S(1)}, u32[]{:S(2)}, u32[]{:S(2)}) collective-permute-start(f32[1024,128]{1,0:T(8,128)S(1)} %payload.23.refs_4_), channel_id=1, source_target_pairs={{0,2},{3,5},{4,6},{2,0},{5,3},{6,4},{8,10},{11,13},{12,14},{10,8},... | collective-permute-start | bytes 1572872 | tf_op jit(solution)/shard_map/ppermute | solution.py:466
  118.3 4.0 %collective-permute-start.42 = (f32[512,128]{1,0:T(8,128)S(1)}, f32[512,128]{1,0:T(8,128)S(1)}, u32[]{:S(2)}, u32[]{:S(2)}) collective-permute-start(f32[512,128]{1,0:T(8,128)S(1)} %get-tuple-element.82), channel_id=1, source_target_pairs={{0,1},{1,0},{2,3},{3,2},{4,5},{5,4},{6,7},{7,6},{8,9},{9,8},{10,11... | collective-permute-start | bytes 786440 | tf_op jit(solution)/shard_map/ppermute | solution.py:463
  119.6 2.8 %collective-permute-start.41 = (f32[512,128]{1,0:T(8,128)S(1)}, f32[512,128]{1,0:T(8,128)S(1)}, u32[]{:S(2)}, u32[]{:S(2)}) collective-permute-start(f32[512,128]{1,0:T(8,128)S(1)} %get-tuple-element.83), channel_id=1, source_target_pairs={{0,1},{1,0},{2,3},{3,2},{4,5},{5,4},{6,7},{7,6},{8,9},{9,8},{10,11... | collective-permute-start | bytes 786440 | tf_op jit(solution)/shard_map/ppermute | solution.py:463

commit v11 on v8

--- a/solution.py
+++ b/solution.py
@@ -114,24 +114,22 @@
         one_slot(pair, held, parts, outs[2 * slot], outs[2 * slot + 1])
 
 
-def two_blocks(numbers, parts, first, last, scale, rows, matrix, *refs):
-    modes = matrix.shape[1]
-    blocks, refs = [[refs[0]], refs[1 : 1 + parts]], refs[1 + parts :]
-    if not first:
-        before, refs = refs[0], refs[1:]
-    if last:
-        base, refs = refs[0], refs[1:]
-    total = None if first else before[...]
-    for k, pieces in enumerate(blocks):
-        block = jnp.concatenate([piece[...] for piece in pieces], axis=0)
-        pieces = list(halves(block[:modes].T))
+def whole_product(scale, rows, matrix, gathered, base, *refs):
+    outs, (held, sems) = refs[:-2], refs[-2:]
+    modes, cells = base.shape
+    copies = []
+    for k in range(gathered.shape[0]):
+        copies.append(pltpu.make_async_copy(gathered.at[k], held.at[k], sems.at[k]))
+        copies[-1].start()
+    total = None
+    for k, copy in enumerate(copies):
+        copy.wait()
+        pieces = list(halves(held[k, :modes].T))
         if rows:
+            per = modes // LANES
             weights = [
                 jnp.concatenate(
-                    [
-                        block[modes + i : modes + i + 1, :]
-                        for i in range(d * modes // LANES, (d + 1) * modes // LANES)
-                    ],
+                    [held[k, modes + i : modes + i + 1, :] for i in range(d * per, (d + 1) * per)],
                     axis=1,
                 )
                 for d in range(2)
@@ -139,18 +137,14 @@
             weights.append(jnp.zeros((6, modes), jnp.float32))
             pieces += halves(jnp.concatenate(weights, axis=0))
         left = jnp.concatenate(pieces, axis=0)
-        there = rows_of(matrix, for_device(numbers[k]))
-        term = jnp.dot(left, matrix[there, :], preferred_element_type=jnp.float32)
+        block = matrix[k * modes : (k + 1) * modes, :]
+        term = jnp.dot(left, block, preferred_element_type=jnp.float32)
         total = term if total is None else total + term
-    if not last:
-        refs[0][...] = total
-        return
-    cells = base.shape[1]
     value = base[...] - scale * (total[:cells] + total[cells : 2 * cells]).T
-    refs[0][...] = value
+    outs[0][...] = value
     if rows:
-        refs[1][...] = value.T[:HALO]
-        refs[2][...] = total[2 * cells : 2 * cells + 8] + total[2 * cells + 8 :]
+        outs[1][...] = value.T[:HALO]
+        outs[2][...] = total[2 * cells : 2 * cells + 8] + total[2 * cells + 8 :]
 
 
 def own_rows(distribution, velocity, capacity, out, token, speeds, weight, sems):
@@ -178,33 +172,15 @@
     copies[2].wait()
 
 
-def payload(numbers, slots, arrived, *refs):
-    out = refs[-1]
+def payload(numbers, slots, *refs):
+    *arrived, out = (refs[0], refs[-1]) if len(refs) > len(slots) + 1 else (refs[-1],)
+    terms = refs[len(arrived) : -1]
     slot_here = for_device(numbers)
-
     for k, slot in enumerate(slots):
 
         @pl.when(slot_here == slot)
         def _(k=k):
-            terms = refs[k]
-            modes = terms.shape[0]
-            out[:modes] = arrived[:modes] + terms[...]
-            if out.shape[0] > modes:
-                out[modes:] = arrived[modes:]
-
-    @pl.when(slot_here < 0)
-    def _():
-        out[...] = arrived[...]
-
-
-def pick(numbers, *refs):
-    out = refs[-1]
-    choice = for_device(numbers)
-    for k, ref in enumerate(refs[:-1]):
-
-        @pl.when(choice == k)
-        def _(ref=ref):
-            out[...] = ref[...]
+            out[...] = arrived[0][...] + terms[k][...] if arrived else terms[k][...]
 
 
 def add(one, *refs):
@@ -378,54 +354,27 @@
     def __init__(self, chips):
         self.chips = chips
         self.devices = range(2 * chips)
-        sources = [self.sources(d) for d in self.devices]
         targets = [self.targets(d // 2) for d in self.devices]
-        self.blocks = [
-            [
-                [2 * sources[e][slot][2] + e % 2 for e in (d ^ other for d in self.devices)]
-                for other in (0, 1)
-            ]
-            for slot in range(chips)
-        ]
         self.rows = [
             [[2 * targets[d][slot] + (d % 2 ^ other) for d in self.devices] for other in (0, 1)]
             for slot in range(chips)
         ]
-        self.choices = [
-            sorted({sources[d][slot][:2] for d in self.devices}) for slot in range(chips)
-        ]
-        self.picked = [
-            [self.choices[slot].index(sources[d][slot][:2]) for d in self.devices]
-            for slot in range(chips)
-        ]
-        self.sent = {}
+        self.sent, self.pairs = {}, {}
         for stream in (0, 1):
             for step in range(1, chips):
-                numbers = []
+                numbers, pairs = [], []
                 for d in self.devices:
                     way = self.way(d, stream)
                     place = d // 2 if way > 0 else chips - 1 - d // 2
+                    sends = place < step
                     target = d // 2 + way * (chips - step)
-                    numbers.append(targets[d].index(target) if place < step else -1)
-                self.sent[stream, step] = numbers
-        self.pairs = []
-        for stream in (0, 1):
-            up = [
-                (d, d + 2) for d in self.devices[:-2] if self.way(d, stream) > 0
-            ]
-            self.pairs.append(up + [(j, i) for i, j in up])
+                    numbers.append(targets[d].index(target) if sends else -1)
+                    if sends:
+                        pairs.append((d, d + 2 * way))
+                self.sent[stream, step], self.pairs[stream, step] = numbers, pairs
 
     def way(self, device, stream):
         return 1 if (device // 2 + device % 2 + stream) % 2 == 0 else -1
-
-    def sources(self, device):
-        found = [(-1, -1, device // 2)]
-        for step in range(self.chips - 1):
-            for stream in (step % 2, 1 - step % 2):
-                chip = device // 2 + self.way(device, stream) * (step + 1)
-                if 0 <= chip < self.chips:
-                    found.append((stream, step, chip))
-        return found
 
     def targets(self, chip):
         found = []
@@ -458,30 +407,18 @@
         ends = [cut * k for k in range(parts)] + [value.shape[0]]
         return [lax.ppermute(value[i:j], "mode", across) for i, j in zip(ends, ends[1:])]
 
-    def along(stream, value):
-        return lax.ppermute(value, "mode", plan.pairs[stream])
-
-    class Round:
-        def __init__(self, matrix, scale, rows):
-            self.matrix, self.scale, self.rows = matrix, scale, rows
-            self.terms, self.total = [], None
-
-        def begin(self, own):
-            self.own = own
-            self.arrived = [[along(0, own)], [along(1, own)]]
-            self.blocks = []
-
-        def add_terms(self, field, parts=1):
+    class Sums:
+        def __init__(self, scale):
+            self.scale, self.terms, self.arrived = scale, [], [[None], [None]]
+
+        def add_terms(self, field):
             kernel = functools.partial(slot_products, plan.rows[len(self.terms)])
-            mine, other = call(kernel, [part] * 2, [self.matrix, field])
-            self.terms.append((mine, *exchange(other, parts)))
+            mine, other = call(kernel, [part] * 2, [matrix, field])
+            self.terms.append((mine, *exchange(other)))
 
         def join_terms(self, *slots):
             for slot in slots:
                 (self.terms[slot],) = call(add, [part], self.terms[slot])
-
-        def take_own(self):
-            self.blocks.append((self.own, *exchange(self.own)))
 
         def send(self, step, between=None):
             sent = {}
@@ -490,38 +427,16 @@
                     between()
                 numbers = plan.sent[stream, step]
                 slots = sorted({n for n in numbers if n >= 0})
-                for slot in slots:
-                    if isinstance(self.terms[slot], tuple):
-                        self.join_terms(slot)
                 arrived = self.arrived[1 - stream][step - 1]
-                kernel = functools.partial(payload, numbers, slots)
-                arrays = [arrived] + [self.terms[s] for s in slots]
-                (value,) = call(kernel, [arrived.shape], arrays)
-                sent[stream] = along(stream, value)
+                arrays = [] if arrived is None else [arrived]
+                if step == 1:
+                    value = self.terms[0]
+                else:
+                    kernel = functools.partial(payload, numbers, slots)
+                    (value,) = call(kernel, [part], arrays + [self.terms[s] for s in slots])
+                sent[stream] = lax.ppermute(value, "mode", plan.pairs[stream, step])
             for stream in (0, 1):
                 self.arrived[stream].append(sent[stream])
-
-        def take(self, slot, parts=1):
-            arrays = [self.arrived[stream][step] for stream, step in plan.choices[slot]]
-            kernel = functools.partial(pick, plan.picked[slot])
-            (here,) = call(kernel, [arrays[0].shape], arrays)
-            self.blocks.append((here, *exchange(here, parts)))
-
-        def multiply(self, slot, base=None):
-            first, last = slot == 0, base is not None
-            blocks = self.blocks[slot]
-            kernel = functools.partial(
-                two_blocks, plan.blocks[slot], len(blocks) - 1, first, last, self.scale, self.rows
-            )
-            arrays = [self.matrix, *blocks]
-            arrays += [] if first else [self.total]
-            arrays += [base] if last else []
-            outs = [(2 * half + (16 if self.rows else 0), modes)]
-            if last:
-                outs = [part, (HALO, modes), (8, modes)] if self.rows else [part]
-            results = call(kernel, outs, arrays)
-            self.total = results[0]
-            return results
 
         def first_end(self, base):
             kernel = functools.partial(take_off, self.scale)
@@ -530,6 +445,21 @@
 
         def ends(self):
             return [self.arrived[chips % 2][-1], self.rest]
+
+    def product(gathered, base, scale, rows):
+        kernel = functools.partial(whole_product, scale, rows)
+        outs = [part, (HALO, modes), (8, modes)] if rows else [part]
+        return call(
+            kernel,
+            outs,
+            [matrix, gathered, base],
+            places=[VMEM, HBM, VMEM],
+            scratch=[
+                pltpu.VMEM(gathered.shape, jnp.float32),
+                pltpu.SemaphoreType.DMA((devices,)),
+            ],
+            room=24,
+        )
 
     own, _ = call(
         own_rows,
@@ -543,8 +473,7 @@
         ],
         room=56,
     )
-    one = Round(None, time_step, True)
-    one.begin(own)
+    gathered = lax.all_gather(own, "mode")
     *terms, matrix = call(
         functools.partial(load_and_products, plan.rows, half),
         [part] * (2 * chips) + [jax.ShapeDtypeStruct(scatter_matrix.shape, jnp.bfloat16)],
@@ -556,9 +485,6 @@
         ],
         room=28,
     )
-    one.matrix = matrix
-    one.terms = [(terms[2 * s], *exchange(terms[2 * s + 1])) for s in range(chips)]
-    one.take_own()
     operators = jnp.asarray(differences(cells))
     strips = None
 
@@ -567,67 +493,52 @@
         shape = jax.ShapeDtypeStruct((modes, 4 * HALO), jnp.bfloat16)
         (strips,) = call(strip_columns, [shape], strips)
 
-    for step in range(1, chips):
-        if step == 1:
-            one.take(1)
+    one = Sums(time_step)
+    one.terms = [(terms[2 * s], *exchange(terms[2 * s + 1])) for s in range(chips)]
+    one.join_terms(0)
+    one.send(1)
+    one.join_terms(*range(1, chips))
+    strips = call(strip_rows, [(HALO, modes)] * 2, [distribution])
+    strips = paired(*call(strip_pairs, [(HALO, modes)] * 2, strips))
+    for step in range(2, chips):
         one.send(step, unpack if step == 2 else None)
-        if step == 1:
-            one.join_terms(*(s for s in range(chips) if isinstance(one.terms[s], tuple)))
-            strips = call(strip_rows, [(HALO, modes)] * 2, [distribution])
-            strips = paired(*call(strip_pairs, [(HALO, modes)] * 2, strips))
-        else:
-            one.take(step, 2 if step == chips - 1 else 1)
-        one.multiply(step - 1)
-        if step == min(2, chips - 1):
+        if step == 2:
             base_a, base_b = call(
-                first_rest,
-                [part] * 2,
-                [distribution, strips, operators, table, kinds],
+                first_rest, [part] * 2, [distribution, strips, operators, table, kinds]
             )
-    mid_a, leading, scattered = one.multiply(chips - 1, base_a)
-
-    two = Round(matrix, step_size, False)
-    two.add_terms(mid_a, 1)
     one.first_end(base_b)
     mid_b, last = call(
         functools.partial(turn_sum, time_step), [part, (HALO, modes)], one.ends()
     )
-    two.begin(mid_b)
+    gathered_mid = lax.all_gather(mid_b, "mode")
+    mid_a, leading, scattered = product(gathered, base_a, time_step, True)
+
+    two = Sums(step_size)
     two.add_terms(mid_a)
     two.add_terms(mid_a)
     two.join_terms(0)
+    two.send(1)
     strips = paired(*call(strip_pairs, [(HALO, modes)] * 2, [leading, last]))
+    for slot in range(2, chips):
+        two.add_terms(mid_a)
+    two.join_terms(*range(1, chips))
     flux = None
-    for step in range(1, chips):
-        if step == 1:
+    for step in range(2, chips):
+        if step == 2:
             two.send(step, unpack)
-            two.take_own()
-            two.join_terms(1, 2)
-        elif step == 2:
-            two.send(step, lambda: flux.over(1))
-            two.join_terms(*range(3, chips))
-        elif step == chips - 1:
-            two.send(step, lambda: flux.over(*range(2, devices, 2)))
-        else:
-            two.send(step)
-        two.take(step, 2 if step >= chips - 2 else 1)
-        if step == 1:
-            for slot in range(3, chips):
-                two.add_terms(mid_a)
-        if step < chips - 1:
-            two.multiply(step - 1)
-        if step == chips - 2:
-            two.multiply(step)
-        if step == 1:
             end_a, end_b, part_flux = call(
                 functools.partial(second_rest, 1.0 / math.sqrt(total_modes)),
                 [part, part, (2, cells)],
                 [distribution, mid_a, mid_b, strips, operators, table, kinds, scattered],
             )
             flux = Flux(call, part_flux, devices)
-    (last_b,) = two.multiply(chips - 1, end_b)
+            flux.over(1)
+        else:
+            two.send(step)
+    flux.over(*range(2, devices, 2))
     heat_flux = flux.value
     two.first_end(end_a)
+    (last_b,) = product(gathered_mid, end_b, step_size, False)
     (updated,) = call(
         functools.partial(last_sum, step_size),
         [(modes, cells)],

time: 140 us -> 203 us (1.45)
  the two profiles are of different devices: /device:TPU:13 before, /device:TPU:0 now
where the time goes in v11:
time: 203 us; the launch traced here: 202 us
  waiting for transfers between devices  71.1 us (35%)
  starting transfers between devices  49.1 us (24%)
  Pallas kernels  36.3 us (18%)
  local copies, waits for them, and re-layouts  31.1 us (15%)
  between operations  14.6 us (7%)
    ppermute x12, waiting for transfers between devices, send(): sent[stream] = lax.ppermute(value, 'mode', plan.pairs[stream, step])  57.7 us
    pallas_call x37, Pallas kernels, __call__(): pl.pallas_call(body, out_shape=[jax.ShapeDtypeStruct(shape, jnp.float32)...  36.3 us
    unnamed x34, local copies, waits for them, and re-layouts  31 us
    ppermute x12, starting transfers between devices, send(): sent[stream] = lax.ppermute(value, 'mode', plan.pairs[stream, step])  30.3 us
    ppermute x4, starting transfers between devices, over(): lax.ppermute(self.value, 'mode', [(i, i ^ bit) for i in range(self.device...  11.9 us
    ppermute x4, waiting for transfers between devices, over(): lax.ppermute(self.value, 'mode', [(i, i ^ bit) for i in range(self.device...  9.4 us
    ppermute x4, starting transfers between devices, paired(): lax.ppermute(value, 'space', pairs + [(j, i) for i, j in pairs])  4.42 us
  transfers between devices with their start and end apart: 30, of which 11 were waited for; matrix products, arithmetic and copies ran while one was open for 0% of the time, Pallas kernels for 17%

profile of v11, /device:TPU:0, one launch (start us, length us, event | category | flops | bytes accessed | tf_op | source)
XLA Modules:
  0.0 202.2 jit_solution(15893039319392788529)
XLA Ops:
  7.2 1.9 own_rows.1
  9.2 1.2 copy-done.4
  10.4 0.7 copy-done.9
  11.1 7.4 %load_and_products.1 = (f32[1024,128]{1,0:T(8,128)S(1)}, f32[1024,128]{1,0:T(8,128)S(1)}, f32[1024,128]{1,0:T(8,128)S(1)}, f32[1024,128]{1,0:T(8,128)S(1)}, f32[...) custom-call(bf16[8192,1024]{1,0:T(8,128)(2,1)} %refs_0_.6, ...), custom_call_target="tpu_custom_call" | custom-call | flops 1024 | bytes 1024 | tf_op jit(solution)/shard_map/load_and_products/pallas_call | solution.py:39
  18.5 0.5 collective-permute-start.3
  19.1 0.4 collective-permute-start.1
  19.6 0.9 collective-permute-done.3.refs_1_
  20.6 4.1 %copy-done = bf16[8192,1024]{1,0:T(8,128)(2,1)} copy-done((bf16[8192,1024]{1,0:T(8,128)(2,1)}, bf16[8192,1024]{1,0:T(8,128)(2,1)S(1)}, u32[]{:S(2)}) %copy-start) | copy-done | bytes 16777240
  24.7 0.7 collective-permute-start.6
  25.4 4.8 %collective-permute-start.7 = (f32[1024,128]{1,0:T(8,128)S(1)}, f32[1024,128]{1,0:T(8,128)S(1)}, u32[]{:S(2)}, u32[]{:S(2)}) collective-permute-start(f32[1024,128]{1,0:T(8,128)S(1)} %add.8.refs_2_.refs_1_), channel_id=1, source_target_pairs={{0,2},{6,4},{8,10},{14,12},{16,18},{22,20},{24,26},{30,28}} | collective-permute-start | bytes 1572872 | tf_op jit(solution)/shard_map/ppermute | solution.py:437
  30.4 0.3 strip_rows.1
  30.8 1.6 collective-permute-start.4
  32.4 0.7 collective-permute-start.5
  33.0 0.1 payload.8.refs_2_
  33.1 1.3 collective-permute-start.9
  34.5 1.4 collective-permute-done.4.refs_0_
  35.9 0.1 strip_columns.2.refs_3_.refs_1_
  36.1 17.0 %collective-permute-done.7.refs_0_ = f32[1024,128]{1,0:T(8,128)S(1)} collective-permute-done((f32[1024,128]{1,0:T(8,128)S(1)}, f32[1024,128]{1,0:T(8,128)S(1)}, u32[]{:S(2)}, u32[]{:S(2)}) %collective-permute-start.7) | collective-permute-done | bytes 524320 | tf_op jit(solution)/shard_map/ppermute | solution.py:437
  53.0 0.7 collective-permute-start.8
  53.9 2.0 first_rest.1
  55.9 17.5 %collective-permute-done.9.refs_0_ = f32[1024,128]{1,0:T(8,128)S(1)} collective-permute-done((f32[1024,128]{1,0:T(8,128)S(1)}, f32[1024,128]{1,0:T(8,128)S(1)}, u32[]{:S(2)}, u32[]{:S(2)}) %collective-permute-start.9) | collective-permute-done | bytes 524320 | tf_op jit(solution)/shard_map/ppermute | solution.py:437
  73.4 0.7 collective-permute-start.11
  74.1 0.1 payload.11.refs_3_
  74.2 7.8 %collective-permute-start.10 = (f32[1024,128]{1,0:T(8,128)S(1)}, f32[1024,128]{1,0:T(8,128)S(1)}, u32[]{:S(2)}, u32[]{:S(2)}) collective-permute-start(f32[1024,128]{1,0:T(8,128)S(1)} %payload.11.refs_3_), channel_id=1, source_target_pairs={{0,2},{2,0},{3,5},{4,6},{5,3},{6,4},{8,10},{10,8},{11,13},{12,14},... | collective-permute-start | bytes 1572872 | tf_op jit(solution)/shard_map/ppermute | solution.py:437
  82.1 8.8 %collective-permute-done.10.refs_0_ = f32[1024,128]{1,0:T(8,128)S(1)} collective-permute-done((f32[1024,128]{1,0:T(8,128)S(1)}, f32[1024,128]{1,0:T(8,128)S(1)}, u32[]{:S(2)}, u32[]{:S(2)}) %collective-permute-start.10) | collective-permute-done | bytes 524320 | tf_op jit(solution)/shard_map/ppermute | solution.py:437
  90.9 0.9 turn_sum.1
  91.8 5.8 %copy-done.1 = bf16[8192,1024]{1,0:T(8,128)(2,1)S(1)} copy-done((bf16[8192,1024]{1,0:T(8,128)(2,1)S(1)}, bf16[8192,1024]{1,0:T(8,128)(2,1)}, u32[]{:S(2)}) %copy-start.1) | copy-done | bytes 16777240
  97.6 2.4 %copy-done.7 = f32[8320,128]{1,0:T(8,128)S(1)} copy-done((f32[8320,128]{1,0:T(8,128)S(1)}, f32[8320,128]{1,0:T(8,128)}, u32[]{:S(2)}) %copy-start.7) | copy-done | bytes 4259864
  100.0 6.3 %whole_product.2 = (f32[1024,128]{1,0:T(8,128)S(1)}, f32[32,1024]{1,0:T(8,128)S(1)}, f32[8,1024]{1,0:T(8,128)S(1)}) custom-call(bf16[8192,1024]{1,0:T(8,128)(2,1)S(1)} %copy-done.1, f32[8,1040,128]{2,1,0:T(8,128)S(1)} %bitcast.6, f32[1024,128]{1,0:T(8,128)S(1)} %get-tuple-element.56.refs_2_, f32[32,1024]{1,0:T(8,128)S(1)} %get-tuple-element.58.refs_3_.refs_1_), custom_call_target="tpu_custom_call" | custom-call | flops 1024 | bytes 1024 | tf_op jit(solution)/shard_map/whole_product/pallas_call | solution.py:39
  106.3 5.9 %copy-done.2 = bf16[8192,1024]{1,0:T(8,128)(2,1)S(1)} copy-done((bf16[8192,1024]{1,0:T(8,128)(2,1)S(1)}, bf16[8192,1024]{1,0:T(8,128)(2,1)}, u32[]{:S(2)}) %copy-start.2) | copy-done | bytes 16777240
  112.3 1.2 slot_products.4
  113.6 1.3 slot_products.5
  114.9 0.6 collective-permute-start.14
  115.6 0.2 slice-done.1
  115.8 1.4 slice-done.2
  117.2 1.3 slice-done.3
  118.5 1.3 slot_products.6
  119.8 1.3 slot_products.7
  121.1 0.6 collective-permute-start.18
  121.7 0.7 collective-permute-start.17
  122.3 3.5 %collective-permute-start.13 = (f32[1024,128]{1,0:T(8,128)S(1)}, f32[1024,128]{1,0:T(8,128)S(1)}, u32[]{:S(2)}, u32[]{:S(2)}) collective-permute-start(f32[1024,128]{1,0:T(8,128)S(1)} %add.12.refs_2_.refs_1_), channel_id=1, source_target_pairs={{0,2},{6,4},{8,10},{14,12},{16,18},{22,20},{24,26},{30,28}} | collective-permute-start | bytes 1572872 | tf_op jit(solution)/shard_map/ppermute | solution.py:437
  125.9 1.5 collective-permute-start.15
  127.5 0.7 collective-permute-start.16
  128.4 1.5 collective-permute-start.21
  129.9 1.4 collective-permute-done.15.refs_0_
  131.3 0.1 strip_columns.3.refs_3_
  131.5 14.4 %collective-permute-done.13.refs_0_ = f32[1024,128]{1,0:T(8,128)S(1)} collective-permute-done((f32[1024,128]{1,0:T(8,128)S(1)}, f32[1024,128]{1,0:T(8,128)S(1)}, u32[]{:S(2)}, u32[]{:S(2)}) %collective-permute-start.13) | collective-permute-done | bytes 524320 | tf_op jit(solution)/shard_map/ppermute | solution.py:437
  145.9 0.7 collective-permute-start.20
  146.6 3.6 %second_rest.1 = (f32[1024,128]{1,0:T(8,128)S(1)}, f32[1024,128]{1,0:T(8,128)S(1)}, f32[2,256]{1,0:T(2,128)S(1)}) custom-call(f32[1024,256]{1,0:T(8,128)S(1)} %copy-done.5, f32[1024,128]{1,0:T(8,128)S(1)} %get-tuple-element.59.refs_1_, f32[1024,128]{1,0:T(8,128)} %get-tuple-element.72.refs_2_, bf16[1024,128]{1,0:T(8,128)(2,1)S(1)} %strip_columns.3.refs_3_, ...), custom_call_target="tpu_custom_call" | custom-call | flops 1024 | bytes 1024 | tf_op jit(solution)/shard_map/second_rest/pallas_call | solution.py:39
  150.3 7.4 %collective-permute-start.22 = (f32[2,256]{1,0:T(2,128)S(1)}, f32[2,256]{1,0:T(2,128)S(1)}, u32[]{:S(2)}, u32[]{:S(2)}) collective-permute-start(f32[2,256]{1,0:T(2,128)S(1)} %get-tuple-element.73.refs_0_.refs_2_), channel_id=1, source_target_pairs={{0,1},{1,0},{2,3},{3,2},{4,5},{5,4},{6,7},{7,6},{8,9},{9,8},{10,11... | collective-permute-start | bytes 6152 | tf_op jit(solution)/shard_map/ppermute | solution.py:558
  157.7 0.8 collective-permute-done.22.refs_1_
  158.5 0.7 collective-permute-start.24
  159.2 0.1 payload.15.refs_4_
  159.3 7.3 %collective-permute-start.23 = (f32[1024,128]{1,0:T(8,128)S(1)}, f32[1024,128]{1,0:T(8,128)S(1)}, u32[]{:S(2)}, u32[]{:S(2)}) collective-permute-start(f32[1024,128]{1,0:T(8,128)S(1)} %payload.15.refs_4_), channel_id=1, source_target_pairs={{0,2},{2,0},{3,5},{4,6},{5,3},{6,4},{8,10},{10,8},{11,13},{12,14},... | collective-permute-start | bytes 1572872 | tf_op jit(solution)/shard_map/ppermute | solution.py:437
  166.7 3.2 %collective-permute-start.26 = (f32[2,256]{1,0:T(2,128)S(1)}, f32[2,256]{1,0:T(2,128)S(1)}, u32[]{:S(2)}, u32[]{:S(2)}) collective-permute-start(f32[2,256]{1,0:T(2,128)S(1)} %get-tuple-element.76.refs_0_), channel_id=1, source_target_pairs={{0,4},{1,5},{2,6},{3,7},{4,0},{5,1},{6,2},{7,3},{8,12},{9,13},{10,... | collective-permute-start | bytes 6152 | tf_op jit(solution)/shard_map/ppermute | solution.py:558
  169.9 1.2 collective-permute-start.27
  171.1 6.5 %collective-permute-done.25.refs_1_ = f32[2,256]{1,0:T(2,128)S(1)} collective-permute-done((f32[2,256]{1,0:T(2,128)S(1)}, f32[2,256]{1,0:T(2,128)S(1)}, u32[]{:S(2)}, u32[]{:S(2)}) %collective-permute-start.25) | collective-permute-done | bytes 2080 | tf_op jit(solution)/shard_map/ppermute | solution.py:558
  177.6 2.0 %collective-permute-done.27.refs_3_ = f32[2,256]{1,0:T(2,128)S(1)} collective-permute-done((f32[2,256]{1,0:T(2,128)S(1)}, f32[2,256]{1,0:T(2,128)S(1)}, u32[]{:S(2)}, u32[]{:S(2)}) %collective-permute-start.27) | collective-permute-done | bytes 2080 | tf_op jit(solution)/shard_map/ppermute | solution.py:558
  179.7 0.6 add_all.3
  180.3 0.1 take_off.3.refs_3_.refs_1_
  180.4 5.8 %copy-done.3 = bf16[8192,1024]{1,0:T(8,128)(2,1)S(1)} copy-done((bf16[8192,1024]{1,0:T(8,128)(2,1)S(1)}, bf16[8192,1024]{1,0:T(8,128)(2,1)}, u32[]{:S(2)}) %copy-start.3) | copy-done | bytes 16777240
  186.2 2.2 %copy-done.8 = f32[8192,128]{1,0:T(8,128)S(1)} copy-done((f32[8192,128]{1,0:T(8,128)S(1)}, f32[8192,128]{1,0:T(8,128)}, u32[]{:S(2)}) %copy-start.8) | copy-done | bytes 4194328
  188.4 6.0 %whole_product.3.refs_2_.refs_3_ = f32[1024,128]{1,0:T(8,128)S(1)} custom-call(bf16[8192,1024]{1,0:T(8,128)(2,1)S(1)} %copy-done.3, f32[8,1024,128]{2,1,0:T(8,128)S(1)} %bitcast.7, f32[1024,128]{1,0:T(8,128)S(1)} %get-tuple-element.78.refs_2_, f32[1024,128]{1,0:T(8,128)S(1)} %take_off.3.refs_3_.refs_1_), custom_call_target="tpu_custom_call" | custom-call | flops 1024 | bytes 1024 | tf_op jit(solution)/shard_map/whole_product/pallas_call | solution.py:39
  194.3 1.0 last_sum.1
  (74 shorter events, 1.6 us)
Async XLA Ops:
  7.2 84.7 %all-gather.5.cloned.1.call-start = ((), (), s32[]{:S(2)}) async-start(), calls=%async_computation | async-start | bytes 4792320 | tf_op jit(solution)/shard_map/all_gather | solution.py:476
  9.1 171.3 %all-gather.7.cloned.1.call-start = ((), (), s32[]{:S(2)}) async-start(), calls=%async_computation.1 | async-start | bytes 4718592 | tf_op jit(solution)/shard_map/all_gather | solution.py:513
  9.2 1.2 copy-start.4
  10.4 0.7 copy-start.9
  18.5 6.2 %copy-start = (bf16[8192,1024]{1,0:T(8,128)(2,1)}, bf16[8192,1024]{1,0:T(8,128)(2,1)S(1)}, u32[]{:S(2)}) copy-start(bf16[8192,1024]{1,0:T(8,128)(2,1)S(1)} %get-tuple-element.42.refs_2_.refs_0_) | copy-start | bytes 50331652
  18.5 2.1 %collective-permute-start.3 = (f32[1024,128]{1,0:T(8,128)S(1)}, f32[1024,128]{1,0:T(8,128)S(1)}, u32[]{:S(2)}, u32[]{:S(2)}) collective-permute-start(f32[1024,128]{1,0:T(8,128)S(1)} %get-tuple-element.51), channel_id=1, source_target_pairs={{0,1},{1,0},{2,3},{3,2},{4,5},{5,4},{6,7},{7,6},{8,9},{9,8},{10,11... | collective-permute-start | bytes 1572872 | tf_op jit(solution)/shard_map/ppermute | solution.py:408
  19.0 11.2 %collective-permute-start.2 = (f32[1024,128]{1,0:T(8,128)S(1)}, f32[1024,128]{1,0:T(8,128)S(1)}, u32[]{:S(2)}, u32[]{:S(2)}) collective-permute-start(f32[1024,128]{1,0:T(8,128)S(1)} %get-tuple-element.49), channel_id=1, source_target_pairs={{0,1},{1,0},{2,3},{3,2},{4,5},{5,4},{6,7},{7,6},{8,9},{9,8},{10,11... | collective-permute-start | bytes 1572872 | tf_op jit(solution)/shard_map/ppermute | solution.py:408
  19.1 11.2 %collective-permute-start.1 = (f32[1024,128]{1,0:T(8,128)S(1)}, f32[1024,128]{1,0:T(8,128)S(1)}, u32[]{:S(2)}, u32[]{:S(2)}) collective-permute-start(f32[1024,128]{1,0:T(8,128)S(1)} %get-tuple-element.47), channel_id=1, source_target_pairs={{0,1},{1,0},{2,3},{3,2},{4,5},{5,4},{6,7},{7,6},{8,9},{9,8},{10,11... | collective-permute-start | bytes 1572872 | tf_op jit(solution)/shard_map/ppermute | solution.py:408
  19.5 10.8 %collective-permute-start = (f32[1024,128]{1,0:T(8,128)S(1)}, f32[1024,128]{1,0:T(8,128)S(1)}, u32[]{:S(2)}, u32[]{:S(2)}) collective-permute-start(f32[1024,128]{1,0:T(8,128)S(1)} %get-tuple-element.45), channel_id=1, source_target_pairs={{0,1},{1,0},{2,3},{3,2},{4,5},{5,4},{6,7},{7,6},{8,9},{9,8},{10,11... | collective-permute-start | bytes 1572872 | tf_op jit(solution)/shard_map/ppermute | solution.py:408
  24.7 8.3 %collective-permute-start.6 = (f32[1024,128]{1,0:T(8,128)S(1)}, f32[1024,128]{1,0:T(8,128)S(1)}, u32[]{:S(2)}, u32[]{:S(2)}) collective-permute-start(f32[1024,128]{1,0:T(8,128)S(1)} %add.8.refs_2_.refs_1_), channel_id=1, source_target_pairs={{1,3},{7,5},{9,11},{15,13},{17,19},{23,21},{25,27},{31,29}} | collective-permute-start | bytes 1572872 | tf_op jit(solution)/shard_map/ppermute | solution.py:437
  25.4 27.6 %collective-permute-start.7 = (f32[1024,128]{1,0:T(8,128)S(1)}, f32[1024,128]{1,0:T(8,128)S(1)}, u32[]{:S(2)}, u32[]{:S(2)}) collective-permute-start(f32[1024,128]{1,0:T(8,128)S(1)} %add.8.refs_2_.refs_1_), channel_id=1, source_target_pairs={{0,2},{6,4},{8,10},{14,12},{16,18},{22,20},{24,26},{30,28}} | collective-permute-start | bytes 1572872 | tf_op jit(solution)/shard_map/ppermute | solution.py:437
  30.4 23.4 %copy-start.11 = (f32[2,1024]{1,0:T(2,128)S(1)}, f32[2,1024]{1,0:T(2,128)}, u32[]{:S(2)}) copy-start(f32[2,1024]{1,0:T(2,128)} %refs_1_.2) | copy-start | bytes 24580
  30.4 23.4 %copy-start.12 = (f32[1024]{0:T(1024)S(1)}, f32[1024]{0:T(1024)}, u32[]{:S(2)}) copy-start(f32[1024]{0:T(1024)} %param.9) | copy-start | bytes 12292
  30.4 23.5 %copy-start.6 = (bf16[640,1024]{1,0:T(8,128)(2,1)S(1)}, bf16[640,1024]{1,0:T(8,128)(2,1)}, u32[]{:S(2)}) copy-start(bf16[640,1024]{1,0:T(8,128)(2,1)} %constant.4.clone.refs_2_.refs_4_) | copy-start | bytes 3932164
  30.4 23.5 %copy-start.10 = (s32[256]{0:T(256)S(1)}, s32[256]{0:T(256)}, u32[]{:S(2)}) copy-start(s32[256]{0:T(256)} %param.10) | copy-start | bytes 3076
  30.8 5.1 %collective-permute-start.4 = (f32[32,1024]{1,0:T(8,128)S(1)}, f32[32,1024]{1,0:T(8,128)S(1)}, u32[]{:S(2)}, u32[]{:S(2)}) collective-permute-start(f32[32,1024]{1,0:T(8,128)S(1)} %get-tuple-element.54), channel_id=1, source_target_pairs={{0,8},{16,24},{8,0},{24,16},{1,9},{17,25},{9,1},{25,17},{2,10},{18... | collective-permute-start | bytes 393224 | tf_op jit(solution)/shard_map/ppermute | solution.py:349
  32.4 3.5 %collective-permute-start.5 = (f32[32,1024]{1,0:T(8,128)S(1)}, f32[32,1024]{1,0:T(8,128)S(1)}, u32[]{:S(2)}, u32[]{:S(2)}) collective-permute-start(f32[32,1024]{1,0:T(8,128)S(1)} %get-tuple-element.55.refs_3_), channel_id=1, source_target_pairs={{8,16},{16,8},{9,17},{17,9},{10,18},{18,10},{11,19},{19,11},{12,20... | collective-permute-start | bytes 393224 | tf_op jit(solution)/shard_map/ppermute | solution.py:349
  33.1 40.2 %collective-permute-start.9 = (f32[1024,128]{1,0:T(8,128)S(1)}, f32[1024,128]{1,0:T(8,128)S(1)}, u32[]{:S(2)}, u32[]{:S(2)}) collective-permute-start(f32[1024,128]{1,0:T(8,128)S(1)} %payload.8.refs_2_), channel_id=1, source_target_pairs={{0,2},{3,5},{5,3},{6,4},{8,10},{11,13},{13,11},{14,12},{16,18},{19... | collective-permute-start | bytes 1572872 | tf_op jit(solution)/shard_map/ppermute | solution.py:437
  53.0 21.1 %collective-permute-start.8 = (f32[1024,128]{1,0:T(8,128)S(1)}, f32[1024,128]{1,0:T(8,128)S(1)}, u32[]{:S(2)}, u32[]{:S(2)}) collective-permute-start(f32[1024,128]{1,0:T(8,128)S(1)} %payload.9.refs_5_), channel_id=1, source_target_pairs={{1,3},{2,4},{4,2},{7,5},{9,11},{10,12},{12,10},{15,13},{17,19},{18... | collective-permute-start | bytes 1572872 | tf_op jit(solution)/shard_map/ppermute | solution.py:437
  73.4 8.7 %collective-permute-start.11 = (f32[1024,128]{1,0:T(8,128)S(1)}, f32[1024,128]{1,0:T(8,128)S(1)}, u32[]{:S(2)}, u32[]{:S(2)}) collective-permute-start(f32[1024,128]{1,0:T(8,128)S(1)} %payload.10.refs_3_), channel_id=1, source_target_pairs={{1,3},{2,4},{3,1},{4,2},{5,7},{7,5},{9,11},{10,12},{11,9},{12,10},... | collective-permute-start | bytes 1572872 | tf_op jit(solution)/shard_map/ppermute | solution.py:437
  74.2 16.7 %collective-permute-start.10 = (f32[1024,128]{1,0:T(8,128)S(1)}, f32[1024,128]{1,0:T(8,128)S(1)}, u32[]{:S(2)}, u32[]{:S(2)}) collective-permute-start(f32[1024,128]{1,0:T(8,128)S(1)} %payload.11.refs_3_), channel_id=1, source_target_pairs={{0,2},{2,0},{3,5},{4,6},{5,3},{6,4},{8,10},{10,8},{11,13},{12,14},... | collective-permute-start | bytes 1572872 | tf_op jit(solution)/shard_map/ppermute | solution.py:437
  91.8 5.8 %copy-start.1 = (bf16[8192,1024]{1,0:T(8,128)(2,1)S(1)}, bf16[8192,1024]{1,0:T(8,128)(2,1)}, u32[]{:S(2)}) copy-start(bf16[8192,1024]{1,0:T(8,128)(2,1)} %copy-done) | copy-start | bytes 50331652
  97.6 2.4 %copy-start.7 = (f32[8320,128]{1,0:T(8,128)S(1)}, f32[8320,128]{1,0:T(8,128)}, u32[]{:S(2)}) copy-start(f32[8320,128]{1,0:T(8,128)} %all-gather.5.cloned.1.call-done) | copy-start | bytes 12779524
  106.3 5.9 %copy-start.2 = (bf16[8192,1024]{1,0:T(8,128)(2,1)S(1)}, bf16[8192,1024]{1,0:T(8,128)(2,1)}, u32[]{:S(2)}) copy-start(bf16[8192,1024]{1,0:T(8,128)(2,1)} %copy-done) | copy-start | bytes 50331652
  112.2 3.4 %slice-start = ((s8[16777216]{0:T(1024)(128)(4,1)}), s8[4194304]{0:T(1024)(128)(4,1)S(1)}, s32[]{:S(2)}) async-start(s8[16777216]{0:T(1024)(128)(4,1)} %bitcast.4), calls=%async_computation.2 | async-start | bytes 8388608
  112.2 3.6 %slice-start.1 = ((s8[16777216]{0:T(1024)(128)(4,1)}), s8[4194304]{0:T(1024)(128)(4,1)S(1)}, s32[]{:S(2)}) async-start(s8[16777216]{0:T(1024)(128)(4,1)} %bitcast.4), calls=%async_computation.3 | async-start | bytes 8388608
  113.5 3.7 %slice-start.2 = ((s8[16777216]{0:T(1024)(128)(4,1)}), s8[4194304]{0:T(1024)(128)(4,1)S(1)}, s32[]{:S(2)}) async-start(s8[16777216]{0:T(1024)(128)(4,1)} %bitcast.4), calls=%async_computation.4 | async-start | bytes 8388608
  113.5 5.0 %slice-start.3 = ((s8[16777216]{0:T(1024)(128)(4,1)}), s8[4194304]{0:T(1024)(128)(4,1)S(1)}, s32[]{:S(2)}) async-start(s8[16777216]{0:T(1024)(128)(4,1)} %bitcast.4), calls=%async_computation.5 | async-start | bytes 8388608
  113.5 2.0 collective-permute-start.12
  114.9 11.0 %collective-permute-start.14 = (f32[1024,128]{1,0:T(8,128)S(1)}, f32[1024,128]{1,0:T(8,128)S(1)}, u32[]{:S(2)}, u32[]{:S(2)}) collective-permute-start(f32[1024,128]{1,0:T(8,128)S(1)} %get-tuple-element.63.refs_2_), channel_id=1, source_target_pairs={{0,1},{1,0},{2,3},{3,2},{4,5},{5,4},{6,7},{7,6},{8,9},{9,8},{10,11... | collective-permute-start | bytes 1572872 | tf_op jit(solution)/shard_map/ppermute | solution.py:408
  119.8 7.7 %collective-permute-start.19 = (f32[1024,128]{1,0:T(8,128)S(1)}, f32[1024,128]{1,0:T(8,128)S(1)}, u32[]{:S(2)}, u32[]{:S(2)}) collective-permute-start(f32[1024,128]{1,0:T(8,128)S(1)} %get-tuple-element.67.refs_2_), channel_id=1, source_target_pairs={{0,1},{1,0},{2,3},{3,2},{4,5},{5,4},{6,7},{7,6},{8,9},{9,8},{10,11... | collective-permute-start | bytes 1572872 | tf_op jit(solution)/shard_map/ppermute | solution.py:408
  121.1 7.2 %collective-permute-start.18 = (f32[1024,128]{1,0:T(8,128)S(1)}, f32[1024,128]{1,0:T(8,128)S(1)}, u32[]{:S(2)}, u32[]{:S(2)}) collective-permute-start(f32[1024,128]{1,0:T(8,128)S(1)} %get-tuple-element.68.refs_2_), channel_id=1, source_target_pairs={{0,1},{1,0},{2,3},{3,2},{4,5},{5,4},{6,7},{7,6},{8,9},{9,8},{10,11... | collective-permute-start | bytes 1572872 | tf_op jit(solution)/shard_map/ppermute | solution.py:408
  121.7 6.7 %collective-permute-start.17 = (f32[1024,128]{1,0:T(8,128)S(1)}, f32[1024,128]{1,0:T(8,128)S(1)}, u32[]{:S(2)}, u32[]{:S(2)}) collective-permute-start(f32[1024,128]{1,0:T(8,128)S(1)} %add.12.refs_2_.refs_1_), channel_id=1, source_target_pairs={{1,3},{7,5},{9,11},{15,13},{17,19},{23,21},{25,27},{31,29}} | collective-permute-start | bytes 1572872 | tf_op jit(solution)/shard_map/ppermute | solution.py:437
  122.3 23.6 %collective-permute-start.13 = (f32[1024,128]{1,0:T(8,128)S(1)}, f32[1024,128]{1,0:T(8,128)S(1)}, u32[]{:S(2)}, u32[]{:S(2)}) collective-permute-start(f32[1024,128]{1,0:T(8,128)S(1)} %add.12.refs_2_.refs_1_), channel_id=1, source_target_pairs={{0,2},{6,4},{8,10},{14,12},{16,18},{22,20},{24,26},{30,28}} | collective-permute-start | bytes 1572872 | tf_op jit(solution)/shard_map/ppermute | solution.py:437
  125.9 5.4 %collective-permute-start.15 = (f32[32,1024]{1,0:T(8,128)S(1)}, f32[32,1024]{1,0:T(8,128)S(1)}, u32[]{:S(2)}, u32[]{:S(2)}) collective-permute-start(f32[32,1024]{1,0:T(8,128)S(1)} %get-tuple-element.69), channel_id=1, source_target_pairs={{0,8},{16,24},{8,0},{24,16},{1,9},{17,25},{9,1},{25,17},{2,10},{18... | collective-permute-start | bytes 393224 | tf_op jit(solution)/shard_map/ppermute | solution.py:349
  127.5 3.9 %collective-permute-start.16 = (f32[32,1024]{1,0:T(8,128)S(1)}, f32[32,1024]{1,0:T(8,128)S(1)}, u32[]{:S(2)}, u32[]{:S(2)}) collective-permute-start(f32[32,1024]{1,0:T(8,128)S(1)} %get-tuple-element.66.refs_2_), channel_id=1, source_target_pairs={{8,16},{16,8},{9,17},{17,9},{10,18},{18,10},{11,19},{19,11},{12,20... | collective-permute-start | bytes 393224 | tf_op jit(solution)/shard_map/ppermute | solution.py:349
  128.2 18.4 %copy-start.5 = (f32[1024,256]{1,0:T(8,128)S(1)}, f32[1024,256]{1,0:T(8,128)}, u32[]{:S(2)}) copy-start(f32[1024,256]{1,0:T(8,128)} %refs_0_.9) | copy-start | bytes 3145732
  128.4 30.1 %collective-permute-start.21 = (f32[1024,128]{1,0:T(8,128)S(1)}, f32[1024,128]{1,0:T(8,128)S(1)}, u32[]{:S(2)}, u32[]{:S(2)}) collective-permute-start(f32[1024,128]{1,0:T(8,128)S(1)} %payload.12.refs_2_), channel_id=1, source_target_pairs={{0,2},{3,5},{5,3},{6,4},{8,10},{11,13},{13,11},{14,12},{16,18},{19... | collective-permute-start | bytes 1572872 | tf_op jit(solution)/shard_map/ppermute | solution.py:437
  145.9 13.3 %collective-permute-start.20 = (f32[1024,128]{1,0:T(8,128)S(1)}, f32[1024,128]{1,0:T(8,128)S(1)}, u32[]{:S(2)}, u32[]{:S(2)}) collective-permute-start(f32[1024,128]{1,0:T(8,128)S(1)} %payload.13.refs_8_), channel_id=1, source_target_pairs={{1,3},{2,4},{4,2},{7,5},{9,11},{10,12},{12,10},{15,13},{17,19},{18... | collective-permute-start | bytes 1572872 | tf_op jit(solution)/shard_map/ppermute | solution.py:437
  150.3 8.2 %collective-permute-start.22 = (f32[2,256]{1,0:T(2,128)S(1)}, f32[2,256]{1,0:T(2,128)S(1)}, u32[]{:S(2)}, u32[]{:S(2)}) collective-permute-start(f32[2,256]{1,0:T(2,128)S(1)} %get-tuple-element.73.refs_0_.refs_2_), channel_id=1, source_target_pairs={{0,1},{1,0},{2,3},{3,2},{4,5},{5,4},{6,7},{7,6},{8,9},{9,8},{10,11... | collective-permute-start | bytes 6152 | tf_op jit(solution)/shard_map/ppermute | solution.py:558
  158.5 21.8 %collective-permute-start.24 = (f32[1024,128]{1,0:T(8,128)S(1)}, f32[1024,128]{1,0:T(8,128)S(1)}, u32[]{:S(2)}, u32[]{:S(2)}) collective-permute-start(f32[1024,128]{1,0:T(8,128)S(1)} %payload.14.refs_3_), channel_id=1, source_target_pairs={{1,3},{2,4},{3,1},{4,2},{5,7},{7,5},{9,11},{10,12},{11,9},{12,10},... | collective-permute-start | bytes 1572872 | tf_op jit(solution)/shard_map/ppermute | solution.py:437
  159.3 35.0 %collective-permute-start.23 = (f32[1024,128]{1,0:T(8,128)S(1)}, f32[1024,128]{1,0:T(8,128)S(1)}, u32[]{:S(2)}, u32[]{:S(2)}) collective-permute-start(f32[1024,128]{1,0:T(8,128)S(1)} %payload.15.refs_4_), channel_id=1, source_target_pairs={{0,2},{2,0},{3,5},{4,6},{5,3},{6,4},{8,10},{10,8},{11,13},{12,14},... | collective-permute-start | bytes 1572872 | tf_op jit(solution)/shard_map/ppermute | solution.py:437
  166.6 11.0 %collective-permute-start.25 = (f32[2,256]{1,0:T(2,128)S(1)}, f32[2,256]{1,0:T(2,128)S(1)}, u32[]{:S(2)}, u32[]{:S(2)}) collective-permute-start(f32[2,256]{1,0:T(2,128)S(1)} %get-tuple-element.76.refs_0_), channel_id=1, source_target_pairs={{0,2},{1,3},{2,0},{3,1},{4,6},{5,7},{6,4},{7,5},{8,10},{9,11},{10,... | collective-permute-start | bytes 6152 | tf_op jit(solution)/shard_map/ppermute | solution.py:558
  166.7 10.9 %collective-permute-start.26 = (f32[2,256]{1,0:T(2,128)S(1)}, f32[2,256]{1,0:T(2,128)S(1)}, u32[]{:S(2)}, u32[]{:S(2)}) collective-permute-start(f32[2,256]{1,0:T(2,128)S(1)} %get-tuple-element.76.refs_0_), channel_id=1, source_target_pairs={{0,4},{1,5},{2,6},{3,7},{4,0},{5,1},{6,2},{7,3},{8,12},{9,13},{10,... | collective-permute-start | bytes 6152 | tf_op jit(solution)/shard_map/ppermute | solution.py:558
  169.9 9.8 %collective-permute-start.27 = (f32[2,256]{1,0:T(2,128)S(1)}, f32[2,256]{1,0:T(2,128)S(1)}, u32[]{:S(2)}, u32[]{:S(2)}) collective-permute-start(f32[2,256]{1,0:T(2,128)S(1)} %get-tuple-element.76.refs_0_), channel_id=1, source_target_pairs={{0,6},{1,7},{2,4},{3,5},{4,2},{5,3},{6,0},{7,1},{8,14},{9,15},{10,... | collective-permute-start | bytes 6152 | tf_op jit(solution)/shard_map/ppermute | solution.py:558
  180.4 5.8 %copy-start.3 = (bf16[8192,1024]{1,0:T(8,128)(2,1)S(1)}, bf16[8192,1024]{1,0:T(8,128)(2,1)}, u32[]{:S(2)}) copy-start(bf16[8192,1024]{1,0:T(8,128)(2,1)} %copy-done) | copy-start | bytes 50331652
  186.2 2.2 %copy-start.8 = (f32[8192,128]{1,0:T(8,128)S(1)}, f32[8192,128]{1,0:T(8,128)}, u32[]{:S(2)}) copy-start(f32[8192,128]{1,0:T(8,128)} %all-gather.7.cloned.1.call-done) | copy-start | bytes 12582916
Sparse Core Ops, SparseCore 0:
  10.2 67.0 all-gather.4
  91.9 51.6 all-gather.6

commit v12 on v10

--- a/solution.py
+++ b/solution.py
@@ -14,6 +14,7 @@
 HALO = 2 * NY
 LANES = 128
 BLOCK = 512
+PIECES = 4
 
 
 relax_rate = 0.5
@@ -153,29 +154,42 @@
         refs[2][...] = total[2 * cells : 2 * cells + 8] + total[2 * cells + 8 :]
 
 
-def own_rows(distribution, velocity, capacity, out, token, speeds, weight, sems):
-    modes, cells = velocity.shape[1], out.shape[1]
+def own_rows(distribution, velocity, capacity, out, token, field, speeds, weight, extra, sems):
+    modes, cells = field.shape
+    pieces = [pl.ds(r, modes // PIECES) for r in range(0, modes, modes // PIECES)]
     copies = [
         pltpu.make_async_copy(velocity, speeds, sems.at[0]),
         pltpu.make_async_copy(capacity, weight, sems.at[1]),
+    ]
+    copies += [
         pltpu.make_async_copy(
-            distribution.at[:, pl.ds(0, cells)], out.at[pl.ds(0, modes), :], sems.at[2]
-        ),
+            distribution.at[rows, pl.ds(0, cells)], field.at[rows, :], sems.at[2 + k]
+        )
+        for k, rows in enumerate(pieces)
     ]
     for copy in copies:
         copy.start()
     token[...] = jnp.zeros_like(token)
+    extra[...] = jnp.zeros_like(extra)
     for copy in copies[:2]:
         copy.wait()
     per = modes // LANES
-    out[modes:] = jnp.zeros((out.shape[0] - modes, LANES), jnp.float32)
     for d in range(2):
         for i in range(per):
             lanes = slice(i * LANES, (i + 1) * LANES)
-            out[modes + d * per + i : modes + d * per + i + 1, :] = (
-                speeds[d : d + 1, lanes] * weight[:, lanes]
-            )
-    copies[2].wait()
+            extra[d * per + i : d * per + i + 1, :] = speeds[d : d + 1, lanes] * weight[:, lanes]
+    onward = [
+        pltpu.make_async_copy(extra, out.at[pl.ds(modes, extra.shape[0]), :], sems.at[0])
+    ]
+    onward[0].start()
+    for k, rows in enumerate(pieces):
+        copies[2 + k].wait()
+        onward.append(
+            pltpu.make_async_copy(field.at[rows, :], out.at[rows, :], sems.at[2 + PIECES + k])
+        )
+        onward[-1].start()
+    for copy in onward:
+        copy.wait()
 
 
 def payload(numbers, slots, arrived, *refs):
@@ -194,7 +208,7 @@
 
     @pl.when(slot_here < 0)
     def _():
-        out[...] = arrived[...]
+        out[...] = arrived[: out.shape[0]]
 
 
 def pick(numbers, *refs):
@@ -241,14 +255,20 @@
 
 
 def last_sum(scale, arrived, base, other, out, value, sems):
-    cells = base.shape[1]
-    ahead = pltpu.make_async_copy(other, out.at[:, pl.ds(cells, cells)], sems.at[0])
-    ahead.start()
-    value[...] = base[...] - scale * arrived[...]
-    copy = pltpu.make_async_copy(value, out.at[:, pl.ds(0, cells)], sems.at[1])
-    copy.start()
-    ahead.wait()
-    copy.wait()
+    modes, cells = base.shape
+    copies = [pltpu.make_async_copy(other, out.at[:, pl.ds(cells, cells)], sems.at[0])]
+    copies[0].start()
+    for k in range(PIECES):
+        rows = pl.ds(k * modes // PIECES, modes // PIECES)
+        value[rows, :] = base[rows, :] - scale * arrived[rows, :]
+        copies.append(
+            pltpu.make_async_copy(
+                value.at[rows, :], out.at[rows, pl.ds(0, cells)], sems.at[1 + k]
+            )
+        )
+        copies[-1].start()
+    for copy in copies:
+        copy.wait()
 
 
 def strip_rows(distribution, leading, last):
@@ -501,7 +521,8 @@
                 arrived = self.arrived[1 - stream][step - 1]
                 kernel = functools.partial(payload, numbers, slots)
                 arrays = [arrived] + [self.terms[s] for s in slots]
-                (value,) = call(kernel, [arrived.shape], arrays)
+                shape = part if step == chips - 1 else arrived.shape
+                (value,) = call(kernel, [shape], arrays)
                 sent[stream] = along(stream, value)
             for stream in (0, 1):
                 self.arrived[stream].append(sent[stream])
@@ -548,10 +569,13 @@
         [distribution, velocity, cap],
         places=[HBM] * 3,
         scratch=[
+            pltpu.VMEM(part, jnp.float32),
             pltpu.VMEM((2, modes), jnp.float32),
             pltpu.VMEM((1, modes), jnp.float32),
-            pltpu.SemaphoreType.DMA((3,)),
+            pltpu.VMEM((extra, LANES), jnp.float32),
+            pltpu.SemaphoreType.DMA((2 + 2 * PIECES,)),
         ],
+        out_specs=[HBM, VMEM],
         room=56,
     )
     one = Round(None, time_step, True)
@@ -588,7 +612,10 @@
             strips = paired(*call(strip_pairs, [(HALO, modes)] * 2, strips))
         else:
             one.take(step, 2 if step == chips - 1 else 1)
-        one.multiply(step - 1)
+        if step == 2:
+            one.multiply(0)
+        if step > 1:
+            one.multiply(step - 1)
         if step == min(2, chips - 1):
             base_a, base_b = call(
                 first_rest,
@@ -645,7 +672,7 @@
         functools.partial(last_sum, step_size),
         [(modes, cells)],
         [*two.ends(), last_b],
-        scratch=[pltpu.VMEM(part, jnp.float32), pltpu.SemaphoreType.DMA((2,))],
+        scratch=[pltpu.VMEM(part, jnp.float32), pltpu.SemaphoreType.DMA((1 + PIECES,))],
         out_specs=[HBM],
     )
     return (updated, heat_flux)

time: 131 us -> 133 us (1.015)
  starting transfers between devices: 66.4 us -> 70.9 us
  waiting for transfers between devices: 25.8 us -> 23.4 us
    ppermute x19, starting transfers between devices: 13.3 us -> 20.4 us  [exchange(): lax.ppermute(value[i:j], 'mode', across)]
    ppermute x16, waiting for transfers between devices: 21.5 us -> 18.2 us  [along(): return lax.ppermute(value, 'mode', plan.pairs[stream])]
    ppermute x16, starting transfers between devices: 43.3 us -> 40.7 us  [along(): return lax.ppermute(value, 'mode', plan.pairs[stream])]
  transfers between devices with their start and end apart: 43 -> 43, of which waited for: 14 -> 14; matrix products, arithmetic and copies ran while one was open for 0% -> 0% of each run, Pallas kernels for 25% -> 24%
where the time goes in v12:
time: 133 us; the launch traced here: 132 us
  starting transfers between devices  70.9 us (53%)
  Pallas kernels  35.4 us (27%)
  waiting for transfers between devices  23.4 us (18%)
  between operations  1.63 us (1%)
    ppermute x16, starting transfers between devices, along(): return lax.ppermute(value, 'mode', plan.pairs[stream])  40.7 us
    pallas_call x55, Pallas kernels, __call__(): pl.pallas_call(body, out_shape=[jax.ShapeDtypeStruct(shape, jnp.float32)...  35.4 us
    ppermute x19, starting transfers between devices, exchange(): lax.ppermute(value[i:j], 'mode', across)  20.4 us
    ppermute x16, waiting for transfers between devices, along(): return lax.ppermute(value, 'mode', plan.pairs[stream])  18.2 us
    ppermute x4, starting transfers between devices, paired(): lax.ppermute(value, 'space', pairs + [(j, i) for i, j in pairs])  6.75 us
    ppermute x4, starting transfers between devices, over(): lax.ppermute(self.value, 'mode', [(i, i ^ bit) for i in range(self.device...  3.13 us
  transfers between devices with their start and end apart: 43, of which 14 were waited for; matrix products, arithmetic and copies ran while one was open for 0% of the time, Pallas kernels for 24%

profile of v12, /device:TPU:13, one launch (start us, length us, event | category | flops | bytes accessed | tf_op | source)
XLA Modules:
  0.0 132.4 jit_solution(7968092266756145221)
XLA Ops:
  0.6 2.5 %own_rows.1 = (f32[1040,128]{1,0:T(8,128)}, f32[8,128]{1,0:T(8,128)}) custom-call(f32[1024,256]{1,0:T(8,128)} %refs_0_.9, f32[2,1024]{1,0:T(2,128)} %refs_1_.2, f32[1,1024]{1,0:T(1,128)} %bitcast.4), custom_call_target="tpu_custom_call" | custom-call | flops 1024 | bytes 1024 | tf_op jit(solution)/shard_map/own_rows/pallas_call | solution.py:40
  3.2 3.2 %collective-permute-start.2 = (f32[1040,128]{1,0:T(8,128)}, f32[1040,128]{1,0:T(8,128)S(1)}, u32[]{:S(2)}, u32[]{:S(2)}) collective-permute-start(f32[1040,128]{1,0:T(8,128)} %get-tuple-element.41.refs_1_), channel_id=1, source_target_pairs={{0,2},{3,5},{4,6},{2,0},{5,3},{6,4},{8,10},{11,13},{12,14},{10,8},... | collective-permute-start | bytes 1597448 | tf_op jit(solution)/shard_map/ppermute | solution.py:486
  6.4 1.9 %collective-permute-start = (f32[1040,128]{1,0:T(8,128)}, f32[1040,128]{1,0:T(8,128)S(1)}, u32[]{:S(2)}, u32[]{:S(2)}) collective-permute-start(f32[1040,128]{1,0:T(8,128)} %get-tuple-element.41.refs_1_), channel_id=1, source_target_pairs={{1,3},{2,4},{5,7},{3,1},{4,2},{7,5},{9,11},{10,12},{13,15},{11,9},... | collective-permute-start | bytes 1597448 | tf_op jit(solution)/shard_map/ppermute | solution.py:486
  8.4 0.7 copy-done.3
  9.0 7.4 %load_and_products.1 = (f32[1024,128]{1,0:T(8,128)S(1)}, f32[1024,128]{1,0:T(8,128)S(1)}, f32[1024,128]{1,0:T(8,128)S(1)}, f32[1024,128]{1,0:T(8,128)S(1)}, f32[...) custom-call(bf16[8192,1024]{1,0:T(8,128)(2,1)} %refs_0_.6, ...), custom_call_target="tpu_custom_call" | custom-call | flops 1024 | bytes 1024 | tf_op jit(solution)/shard_map/load_and_products/pallas_call | solution.py:40
  16.4 2.6 %collective-permute-start.1 = (f32[1024,128]{1,0:T(8,128)S(1)}, f32[1024,128]{1,0:T(8,128)S(1)}, u32[]{:S(2)}, u32[]{:S(2)}) collective-permute-start(f32[1024,128]{1,0:T(8,128)S(1)} %get-tuple-element.44), channel_id=1, source_target_pairs={{0,1},{1,0},{2,3},{3,2},{4,5},{5,4},{6,7},{7,6},{8,9},{9,8},{10,11... | collective-permute-start | bytes 1572872 | tf_op jit(solution)/shard_map/ppermute | solution.py:483
  19.1 0.4 collective-permute-start.6
  19.6 0.7 collective-permute-done.refs_1_.refs_0_
  20.6 1.9 %collective-permute-start.9 = (f32[1040,128]{1,0:T(8,128)S(1)}, f32[1040,128]{1,0:T(8,128)S(1)}, u32[]{:S(2)}, u32[]{:S(2)}) collective-permute-start(f32[1040,128]{1,0:T(8,128)S(1)} %payload.12.refs_2_), channel_id=1, source_target_pairs={{1,3},{2,4},{5,7},{3,1},{4,2},{7,5},{9,11},{10,12},{13,15},{11,9},... | collective-permute-start | bytes 1597448 | tf_op jit(solution)/shard_map/ppermute | solution.py:486
  22.6 4.7 %collective-permute-start.3 = (f32[1040,128]{1,0:T(8,128)S(1)}, f32[1040,128]{1,0:T(8,128)S(1)}, u32[]{:S(2)}, u32[]{:S(2)}) collective-permute-start(f32[1040,128]{1,0:T(8,128)S(1)} %payload.13.refs_2_), channel_id=1, source_target_pairs={{0,2},{3,5},{4,6},{2,0},{5,3},{6,4},{8,10},{11,13},{12,14},{10,8},... | collective-permute-start | bytes 1597448 | tf_op jit(solution)/shard_map/ppermute | solution.py:486
  27.9 1.3 collective-permute-start.7
  29.2 2.1 %collective-permute-start.8 = (f32[32,1024]{1,0:T(8,128)S(1)}, f32[32,1024]{1,0:T(8,128)S(1)}, u32[]{:S(2)}, u32[]{:S(2)}) collective-permute-start(f32[32,1024]{1,0:T(8,128)S(1)} %get-tuple-element.55.refs_3_), channel_id=1, source_target_pairs={{8,16},{16,8},{9,17},{17,9},{10,18},{18,10},{11,19},{19,11},{12,20... | collective-permute-start | bytes 393224 | tf_op jit(solution)/shard_map/ppermute | solution.py:397
  31.4 1.6 %collective-permute-done.9.refs_0_.refs_2_ = f32[1040,128]{1,0:T(8,128)S(1)} collective-permute-done((f32[1040,128]{1,0:T(8,128)S(1)}, f32[1040,128]{1,0:T(8,128)S(1)}, u32[]{:S(2)}, u32[]{:S(2)}) %collective-permute-start.9) | collective-permute-done | bytes 532512 | tf_op jit(solution)/shard_map/ppermute | solution.py:486
  33.0 2.3 %collective-permute-start.12 = (f32[1040,128]{1,0:T(8,128)S(1)}, f32[1040,128]{1,0:T(8,128)S(1)}, u32[]{:S(2)}, u32[]{:S(2)}) collective-permute-start(f32[1040,128]{1,0:T(8,128)S(1)} %pick.6.refs_2_.refs_1_), channel_id=1, source_target_pairs={{0,1},{1,0},{2,3},{3,2},{4,5},{5,4},{6,7},{7,6},{8,9},{9,8},{10,11... | collective-permute-start | bytes 1597448 | tf_op jit(solution)/shard_map/ppermute | solution.py:483
  35.4 2.2 %collective-permute-start.11 = (f32[1040,128]{1,0:T(8,128)S(1)}, f32[1040,128]{1,0:T(8,128)S(1)}, u32[]{:S(2)}, u32[]{:S(2)}) collective-permute-start(f32[1040,128]{1,0:T(8,128)S(1)} %payload.14.refs_2_), channel_id=1, source_target_pairs={{0,2},{3,5},{4,6},{2,0},{5,3},{6,4},{8,10},{11,13},{12,14},{10,8},... | collective-permute-start | bytes 1597448 | tf_op jit(solution)/shard_map/ppermute | solution.py:486
  37.9 1.9 %collective-permute-start.10 = (f32[1040,128]{1,0:T(8,128)S(1)}, f32[1040,128]{1,0:T(8,128)S(1)}, u32[]{:S(2)}, u32[]{:S(2)}) collective-permute-start(f32[1040,128]{1,0:T(8,128)S(1)} %payload.15.refs_3_), channel_id=1, source_target_pairs={{1,3},{2,4},{5,7},{3,1},{4,2},{7,5},{9,11},{10,12},{13,15},{11,9},... | collective-permute-start | bytes 1597448 | tf_op jit(solution)/shard_map/ppermute | solution.py:486
  40.0 3.3 %collective-permute-start.18 = (f32[1040,128]{1,0:T(8,128)S(1)}, f32[1040,128]{1,0:T(8,128)S(1)}, u32[]{:S(2)}, u32[]{:S(2)}) collective-permute-start(f32[1040,128]{1,0:T(8,128)S(1)} %pick.7.refs_3_.refs_1_), channel_id=1, source_target_pairs={{0,1},{1,0},{2,3},{3,2},{4,5},{5,4},{6,7},{7,6},{8,9},{9,8},{10,11... | collective-permute-start | bytes 1597448 | tf_op jit(solution)/shard_map/ppermute | solution.py:483
  43.4 1.4 %two_blocks.8.refs_3_.refs_4_ = f32[272,1024]{1,0:T(8,128)S(1)} custom-call(bf16[8192,1024]{1,0:T(8,128)(2,1)S(1)} %get-tuple-element.45.refs_2_.refs_0_, f32[1040,128]{1,0:T(8,128)S(1)} %copy-done.2, f32[1040,128]{1,0:T(8,128)S(1)} %collective-permute-done.13.refs_2_, f32[1040,128]{1,0:T(8,128)S(1)} %pick.7.refs_3_.refs_1_), custom_call_target="tpu_custom_call" | custom-call | flops 1024 | bytes 1024 | tf_op jit(solution)/shard_map/two_blocks/pallas_call | solution.py:40
  44.8 1.4 %two_blocks.9.refs_5_.refs_3_ = f32[272,1024]{1,0:T(8,128)S(1)} custom-call(bf16[8192,1024]{1,0:T(8,128)(2,1)S(1)} %get-tuple-element.45.refs_2_.refs_0_, f32[1040,128]{1,0:T(8,128)S(1)} %pick.6.refs_2_.refs_1_, f32[1040,128]{1,0:T(8,128)S(1)} %collective-permute-done.12.refs_2_, f32[272,1024]{1,0:T(8,128)S(1)} %two_blocks.8.refs_3_.refs_4_, ...), custom_call_target="tpu_custom_call" | custom-call | flops 1024 | bytes 1024 | tf_op jit(solution)/shard_map/two_blocks/pallas_call | solution.py:40
  46.2 2.0 %first_rest.1 = (f32[1024,128]{1,0:T(8,128)S(1)}, f32[1024,128]{1,0:T(8,128)S(1)}) custom-call(f32[1024,256]{1,0:T(8,128)S(1)} %copy-done, bf16[1024,128]{1,0:T(8,128)(2,1)S(1)} %strip_columns.2.refs_3_.refs_1_, bf16[640,1024]{1,0:T(8,128)(2,1)S(1)} %copy-done.1, f32[8,1024]{1,0:T(8,128)S(1)} %maximum_maximum_fusion.refs_3_.refs_5_, s32[1,256]{1,0:T(1,128)S(1)} %bitcast.2, ...), custom_call_target="tpu_custom_call" | custom-call | flops 1024 | bytes 1024 | tf_op jit(solution)/shard_map/first_rest/pallas_call | solution.py:40
  48.4 1.9 %collective-permute-start.15 = (f32[1024,128]{1,0:T(8,128)S(1)}, f32[1024,128]{1,0:T(8,128)S(1)}, u32[]{:S(2)}, u32[]{:S(2)}) collective-permute-start(f32[1024,128]{1,0:T(8,128)S(1)} %payload.16.refs_3_), channel_id=1, source_target_pairs={{1,3},{2,4},{5,7},{3,1},{4,2},{7,5},{9,11},{10,12},{13,15},{11,9},... | collective-permute-start | bytes 1572872 | tf_op jit(solution)/shard_map/ppermute | solution.py:486
  50.3 1.2 collective-permute-done.10.refs_0_.refs_3_
  51.7 3.2 %collective-permute-start.14 = (f32[1024,128]{1,0:T(8,128)S(1)}, f32[1024,128]{1,0:T(8,128)S(1)}, u32[]{:S(2)}, u32[]{:S(2)}) collective-permute-start(f32[1024,128]{1,0:T(8,128)S(1)} %payload.17.refs_4_), channel_id=1, source_target_pairs={{0,2},{3,5},{4,6},{2,0},{5,3},{6,4},{8,10},{11,13},{12,14},{10,8},... | collective-permute-start | bytes 1572872 | tf_op jit(solution)/shard_map/ppermute | solution.py:486
  55.2 2.4 %collective-permute-start.17 = (f32[520,128]{1,0:T(8,128)S(1)}, f32[520,128]{1,0:T(8,128)S(1)}, u32[]{:S(2)}, u32[]{:S(2)}) collective-permute-start(f32[520,128]{1,0:T(8,128)S(1)} %get-tuple-element.80), channel_id=1, source_target_pairs={{0,1},{1,0},{2,3},{3,2},{4,5},{5,4},{6,7},{7,6},{8,9},{9,8},{10,11... | collective-permute-start | bytes 798728 | tf_op jit(solution)/shard_map/ppermute | solution.py:483
  57.6 1.4 %two_blocks.10.refs_4_.refs_6_ = f32[272,1024]{1,0:T(8,128)S(1)} custom-call(bf16[8192,1024]{1,0:T(8,128)(2,1)S(1)} %get-tuple-element.45.refs_2_.refs_0_, f32[1040,128]{1,0:T(8,128)S(1)} %pick.7.refs_3_.refs_1_, f32[1040,128]{1,0:T(8,128)S(1)} %collective-permute-done.18.refs_2_, f32[272,1024]{1,0:T(8,128)S(1)} %two_blocks.9.refs_5_.refs_3_, ...), custom_call_target="tpu_custom_call" | custom-call | flops 1024 | bytes 1024 | tf_op jit(solution)/shard_map/two_blocks/pallas_call | solution.py:40
  59.1 1.5 %two_blocks.11 = (f32[1024,128]{1,0:T(8,128)S(1)}, f32[32,1024]{1,0:T(8,128)S(1)}, f32[8,1024]{1,0:T(8,128)S(1)}) custom-call(bf16[8192,1024]{1,0:T(8,128)(2,1)S(1)} %get-tuple-element.45.refs_2_.refs_0_, f32[1040,128]{1,0:T(8,128)S(1)} %pick.8.refs_4_.refs_1_, f32[520,128]{1,0:T(8,128)S(1)} %collective-permute-done.16.refs_2_, ...), custom_call_target="tpu_custom_call" | custom-call | flops 1024 | bytes 1024 | tf_op jit(solution)/shard_map/two_blocks/pallas_call | solution.py:40
  60.6 1.3 slot_products.4
  61.9 0.4 collective-permute-start.20
  62.4 5.0 %collective-permute-done.14.refs_0_ = f32[1024,128]{1,0:T(8,128)S(1)} collective-permute-done((f32[1024,128]{1,0:T(8,128)S(1)}, f32[1024,128]{1,0:T(8,128)S(1)}, u32[]{:S(2)}, u32[]{:S(2)}) %collective-permute-start.14) | collective-permute-done | bytes 524320 | tf_op jit(solution)/shard_map/ppermute | solution.py:486
  67.7 2.8 %collective-permute-start.23 = (f32[1024,128]{1,0:T(8,128)S(1)}, f32[1024,128]{1,0:T(8,128)S(1)}, u32[]{:S(2)}, u32[]{:S(2)}) collective-permute-start(f32[1024,128]{1,0:T(8,128)S(1)} %get-tuple-element.61.refs_2_.refs_1_), channel_id=1, source_target_pairs={{0,2},{3,5},{4,6},{2,0},{5,3},{6,4},{8,10},{11,13},{12,14},{10,8},... | collective-permute-start | bytes 1572872 | tf_op jit(solution)/shard_map/ppermute | solution.py:486
  70.5 1.9 %collective-permute-start.19 = (f32[1024,128]{1,0:T(8,128)S(1)}, f32[1024,128]{1,0:T(8,128)S(1)}, u32[]{:S(2)}, u32[]{:S(2)}) collective-permute-start(f32[1024,128]{1,0:T(8,128)S(1)} %get-tuple-element.61.refs_2_.refs_1_), channel_id=1, source_target_pairs={{1,3},{2,4},{5,7},{3,1},{4,2},{7,5},{9,11},{10,12},{13,15},{11,9},... | collective-permute-start | bytes 1572872 | tf_op jit(solution)/shard_map/ppermute | solution.py:486
  72.4 1.3 slot_products.5
  73.7 1.3 collective-permute-start.25
  75.1 1.3 collective-permute-start.21
  76.3 2.1 %collective-permute-start.22 = (f32[32,1024]{1,0:T(8,128)S(1)}, f32[32,1024]{1,0:T(8,128)S(1)}, u32[]{:S(2)}, u32[]{:S(2)}) collective-permute-start(f32[32,1024]{1,0:T(8,128)S(1)} %get-tuple-element.67.refs_2_), channel_id=1, source_target_pairs={{8,16},{16,8},{9,17},{17,9},{10,18},{18,10},{11,19},{19,11},{12,20... | collective-permute-start | bytes 393224 | tf_op jit(solution)/shard_map/ppermute | solution.py:397
  78.4 2.0 %collective-permute-done.23.refs_0_ = f32[1024,128]{1,0:T(8,128)S(1)} collective-permute-done((f32[1024,128]{1,0:T(8,128)S(1)}, f32[1024,128]{1,0:T(8,128)S(1)}, u32[]{:S(2)}, u32[]{:S(2)}) %collective-permute-start.23) | collective-permute-done | bytes 524320 | tf_op jit(solution)/shard_map/ppermute | solution.py:486
  80.5 1.9 %collective-permute-start.27 = (f32[1024,128]{1,0:T(8,128)S(1)}, f32[1024,128]{1,0:T(8,128)S(1)}, u32[]{:S(2)}, u32[]{:S(2)}) collective-permute-start(f32[1024,128]{1,0:T(8,128)S(1)} %payload.18.refs_2_), channel_id=1, source_target_pairs={{1,3},{2,4},{5,7},{3,1},{4,2},{7,5},{9,11},{10,12},{13,15},{11,9},... | collective-permute-start | bytes 1572872 | tf_op jit(solution)/shard_map/ppermute | solution.py:486
  82.5 1.4 %collective-permute-done.22.refs_1_ = f32[32,1024]{1,0:T(8,128)S(1)} collective-permute-done((f32[32,1024]{1,0:T(8,128)S(1)}, f32[32,1024]{1,0:T(8,128)S(1)}, u32[]{:S(2)}, u32[]{:S(2)}) %collective-permute-start.22) | collective-permute-done | bytes 131104 | tf_op jit(solution)/shard_map/ppermute | solution.py:397
  84.1 0.4 collective-permute-done.19.refs_0_.refs_1_
  84.5 2.9 %collective-permute-start.24 = (f32[1024,128]{1,0:T(8,128)S(1)}, f32[1024,128]{1,0:T(8,128)S(1)}, u32[]{:S(2)}, u32[]{:S(2)}) collective-permute-start(f32[1024,128]{1,0:T(8,128)S(1)} %payload.19.refs_2_), channel_id=1, source_target_pairs={{0,2},{3,5},{4,6},{2,0},{5,3},{6,4},{8,10},{11,13},{12,14},{10,8},... | collective-permute-start | bytes 1572872 | tf_op jit(solution)/shard_map/ppermute | solution.py:486
  87.6 1.3 slot_products.6
  88.8 2.1 %collective-permute-start.29 = (f32[1024,128]{1,0:T(8,128)S(1)}, f32[1024,128]{1,0:T(8,128)S(1)}, u32[]{:S(2)}, u32[]{:S(2)}) collective-permute-start(f32[1024,128]{1,0:T(8,128)S(1)} %get-tuple-element.69.refs_2_), channel_id=1, source_target_pairs={{0,1},{1,0},{2,3},{3,2},{4,5},{5,4},{6,7},{7,6},{8,9},{9,8},{10,11... | collective-permute-start | bytes 1572872 | tf_op jit(solution)/shard_map/ppermute | solution.py:483
  91.0 1.3 slot_products.7
  92.3 2.7 %second_rest.1 = (f32[1024,128]{1,0:T(8,128)S(1)}, f32[1024,128]{1,0:T(8,128)S(1)}, f32[2,256]{1,0:T(2,128)S(1)}) custom-call(f32[1024,256]{1,0:T(8,128)S(1)} %copy-done, f32[1024,128]{1,0:T(8,128)S(1)} %get-tuple-element.58.refs_1_, f32[1024,128]{1,0:T(8,128)S(1)} %get-tuple-element.61.refs_2_.refs_1_, bf16[1024,128]{1,0:T(8,128)(2,1)S(1)} %strip_columns.3.refs_2_.refs_3_, ...), custom_call_target="tpu_custom_call" | custom-call | flops 1024 | bytes 1024 | tf_op jit(solution)/shard_map/second_rest/pallas_call | solution.py:40
  95.0 0.6 collective-permute-start.26
  95.6 0.8 collective-permute-done.26.refs_1_
  96.4 0.3 collective-permute-start.38
  96.7 2.8 %collective-permute-start.37 = (f32[1024,128]{1,0:T(8,128)S(1)}, f32[1024,128]{1,0:T(8,128)S(1)}, u32[]{:S(2)}, u32[]{:S(2)}) collective-permute-start(f32[1024,128]{1,0:T(8,128)S(1)} %pick.9.refs_2_.refs_1_), channel_id=1, source_target_pairs={{0,1},{1,0},{2,3},{3,2},{4,5},{5,4},{6,7},{7,6},{8,9},{9,8},{10,11... | collective-permute-start | bytes 1572872 | tf_op jit(solution)/shard_map/ppermute | solution.py:483
  99.7 4.1 %collective-permute-start.33 = (f32[1024,128]{1,0:T(8,128)S(1)}, f32[1024,128]{1,0:T(8,128)S(1)}, u32[]{:S(2)}, u32[]{:S(2)}) collective-permute-start(f32[1024,128]{1,0:T(8,128)S(1)} %payload.20.refs_2_), channel_id=1, source_target_pairs={{0,2},{3,5},{4,6},{2,0},{5,3},{6,4},{8,10},{11,13},{12,14},{10,8},... | collective-permute-start | bytes 1572872 | tf_op jit(solution)/shard_map/ppermute | solution.py:486
  103.9 1.9 %collective-permute-start.28 = (f32[1024,128]{1,0:T(8,128)S(1)}, f32[1024,128]{1,0:T(8,128)S(1)}, u32[]{:S(2)}, u32[]{:S(2)}) collective-permute-start(f32[1024,128]{1,0:T(8,128)S(1)} %payload.21.refs_2_), channel_id=1, source_target_pairs={{1,3},{2,4},{5,7},{3,1},{4,2},{7,5},{9,11},{10,12},{13,15},{11,9},... | collective-permute-start | bytes 1572872 | tf_op jit(solution)/shard_map/ppermute | solution.py:486
  106.6 1.0 collective-permute-done.36.refs_3_
  107.6 2.5 %collective-permute-start.31 = (f32[2,256]{1,0:T(2,128)S(1)}, f32[2,256]{1,0:T(2,128)S(1)}, u32[]{:S(2)}, u32[]{:S(2)}) collective-permute-start(f32[2,256]{1,0:T(2,128)S(1)} %get-tuple-element.74.refs_0_), channel_id=1, source_target_pairs={{0,4},{1,5},{2,6},{3,7},{4,0},{5,1},{6,2},{7,3},{8,12},{9,13},{10,... | collective-permute-start | bytes 6152 | tf_op jit(solution)/shard_map/ppermute | solution.py:687
  110.3 1.3 two_blocks.12.refs_3_
  111.6 2.4 %collective-permute-done.33.refs_0_.refs_1_ = f32[1024,128]{1,0:T(8,128)S(1)} collective-permute-done((f32[1024,128]{1,0:T(8,128)S(1)}, f32[1024,128]{1,0:T(8,128)S(1)}, u32[]{:S(2)}, u32[]{:S(2)}) %collective-permute-start.33) | collective-permute-done | bytes 524320 | tf_op jit(solution)/shard_map/ppermute | solution.py:486
  114.0 1.9 %collective-permute-start.40 = (f32[1024,128]{1,0:T(8,128)S(1)}, f32[1024,128]{1,0:T(8,128)S(1)}, u32[]{:S(2)}, u32[]{:S(2)}) collective-permute-start(f32[1024,128]{1,0:T(8,128)S(1)} %payload.22.refs_4_), channel_id=1, source_target_pairs={{1,3},{2,4},{5,7},{3,1},{4,2},{7,5},{9,11},{10,12},{13,15},{11,9},... | collective-permute-start | bytes 1572872 | tf_op jit(solution)/shard_map/ppermute | solution.py:486
  116.0 1.7 %collective-permute-done.31.refs_2_ = f32[2,256]{1,0:T(2,128)S(1)} collective-permute-done((f32[2,256]{1,0:T(2,128)S(1)}, f32[2,256]{1,0:T(2,128)S(1)}, u32[]{:S(2)}, u32[]{:S(2)}) %collective-permute-start.31) | collective-permute-done | bytes 2080 | tf_op jit(solution)/shard_map/ppermute | solution.py:687
  117.6 0.6 add_all.3
  118.3 2.2 %collective-permute-start.39 = (f32[1024,128]{1,0:T(8,128)S(1)}, f32[1024,128]{1,0:T(8,128)S(1)}, u32[]{:S(2)}, u32[]{:S(2)}) collective-permute-start(f32[1024,128]{1,0:T(8,128)S(1)} %payload.23.refs_4_), channel_id=1, source_target_pairs={{0,2},{3,5},{4,6},{2,0},{5,3},{6,4},{8,10},{11,13},{12,14},{10,8},... | collective-permute-start | bytes 1572872 | tf_op jit(solution)/shard_map/ppermute | solution.py:486
  120.9 1.3 collective-permute-start.42
  122.2 1.3 %two_blocks.13.refs_3_.refs_4_ = f32[256,1024]{1,0:T(8,128)S(1)} custom-call(bf16[8192,1024]{1,0:T(8,128)(2,1)S(1)} %get-tuple-element.45.refs_2_.refs_0_, f32[1024,128]{1,0:T(8,128)S(1)} %get-tuple-element.61.refs_2_.refs_1_, f32[1024,128]{1,0:T(8,128)S(1)} %pass_on.2.refs_1_.refs_2_, f32[256,1024]{1,0:T(8,128)S(1)} %two_blocks.12.refs_3_, ...), custom_call_target="tpu_custom_call" | custom-call | flops 1024 | bytes 1024 | tf_op jit(solution)/shard_map/two_blocks/pallas_call | solution.py:40
  123.5 1.3 two_blocks.14.refs_4_.refs_6_
  124.9 1.4 %two_blocks.15.refs_3_.refs_2_ = f32[1024,128]{1,0:T(8,128)S(1)} custom-call(bf16[8192,1024]{1,0:T(8,128)(2,1)S(1)} %get-tuple-element.45.refs_2_.refs_0_, f32[1024,128]{1,0:T(8,128)S(1)} %pick.11.refs_4_.refs_1_, f32[512,128]{1,0:T(8,128)S(1)} %collective-permute-done.41.refs_2_, f32[512,128]{1,0:T(8,128)S(1)} %collective-permute-done.42.refs_3_, ...), custom_call_target="tpu_custom_call" | custom-call | flops 1024 | bytes 1024 | tf_op jit(solution)/shard_map/two_blocks/pallas_call | solution.py:40
  126.4 4.8 %collective-permute-done.39.refs_0_ = f32[1024,128]{1,0:T(8,128)S(1)} collective-permute-done((f32[1024,128]{1,0:T(8,128)S(1)}, f32[1024,128]{1,0:T(8,128)S(1)}, u32[]{:S(2)}, u32[]{:S(2)}) %collective-permute-start.39) | collective-permute-done | bytes 524320 | tf_op jit(solution)/shard_map/ppermute | solution.py:486
  131.2 1.0 last_sum.1
  (98 shorter events, 4.8 us)
Async XLA Ops:
  0.6 7.7 %copy-start = (f32[1024,256]{1,0:T(8,128)S(1)}, f32[1024,256]{1,0:T(8,128)}, u32[]{:S(2)}) copy-start(f32[1024,256]{1,0:T(8,128)} %refs_0_.9) | copy-start | bytes 3145732
  3.2 16.3 %collective-permute-start.2 = (f32[1040,128]{1,0:T(8,128)}, f32[1040,128]{1,0:T(8,128)S(1)}, u32[]{:S(2)}, u32[]{:S(2)}) collective-permute-start(f32[1040,128]{1,0:T(8,128)} %get-tuple-element.41.refs_1_), channel_id=1, source_target_pairs={{0,2},{3,5},{4,6},{2,0},{5,3},{6,4},{8,10},{11,13},{12,14},{10,8},... | collective-permute-start | bytes 1597448 | tf_op jit(solution)/shard_map/ppermute | solution.py:486
  6.4 13.9 %collective-permute-start = (f32[1040,128]{1,0:T(8,128)}, f32[1040,128]{1,0:T(8,128)S(1)}, u32[]{:S(2)}, u32[]{:S(2)}) collective-permute-start(f32[1040,128]{1,0:T(8,128)} %get-tuple-element.41.refs_1_), channel_id=1, source_target_pairs={{1,3},{2,4},{5,7},{3,1},{4,2},{7,5},{9,11},{10,12},{13,15},{11,9},... | collective-permute-start | bytes 1597448 | tf_op jit(solution)/shard_map/ppermute | solution.py:486
  8.3 0.7 copy-start.3
  16.4 4.1 %collective-permute-start.1 = (f32[1024,128]{1,0:T(8,128)S(1)}, f32[1024,128]{1,0:T(8,128)S(1)}, u32[]{:S(2)}, u32[]{:S(2)}) collective-permute-start(f32[1024,128]{1,0:T(8,128)S(1)} %get-tuple-element.44), channel_id=1, source_target_pairs={{0,1},{1,0},{2,3},{3,2},{4,5},{5,4},{6,7},{7,6},{8,9},{9,8},{10,11... | collective-permute-start | bytes 1572872 | tf_op jit(solution)/shard_map/ppermute | solution.py:483
  19.0 8.3 %collective-permute-start.4 = (f32[1024,128]{1,0:T(8,128)S(1)}, f32[1024,128]{1,0:T(8,128)S(1)}, u32[]{:S(2)}, u32[]{:S(2)}) collective-permute-start(f32[1024,128]{1,0:T(8,128)S(1)} %get-tuple-element.47), channel_id=1, source_target_pairs={{0,1},{1,0},{2,3},{3,2},{4,5},{5,4},{6,7},{7,6},{8,9},{9,8},{10,11... | collective-permute-start | bytes 1572872 | tf_op jit(solution)/shard_map/ppermute | solution.py:483
  19.1 8.3 %collective-permute-start.6 = (f32[1024,128]{1,0:T(8,128)S(1)}, f32[1024,128]{1,0:T(8,128)S(1)}, u32[]{:S(2)}, u32[]{:S(2)}) collective-permute-start(f32[1024,128]{1,0:T(8,128)S(1)} %get-tuple-element.51), channel_id=1, source_target_pairs={{0,1},{1,0},{2,3},{3,2},{4,5},{5,4},{6,7},{7,6},{8,9},{9,8},{10,11... | collective-permute-start | bytes 1572872 | tf_op jit(solution)/shard_map/ppermute | solution.py:483
  19.5 8.0 %collective-permute-start.5 = (f32[1024,128]{1,0:T(8,128)S(1)}, f32[1024,128]{1,0:T(8,128)S(1)}, u32[]{:S(2)}, u32[]{:S(2)}) collective-permute-start(f32[1024,128]{1,0:T(8,128)S(1)} %get-tuple-element.49), channel_id=1, source_target_pairs={{0,1},{1,0},{2,3},{3,2},{4,5},{5,4},{6,7},{7,6},{8,9},{9,8},{10,11... | collective-permute-start | bytes 1572872 | tf_op jit(solution)/shard_map/ppermute | solution.py:483
  20.6 12.4 %collective-permute-start.9 = (f32[1040,128]{1,0:T(8,128)S(1)}, f32[1040,128]{1,0:T(8,128)S(1)}, u32[]{:S(2)}, u32[]{:S(2)}) collective-permute-start(f32[1040,128]{1,0:T(8,128)S(1)} %payload.12.refs_2_), channel_id=1, source_target_pairs={{1,3},{2,4},{5,7},{3,1},{4,2},{7,5},{9,11},{10,12},{13,15},{11,9},... | collective-permute-start | bytes 1597448 | tf_op jit(solution)/shard_map/ppermute | solution.py:486
  22.6 15.2 %collective-permute-start.3 = (f32[1040,128]{1,0:T(8,128)S(1)}, f32[1040,128]{1,0:T(8,128)S(1)}, u32[]{:S(2)}, u32[]{:S(2)}) collective-permute-start(f32[1040,128]{1,0:T(8,128)S(1)} %payload.13.refs_2_), channel_id=1, source_target_pairs={{0,2},{3,5},{4,6},{2,0},{5,3},{6,4},{8,10},{11,13},{12,14},{10,8},... | collective-permute-start | bytes 1597448 | tf_op jit(solution)/shard_map/ppermute | solution.py:486
  27.5 3.8 %copy-start.2 = (f32[1040,128]{1,0:T(8,128)S(1)}, f32[1040,128]{1,0:T(8,128)}, u32[]{:S(2)}) copy-start(f32[1040,128]{1,0:T(8,128)} %get-tuple-element.41.refs_1_) | copy-start | bytes 1597444
  27.9 7.5 %collective-permute-start.7 = (f32[32,1024]{1,0:T(8,128)S(1)}, f32[32,1024]{1,0:T(8,128)S(1)}, u32[]{:S(2)}, u32[]{:S(2)}) collective-permute-start(f32[32,1024]{1,0:T(8,128)S(1)} %get-tuple-element.54), channel_id=1, source_target_pairs={{0,8},{16,24},{8,0},{24,16},{1,9},{17,25},{9,1},{25,17},{2,10},{18... | collective-permute-start | bytes 393224 | tf_op jit(solution)/shard_map/ppermute | solution.py:397
  29.2 8.5 %collective-permute-start.8 = (f32[32,1024]{1,0:T(8,128)S(1)}, f32[32,1024]{1,0:T(8,128)S(1)}, u32[]{:S(2)}, u32[]{:S(2)}) collective-permute-start(f32[32,1024]{1,0:T(8,128)S(1)} %get-tuple-element.55.refs_3_), channel_id=1, source_target_pairs={{8,16},{16,8},{9,17},{17,9},{10,18},{18,10},{11,19},{19,11},{12,20... | collective-permute-start | bytes 393224 | tf_op jit(solution)/shard_map/ppermute | solution.py:397
  31.3 12.1 %collective-permute-start.13 = (f32[1040,128]{1,0:T(8,128)S(1)}, f32[1040,128]{1,0:T(8,128)S(1)}, u32[]{:S(2)}, u32[]{:S(2)}) collective-permute-start(f32[1040,128]{1,0:T(8,128)S(1)} %copy-done.2), channel_id=1, source_target_pairs={{0,1},{1,0},{2,3},{3,2},{4,5},{5,4},{6,7},{7,6},{8,9},{9,8},{10,11... | collective-permute-start | bytes 1597448 | tf_op jit(solution)/shard_map/ppermute | solution.py:483
  33.0 11.8 %collective-permute-start.12 = (f32[1040,128]{1,0:T(8,128)S(1)}, f32[1040,128]{1,0:T(8,128)S(1)}, u32[]{:S(2)}, u32[]{:S(2)}) collective-permute-start(f32[1040,128]{1,0:T(8,128)S(1)} %pick.6.refs_2_.refs_1_), channel_id=1, source_target_pairs={{0,1},{1,0},{2,3},{3,2},{4,5},{5,4},{6,7},{7,6},{8,9},{9,8},{10,11... | collective-permute-start | bytes 1597448 | tf_op jit(solution)/shard_map/ppermute | solution.py:483
  35.4 12.9 %collective-permute-start.11 = (f32[1040,128]{1,0:T(8,128)S(1)}, f32[1040,128]{1,0:T(8,128)S(1)}, u32[]{:S(2)}, u32[]{:S(2)}) collective-permute-start(f32[1040,128]{1,0:T(8,128)S(1)} %payload.14.refs_2_), channel_id=1, source_target_pairs={{0,2},{3,5},{4,6},{2,0},{5,3},{6,4},{8,10},{11,13},{12,14},{10,8},... | collective-permute-start | bytes 1597448 | tf_op jit(solution)/shard_map/ppermute | solution.py:486
  37.8 2.1 %copy-start.5 = (f32[2,1024]{1,0:T(2,128)S(1)}, f32[2,1024]{1,0:T(2,128)}, u32[]{:S(2)}) copy-start(f32[2,1024]{1,0:T(2,128)} %refs_1_.2) | copy-start | bytes 24580
  37.8 2.1 %copy-start.6 = (f32[1024]{0:T(1024)S(1)}, f32[1024]{0:T(1024)}, u32[]{:S(2)}) copy-start(f32[1024]{0:T(1024)} %param.9) | copy-start | bytes 12292
  37.9 13.6 %collective-permute-start.10 = (f32[1040,128]{1,0:T(8,128)S(1)}, f32[1040,128]{1,0:T(8,128)S(1)}, u32[]{:S(2)}, u32[]{:S(2)}) collective-permute-start(f32[1040,128]{1,0:T(8,128)S(1)} %payload.15.refs_3_), channel_id=1, source_target_pairs={{1,3},{2,4},{5,7},{3,1},{4,2},{7,5},{9,11},{10,12},{13,15},{11,9},... | collective-permute-start | bytes 1597448 | tf_op jit(solution)/shard_map/ppermute | solution.py:486
  40.0 17.6 %collective-permute-start.18 = (f32[1040,128]{1,0:T(8,128)S(1)}, f32[1040,128]{1,0:T(8,128)S(1)}, u32[]{:S(2)}, u32[]{:S(2)}) collective-permute-start(f32[1040,128]{1,0:T(8,128)S(1)} %pick.7.refs_3_.refs_1_), channel_id=1, source_target_pairs={{0,1},{1,0},{2,3},{3,2},{4,5},{5,4},{6,7},{7,6},{8,9},{9,8},{10,11... | collective-permute-start | bytes 1597448 | tf_op jit(solution)/shard_map/ppermute | solution.py:483
  44.8 1.4 %copy-start.1 = (bf16[640,1024]{1,0:T(8,128)(2,1)S(1)}, bf16[640,1024]{1,0:T(8,128)(2,1)}, u32[]{:S(2)}) copy-start(bf16[640,1024]{1,0:T(8,128)(2,1)} %constant.4.clone.refs_2_.refs_4_) | copy-start | bytes 3932164
  44.8 1.4 %copy-start.4 = (s32[256]{0:T(256)S(1)}, s32[256]{0:T(256)}, u32[]{:S(2)}) copy-start(s32[256]{0:T(256)} %param.10) | copy-start | bytes 3076
  48.4 14.0 %collective-permute-start.15 = (f32[1024,128]{1,0:T(8,128)S(1)}, f32[1024,128]{1,0:T(8,128)S(1)}, u32[]{:S(2)}, u32[]{:S(2)}) collective-permute-start(f32[1024,128]{1,0:T(8,128)S(1)} %payload.16.refs_3_), channel_id=1, source_target_pairs={{1,3},{2,4},{5,7},{3,1},{4,2},{7,5},{9,11},{10,12},{13,15},{11,9},... | collective-permute-start | bytes 1572872 | tf_op jit(solution)/shard_map/ppermute | solution.py:486
  51.7 15.8 %collective-permute-start.14 = (f32[1024,128]{1,0:T(8,128)S(1)}, f32[1024,128]{1,0:T(8,128)S(1)}, u32[]{:S(2)}, u32[]{:S(2)}) collective-permute-start(f32[1024,128]{1,0:T(8,128)S(1)} %payload.17.refs_4_), channel_id=1, source_target_pairs={{0,2},{3,5},{4,6},{2,0},{5,3},{6,4},{8,10},{11,13},{12,14},{10,8},... | collective-permute-start | bytes 1572872 | tf_op jit(solution)/shard_map/ppermute | solution.py:486
  55.2 3.9 %collective-permute-start.17 = (f32[520,128]{1,0:T(8,128)S(1)}, f32[520,128]{1,0:T(8,128)S(1)}, u32[]{:S(2)}, u32[]{:S(2)}) collective-permute-start(f32[520,128]{1,0:T(8,128)S(1)} %get-tuple-element.80), channel_id=1, source_target_pairs={{0,1},{1,0},{2,3},{3,2},{4,5},{5,4},{6,7},{7,6},{8,9},{9,8},{10,11... | collective-permute-start | bytes 798728 | tf_op jit(solution)/shard_map/ppermute | solution.py:483
  57.6 1.5 %collective-permute-start.16 = (f32[520,128]{1,0:T(8,128)S(1)}, f32[520,128]{1,0:T(8,128)S(1)}, u32[]{:S(2)}, u32[]{:S(2)}) collective-permute-start(f32[520,128]{1,0:T(8,128)S(1)} %get-tuple-element.81), channel_id=1, source_target_pairs={{0,1},{1,0},{2,3},{3,2},{4,5},{5,4},{6,7},{7,6},{8,9},{9,8},{10,11... | collective-permute-start | bytes 798728 | tf_op jit(solution)/shard_map/ppermute | solution.py:483
  61.9 13.0 %collective-permute-start.20 = (f32[1024,128]{1,0:T(8,128)S(1)}, f32[1024,128]{1,0:T(8,128)S(1)}, u32[]{:S(2)}, u32[]{:S(2)}) collective-permute-start(f32[1024,128]{1,0:T(8,128)S(1)} %get-tuple-element.60.refs_3_), channel_id=1, source_target_pairs={{0,1},{1,0},{2,3},{3,2},{4,5},{5,4},{6,7},{7,6},{8,9},{9,8},{10,11... | collective-permute-start | bytes 1572872 | tf_op jit(solution)/shard_map/ppermute | solution.py:483
  67.7 12.8 %collective-permute-start.23 = (f32[1024,128]{1,0:T(8,128)S(1)}, f32[1024,128]{1,0:T(8,128)S(1)}, u32[]{:S(2)}, u32[]{:S(2)}) collective-permute-start(f32[1024,128]{1,0:T(8,128)S(1)} %get-tuple-element.61.refs_2_.refs_1_), channel_id=1, source_target_pairs={{0,2},{3,5},{4,6},{2,0},{5,3},{6,4},{8,10},{11,13},{12,14},{10,8},... | collective-permute-start | bytes 1572872 | tf_op jit(solution)/shard_map/ppermute | solution.py:486
  70.5 14.0 %collective-permute-start.19 = (f32[1024,128]{1,0:T(8,128)S(1)}, f32[1024,128]{1,0:T(8,128)S(1)}, u32[]{:S(2)}, u32[]{:S(2)}) collective-permute-start(f32[1024,128]{1,0:T(8,128)S(1)} %get-tuple-element.61.refs_2_.refs_1_), channel_id=1, source_target_pairs={{1,3},{2,4},{5,7},{3,1},{4,2},{7,5},{9,11},{10,12},{13,15},{11,9},... | collective-permute-start | bytes 1572872 | tf_op jit(solution)/shard_map/ppermute | solution.py:486
  73.7 13.8 %collective-permute-start.25 = (f32[1024,128]{1,0:T(8,128)S(1)}, f32[1024,128]{1,0:T(8,128)S(1)}, u32[]{:S(2)}, u32[]{:S(2)}) collective-permute-start(f32[1024,128]{1,0:T(8,128)S(1)} %get-tuple-element.64.refs_2_), channel_id=1, source_target_pairs={{0,1},{1,0},{2,3},{3,2},{4,5},{5,4},{6,7},{7,6},{8,9},{9,8},{10,11... | collective-permute-start | bytes 1572872 | tf_op jit(solution)/shard_map/ppermute | solution.py:483
  75.1 7.4 %collective-permute-start.21 = (f32[32,1024]{1,0:T(8,128)S(1)}, f32[32,1024]{1,0:T(8,128)S(1)}, u32[]{:S(2)}, u32[]{:S(2)}) collective-permute-start(f32[32,1024]{1,0:T(8,128)S(1)} %get-tuple-element.66), channel_id=1, source_target_pairs={{0,8},{16,24},{8,0},{24,16},{1,9},{17,25},{9,1},{25,17},{2,10},{18... | collective-permute-start | bytes 393224 | tf_op jit(solution)/shard_map/ppermute | solution.py:397
  76.3 7.6 %collective-permute-start.22 = (f32[32,1024]{1,0:T(8,128)S(1)}, f32[32,1024]{1,0:T(8,128)S(1)}, u32[]{:S(2)}, u32[]{:S(2)}) collective-permute-start(f32[32,1024]{1,0:T(8,128)S(1)} %get-tuple-element.67.refs_2_), channel_id=1, source_target_pairs={{8,16},{16,8},{9,17},{17,9},{10,18},{18,10},{11,19},{19,11},{12,20... | collective-permute-start | bytes 393224 | tf_op jit(solution)/shard_map/ppermute | solution.py:397
  80.5 16.2 %collective-permute-start.27 = (f32[1024,128]{1,0:T(8,128)S(1)}, f32[1024,128]{1,0:T(8,128)S(1)}, u32[]{:S(2)}, u32[]{:S(2)}) collective-permute-start(f32[1024,128]{1,0:T(8,128)S(1)} %payload.18.refs_2_), channel_id=1, source_target_pairs={{1,3},{2,4},{5,7},{3,1},{4,2},{7,5},{9,11},{10,12},{13,15},{11,9},... | collective-permute-start | bytes 1572872 | tf_op jit(solution)/shard_map/ppermute | solution.py:486
  84.5 15.1 %collective-permute-start.24 = (f32[1024,128]{1,0:T(8,128)S(1)}, f32[1024,128]{1,0:T(8,128)S(1)}, u32[]{:S(2)}, u32[]{:S(2)}) collective-permute-start(f32[1024,128]{1,0:T(8,128)S(1)} %payload.19.refs_2_), channel_id=1, source_target_pairs={{0,2},{3,5},{4,6},{2,0},{5,3},{6,4},{8,10},{11,13},{12,14},{10,8},... | collective-permute-start | bytes 1572872 | tf_op jit(solution)/shard_map/ppermute | solution.py:486
  88.8 15.0 %collective-permute-start.29 = (f32[1024,128]{1,0:T(8,128)S(1)}, f32[1024,128]{1,0:T(8,128)S(1)}, u32[]{:S(2)}, u32[]{:S(2)}) collective-permute-start(f32[1024,128]{1,0:T(8,128)S(1)} %get-tuple-element.69.refs_2_), channel_id=1, source_target_pairs={{0,1},{1,0},{2,3},{3,2},{4,5},{5,4},{6,7},{7,6},{8,9},{9,8},{10,11... | collective-permute-start | bytes 1572872 | tf_op jit(solution)/shard_map/ppermute | solution.py:483
  92.2 13.6 %collective-permute-start.34 = (f32[1024,128]{1,0:T(8,128)S(1)}, f32[1024,128]{1,0:T(8,128)S(1)}, u32[]{:S(2)}, u32[]{:S(2)}) collective-permute-start(f32[1024,128]{1,0:T(8,128)S(1)} %get-tuple-element.70.refs_8_), channel_id=1, source_target_pairs={{0,1},{1,0},{2,3},{3,2},{4,5},{5,4},{6,7},{7,6},{8,9},{9,8},{10,11... | collective-permute-start | bytes 1572872 | tf_op jit(solution)/shard_map/ppermute | solution.py:483
  95.0 1.4 %collective-permute-start.26 = (f32[2,256]{1,0:T(2,128)S(1)}, f32[2,256]{1,0:T(2,128)S(1)}, u32[]{:S(2)}, u32[]{:S(2)}) collective-permute-start(f32[2,256]{1,0:T(2,128)S(1)} %get-tuple-element.71.refs_3_.refs_0_), channel_id=1, source_target_pairs={{0,1},{1,0},{2,3},{3,2},{4,5},{5,4},{6,7},{7,6},{8,9},{9,8},{10,11... | collective-permute-start | bytes 6152 | tf_op jit(solution)/shard_map/ppermute | solution.py:687
  96.4 10.0 %collective-permute-start.38 = (f32[1024,128]{1,0:T(8,128)S(1)}, f32[1024,128]{1,0:T(8,128)S(1)}, u32[]{:S(2)}, u32[]{:S(2)}) collective-permute-start(f32[1024,128]{1,0:T(8,128)S(1)} %get-tuple-element.61.refs_2_.refs_1_), channel_id=1, source_target_pairs={{0,1},{1,0},{2,3},{3,2},{4,5},{5,4},{6,7},{7,6},{8,9},{9,8},{10,11... | collective-permute-start | bytes 1572872 | tf_op jit(solution)/shard_map/ppermute | solution.py:483
  96.7 9.9 %collective-permute-start.37 = (f32[1024,128]{1,0:T(8,128)S(1)}, f32[1024,128]{1,0:T(8,128)S(1)}, u32[]{:S(2)}, u32[]{:S(2)}) collective-permute-start(f32[1024,128]{1,0:T(8,128)S(1)} %pick.9.refs_2_.refs_1_), channel_id=1, source_target_pairs={{0,1},{1,0},{2,3},{3,2},{4,5},{5,4},{6,7},{7,6},{8,9},{9,8},{10,11... | collective-permute-start | bytes 1572872 | tf_op jit(solution)/shard_map/ppermute | solution.py:483
  99.7 14.3 %collective-permute-start.33 = (f32[1024,128]{1,0:T(8,128)S(1)}, f32[1024,128]{1,0:T(8,128)S(1)}, u32[]{:S(2)}, u32[]{:S(2)}) collective-permute-start(f32[1024,128]{1,0:T(8,128)S(1)} %payload.20.refs_2_), channel_id=1, source_target_pairs={{0,2},{3,5},{4,6},{2,0},{5,3},{6,4},{8,10},{11,13},{12,14},{10,8},... | collective-permute-start | bytes 1572872 | tf_op jit(solution)/shard_map/ppermute | solution.py:486
  103.9 14.4 %collective-permute-start.28 = (f32[1024,128]{1,0:T(8,128)S(1)}, f32[1024,128]{1,0:T(8,128)S(1)}, u32[]{:S(2)}, u32[]{:S(2)}) collective-permute-start(f32[1024,128]{1,0:T(8,128)S(1)} %payload.21.refs_2_), channel_id=1, source_target_pairs={{1,3},{2,4},{5,7},{3,1},{4,2},{7,5},{9,11},{10,12},{13,15},{11,9},... | collective-permute-start | bytes 1572872 | tf_op jit(solution)/shard_map/ppermute | solution.py:486
  106.0 1.6 %collective-permute-start.36 = (f32[512,128]{1,0:T(8,128)S(1)}, f32[512,128]{1,0:T(8,128)S(1)}, u32[]{:S(2)}, u32[]{:S(2)}) collective-permute-start(f32[512,128]{1,0:T(8,128)S(1)} %get-tuple-element.84), channel_id=1, source_target_pairs={{0,1},{1,0},{2,3},{3,2},{4,5},{5,4},{6,7},{7,6},{8,9},{9,8},{10,11... | collective-permute-start | bytes 786440 | tf_op jit(solution)/shard_map/ppermute | solution.py:483
  106.4 3.8 %collective-permute-start.35 = (f32[512,128]{1,0:T(8,128)S(1)}, f32[512,128]{1,0:T(8,128)S(1)}, u32[]{:S(2)}, u32[]{:S(2)}) collective-permute-start(f32[512,128]{1,0:T(8,128)S(1)} %get-tuple-element.85), channel_id=1, source_target_pairs={{0,1},{1,0},{2,3},{3,2},{4,5},{5,4},{6,7},{7,6},{8,9},{9,8},{10,11... | collective-permute-start | bytes 786440 | tf_op jit(solution)/shard_map/ppermute | solution.py:483
  106.6 9.4 %collective-permute-start.32 = (f32[2,256]{1,0:T(2,128)S(1)}, f32[2,256]{1,0:T(2,128)S(1)}, u32[]{:S(2)}, u32[]{:S(2)}) collective-permute-start(f32[2,256]{1,0:T(2,128)S(1)} %get-tuple-element.74.refs_0_), channel_id=1, source_target_pairs={{0,6},{1,7},{2,4},{3,5},{4,2},{5,3},{6,0},{7,1},{8,14},{9,15},{10,... | collective-permute-start | bytes 6152 | tf_op jit(solution)/shard_map/ppermute | solution.py:687
  107.6 10.0 %collective-permute-start.31 = (f32[2,256]{1,0:T(2,128)S(1)}, f32[2,256]{1,0:T(2,128)S(1)}, u32[]{:S(2)}, u32[]{:S(2)}) collective-permute-start(f32[2,256]{1,0:T(2,128)S(1)} %get-tuple-element.74.refs_0_), channel_id=1, source_target_pairs={{0,4},{1,5},{2,6},{3,7},{4,0},{5,1},{6,2},{7,3},{8,12},{9,13},{10,... | collective-permute-start | bytes 6152 | tf_op jit(solution)/shard_map/ppermute | solution.py:687
  110.2 7.5 %collective-permute-start.30 = (f32[2,256]{1,0:T(2,128)S(1)}, f32[2,256]{1,0:T(2,128)S(1)}, u32[]{:S(2)}, u32[]{:S(2)}) collective-permute-start(f32[2,256]{1,0:T(2,128)S(1)} %get-tuple-element.74.refs_0_), channel_id=1, source_target_pairs={{0,2},{1,3},{2,0},{3,1},{4,6},{5,7},{6,4},{7,5},{8,10},{9,11},{10,... | collective-permute-start | bytes 6152 | tf_op jit(solution)/shard_map/ppermute | solution.py:687
  114.0 12.3 %collective-permute-start.40 = (f32[1024,128]{1,0:T(8,128)S(1)}, f32[1024,128]{1,0:T(8,128)S(1)}, u32[]{:S(2)}, u32[]{:S(2)}) collective-permute-start(f32[1024,128]{1,0:T(8,128)S(1)} %payload.22.refs_4_), channel_id=1, source_target_pairs={{1,3},{2,4},{5,7},{3,1},{4,2},{7,5},{9,11},{10,12},{13,15},{11,9},... | collective-permute-start | bytes 1572872 | tf_op jit(solution)/shard_map/ppermute | solution.py:486
  118.3 12.9 %collective-permute-start.39 = (f32[1024,128]{1,0:T(8,128)S(1)}, f32[1024,128]{1,0:T(8,128)S(1)}, u32[]{:S(2)}, u32[]{:S(2)}) collective-permute-start(f32[1024,128]{1,0:T(8,128)S(1)} %payload.23.refs_4_), channel_id=1, source_target_pairs={{0,2},{3,5},{4,6},{2,0},{5,3},{6,4},{8,10},{11,13},{12,14},{10,8},... | collective-permute-start | bytes 1572872 | tf_op jit(solution)/shard_map/ppermute | solution.py:486
  120.9 4.0 %collective-permute-start.42 = (f32[512,128]{1,0:T(8,128)S(1)}, f32[512,128]{1,0:T(8,128)S(1)}, u32[]{:S(2)}, u32[]{:S(2)}) collective-permute-start(f32[512,128]{1,0:T(8,128)S(1)} %get-tuple-element.82), channel_id=1, source_target_pairs={{0,1},{1,0},{2,3},{3,2},{4,5},{5,4},{6,7},{7,6},{8,9},{9,8},{10,11... | collective-permute-start | bytes 786440 | tf_op jit(solution)/shard_map/ppermute | solution.py:483
  122.1 2.8 %collective-permute-start.41 = (f32[512,128]{1,0:T(8,128)S(1)}, f32[512,128]{1,0:T(8,128)S(1)}, u32[]{:S(2)}, u32[]{:S(2)}) collective-permute-start(f32[512,128]{1,0:T(8,128)S(1)} %get-tuple-element.83), channel_id=1, source_target_pairs={{0,1},{1,0},{2,3},{3,2},{4,5},{5,4},{6,7},{7,6},{8,9},{9,8},{10,11... | collective-permute-start | bytes 786440 | tf_op jit(solution)/shard_map/ppermute | solution.py:483

commit v13 on v10

--- a/solution.py
+++ b/solution.py
@@ -598,23 +598,23 @@
     mid_a, leading, scattered = one.multiply(chips - 1, base_a)
 
     two = Round(matrix, step_size, False)
-    two.add_terms(mid_a, 1)
+    two.add_terms(mid_a)
+    two.add_terms(mid_a)
     one.first_end(base_b)
     mid_b, last = call(
         functools.partial(turn_sum, time_step), [part, (HALO, modes)], one.ends()
     )
     two.begin(mid_b)
-    two.add_terms(mid_a)
-    two.join_terms(0)
+    two.join_terms(0, 1)
+    two.take_own()
     strips = paired(*call(strip_pairs, [(HALO, modes)] * 2, [leading, last]))
     flux = None
     for step in range(1, chips):
         if step == 1:
             two.send(step, unpack)
-            two.take_own()
-            two.join_terms(1)
+            two.hold(0)
         elif step == 2:
-            two.send(step, lambda: flux.over(1))
+            two.send(step)
             two.join_terms(*range(2, chips))
         elif step == chips - 1:
             two.send(step, lambda: flux.over(*range(2, devices, 2)))
@@ -625,7 +625,7 @@
             for slot in range(2, chips):
                 two.add_terms(mid_a)
         if 1 < step < chips - 1:
-            two.hold(*range(step) if step == 2 else (step - 1,))
+            two.hold(step - 1)
         if step == chips - 2:
             two.multiply(step, first=True)
         if step == chips - 1:
@@ -638,6 +638,7 @@
                 [distribution, mid_a, mid_b, strips, operators, table, kinds, scattered],
             )
             flux = Flux(call, part_flux, devices)
+    flux.over(1)
     (last_b,) = two.multiply(chips - 1, end_b)
     heat_flux = flux.value
     two.first_end(end_a)

time: 131 us -> 132 us (level); the launches traced: 130 us -> 129 us
  waiting for transfers between devices: 25.8 us -> 23.3 us
  starting transfers between devices: 66.4 us -> 68.4 us
    ppermute x19, starting transfers between devices: 13.3 us -> 18.1 us  [exchange(): lax.ppermute(value[i:j], 'mode', across)]
    ppermute x16, waiting for transfers between devices: 21.5 us -> 18.3 us  [along(): return lax.ppermute(value, 'mode', plan.pairs[stream])]
    ppermute x4, starting transfers between devices: 3.13 us -> 1.64 us  [over(): lax.ppermute(self.value, 'mode', [(i, i ^ bit) for i in range(self.device...]
    ppermute x16, starting transfers between devices: 43.3 us -> 41.9 us  [along(): return lax.ppermute(value, 'mode', plan.pairs[stream])]
  transfers between devices with their start and end apart: 43 -> 43, of which waited for: 14 -> 13; matrix products, arithmetic and copies ran while one was open for 0% -> 0% of each run, Pallas kernels for 25% -> 25%
where the time goes in v13:
time: 132 us; the launch traced here: 129 us
  starting transfers between devices  68.4 us (52%)
  Pallas kernels  35 us (27%)
  waiting for transfers between devices  23.3 us (18%)
  between operations  1.58 us (1%)
    ppermute x16, starting transfers between devices, along(): return lax.ppermute(value, 'mode', plan.pairs[stream])  41.9 us
    pallas_call x55, Pallas kernels, __call__(): pl.pallas_call(body, out_shape=[jax.ShapeDtypeStruct(shape, jnp.float32)...  35 us
    ppermute x16, waiting for transfers between devices, along(): return lax.ppermute(value, 'mode', plan.pairs[stream])  18.3 us
    ppermute x19, starting transfers between devices, exchange(): lax.ppermute(value[i:j], 'mode', across)  18.1 us
    ppermute x4, starting transfers between devices, paired(): lax.ppermute(value, 'space', pairs + [(j, i) for i, j in pairs])  6.74 us
    ppermute x4, waiting for transfers between devices, over(): lax.ppermute(self.value, 'mode', [(i, i ^ bit) for i in range(self.device...  3.17 us
  transfers between devices with their start and end apart: 43, of which 13 were waited for; matrix products, arithmetic and copies ran while one was open for 0% of the time, Pallas kernels for 25%

profile of v13, /device:TPU:13, one launch (start us, length us, event | category | flops | bytes accessed | tf_op | source)
XLA Modules:
  0.0 129.2 jit_solution(13981612415766332190)
XLA Ops:
  0.6 2.0 %own_rows.1 = (f32[1040,128]{1,0:T(8,128)}, f32[8,128]{1,0:T(8,128)}) custom-call(f32[1024,256]{1,0:T(8,128)} %refs_0_.9, f32[2,1024]{1,0:T(2,128)} %refs_1_.2, f32[1,1024]{1,0:T(1,128)} %bitcast.4), custom_call_target="tpu_custom_call" | custom-call | flops 1024 | bytes 1024 | tf_op jit(solution)/shard_map/own_rows/pallas_call | solution.py:39
  2.6 3.2 %collective-permute-start.2 = (f32[1040,128]{1,0:T(8,128)}, f32[1040,128]{1,0:T(8,128)S(1)}, u32[]{:S(2)}, u32[]{:S(2)}) collective-permute-start(f32[1040,128]{1,0:T(8,128)} %get-tuple-element.41.refs_1_), channel_id=1, source_target_pairs={{0,2},{3,5},{4,6},{2,0},{5,3},{6,4},{8,10},{11,13},{12,14},{10,8},... | collective-permute-start | bytes 1597448 | tf_op jit(solution)/shard_map/ppermute | solution.py:466
  5.8 1.9 %collective-permute-start = (f32[1040,128]{1,0:T(8,128)}, f32[1040,128]{1,0:T(8,128)S(1)}, u32[]{:S(2)}, u32[]{:S(2)}) collective-permute-start(f32[1040,128]{1,0:T(8,128)} %get-tuple-element.41.refs_1_), channel_id=1, source_target_pairs={{1,3},{2,4},{5,7},{3,1},{4,2},{7,5},{9,11},{10,12},{13,15},{11,9},... | collective-permute-start | bytes 1597448 | tf_op jit(solution)/shard_map/ppermute | solution.py:466
  7.8 0.7 copy-done.3
  8.5 7.4 %load_and_products.1 = (f32[1024,128]{1,0:T(8,128)S(1)}, f32[1024,128]{1,0:T(8,128)S(1)}, f32[1024,128]{1,0:T(8,128)S(1)}, f32[1024,128]{1,0:T(8,128)S(1)}, f32[...) custom-call(bf16[8192,1024]{1,0:T(8,128)(2,1)} %refs_0_.6, ...), custom_call_target="tpu_custom_call" | custom-call | flops 1024 | bytes 1024 | tf_op jit(solution)/shard_map/load_and_products/pallas_call | solution.py:39
  15.9 2.6 %collective-permute-start.1 = (f32[1024,128]{1,0:T(8,128)S(1)}, f32[1024,128]{1,0:T(8,128)S(1)}, u32[]{:S(2)}, u32[]{:S(2)}) collective-permute-start(f32[1024,128]{1,0:T(8,128)S(1)} %get-tuple-element.44), channel_id=1, source_target_pairs={{0,1},{1,0},{2,3},{3,2},{4,5},{5,4},{6,7},{7,6},{8,9},{9,8},{10,11... | collective-permute-start | bytes 1572872 | tf_op jit(solution)/shard_map/ppermute | solution.py:463
  18.5 0.4 collective-permute-start.6
  19.1 0.6 collective-permute-done.refs_1_.refs_0_
  20.1 1.9 %collective-permute-start.9 = (f32[1040,128]{1,0:T(8,128)S(1)}, f32[1040,128]{1,0:T(8,128)S(1)}, u32[]{:S(2)}, u32[]{:S(2)}) collective-permute-start(f32[1040,128]{1,0:T(8,128)S(1)} %payload.12.refs_2_), channel_id=1, source_target_pairs={{1,3},{2,4},{5,7},{3,1},{4,2},{7,5},{9,11},{10,12},{13,15},{11,9},... | collective-permute-start | bytes 1597448 | tf_op jit(solution)/shard_map/ppermute | solution.py:466
  22.1 4.7 %collective-permute-start.3 = (f32[1040,128]{1,0:T(8,128)S(1)}, f32[1040,128]{1,0:T(8,128)S(1)}, u32[]{:S(2)}, u32[]{:S(2)}) collective-permute-start(f32[1040,128]{1,0:T(8,128)S(1)} %payload.13.refs_2_), channel_id=1, source_target_pairs={{0,2},{3,5},{4,6},{2,0},{5,3},{6,4},{8,10},{11,13},{12,14},{10,8},... | collective-permute-start | bytes 1597448 | tf_op jit(solution)/shard_map/ppermute | solution.py:466
  27.0 0.3 strip_rows.1
  27.4 1.3 collective-permute-start.7
  28.7 2.1 %collective-permute-start.8 = (f32[32,1024]{1,0:T(8,128)S(1)}, f32[32,1024]{1,0:T(8,128)S(1)}, u32[]{:S(2)}, u32[]{:S(2)}) collective-permute-start(f32[32,1024]{1,0:T(8,128)S(1)} %get-tuple-element.55.refs_3_), channel_id=1, source_target_pairs={{8,16},{16,8},{9,17},{17,9},{10,18},{18,10},{11,19},{19,11},{12,20... | collective-permute-start | bytes 393224 | tf_op jit(solution)/shard_map/ppermute | solution.py:377
  30.9 1.4 %two_blocks.8.refs_3_ = f32[272,1024]{1,0:T(8,128)S(1)} custom-call(bf16[8192,1024]{1,0:T(8,128)(2,1)S(1)} %get-tuple-element.45.refs_2_.refs_0_, f32[1040,128]{1,0:T(8,128)S(1)} %copy-done.2, f32[1040,128]{1,0:T(8,128)S(1)} %collective-permute-done.10.refs_2_, f32[32,1024]{1,0:T(8,128)S(1)} %get-tuple-element.55.refs_3_), custom_call_target="tpu_custom_call" | custom-call | flops 1024 | bytes 1024 | tf_op jit(solution)/shard_map/two_blocks/pallas_call | solution.py:39
  32.4 4.6 %collective-permute-start.12 = (f32[1040,128]{1,0:T(8,128)S(1)}, f32[1040,128]{1,0:T(8,128)S(1)}, u32[]{:S(2)}, u32[]{:S(2)}) collective-permute-start(f32[1040,128]{1,0:T(8,128)S(1)} %payload.14.refs_2_), channel_id=1, source_target_pairs={{0,2},{3,5},{4,6},{2,0},{5,3},{6,4},{8,10},{11,13},{12,14},{10,8},... | collective-permute-start | bytes 1597448 | tf_op jit(solution)/shard_map/ppermute | solution.py:466
  37.3 1.9 %collective-permute-start.11 = (f32[1040,128]{1,0:T(8,128)S(1)}, f32[1040,128]{1,0:T(8,128)S(1)}, u32[]{:S(2)}, u32[]{:S(2)}) collective-permute-start(f32[1040,128]{1,0:T(8,128)S(1)} %payload.15.refs_3_), channel_id=1, source_target_pairs={{1,3},{2,4},{5,7},{3,1},{4,2},{7,5},{9,11},{10,12},{13,15},{11,9},... | collective-permute-start | bytes 1597448 | tf_op jit(solution)/shard_map/ppermute | solution.py:466
  39.4 1.1 collective-permute-start.18
  40.5 1.4 %two_blocks.9.refs_5_.refs_3_ = f32[272,1024]{1,0:T(8,128)S(1)} custom-call(bf16[8192,1024]{1,0:T(8,128)(2,1)S(1)} %get-tuple-element.45.refs_2_.refs_0_, f32[1040,128]{1,0:T(8,128)S(1)} %pick.6.refs_2_.refs_1_, f32[1040,128]{1,0:T(8,128)S(1)} %collective-permute-done.13.refs_2_, f32[272,1024]{1,0:T(8,128)S(1)} %two_blocks.8.refs_3_, ...), custom_call_target="tpu_custom_call" | custom-call | flops 1024 | bytes 1024 | tf_op jit(solution)/shard_map/two_blocks/pallas_call | solution.py:39
  41.9 2.0 %first_rest.1 = (f32[1024,128]{1,0:T(8,128)S(1)}, f32[1024,128]{1,0:T(8,128)S(1)}) custom-call(f32[1024,256]{1,0:T(8,128)S(1)} %copy-done, bf16[1024,128]{1,0:T(8,128)(2,1)S(1)} %strip_columns.2.refs_3_.refs_1_, bf16[640,1024]{1,0:T(8,128)(2,1)S(1)} %copy-done.1, f32[8,1024]{1,0:T(8,128)S(1)} %maximum_maximum_fusion.refs_3_.refs_5_, s32[1,256]{1,0:T(1,128)S(1)} %bitcast.2, ...), custom_call_target="tpu_custom_call" | custom-call | flops 1024 | bytes 1024 | tf_op jit(solution)/shard_map/first_rest/pallas_call | solution.py:39
  43.9 1.5 %collective-permute-done.12.refs_0_.refs_1_ = f32[1040,128]{1,0:T(8,128)S(1)} collective-permute-done((f32[1040,128]{1,0:T(8,128)S(1)}, f32[1040,128]{1,0:T(8,128)S(1)}, u32[]{:S(2)}, u32[]{:S(2)}) %collective-permute-start.12) | collective-permute-done | bytes 532512 | tf_op jit(solution)/shard_map/ppermute | solution.py:466
  45.5 1.9 %collective-permute-start.15 = (f32[1040,128]{1,0:T(8,128)S(1)}, f32[1040,128]{1,0:T(8,128)S(1)}, u32[]{:S(2)}, u32[]{:S(2)}) collective-permute-start(f32[1040,128]{1,0:T(8,128)S(1)} %payload.16.refs_3_), channel_id=1, source_target_pairs={{1,3},{2,4},{5,7},{3,1},{4,2},{7,5},{9,11},{10,12},{13,15},{11,9},... | collective-permute-start | bytes 1597448 | tf_op jit(solution)/shard_map/ppermute | solution.py:466
  47.4 3.6 %collective-permute-done.11.refs_0_.refs_3_ = f32[1040,128]{1,0:T(8,128)S(1)} collective-permute-done((f32[1040,128]{1,0:T(8,128)S(1)}, f32[1040,128]{1,0:T(8,128)S(1)}, u32[]{:S(2)}, u32[]{:S(2)}) %collective-permute-start.11) | collective-permute-done | bytes 532512 | tf_op jit(solution)/shard_map/ppermute | solution.py:466
  51.1 2.8 %collective-permute-start.14 = (f32[1040,128]{1,0:T(8,128)S(1)}, f32[1040,128]{1,0:T(8,128)S(1)}, u32[]{:S(2)}, u32[]{:S(2)}) collective-permute-start(f32[1040,128]{1,0:T(8,128)S(1)} %payload.17.refs_4_), channel_id=1, source_target_pairs={{0,2},{3,5},{4,6},{2,0},{5,3},{6,4},{8,10},{11,13},{12,14},{10,8},... | collective-permute-start | bytes 1597448 | tf_op jit(solution)/shard_map/ppermute | solution.py:466
  54.2 1.3 %collective-permute-start.17 = (f32[520,128]{1,0:T(8,128)S(1)}, f32[520,128]{1,0:T(8,128)S(1)}, u32[]{:S(2)}, u32[]{:S(2)}) collective-permute-start(f32[520,128]{1,0:T(8,128)S(1)} %get-tuple-element.80), channel_id=1, source_target_pairs={{0,1},{1,0},{2,3},{3,2},{4,5},{5,4},{6,7},{7,6},{8,9},{9,8},{10,11... | collective-permute-start | bytes 798728 | tf_op jit(solution)/shard_map/ppermute | solution.py:463
  55.6 1.4 %two_blocks.10.refs_4_.refs_6_ = f32[272,1024]{1,0:T(8,128)S(1)} custom-call(bf16[8192,1024]{1,0:T(8,128)(2,1)S(1)} %get-tuple-element.45.refs_2_.refs_0_, f32[1040,128]{1,0:T(8,128)S(1)} %pick.7.refs_4_.refs_1_, f32[1040,128]{1,0:T(8,128)S(1)} %collective-permute-done.18.refs_2_, f32[272,1024]{1,0:T(8,128)S(1)} %two_blocks.9.refs_5_.refs_3_, ...), custom_call_target="tpu_custom_call" | custom-call | flops 1024 | bytes 1024 | tf_op jit(solution)/shard_map/two_blocks/pallas_call | solution.py:39
  57.1 1.5 %two_blocks.11 = (f32[1024,128]{1,0:T(8,128)S(1)}, f32[32,1024]{1,0:T(8,128)S(1)}, f32[8,1024]{1,0:T(8,128)S(1)}) custom-call(bf16[8192,1024]{1,0:T(8,128)(2,1)S(1)} %get-tuple-element.45.refs_2_.refs_0_, f32[1040,128]{1,0:T(8,128)S(1)} %pick.8.refs_4_.refs_1_, f32[520,128]{1,0:T(8,128)S(1)} %collective-permute-done.16.refs_2_, ...), custom_call_target="tpu_custom_call" | custom-call | flops 1024 | bytes 1024 | tf_op jit(solution)/shard_map/two_blocks/pallas_call | solution.py:39
  58.6 1.3 slot_products.4
  59.9 0.4 collective-permute-start.20
  60.3 1.2 slot_products.5
  61.9 4.0 %collective-permute-done.14.refs_0_ = f32[1040,128]{1,0:T(8,128)S(1)} collective-permute-done((f32[1040,128]{1,0:T(8,128)S(1)}, f32[1040,128]{1,0:T(8,128)S(1)}, u32[]{:S(2)}, u32[]{:S(2)}) %collective-permute-start.14) | collective-permute-done | bytes 532512 | tf_op jit(solution)/shard_map/ppermute | solution.py:466
  66.2 3.1 %collective-permute-start.24 = (f32[1024,128]{1,0:T(8,128)S(1)}, f32[1024,128]{1,0:T(8,128)S(1)}, u32[]{:S(2)}, u32[]{:S(2)}) collective-permute-start(f32[1024,128]{1,0:T(8,128)S(1)} %get-tuple-element.62.refs_2_.refs_1_), channel_id=1, source_target_pairs={{0,2},{3,5},{4,6},{2,0},{5,3},{6,4},{8,10},{11,13},{12,14},{10,8},... | collective-permute-start | bytes 1572872 | tf_op jit(solution)/shard_map/ppermute | solution.py:466
  69.3 1.9 %collective-permute-start.19 = (f32[1024,128]{1,0:T(8,128)S(1)}, f32[1024,128]{1,0:T(8,128)S(1)}, u32[]{:S(2)}, u32[]{:S(2)}) collective-permute-start(f32[1024,128]{1,0:T(8,128)S(1)} %get-tuple-element.62.refs_2_.refs_1_), channel_id=1, source_target_pairs={{1,3},{2,4},{5,7},{3,1},{4,2},{7,5},{9,11},{10,12},{13,15},{11,9},... | collective-permute-start | bytes 1572872 | tf_op jit(solution)/shard_map/ppermute | solution.py:466
  71.2 0.6 collective-permute-start.27
  72.0 1.3 collective-permute-start.22
  73.3 2.1 %collective-permute-start.23 = (f32[32,1024]{1,0:T(8,128)S(1)}, f32[32,1024]{1,0:T(8,128)S(1)}, u32[]{:S(2)}, u32[]{:S(2)}) collective-permute-start(f32[32,1024]{1,0:T(8,128)S(1)} %get-tuple-element.68.refs_2_), channel_id=1, source_target_pairs={{8,16},{16,8},{9,17},{17,9},{10,18},{18,10},{11,19},{19,11},{12,20... | collective-permute-start | bytes 393224 | tf_op jit(solution)/shard_map/ppermute | solution.py:377
  75.4 4.3 %collective-permute-done.24.refs_0_ = f32[1024,128]{1,0:T(8,128)S(1)} collective-permute-done((f32[1024,128]{1,0:T(8,128)S(1)}, f32[1024,128]{1,0:T(8,128)S(1)}, u32[]{:S(2)}, u32[]{:S(2)}) %collective-permute-start.24) | collective-permute-done | bytes 524320 | tf_op jit(solution)/shard_map/ppermute | solution.py:466
  79.7 1.9 %collective-permute-start.26 = (f32[1024,128]{1,0:T(8,128)S(1)}, f32[1024,128]{1,0:T(8,128)S(1)}, u32[]{:S(2)}, u32[]{:S(2)}) collective-permute-start(f32[1024,128]{1,0:T(8,128)S(1)} %payload.18.refs_2_), channel_id=1, source_target_pairs={{1,3},{2,4},{5,7},{3,1},{4,2},{7,5},{9,11},{10,12},{13,15},{11,9},... | collective-permute-start | bytes 1572872 | tf_op jit(solution)/shard_map/ppermute | solution.py:466
  81.8 0.3 collective-permute-done.19.refs_0_.refs_1_
  82.1 3.4 %collective-permute-start.25 = (f32[1024,128]{1,0:T(8,128)S(1)}, f32[1024,128]{1,0:T(8,128)S(1)}, u32[]{:S(2)}, u32[]{:S(2)}) collective-permute-start(f32[1024,128]{1,0:T(8,128)S(1)} %payload.19.refs_1_), channel_id=1, source_target_pairs={{0,2},{3,5},{4,6},{2,0},{5,3},{6,4},{8,10},{11,13},{12,14},{10,8},... | collective-permute-start | bytes 1572872 | tf_op jit(solution)/shard_map/ppermute | solution.py:466
  85.7 1.3 slot_products.6
  87.0 1.7 %collective-permute-start.29 = (f32[1024,128]{1,0:T(8,128)S(1)}, f32[1024,128]{1,0:T(8,128)S(1)}, u32[]{:S(2)}, u32[]{:S(2)}) collective-permute-start(f32[1024,128]{1,0:T(8,128)S(1)} %get-tuple-element.69.refs_2_), channel_id=1, source_target_pairs={{0,1},{1,0},{2,3},{3,2},{4,5},{5,4},{6,7},{7,6},{8,9},{9,8},{10,11... | collective-permute-start | bytes 1572872 | tf_op jit(solution)/shard_map/ppermute | solution.py:463
  88.6 1.3 slot_products.7
  90.0 0.5 collective-permute-start.37
  90.5 2.7 %second_rest.1 = (f32[1024,128]{1,0:T(8,128)S(1)}, f32[1024,128]{1,0:T(8,128)S(1)}, f32[2,256]{1,0:T(2,128)S(1)}) custom-call(f32[1024,256]{1,0:T(8,128)S(1)} %copy-done, f32[1024,128]{1,0:T(8,128)S(1)} %get-tuple-element.58.refs_1_, f32[1024,128]{1,0:T(8,128)S(1)} %get-tuple-element.62.refs_2_.refs_1_, bf16[1024,128]{1,0:T(8,128)(2,1)S(1)} %strip_columns.3.refs_2_.refs_3_, ...), custom_call_target="tpu_custom_call" | custom-call | flops 1024 | bytes 1024 | tf_op jit(solution)/shard_map/second_rest/pallas_call | solution.py:39
  93.3 1.9 %collective-permute-start.33 = (f32[1024,128]{1,0:T(8,128)S(1)}, f32[1024,128]{1,0:T(8,128)S(1)}, u32[]{:S(2)}, u32[]{:S(2)}) collective-permute-start(f32[1024,128]{1,0:T(8,128)S(1)} %payload.20.refs_3_), channel_id=1, source_target_pairs={{0,2},{3,5},{4,6},{2,0},{5,3},{6,4},{8,10},{11,13},{12,14},{10,8},... | collective-permute-start | bytes 1572872 | tf_op jit(solution)/shard_map/ppermute | solution.py:466
  95.2 1.9 %collective-permute-done.25.refs_0_ = f32[1024,128]{1,0:T(8,128)S(1)} collective-permute-done((f32[1024,128]{1,0:T(8,128)S(1)}, f32[1024,128]{1,0:T(8,128)S(1)}, u32[]{:S(2)}, u32[]{:S(2)}) %collective-permute-start.25) | collective-permute-done | bytes 524320 | tf_op jit(solution)/shard_map/ppermute | solution.py:466
  97.1 1.9 %collective-permute-start.28 = (f32[1024,128]{1,0:T(8,128)S(1)}, f32[1024,128]{1,0:T(8,128)S(1)}, u32[]{:S(2)}, u32[]{:S(2)}) collective-permute-start(f32[1024,128]{1,0:T(8,128)S(1)} %payload.21.refs_2_), channel_id=1, source_target_pairs={{1,3},{2,4},{5,7},{3,1},{4,2},{7,5},{9,11},{10,12},{13,15},{11,9},... | collective-permute-start | bytes 1572872 | tf_op jit(solution)/shard_map/ppermute | solution.py:466
  99.3 4.5 %collective-permute-start.36 = (f32[512,128]{1,0:T(8,128)S(1)}, f32[512,128]{1,0:T(8,128)S(1)}, u32[]{:S(2)}, u32[]{:S(2)}) collective-permute-start(f32[512,128]{1,0:T(8,128)S(1)} %get-tuple-element.84), channel_id=1, source_target_pairs={{0,1},{1,0},{2,3},{3,2},{4,5},{5,4},{6,7},{7,6},{8,9},{9,8},{10,11... | collective-permute-start | bytes 786440 | tf_op jit(solution)/shard_map/ppermute | solution.py:463
  103.9 1.1 collective-permute-done.36.refs_3_
  105.0 0.4 collective-permute-done.35.refs_2_
  105.4 1.2 collective-permute-start.30
  106.6 1.3 %two_blocks.12.refs_3_ = f32[256,1024]{1,0:T(8,128)S(1)} custom-call(bf16[8192,1024]{1,0:T(8,128)(2,1)S(1)} %get-tuple-element.45.refs_2_.refs_0_, f32[1024,128]{1,0:T(8,128)S(1)} %pick.10.refs_1_, f32[512,128]{1,0:T(8,128)S(1)} %collective-permute-done.35.refs_2_, f32[512,128]{1,0:T(8,128)S(1)} %collective-permute-done.36.refs_3_, ...), custom_call_target="tpu_custom_call" | custom-call | flops 1024 | bytes 1024 | tf_op jit(solution)/shard_map/two_blocks/pallas_call | solution.py:39
  108.0 2.2 %collective-permute-start.39 = (f32[1024,128]{1,0:T(8,128)S(1)}, f32[1024,128]{1,0:T(8,128)S(1)}, u32[]{:S(2)}, u32[]{:S(2)}) collective-permute-start(f32[1024,128]{1,0:T(8,128)S(1)} %payload.22.refs_4_), channel_id=1, source_target_pairs={{1,3},{2,4},{5,7},{3,1},{4,2},{7,5},{9,11},{10,12},{13,15},{11,9},... | collective-permute-start | bytes 1572872 | tf_op jit(solution)/shard_map/ppermute | solution.py:466
  110.2 3.2 %collective-permute-done.31.refs_2_ = f32[2,256]{1,0:T(2,128)S(1)} collective-permute-done((f32[2,256]{1,0:T(2,128)S(1)}, f32[2,256]{1,0:T(2,128)S(1)}, u32[]{:S(2)}, u32[]{:S(2)}) %collective-permute-start.31) | collective-permute-done | bytes 2080 | tf_op jit(solution)/shard_map/ppermute | solution.py:661
  113.5 2.5 %collective-permute-start.38 = (f32[1024,128]{1,0:T(8,128)S(1)}, f32[1024,128]{1,0:T(8,128)S(1)}, u32[]{:S(2)}, u32[]{:S(2)}) collective-permute-start(f32[1024,128]{1,0:T(8,128)S(1)} %payload.23.refs_4_), channel_id=1, source_target_pairs={{0,2},{3,5},{4,6},{2,0},{5,3},{6,4},{8,10},{11,13},{12,14},{10,8},... | collective-permute-start | bytes 1572872 | tf_op jit(solution)/shard_map/ppermute | solution.py:466
  116.0 0.3 pick.11.refs_4_.refs_1_
  116.3 4.3 %collective-permute-start.41 = (f32[512,128]{1,0:T(8,128)S(1)}, f32[512,128]{1,0:T(8,128)S(1)}, u32[]{:S(2)}, u32[]{:S(2)}) collective-permute-start(f32[512,128]{1,0:T(8,128)S(1)} %get-tuple-element.82), channel_id=1, source_target_pairs={{0,1},{1,0},{2,3},{3,2},{4,5},{5,4},{6,7},{7,6},{8,9},{9,8},{10,11... | collective-permute-start | bytes 786440 | tf_op jit(solution)/shard_map/ppermute | solution.py:463
  120.7 0.4 collective-permute-start.42
  121.1 1.3 %two_blocks.13.refs_3_.refs_4_ = f32[256,1024]{1,0:T(8,128)S(1)} custom-call(bf16[8192,1024]{1,0:T(8,128)(2,1)S(1)} %get-tuple-element.45.refs_2_.refs_0_, f32[1024,128]{1,0:T(8,128)S(1)} %get-tuple-element.62.refs_2_.refs_1_, f32[1024,128]{1,0:T(8,128)S(1)} %pass_on.2.refs_2_, f32[256,1024]{1,0:T(8,128)S(1)} %two_blocks.12.refs_3_, ...), custom_call_target="tpu_custom_call" | custom-call | flops 1024 | bytes 1024 | tf_op jit(solution)/shard_map/two_blocks/pallas_call | solution.py:39
  122.5 1.3 %two_blocks.14.refs_2_.refs_4_ = f32[256,1024]{1,0:T(8,128)S(1)} custom-call(bf16[8192,1024]{1,0:T(8,128)(2,1)S(1)} %get-tuple-element.45.refs_2_.refs_0_, f32[1024,128]{1,0:T(8,128)S(1)} %pick.9.refs_2_.refs_1_, f32[1024,128]{1,0:T(8,128)S(1)} %pass_on.3.refs_4_.refs_2_, f32[256,1024]{1,0:T(8,128)S(1)} %two_blocks.13.refs_3_.refs_4_, ...), custom_call_target="tpu_custom_call" | custom-call | flops 1024 | bytes 1024 | tf_op jit(solution)/shard_map/two_blocks/pallas_call | solution.py:39
  123.8 0.6 add_all.3
  124.4 1.5 %two_blocks.15.refs_3_.refs_2_ = f32[1024,128]{1,0:T(8,128)S(1)} custom-call(bf16[8192,1024]{1,0:T(8,128)(2,1)S(1)} %get-tuple-element.45.refs_2_.refs_0_, f32[1024,128]{1,0:T(8,128)S(1)} %pick.11.refs_4_.refs_1_, f32[512,128]{1,0:T(8,128)S(1)} %collective-permute-done.40.refs_2_, f32[512,128]{1,0:T(8,128)S(1)} %collective-permute-done.41.refs_3_, ...), custom_call_target="tpu_custom_call" | custom-call | flops 1024 | bytes 1024 | tf_op jit(solution)/shard_map/two_blocks/pallas_call | solution.py:39
  126.0 2.1 %collective-permute-done.38.refs_0_ = f32[1024,128]{1,0:T(8,128)S(1)} collective-permute-done((f32[1024,128]{1,0:T(8,128)S(1)}, f32[1024,128]{1,0:T(8,128)S(1)}, u32[]{:S(2)}, u32[]{:S(2)}) %collective-permute-start.38) | collective-permute-done | bytes 524320 | tf_op jit(solution)/shard_map/ppermute | solution.py:466
  128.1 1.0 last_sum.1
  (98 shorter events, 4.1 us)
Async XLA Ops:
  0.6 7.1 %copy-start = (f32[1024,256]{1,0:T(8,128)S(1)}, f32[1024,256]{1,0:T(8,128)}, u32[]{:S(2)}) copy-start(f32[1024,256]{1,0:T(8,128)} %refs_0_.9) | copy-start | bytes 3145732
  2.6 16.3 %collective-permute-start.2 = (f32[1040,128]{1,0:T(8,128)}, f32[1040,128]{1,0:T(8,128)S(1)}, u32[]{:S(2)}, u32[]{:S(2)}) collective-permute-start(f32[1040,128]{1,0:T(8,128)} %get-tuple-element.41.refs_1_), channel_id=1, source_target_pairs={{0,2},{3,5},{4,6},{2,0},{5,3},{6,4},{8,10},{11,13},{12,14},{10,8},... | collective-permute-start | bytes 1597448 | tf_op jit(solution)/shard_map/ppermute | solution.py:466
  5.8 13.9 %collective-permute-start = (f32[1040,128]{1,0:T(8,128)}, f32[1040,128]{1,0:T(8,128)S(1)}, u32[]{:S(2)}, u32[]{:S(2)}) collective-permute-start(f32[1040,128]{1,0:T(8,128)} %get-tuple-element.41.refs_1_), channel_id=1, source_target_pairs={{1,3},{2,4},{5,7},{3,1},{4,2},{7,5},{9,11},{10,12},{13,15},{11,9},... | collective-permute-start | bytes 1597448 | tf_op jit(solution)/shard_map/ppermute | solution.py:466
  7.8 0.7 copy-start.3
  8.5 11.2 %copy-start.2 = (f32[1040,128]{1,0:T(8,128)S(1)}, f32[1040,128]{1,0:T(8,128)}, u32[]{:S(2)}) copy-start(f32[1040,128]{1,0:T(8,128)} %get-tuple-element.41.refs_1_) | copy-start | bytes 1597444
  15.9 4.1 %collective-permute-start.1 = (f32[1024,128]{1,0:T(8,128)S(1)}, f32[1024,128]{1,0:T(8,128)S(1)}, u32[]{:S(2)}, u32[]{:S(2)}) collective-permute-start(f32[1024,128]{1,0:T(8,128)S(1)} %get-tuple-element.44), channel_id=1, source_target_pairs={{0,1},{1,0},{2,3},{3,2},{4,5},{5,4},{6,7},{7,6},{8,9},{9,8},{10,11... | collective-permute-start | bytes 1572872 | tf_op jit(solution)/shard_map/ppermute | solution.py:463
  18.5 3.7 %collective-permute-start.4 = (f32[1024,128]{1,0:T(8,128)S(1)}, f32[1024,128]{1,0:T(8,128)S(1)}, u32[]{:S(2)}, u32[]{:S(2)}) collective-permute-start(f32[1024,128]{1,0:T(8,128)S(1)} %get-tuple-element.47), channel_id=1, source_target_pairs={{0,1},{1,0},{2,3},{3,2},{4,5},{5,4},{6,7},{7,6},{8,9},{9,8},{10,11... | collective-permute-start | bytes 1572872 | tf_op jit(solution)/shard_map/ppermute | solution.py:463
  18.5 8.3 %collective-permute-start.6 = (f32[1024,128]{1,0:T(8,128)S(1)}, f32[1024,128]{1,0:T(8,128)S(1)}, u32[]{:S(2)}, u32[]{:S(2)}) collective-permute-start(f32[1024,128]{1,0:T(8,128)S(1)} %get-tuple-element.51), channel_id=1, source_target_pairs={{0,1},{1,0},{2,3},{3,2},{4,5},{5,4},{6,7},{7,6},{8,9},{9,8},{10,11... | collective-permute-start | bytes 1572872 | tf_op jit(solution)/shard_map/ppermute | solution.py:463
  19.0 8.0 %collective-permute-start.5 = (f32[1024,128]{1,0:T(8,128)S(1)}, f32[1024,128]{1,0:T(8,128)S(1)}, u32[]{:S(2)}, u32[]{:S(2)}) collective-permute-start(f32[1024,128]{1,0:T(8,128)S(1)} %get-tuple-element.49), channel_id=1, source_target_pairs={{0,1},{1,0},{2,3},{3,2},{4,5},{5,4},{6,7},{7,6},{8,9},{9,8},{10,11... | collective-permute-start | bytes 1572872 | tf_op jit(solution)/shard_map/ppermute | solution.py:463
  19.7 11.1 %collective-permute-start.10 = (f32[1040,128]{1,0:T(8,128)S(1)}, f32[1040,128]{1,0:T(8,128)S(1)}, u32[]{:S(2)}, u32[]{:S(2)}) collective-permute-start(f32[1040,128]{1,0:T(8,128)S(1)} %copy-done.2), channel_id=1, source_target_pairs={{0,1},{1,0},{2,3},{3,2},{4,5},{5,4},{6,7},{7,6},{8,9},{9,8},{10,11... | collective-permute-start | bytes 1597448 | tf_op jit(solution)/shard_map/ppermute | solution.py:463
  20.1 12.2 %collective-permute-start.9 = (f32[1040,128]{1,0:T(8,128)S(1)}, f32[1040,128]{1,0:T(8,128)S(1)}, u32[]{:S(2)}, u32[]{:S(2)}) collective-permute-start(f32[1040,128]{1,0:T(8,128)S(1)} %payload.12.refs_2_), channel_id=1, source_target_pairs={{1,3},{2,4},{5,7},{3,1},{4,2},{7,5},{9,11},{10,12},{13,15},{11,9},... | collective-permute-start | bytes 1597448 | tf_op jit(solution)/shard_map/ppermute | solution.py:466
  22.1 15.1 %collective-permute-start.3 = (f32[1040,128]{1,0:T(8,128)S(1)}, f32[1040,128]{1,0:T(8,128)S(1)}, u32[]{:S(2)}, u32[]{:S(2)}) collective-permute-start(f32[1040,128]{1,0:T(8,128)S(1)} %payload.13.refs_2_), channel_id=1, source_target_pairs={{0,2},{3,5},{4,6},{2,0},{5,3},{6,4},{8,10},{11,13},{12,14},{10,8},... | collective-permute-start | bytes 1597448 | tf_op jit(solution)/shard_map/ppermute | solution.py:466
  27.4 9.6 %collective-permute-start.7 = (f32[32,1024]{1,0:T(8,128)S(1)}, f32[32,1024]{1,0:T(8,128)S(1)}, u32[]{:S(2)}, u32[]{:S(2)}) collective-permute-start(f32[32,1024]{1,0:T(8,128)S(1)} %get-tuple-element.54), channel_id=1, source_target_pairs={{0,8},{16,24},{8,0},{24,16},{1,9},{17,25},{9,1},{25,17},{2,10},{18... | collective-permute-start | bytes 393224 | tf_op jit(solution)/shard_map/ppermute | solution.py:377
  28.7 8.3 %collective-permute-start.8 = (f32[32,1024]{1,0:T(8,128)S(1)}, f32[32,1024]{1,0:T(8,128)S(1)}, u32[]{:S(2)}, u32[]{:S(2)}) collective-permute-start(f32[32,1024]{1,0:T(8,128)S(1)} %get-tuple-element.55.refs_3_), channel_id=1, source_target_pairs={{8,16},{16,8},{9,17},{17,9},{10,18},{18,10},{11,19},{19,11},{12,20... | collective-permute-start | bytes 393224 | tf_op jit(solution)/shard_map/ppermute | solution.py:377
  30.8 9.7 %collective-permute-start.13 = (f32[1040,128]{1,0:T(8,128)S(1)}, f32[1040,128]{1,0:T(8,128)S(1)}, u32[]{:S(2)}, u32[]{:S(2)}) collective-permute-start(f32[1040,128]{1,0:T(8,128)S(1)} %pick.6.refs_2_.refs_1_), channel_id=1, source_target_pairs={{0,1},{1,0},{2,3},{3,2},{4,5},{5,4},{6,7},{7,6},{8,9},{9,8},{10,11... | collective-permute-start | bytes 1597448 | tf_op jit(solution)/shard_map/ppermute | solution.py:463
  32.4 13.1 %collective-permute-start.12 = (f32[1040,128]{1,0:T(8,128)S(1)}, f32[1040,128]{1,0:T(8,128)S(1)}, u32[]{:S(2)}, u32[]{:S(2)}) collective-permute-start(f32[1040,128]{1,0:T(8,128)S(1)} %payload.14.refs_2_), channel_id=1, source_target_pairs={{0,2},{3,5},{4,6},{2,0},{5,3},{6,4},{8,10},{11,13},{12,14},{10,8},... | collective-permute-start | bytes 1597448 | tf_op jit(solution)/shard_map/ppermute | solution.py:466
  37.2 2.1 %copy-start.5 = (f32[2,1024]{1,0:T(2,128)S(1)}, f32[2,1024]{1,0:T(2,128)}, u32[]{:S(2)}) copy-start(f32[2,1024]{1,0:T(2,128)} %refs_1_.2) | copy-start | bytes 24580
  37.2 2.1 %copy-start.6 = (f32[1024]{0:T(1024)S(1)}, f32[1024]{0:T(1024)}, u32[]{:S(2)}) copy-start(f32[1024]{0:T(1024)} %param.9) | copy-start | bytes 12292
  37.3 13.8 %collective-permute-start.11 = (f32[1040,128]{1,0:T(8,128)S(1)}, f32[1040,128]{1,0:T(8,128)S(1)}, u32[]{:S(2)}, u32[]{:S(2)}) collective-permute-start(f32[1040,128]{1,0:T(8,128)S(1)} %payload.15.refs_3_), channel_id=1, source_target_pairs={{1,3},{2,4},{5,7},{3,1},{4,2},{7,5},{9,11},{10,12},{13,15},{11,9},... | collective-permute-start | bytes 1597448 | tf_op jit(solution)/shard_map/ppermute | solution.py:466
  39.4 16.3 %collective-permute-start.18 = (f32[1040,128]{1,0:T(8,128)S(1)}, f32[1040,128]{1,0:T(8,128)S(1)}, u32[]{:S(2)}, u32[]{:S(2)}) collective-permute-start(f32[1040,128]{1,0:T(8,128)S(1)} %pick.7.refs_4_.refs_1_), channel_id=1, source_target_pairs={{0,1},{1,0},{2,3},{3,2},{4,5},{5,4},{6,7},{7,6},{8,9},{9,8},{10,11... | collective-permute-start | bytes 1597448 | tf_op jit(solution)/shard_map/ppermute | solution.py:463
  40.5 1.4 %copy-start.1 = (bf16[640,1024]{1,0:T(8,128)(2,1)S(1)}, bf16[640,1024]{1,0:T(8,128)(2,1)}, u32[]{:S(2)}) copy-start(bf16[640,1024]{1,0:T(8,128)(2,1)} %constant.4.clone.refs_2_.refs_4_) | copy-start | bytes 3932164
  40.5 1.4 %copy-start.4 = (s32[256]{0:T(256)S(1)}, s32[256]{0:T(256)}, u32[]{:S(2)}) copy-start(s32[256]{0:T(256)} %param.10) | copy-start | bytes 3076
  45.5 16.3 %collective-permute-start.15 = (f32[1040,128]{1,0:T(8,128)S(1)}, f32[1040,128]{1,0:T(8,128)S(1)}, u32[]{:S(2)}, u32[]{:S(2)}) collective-permute-start(f32[1040,128]{1,0:T(8,128)S(1)} %payload.16.refs_3_), channel_id=1, source_target_pairs={{1,3},{2,4},{5,7},{3,1},{4,2},{7,5},{9,11},{10,12},{13,15},{11,9},... | collective-permute-start | bytes 1597448 | tf_op jit(solution)/shard_map/ppermute | solution.py:466
  51.1 14.8 %collective-permute-start.14 = (f32[1040,128]{1,0:T(8,128)S(1)}, f32[1040,128]{1,0:T(8,128)S(1)}, u32[]{:S(2)}, u32[]{:S(2)}) collective-permute-start(f32[1040,128]{1,0:T(8,128)S(1)} %payload.17.refs_4_), channel_id=1, source_target_pairs={{0,2},{3,5},{4,6},{2,0},{5,3},{6,4},{8,10},{11,13},{12,14},{10,8},... | collective-permute-start | bytes 1597448 | tf_op jit(solution)/shard_map/ppermute | solution.py:466
  54.2 2.8 %collective-permute-start.17 = (f32[520,128]{1,0:T(8,128)S(1)}, f32[520,128]{1,0:T(8,128)S(1)}, u32[]{:S(2)}, u32[]{:S(2)}) collective-permute-start(f32[520,128]{1,0:T(8,128)S(1)} %get-tuple-element.80), channel_id=1, source_target_pairs={{0,1},{1,0},{2,3},{3,2},{4,5},{5,4},{6,7},{7,6},{8,9},{9,8},{10,11... | collective-permute-start | bytes 798728 | tf_op jit(solution)/shard_map/ppermute | solution.py:463
  55.6 1.5 %collective-permute-start.16 = (f32[520,128]{1,0:T(8,128)S(1)}, f32[520,128]{1,0:T(8,128)S(1)}, u32[]{:S(2)}, u32[]{:S(2)}) collective-permute-start(f32[520,128]{1,0:T(8,128)S(1)} %get-tuple-element.81), channel_id=1, source_target_pairs={{0,1},{1,0},{2,3},{3,2},{4,5},{5,4},{6,7},{7,6},{8,9},{9,8},{10,11... | collective-permute-start | bytes 798728 | tf_op jit(solution)/shard_map/ppermute | solution.py:463
  59.9 11.9 %collective-permute-start.20 = (f32[1024,128]{1,0:T(8,128)S(1)}, f32[1024,128]{1,0:T(8,128)S(1)}, u32[]{:S(2)}, u32[]{:S(2)}) collective-permute-start(f32[1024,128]{1,0:T(8,128)S(1)} %get-tuple-element.60.refs_2_), channel_id=1, source_target_pairs={{0,1},{1,0},{2,3},{3,2},{4,5},{5,4},{6,7},{7,6},{8,9},{9,8},{10,11... | collective-permute-start | bytes 1572872 | tf_op jit(solution)/shard_map/ppermute | solution.py:463
  61.6 10.3 %collective-permute-start.21 = (f32[1024,128]{1,0:T(8,128)S(1)}, f32[1024,128]{1,0:T(8,128)S(1)}, u32[]{:S(2)}, u32[]{:S(2)}) collective-permute-start(f32[1024,128]{1,0:T(8,128)S(1)} %get-tuple-element.61.refs_3_), channel_id=1, source_target_pairs={{0,1},{1,0},{2,3},{3,2},{4,5},{5,4},{6,7},{7,6},{8,9},{9,8},{10,11... | collective-permute-start | bytes 1572872 | tf_op jit(solution)/shard_map/ppermute | solution.py:463
  66.2 13.5 %collective-permute-start.24 = (f32[1024,128]{1,0:T(8,128)S(1)}, f32[1024,128]{1,0:T(8,128)S(1)}, u32[]{:S(2)}, u32[]{:S(2)}) collective-permute-start(f32[1024,128]{1,0:T(8,128)S(1)} %get-tuple-element.62.refs_2_.refs_1_), channel_id=1, source_target_pairs={{0,2},{3,5},{4,6},{2,0},{5,3},{6,4},{8,10},{11,13},{12,14},{10,8},... | collective-permute-start | bytes 1572872 | tf_op jit(solution)/shard_map/ppermute | solution.py:466
  69.3 12.8 %collective-permute-start.19 = (f32[1024,128]{1,0:T(8,128)S(1)}, f32[1024,128]{1,0:T(8,128)S(1)}, u32[]{:S(2)}, u32[]{:S(2)}) collective-permute-start(f32[1024,128]{1,0:T(8,128)S(1)} %get-tuple-element.62.refs_2_.refs_1_), channel_id=1, source_target_pairs={{1,3},{2,4},{5,7},{3,1},{4,2},{7,5},{9,11},{10,12},{13,15},{11,9},... | collective-permute-start | bytes 1572872 | tf_op jit(solution)/shard_map/ppermute | solution.py:466
  71.2 14.4 %collective-permute-start.27 = (f32[1024,128]{1,0:T(8,128)S(1)}, f32[1024,128]{1,0:T(8,128)S(1)}, u32[]{:S(2)}, u32[]{:S(2)}) collective-permute-start(f32[1024,128]{1,0:T(8,128)S(1)} %get-tuple-element.62.refs_2_.refs_1_), channel_id=1, source_target_pairs={{0,1},{1,0},{2,3},{3,2},{4,5},{5,4},{6,7},{7,6},{8,9},{9,8},{10,11... | collective-permute-start | bytes 1572872 | tf_op jit(solution)/shard_map/ppermute | solution.py:463
  72.0 9.6 %collective-permute-start.22 = (f32[32,1024]{1,0:T(8,128)S(1)}, f32[32,1024]{1,0:T(8,128)S(1)}, u32[]{:S(2)}, u32[]{:S(2)}) collective-permute-start(f32[32,1024]{1,0:T(8,128)S(1)} %get-tuple-element.67), channel_id=1, source_target_pairs={{0,8},{16,24},{8,0},{24,16},{1,9},{17,25},{9,1},{25,17},{2,10},{18... | collective-permute-start | bytes 393224 | tf_op jit(solution)/shard_map/ppermute | solution.py:377
  73.3 8.3 %collective-permute-start.23 = (f32[32,1024]{1,0:T(8,128)S(1)}, f32[32,1024]{1,0:T(8,128)S(1)}, u32[]{:S(2)}, u32[]{:S(2)}) collective-permute-start(f32[32,1024]{1,0:T(8,128)S(1)} %get-tuple-element.68.refs_2_), channel_id=1, source_target_pairs={{8,16},{16,8},{9,17},{17,9},{10,18},{18,10},{11,19},{19,11},{12,20... | collective-permute-start | bytes 393224 | tf_op jit(solution)/shard_map/ppermute | solution.py:377
  79.7 13.5 %collective-permute-start.26 = (f32[1024,128]{1,0:T(8,128)S(1)}, f32[1024,128]{1,0:T(8,128)S(1)}, u32[]{:S(2)}, u32[]{:S(2)}) collective-permute-start(f32[1024,128]{1,0:T(8,128)S(1)} %payload.18.refs_2_), channel_id=1, source_target_pairs={{1,3},{2,4},{5,7},{3,1},{4,2},{7,5},{9,11},{10,12},{13,15},{11,9},... | collective-permute-start | bytes 1572872 | tf_op jit(solution)/shard_map/ppermute | solution.py:466
  82.1 15.0 %collective-permute-start.25 = (f32[1024,128]{1,0:T(8,128)S(1)}, f32[1024,128]{1,0:T(8,128)S(1)}, u32[]{:S(2)}, u32[]{:S(2)}) collective-permute-start(f32[1024,128]{1,0:T(8,128)S(1)} %payload.19.refs_1_), channel_id=1, source_target_pairs={{0,2},{3,5},{4,6},{2,0},{5,3},{6,4},{8,10},{11,13},{12,14},{10,8},... | collective-permute-start | bytes 1572872 | tf_op jit(solution)/shard_map/ppermute | solution.py:466
  87.0 12.1 %collective-permute-start.29 = (f32[1024,128]{1,0:T(8,128)S(1)}, f32[1024,128]{1,0:T(8,128)S(1)}, u32[]{:S(2)}, u32[]{:S(2)}) collective-permute-start(f32[1024,128]{1,0:T(8,128)S(1)} %get-tuple-element.69.refs_2_), channel_id=1, source_target_pairs={{0,1},{1,0},{2,3},{3,2},{4,5},{5,4},{6,7},{7,6},{8,9},{9,8},{10,11... | collective-permute-start | bytes 1572872 | tf_op jit(solution)/shard_map/ppermute | solution.py:463
  89.9 9.2 %collective-permute-start.34 = (f32[1024,128]{1,0:T(8,128)S(1)}, f32[1024,128]{1,0:T(8,128)S(1)}, u32[]{:S(2)}, u32[]{:S(2)}) collective-permute-start(f32[1024,128]{1,0:T(8,128)S(1)} %get-tuple-element.70.refs_8_), channel_id=1, source_target_pairs={{0,1},{1,0},{2,3},{3,2},{4,5},{5,4},{6,7},{7,6},{8,9},{9,8},{10,11... | collective-permute-start | bytes 1572872 | tf_op jit(solution)/shard_map/ppermute | solution.py:463
  90.0 13.9 %collective-permute-start.37 = (f32[1024,128]{1,0:T(8,128)S(1)}, f32[1024,128]{1,0:T(8,128)S(1)}, u32[]{:S(2)}, u32[]{:S(2)}) collective-permute-start(f32[1024,128]{1,0:T(8,128)S(1)} %pick.9.refs_2_.refs_1_), channel_id=1, source_target_pairs={{0,1},{1,0},{2,3},{3,2},{4,5},{5,4},{6,7},{7,6},{8,9},{9,8},{10,11... | collective-permute-start | bytes 1572872 | tf_op jit(solution)/shard_map/ppermute | solution.py:463
  93.3 14.7 %collective-permute-start.33 = (f32[1024,128]{1,0:T(8,128)S(1)}, f32[1024,128]{1,0:T(8,128)S(1)}, u32[]{:S(2)}, u32[]{:S(2)}) collective-permute-start(f32[1024,128]{1,0:T(8,128)S(1)} %payload.20.refs_3_), channel_id=1, source_target_pairs={{0,2},{3,5},{4,6},{2,0},{5,3},{6,4},{8,10},{11,13},{12,14},{10,8},... | collective-permute-start | bytes 1572872 | tf_op jit(solution)/shard_map/ppermute | solution.py:466
  97.1 16.3 %collective-permute-start.28 = (f32[1024,128]{1,0:T(8,128)S(1)}, f32[1024,128]{1,0:T(8,128)S(1)}, u32[]{:S(2)}, u32[]{:S(2)}) collective-permute-start(f32[1024,128]{1,0:T(8,128)S(1)} %payload.21.refs_2_), channel_id=1, source_target_pairs={{1,3},{2,4},{5,7},{3,1},{4,2},{7,5},{9,11},{10,12},{13,15},{11,9},... | collective-permute-start | bytes 1572872 | tf_op jit(solution)/shard_map/ppermute | solution.py:466
  99.3 5.6 %collective-permute-start.36 = (f32[512,128]{1,0:T(8,128)S(1)}, f32[512,128]{1,0:T(8,128)S(1)}, u32[]{:S(2)}, u32[]{:S(2)}) collective-permute-start(f32[512,128]{1,0:T(8,128)S(1)} %get-tuple-element.84), channel_id=1, source_target_pairs={{0,1},{1,0},{2,3},{3,2},{4,5},{5,4},{6,7},{7,6},{8,9},{9,8},{10,11... | collective-permute-start | bytes 786440 | tf_op jit(solution)/shard_map/ppermute | solution.py:463
  103.8 1.5 %collective-permute-start.35 = (f32[512,128]{1,0:T(8,128)S(1)}, f32[512,128]{1,0:T(8,128)S(1)}, u32[]{:S(2)}, u32[]{:S(2)}) collective-permute-start(f32[512,128]{1,0:T(8,128)S(1)} %get-tuple-element.85), channel_id=1, source_target_pairs={{0,1},{1,0},{2,3},{3,2},{4,5},{5,4},{6,7},{7,6},{8,9},{9,8},{10,11... | collective-permute-start | bytes 786440 | tf_op jit(solution)/shard_map/ppermute | solution.py:463
  103.9 6.3 %collective-permute-start.32 = (f32[2,256]{1,0:T(2,128)S(1)}, f32[2,256]{1,0:T(2,128)S(1)}, u32[]{:S(2)}, u32[]{:S(2)}) collective-permute-start(f32[2,256]{1,0:T(2,128)S(1)} %get-tuple-element.71.refs_3_.refs_0_), channel_id=1, source_target_pairs={{0,6},{1,7},{2,4},{3,5},{4,2},{5,3},{6,0},{7,1},{8,14},{9,15},{10,... | collective-permute-start | bytes 6152 | tf_op jit(solution)/shard_map/ppermute | solution.py:661
  105.0 8.4 %collective-permute-start.31 = (f32[2,256]{1,0:T(2,128)S(1)}, f32[2,256]{1,0:T(2,128)S(1)}, u32[]{:S(2)}, u32[]{:S(2)}) collective-permute-start(f32[2,256]{1,0:T(2,128)S(1)} %get-tuple-element.71.refs_3_.refs_0_), channel_id=1, source_target_pairs={{0,4},{1,5},{2,6},{3,7},{4,0},{5,1},{6,2},{7,3},{8,12},{9,13},{10,... | collective-permute-start | bytes 6152 | tf_op jit(solution)/shard_map/ppermute | solution.py:661
  105.4 8.0 %collective-permute-start.30 = (f32[2,256]{1,0:T(2,128)S(1)}, f32[2,256]{1,0:T(2,128)S(1)}, u32[]{:S(2)}, u32[]{:S(2)}) collective-permute-start(f32[2,256]{1,0:T(2,128)S(1)} %get-tuple-element.71.refs_3_.refs_0_), channel_id=1, source_target_pairs={{0,2},{1,3},{2,0},{3,1},{4,6},{5,7},{6,4},{7,5},{8,10},{9,11},{10,... | collective-permute-start | bytes 6152 | tf_op jit(solution)/shard_map/ppermute | solution.py:661
  108.0 17.8 %collective-permute-start.39 = (f32[1024,128]{1,0:T(8,128)S(1)}, f32[1024,128]{1,0:T(8,128)S(1)}, u32[]{:S(2)}, u32[]{:S(2)}) collective-permute-start(f32[1024,128]{1,0:T(8,128)S(1)} %payload.22.refs_4_), channel_id=1, source_target_pairs={{1,3},{2,4},{5,7},{3,1},{4,2},{7,5},{9,11},{10,12},{13,15},{11,9},... | collective-permute-start | bytes 1572872 | tf_op jit(solution)/shard_map/ppermute | solution.py:466
  113.5 14.6 %collective-permute-start.38 = (f32[1024,128]{1,0:T(8,128)S(1)}, f32[1024,128]{1,0:T(8,128)S(1)}, u32[]{:S(2)}, u32[]{:S(2)}) collective-permute-start(f32[1024,128]{1,0:T(8,128)S(1)} %payload.23.refs_4_), channel_id=1, source_target_pairs={{0,2},{3,5},{4,6},{2,0},{5,3},{6,4},{8,10},{11,13},{12,14},{10,8},... | collective-permute-start | bytes 1572872 | tf_op jit(solution)/shard_map/ppermute | solution.py:466
  116.3 8.1 %collective-permute-start.41 = (f32[512,128]{1,0:T(8,128)S(1)}, f32[512,128]{1,0:T(8,128)S(1)}, u32[]{:S(2)}, u32[]{:S(2)}) collective-permute-start(f32[512,128]{1,0:T(8,128)S(1)} %get-tuple-element.82), channel_id=1, source_target_pairs={{0,1},{1,0},{2,3},{3,2},{4,5},{5,4},{6,7},{7,6},{8,9},{9,8},{10,11... | collective-permute-start | bytes 786440 | tf_op jit(solution)/shard_map/ppermute | solution.py:463
  120.6 3.8 %collective-permute-start.40 = (f32[512,128]{1,0:T(8,128)S(1)}, f32[512,128]{1,0:T(8,128)S(1)}, u32[]{:S(2)}, u32[]{:S(2)}) collective-permute-start(f32[512,128]{1,0:T(8,128)S(1)} %get-tuple-element.83), channel_id=1, source_target_pairs={{0,1},{1,0},{2,3},{3,2},{4,5},{5,4},{6,7},{7,6},{8,9},{9,8},{10,11... | collective-permute-start | bytes 786440 | tf_op jit(solution)/shard_map/ppermute | solution.py:463
  120.7 3.1 %collective-permute-start.42 = (f32[2,256]{1,0:T(2,128)S(1)}, f32[2,256]{1,0:T(2,128)S(1)}, u32[]{:S(2)}, u32[]{:S(2)}) collective-permute-start(f32[2,256]{1,0:T(2,128)S(1)} %get-tuple-element.77.refs_0_), channel_id=1, source_target_pairs={{0,1},{1,0},{2,3},{3,2},{4,5},{5,4},{6,7},{7,6},{8,9},{9,8},{10,11... | collective-permute-start | bytes 6152 | tf_op jit(solution)/shard_map/ppermute | solution.py:661

commit v14 on v13

--- a/solution.py
+++ b/solution.py
@@ -81,37 +81,34 @@
         out[...] = both[:, :cells] + both[:, cells:]
 
 
-def slot_products(blocks, matrix, field, mine, other):
+def slot_products(blocks, column, matrix, field, mine, other):
     blocks = [for_device(numbers) for numbers in blocks]
-    parts = jnp.concatenate(halves(field[...]), axis=1)
+    parts = jnp.concatenate(halves(field[:, column : column + mine.shape[1]]), axis=1)
     one_slot(blocks, matrix, parts, mine, other)
 
 
 def load_and_products(blocks, column, matrix, distribution, *refs):
-    slots = len(blocks)
+    slots = len(blocks) - 1
     outs, (held, field, sems) = refs[: 2 * slots], refs[2 * slots :]
     cells = field.shape[1]
-    start = pltpu.make_async_copy(
-        distribution.at[:, pl.ds(column, cells)], field, sems.at[2 * slots]
-    )
+    start = pltpu.make_async_copy(distribution.at[:, pl.ds(column, cells)], field, sems.at[0])
     start.start()
     blocks = [[for_device(numbers) for numbers in pair] for pair in blocks]
     copies = []
-    for slot, pair in enumerate(blocks):
-        for k, block in enumerate(pair):
-            rows = rows_of(held, block)
-            copies.append(
-                pltpu.make_async_copy(
-                    matrix.at[rows, :], held.at[rows, :], sems.at[2 * slot + k]
-                )
-            )
-            copies[-1].start()
+    for block in (block for pair in blocks for block in pair):
+        rows = rows_of(held, block)
+        copies.append(
+            pltpu.make_async_copy(matrix.at[rows, :], held.at[rows, :], sems.at[1 + len(copies)])
+        )
+        copies[-1].start()
     start.wait()
     parts = jnp.concatenate(halves(field[...]), axis=1)
-    for slot, pair in enumerate(blocks):
-        for k in range(2):
-            copies[2 * slot + k].wait()
+    for slot, pair in enumerate(blocks[:-1]):
+        for copy in copies[2 * slot : 2 * slot + 2]:
+            copy.wait()
         one_slot(pair, held, parts, outs[2 * slot], outs[2 * slot + 1])
+    for copy in copies[2 * slots :]:
+        copy.wait()
 
 
 def two_blocks(numbers, parts, first, last, scale, rows, matrix, *refs):
@@ -475,10 +472,10 @@
             self.arrived = [[along(0, own)], [along(1, own)]]
             self.blocks = []
 
-        def add_terms(self, field, parts=1):
-            kernel = functools.partial(slot_products, plan.rows[len(self.terms)])
+        def add_terms(self, field, column=0):
+            kernel = functools.partial(slot_products, plan.rows[len(self.terms)], column)
             mine, other = call(kernel, [part] * 2, [self.matrix, field])
-            self.terms.append((mine, *exchange(other, parts)))
+            self.terms.append((mine, *exchange(other)))
 
         def join_terms(self, *slots):
             for slot in slots:
@@ -558,7 +555,7 @@
     one.begin(own)
     *terms, matrix = call(
         functools.partial(load_and_products, plan.rows, half),
-        [part] * (2 * chips) + [jax.ShapeDtypeStruct(scatter_matrix.shape, jnp.bfloat16)],
+        [part] * (2 * chips - 2) + [jax.ShapeDtypeStruct(scatter_matrix.shape, jnp.bfloat16)],
         [scatter_matrix, distribution],
         places=[HBM] * 2,
         scratch=[
@@ -568,7 +565,7 @@
         room=28,
     )
     one.matrix = matrix
-    one.terms = [(terms[2 * s], *exchange(terms[2 * s + 1])) for s in range(chips)]
+    one.terms = [(terms[2 * s], *exchange(terms[2 * s + 1])) for s in range(chips - 1)]
     one.take_own()
     operators = jnp.asarray(differences(cells))
     strips = None
@@ -583,11 +580,15 @@
             one.take(1)
         one.send(step, unpack if step == 2 else None)
         if step == 1:
-            one.join_terms(*(s for s in range(chips) if isinstance(one.terms[s], tuple)))
+            one.join_terms(*(s for s in range(chips - 1) if isinstance(one.terms[s], tuple)))
             strips = call(strip_rows, [(HALO, modes)] * 2, [distribution])
             strips = paired(*call(strip_pairs, [(HALO, modes)] * 2, strips))
         else:
             one.take(step, 2 if step == chips - 1 else 1)
+        if step == 2:
+            one.add_terms(distribution, half)
+        if step == chips - 1:
+            one.join_terms(chips - 1)
         one.multiply(step - 1)
         if step == min(2, chips - 1):
             base_a, base_b = call(

time: 132 us -> 130 us (0.985)
  waiting for transfers between devices: 23.3 us -> 19.9 us
  starting transfers between devices: 68.4 us -> 70.2 us
    ppermute x16, waiting for transfers between devices: 18.3 us -> 14.6 us  [along(): return lax.ppermute(value, 'mode', plan.pairs[stream])]
    ppermute x16, starting transfers between devices: 41.9 us -> 43.4 us  [along(): return lax.ppermute(value, 'mode', plan.pairs[stream])]
    pallas_call x55 -> x56, Pallas kernels: 35 us -> 34.8 us  [__call__(): pl.pallas_call(body, out_shape=[jax.ShapeDtypeStruct(shape, jnp.float32)...]
  transfers between devices with their start and end apart: 43 -> 43, of which waited for: 13 -> 12; matrix products, arithmetic and copies ran while one was open for 0% -> 0% of each run, Pallas kernels for 25% -> 25%
where the time goes in v14:
time: 130 us; the launch traced here: 127 us
  starting transfers between devices  70.2 us (54%)
  Pallas kernels  34.8 us (27%)
  waiting for transfers between devices  19.9 us (15%)
  between operations  1.61 us (1%)
    ppermute x16, starting transfers between devices, along(): return lax.ppermute(value, 'mode', plan.pairs[stream])  43.4 us
    pallas_call x56, Pallas kernels, __call__(): pl.pallas_call(body, out_shape=[jax.ShapeDtypeStruct(shape, jnp.float32)...  34.8 us
    ppermute x19, starting transfers between devices, exchange(): lax.ppermute(value[i:j], 'mode', across)  18.4 us
    ppermute x16, waiting for transfers between devices, along(): return lax.ppermute(value, 'mode', plan.pairs[stream])  14.6 us
    ppermute x4, starting transfers between devices, paired(): lax.ppermute(value, 'space', pairs + [(j, i) for i, j in pairs])  6.74 us
    ppermute x4, waiting for transfers between devices, over(): lax.ppermute(self.value, 'mode', [(i, i ^ bit) for i in range(self.device...  3.17 us
  transfers between devices with their start and end apart: 43, of which 12 were waited for; matrix products, arithmetic and copies ran while one was open for 0% of the time, Pallas kernels for 25%

profile of v14, /device:TPU:13, one launch (start us, length us, event | category | flops | bytes accessed | tf_op | source)
XLA Modules:
  0.0 127.5 jit_solution(12068767571041385018)
XLA Ops:
  0.6 2.0 %own_rows.1 = (f32[1040,128]{1,0:T(8,128)}, f32[8,128]{1,0:T(8,128)}) custom-call(f32[1024,256]{1,0:T(8,128)} %refs_0_.9, f32[2,1024]{1,0:T(2,128)} %refs_1_.3, f32[1,1024]{1,0:T(1,128)} %bitcast.4), custom_call_target="tpu_custom_call" | custom-call | flops 1024 | bytes 1024 | tf_op jit(solution)/shard_map/own_rows/pallas_call | solution.py:39
  2.6 3.2 %collective-permute-start.2 = (f32[1040,128]{1,0:T(8,128)}, f32[1040,128]{1,0:T(8,128)S(1)}, u32[]{:S(2)}, u32[]{:S(2)}) collective-permute-start(f32[1040,128]{1,0:T(8,128)} %get-tuple-element.41.refs_1_), channel_id=1, source_target_pairs={{0,2},{3,5},{4,6},{2,0},{5,3},{6,4},{8,10},{11,13},{12,14},{10,8},... | collective-permute-start | bytes 1597448 | tf_op jit(solution)/shard_map/ppermute | solution.py:463
  5.8 1.9 %collective-permute-start = (f32[1040,128]{1,0:T(8,128)}, f32[1040,128]{1,0:T(8,128)S(1)}, u32[]{:S(2)}, u32[]{:S(2)}) collective-permute-start(f32[1040,128]{1,0:T(8,128)} %get-tuple-element.41.refs_1_), channel_id=1, source_target_pairs={{1,3},{2,4},{5,7},{3,1},{4,2},{7,5},{9,11},{10,12},{13,15},{11,9},... | collective-permute-start | bytes 1597448 | tf_op jit(solution)/shard_map/ppermute | solution.py:463
  7.8 0.7 copy-done.3
  8.5 6.2 %load_and_products.1 = (f32[1024,128]{1,0:T(8,128)S(1)}, f32[1024,128]{1,0:T(8,128)S(1)}, f32[1024,128]{1,0:T(8,128)S(1)}, f32[1024,128]{1,0:T(8,128)S(1)}, f32[...) custom-call(bf16[8192,1024]{1,0:T(8,128)(2,1)} %refs_0_.6, f32[1024,256]{1,0:T(8,128)S(1)} %copy-done, ...), custom_call_target="tpu_custom_call" | custom-call | flops 1024 | bytes 1024 | tf_op jit(solution)/shard_map/load_and_products/pallas_call | solution.py:39
  14.6 2.6 %collective-permute-start.1 = (f32[1024,128]{1,0:T(8,128)S(1)}, f32[1024,128]{1,0:T(8,128)S(1)}, u32[]{:S(2)}, u32[]{:S(2)}) collective-permute-start(f32[1024,128]{1,0:T(8,128)S(1)} %get-tuple-element.44), channel_id=1, source_target_pairs={{0,1},{1,0},{2,3},{3,2},{4,5},{5,4},{6,7},{7,6},{8,9},{9,8},{10,11... | collective-permute-start | bytes 1572872 | tf_op jit(solution)/shard_map/ppermute | solution.py:460
  17.3 0.4 collective-permute-start.5
  17.7 0.5 collective-permute-start.9
  18.2 1.5 %collective-permute-done.refs_1_.refs_0_ = f32[1040,128]{1,0:T(8,128)S(1)} collective-permute-done((f32[1040,128]{1,0:T(8,128)}, f32[1040,128]{1,0:T(8,128)S(1)}, u32[]{:S(2)}, u32[]{:S(2)}) %collective-permute-start) | collective-permute-done | bytes 532512 | tf_op jit(solution)/shard_map/ppermute | solution.py:463
  19.9 2.1 %collective-permute-start.8 = (f32[1040,128]{1,0:T(8,128)S(1)}, f32[1040,128]{1,0:T(8,128)S(1)}, u32[]{:S(2)}, u32[]{:S(2)}) collective-permute-start(f32[1040,128]{1,0:T(8,128)S(1)} %payload.12.refs_2_), channel_id=1, source_target_pairs={{1,3},{2,4},{5,7},{3,1},{4,2},{7,5},{9,11},{10,12},{13,15},{11,9},... | collective-permute-start | bytes 1597448 | tf_op jit(solution)/shard_map/ppermute | solution.py:463
  22.0 4.7 %collective-permute-start.3 = (f32[1040,128]{1,0:T(8,128)S(1)}, f32[1040,128]{1,0:T(8,128)S(1)}, u32[]{:S(2)}, u32[]{:S(2)}) collective-permute-start(f32[1040,128]{1,0:T(8,128)S(1)} %payload.13.refs_2_), channel_id=1, source_target_pairs={{0,2},{3,5},{4,6},{2,0},{5,3},{6,4},{8,10},{11,13},{12,14},{10,8},... | collective-permute-start | bytes 1597448 | tf_op jit(solution)/shard_map/ppermute | solution.py:463
  27.3 1.3 %collective-permute-start.6 = (f32[32,1024]{1,0:T(8,128)S(1)}, f32[32,1024]{1,0:T(8,128)S(1)}, u32[]{:S(2)}, u32[]{:S(2)}) collective-permute-start(f32[32,1024]{1,0:T(8,128)S(1)} %get-tuple-element.52), channel_id=1, source_target_pairs={{0,8},{16,24},{8,0},{24,16},{1,9},{17,25},{9,1},{25,17},{2,10},{18... | collective-permute-start | bytes 393224 | tf_op jit(solution)/shard_map/ppermute | solution.py:374
  28.6 2.1 %collective-permute-start.7 = (f32[32,1024]{1,0:T(8,128)S(1)}, f32[32,1024]{1,0:T(8,128)S(1)}, u32[]{:S(2)}, u32[]{:S(2)}) collective-permute-start(f32[32,1024]{1,0:T(8,128)S(1)} %get-tuple-element.53.refs_3_), channel_id=1, source_target_pairs={{8,16},{16,8},{9,17},{17,9},{10,18},{18,10},{11,19},{19,11},{12,20... | collective-permute-start | bytes 393224 | tf_op jit(solution)/shard_map/ppermute | solution.py:374
  30.7 1.4 %two_blocks.8.refs_3_ = f32[272,1024]{1,0:T(8,128)S(1)} custom-call(bf16[8192,1024]{1,0:T(8,128)(2,1)S(1)} %get-tuple-element.45.refs_2_.refs_0_, f32[1040,128]{1,0:T(8,128)S(1)} %copy-done.2, f32[1040,128]{1,0:T(8,128)S(1)} %collective-permute-done.9.refs_2_, f32[32,1024]{1,0:T(8,128)S(1)} %get-tuple-element.53.refs_3_), custom_call_target="tpu_custom_call" | custom-call | flops 1024 | bytes 1024 | tf_op jit(solution)/shard_map/two_blocks/pallas_call | solution.py:39
  32.2 5.1 %collective-permute-start.11 = (f32[1040,128]{1,0:T(8,128)S(1)}, f32[1040,128]{1,0:T(8,128)S(1)}, u32[]{:S(2)}, u32[]{:S(2)}) collective-permute-start(f32[1040,128]{1,0:T(8,128)S(1)} %payload.14.refs_2_), channel_id=1, source_target_pairs={{0,2},{3,5},{4,6},{2,0},{5,3},{6,4},{8,10},{11,13},{12,14},{10,8},... | collective-permute-start | bytes 1597448 | tf_op jit(solution)/shard_map/ppermute | solution.py:463
  37.6 1.9 %collective-permute-start.10 = (f32[1040,128]{1,0:T(8,128)S(1)}, f32[1040,128]{1,0:T(8,128)S(1)}, u32[]{:S(2)}, u32[]{:S(2)}) collective-permute-start(f32[1040,128]{1,0:T(8,128)S(1)} %payload.15.refs_3_), channel_id=1, source_target_pairs={{1,3},{2,4},{5,7},{3,1},{4,2},{7,5},{9,11},{10,12},{13,15},{11,9},... | collective-permute-start | bytes 1597448 | tf_op jit(solution)/shard_map/ppermute | solution.py:463
  39.6 1.3 slot_products.5
  40.9 0.6 collective-permute-start.15
  41.7 1.4 %two_blocks.9.refs_5_.refs_3_ = f32[272,1024]{1,0:T(8,128)S(1)} custom-call(bf16[8192,1024]{1,0:T(8,128)(2,1)S(1)} %get-tuple-element.45.refs_2_.refs_0_, f32[1040,128]{1,0:T(8,128)S(1)} %pick.6.refs_2_.refs_1_, f32[1040,128]{1,0:T(8,128)S(1)} %collective-permute-done.12.refs_2_, f32[272,1024]{1,0:T(8,128)S(1)} %two_blocks.8.refs_3_, ...), custom_call_target="tpu_custom_call" | custom-call | flops 1024 | bytes 1024 | tf_op jit(solution)/shard_map/two_blocks/pallas_call | solution.py:39
  43.1 2.0 %first_rest.1 = (f32[1024,128]{1,0:T(8,128)S(1)}, f32[1024,128]{1,0:T(8,128)S(1)}) custom-call(f32[1024,256]{1,0:T(8,128)S(1)} %copy-done, bf16[1024,128]{1,0:T(8,128)(2,1)S(1)} %strip_columns.2.refs_3_.refs_1_, bf16[640,1024]{1,0:T(8,128)(2,1)S(1)} %copy-done.1, f32[8,1024]{1,0:T(8,128)S(1)} %maximum_maximum_fusion.refs_3_.refs_5_, s32[1,256]{1,0:T(1,128)S(1)} %bitcast.2, ...), custom_call_target="tpu_custom_call" | custom-call | flops 1024 | bytes 1024 | tf_op jit(solution)/shard_map/first_rest/pallas_call | solution.py:39
  45.1 2.0 %collective-permute-done.11.refs_0_.refs_1_ = f32[1040,128]{1,0:T(8,128)S(1)} collective-permute-done((f32[1040,128]{1,0:T(8,128)S(1)}, f32[1040,128]{1,0:T(8,128)S(1)}, u32[]{:S(2)}, u32[]{:S(2)}) %collective-permute-start.11) | collective-permute-done | bytes 532512 | tf_op jit(solution)/shard_map/ppermute | solution.py:463
  47.2 1.9 %collective-permute-start.14 = (f32[1040,128]{1,0:T(8,128)S(1)}, f32[1040,128]{1,0:T(8,128)S(1)}, u32[]{:S(2)}, u32[]{:S(2)}) collective-permute-start(f32[1040,128]{1,0:T(8,128)S(1)} %payload.16.refs_3_), channel_id=1, source_target_pairs={{1,3},{2,4},{5,7},{3,1},{4,2},{7,5},{9,11},{10,12},{13,15},{11,9},... | collective-permute-start | bytes 1597448 | tf_op jit(solution)/shard_map/ppermute | solution.py:463
  49.3 3.5 %collective-permute-start.13 = (f32[1040,128]{1,0:T(8,128)S(1)}, f32[1040,128]{1,0:T(8,128)S(1)}, u32[]{:S(2)}, u32[]{:S(2)}) collective-permute-start(f32[1040,128]{1,0:T(8,128)S(1)} %payload.17.refs_4_), channel_id=1, source_target_pairs={{0,2},{3,5},{4,6},{2,0},{5,3},{6,4},{8,10},{11,13},{12,14},{10,8},... | collective-permute-start | bytes 1597448 | tf_op jit(solution)/shard_map/ppermute | solution.py:463
  53.2 0.5 collective-permute-start.16
  53.8 1.4 %two_blocks.10.refs_4_.refs_6_ = f32[272,1024]{1,0:T(8,128)S(1)} custom-call(bf16[8192,1024]{1,0:T(8,128)(2,1)S(1)} %get-tuple-element.45.refs_2_.refs_0_, f32[1040,128]{1,0:T(8,128)S(1)} %pick.7.refs_2_.refs_1_, f32[1040,128]{1,0:T(8,128)S(1)} %collective-permute-done.18.refs_2_, f32[272,1024]{1,0:T(8,128)S(1)} %two_blocks.9.refs_5_.refs_3_, ...), custom_call_target="tpu_custom_call" | custom-call | flops 1024 | bytes 1024 | tf_op jit(solution)/shard_map/two_blocks/pallas_call | solution.py:39
  55.2 1.5 %two_blocks.11 = (f32[1024,128]{1,0:T(8,128)S(1)}, f32[32,1024]{1,0:T(8,128)S(1)}, f32[8,1024]{1,0:T(8,128)S(1)}) custom-call(bf16[8192,1024]{1,0:T(8,128)(2,1)S(1)} %get-tuple-element.45.refs_2_.refs_0_, f32[1040,128]{1,0:T(8,128)S(1)} %pick.8.refs_2_.refs_1_, f32[520,128]{1,0:T(8,128)S(1)} %collective-permute-done.16.refs_2_, ...), custom_call_target="tpu_custom_call" | custom-call | flops 1024 | bytes 1024 | tf_op jit(solution)/shard_map/two_blocks/pallas_call | solution.py:39
  56.7 1.3 slot_products.6
  58.2 1.3 slot_products.7
  59.4 0.5 collective-permute-start.21
  60.0 3.2 %collective-permute-done.13.refs_0_ = f32[1040,128]{1,0:T(8,128)S(1)} collective-permute-done((f32[1040,128]{1,0:T(8,128)S(1)}, f32[1040,128]{1,0:T(8,128)S(1)}, u32[]{:S(2)}, u32[]{:S(2)}) %collective-permute-start.13) | collective-permute-done | bytes 532512 | tf_op jit(solution)/shard_map/ppermute | solution.py:463
  63.4 3.3 %collective-permute-start.24 = (f32[1024,128]{1,0:T(8,128)S(1)}, f32[1024,128]{1,0:T(8,128)S(1)}, u32[]{:S(2)}, u32[]{:S(2)}) collective-permute-start(f32[1024,128]{1,0:T(8,128)S(1)} %get-tuple-element.62.refs_2_.refs_1_), channel_id=1, source_target_pairs={{0,2},{3,5},{4,6},{2,0},{5,3},{6,4},{8,10},{11,13},{12,14},{10,8},... | collective-permute-start | bytes 1572872 | tf_op jit(solution)/shard_map/ppermute | solution.py:463
  66.8 1.9 %collective-permute-start.19 = (f32[1024,128]{1,0:T(8,128)S(1)}, f32[1024,128]{1,0:T(8,128)S(1)}, u32[]{:S(2)}, u32[]{:S(2)}) collective-permute-start(f32[1024,128]{1,0:T(8,128)S(1)} %get-tuple-element.62.refs_2_.refs_1_), channel_id=1, source_target_pairs={{1,3},{2,4},{5,7},{3,1},{4,2},{7,5},{9,11},{10,12},{13,15},{11,9},... | collective-permute-start | bytes 1572872 | tf_op jit(solution)/shard_map/ppermute | solution.py:463
  68.7 1.0 collective-permute-start.27
  69.9 1.3 %collective-permute-start.22 = (f32[32,1024]{1,0:T(8,128)S(1)}, f32[32,1024]{1,0:T(8,128)S(1)}, u32[]{:S(2)}, u32[]{:S(2)}) collective-permute-start(f32[32,1024]{1,0:T(8,128)S(1)} %get-tuple-element.67), channel_id=1, source_target_pairs={{0,8},{16,24},{8,0},{24,16},{1,9},{17,25},{9,1},{25,17},{2,10},{18... | collective-permute-start | bytes 393224 | tf_op jit(solution)/shard_map/ppermute | solution.py:374
  71.2 2.1 %collective-permute-start.23 = (f32[32,1024]{1,0:T(8,128)S(1)}, f32[32,1024]{1,0:T(8,128)S(1)}, u32[]{:S(2)}, u32[]{:S(2)}) collective-permute-start(f32[32,1024]{1,0:T(8,128)S(1)} %get-tuple-element.68.refs_2_), channel_id=1, source_target_pairs={{8,16},{16,8},{9,17},{17,9},{10,18},{18,10},{11,19},{19,11},{12,20... | collective-permute-start | bytes 393224 | tf_op jit(solution)/shard_map/ppermute | solution.py:374
  73.3 2.9 %collective-permute-done.24.refs_0_ = f32[1024,128]{1,0:T(8,128)S(1)} collective-permute-done((f32[1024,128]{1,0:T(8,128)S(1)}, f32[1024,128]{1,0:T(8,128)S(1)}, u32[]{:S(2)}, u32[]{:S(2)}) %collective-permute-start.24) | collective-permute-done | bytes 524320 | tf_op jit(solution)/shard_map/ppermute | solution.py:463
  76.2 1.9 %collective-permute-start.26 = (f32[1024,128]{1,0:T(8,128)S(1)}, f32[1024,128]{1,0:T(8,128)S(1)}, u32[]{:S(2)}, u32[]{:S(2)}) collective-permute-start(f32[1024,128]{1,0:T(8,128)S(1)} %payload.18.refs_2_), channel_id=1, source_target_pairs={{1,3},{2,4},{5,7},{3,1},{4,2},{7,5},{9,11},{10,12},{13,15},{11,9},... | collective-permute-start | bytes 1572872 | tf_op jit(solution)/shard_map/ppermute | solution.py:463
  78.1 0.6 collective-permute-done.23.refs_1_
  78.9 1.0 collective-permute-done.19.refs_0_.refs_1_
  79.9 3.3 %collective-permute-start.25 = (f32[1024,128]{1,0:T(8,128)S(1)}, f32[1024,128]{1,0:T(8,128)S(1)}, u32[]{:S(2)}, u32[]{:S(2)}) collective-permute-start(f32[1024,128]{1,0:T(8,128)S(1)} %payload.19.refs_1_), channel_id=1, source_target_pairs={{0,2},{3,5},{4,6},{2,0},{5,3},{6,4},{8,10},{11,13},{12,14},{10,8},... | collective-permute-start | bytes 1572872 | tf_op jit(solution)/shard_map/ppermute | solution.py:463
  83.3 1.3 slot_products.8
  84.6 2.1 %collective-permute-start.29 = (f32[1024,128]{1,0:T(8,128)S(1)}, f32[1024,128]{1,0:T(8,128)S(1)}, u32[]{:S(2)}, u32[]{:S(2)}) collective-permute-start(f32[1024,128]{1,0:T(8,128)S(1)} %get-tuple-element.69.refs_2_), channel_id=1, source_target_pairs={{0,1},{1,0},{2,3},{3,2},{4,5},{5,4},{6,7},{7,6},{8,9},{9,8},{10,11... | collective-permute-start | bytes 1572872 | tf_op jit(solution)/shard_map/ppermute | solution.py:460
  86.6 1.2 slot_products.9
  88.0 0.5 collective-permute-start.37
  88.5 2.6 %second_rest.1 = (f32[1024,128]{1,0:T(8,128)S(1)}, f32[1024,128]{1,0:T(8,128)S(1)}, f32[2,256]{1,0:T(2,128)S(1)}) custom-call(f32[1024,256]{1,0:T(8,128)S(1)} %copy-done, f32[1024,128]{1,0:T(8,128)S(1)} %get-tuple-element.58.refs_1_, f32[1024,128]{1,0:T(8,128)S(1)} %get-tuple-element.62.refs_2_.refs_1_, bf16[1024,128]{1,0:T(8,128)(2,1)S(1)} %strip_columns.3.refs_2_.refs_3_, ...), custom_call_target="tpu_custom_call" | custom-call | flops 1024 | bytes 1024 | tf_op jit(solution)/shard_map/second_rest/pallas_call | solution.py:39
  91.2 1.9 %collective-permute-start.33 = (f32[1024,128]{1,0:T(8,128)S(1)}, f32[1024,128]{1,0:T(8,128)S(1)}, u32[]{:S(2)}, u32[]{:S(2)}) collective-permute-start(f32[1024,128]{1,0:T(8,128)S(1)} %payload.20.refs_3_), channel_id=1, source_target_pairs={{0,2},{3,5},{4,6},{2,0},{5,3},{6,4},{8,10},{11,13},{12,14},{10,8},... | collective-permute-start | bytes 1572872 | tf_op jit(solution)/shard_map/ppermute | solution.py:463
  93.1 1.9 %collective-permute-done.25.refs_0_ = f32[1024,128]{1,0:T(8,128)S(1)} collective-permute-done((f32[1024,128]{1,0:T(8,128)S(1)}, f32[1024,128]{1,0:T(8,128)S(1)}, u32[]{:S(2)}, u32[]{:S(2)}) %collective-permute-start.25) | collective-permute-done | bytes 524320 | tf_op jit(solution)/shard_map/ppermute | solution.py:463
  95.1 1.9 %collective-permute-start.28 = (f32[1024,128]{1,0:T(8,128)S(1)}, f32[1024,128]{1,0:T(8,128)S(1)}, u32[]{:S(2)}, u32[]{:S(2)}) collective-permute-start(f32[1024,128]{1,0:T(8,128)S(1)} %payload.21.refs_2_), channel_id=1, source_target_pairs={{1,3},{2,4},{5,7},{3,1},{4,2},{7,5},{9,11},{10,12},{13,15},{11,9},... | collective-permute-start | bytes 1572872 | tf_op jit(solution)/shard_map/ppermute | solution.py:463
  97.3 4.8 %collective-permute-start.36 = (f32[512,128]{1,0:T(8,128)S(1)}, f32[512,128]{1,0:T(8,128)S(1)}, u32[]{:S(2)}, u32[]{:S(2)}) collective-permute-start(f32[512,128]{1,0:T(8,128)S(1)} %get-tuple-element.84), channel_id=1, source_target_pairs={{0,1},{1,0},{2,3},{3,2},{4,5},{5,4},{6,7},{7,6},{8,9},{9,8},{10,11... | collective-permute-start | bytes 786440 | tf_op jit(solution)/shard_map/ppermute | solution.py:460
  102.2 1.1 collective-permute-done.36.refs_3_
  103.3 0.4 collective-permute-done.35.refs_2_
  103.7 1.2 collective-permute-start.30
  104.9 1.3 %two_blocks.12.refs_3_ = f32[256,1024]{1,0:T(8,128)S(1)} custom-call(bf16[8192,1024]{1,0:T(8,128)(2,1)S(1)} %get-tuple-element.45.refs_2_.refs_0_, f32[1024,128]{1,0:T(8,128)S(1)} %pick.10.refs_1_, f32[512,128]{1,0:T(8,128)S(1)} %collective-permute-done.35.refs_2_, f32[512,128]{1,0:T(8,128)S(1)} %collective-permute-done.36.refs_3_, ...), custom_call_target="tpu_custom_call" | custom-call | flops 1024 | bytes 1024 | tf_op jit(solution)/shard_map/two_blocks/pallas_call | solution.py:39
  106.3 2.2 %collective-permute-start.39 = (f32[1024,128]{1,0:T(8,128)S(1)}, f32[1024,128]{1,0:T(8,128)S(1)}, u32[]{:S(2)}, u32[]{:S(2)}) collective-permute-start(f32[1024,128]{1,0:T(8,128)S(1)} %payload.22.refs_4_), channel_id=1, source_target_pairs={{1,3},{2,4},{5,7},{3,1},{4,2},{7,5},{9,11},{10,12},{13,15},{11,9},... | collective-permute-start | bytes 1572872 | tf_op jit(solution)/shard_map/ppermute | solution.py:463
  108.5 3.2 %collective-permute-done.31.refs_2_ = f32[2,256]{1,0:T(2,128)S(1)} collective-permute-done((f32[2,256]{1,0:T(2,128)S(1)}, f32[2,256]{1,0:T(2,128)S(1)}, u32[]{:S(2)}, u32[]{:S(2)}) %collective-permute-start.31) | collective-permute-done | bytes 2080 | tf_op jit(solution)/shard_map/ppermute | solution.py:662
  111.8 2.5 %collective-permute-start.38 = (f32[1024,128]{1,0:T(8,128)S(1)}, f32[1024,128]{1,0:T(8,128)S(1)}, u32[]{:S(2)}, u32[]{:S(2)}) collective-permute-start(f32[1024,128]{1,0:T(8,128)S(1)} %payload.23.refs_4_), channel_id=1, source_target_pairs={{0,2},{3,5},{4,6},{2,0},{5,3},{6,4},{8,10},{11,13},{12,14},{10,8},... | collective-permute-start | bytes 1572872 | tf_op jit(solution)/shard_map/ppermute | solution.py:463
  114.6 4.3 %collective-permute-start.41 = (f32[512,128]{1,0:T(8,128)S(1)}, f32[512,128]{1,0:T(8,128)S(1)}, u32[]{:S(2)}, u32[]{:S(2)}) collective-permute-start(f32[512,128]{1,0:T(8,128)S(1)} %get-tuple-element.82), channel_id=1, source_target_pairs={{0,1},{1,0},{2,3},{3,2},{4,5},{5,4},{6,7},{7,6},{8,9},{9,8},{10,11... | collective-permute-start | bytes 786440 | tf_op jit(solution)/shard_map/ppermute | solution.py:460
  119.0 0.4 collective-permute-start.42
  119.5 1.3 %two_blocks.13.refs_3_.refs_4_ = f32[256,1024]{1,0:T(8,128)S(1)} custom-call(bf16[8192,1024]{1,0:T(8,128)(2,1)S(1)} %get-tuple-element.45.refs_2_.refs_0_, f32[1024,128]{1,0:T(8,128)S(1)} %get-tuple-element.62.refs_2_.refs_1_, f32[1024,128]{1,0:T(8,128)S(1)} %pass_on.2.refs_2_, f32[256,1024]{1,0:T(8,128)S(1)} %two_blocks.12.refs_3_, ...), custom_call_target="tpu_custom_call" | custom-call | flops 1024 | bytes 1024 | tf_op jit(solution)/shard_map/two_blocks/pallas_call | solution.py:39
  120.8 1.3 %two_blocks.14.refs_2_.refs_4_ = f32[256,1024]{1,0:T(8,128)S(1)} custom-call(bf16[8192,1024]{1,0:T(8,128)(2,1)S(1)} %get-tuple-element.45.refs_2_.refs_0_, f32[1024,128]{1,0:T(8,128)S(1)} %pick.9.refs_2_.refs_1_, f32[1024,128]{1,0:T(8,128)S(1)} %pass_on.3.refs_4_.refs_2_, f32[256,1024]{1,0:T(8,128)S(1)} %two_blocks.13.refs_3_.refs_4_, ...), custom_call_target="tpu_custom_call" | custom-call | flops 1024 | bytes 1024 | tf_op jit(solution)/shard_map/two_blocks/pallas_call | solution.py:39
  122.1 0.6 add_all.3
  122.7 1.4 %two_blocks.15.refs_3_.refs_2_ = f32[1024,128]{1,0:T(8,128)S(1)} custom-call(bf16[8192,1024]{1,0:T(8,128)(2,1)S(1)} %get-tuple-element.45.refs_2_.refs_0_, f32[1024,128]{1,0:T(8,128)S(1)} %pick.11.refs_4_.refs_1_, f32[512,128]{1,0:T(8,128)S(1)} %collective-permute-done.40.refs_2_, f32[512,128]{1,0:T(8,128)S(1)} %collective-permute-done.41.refs_3_, ...), custom_call_target="tpu_custom_call" | custom-call | flops 1024 | bytes 1024 | tf_op jit(solution)/shard_map/two_blocks/pallas_call | solution.py:39
  124.2 2.1 %collective-permute-done.38.refs_0_ = f32[1024,128]{1,0:T(8,128)S(1)} collective-permute-done((f32[1024,128]{1,0:T(8,128)S(1)}, f32[1024,128]{1,0:T(8,128)S(1)}, u32[]{:S(2)}, u32[]{:S(2)}) %collective-permute-start.38) | collective-permute-done | bytes 524320 | tf_op jit(solution)/shard_map/ppermute | solution.py:463
  126.3 1.0 last_sum.1
  (99 shorter events, 4.4 us)
Async XLA Ops:
  0.6 7.1 %copy-start = (f32[1024,256]{1,0:T(8,128)S(1)}, f32[1024,256]{1,0:T(8,128)}, u32[]{:S(2)}) copy-start(f32[1024,256]{1,0:T(8,128)} %refs_0_.9) | copy-start | bytes 3145732
  2.6 15.1 %collective-permute-start.2 = (f32[1040,128]{1,0:T(8,128)}, f32[1040,128]{1,0:T(8,128)S(1)}, u32[]{:S(2)}, u32[]{:S(2)}) collective-permute-start(f32[1040,128]{1,0:T(8,128)} %get-tuple-element.41.refs_1_), channel_id=1, source_target_pairs={{0,2},{3,5},{4,6},{2,0},{5,3},{6,4},{8,10},{11,13},{12,14},{10,8},... | collective-permute-start | bytes 1597448 | tf_op jit(solution)/shard_map/ppermute | solution.py:463
  5.8 13.9 %collective-permute-start = (f32[1040,128]{1,0:T(8,128)}, f32[1040,128]{1,0:T(8,128)S(1)}, u32[]{:S(2)}, u32[]{:S(2)}) collective-permute-start(f32[1040,128]{1,0:T(8,128)} %get-tuple-element.41.refs_1_), channel_id=1, source_target_pairs={{1,3},{2,4},{5,7},{3,1},{4,2},{7,5},{9,11},{10,12},{13,15},{11,9},... | collective-permute-start | bytes 1597448 | tf_op jit(solution)/shard_map/ppermute | solution.py:463
  7.8 0.7 copy-start.3
  8.5 9.3 %copy-start.2 = (f32[1040,128]{1,0:T(8,128)S(1)}, f32[1040,128]{1,0:T(8,128)}, u32[]{:S(2)}) copy-start(f32[1040,128]{1,0:T(8,128)} %get-tuple-element.41.refs_1_) | copy-start | bytes 1597444
  14.6 5.1 %collective-permute-start.1 = (f32[1024,128]{1,0:T(8,128)S(1)}, f32[1024,128]{1,0:T(8,128)S(1)}, u32[]{:S(2)}, u32[]{:S(2)}) collective-permute-start(f32[1024,128]{1,0:T(8,128)S(1)} %get-tuple-element.44), channel_id=1, source_target_pairs={{0,1},{1,0},{2,3},{3,2},{4,5},{5,4},{6,7},{7,6},{8,9},{9,8},{10,11... | collective-permute-start | bytes 1572872 | tf_op jit(solution)/shard_map/ppermute | solution.py:460
  17.2 9.5 %collective-permute-start.4 = (f32[1024,128]{1,0:T(8,128)S(1)}, f32[1024,128]{1,0:T(8,128)S(1)}, u32[]{:S(2)}, u32[]{:S(2)}) collective-permute-start(f32[1024,128]{1,0:T(8,128)S(1)} %get-tuple-element.47), channel_id=1, source_target_pairs={{0,1},{1,0},{2,3},{3,2},{4,5},{5,4},{6,7},{7,6},{8,9},{9,8},{10,11... | collective-permute-start | bytes 1572872 | tf_op jit(solution)/shard_map/ppermute | solution.py:460
  17.3 9.5 %collective-permute-start.5 = (f32[1024,128]{1,0:T(8,128)S(1)}, f32[1024,128]{1,0:T(8,128)S(1)}, u32[]{:S(2)}, u32[]{:S(2)}) collective-permute-start(f32[1024,128]{1,0:T(8,128)S(1)} %get-tuple-element.49), channel_id=1, source_target_pairs={{0,1},{1,0},{2,3},{3,2},{4,5},{5,4},{6,7},{7,6},{8,9},{9,8},{10,11... | collective-permute-start | bytes 1572872 | tf_op jit(solution)/shard_map/ppermute | solution.py:460
  17.7 12.9 %collective-permute-start.9 = (f32[1040,128]{1,0:T(8,128)S(1)}, f32[1040,128]{1,0:T(8,128)S(1)}, u32[]{:S(2)}, u32[]{:S(2)}) collective-permute-start(f32[1040,128]{1,0:T(8,128)S(1)} %copy-done.2), channel_id=1, source_target_pairs={{0,1},{1,0},{2,3},{3,2},{4,5},{5,4},{6,7},{7,6},{8,9},{9,8},{10,11... | collective-permute-start | bytes 1597448 | tf_op jit(solution)/shard_map/ppermute | solution.py:460
  19.9 12.2 %collective-permute-start.8 = (f32[1040,128]{1,0:T(8,128)S(1)}, f32[1040,128]{1,0:T(8,128)S(1)}, u32[]{:S(2)}, u32[]{:S(2)}) collective-permute-start(f32[1040,128]{1,0:T(8,128)S(1)} %payload.12.refs_2_), channel_id=1, source_target_pairs={{1,3},{2,4},{5,7},{3,1},{4,2},{7,5},{9,11},{10,12},{13,15},{11,9},... | collective-permute-start | bytes 1597448 | tf_op jit(solution)/shard_map/ppermute | solution.py:463
  22.0 15.5 %collective-permute-start.3 = (f32[1040,128]{1,0:T(8,128)S(1)}, f32[1040,128]{1,0:T(8,128)S(1)}, u32[]{:S(2)}, u32[]{:S(2)}) collective-permute-start(f32[1040,128]{1,0:T(8,128)S(1)} %payload.13.refs_2_), channel_id=1, source_target_pairs={{0,2},{3,5},{4,6},{2,0},{5,3},{6,4},{8,10},{11,13},{12,14},{10,8},... | collective-permute-start | bytes 1597448 | tf_op jit(solution)/shard_map/ppermute | solution.py:463
  27.3 10.1 %collective-permute-start.6 = (f32[32,1024]{1,0:T(8,128)S(1)}, f32[32,1024]{1,0:T(8,128)S(1)}, u32[]{:S(2)}, u32[]{:S(2)}) collective-permute-start(f32[32,1024]{1,0:T(8,128)S(1)} %get-tuple-element.52), channel_id=1, source_target_pairs={{0,8},{16,24},{8,0},{24,16},{1,9},{17,25},{9,1},{25,17},{2,10},{18... | collective-permute-start | bytes 393224 | tf_op jit(solution)/shard_map/ppermute | solution.py:374
  28.6 8.8 %collective-permute-start.7 = (f32[32,1024]{1,0:T(8,128)S(1)}, f32[32,1024]{1,0:T(8,128)S(1)}, u32[]{:S(2)}, u32[]{:S(2)}) collective-permute-start(f32[32,1024]{1,0:T(8,128)S(1)} %get-tuple-element.53.refs_3_), channel_id=1, source_target_pairs={{8,16},{16,8},{9,17},{17,9},{10,18},{18,10},{11,19},{19,11},{12,20... | collective-permute-start | bytes 393224 | tf_op jit(solution)/shard_map/ppermute | solution.py:374
  30.7 11.0 %collective-permute-start.12 = (f32[1040,128]{1,0:T(8,128)S(1)}, f32[1040,128]{1,0:T(8,128)S(1)}, u32[]{:S(2)}, u32[]{:S(2)}) collective-permute-start(f32[1040,128]{1,0:T(8,128)S(1)} %pick.6.refs_2_.refs_1_), channel_id=1, source_target_pairs={{0,1},{1,0},{2,3},{3,2},{4,5},{5,4},{6,7},{7,6},{8,9},{9,8},{10,11... | collective-permute-start | bytes 1597448 | tf_op jit(solution)/shard_map/ppermute | solution.py:460
  32.2 14.9 %collective-permute-start.11 = (f32[1040,128]{1,0:T(8,128)S(1)}, f32[1040,128]{1,0:T(8,128)S(1)}, u32[]{:S(2)}, u32[]{:S(2)}) collective-permute-start(f32[1040,128]{1,0:T(8,128)S(1)} %payload.14.refs_2_), channel_id=1, source_target_pairs={{0,2},{3,5},{4,6},{2,0},{5,3},{6,4},{8,10},{11,13},{12,14},{10,8},... | collective-permute-start | bytes 1597448 | tf_op jit(solution)/shard_map/ppermute | solution.py:463
  37.6 11.6 %collective-permute-start.10 = (f32[1040,128]{1,0:T(8,128)S(1)}, f32[1040,128]{1,0:T(8,128)S(1)}, u32[]{:S(2)}, u32[]{:S(2)}) collective-permute-start(f32[1040,128]{1,0:T(8,128)S(1)} %payload.15.refs_3_), channel_id=1, source_target_pairs={{1,3},{2,4},{5,7},{3,1},{4,2},{7,5},{9,11},{10,12},{13,15},{11,9},... | collective-permute-start | bytes 1597448 | tf_op jit(solution)/shard_map/ppermute | solution.py:463
  39.6 1.9 %copy-start.5 = (f32[2,1024]{1,0:T(2,128)S(1)}, f32[2,1024]{1,0:T(2,128)}, u32[]{:S(2)}) copy-start(f32[2,1024]{1,0:T(2,128)} %refs_1_.3) | copy-start | bytes 24580
  39.6 1.9 %copy-start.6 = (f32[1024]{0:T(1024)S(1)}, f32[1024]{0:T(1024)}, u32[]{:S(2)}) copy-start(f32[1024]{0:T(1024)} %param.9) | copy-start | bytes 12292
  40.9 12.3 %collective-permute-start.15 = (f32[1024,128]{1,0:T(8,128)S(1)}, f32[1024,128]{1,0:T(8,128)S(1)}, u32[]{:S(2)}, u32[]{:S(2)}) collective-permute-start(f32[1024,128]{1,0:T(8,128)S(1)} %get-tuple-element.54.refs_4_), channel_id=1, source_target_pairs={{0,1},{1,0},{2,3},{3,2},{4,5},{5,4},{6,7},{7,6},{8,9},{9,8},{10,11... | collective-permute-start | bytes 1572872 | tf_op jit(solution)/shard_map/ppermute | solution.py:460
  41.6 12.2 %collective-permute-start.18 = (f32[1040,128]{1,0:T(8,128)S(1)}, f32[1040,128]{1,0:T(8,128)S(1)}, u32[]{:S(2)}, u32[]{:S(2)}) collective-permute-start(f32[1040,128]{1,0:T(8,128)S(1)} %pick.7.refs_2_.refs_1_), channel_id=1, source_target_pairs={{0,1},{1,0},{2,3},{3,2},{4,5},{5,4},{6,7},{7,6},{8,9},{9,8},{10,11... | collective-permute-start | bytes 1597448 | tf_op jit(solution)/shard_map/ppermute | solution.py:460
  41.7 1.4 %copy-start.1 = (bf16[640,1024]{1,0:T(8,128)(2,1)S(1)}, bf16[640,1024]{1,0:T(8,128)(2,1)}, u32[]{:S(2)}) copy-start(bf16[640,1024]{1,0:T(8,128)(2,1)} %constant.4.clone.refs_2_.refs_4_) | copy-start | bytes 3932164
  41.7 1.4 %copy-start.4 = (s32[256]{0:T(256)S(1)}, s32[256]{0:T(256)}, u32[]{:S(2)}) copy-start(s32[256]{0:T(256)} %param.10) | copy-start | bytes 3076
  47.2 12.7 %collective-permute-start.14 = (f32[1040,128]{1,0:T(8,128)S(1)}, f32[1040,128]{1,0:T(8,128)S(1)}, u32[]{:S(2)}, u32[]{:S(2)}) collective-permute-start(f32[1040,128]{1,0:T(8,128)S(1)} %payload.16.refs_3_), channel_id=1, source_target_pairs={{1,3},{2,4},{5,7},{3,1},{4,2},{7,5},{9,11},{10,12},{13,15},{11,9},... | collective-permute-start | bytes 1597448 | tf_op jit(solution)/shard_map/ppermute | solution.py:463
  49.3 13.9 %collective-permute-start.13 = (f32[1040,128]{1,0:T(8,128)S(1)}, f32[1040,128]{1,0:T(8,128)S(1)}, u32[]{:S(2)}, u32[]{:S(2)}) collective-permute-start(f32[1040,128]{1,0:T(8,128)S(1)} %payload.17.refs_4_), channel_id=1, source_target_pairs={{0,2},{3,5},{4,6},{2,0},{5,3},{6,4},{8,10},{11,13},{12,14},{10,8},... | collective-permute-start | bytes 1597448 | tf_op jit(solution)/shard_map/ppermute | solution.py:463
  53.1 2.0 %collective-permute-start.17 = (f32[520,128]{1,0:T(8,128)S(1)}, f32[520,128]{1,0:T(8,128)S(1)}, u32[]{:S(2)}, u32[]{:S(2)}) collective-permute-start(f32[520,128]{1,0:T(8,128)S(1)} %get-tuple-element.80), channel_id=1, source_target_pairs={{0,1},{1,0},{2,3},{3,2},{4,5},{5,4},{6,7},{7,6},{8,9},{9,8},{10,11... | collective-permute-start | bytes 798728 | tf_op jit(solution)/shard_map/ppermute | solution.py:460
  53.2 2.0 %collective-permute-start.16 = (f32[520,128]{1,0:T(8,128)S(1)}, f32[520,128]{1,0:T(8,128)S(1)}, u32[]{:S(2)}, u32[]{:S(2)}) collective-permute-start(f32[520,128]{1,0:T(8,128)S(1)} %get-tuple-element.81), channel_id=1, source_target_pairs={{0,1},{1,0},{2,3},{3,2},{4,5},{5,4},{6,7},{7,6},{8,9},{9,8},{10,11... | collective-permute-start | bytes 798728 | tf_op jit(solution)/shard_map/ppermute | solution.py:460
  58.0 11.7 %collective-permute-start.20 = (f32[1024,128]{1,0:T(8,128)S(1)}, f32[1024,128]{1,0:T(8,128)S(1)}, u32[]{:S(2)}, u32[]{:S(2)}) collective-permute-start(f32[1024,128]{1,0:T(8,128)S(1)} %get-tuple-element.60.refs_2_), channel_id=1, source_target_pairs={{0,1},{1,0},{2,3},{3,2},{4,5},{5,4},{6,7},{7,6},{8,9},{9,8},{10,11... | collective-permute-start | bytes 1572872 | tf_op jit(solution)/shard_map/ppermute | solution.py:460
  59.4 10.3 %collective-permute-start.21 = (f32[1024,128]{1,0:T(8,128)S(1)}, f32[1024,128]{1,0:T(8,128)S(1)}, u32[]{:S(2)}, u32[]{:S(2)}) collective-permute-start(f32[1024,128]{1,0:T(8,128)S(1)} %get-tuple-element.61.refs_3_), channel_id=1, source_target_pairs={{0,1},{1,0},{2,3},{3,2},{4,5},{5,4},{6,7},{7,6},{8,9},{9,8},{10,11... | collective-permute-start | bytes 1572872 | tf_op jit(solution)/shard_map/ppermute | solution.py:460
  63.4 12.7 %collective-permute-start.24 = (f32[1024,128]{1,0:T(8,128)S(1)}, f32[1024,128]{1,0:T(8,128)S(1)}, u32[]{:S(2)}, u32[]{:S(2)}) collective-permute-start(f32[1024,128]{1,0:T(8,128)S(1)} %get-tuple-element.62.refs_2_.refs_1_), channel_id=1, source_target_pairs={{0,2},{3,5},{4,6},{2,0},{5,3},{6,4},{8,10},{11,13},{12,14},{10,8},... | collective-permute-start | bytes 1572872 | tf_op jit(solution)/shard_map/ppermute | solution.py:463
  66.8 13.0 %collective-permute-start.19 = (f32[1024,128]{1,0:T(8,128)S(1)}, f32[1024,128]{1,0:T(8,128)S(1)}, u32[]{:S(2)}, u32[]{:S(2)}) collective-permute-start(f32[1024,128]{1,0:T(8,128)S(1)} %get-tuple-element.62.refs_2_.refs_1_), channel_id=1, source_target_pairs={{1,3},{2,4},{5,7},{3,1},{4,2},{7,5},{9,11},{10,12},{13,15},{11,9},... | collective-permute-start | bytes 1572872 | tf_op jit(solution)/shard_map/ppermute | solution.py:463
  68.7 14.5 %collective-permute-start.27 = (f32[1024,128]{1,0:T(8,128)S(1)}, f32[1024,128]{1,0:T(8,128)S(1)}, u32[]{:S(2)}, u32[]{:S(2)}) collective-permute-start(f32[1024,128]{1,0:T(8,128)S(1)} %get-tuple-element.62.refs_2_.refs_1_), channel_id=1, source_target_pairs={{0,1},{1,0},{2,3},{3,2},{4,5},{5,4},{6,7},{7,6},{8,9},{9,8},{10,11... | collective-permute-start | bytes 1572872 | tf_op jit(solution)/shard_map/ppermute | solution.py:460
  69.9 8.2 %collective-permute-start.22 = (f32[32,1024]{1,0:T(8,128)S(1)}, f32[32,1024]{1,0:T(8,128)S(1)}, u32[]{:S(2)}, u32[]{:S(2)}) collective-permute-start(f32[32,1024]{1,0:T(8,128)S(1)} %get-tuple-element.67), channel_id=1, source_target_pairs={{0,8},{16,24},{8,0},{24,16},{1,9},{17,25},{9,1},{25,17},{2,10},{18... | collective-permute-start | bytes 393224 | tf_op jit(solution)/shard_map/ppermute | solution.py:374
  71.2 7.6 %collective-permute-start.23 = (f32[32,1024]{1,0:T(8,128)S(1)}, f32[32,1024]{1,0:T(8,128)S(1)}, u32[]{:S(2)}, u32[]{:S(2)}) collective-permute-start(f32[32,1024]{1,0:T(8,128)S(1)} %get-tuple-element.68.refs_2_), channel_id=1, source_target_pairs={{8,16},{16,8},{9,17},{17,9},{10,18},{18,10},{11,19},{19,11},{12,20... | collective-permute-start | bytes 393224 | tf_op jit(solution)/shard_map/ppermute | solution.py:374
  76.2 14.9 %collective-permute-start.26 = (f32[1024,128]{1,0:T(8,128)S(1)}, f32[1024,128]{1,0:T(8,128)S(1)}, u32[]{:S(2)}, u32[]{:S(2)}) collective-permute-start(f32[1024,128]{1,0:T(8,128)S(1)} %payload.18.refs_2_), channel_id=1, source_target_pairs={{1,3},{2,4},{5,7},{3,1},{4,2},{7,5},{9,11},{10,12},{13,15},{11,9},... | collective-permute-start | bytes 1572872 | tf_op jit(solution)/shard_map/ppermute | solution.py:463
  79.9 15.2 %collective-permute-start.25 = (f32[1024,128]{1,0:T(8,128)S(1)}, f32[1024,128]{1,0:T(8,128)S(1)}, u32[]{:S(2)}, u32[]{:S(2)}) collective-permute-start(f32[1024,128]{1,0:T(8,128)S(1)} %payload.19.refs_1_), channel_id=1, source_target_pairs={{0,2},{3,5},{4,6},{2,0},{5,3},{6,4},{8,10},{11,13},{12,14},{10,8},... | collective-permute-start | bytes 1572872 | tf_op jit(solution)/shard_map/ppermute | solution.py:463
  84.6 12.5 %collective-permute-start.29 = (f32[1024,128]{1,0:T(8,128)S(1)}, f32[1024,128]{1,0:T(8,128)S(1)}, u32[]{:S(2)}, u32[]{:S(2)}) collective-permute-start(f32[1024,128]{1,0:T(8,128)S(1)} %get-tuple-element.69.refs_2_), channel_id=1, source_target_pairs={{0,1},{1,0},{2,3},{3,2},{4,5},{5,4},{6,7},{7,6},{8,9},{9,8},{10,11... | collective-permute-start | bytes 1572872 | tf_op jit(solution)/shard_map/ppermute | solution.py:460
  87.9 9.2 %collective-permute-start.34 = (f32[1024,128]{1,0:T(8,128)S(1)}, f32[1024,128]{1,0:T(8,128)S(1)}, u32[]{:S(2)}, u32[]{:S(2)}) collective-permute-start(f32[1024,128]{1,0:T(8,128)S(1)} %get-tuple-element.70.refs_8_), channel_id=1, source_target_pairs={{0,1},{1,0},{2,3},{3,2},{4,5},{5,4},{6,7},{7,6},{8,9},{9,8},{10,11... | collective-permute-start | bytes 1572872 | tf_op jit(solution)/shard_map/ppermute | solution.py:460
  88.0 14.2 %collective-permute-start.37 = (f32[1024,128]{1,0:T(8,128)S(1)}, f32[1024,128]{1,0:T(8,128)S(1)}, u32[]{:S(2)}, u32[]{:S(2)}) collective-permute-start(f32[1024,128]{1,0:T(8,128)S(1)} %pick.9.refs_2_.refs_1_), channel_id=1, source_target_pairs={{0,1},{1,0},{2,3},{3,2},{4,5},{5,4},{6,7},{7,6},{8,9},{9,8},{10,11... | collective-permute-start | bytes 1572872 | tf_op jit(solution)/shard_map/ppermute | solution.py:460
  91.2 15.0 %collective-permute-start.33 = (f32[1024,128]{1,0:T(8,128)S(1)}, f32[1024,128]{1,0:T(8,128)S(1)}, u32[]{:S(2)}, u32[]{:S(2)}) collective-permute-start(f32[1024,128]{1,0:T(8,128)S(1)} %payload.20.refs_3_), channel_id=1, source_target_pairs={{0,2},{3,5},{4,6},{2,0},{5,3},{6,4},{8,10},{11,13},{12,14},{10,8},... | collective-permute-start | bytes 1572872 | tf_op jit(solution)/shard_map/ppermute | solution.py:463
  95.1 16.5 %collective-permute-start.28 = (f32[1024,128]{1,0:T(8,128)S(1)}, f32[1024,128]{1,0:T(8,128)S(1)}, u32[]{:S(2)}, u32[]{:S(2)}) collective-permute-start(f32[1024,128]{1,0:T(8,128)S(1)} %payload.21.refs_2_), channel_id=1, source_target_pairs={{1,3},{2,4},{5,7},{3,1},{4,2},{7,5},{9,11},{10,12},{13,15},{11,9},... | collective-permute-start | bytes 1572872 | tf_op jit(solution)/shard_map/ppermute | solution.py:463
  97.3 5.9 %collective-permute-start.36 = (f32[512,128]{1,0:T(8,128)S(1)}, f32[512,128]{1,0:T(8,128)S(1)}, u32[]{:S(2)}, u32[]{:S(2)}) collective-permute-start(f32[512,128]{1,0:T(8,128)S(1)} %get-tuple-element.84), channel_id=1, source_target_pairs={{0,1},{1,0},{2,3},{3,2},{4,5},{5,4},{6,7},{7,6},{8,9},{9,8},{10,11... | collective-permute-start | bytes 786440 | tf_op jit(solution)/shard_map/ppermute | solution.py:460
  102.1 1.5 %collective-permute-start.35 = (f32[512,128]{1,0:T(8,128)S(1)}, f32[512,128]{1,0:T(8,128)S(1)}, u32[]{:S(2)}, u32[]{:S(2)}) collective-permute-start(f32[512,128]{1,0:T(8,128)S(1)} %get-tuple-element.85), channel_id=1, source_target_pairs={{0,1},{1,0},{2,3},{3,2},{4,5},{5,4},{6,7},{7,6},{8,9},{9,8},{10,11... | collective-permute-start | bytes 786440 | tf_op jit(solution)/shard_map/ppermute | solution.py:460
  102.2 6.3 %collective-permute-start.32 = (f32[2,256]{1,0:T(2,128)S(1)}, f32[2,256]{1,0:T(2,128)S(1)}, u32[]{:S(2)}, u32[]{:S(2)}) collective-permute-start(f32[2,256]{1,0:T(2,128)S(1)} %get-tuple-element.71.refs_3_.refs_0_), channel_id=1, source_target_pairs={{0,6},{1,7},{2,4},{3,5},{4,2},{5,3},{6,0},{7,1},{8,14},{9,15},{10,... | collective-permute-start | bytes 6152 | tf_op jit(solution)/shard_map/ppermute | solution.py:662
  103.3 8.4 %collective-permute-start.31 = (f32[2,256]{1,0:T(2,128)S(1)}, f32[2,256]{1,0:T(2,128)S(1)}, u32[]{:S(2)}, u32[]{:S(2)}) collective-permute-start(f32[2,256]{1,0:T(2,128)S(1)} %get-tuple-element.71.refs_3_.refs_0_), channel_id=1, source_target_pairs={{0,4},{1,5},{2,6},{3,7},{4,0},{5,1},{6,2},{7,3},{8,12},{9,13},{10,... | collective-permute-start | bytes 6152 | tf_op jit(solution)/shard_map/ppermute | solution.py:662
  103.7 8.0 %collective-permute-start.30 = (f32[2,256]{1,0:T(2,128)S(1)}, f32[2,256]{1,0:T(2,128)S(1)}, u32[]{:S(2)}, u32[]{:S(2)}) collective-permute-start(f32[2,256]{1,0:T(2,128)S(1)} %get-tuple-element.71.refs_3_.refs_0_), channel_id=1, source_target_pairs={{0,2},{1,3},{2,0},{3,1},{4,6},{5,7},{6,4},{7,5},{8,10},{9,11},{10,... | collective-permute-start | bytes 6152 | tf_op jit(solution)/shard_map/ppermute | solution.py:662
  106.3 17.8 %collective-permute-start.39 = (f32[1024,128]{1,0:T(8,128)S(1)}, f32[1024,128]{1,0:T(8,128)S(1)}, u32[]{:S(2)}, u32[]{:S(2)}) collective-permute-start(f32[1024,128]{1,0:T(8,128)S(1)} %payload.22.refs_4_), channel_id=1, source_target_pairs={{1,3},{2,4},{5,7},{3,1},{4,2},{7,5},{9,11},{10,12},{13,15},{11,9},... | collective-permute-start | bytes 1572872 | tf_op jit(solution)/shard_map/ppermute | solution.py:463
  111.8 14.6 %collective-permute-start.38 = (f32[1024,128]{1,0:T(8,128)S(1)}, f32[1024,128]{1,0:T(8,128)S(1)}, u32[]{:S(2)}, u32[]{:S(2)}) collective-permute-start(f32[1024,128]{1,0:T(8,128)S(1)} %payload.23.refs_4_), channel_id=1, source_target_pairs={{0,2},{3,5},{4,6},{2,0},{5,3},{6,4},{8,10},{11,13},{12,14},{10,8},... | collective-permute-start | bytes 1572872 | tf_op jit(solution)/shard_map/ppermute | solution.py:463
  114.6 8.0 %collective-permute-start.41 = (f32[512,128]{1,0:T(8,128)S(1)}, f32[512,128]{1,0:T(8,128)S(1)}, u32[]{:S(2)}, u32[]{:S(2)}) collective-permute-start(f32[512,128]{1,0:T(8,128)S(1)} %get-tuple-element.82), channel_id=1, source_target_pairs={{0,1},{1,0},{2,3},{3,2},{4,5},{5,4},{6,7},{7,6},{8,9},{9,8},{10,11... | collective-permute-start | bytes 786440 | tf_op jit(solution)/shard_map/ppermute | solution.py:460
  118.9 3.7 %collective-permute-start.40 = (f32[512,128]{1,0:T(8,128)S(1)}, f32[512,128]{1,0:T(8,128)S(1)}, u32[]{:S(2)}, u32[]{:S(2)}) collective-permute-start(f32[512,128]{1,0:T(8,128)S(1)} %get-tuple-element.83), channel_id=1, source_target_pairs={{0,1},{1,0},{2,3},{3,2},{4,5},{5,4},{6,7},{7,6},{8,9},{9,8},{10,11... | collective-permute-start | bytes 786440 | tf_op jit(solution)/shard_map/ppermute | solution.py:460
  119.0 3.1 %collective-permute-start.42 = (f32[2,256]{1,0:T(2,128)S(1)}, f32[2,256]{1,0:T(2,128)S(1)}, u32[]{:S(2)}, u32[]{:S(2)}) collective-permute-start(f32[2,256]{1,0:T(2,128)S(1)} %get-tuple-element.77.refs_0_), channel_id=1, source_target_pairs={{0,1},{1,0},{2,3},{3,2},{4,5},{5,4},{6,7},{7,6},{8,9},{9,8},{10,11... | collective-permute-start | bytes 6152 | tf_op jit(solution)/shard_map/ppermute | solution.py:662

commit v15 on v14

--- a/solution.py
+++ b/solution.py
@@ -565,7 +565,9 @@
         room=28,
     )
     one.matrix = matrix
-    one.terms = [(terms[2 * s], *exchange(terms[2 * s + 1])) for s in range(chips - 1)]
+    one.terms = [
+        (terms[2 * s], *exchange(terms[2 * s + 1], 1 if s == 0 else 1)) for s in range(chips - 1)
+    ]
     one.take_own()
     operators = jnp.asarray(differences(cells))
     strips = None
@@ -576,10 +578,9 @@
         (strips,) = call(strip_columns, [shape], strips)
 
     for step in range(1, chips):
+        one.send(step, unpack if step == 2 else None)
         if step == 1:
             one.take(1)
-        one.send(step, unpack if step == 2 else None)
-        if step == 1:
             one.join_terms(*(s for s in range(chips - 1) if isinstance(one.terms[s], tuple)))
             strips = call(strip_rows, [(HALO, modes)] * 2, [distribution])
             strips = paired(*call(strip_pairs, [(HALO, modes)] * 2, strips))

time: 130 us -> 132 us (1.015)
  the two profiles are of different devices: /device:TPU:13 before, /device:TPU:0 now
where the time goes in v15:
time: 132 us; the launch traced here: 131 us
  starting transfers between devices  69.3 us (52%)
  Pallas kernels  34.9 us (26%)
  waiting for transfers between devices  24.5 us (19%)
  between operations  1.7 us (1%)
    ppermute x16, starting transfers between devices, along(): return lax.ppermute(value, 'mode', plan.pairs[stream])  53.7 us
    pallas_call x56, Pallas kernels, __call__(): pl.pallas_call(body, out_shape=[jax.ShapeDtypeStruct(shape, jnp.float32)...  34.9 us
    ppermute x16, waiting for transfers between devices, along(): return lax.ppermute(value, 'mode', plan.pairs[stream])  22.1 us
    ppermute x19, starting transfers between devices, exchange(): lax.ppermute(value[i:j], 'mode', across)  6.73 us
    ppermute x4, starting transfers between devices, over(): lax.ppermute(self.value, 'mode', [(i, i ^ bit) for i in range(self.device...  4.47 us
    ppermute x4, starting transfers between devices, paired(): lax.ppermute(value, 'space', pairs + [(j, i) for i, j in pairs])  4.43 us
  transfers between devices with their start and end apart: 43, of which 6 were waited for; matrix products, arithmetic and copies ran while one was open for 0% of the time, Pallas kernels for 24%

profile of v15, /device:TPU:0, one launch (start us, length us, event | category | flops | bytes accessed | tf_op | source)
XLA Modules:
  0.0 131.4 jit_solution(10658717985396863720)
XLA Ops:
  0.6 2.0 %own_rows.1 = (f32[1040,128]{1,0:T(8,128)}, f32[8,128]{1,0:T(8,128)}) custom-call(f32[1024,256]{1,0:T(8,128)} %refs_0_.9, f32[2,1024]{1,0:T(2,128)} %refs_1_.3, f32[1,1024]{1,0:T(1,128)} %bitcast.4), custom_call_target="tpu_custom_call" | custom-call | flops 1024 | bytes 1024 | tf_op jit(solution)/shard_map/own_rows/pallas_call | solution.py:39
  2.6 4.9 %collective-permute-start.2 = (f32[1040,128]{1,0:T(8,128)}, f32[1040,128]{1,0:T(8,128)S(1)}, u32[]{:S(2)}, u32[]{:S(2)}) collective-permute-start(f32[1040,128]{1,0:T(8,128)} %get-tuple-element.41.refs_1_), channel_id=1, source_target_pairs={{0,2},{3,5},{4,6},{2,0},{5,3},{6,4},{8,10},{11,13},{12,14},{10,8},... | collective-permute-start | bytes 1597448 | tf_op jit(solution)/shard_map/ppermute | solution.py:463
  7.6 0.7 collective-permute-start
  8.3 0.7 copy-done.3
  9.0 6.2 %load_and_products.1 = (f32[1024,128]{1,0:T(8,128)S(1)}, f32[1024,128]{1,0:T(8,128)S(1)}, f32[1024,128]{1,0:T(8,128)S(1)}, f32[1024,128]{1,0:T(8,128)S(1)}, f32[...) custom-call(bf16[8192,1024]{1,0:T(8,128)(2,1)} %refs_0_.6, f32[1024,256]{1,0:T(8,128)S(1)} %copy-done, ...), custom_call_target="tpu_custom_call" | custom-call | flops 1024 | bytes 1024 | tf_op jit(solution)/shard_map/load_and_products/pallas_call | solution.py:39
  15.1 2.1 %collective-permute-start.1 = (f32[1024,128]{1,0:T(8,128)S(1)}, f32[1024,128]{1,0:T(8,128)S(1)}, u32[]{:S(2)}, u32[]{:S(2)}) collective-permute-start(f32[1024,128]{1,0:T(8,128)S(1)} %get-tuple-element.44), channel_id=1, source_target_pairs={{0,1},{1,0},{2,3},{3,2},{4,5},{5,4},{6,7},{7,6},{8,9},{9,8},{10,11... | collective-permute-start | bytes 1572872 | tf_op jit(solution)/shard_map/ppermute | solution.py:460
  17.3 0.4 collective-permute-start.5
  17.8 1.0 collective-permute-done.1.refs_1_
  18.8 0.4 collective-permute-start.9
  19.3 0.7 collective-permute-start.8
  20.1 7.2 %collective-permute-start.3 = (f32[1040,128]{1,0:T(8,128)S(1)}, f32[1040,128]{1,0:T(8,128)S(1)}, u32[]{:S(2)}, u32[]{:S(2)}) collective-permute-start(f32[1040,128]{1,0:T(8,128)S(1)} %payload.13.refs_2_), channel_id=1, source_target_pairs={{0,2},{3,5},{4,6},{2,0},{5,3},{6,4},{8,10},{11,13},{12,14},{10,8},... | collective-permute-start | bytes 1597448 | tf_op jit(solution)/shard_map/ppermute | solution.py:463
  27.5 0.3 strip_rows.1
  27.9 1.6 %collective-permute-start.6 = (f32[32,1024]{1,0:T(8,128)S(1)}, f32[32,1024]{1,0:T(8,128)S(1)}, u32[]{:S(2)}, u32[]{:S(2)}) collective-permute-start(f32[32,1024]{1,0:T(8,128)S(1)} %get-tuple-element.52), channel_id=1, source_target_pairs={{0,8},{16,24},{8,0},{24,16},{1,9},{17,25},{9,1},{25,17},{2,10},{18... | collective-permute-start | bytes 393224 | tf_op jit(solution)/shard_map/ppermute | solution.py:374
  29.5 0.7 collective-permute-start.7
  30.2 1.4 %two_blocks.8.refs_3_ = f32[272,1024]{1,0:T(8,128)S(1)} custom-call(bf16[8192,1024]{1,0:T(8,128)(2,1)S(1)} %get-tuple-element.45.refs_2_.refs_0_, f32[1040,128]{1,0:T(8,128)S(1)} %copy-done.2, f32[1040,128]{1,0:T(8,128)S(1)} %collective-permute-done.9.refs_2_, f32[32,1024]{1,0:T(8,128)S(1)} %get-tuple-element.53.refs_3_), custom_call_target="tpu_custom_call" | custom-call | flops 1024 | bytes 1024 | tf_op jit(solution)/shard_map/two_blocks/pallas_call | solution.py:39
  31.7 8.0 %collective-permute-start.11 = (f32[1040,128]{1,0:T(8,128)S(1)}, f32[1040,128]{1,0:T(8,128)S(1)}, u32[]{:S(2)}, u32[]{:S(2)}) collective-permute-start(f32[1040,128]{1,0:T(8,128)S(1)} %payload.14.refs_2_), channel_id=1, source_target_pairs={{0,2},{3,5},{4,6},{2,0},{5,3},{6,4},{8,10},{11,13},{12,14},{10,8},... | collective-permute-start | bytes 1597448 | tf_op jit(solution)/shard_map/ppermute | solution.py:463
  39.7 0.2 strip_columns.2.refs_3_.refs_1_
  40.0 0.7 collective-permute-start.10
  40.8 1.3 slot_products.5
  42.2 0.5 collective-permute-start.18
  42.8 1.4 %two_blocks.9.refs_5_.refs_3_ = f32[272,1024]{1,0:T(8,128)S(1)} custom-call(bf16[8192,1024]{1,0:T(8,128)(2,1)S(1)} %get-tuple-element.45.refs_2_.refs_0_, f32[1040,128]{1,0:T(8,128)S(1)} %pick.6.refs_2_.refs_1_, f32[1040,128]{1,0:T(8,128)S(1)} %collective-permute-done.12.refs_2_, f32[272,1024]{1,0:T(8,128)S(1)} %two_blocks.8.refs_3_, ...), custom_call_target="tpu_custom_call" | custom-call | flops 1024 | bytes 1024 | tf_op jit(solution)/shard_map/two_blocks/pallas_call | solution.py:39
  44.2 2.0 %first_rest.1 = (f32[1024,128]{1,0:T(8,128)S(1)}, f32[1024,128]{1,0:T(8,128)S(1)}) custom-call(f32[1024,256]{1,0:T(8,128)S(1)} %copy-done, bf16[1024,128]{1,0:T(8,128)(2,1)S(1)} %strip_columns.2.refs_3_.refs_1_, bf16[640,1024]{1,0:T(8,128)(2,1)S(1)} %copy-done.1, f32[8,1024]{1,0:T(8,128)S(1)} %maximum_maximum_fusion.refs_3_.refs_5_, s32[1,256]{1,0:T(1,128)S(1)} %bitcast.2, ...), custom_call_target="tpu_custom_call" | custom-call | flops 1024 | bytes 1024 | tf_op jit(solution)/shard_map/first_rest/pallas_call | solution.py:39
  46.2 6.4 %collective-permute-done.11.refs_0_.refs_1_ = f32[1040,128]{1,0:T(8,128)S(1)} collective-permute-done((f32[1040,128]{1,0:T(8,128)S(1)}, f32[1040,128]{1,0:T(8,128)S(1)}, u32[]{:S(2)}, u32[]{:S(2)}) %collective-permute-start.11) | collective-permute-done | bytes 532512 | tf_op jit(solution)/shard_map/ppermute | solution.py:463
  52.7 0.7 collective-permute-start.14
  53.5 7.6 %collective-permute-start.13 = (f32[1040,128]{1,0:T(8,128)S(1)}, f32[1040,128]{1,0:T(8,128)S(1)}, u32[]{:S(2)}, u32[]{:S(2)}) collective-permute-start(f32[1040,128]{1,0:T(8,128)S(1)} %payload.17.refs_4_), channel_id=1, source_target_pairs={{0,2},{3,5},{4,6},{2,0},{5,3},{6,4},{8,10},{11,13},{12,14},{10,8},... | collective-permute-start | bytes 1597448 | tf_op jit(solution)/shard_map/ppermute | solution.py:463
  61.1 0.2 pick.8.refs_2_.refs_1_
  61.5 0.5 collective-permute-start.16
  62.1 1.4 %two_blocks.10.refs_4_.refs_6_ = f32[272,1024]{1,0:T(8,128)S(1)} custom-call(bf16[8192,1024]{1,0:T(8,128)(2,1)S(1)} %get-tuple-element.45.refs_2_.refs_0_, f32[1040,128]{1,0:T(8,128)S(1)} %pick.7.refs_2_.refs_1_, f32[1040,128]{1,0:T(8,128)S(1)} %collective-permute-done.18.refs_2_, f32[272,1024]{1,0:T(8,128)S(1)} %two_blocks.9.refs_5_.refs_3_, ...), custom_call_target="tpu_custom_call" | custom-call | flops 1024 | bytes 1024 | tf_op jit(solution)/shard_map/two_blocks/pallas_call | solution.py:39
  63.5 1.5 %two_blocks.11 = (f32[1024,128]{1,0:T(8,128)S(1)}, f32[32,1024]{1,0:T(8,128)S(1)}, f32[8,1024]{1,0:T(8,128)S(1)}) custom-call(bf16[8192,1024]{1,0:T(8,128)(2,1)S(1)} %get-tuple-element.45.refs_2_.refs_0_, f32[1040,128]{1,0:T(8,128)S(1)} %pick.8.refs_2_.refs_1_, f32[520,128]{1,0:T(8,128)S(1)} %collective-permute-done.16.refs_2_, ...), custom_call_target="tpu_custom_call" | custom-call | flops 1024 | bytes 1024 | tf_op jit(solution)/shard_map/two_blocks/pallas_call | solution.py:39
  65.0 1.3 slot_products.6
  66.3 0.1 collective-permute-start.20
  66.4 1.3 slot_products.7
  67.7 0.5 collective-permute-start.21
  68.4 0.2 turn_sum.1
  68.6 3.9 %collective-permute-start.24 = (f32[1024,128]{1,0:T(8,128)S(1)}, f32[1024,128]{1,0:T(8,128)S(1)}, u32[]{:S(2)}, u32[]{:S(2)}) collective-permute-start(f32[1024,128]{1,0:T(8,128)S(1)} %get-tuple-element.62.refs_2_.refs_1_), channel_id=1, source_target_pairs={{0,2},{3,5},{4,6},{2,0},{5,3},{6,4},{8,10},{11,13},{12,14},{10,8},... | collective-permute-start | bytes 1572872 | tf_op jit(solution)/shard_map/ppermute | solution.py:463
  72.5 0.7 collective-permute-start.19
  73.5 1.6 %collective-permute-start.22 = (f32[32,1024]{1,0:T(8,128)S(1)}, f32[32,1024]{1,0:T(8,128)S(1)}, u32[]{:S(2)}, u32[]{:S(2)}) collective-permute-start(f32[32,1024]{1,0:T(8,128)S(1)} %get-tuple-element.67), channel_id=1, source_target_pairs={{0,8},{16,24},{8,0},{24,16},{1,9},{17,25},{9,1},{25,17},{2,10},{18... | collective-permute-start | bytes 393224 | tf_op jit(solution)/shard_map/ppermute | solution.py:374
  75.1 0.7 collective-permute-start.23
  75.7 9.6 %collective-permute-done.24.refs_0_ = f32[1024,128]{1,0:T(8,128)S(1)} collective-permute-done((f32[1024,128]{1,0:T(8,128)S(1)}, f32[1024,128]{1,0:T(8,128)S(1)}, u32[]{:S(2)}, u32[]{:S(2)}) %collective-permute-start.24) | collective-permute-done | bytes 524320 | tf_op jit(solution)/shard_map/ppermute | solution.py:463
  85.3 0.7 collective-permute-start.26
  86.0 0.2 strip_columns.3.refs_2_.refs_3_
  86.3 6.3 %collective-permute-start.25 = (f32[1024,128]{1,0:T(8,128)S(1)}, f32[1024,128]{1,0:T(8,128)S(1)}, u32[]{:S(2)}, u32[]{:S(2)}) collective-permute-start(f32[1024,128]{1,0:T(8,128)S(1)} %payload.19.refs_1_), channel_id=1, source_target_pairs={{0,2},{3,5},{4,6},{2,0},{5,3},{6,4},{8,10},{11,13},{12,14},{10,8},... | collective-permute-start | bytes 1572872 | tf_op jit(solution)/shard_map/ppermute | solution.py:463
  92.8 1.3 slot_products.8
  94.1 1.3 slot_products.9
  95.4 0.6 collective-permute-start.34
  96.0 2.6 %second_rest.1 = (f32[1024,128]{1,0:T(8,128)S(1)}, f32[1024,128]{1,0:T(8,128)S(1)}, f32[2,256]{1,0:T(2,128)S(1)}) custom-call(f32[1024,256]{1,0:T(8,128)S(1)} %copy-done, f32[1024,128]{1,0:T(8,128)S(1)} %get-tuple-element.58.refs_1_, f32[1024,128]{1,0:T(8,128)S(1)} %get-tuple-element.62.refs_2_.refs_1_, bf16[1024,128]{1,0:T(8,128)(2,1)S(1)} %strip_columns.3.refs_2_.refs_3_, ...), custom_call_target="tpu_custom_call" | custom-call | flops 1024 | bytes 1024 | tf_op jit(solution)/shard_map/second_rest/pallas_call | solution.py:39
  98.7 5.1 %collective-permute-start.33 = (f32[1024,128]{1,0:T(8,128)S(1)}, f32[1024,128]{1,0:T(8,128)S(1)}, u32[]{:S(2)}, u32[]{:S(2)}) collective-permute-start(f32[1024,128]{1,0:T(8,128)S(1)} %payload.20.refs_3_), channel_id=1, source_target_pairs={{0,2},{3,5},{4,6},{2,0},{5,3},{6,4},{8,10},{11,13},{12,14},{10,8},... | collective-permute-start | bytes 1572872 | tf_op jit(solution)/shard_map/ppermute | solution.py:463
  103.9 0.7 collective-permute-start.28
  105.0 0.5 collective-permute-start.35
  105.5 2.5 %collective-permute-start.32 = (f32[2,256]{1,0:T(2,128)S(1)}, f32[2,256]{1,0:T(2,128)S(1)}, u32[]{:S(2)}, u32[]{:S(2)}) collective-permute-start(f32[2,256]{1,0:T(2,128)S(1)} %get-tuple-element.71.refs_3_.refs_0_), channel_id=1, source_target_pairs={{0,6},{1,7},{2,4},{3,5},{4,2},{5,3},{6,0},{7,1},{8,14},{9,15},{10,... | collective-permute-start | bytes 6152 | tf_op jit(solution)/shard_map/ppermute | solution.py:663
  108.0 1.8 %collective-permute-start.31 = (f32[2,256]{1,0:T(2,128)S(1)}, f32[2,256]{1,0:T(2,128)S(1)}, u32[]{:S(2)}, u32[]{:S(2)}) collective-permute-start(f32[2,256]{1,0:T(2,128)S(1)} %get-tuple-element.71.refs_3_.refs_0_), channel_id=1, source_target_pairs={{0,4},{1,5},{2,6},{3,7},{4,0},{5,1},{6,2},{7,3},{8,12},{9,13},{10,... | collective-permute-start | bytes 6152 | tf_op jit(solution)/shard_map/ppermute | solution.py:663
  109.9 1.3 two_blocks.12.refs_3_
  111.2 4.7 %collective-permute-done.33.refs_0_.refs_1_ = f32[1024,128]{1,0:T(8,128)S(1)} collective-permute-done((f32[1024,128]{1,0:T(8,128)S(1)}, f32[1024,128]{1,0:T(8,128)S(1)}, u32[]{:S(2)}, u32[]{:S(2)}) %collective-permute-start.33) | collective-permute-done | bytes 524320 | tf_op jit(solution)/shard_map/ppermute | solution.py:463
  115.9 0.7 collective-permute-start.39
  116.6 1.3 collective-permute-done.32.refs_3_
  118.0 5.0 %collective-permute-start.38 = (f32[1024,128]{1,0:T(8,128)S(1)}, f32[1024,128]{1,0:T(8,128)S(1)}, u32[]{:S(2)}, u32[]{:S(2)}) collective-permute-start(f32[1024,128]{1,0:T(8,128)S(1)} %payload.23.refs_4_), channel_id=1, source_target_pairs={{0,2},{3,5},{4,6},{2,0},{5,3},{6,4},{8,10},{11,13},{12,14},{10,8},... | collective-permute-start | bytes 1572872 | tf_op jit(solution)/shard_map/ppermute | solution.py:463
  123.1 0.3 pick.11.refs_4_.refs_1_
  123.5 0.5 collective-permute-start.40
  124.0 1.3 two_blocks.13.refs_3_.refs_4_
  125.4 1.3 two_blocks.14.refs_2_.refs_4_
  126.7 0.6 add_all.3
  127.3 1.4 %two_blocks.15.refs_3_.refs_2_ = f32[1024,128]{1,0:T(8,128)S(1)} custom-call(bf16[8192,1024]{1,0:T(8,128)(2,1)S(1)} %get-tuple-element.45.refs_2_.refs_0_, f32[1024,128]{1,0:T(8,128)S(1)} %pick.11.refs_4_.refs_1_, f32[512,128]{1,0:T(8,128)S(1)} %collective-permute-done.40.refs_2_, f32[512,128]{1,0:T(8,128)S(1)} %collective-permute-done.41.refs_3_, ...), custom_call_target="tpu_custom_call" | custom-call | flops 1024 | bytes 1024 | tf_op jit(solution)/shard_map/two_blocks/pallas_call | solution.py:39
  128.8 1.4 %collective-permute-done.38.refs_0_ = f32[1024,128]{1,0:T(8,128)S(1)} collective-permute-done((f32[1024,128]{1,0:T(8,128)S(1)}, f32[1024,128]{1,0:T(8,128)S(1)}, u32[]{:S(2)}, u32[]{:S(2)}) %collective-permute-start.38) | collective-permute-done | bytes 524320 | tf_op jit(solution)/shard_map/ppermute | solution.py:463
  130.2 1.0 last_sum.1
  (99 shorter events, 3.1 us)
Async XLA Ops:
  0.6 7.6 %copy-start = (f32[1024,256]{1,0:T(8,128)S(1)}, f32[1024,256]{1,0:T(8,128)}, u32[]{:S(2)}) copy-start(f32[1024,256]{1,0:T(8,128)} %refs_0_.9) | copy-start | bytes 3145732
  2.6 16.6 %collective-permute-start.2 = (f32[1040,128]{1,0:T(8,128)}, f32[1040,128]{1,0:T(8,128)S(1)}, u32[]{:S(2)}, u32[]{:S(2)}) collective-permute-start(f32[1040,128]{1,0:T(8,128)} %get-tuple-element.41.refs_1_), channel_id=1, source_target_pairs={{0,2},{3,5},{4,6},{2,0},{5,3},{6,4},{8,10},{11,13},{12,14},{10,8},... | collective-permute-start | bytes 1597448 | tf_op jit(solution)/shard_map/ppermute | solution.py:463
  7.6 12.4 %collective-permute-start = (f32[1040,128]{1,0:T(8,128)}, f32[1040,128]{1,0:T(8,128)S(1)}, u32[]{:S(2)}, u32[]{:S(2)}) collective-permute-start(f32[1040,128]{1,0:T(8,128)} %get-tuple-element.41.refs_1_), channel_id=1, source_target_pairs={{1,3},{2,4},{5,7},{3,1},{4,2},{7,5},{9,11},{10,12},{13,15},{11,9},... | collective-permute-start | bytes 1597448 | tf_op jit(solution)/shard_map/ppermute | solution.py:463
  8.3 0.7 copy-start.3
  9.0 9.8 %copy-start.2 = (f32[1040,128]{1,0:T(8,128)S(1)}, f32[1040,128]{1,0:T(8,128)}, u32[]{:S(2)}) copy-start(f32[1040,128]{1,0:T(8,128)} %get-tuple-element.41.refs_1_) | copy-start | bytes 1597444
  15.1 3.7 %collective-permute-start.1 = (f32[1024,128]{1,0:T(8,128)S(1)}, f32[1024,128]{1,0:T(8,128)S(1)}, u32[]{:S(2)}, u32[]{:S(2)}) collective-permute-start(f32[1024,128]{1,0:T(8,128)S(1)} %get-tuple-element.44), channel_id=1, source_target_pairs={{0,1},{1,0},{2,3},{3,2},{4,5},{5,4},{6,7},{7,6},{8,9},{9,8},{10,11... | collective-permute-start | bytes 1572872 | tf_op jit(solution)/shard_map/ppermute | solution.py:460
  17.3 10.1 %collective-permute-start.4 = (f32[1024,128]{1,0:T(8,128)S(1)}, f32[1024,128]{1,0:T(8,128)S(1)}, u32[]{:S(2)}, u32[]{:S(2)}) collective-permute-start(f32[1024,128]{1,0:T(8,128)S(1)} %get-tuple-element.47), channel_id=1, source_target_pairs={{0,1},{1,0},{2,3},{3,2},{4,5},{5,4},{6,7},{7,6},{8,9},{9,8},{10,11... | collective-permute-start | bytes 1572872 | tf_op jit(solution)/shard_map/ppermute | solution.py:460
  17.3 10.1 %collective-permute-start.5 = (f32[1024,128]{1,0:T(8,128)S(1)}, f32[1024,128]{1,0:T(8,128)S(1)}, u32[]{:S(2)}, u32[]{:S(2)}) collective-permute-start(f32[1024,128]{1,0:T(8,128)S(1)} %get-tuple-element.49), channel_id=1, source_target_pairs={{0,1},{1,0},{2,3},{3,2},{4,5},{5,4},{6,7},{7,6},{8,9},{9,8},{10,11... | collective-permute-start | bytes 1572872 | tf_op jit(solution)/shard_map/ppermute | solution.py:460
  18.8 11.3 %collective-permute-start.9 = (f32[1040,128]{1,0:T(8,128)S(1)}, f32[1040,128]{1,0:T(8,128)S(1)}, u32[]{:S(2)}, u32[]{:S(2)}) collective-permute-start(f32[1040,128]{1,0:T(8,128)S(1)} %copy-done.2), channel_id=1, source_target_pairs={{0,1},{1,0},{2,3},{3,2},{4,5},{5,4},{6,7},{7,6},{8,9},{9,8},{10,11... | collective-permute-start | bytes 1597448 | tf_op jit(solution)/shard_map/ppermute | solution.py:460
  19.3 12.3 %collective-permute-start.8 = (f32[1040,128]{1,0:T(8,128)S(1)}, f32[1040,128]{1,0:T(8,128)S(1)}, u32[]{:S(2)}, u32[]{:S(2)}) collective-permute-start(f32[1040,128]{1,0:T(8,128)S(1)} %payload.12.refs_2_), channel_id=1, source_target_pairs={{1,3},{2,4},{5,7},{3,1},{4,2},{7,5},{9,11},{10,12},{13,15},{11,9},... | collective-permute-start | bytes 1597448 | tf_op jit(solution)/shard_map/ppermute | solution.py:463
  20.1 19.8 %collective-permute-start.3 = (f32[1040,128]{1,0:T(8,128)S(1)}, f32[1040,128]{1,0:T(8,128)S(1)}, u32[]{:S(2)}, u32[]{:S(2)}) collective-permute-start(f32[1040,128]{1,0:T(8,128)S(1)} %payload.13.refs_2_), channel_id=1, source_target_pairs={{0,2},{3,5},{4,6},{2,0},{5,3},{6,4},{8,10},{11,13},{12,14},{10,8},... | collective-permute-start | bytes 1597448 | tf_op jit(solution)/shard_map/ppermute | solution.py:463
  27.9 11.8 %collective-permute-start.6 = (f32[32,1024]{1,0:T(8,128)S(1)}, f32[32,1024]{1,0:T(8,128)S(1)}, u32[]{:S(2)}, u32[]{:S(2)}) collective-permute-start(f32[32,1024]{1,0:T(8,128)S(1)} %get-tuple-element.52), channel_id=1, source_target_pairs={{0,8},{16,24},{8,0},{24,16},{1,9},{17,25},{9,1},{25,17},{2,10},{18... | collective-permute-start | bytes 393224 | tf_op jit(solution)/shard_map/ppermute | solution.py:374
  29.5 10.3 %collective-permute-start.7 = (f32[32,1024]{1,0:T(8,128)S(1)}, f32[32,1024]{1,0:T(8,128)S(1)}, u32[]{:S(2)}, u32[]{:S(2)}) collective-permute-start(f32[32,1024]{1,0:T(8,128)S(1)} %get-tuple-element.53.refs_3_), channel_id=1, source_target_pairs={{8,16},{16,8},{9,17},{17,9},{10,18},{18,10},{11,19},{19,11},{12,20... | collective-permute-start | bytes 393224 | tf_op jit(solution)/shard_map/ppermute | solution.py:374
  30.1 12.7 %collective-permute-start.12 = (f32[1040,128]{1,0:T(8,128)S(1)}, f32[1040,128]{1,0:T(8,128)S(1)}, u32[]{:S(2)}, u32[]{:S(2)}) collective-permute-start(f32[1040,128]{1,0:T(8,128)S(1)} %pick.6.refs_2_.refs_1_), channel_id=1, source_target_pairs={{0,1},{1,0},{2,3},{3,2},{4,5},{5,4},{6,7},{7,6},{8,9},{9,8},{10,11... | collective-permute-start | bytes 1597448 | tf_op jit(solution)/shard_map/ppermute | solution.py:460
  31.7 21.0 %collective-permute-start.11 = (f32[1040,128]{1,0:T(8,128)S(1)}, f32[1040,128]{1,0:T(8,128)S(1)}, u32[]{:S(2)}, u32[]{:S(2)}) collective-permute-start(f32[1040,128]{1,0:T(8,128)S(1)} %payload.14.refs_2_), channel_id=1, source_target_pairs={{0,2},{3,5},{4,6},{2,0},{5,3},{6,4},{8,10},{11,13},{12,14},{10,8},... | collective-permute-start | bytes 1597448 | tf_op jit(solution)/shard_map/ppermute | solution.py:463
  40.0 13.4 %collective-permute-start.10 = (f32[1040,128]{1,0:T(8,128)S(1)}, f32[1040,128]{1,0:T(8,128)S(1)}, u32[]{:S(2)}, u32[]{:S(2)}) collective-permute-start(f32[1040,128]{1,0:T(8,128)S(1)} %payload.15.refs_3_), channel_id=1, source_target_pairs={{1,3},{2,4},{5,7},{3,1},{4,2},{7,5},{9,11},{10,12},{13,15},{11,9},... | collective-permute-start | bytes 1597448 | tf_op jit(solution)/shard_map/ppermute | solution.py:463
  40.7 1.4 %copy-start.5 = (f32[2,1024]{1,0:T(2,128)S(1)}, f32[2,1024]{1,0:T(2,128)}, u32[]{:S(2)}) copy-start(f32[2,1024]{1,0:T(2,128)} %refs_1_.3) | copy-start | bytes 24580
  40.7 1.4 %copy-start.6 = (f32[1024]{0:T(1024)S(1)}, f32[1024]{0:T(1024)}, u32[]{:S(2)}) copy-start(f32[1024]{0:T(1024)} %param.9) | copy-start | bytes 12292
  42.0 19.5 %collective-permute-start.15 = (f32[1024,128]{1,0:T(8,128)S(1)}, f32[1024,128]{1,0:T(8,128)S(1)}, u32[]{:S(2)}, u32[]{:S(2)}) collective-permute-start(f32[1024,128]{1,0:T(8,128)S(1)} %get-tuple-element.54.refs_4_), channel_id=1, source_target_pairs={{0,1},{1,0},{2,3},{3,2},{4,5},{5,4},{6,7},{7,6},{8,9},{9,8},{10,11... | collective-permute-start | bytes 1572872 | tf_op jit(solution)/shard_map/ppermute | solution.py:460
  42.2 19.8 %collective-permute-start.18 = (f32[1040,128]{1,0:T(8,128)S(1)}, f32[1040,128]{1,0:T(8,128)S(1)}, u32[]{:S(2)}, u32[]{:S(2)}) collective-permute-start(f32[1040,128]{1,0:T(8,128)S(1)} %pick.7.refs_2_.refs_1_), channel_id=1, source_target_pairs={{0,1},{1,0},{2,3},{3,2},{4,5},{5,4},{6,7},{7,6},{8,9},{9,8},{10,11... | collective-permute-start | bytes 1597448 | tf_op jit(solution)/shard_map/ppermute | solution.py:460
  42.8 1.4 %copy-start.1 = (bf16[640,1024]{1,0:T(8,128)(2,1)S(1)}, bf16[640,1024]{1,0:T(8,128)(2,1)}, u32[]{:S(2)}) copy-start(bf16[640,1024]{1,0:T(8,128)(2,1)} %constant.4.clone.refs_2_.refs_4_) | copy-start | bytes 3932164
  42.8 1.4 %copy-start.4 = (s32[256]{0:T(256)S(1)}, s32[256]{0:T(256)}, u32[]{:S(2)}) copy-start(s32[256]{0:T(256)} %param.10) | copy-start | bytes 3076
  52.7 15.5 %collective-permute-start.14 = (f32[1040,128]{1,0:T(8,128)S(1)}, f32[1040,128]{1,0:T(8,128)S(1)}, u32[]{:S(2)}, u32[]{:S(2)}) collective-permute-start(f32[1040,128]{1,0:T(8,128)S(1)} %payload.16.refs_3_), channel_id=1, source_target_pairs={{1,3},{2,4},{5,7},{3,1},{4,2},{7,5},{9,11},{10,12},{13,15},{11,9},... | collective-permute-start | bytes 1597448 | tf_op jit(solution)/shard_map/ppermute | solution.py:463
  53.5 14.9 %collective-permute-start.13 = (f32[1040,128]{1,0:T(8,128)S(1)}, f32[1040,128]{1,0:T(8,128)S(1)}, u32[]{:S(2)}, u32[]{:S(2)}) collective-permute-start(f32[1040,128]{1,0:T(8,128)S(1)} %payload.17.refs_4_), channel_id=1, source_target_pairs={{0,2},{3,5},{4,6},{2,0},{5,3},{6,4},{8,10},{11,13},{12,14},{10,8},... | collective-permute-start | bytes 1597448 | tf_op jit(solution)/shard_map/ppermute | solution.py:463
  61.4 2.0 %collective-permute-start.17 = (f32[520,128]{1,0:T(8,128)S(1)}, f32[520,128]{1,0:T(8,128)S(1)}, u32[]{:S(2)}, u32[]{:S(2)}) collective-permute-start(f32[520,128]{1,0:T(8,128)S(1)} %get-tuple-element.80), channel_id=1, source_target_pairs={{0,1},{1,0},{2,3},{3,2},{4,5},{5,4},{6,7},{7,6},{8,9},{9,8},{10,11... | collective-permute-start | bytes 798728 | tf_op jit(solution)/shard_map/ppermute | solution.py:460
  61.5 2.0 %collective-permute-start.16 = (f32[520,128]{1,0:T(8,128)S(1)}, f32[520,128]{1,0:T(8,128)S(1)}, u32[]{:S(2)}, u32[]{:S(2)}) collective-permute-start(f32[520,128]{1,0:T(8,128)S(1)} %get-tuple-element.81), channel_id=1, source_target_pairs={{0,1},{1,0},{2,3},{3,2},{4,5},{5,4},{6,7},{7,6},{8,9},{9,8},{10,11... | collective-permute-start | bytes 798728 | tf_op jit(solution)/shard_map/ppermute | solution.py:460
  66.3 7.0 %collective-permute-start.20 = (f32[1024,128]{1,0:T(8,128)S(1)}, f32[1024,128]{1,0:T(8,128)S(1)}, u32[]{:S(2)}, u32[]{:S(2)}) collective-permute-start(f32[1024,128]{1,0:T(8,128)S(1)} %get-tuple-element.60.refs_2_), channel_id=1, source_target_pairs={{0,1},{1,0},{2,3},{3,2},{4,5},{5,4},{6,7},{7,6},{8,9},{9,8},{10,11... | collective-permute-start | bytes 1572872 | tf_op jit(solution)/shard_map/ppermute | solution.py:460
  67.7 5.7 %collective-permute-start.21 = (f32[1024,128]{1,0:T(8,128)S(1)}, f32[1024,128]{1,0:T(8,128)S(1)}, u32[]{:S(2)}, u32[]{:S(2)}) collective-permute-start(f32[1024,128]{1,0:T(8,128)S(1)} %get-tuple-element.61.refs_3_), channel_id=1, source_target_pairs={{0,1},{1,0},{2,3},{3,2},{4,5},{5,4},{6,7},{7,6},{8,9},{9,8},{10,11... | collective-permute-start | bytes 1572872 | tf_op jit(solution)/shard_map/ppermute | solution.py:460
  68.6 16.7 %collective-permute-start.24 = (f32[1024,128]{1,0:T(8,128)S(1)}, f32[1024,128]{1,0:T(8,128)S(1)}, u32[]{:S(2)}, u32[]{:S(2)}) collective-permute-start(f32[1024,128]{1,0:T(8,128)S(1)} %get-tuple-element.62.refs_2_.refs_1_), channel_id=1, source_target_pairs={{0,2},{3,5},{4,6},{2,0},{5,3},{6,4},{8,10},{11,13},{12,14},{10,8},... | collective-permute-start | bytes 1572872 | tf_op jit(solution)/shard_map/ppermute | solution.py:463
  72.5 13.7 %collective-permute-start.19 = (f32[1024,128]{1,0:T(8,128)S(1)}, f32[1024,128]{1,0:T(8,128)S(1)}, u32[]{:S(2)}, u32[]{:S(2)}) collective-permute-start(f32[1024,128]{1,0:T(8,128)S(1)} %get-tuple-element.62.refs_2_.refs_1_), channel_id=1, source_target_pairs={{1,3},{2,4},{5,7},{3,1},{4,2},{7,5},{9,11},{10,12},{13,15},{11,9},... | collective-permute-start | bytes 1572872 | tf_op jit(solution)/shard_map/ppermute | solution.py:463
  73.2 19.4 %collective-permute-start.27 = (f32[1024,128]{1,0:T(8,128)S(1)}, f32[1024,128]{1,0:T(8,128)S(1)}, u32[]{:S(2)}, u32[]{:S(2)}) collective-permute-start(f32[1024,128]{1,0:T(8,128)S(1)} %get-tuple-element.62.refs_2_.refs_1_), channel_id=1, source_target_pairs={{0,1},{1,0},{2,3},{3,2},{4,5},{5,4},{6,7},{7,6},{8,9},{9,8},{10,11... | collective-permute-start | bytes 1572872 | tf_op jit(solution)/shard_map/ppermute | solution.py:460
  73.5 12.5 %collective-permute-start.22 = (f32[32,1024]{1,0:T(8,128)S(1)}, f32[32,1024]{1,0:T(8,128)S(1)}, u32[]{:S(2)}, u32[]{:S(2)}) collective-permute-start(f32[32,1024]{1,0:T(8,128)S(1)} %get-tuple-element.67), channel_id=1, source_target_pairs={{0,8},{16,24},{8,0},{24,16},{1,9},{17,25},{9,1},{25,17},{2,10},{18... | collective-permute-start | bytes 393224 | tf_op jit(solution)/shard_map/ppermute | solution.py:374
  75.1 11.0 %collective-permute-start.23 = (f32[32,1024]{1,0:T(8,128)S(1)}, f32[32,1024]{1,0:T(8,128)S(1)}, u32[]{:S(2)}, u32[]{:S(2)}) collective-permute-start(f32[32,1024]{1,0:T(8,128)S(1)} %get-tuple-element.68.refs_2_), channel_id=1, source_target_pairs={{8,16},{16,8},{9,17},{17,9},{10,18},{18,10},{11,19},{19,11},{12,20... | collective-permute-start | bytes 393224 | tf_op jit(solution)/shard_map/ppermute | solution.py:374
  85.3 13.3 %collective-permute-start.26 = (f32[1024,128]{1,0:T(8,128)S(1)}, f32[1024,128]{1,0:T(8,128)S(1)}, u32[]{:S(2)}, u32[]{:S(2)}) collective-permute-start(f32[1024,128]{1,0:T(8,128)S(1)} %payload.18.refs_2_), channel_id=1, source_target_pairs={{1,3},{2,4},{5,7},{3,1},{4,2},{7,5},{9,11},{10,12},{13,15},{11,9},... | collective-permute-start | bytes 1572872 | tf_op jit(solution)/shard_map/ppermute | solution.py:463
  86.3 17.5 %collective-permute-start.25 = (f32[1024,128]{1,0:T(8,128)S(1)}, f32[1024,128]{1,0:T(8,128)S(1)}, u32[]{:S(2)}, u32[]{:S(2)}) collective-permute-start(f32[1024,128]{1,0:T(8,128)S(1)} %payload.19.refs_1_), channel_id=1, source_target_pairs={{0,2},{3,5},{4,6},{2,0},{5,3},{6,4},{8,10},{11,13},{12,14},{10,8},... | collective-permute-start | bytes 1572872 | tf_op jit(solution)/shard_map/ppermute | solution.py:463
  94.0 10.6 %collective-permute-start.29 = (f32[1024,128]{1,0:T(8,128)S(1)}, f32[1024,128]{1,0:T(8,128)S(1)}, u32[]{:S(2)}, u32[]{:S(2)}) collective-permute-start(f32[1024,128]{1,0:T(8,128)S(1)} %get-tuple-element.69.refs_2_), channel_id=1, source_target_pairs={{0,1},{1,0},{2,3},{3,2},{4,5},{5,4},{6,7},{7,6},{8,9},{9,8},{10,11... | collective-permute-start | bytes 1572872 | tf_op jit(solution)/shard_map/ppermute | solution.py:460
  95.4 9.3 %collective-permute-start.34 = (f32[1024,128]{1,0:T(8,128)S(1)}, f32[1024,128]{1,0:T(8,128)S(1)}, u32[]{:S(2)}, u32[]{:S(2)}) collective-permute-start(f32[1024,128]{1,0:T(8,128)S(1)} %get-tuple-element.70.refs_8_), channel_id=1, source_target_pairs={{0,1},{1,0},{2,3},{3,2},{4,5},{5,4},{6,7},{7,6},{8,9},{9,8},{10,11... | collective-permute-start | bytes 1572872 | tf_op jit(solution)/shard_map/ppermute | solution.py:460
  95.9 9.6 %collective-permute-start.37 = (f32[1024,128]{1,0:T(8,128)S(1)}, f32[1024,128]{1,0:T(8,128)S(1)}, u32[]{:S(2)}, u32[]{:S(2)}) collective-permute-start(f32[1024,128]{1,0:T(8,128)S(1)} %pick.9.refs_2_.refs_1_), channel_id=1, source_target_pairs={{0,1},{1,0},{2,3},{3,2},{4,5},{5,4},{6,7},{7,6},{8,9},{9,8},{10,11... | collective-permute-start | bytes 1572872 | tf_op jit(solution)/shard_map/ppermute | solution.py:460
  98.7 17.1 %collective-permute-start.33 = (f32[1024,128]{1,0:T(8,128)S(1)}, f32[1024,128]{1,0:T(8,128)S(1)}, u32[]{:S(2)}, u32[]{:S(2)}) collective-permute-start(f32[1024,128]{1,0:T(8,128)S(1)} %payload.20.refs_3_), channel_id=1, source_target_pairs={{0,2},{3,5},{4,6},{2,0},{5,3},{6,4},{8,10},{11,13},{12,14},{10,8},... | collective-permute-start | bytes 1572872 | tf_op jit(solution)/shard_map/ppermute | solution.py:463
  103.9 14.0 %collective-permute-start.28 = (f32[1024,128]{1,0:T(8,128)S(1)}, f32[1024,128]{1,0:T(8,128)S(1)}, u32[]{:S(2)}, u32[]{:S(2)}) collective-permute-start(f32[1024,128]{1,0:T(8,128)S(1)} %payload.21.refs_2_), channel_id=1, source_target_pairs={{1,3},{2,4},{5,7},{3,1},{4,2},{7,5},{9,11},{10,12},{13,15},{11,9},... | collective-permute-start | bytes 1572872 | tf_op jit(solution)/shard_map/ppermute | solution.py:463
  104.9 3.1 %collective-permute-start.36 = (f32[512,128]{1,0:T(8,128)S(1)}, f32[512,128]{1,0:T(8,128)S(1)}, u32[]{:S(2)}, u32[]{:S(2)}) collective-permute-start(f32[512,128]{1,0:T(8,128)S(1)} %get-tuple-element.84), channel_id=1, source_target_pairs={{0,1},{1,0},{2,3},{3,2},{4,5},{5,4},{6,7},{7,6},{8,9},{9,8},{10,11... | collective-permute-start | bytes 786440 | tf_op jit(solution)/shard_map/ppermute | solution.py:460
  105.0 4.8 %collective-permute-start.35 = (f32[512,128]{1,0:T(8,128)S(1)}, f32[512,128]{1,0:T(8,128)S(1)}, u32[]{:S(2)}, u32[]{:S(2)}) collective-permute-start(f32[512,128]{1,0:T(8,128)S(1)} %get-tuple-element.85), channel_id=1, source_target_pairs={{0,1},{1,0},{2,3},{3,2},{4,5},{5,4},{6,7},{7,6},{8,9},{9,8},{10,11... | collective-permute-start | bytes 786440 | tf_op jit(solution)/shard_map/ppermute | solution.py:460
  105.5 12.4 %collective-permute-start.32 = (f32[2,256]{1,0:T(2,128)S(1)}, f32[2,256]{1,0:T(2,128)S(1)}, u32[]{:S(2)}, u32[]{:S(2)}) collective-permute-start(f32[2,256]{1,0:T(2,128)S(1)} %get-tuple-element.71.refs_3_.refs_0_), channel_id=1, source_target_pairs={{0,6},{1,7},{2,4},{3,5},{4,2},{5,3},{6,0},{7,1},{8,14},{9,15},{10,... | collective-permute-start | bytes 6152 | tf_op jit(solution)/shard_map/ppermute | solution.py:663
  108.0 9.9 %collective-permute-start.31 = (f32[2,256]{1,0:T(2,128)S(1)}, f32[2,256]{1,0:T(2,128)S(1)}, u32[]{:S(2)}, u32[]{:S(2)}) collective-permute-start(f32[2,256]{1,0:T(2,128)S(1)} %get-tuple-element.71.refs_3_.refs_0_), channel_id=1, source_target_pairs={{0,4},{1,5},{2,6},{3,7},{4,0},{5,1},{6,2},{7,3},{8,12},{9,13},{10,... | collective-permute-start | bytes 6152 | tf_op jit(solution)/shard_map/ppermute | solution.py:663
  109.8 8.1 %collective-permute-start.30 = (f32[2,256]{1,0:T(2,128)S(1)}, f32[2,256]{1,0:T(2,128)S(1)}, u32[]{:S(2)}, u32[]{:S(2)}) collective-permute-start(f32[2,256]{1,0:T(2,128)S(1)} %get-tuple-element.71.refs_3_.refs_0_), channel_id=1, source_target_pairs={{0,2},{1,3},{2,0},{3,1},{4,6},{5,7},{6,4},{7,5},{8,10},{9,11},{10,... | collective-permute-start | bytes 6152 | tf_op jit(solution)/shard_map/ppermute | solution.py:663
  115.9 12.8 %collective-permute-start.39 = (f32[1024,128]{1,0:T(8,128)S(1)}, f32[1024,128]{1,0:T(8,128)S(1)}, u32[]{:S(2)}, u32[]{:S(2)}) collective-permute-start(f32[1024,128]{1,0:T(8,128)S(1)} %payload.22.refs_4_), channel_id=1, source_target_pairs={{1,3},{2,4},{5,7},{3,1},{4,2},{7,5},{9,11},{10,12},{13,15},{11,9},... | collective-permute-start | bytes 1572872 | tf_op jit(solution)/shard_map/ppermute | solution.py:463
  118.0 12.2 %collective-permute-start.38 = (f32[1024,128]{1,0:T(8,128)S(1)}, f32[1024,128]{1,0:T(8,128)S(1)}, u32[]{:S(2)}, u32[]{:S(2)}) collective-permute-start(f32[1024,128]{1,0:T(8,128)S(1)} %payload.23.refs_4_), channel_id=1, source_target_pairs={{0,2},{3,5},{4,6},{2,0},{5,3},{6,4},{8,10},{11,13},{12,14},{10,8},... | collective-permute-start | bytes 1572872 | tf_op jit(solution)/shard_map/ppermute | solution.py:463
  123.4 3.9 %collective-permute-start.41 = (f32[512,128]{1,0:T(8,128)S(1)}, f32[512,128]{1,0:T(8,128)S(1)}, u32[]{:S(2)}, u32[]{:S(2)}) collective-permute-start(f32[512,128]{1,0:T(8,128)S(1)} %get-tuple-element.82), channel_id=1, source_target_pairs={{0,1},{1,0},{2,3},{3,2},{4,5},{5,4},{6,7},{7,6},{8,9},{9,8},{10,11... | collective-permute-start | bytes 786440 | tf_op jit(solution)/shard_map/ppermute | solution.py:460
  123.5 3.8 %collective-permute-start.40 = (f32[512,128]{1,0:T(8,128)S(1)}, f32[512,128]{1,0:T(8,128)S(1)}, u32[]{:S(2)}, u32[]{:S(2)}) collective-permute-start(f32[512,128]{1,0:T(8,128)S(1)} %get-tuple-element.83), channel_id=1, source_target_pairs={{0,1},{1,0},{2,3},{3,2},{4,5},{5,4},{6,7},{7,6},{8,9},{9,8},{10,11... | collective-permute-start | bytes 786440 | tf_op jit(solution)/shard_map/ppermute | solution.py:460
  124.0 2.7 %collective-permute-start.42 = (f32[2,256]{1,0:T(2,128)S(1)}, f32[2,256]{1,0:T(2,128)S(1)}, u32[]{:S(2)}, u32[]{:S(2)}) collective-permute-start(f32[2,256]{1,0:T(2,128)S(1)} %get-tuple-element.77.refs_0_), channel_id=1, source_target_pairs={{0,1},{1,0},{2,3},{3,2},{4,5},{5,4},{6,7},{7,6},{8,9},{9,8},{10,11... | collective-permute-start | bytes 6152 | tf_op jit(solution)/shard_map/ppermute | solution.py:663

commit v16 on v14

--- a/solution.py
+++ b/solution.py
@@ -600,22 +600,22 @@
 
     two = Round(matrix, step_size, False)
     two.add_terms(mid_a)
-    two.add_terms(mid_a)
     one.first_end(base_b)
     mid_b, last = call(
         functools.partial(turn_sum, time_step), [part, (HALO, modes)], one.ends()
     )
     two.begin(mid_b)
-    two.join_terms(0, 1)
-    two.take_own()
+    two.add_terms(mid_a)
+    two.join_terms(0)
     strips = paired(*call(strip_pairs, [(HALO, modes)] * 2, [leading, last]))
     flux = None
     for step in range(1, chips):
         if step == 1:
             two.send(step, unpack)
-            two.hold(0)
+            two.take_own()
+            two.join_terms(1)
         elif step == 2:
-            two.send(step)
+            two.send(step, lambda: flux.over(1))
             two.join_terms(*range(2, chips))
         elif step == chips - 1:
             two.send(step, lambda: flux.over(*range(2, devices, 2)))
@@ -626,7 +626,7 @@
             for slot in range(2, chips):
                 two.add_terms(mid_a)
         if 1 < step < chips - 1:
-            two.hold(step - 1)
+            two.hold(*range(step) if step == 2 else (step - 1,))
         if step == chips - 2:
             two.multiply(step, first=True)
         if step == chips - 1:
@@ -639,7 +639,6 @@
                 [distribution, mid_a, mid_b, strips, operators, table, kinds, scattered],
             )
             flux = Flux(call, part_flux, devices)
-    flux.over(1)
     (last_b,) = two.multiply(chips - 1, end_b)
     heat_flux = flux.value
     two.first_end(end_a)

time: 130 us -> 129 us (level); the launches traced: 127 us -> 128 us
  waiting for transfers between devices: 19.9 us -> 22.8 us
  starting transfers between devices: 70.2 us -> 68.3 us
    ppermute x19, starting transfers between devices: 18.4 us -> 13.4 us  [exchange(): lax.ppermute(value[i:j], 'mode', across)]
    ppermute x16, waiting for transfers between devices: 14.6 us -> 17.5 us  [along(): return lax.ppermute(value, 'mode', plan.pairs[stream])]
    ppermute x16, starting transfers between devices: 43.4 us -> 45 us  [along(): return lax.ppermute(value, 'mode', plan.pairs[stream])]
    ppermute x4, starting transfers between devices: 1.64 us -> 3.13 us  [over(): lax.ppermute(self.value, 'mode', [(i, i ^ bit) for i in range(self.device...]
  transfers between devices with their start and end apart: 43 -> 43, of which waited for: 12 -> 13; matrix products, arithmetic and copies ran while one was open for 0% -> 0% of each run, Pallas kernels for 25% -> 25%
where the time goes in v16:
time: 129 us; the launch traced here: 128 us
  starting transfers between devices  68.3 us (53%)
  Pallas kernels  34.4 us (27%)
  waiting for transfers between devices  22.8 us (18%)
  between operations  1.6 us (1%)
    ppermute x16, starting transfers between devices, along(): return lax.ppermute(value, 'mode', plan.pairs[stream])  45 us
    pallas_call x56, Pallas kernels, __call__(): pl.pallas_call(body, out_shape=[jax.ShapeDtypeStruct(shape, jnp.float32)...  34.4 us
    ppermute x16, waiting for transfers between devices, along(): return lax.ppermute(value, 'mode', plan.pairs[stream])  17.5 us
    ppermute x19, starting transfers between devices, exchange(): lax.ppermute(value[i:j], 'mode', across)  13.4 us
    ppermute x4, starting transfers between devices, paired(): lax.ppermute(value, 'space', pairs + [(j, i) for i, j in pairs])  6.75 us
    ppermute x4, starting transfers between devices, over(): lax.ppermute(self.value, 'mode', [(i, i ^ bit) for i in range(self.device...  3.13 us
  transfers between devices with their start and end apart: 43, of which 13 were waited for; matrix products, arithmetic and copies ran while one was open for 0% of the time, Pallas kernels for 25%

profile of v16, /device:TPU:13, one launch (start us, length us, event | category | flops | bytes accessed | tf_op | source)
XLA Modules:
  0.0 128.1 jit_solution(11532980822531553797)
XLA Ops:
  0.6 2.0 %own_rows.1 = (f32[1040,128]{1,0:T(8,128)}, f32[8,128]{1,0:T(8,128)}) custom-call(f32[1024,256]{1,0:T(8,128)} %refs_0_.9, f32[2,1024]{1,0:T(2,128)} %refs_1_.3, f32[1,1024]{1,0:T(1,128)} %bitcast.4), custom_call_target="tpu_custom_call" | custom-call | flops 1024 | bytes 1024 | tf_op jit(solution)/shard_map/own_rows/pallas_call | solution.py:39
  2.6 3.2 %collective-permute-start.2 = (f32[1040,128]{1,0:T(8,128)}, f32[1040,128]{1,0:T(8,128)S(1)}, u32[]{:S(2)}, u32[]{:S(2)}) collective-permute-start(f32[1040,128]{1,0:T(8,128)} %get-tuple-element.41.refs_1_), channel_id=1, source_target_pairs={{0,2},{3,5},{4,6},{2,0},{5,3},{6,4},{8,10},{11,13},{12,14},{10,8},... | collective-permute-start | bytes 1597448 | tf_op jit(solution)/shard_map/ppermute | solution.py:463
  5.8 1.9 %collective-permute-start = (f32[1040,128]{1,0:T(8,128)}, f32[1040,128]{1,0:T(8,128)S(1)}, u32[]{:S(2)}, u32[]{:S(2)}) collective-permute-start(f32[1040,128]{1,0:T(8,128)} %get-tuple-element.41.refs_1_), channel_id=1, source_target_pairs={{1,3},{2,4},{5,7},{3,1},{4,2},{7,5},{9,11},{10,12},{13,15},{11,9},... | collective-permute-start | bytes 1597448 | tf_op jit(solution)/shard_map/ppermute | solution.py:463
  7.8 0.7 copy-done.3
  8.5 6.2 %load_and_products.1 = (f32[1024,128]{1,0:T(8,128)S(1)}, f32[1024,128]{1,0:T(8,128)S(1)}, f32[1024,128]{1,0:T(8,128)S(1)}, f32[1024,128]{1,0:T(8,128)S(1)}, f32[...) custom-call(bf16[8192,1024]{1,0:T(8,128)(2,1)} %refs_0_.6, f32[1024,256]{1,0:T(8,128)S(1)} %copy-done, ...), custom_call_target="tpu_custom_call" | custom-call | flops 1024 | bytes 1024 | tf_op jit(solution)/shard_map/load_and_products/pallas_call | solution.py:39
  14.6 2.6 %collective-permute-start.1 = (f32[1024,128]{1,0:T(8,128)S(1)}, f32[1024,128]{1,0:T(8,128)S(1)}, u32[]{:S(2)}, u32[]{:S(2)}) collective-permute-start(f32[1024,128]{1,0:T(8,128)S(1)} %get-tuple-element.44), channel_id=1, source_target_pairs={{0,1},{1,0},{2,3},{3,2},{4,5},{5,4},{6,7},{7,6},{8,9},{9,8},{10,11... | collective-permute-start | bytes 1572872 | tf_op jit(solution)/shard_map/ppermute | solution.py:460
  17.3 0.4 collective-permute-start.5
  17.7 0.5 collective-permute-start.9
  18.2 1.5 %collective-permute-done.refs_1_.refs_0_ = f32[1040,128]{1,0:T(8,128)S(1)} collective-permute-done((f32[1040,128]{1,0:T(8,128)}, f32[1040,128]{1,0:T(8,128)S(1)}, u32[]{:S(2)}, u32[]{:S(2)}) %collective-permute-start) | collective-permute-done | bytes 532512 | tf_op jit(solution)/shard_map/ppermute | solution.py:463
  19.9 2.1 %collective-permute-start.8 = (f32[1040,128]{1,0:T(8,128)S(1)}, f32[1040,128]{1,0:T(8,128)S(1)}, u32[]{:S(2)}, u32[]{:S(2)}) collective-permute-start(f32[1040,128]{1,0:T(8,128)S(1)} %payload.12.refs_2_), channel_id=1, source_target_pairs={{1,3},{2,4},{5,7},{3,1},{4,2},{7,5},{9,11},{10,12},{13,15},{11,9},... | collective-permute-start | bytes 1597448 | tf_op jit(solution)/shard_map/ppermute | solution.py:463
  22.0 4.7 %collective-permute-start.3 = (f32[1040,128]{1,0:T(8,128)S(1)}, f32[1040,128]{1,0:T(8,128)S(1)}, u32[]{:S(2)}, u32[]{:S(2)}) collective-permute-start(f32[1040,128]{1,0:T(8,128)S(1)} %payload.13.refs_2_), channel_id=1, source_target_pairs={{0,2},{3,5},{4,6},{2,0},{5,3},{6,4},{8,10},{11,13},{12,14},{10,8},... | collective-permute-start | bytes 1597448 | tf_op jit(solution)/shard_map/ppermute | solution.py:463
  27.3 1.3 collective-permute-start.6
  28.6 2.1 %collective-permute-start.7 = (f32[32,1024]{1,0:T(8,128)S(1)}, f32[32,1024]{1,0:T(8,128)S(1)}, u32[]{:S(2)}, u32[]{:S(2)}) collective-permute-start(f32[32,1024]{1,0:T(8,128)S(1)} %get-tuple-element.53.refs_3_), channel_id=1, source_target_pairs={{8,16},{16,8},{9,17},{17,9},{10,18},{18,10},{11,19},{19,11},{12,20... | collective-permute-start | bytes 393224 | tf_op jit(solution)/shard_map/ppermute | solution.py:374
  30.7 1.4 %two_blocks.8.refs_3_ = f32[272,1024]{1,0:T(8,128)S(1)} custom-call(bf16[8192,1024]{1,0:T(8,128)(2,1)S(1)} %get-tuple-element.45.refs_2_.refs_0_, f32[1040,128]{1,0:T(8,128)S(1)} %copy-done.2, f32[1040,128]{1,0:T(8,128)S(1)} %collective-permute-done.9.refs_2_, f32[32,1024]{1,0:T(8,128)S(1)} %get-tuple-element.53.refs_3_), custom_call_target="tpu_custom_call" | custom-call | flops 1024 | bytes 1024 | tf_op jit(solution)/shard_map/two_blocks/pallas_call | solution.py:39
  32.2 5.1 %collective-permute-start.11 = (f32[1040,128]{1,0:T(8,128)S(1)}, f32[1040,128]{1,0:T(8,128)S(1)}, u32[]{:S(2)}, u32[]{:S(2)}) collective-permute-start(f32[1040,128]{1,0:T(8,128)S(1)} %payload.14.refs_2_), channel_id=1, source_target_pairs={{0,2},{3,5},{4,6},{2,0},{5,3},{6,4},{8,10},{11,13},{12,14},{10,8},... | collective-permute-start | bytes 1597448 | tf_op jit(solution)/shard_map/ppermute | solution.py:463
  37.6 1.9 %collective-permute-start.10 = (f32[1040,128]{1,0:T(8,128)S(1)}, f32[1040,128]{1,0:T(8,128)S(1)}, u32[]{:S(2)}, u32[]{:S(2)}) collective-permute-start(f32[1040,128]{1,0:T(8,128)S(1)} %payload.15.refs_3_), channel_id=1, source_target_pairs={{1,3},{2,4},{5,7},{3,1},{4,2},{7,5},{9,11},{10,12},{13,15},{11,9},... | collective-permute-start | bytes 1597448 | tf_op jit(solution)/shard_map/ppermute | solution.py:463
  39.6 1.3 slot_products.5
  40.9 0.6 collective-permute-start.15
  41.7 1.4 %two_blocks.9.refs_5_.refs_3_ = f32[272,1024]{1,0:T(8,128)S(1)} custom-call(bf16[8192,1024]{1,0:T(8,128)(2,1)S(1)} %get-tuple-element.45.refs_2_.refs_0_, f32[1040,128]{1,0:T(8,128)S(1)} %pick.6.refs_2_.refs_1_, f32[1040,128]{1,0:T(8,128)S(1)} %collective-permute-done.12.refs_2_, f32[272,1024]{1,0:T(8,128)S(1)} %two_blocks.8.refs_3_, ...), custom_call_target="tpu_custom_call" | custom-call | flops 1024 | bytes 1024 | tf_op jit(solution)/shard_map/two_blocks/pallas_call | solution.py:39
  43.1 2.0 %first_rest.1 = (f32[1024,128]{1,0:T(8,128)S(1)}, f32[1024,128]{1,0:T(8,128)S(1)}) custom-call(f32[1024,256]{1,0:T(8,128)S(1)} %copy-done, bf16[1024,128]{1,0:T(8,128)(2,1)S(1)} %strip_columns.2.refs_3_.refs_1_, bf16[640,1024]{1,0:T(8,128)(2,1)S(1)} %copy-done.1, f32[8,1024]{1,0:T(8,128)S(1)} %maximum_maximum_fusion.refs_3_.refs_5_, s32[1,256]{1,0:T(1,128)S(1)} %bitcast.2, ...), custom_call_target="tpu_custom_call" | custom-call | flops 1024 | bytes 1024 | tf_op jit(solution)/shard_map/first_rest/pallas_call | solution.py:39
  45.1 2.0 %collective-permute-done.11.refs_0_.refs_1_ = f32[1040,128]{1,0:T(8,128)S(1)} collective-permute-done((f32[1040,128]{1,0:T(8,128)S(1)}, f32[1040,128]{1,0:T(8,128)S(1)}, u32[]{:S(2)}, u32[]{:S(2)}) %collective-permute-start.11) | collective-permute-done | bytes 532512 | tf_op jit(solution)/shard_map/ppermute | solution.py:463
  47.2 1.9 %collective-permute-start.14 = (f32[1040,128]{1,0:T(8,128)S(1)}, f32[1040,128]{1,0:T(8,128)S(1)}, u32[]{:S(2)}, u32[]{:S(2)}) collective-permute-start(f32[1040,128]{1,0:T(8,128)S(1)} %payload.16.refs_3_), channel_id=1, source_target_pairs={{1,3},{2,4},{5,7},{3,1},{4,2},{7,5},{9,11},{10,12},{13,15},{11,9},... | collective-permute-start | bytes 1597448 | tf_op jit(solution)/shard_map/ppermute | solution.py:463
  49.3 3.5 %collective-permute-start.13 = (f32[1040,128]{1,0:T(8,128)S(1)}, f32[1040,128]{1,0:T(8,128)S(1)}, u32[]{:S(2)}, u32[]{:S(2)}) collective-permute-start(f32[1040,128]{1,0:T(8,128)S(1)} %payload.17.refs_4_), channel_id=1, source_target_pairs={{0,2},{3,5},{4,6},{2,0},{5,3},{6,4},{8,10},{11,13},{12,14},{10,8},... | collective-permute-start | bytes 1597448 | tf_op jit(solution)/shard_map/ppermute | solution.py:463
  53.2 0.5 collective-permute-start.16
  53.8 1.4 %two_blocks.10.refs_4_.refs_6_ = f32[272,1024]{1,0:T(8,128)S(1)} custom-call(bf16[8192,1024]{1,0:T(8,128)(2,1)S(1)} %get-tuple-element.45.refs_2_.refs_0_, f32[1040,128]{1,0:T(8,128)S(1)} %pick.7.refs_2_.refs_1_, f32[1040,128]{1,0:T(8,128)S(1)} %collective-permute-done.18.refs_2_, f32[272,1024]{1,0:T(8,128)S(1)} %two_blocks.9.refs_5_.refs_3_, ...), custom_call_target="tpu_custom_call" | custom-call | flops 1024 | bytes 1024 | tf_op jit(solution)/shard_map/two_blocks/pallas_call | solution.py:39
  55.2 1.5 %two_blocks.11 = (f32[1024,128]{1,0:T(8,128)S(1)}, f32[32,1024]{1,0:T(8,128)S(1)}, f32[8,1024]{1,0:T(8,128)S(1)}) custom-call(bf16[8192,1024]{1,0:T(8,128)(2,1)S(1)} %get-tuple-element.45.refs_2_.refs_0_, f32[1040,128]{1,0:T(8,128)S(1)} %pick.8.refs_2_.refs_1_, f32[520,128]{1,0:T(8,128)S(1)} %collective-permute-done.16.refs_2_, ...), custom_call_target="tpu_custom_call" | custom-call | flops 1024 | bytes 1024 | tf_op jit(solution)/shard_map/two_blocks/pallas_call | solution.py:39
  56.7 1.3 slot_products.6
  58.2 0.9 collective-permute-done.14.refs_0_
  59.2 4.0 %collective-permute-done.13.refs_0_ = f32[1040,128]{1,0:T(8,128)S(1)} collective-permute-done((f32[1040,128]{1,0:T(8,128)S(1)}, f32[1040,128]{1,0:T(8,128)S(1)}, u32[]{:S(2)}, u32[]{:S(2)}) %collective-permute-start.13) | collective-permute-done | bytes 532512 | tf_op jit(solution)/shard_map/ppermute | solution.py:463
  63.4 3.3 %collective-permute-start.23 = (f32[1024,128]{1,0:T(8,128)S(1)}, f32[1024,128]{1,0:T(8,128)S(1)}, u32[]{:S(2)}, u32[]{:S(2)}) collective-permute-start(f32[1024,128]{1,0:T(8,128)S(1)} %get-tuple-element.61.refs_2_.refs_1_), channel_id=1, source_target_pairs={{0,2},{3,5},{4,6},{2,0},{5,3},{6,4},{8,10},{11,13},{12,14},{10,8},... | collective-permute-start | bytes 1572872 | tf_op jit(solution)/shard_map/ppermute | solution.py:463
  66.8 1.9 %collective-permute-start.19 = (f32[1024,128]{1,0:T(8,128)S(1)}, f32[1024,128]{1,0:T(8,128)S(1)}, u32[]{:S(2)}, u32[]{:S(2)}) collective-permute-start(f32[1024,128]{1,0:T(8,128)S(1)} %get-tuple-element.61.refs_2_.refs_1_), channel_id=1, source_target_pairs={{1,3},{2,4},{5,7},{3,1},{4,2},{7,5},{9,11},{10,12},{13,15},{11,9},... | collective-permute-start | bytes 1572872 | tf_op jit(solution)/shard_map/ppermute | solution.py:463
  68.7 1.3 slot_products.7
  70.0 1.0 collective-permute-start.25
  71.0 1.3 collective-permute-start.21
  72.3 2.1 %collective-permute-start.22 = (f32[32,1024]{1,0:T(8,128)S(1)}, f32[32,1024]{1,0:T(8,128)S(1)}, u32[]{:S(2)}, u32[]{:S(2)}) collective-permute-start(f32[32,1024]{1,0:T(8,128)S(1)} %get-tuple-element.67.refs_2_), channel_id=1, source_target_pairs={{8,16},{16,8},{9,17},{17,9},{10,18},{18,10},{11,19},{19,11},{12,20... | collective-permute-start | bytes 393224 | tf_op jit(solution)/shard_map/ppermute | solution.py:374
  74.4 1.7 %collective-permute-done.23.refs_0_ = f32[1024,128]{1,0:T(8,128)S(1)} collective-permute-done((f32[1024,128]{1,0:T(8,128)S(1)}, f32[1024,128]{1,0:T(8,128)S(1)}, u32[]{:S(2)}, u32[]{:S(2)}) %collective-permute-start.23) | collective-permute-done | bytes 524320 | tf_op jit(solution)/shard_map/ppermute | solution.py:463
  76.1 1.9 %collective-permute-start.27 = (f32[1024,128]{1,0:T(8,128)S(1)}, f32[1024,128]{1,0:T(8,128)S(1)}, u32[]{:S(2)}, u32[]{:S(2)}) collective-permute-start(f32[1024,128]{1,0:T(8,128)S(1)} %payload.18.refs_2_), channel_id=1, source_target_pairs={{1,3},{2,4},{5,7},{3,1},{4,2},{7,5},{9,11},{10,12},{13,15},{11,9},... | collective-permute-start | bytes 1572872 | tf_op jit(solution)/shard_map/ppermute | solution.py:463
  78.1 1.8 %collective-permute-done.22.refs_1_ = f32[32,1024]{1,0:T(8,128)S(1)} collective-permute-done((f32[32,1024]{1,0:T(8,128)S(1)}, f32[32,1024]{1,0:T(8,128)S(1)}, u32[]{:S(2)}, u32[]{:S(2)}) %collective-permute-start.22) | collective-permute-done | bytes 131104 | tf_op jit(solution)/shard_map/ppermute | solution.py:374
  80.1 3.0 %collective-permute-start.24 = (f32[1024,128]{1,0:T(8,128)S(1)}, f32[1024,128]{1,0:T(8,128)S(1)}, u32[]{:S(2)}, u32[]{:S(2)}) collective-permute-start(f32[1024,128]{1,0:T(8,128)S(1)} %payload.19.refs_2_), channel_id=1, source_target_pairs={{0,2},{3,5},{4,6},{2,0},{5,3},{6,4},{8,10},{11,13},{12,14},{10,8},... | collective-permute-start | bytes 1572872 | tf_op jit(solution)/shard_map/ppermute | solution.py:463
  83.3 1.3 slot_products.8
  84.6 2.1 %collective-permute-start.29 = (f32[1024,128]{1,0:T(8,128)S(1)}, f32[1024,128]{1,0:T(8,128)S(1)}, u32[]{:S(2)}, u32[]{:S(2)}) collective-permute-start(f32[1024,128]{1,0:T(8,128)S(1)} %get-tuple-element.69.refs_2_), channel_id=1, source_target_pairs={{0,1},{1,0},{2,3},{3,2},{4,5},{5,4},{6,7},{7,6},{8,9},{9,8},{10,11... | collective-permute-start | bytes 1572872 | tf_op jit(solution)/shard_map/ppermute | solution.py:460
  86.6 1.3 slot_products.9
  88.0 2.5 %second_rest.1 = (f32[1024,128]{1,0:T(8,128)S(1)}, f32[1024,128]{1,0:T(8,128)S(1)}, f32[2,256]{1,0:T(2,128)S(1)}) custom-call(f32[1024,256]{1,0:T(8,128)S(1)} %copy-done, f32[1024,128]{1,0:T(8,128)S(1)} %get-tuple-element.58.refs_1_, f32[1024,128]{1,0:T(8,128)S(1)} %get-tuple-element.61.refs_2_.refs_1_, bf16[1024,128]{1,0:T(8,128)(2,1)S(1)} %strip_columns.3.refs_2_.refs_3_, ...), custom_call_target="tpu_custom_call" | custom-call | flops 1024 | bytes 1024 | tf_op jit(solution)/shard_map/second_rest/pallas_call | solution.py:39
  90.5 0.6 collective-permute-start.26
  91.1 0.8 collective-permute-done.26.refs_1_
  91.9 0.3 collective-permute-start.38
  92.3 3.0 %collective-permute-start.37 = (f32[1024,128]{1,0:T(8,128)S(1)}, f32[1024,128]{1,0:T(8,128)S(1)}, u32[]{:S(2)}, u32[]{:S(2)}) collective-permute-start(f32[1024,128]{1,0:T(8,128)S(1)} %pick.9.refs_2_.refs_1_), channel_id=1, source_target_pairs={{0,1},{1,0},{2,3},{3,2},{4,5},{5,4},{6,7},{7,6},{8,9},{9,8},{10,11... | collective-permute-start | bytes 1572872 | tf_op jit(solution)/shard_map/ppermute | solution.py:460
  95.3 4.1 %collective-permute-start.33 = (f32[1024,128]{1,0:T(8,128)S(1)}, f32[1024,128]{1,0:T(8,128)S(1)}, u32[]{:S(2)}, u32[]{:S(2)}) collective-permute-start(f32[1024,128]{1,0:T(8,128)S(1)} %payload.20.refs_2_), channel_id=1, source_target_pairs={{0,2},{3,5},{4,6},{2,0},{5,3},{6,4},{8,10},{11,13},{12,14},{10,8},... | collective-permute-start | bytes 1572872 | tf_op jit(solution)/shard_map/ppermute | solution.py:463
  99.6 1.9 %collective-permute-start.28 = (f32[1024,128]{1,0:T(8,128)S(1)}, f32[1024,128]{1,0:T(8,128)S(1)}, u32[]{:S(2)}, u32[]{:S(2)}) collective-permute-start(f32[1024,128]{1,0:T(8,128)S(1)} %payload.21.refs_2_), channel_id=1, source_target_pairs={{1,3},{2,4},{5,7},{3,1},{4,2},{7,5},{9,11},{10,12},{13,15},{11,9},... | collective-permute-start | bytes 1572872 | tf_op jit(solution)/shard_map/ppermute | solution.py:463
  101.8 0.3 collective-permute-start.36
  102.4 1.0 collective-permute-done.36.refs_3_
  103.4 2.5 %collective-permute-start.31 = (f32[2,256]{1,0:T(2,128)S(1)}, f32[2,256]{1,0:T(2,128)S(1)}, u32[]{:S(2)}, u32[]{:S(2)}) collective-permute-start(f32[2,256]{1,0:T(2,128)S(1)} %get-tuple-element.74.refs_0_), channel_id=1, source_target_pairs={{0,4},{1,5},{2,6},{3,7},{4,0},{5,1},{6,2},{7,3},{8,12},{9,13},{10,... | collective-permute-start | bytes 6152 | tf_op jit(solution)/shard_map/ppermute | solution.py:661
  106.0 1.3 %two_blocks.12.refs_3_ = f32[256,1024]{1,0:T(8,128)S(1)} custom-call(bf16[8192,1024]{1,0:T(8,128)(2,1)S(1)} %get-tuple-element.45.refs_2_.refs_0_, f32[1024,128]{1,0:T(8,128)S(1)} %pick.10.refs_1_, f32[512,128]{1,0:T(8,128)S(1)} %collective-permute-done.35.refs_2_, f32[512,128]{1,0:T(8,128)S(1)} %collective-permute-done.36.refs_3_, ...), custom_call_target="tpu_custom_call" | custom-call | flops 1024 | bytes 1024 | tf_op jit(solution)/shard_map/two_blocks/pallas_call | solution.py:39
  107.3 2.4 %collective-permute-done.33.refs_0_.refs_1_ = f32[1024,128]{1,0:T(8,128)S(1)} collective-permute-done((f32[1024,128]{1,0:T(8,128)S(1)}, f32[1024,128]{1,0:T(8,128)S(1)}, u32[]{:S(2)}, u32[]{:S(2)}) %collective-permute-start.33) | collective-permute-done | bytes 524320 | tf_op jit(solution)/shard_map/ppermute | solution.py:463
  109.7 1.9 %collective-permute-start.40 = (f32[1024,128]{1,0:T(8,128)S(1)}, f32[1024,128]{1,0:T(8,128)S(1)}, u32[]{:S(2)}, u32[]{:S(2)}) collective-permute-start(f32[1024,128]{1,0:T(8,128)S(1)} %payload.22.refs_4_), channel_id=1, source_target_pairs={{1,3},{2,4},{5,7},{3,1},{4,2},{7,5},{9,11},{10,12},{13,15},{11,9},... | collective-permute-start | bytes 1572872 | tf_op jit(solution)/shard_map/ppermute | solution.py:463
  111.7 1.7 %collective-permute-done.31.refs_2_ = f32[2,256]{1,0:T(2,128)S(1)} collective-permute-done((f32[2,256]{1,0:T(2,128)S(1)}, f32[2,256]{1,0:T(2,128)S(1)}, u32[]{:S(2)}, u32[]{:S(2)}) %collective-permute-start.31) | collective-permute-done | bytes 2080 | tf_op jit(solution)/shard_map/ppermute | solution.py:661
  113.4 0.6 add_all.3
  114.0 2.4 %collective-permute-start.39 = (f32[1024,128]{1,0:T(8,128)S(1)}, f32[1024,128]{1,0:T(8,128)S(1)}, u32[]{:S(2)}, u32[]{:S(2)}) collective-permute-start(f32[1024,128]{1,0:T(8,128)S(1)} %payload.23.refs_4_), channel_id=1, source_target_pairs={{0,2},{3,5},{4,6},{2,0},{5,3},{6,4},{8,10},{11,13},{12,14},{10,8},... | collective-permute-start | bytes 1572872 | tf_op jit(solution)/shard_map/ppermute | solution.py:463
  116.6 1.3 collective-permute-start.42
  117.9 1.3 %two_blocks.13.refs_3_.refs_4_ = f32[256,1024]{1,0:T(8,128)S(1)} custom-call(bf16[8192,1024]{1,0:T(8,128)(2,1)S(1)} %get-tuple-element.45.refs_2_.refs_0_, f32[1024,128]{1,0:T(8,128)S(1)} %get-tuple-element.61.refs_2_.refs_1_, f32[1024,128]{1,0:T(8,128)S(1)} %pass_on.2.refs_1_.refs_2_, f32[256,1024]{1,0:T(8,128)S(1)} %two_blocks.12.refs_3_, ...), custom_call_target="tpu_custom_call" | custom-call | flops 1024 | bytes 1024 | tf_op jit(solution)/shard_map/two_blocks/pallas_call | solution.py:39
  119.2 1.3 %two_blocks.14.refs_4_.refs_6_ = f32[256,1024]{1,0:T(8,128)S(1)} custom-call(bf16[8192,1024]{1,0:T(8,128)(2,1)S(1)} %get-tuple-element.45.refs_2_.refs_0_, f32[1024,128]{1,0:T(8,128)S(1)} %pick.9.refs_2_.refs_1_, f32[1024,128]{1,0:T(8,128)S(1)} %pass_on.3.refs_4_.refs_2_, f32[256,1024]{1,0:T(8,128)S(1)} %two_blocks.13.refs_3_.refs_4_, ...), custom_call_target="tpu_custom_call" | custom-call | flops 1024 | bytes 1024 | tf_op jit(solution)/shard_map/two_blocks/pallas_call | solution.py:39
  120.5 1.4 %two_blocks.15.refs_3_.refs_2_ = f32[1024,128]{1,0:T(8,128)S(1)} custom-call(bf16[8192,1024]{1,0:T(8,128)(2,1)S(1)} %get-tuple-element.45.refs_2_.refs_0_, f32[1024,128]{1,0:T(8,128)S(1)} %pick.11.refs_4_.refs_1_, f32[512,128]{1,0:T(8,128)S(1)} %collective-permute-done.41.refs_2_, f32[512,128]{1,0:T(8,128)S(1)} %collective-permute-done.42.refs_3_, ...), custom_call_target="tpu_custom_call" | custom-call | flops 1024 | bytes 1024 | tf_op jit(solution)/shard_map/two_blocks/pallas_call | solution.py:39
  122.1 4.8 %collective-permute-done.39.refs_0_ = f32[1024,128]{1,0:T(8,128)S(1)} collective-permute-done((f32[1024,128]{1,0:T(8,128)S(1)}, f32[1024,128]{1,0:T(8,128)S(1)}, u32[]{:S(2)}, u32[]{:S(2)}) %collective-permute-start.39) | collective-permute-done | bytes 524320 | tf_op jit(solution)/shard_map/ppermute | solution.py:463
  126.9 1.0 last_sum.1
  (99 shorter events, 4.4 us)
Async XLA Ops:
  0.6 7.1 %copy-start = (f32[1024,256]{1,0:T(8,128)S(1)}, f32[1024,256]{1,0:T(8,128)}, u32[]{:S(2)}) copy-start(f32[1024,256]{1,0:T(8,128)} %refs_0_.9) | copy-start | bytes 3145732
  2.6 15.1 %collective-permute-start.2 = (f32[1040,128]{1,0:T(8,128)}, f32[1040,128]{1,0:T(8,128)S(1)}, u32[]{:S(2)}, u32[]{:S(2)}) collective-permute-start(f32[1040,128]{1,0:T(8,128)} %get-tuple-element.41.refs_1_), channel_id=1, source_target_pairs={{0,2},{3,5},{4,6},{2,0},{5,3},{6,4},{8,10},{11,13},{12,14},{10,8},... | collective-permute-start | bytes 1597448 | tf_op jit(solution)/shard_map/ppermute | solution.py:463
  5.8 13.9 %collective-permute-start = (f32[1040,128]{1,0:T(8,128)}, f32[1040,128]{1,0:T(8,128)S(1)}, u32[]{:S(2)}, u32[]{:S(2)}) collective-permute-start(f32[1040,128]{1,0:T(8,128)} %get-tuple-element.41.refs_1_), channel_id=1, source_target_pairs={{1,3},{2,4},{5,7},{3,1},{4,2},{7,5},{9,11},{10,12},{13,15},{11,9},... | collective-permute-start | bytes 1597448 | tf_op jit(solution)/shard_map/ppermute | solution.py:463
  7.8 0.7 copy-start.3
  8.5 9.3 %copy-start.2 = (f32[1040,128]{1,0:T(8,128)S(1)}, f32[1040,128]{1,0:T(8,128)}, u32[]{:S(2)}) copy-start(f32[1040,128]{1,0:T(8,128)} %get-tuple-element.41.refs_1_) | copy-start | bytes 1597444
  14.6 5.1 %collective-permute-start.1 = (f32[1024,128]{1,0:T(8,128)S(1)}, f32[1024,128]{1,0:T(8,128)S(1)}, u32[]{:S(2)}, u32[]{:S(2)}) collective-permute-start(f32[1024,128]{1,0:T(8,128)S(1)} %get-tuple-element.44), channel_id=1, source_target_pairs={{0,1},{1,0},{2,3},{3,2},{4,5},{5,4},{6,7},{7,6},{8,9},{9,8},{10,11... | collective-permute-start | bytes 1572872 | tf_op jit(solution)/shard_map/ppermute | solution.py:460
  17.2 9.5 %collective-permute-start.4 = (f32[1024,128]{1,0:T(8,128)S(1)}, f32[1024,128]{1,0:T(8,128)S(1)}, u32[]{:S(2)}, u32[]{:S(2)}) collective-permute-start(f32[1024,128]{1,0:T(8,128)S(1)} %get-tuple-element.47), channel_id=1, source_target_pairs={{0,1},{1,0},{2,3},{3,2},{4,5},{5,4},{6,7},{7,6},{8,9},{9,8},{10,11... | collective-permute-start | bytes 1572872 | tf_op jit(solution)/shard_map/ppermute | solution.py:460
  17.3 9.5 %collective-permute-start.5 = (f32[1024,128]{1,0:T(8,128)S(1)}, f32[1024,128]{1,0:T(8,128)S(1)}, u32[]{:S(2)}, u32[]{:S(2)}) collective-permute-start(f32[1024,128]{1,0:T(8,128)S(1)} %get-tuple-element.49), channel_id=1, source_target_pairs={{0,1},{1,0},{2,3},{3,2},{4,5},{5,4},{6,7},{7,6},{8,9},{9,8},{10,11... | collective-permute-start | bytes 1572872 | tf_op jit(solution)/shard_map/ppermute | solution.py:460
  17.7 12.9 %collective-permute-start.9 = (f32[1040,128]{1,0:T(8,128)S(1)}, f32[1040,128]{1,0:T(8,128)S(1)}, u32[]{:S(2)}, u32[]{:S(2)}) collective-permute-start(f32[1040,128]{1,0:T(8,128)S(1)} %copy-done.2), channel_id=1, source_target_pairs={{0,1},{1,0},{2,3},{3,2},{4,5},{5,4},{6,7},{7,6},{8,9},{9,8},{10,11... | collective-permute-start | bytes 1597448 | tf_op jit(solution)/shard_map/ppermute | solution.py:460
  19.9 12.2 %collective-permute-start.8 = (f32[1040,128]{1,0:T(8,128)S(1)}, f32[1040,128]{1,0:T(8,128)S(1)}, u32[]{:S(2)}, u32[]{:S(2)}) collective-permute-start(f32[1040,128]{1,0:T(8,128)S(1)} %payload.12.refs_2_), channel_id=1, source_target_pairs={{1,3},{2,4},{5,7},{3,1},{4,2},{7,5},{9,11},{10,12},{13,15},{11,9},... | collective-permute-start | bytes 1597448 | tf_op jit(solution)/shard_map/ppermute | solution.py:463
  22.0 15.5 %collective-permute-start.3 = (f32[1040,128]{1,0:T(8,128)S(1)}, f32[1040,128]{1,0:T(8,128)S(1)}, u32[]{:S(2)}, u32[]{:S(2)}) collective-permute-start(f32[1040,128]{1,0:T(8,128)S(1)} %payload.13.refs_2_), channel_id=1, source_target_pairs={{0,2},{3,5},{4,6},{2,0},{5,3},{6,4},{8,10},{11,13},{12,14},{10,8},... | collective-permute-start | bytes 1597448 | tf_op jit(solution)/shard_map/ppermute | solution.py:463
  27.3 10.1 %collective-permute-start.6 = (f32[32,1024]{1,0:T(8,128)S(1)}, f32[32,1024]{1,0:T(8,128)S(1)}, u32[]{:S(2)}, u32[]{:S(2)}) collective-permute-start(f32[32,1024]{1,0:T(8,128)S(1)} %get-tuple-element.52), channel_id=1, source_target_pairs={{0,8},{16,24},{8,0},{24,16},{1,9},{17,25},{9,1},{25,17},{2,10},{18... | collective-permute-start | bytes 393224 | tf_op jit(solution)/shard_map/ppermute | solution.py:374
  28.6 8.8 %collective-permute-start.7 = (f32[32,1024]{1,0:T(8,128)S(1)}, f32[32,1024]{1,0:T(8,128)S(1)}, u32[]{:S(2)}, u32[]{:S(2)}) collective-permute-start(f32[32,1024]{1,0:T(8,128)S(1)} %get-tuple-element.53.refs_3_), channel_id=1, source_target_pairs={{8,16},{16,8},{9,17},{17,9},{10,18},{18,10},{11,19},{19,11},{12,20... | collective-permute-start | bytes 393224 | tf_op jit(solution)/shard_map/ppermute | solution.py:374
  30.7 11.0 %collective-permute-start.12 = (f32[1040,128]{1,0:T(8,128)S(1)}, f32[1040,128]{1,0:T(8,128)S(1)}, u32[]{:S(2)}, u32[]{:S(2)}) collective-permute-start(f32[1040,128]{1,0:T(8,128)S(1)} %pick.6.refs_2_.refs_1_), channel_id=1, source_target_pairs={{0,1},{1,0},{2,3},{3,2},{4,5},{5,4},{6,7},{7,6},{8,9},{9,8},{10,11... | collective-permute-start | bytes 1597448 | tf_op jit(solution)/shard_map/ppermute | solution.py:460
  32.2 14.9 %collective-permute-start.11 = (f32[1040,128]{1,0:T(8,128)S(1)}, f32[1040,128]{1,0:T(8,128)S(1)}, u32[]{:S(2)}, u32[]{:S(2)}) collective-permute-start(f32[1040,128]{1,0:T(8,128)S(1)} %payload.14.refs_2_), channel_id=1, source_target_pairs={{0,2},{3,5},{4,6},{2,0},{5,3},{6,4},{8,10},{11,13},{12,14},{10,8},... | collective-permute-start | bytes 1597448 | tf_op jit(solution)/shard_map/ppermute | solution.py:463
  37.6 11.6 %collective-permute-start.10 = (f32[1040,128]{1,0:T(8,128)S(1)}, f32[1040,128]{1,0:T(8,128)S(1)}, u32[]{:S(2)}, u32[]{:S(2)}) collective-permute-start(f32[1040,128]{1,0:T(8,128)S(1)} %payload.15.refs_3_), channel_id=1, source_target_pairs={{1,3},{2,4},{5,7},{3,1},{4,2},{7,5},{9,11},{10,12},{13,15},{11,9},... | collective-permute-start | bytes 1597448 | tf_op jit(solution)/shard_map/ppermute | solution.py:463
  39.6 1.9 %copy-start.5 = (f32[2,1024]{1,0:T(2,128)S(1)}, f32[2,1024]{1,0:T(2,128)}, u32[]{:S(2)}) copy-start(f32[2,1024]{1,0:T(2,128)} %refs_1_.3) | copy-start | bytes 24580
  39.6 1.9 %copy-start.6 = (f32[1024]{0:T(1024)S(1)}, f32[1024]{0:T(1024)}, u32[]{:S(2)}) copy-start(f32[1024]{0:T(1024)} %param.9) | copy-start | bytes 12292
  40.9 12.3 %collective-permute-start.15 = (f32[1024,128]{1,0:T(8,128)S(1)}, f32[1024,128]{1,0:T(8,128)S(1)}, u32[]{:S(2)}, u32[]{:S(2)}) collective-permute-start(f32[1024,128]{1,0:T(8,128)S(1)} %get-tuple-element.54.refs_4_), channel_id=1, source_target_pairs={{0,1},{1,0},{2,3},{3,2},{4,5},{5,4},{6,7},{7,6},{8,9},{9,8},{10,11... | collective-permute-start | bytes 1572872 | tf_op jit(solution)/shard_map/ppermute | solution.py:460
  41.6 12.2 %collective-permute-start.18 = (f32[1040,128]{1,0:T(8,128)S(1)}, f32[1040,128]{1,0:T(8,128)S(1)}, u32[]{:S(2)}, u32[]{:S(2)}) collective-permute-start(f32[1040,128]{1,0:T(8,128)S(1)} %pick.7.refs_2_.refs_1_), channel_id=1, source_target_pairs={{0,1},{1,0},{2,3},{3,2},{4,5},{5,4},{6,7},{7,6},{8,9},{9,8},{10,11... | collective-permute-start | bytes 1597448 | tf_op jit(solution)/shard_map/ppermute | solution.py:460
  41.7 1.4 %copy-start.1 = (bf16[640,1024]{1,0:T(8,128)(2,1)S(1)}, bf16[640,1024]{1,0:T(8,128)(2,1)}, u32[]{:S(2)}) copy-start(bf16[640,1024]{1,0:T(8,128)(2,1)} %constant.4.clone.refs_2_.refs_4_) | copy-start | bytes 3932164
  41.7 1.4 %copy-start.4 = (s32[256]{0:T(256)S(1)}, s32[256]{0:T(256)}, u32[]{:S(2)}) copy-start(s32[256]{0:T(256)} %param.10) | copy-start | bytes 3076
  47.2 11.9 %collective-permute-start.14 = (f32[1040,128]{1,0:T(8,128)S(1)}, f32[1040,128]{1,0:T(8,128)S(1)}, u32[]{:S(2)}, u32[]{:S(2)}) collective-permute-start(f32[1040,128]{1,0:T(8,128)S(1)} %payload.16.refs_3_), channel_id=1, source_target_pairs={{1,3},{2,4},{5,7},{3,1},{4,2},{7,5},{9,11},{10,12},{13,15},{11,9},... | collective-permute-start | bytes 1597448 | tf_op jit(solution)/shard_map/ppermute | solution.py:463
  49.3 13.8 %collective-permute-start.13 = (f32[1040,128]{1,0:T(8,128)S(1)}, f32[1040,128]{1,0:T(8,128)S(1)}, u32[]{:S(2)}, u32[]{:S(2)}) collective-permute-start(f32[1040,128]{1,0:T(8,128)S(1)} %payload.17.refs_4_), channel_id=1, source_target_pairs={{0,2},{3,5},{4,6},{2,0},{5,3},{6,4},{8,10},{11,13},{12,14},{10,8},... | collective-permute-start | bytes 1597448 | tf_op jit(solution)/shard_map/ppermute | solution.py:463
  53.1 2.0 %collective-permute-start.17 = (f32[520,128]{1,0:T(8,128)S(1)}, f32[520,128]{1,0:T(8,128)S(1)}, u32[]{:S(2)}, u32[]{:S(2)}) collective-permute-start(f32[520,128]{1,0:T(8,128)S(1)} %get-tuple-element.80), channel_id=1, source_target_pairs={{0,1},{1,0},{2,3},{3,2},{4,5},{5,4},{6,7},{7,6},{8,9},{9,8},{10,11... | collective-permute-start | bytes 798728 | tf_op jit(solution)/shard_map/ppermute | solution.py:460
  53.2 2.0 %collective-permute-start.16 = (f32[520,128]{1,0:T(8,128)S(1)}, f32[520,128]{1,0:T(8,128)S(1)}, u32[]{:S(2)}, u32[]{:S(2)}) collective-permute-start(f32[520,128]{1,0:T(8,128)S(1)} %get-tuple-element.81), channel_id=1, source_target_pairs={{0,1},{1,0},{2,3},{3,2},{4,5},{5,4},{6,7},{7,6},{8,9},{9,8},{10,11... | collective-permute-start | bytes 798728 | tf_op jit(solution)/shard_map/ppermute | solution.py:460
  58.0 12.9 %collective-permute-start.20 = (f32[1024,128]{1,0:T(8,128)S(1)}, f32[1024,128]{1,0:T(8,128)S(1)}, u32[]{:S(2)}, u32[]{:S(2)}) collective-permute-start(f32[1024,128]{1,0:T(8,128)S(1)} %get-tuple-element.60.refs_3_), channel_id=1, source_target_pairs={{0,1},{1,0},{2,3},{3,2},{4,5},{5,4},{6,7},{7,6},{8,9},{9,8},{10,11... | collective-permute-start | bytes 1572872 | tf_op jit(solution)/shard_map/ppermute | solution.py:460
  63.4 12.7 %collective-permute-start.23 = (f32[1024,128]{1,0:T(8,128)S(1)}, f32[1024,128]{1,0:T(8,128)S(1)}, u32[]{:S(2)}, u32[]{:S(2)}) collective-permute-start(f32[1024,128]{1,0:T(8,128)S(1)} %get-tuple-element.61.refs_2_.refs_1_), channel_id=1, source_target_pairs={{0,2},{3,5},{4,6},{2,0},{5,3},{6,4},{8,10},{11,13},{12,14},{10,8},... | collective-permute-start | bytes 1572872 | tf_op jit(solution)/shard_map/ppermute | solution.py:463
  66.8 13.3 %collective-permute-start.19 = (f32[1024,128]{1,0:T(8,128)S(1)}, f32[1024,128]{1,0:T(8,128)S(1)}, u32[]{:S(2)}, u32[]{:S(2)}) collective-permute-start(f32[1024,128]{1,0:T(8,128)S(1)} %get-tuple-element.61.refs_2_.refs_1_), channel_id=1, source_target_pairs={{1,3},{2,4},{5,7},{3,1},{4,2},{7,5},{9,11},{10,12},{13,15},{11,9},... | collective-permute-start | bytes 1572872 | tf_op jit(solution)/shard_map/ppermute | solution.py:463
  70.0 13.2 %collective-permute-start.25 = (f32[1024,128]{1,0:T(8,128)S(1)}, f32[1024,128]{1,0:T(8,128)S(1)}, u32[]{:S(2)}, u32[]{:S(2)}) collective-permute-start(f32[1024,128]{1,0:T(8,128)S(1)} %get-tuple-element.64.refs_2_), channel_id=1, source_target_pairs={{0,1},{1,0},{2,3},{3,2},{4,5},{5,4},{6,7},{7,6},{8,9},{9,8},{10,11... | collective-permute-start | bytes 1572872 | tf_op jit(solution)/shard_map/ppermute | solution.py:460
  71.0 7.0 %collective-permute-start.21 = (f32[32,1024]{1,0:T(8,128)S(1)}, f32[32,1024]{1,0:T(8,128)S(1)}, u32[]{:S(2)}, u32[]{:S(2)}) collective-permute-start(f32[32,1024]{1,0:T(8,128)S(1)} %get-tuple-element.66), channel_id=1, source_target_pairs={{0,8},{16,24},{8,0},{24,16},{1,9},{17,25},{9,1},{25,17},{2,10},{18... | collective-permute-start | bytes 393224 | tf_op jit(solution)/shard_map/ppermute | solution.py:374
  72.3 7.6 %collective-permute-start.22 = (f32[32,1024]{1,0:T(8,128)S(1)}, f32[32,1024]{1,0:T(8,128)S(1)}, u32[]{:S(2)}, u32[]{:S(2)}) collective-permute-start(f32[32,1024]{1,0:T(8,128)S(1)} %get-tuple-element.67.refs_2_), channel_id=1, source_target_pairs={{8,16},{16,8},{9,17},{17,9},{10,18},{18,10},{11,19},{19,11},{12,20... | collective-permute-start | bytes 393224 | tf_op jit(solution)/shard_map/ppermute | solution.py:374
  76.1 16.1 %collective-permute-start.27 = (f32[1024,128]{1,0:T(8,128)S(1)}, f32[1024,128]{1,0:T(8,128)S(1)}, u32[]{:S(2)}, u32[]{:S(2)}) collective-permute-start(f32[1024,128]{1,0:T(8,128)S(1)} %payload.18.refs_2_), channel_id=1, source_target_pairs={{1,3},{2,4},{5,7},{3,1},{4,2},{7,5},{9,11},{10,12},{13,15},{11,9},... | collective-permute-start | bytes 1572872 | tf_op jit(solution)/shard_map/ppermute | solution.py:463
  80.1 15.2 %collective-permute-start.24 = (f32[1024,128]{1,0:T(8,128)S(1)}, f32[1024,128]{1,0:T(8,128)S(1)}, u32[]{:S(2)}, u32[]{:S(2)}) collective-permute-start(f32[1024,128]{1,0:T(8,128)S(1)} %payload.19.refs_2_), channel_id=1, source_target_pairs={{0,2},{3,5},{4,6},{2,0},{5,3},{6,4},{8,10},{11,13},{12,14},{10,8},... | collective-permute-start | bytes 1572872 | tf_op jit(solution)/shard_map/ppermute | solution.py:463
  84.6 15.0 %collective-permute-start.29 = (f32[1024,128]{1,0:T(8,128)S(1)}, f32[1024,128]{1,0:T(8,128)S(1)}, u32[]{:S(2)}, u32[]{:S(2)}) collective-permute-start(f32[1024,128]{1,0:T(8,128)S(1)} %get-tuple-element.69.refs_2_), channel_id=1, source_target_pairs={{0,1},{1,0},{2,3},{3,2},{4,5},{5,4},{6,7},{7,6},{8,9},{9,8},{10,11... | collective-permute-start | bytes 1572872 | tf_op jit(solution)/shard_map/ppermute | solution.py:460
  87.9 13.7 %collective-permute-start.34 = (f32[1024,128]{1,0:T(8,128)S(1)}, f32[1024,128]{1,0:T(8,128)S(1)}, u32[]{:S(2)}, u32[]{:S(2)}) collective-permute-start(f32[1024,128]{1,0:T(8,128)S(1)} %get-tuple-element.70.refs_8_), channel_id=1, source_target_pairs={{0,1},{1,0},{2,3},{3,2},{4,5},{5,4},{6,7},{7,6},{8,9},{9,8},{10,11... | collective-permute-start | bytes 1572872 | tf_op jit(solution)/shard_map/ppermute | solution.py:460
  90.5 1.4 %collective-permute-start.26 = (f32[2,256]{1,0:T(2,128)S(1)}, f32[2,256]{1,0:T(2,128)S(1)}, u32[]{:S(2)}, u32[]{:S(2)}) collective-permute-start(f32[2,256]{1,0:T(2,128)S(1)} %get-tuple-element.71.refs_3_.refs_0_), channel_id=1, source_target_pairs={{0,1},{1,0},{2,3},{3,2},{4,5},{5,4},{6,7},{7,6},{8,9},{9,8},{10,11... | collective-permute-start | bytes 6152 | tf_op jit(solution)/shard_map/ppermute | solution.py:661
  91.9 10.2 %collective-permute-start.38 = (f32[1024,128]{1,0:T(8,128)S(1)}, f32[1024,128]{1,0:T(8,128)S(1)}, u32[]{:S(2)}, u32[]{:S(2)}) collective-permute-start(f32[1024,128]{1,0:T(8,128)S(1)} %get-tuple-element.61.refs_2_.refs_1_), channel_id=1, source_target_pairs={{0,1},{1,0},{2,3},{3,2},{4,5},{5,4},{6,7},{7,6},{8,9},{9,8},{10,11... | collective-permute-start | bytes 1572872 | tf_op jit(solution)/shard_map/ppermute | solution.py:460
  92.3 10.1 %collective-permute-start.37 = (f32[1024,128]{1,0:T(8,128)S(1)}, f32[1024,128]{1,0:T(8,128)S(1)}, u32[]{:S(2)}, u32[]{:S(2)}) collective-permute-start(f32[1024,128]{1,0:T(8,128)S(1)} %pick.9.refs_2_.refs_1_), channel_id=1, source_target_pairs={{0,1},{1,0},{2,3},{3,2},{4,5},{5,4},{6,7},{7,6},{8,9},{9,8},{10,11... | collective-permute-start | bytes 1572872 | tf_op jit(solution)/shard_map/ppermute | solution.py:460
  95.3 14.3 %collective-permute-start.33 = (f32[1024,128]{1,0:T(8,128)S(1)}, f32[1024,128]{1,0:T(8,128)S(1)}, u32[]{:S(2)}, u32[]{:S(2)}) collective-permute-start(f32[1024,128]{1,0:T(8,128)S(1)} %payload.20.refs_2_), channel_id=1, source_target_pairs={{0,2},{3,5},{4,6},{2,0},{5,3},{6,4},{8,10},{11,13},{12,14},{10,8},... | collective-permute-start | bytes 1572872 | tf_op jit(solution)/shard_map/ppermute | solution.py:463
  99.6 14.4 %collective-permute-start.28 = (f32[1024,128]{1,0:T(8,128)S(1)}, f32[1024,128]{1,0:T(8,128)S(1)}, u32[]{:S(2)}, u32[]{:S(2)}) collective-permute-start(f32[1024,128]{1,0:T(8,128)S(1)} %payload.21.refs_2_), channel_id=1, source_target_pairs={{1,3},{2,4},{5,7},{3,1},{4,2},{7,5},{9,11},{10,12},{13,15},{11,9},... | collective-permute-start | bytes 1572872 | tf_op jit(solution)/shard_map/ppermute | solution.py:463
  101.8 1.6 %collective-permute-start.36 = (f32[512,128]{1,0:T(8,128)S(1)}, f32[512,128]{1,0:T(8,128)S(1)}, u32[]{:S(2)}, u32[]{:S(2)}) collective-permute-start(f32[512,128]{1,0:T(8,128)S(1)} %get-tuple-element.84), channel_id=1, source_target_pairs={{0,1},{1,0},{2,3},{3,2},{4,5},{5,4},{6,7},{7,6},{8,9},{9,8},{10,11... | collective-permute-start | bytes 786440 | tf_op jit(solution)/shard_map/ppermute | solution.py:460
  102.1 3.8 %collective-permute-start.35 = (f32[512,128]{1,0:T(8,128)S(1)}, f32[512,128]{1,0:T(8,128)S(1)}, u32[]{:S(2)}, u32[]{:S(2)}) collective-permute-start(f32[512,128]{1,0:T(8,128)S(1)} %get-tuple-element.85), channel_id=1, source_target_pairs={{0,1},{1,0},{2,3},{3,2},{4,5},{5,4},{6,7},{7,6},{8,9},{9,8},{10,11... | collective-permute-start | bytes 786440 | tf_op jit(solution)/shard_map/ppermute | solution.py:460
  102.3 9.3 %collective-permute-start.32 = (f32[2,256]{1,0:T(2,128)S(1)}, f32[2,256]{1,0:T(2,128)S(1)}, u32[]{:S(2)}, u32[]{:S(2)}) collective-permute-start(f32[2,256]{1,0:T(2,128)S(1)} %get-tuple-element.74.refs_0_), channel_id=1, source_target_pairs={{0,6},{1,7},{2,4},{3,5},{4,2},{5,3},{6,0},{7,1},{8,14},{9,15},{10,... | collective-permute-start | bytes 6152 | tf_op jit(solution)/shard_map/ppermute | solution.py:661
  103.4 10.0 %collective-permute-start.31 = (f32[2,256]{1,0:T(2,128)S(1)}, f32[2,256]{1,0:T(2,128)S(1)}, u32[]{:S(2)}, u32[]{:S(2)}) collective-permute-start(f32[2,256]{1,0:T(2,128)S(1)} %get-tuple-element.74.refs_0_), channel_id=1, source_target_pairs={{0,4},{1,5},{2,6},{3,7},{4,0},{5,1},{6,2},{7,3},{8,12},{9,13},{10,... | collective-permute-start | bytes 6152 | tf_op jit(solution)/shard_map/ppermute | solution.py:661
  105.9 7.5 %collective-permute-start.30 = (f32[2,256]{1,0:T(2,128)S(1)}, f32[2,256]{1,0:T(2,128)S(1)}, u32[]{:S(2)}, u32[]{:S(2)}) collective-permute-start(f32[2,256]{1,0:T(2,128)S(1)} %get-tuple-element.74.refs_0_), channel_id=1, source_target_pairs={{0,2},{1,3},{2,0},{3,1},{4,6},{5,7},{6,4},{7,5},{8,10},{9,11},{10,... | collective-permute-start | bytes 6152 | tf_op jit(solution)/shard_map/ppermute | solution.py:661
  109.7 12.2 %collective-permute-start.40 = (f32[1024,128]{1,0:T(8,128)S(1)}, f32[1024,128]{1,0:T(8,128)S(1)}, u32[]{:S(2)}, u32[]{:S(2)}) collective-permute-start(f32[1024,128]{1,0:T(8,128)S(1)} %payload.22.refs_4_), channel_id=1, source_target_pairs={{1,3},{2,4},{5,7},{3,1},{4,2},{7,5},{9,11},{10,12},{13,15},{11,9},... | collective-permute-start | bytes 1572872 | tf_op jit(solution)/shard_map/ppermute | solution.py:463
  114.0 12.9 %collective-permute-start.39 = (f32[1024,128]{1,0:T(8,128)S(1)}, f32[1024,128]{1,0:T(8,128)S(1)}, u32[]{:S(2)}, u32[]{:S(2)}) collective-permute-start(f32[1024,128]{1,0:T(8,128)S(1)} %payload.23.refs_4_), channel_id=1, source_target_pairs={{0,2},{3,5},{4,6},{2,0},{5,3},{6,4},{8,10},{11,13},{12,14},{10,8},... | collective-permute-start | bytes 1572872 | tf_op jit(solution)/shard_map/ppermute | solution.py:463
  116.6 4.0 %collective-permute-start.42 = (f32[512,128]{1,0:T(8,128)S(1)}, f32[512,128]{1,0:T(8,128)S(1)}, u32[]{:S(2)}, u32[]{:S(2)}) collective-permute-start(f32[512,128]{1,0:T(8,128)S(1)} %get-tuple-element.82), channel_id=1, source_target_pairs={{0,1},{1,0},{2,3},{3,2},{4,5},{5,4},{6,7},{7,6},{8,9},{9,8},{10,11... | collective-permute-start | bytes 786440 | tf_op jit(solution)/shard_map/ppermute | solution.py:460
  117.8 2.7 %collective-permute-start.41 = (f32[512,128]{1,0:T(8,128)S(1)}, f32[512,128]{1,0:T(8,128)S(1)}, u32[]{:S(2)}, u32[]{:S(2)}) collective-permute-start(f32[512,128]{1,0:T(8,128)S(1)} %get-tuple-element.83), channel_id=1, source_target_pairs={{0,1},{1,0},{2,3},{3,2},{4,5},{5,4},{6,7},{7,6},{8,9},{9,8},{10,11... | collective-permute-start | bytes 786440 | tf_op jit(solution)/shard_map/ppermute | solution.py:460

commit v17 on v16

--- a/solution.py
+++ b/solution.py
@@ -191,7 +191,7 @@
 
     @pl.when(slot_here < 0)
     def _():
-        out[...] = arrived[...]
+        out[...] = arrived[: out.shape[0]]
 
 
 def pick(numbers, *refs):
@@ -237,15 +237,19 @@
     strip[...] = value.T[-HALO:]
 
 
-def last_sum(scale, arrived, base, other, out, value, sems):
+def last_sum(scale, arrived, base, other, flux, out, flux_out, value, sems):
     cells = base.shape[1]
-    ahead = pltpu.make_async_copy(other, out.at[:, pl.ds(cells, cells)], sems.at[0])
-    ahead.start()
+    copies = [
+        pltpu.make_async_copy(other, out.at[:, pl.ds(cells, cells)], sems.at[0]),
+        pltpu.make_async_copy(flux, flux_out, sems.at[1]),
+    ]
+    for copy in copies:
+        copy.start()
     value[...] = base[...] - scale * arrived[...]
-    copy = pltpu.make_async_copy(value, out.at[:, pl.ds(0, cells)], sems.at[1])
-    copy.start()
-    ahead.wait()
-    copy.wait()
+    copies.append(pltpu.make_async_copy(value, out.at[:, pl.ds(0, cells)], sems.at[2]))
+    copies[-1].start()
+    for copy in copies:
+        copy.wait()
 
 
 def strip_rows(distribution, leading, last):
@@ -498,7 +502,8 @@
                 arrived = self.arrived[1 - stream][step - 1]
                 kernel = functools.partial(payload, numbers, slots)
                 arrays = [arrived] + [self.terms[s] for s in slots]
-                (value,) = call(kernel, [arrived.shape], arrays)
+                shape = part if step == chips - 1 else arrived.shape
+                (value,) = call(kernel, [shape], arrays)
                 sent[stream] = along(stream, value)
             for stream in (0, 1):
                 self.arrived[stream].append(sent[stream])
@@ -640,14 +645,13 @@
             )
             flux = Flux(call, part_flux, devices)
     (last_b,) = two.multiply(chips - 1, end_b)
-    heat_flux = flux.value
     two.first_end(end_a)
-    (updated,) = call(
+    updated, heat_flux = call(
         functools.partial(last_sum, step_size),
-        [(modes, cells)],
-        [*two.ends(), last_b],
-        scratch=[pltpu.VMEM(part, jnp.float32), pltpu.SemaphoreType.DMA((2,))],
-        out_specs=[HBM],
+        [(modes, cells), (2, cells)],
+        [*two.ends(), last_b, flux.value],
+        scratch=[pltpu.VMEM(part, jnp.float32), pltpu.SemaphoreType.DMA((3,))],
+        out_specs=[HBM, HBM],
     )
     return (updated, heat_flux)
 

time: 129 us -> 129 us (level)
  transfers between devices with their start and end apart: 43 -> 43, of which waited for: 13 -> 13; matrix products, arithmetic and copies ran while one was open for 0% -> 0% of each run, Pallas kernels for 25% -> 24%
where the time goes in v17:
time: 129 us; the launch traced here: 128 us
  starting transfers between devices  68.3 us (53%)
  Pallas kernels  33.9 us (26%)
  waiting for transfers between devices  23.2 us (18%)
  between operations  1.61 us (1%)
    ppermute x16, starting transfers between devices, along(): return lax.ppermute(value, 'mode', plan.pairs[stream])  45 us
    pallas_call x56, Pallas kernels, __call__(): pl.pallas_call(body, out_shape=[jax.ShapeDtypeStruct(shape, jnp.float32)...  33.9 us
    ppermute x16, waiting for transfers between devices, along(): return lax.ppermute(value, 'mode', plan.pairs[stream])  17.9 us
    ppermute x19, starting transfers between devices, exchange(): lax.ppermute(value[i:j], 'mode', across)  13.5 us
    ppermute x4, starting transfers between devices, paired(): lax.ppermute(value, 'space', pairs + [(j, i) for i, j in pairs])  6.73 us
    ppermute x4, starting transfers between devices, over(): lax.ppermute(self.value, 'mode', [(i, i ^ bit) for i in range(self.device...  3.12 us
  transfers between devices with their start and end apart: 43, of which 13 were waited for; matrix products, arithmetic and copies ran while one was open for 0% of the time, Pallas kernels for 24%

profile of v17, /device:TPU:13, one launch (start us, length us, event | category | flops | bytes accessed | tf_op | source)
XLA Modules:
  0.0 127.9 jit_solution(11433990834480203706)
XLA Ops:
  0.6 2.0 %own_rows.1 = (f32[1040,128]{1,0:T(8,128)}, f32[8,128]{1,0:T(8,128)}) custom-call(f32[1024,256]{1,0:T(8,128)} %refs_0_.9, f32[2,1024]{1,0:T(2,128)} %refs_1_.3, f32[1,1024]{1,0:T(1,128)} %bitcast.4), custom_call_target="tpu_custom_call" | custom-call | flops 1024 | bytes 1024 | tf_op jit(solution)/shard_map/own_rows/pallas_call | solution.py:39
  2.6 3.2 %collective-permute-start.2 = (f32[1040,128]{1,0:T(8,128)}, f32[1040,128]{1,0:T(8,128)S(1)}, u32[]{:S(2)}, u32[]{:S(2)}) collective-permute-start(f32[1040,128]{1,0:T(8,128)} %get-tuple-element.41.refs_1_), channel_id=1, source_target_pairs={{0,2},{3,5},{4,6},{2,0},{5,3},{6,4},{8,10},{11,13},{12,14},{10,8},... | collective-permute-start | bytes 1597448 | tf_op jit(solution)/shard_map/ppermute | solution.py:467
  5.8 1.9 %collective-permute-start = (f32[1040,128]{1,0:T(8,128)}, f32[1040,128]{1,0:T(8,128)S(1)}, u32[]{:S(2)}, u32[]{:S(2)}) collective-permute-start(f32[1040,128]{1,0:T(8,128)} %get-tuple-element.41.refs_1_), channel_id=1, source_target_pairs={{1,3},{2,4},{5,7},{3,1},{4,2},{7,5},{9,11},{10,12},{13,15},{11,9},... | collective-permute-start | bytes 1597448 | tf_op jit(solution)/shard_map/ppermute | solution.py:467
  7.8 0.7 copy-done.3
  8.5 6.2 %load_and_products.1 = (f32[1024,128]{1,0:T(8,128)S(1)}, f32[1024,128]{1,0:T(8,128)S(1)}, f32[1024,128]{1,0:T(8,128)S(1)}, f32[1024,128]{1,0:T(8,128)S(1)}, f32[...) custom-call(bf16[8192,1024]{1,0:T(8,128)(2,1)} %refs_0_.6, f32[1024,256]{1,0:T(8,128)S(1)} %copy-done, ...), custom_call_target="tpu_custom_call" | custom-call | flops 1024 | bytes 1024 | tf_op jit(solution)/shard_map/load_and_products/pallas_call | solution.py:39
  14.6 2.6 %collective-permute-start.1 = (f32[1024,128]{1,0:T(8,128)S(1)}, f32[1024,128]{1,0:T(8,128)S(1)}, u32[]{:S(2)}, u32[]{:S(2)}) collective-permute-start(f32[1024,128]{1,0:T(8,128)S(1)} %get-tuple-element.44), channel_id=1, source_target_pairs={{0,1},{1,0},{2,3},{3,2},{4,5},{5,4},{6,7},{7,6},{8,9},{9,8},{10,11... | collective-permute-start | bytes 1572872 | tf_op jit(solution)/shard_map/ppermute | solution.py:464
  17.3 0.4 collective-permute-start.5
  17.7 0.5 collective-permute-start.9
  18.2 1.5 %collective-permute-done.refs_1_.refs_0_ = f32[1040,128]{1,0:T(8,128)S(1)} collective-permute-done((f32[1040,128]{1,0:T(8,128)}, f32[1040,128]{1,0:T(8,128)S(1)}, u32[]{:S(2)}, u32[]{:S(2)}) %collective-permute-start) | collective-permute-done | bytes 532512 | tf_op jit(solution)/shard_map/ppermute | solution.py:467
  19.9 2.1 %collective-permute-start.8 = (f32[1040,128]{1,0:T(8,128)S(1)}, f32[1040,128]{1,0:T(8,128)S(1)}, u32[]{:S(2)}, u32[]{:S(2)}) collective-permute-start(f32[1040,128]{1,0:T(8,128)S(1)} %payload.12.refs_2_), channel_id=1, source_target_pairs={{1,3},{2,4},{5,7},{3,1},{4,2},{7,5},{9,11},{10,12},{13,15},{11,9},... | collective-permute-start | bytes 1597448 | tf_op jit(solution)/shard_map/ppermute | solution.py:467
  22.0 4.7 %collective-permute-start.3 = (f32[1040,128]{1,0:T(8,128)S(1)}, f32[1040,128]{1,0:T(8,128)S(1)}, u32[]{:S(2)}, u32[]{:S(2)}) collective-permute-start(f32[1040,128]{1,0:T(8,128)S(1)} %payload.13.refs_2_), channel_id=1, source_target_pairs={{0,2},{3,5},{4,6},{2,0},{5,3},{6,4},{8,10},{11,13},{12,14},{10,8},... | collective-permute-start | bytes 1597448 | tf_op jit(solution)/shard_map/ppermute | solution.py:467
  26.9 0.3 strip_rows.1
  27.3 1.3 collective-permute-start.6
  28.6 2.1 %collective-permute-start.7 = (f32[32,1024]{1,0:T(8,128)S(1)}, f32[32,1024]{1,0:T(8,128)S(1)}, u32[]{:S(2)}, u32[]{:S(2)}) collective-permute-start(f32[32,1024]{1,0:T(8,128)S(1)} %get-tuple-element.53.refs_3_), channel_id=1, source_target_pairs={{8,16},{16,8},{9,17},{17,9},{10,18},{18,10},{11,19},{19,11},{12,20... | collective-permute-start | bytes 393224 | tf_op jit(solution)/shard_map/ppermute | solution.py:378
  30.7 1.4 %two_blocks.8.refs_3_ = f32[272,1024]{1,0:T(8,128)S(1)} custom-call(bf16[8192,1024]{1,0:T(8,128)(2,1)S(1)} %get-tuple-element.45.refs_2_.refs_0_, f32[1040,128]{1,0:T(8,128)S(1)} %copy-done.2, f32[1040,128]{1,0:T(8,128)S(1)} %collective-permute-done.9.refs_2_, f32[32,1024]{1,0:T(8,128)S(1)} %get-tuple-element.53.refs_3_), custom_call_target="tpu_custom_call" | custom-call | flops 1024 | bytes 1024 | tf_op jit(solution)/shard_map/two_blocks/pallas_call | solution.py:39
  32.2 5.1 %collective-permute-start.11 = (f32[1040,128]{1,0:T(8,128)S(1)}, f32[1040,128]{1,0:T(8,128)S(1)}, u32[]{:S(2)}, u32[]{:S(2)}) collective-permute-start(f32[1040,128]{1,0:T(8,128)S(1)} %payload.14.refs_2_), channel_id=1, source_target_pairs={{0,2},{3,5},{4,6},{2,0},{5,3},{6,4},{8,10},{11,13},{12,14},{10,8},... | collective-permute-start | bytes 1597448 | tf_op jit(solution)/shard_map/ppermute | solution.py:467
  37.6 1.9 %collective-permute-start.10 = (f32[1040,128]{1,0:T(8,128)S(1)}, f32[1040,128]{1,0:T(8,128)S(1)}, u32[]{:S(2)}, u32[]{:S(2)}) collective-permute-start(f32[1040,128]{1,0:T(8,128)S(1)} %payload.15.refs_3_), channel_id=1, source_target_pairs={{1,3},{2,4},{5,7},{3,1},{4,2},{7,5},{9,11},{10,12},{13,15},{11,9},... | collective-permute-start | bytes 1597448 | tf_op jit(solution)/shard_map/ppermute | solution.py:467
  39.6 1.3 slot_products.5
  40.9 0.6 collective-permute-start.15
  41.7 1.4 %two_blocks.9.refs_5_.refs_3_ = f32[272,1024]{1,0:T(8,128)S(1)} custom-call(bf16[8192,1024]{1,0:T(8,128)(2,1)S(1)} %get-tuple-element.45.refs_2_.refs_0_, f32[1040,128]{1,0:T(8,128)S(1)} %pick.6.refs_2_.refs_1_, f32[1040,128]{1,0:T(8,128)S(1)} %collective-permute-done.12.refs_2_, f32[272,1024]{1,0:T(8,128)S(1)} %two_blocks.8.refs_3_, ...), custom_call_target="tpu_custom_call" | custom-call | flops 1024 | bytes 1024 | tf_op jit(solution)/shard_map/two_blocks/pallas_call | solution.py:39
  43.1 2.0 %first_rest.1 = (f32[1024,128]{1,0:T(8,128)S(1)}, f32[1024,128]{1,0:T(8,128)S(1)}) custom-call(f32[1024,256]{1,0:T(8,128)S(1)} %copy-done, bf16[1024,128]{1,0:T(8,128)(2,1)S(1)} %strip_columns.2.refs_3_.refs_1_, bf16[640,1024]{1,0:T(8,128)(2,1)S(1)} %copy-done.1, f32[8,1024]{1,0:T(8,128)S(1)} %maximum_maximum_fusion.refs_3_.refs_5_, s32[1,256]{1,0:T(1,128)S(1)} %bitcast.2, ...), custom_call_target="tpu_custom_call" | custom-call | flops 1024 | bytes 1024 | tf_op jit(solution)/shard_map/first_rest/pallas_call | solution.py:39
  45.1 2.0 %collective-permute-done.11.refs_0_.refs_1_ = f32[1040,128]{1,0:T(8,128)S(1)} collective-permute-done((f32[1040,128]{1,0:T(8,128)S(1)}, f32[1040,128]{1,0:T(8,128)S(1)}, u32[]{:S(2)}, u32[]{:S(2)}) %collective-permute-start.11) | collective-permute-done | bytes 532512 | tf_op jit(solution)/shard_map/ppermute | solution.py:467
  47.2 1.9 %collective-permute-start.14 = (f32[1024,128]{1,0:T(8,128)S(1)}, f32[1024,128]{1,0:T(8,128)S(1)}, u32[]{:S(2)}, u32[]{:S(2)}) collective-permute-start(f32[1024,128]{1,0:T(8,128)S(1)} %payload.16.refs_3_), channel_id=1, source_target_pairs={{1,3},{2,4},{5,7},{3,1},{4,2},{7,5},{9,11},{10,12},{13,15},{11,9},... | collective-permute-start | bytes 1572872 | tf_op jit(solution)/shard_map/ppermute | solution.py:467
  49.3 3.5 %collective-permute-start.13 = (f32[1024,128]{1,0:T(8,128)S(1)}, f32[1024,128]{1,0:T(8,128)S(1)}, u32[]{:S(2)}, u32[]{:S(2)}) collective-permute-start(f32[1024,128]{1,0:T(8,128)S(1)} %payload.17.refs_4_), channel_id=1, source_target_pairs={{0,2},{3,5},{4,6},{2,0},{5,3},{6,4},{8,10},{11,13},{12,14},{10,8},... | collective-permute-start | bytes 1572872 | tf_op jit(solution)/shard_map/ppermute | solution.py:467
  53.2 0.5 collective-permute-start.16
  53.8 1.4 %two_blocks.10.refs_4_.refs_6_ = f32[272,1024]{1,0:T(8,128)S(1)} custom-call(bf16[8192,1024]{1,0:T(8,128)(2,1)S(1)} %get-tuple-element.45.refs_2_.refs_0_, f32[1040,128]{1,0:T(8,128)S(1)} %pick.7.refs_2_.refs_1_, f32[1040,128]{1,0:T(8,128)S(1)} %collective-permute-done.18.refs_2_, f32[272,1024]{1,0:T(8,128)S(1)} %two_blocks.9.refs_5_.refs_3_, ...), custom_call_target="tpu_custom_call" | custom-call | flops 1024 | bytes 1024 | tf_op jit(solution)/shard_map/two_blocks/pallas_call | solution.py:39
  55.2 1.5 %two_blocks.11 = (f32[1024,128]{1,0:T(8,128)S(1)}, f32[32,1024]{1,0:T(8,128)S(1)}, f32[8,1024]{1,0:T(8,128)S(1)}) custom-call(bf16[8192,1024]{1,0:T(8,128)(2,1)S(1)} %get-tuple-element.45.refs_2_.refs_0_, f32[1040,128]{1,0:T(8,128)S(1)} %pick.8.refs_2_.refs_1_, f32[520,128]{1,0:T(8,128)S(1)} %collective-permute-done.16.refs_2_, ...), custom_call_target="tpu_custom_call" | custom-call | flops 1024 | bytes 1024 | tf_op jit(solution)/shard_map/two_blocks/pallas_call | solution.py:39
  56.7 1.3 slot_products.6
  58.1 0.8 collective-permute-done.14.refs_0_
  59.0 4.0 %collective-permute-done.13.refs_0_ = f32[1024,128]{1,0:T(8,128)S(1)} collective-permute-done((f32[1024,128]{1,0:T(8,128)S(1)}, f32[1024,128]{1,0:T(8,128)S(1)}, u32[]{:S(2)}, u32[]{:S(2)}) %collective-permute-start.13) | collective-permute-done | bytes 524320 | tf_op jit(solution)/shard_map/ppermute | solution.py:467
  63.2 3.3 %collective-permute-start.23 = (f32[1024,128]{1,0:T(8,128)S(1)}, f32[1024,128]{1,0:T(8,128)S(1)}, u32[]{:S(2)}, u32[]{:S(2)}) collective-permute-start(f32[1024,128]{1,0:T(8,128)S(1)} %get-tuple-element.61.refs_2_.refs_1_), channel_id=1, source_target_pairs={{0,2},{3,5},{4,6},{2,0},{5,3},{6,4},{8,10},{11,13},{12,14},{10,8},... | collective-permute-start | bytes 1572872 | tf_op jit(solution)/shard_map/ppermute | solution.py:467
  66.6 1.9 %collective-permute-start.19 = (f32[1024,128]{1,0:T(8,128)S(1)}, f32[1024,128]{1,0:T(8,128)S(1)}, u32[]{:S(2)}, u32[]{:S(2)}) collective-permute-start(f32[1024,128]{1,0:T(8,128)S(1)} %get-tuple-element.61.refs_2_.refs_1_), channel_id=1, source_target_pairs={{1,3},{2,4},{5,7},{3,1},{4,2},{7,5},{9,11},{10,12},{13,15},{11,9},... | collective-permute-start | bytes 1572872 | tf_op jit(solution)/shard_map/ppermute | solution.py:467
  68.5 1.3 slot_products.7
  69.8 1.0 collective-permute-start.25
  70.9 1.3 collective-permute-start.21
  72.2 2.1 %collective-permute-start.22 = (f32[32,1024]{1,0:T(8,128)S(1)}, f32[32,1024]{1,0:T(8,128)S(1)}, u32[]{:S(2)}, u32[]{:S(2)}) collective-permute-start(f32[32,1024]{1,0:T(8,128)S(1)} %get-tuple-element.67.refs_2_), channel_id=1, source_target_pairs={{8,16},{16,8},{9,17},{17,9},{10,18},{18,10},{11,19},{19,11},{12,20... | collective-permute-start | bytes 393224 | tf_op jit(solution)/shard_map/ppermute | solution.py:378
  74.3 1.7 %collective-permute-done.23.refs_0_ = f32[1024,128]{1,0:T(8,128)S(1)} collective-permute-done((f32[1024,128]{1,0:T(8,128)S(1)}, f32[1024,128]{1,0:T(8,128)S(1)}, u32[]{:S(2)}, u32[]{:S(2)}) %collective-permute-start.23) | collective-permute-done | bytes 524320 | tf_op jit(solution)/shard_map/ppermute | solution.py:467
  76.0 1.9 %collective-permute-start.27 = (f32[1024,128]{1,0:T(8,128)S(1)}, f32[1024,128]{1,0:T(8,128)S(1)}, u32[]{:S(2)}, u32[]{:S(2)}) collective-permute-start(f32[1024,128]{1,0:T(8,128)S(1)} %payload.18.refs_2_), channel_id=1, source_target_pairs={{1,3},{2,4},{5,7},{3,1},{4,2},{7,5},{9,11},{10,12},{13,15},{11,9},... | collective-permute-start | bytes 1572872 | tf_op jit(solution)/shard_map/ppermute | solution.py:467
  77.9 1.8 %collective-permute-done.22.refs_1_ = f32[32,1024]{1,0:T(8,128)S(1)} collective-permute-done((f32[32,1024]{1,0:T(8,128)S(1)}, f32[32,1024]{1,0:T(8,128)S(1)}, u32[]{:S(2)}, u32[]{:S(2)}) %collective-permute-start.22) | collective-permute-done | bytes 131104 | tf_op jit(solution)/shard_map/ppermute | solution.py:378
  80.0 3.0 %collective-permute-start.24 = (f32[1024,128]{1,0:T(8,128)S(1)}, f32[1024,128]{1,0:T(8,128)S(1)}, u32[]{:S(2)}, u32[]{:S(2)}) collective-permute-start(f32[1024,128]{1,0:T(8,128)S(1)} %payload.19.refs_2_), channel_id=1, source_target_pairs={{0,2},{3,5},{4,6},{2,0},{5,3},{6,4},{8,10},{11,13},{12,14},{10,8},... | collective-permute-start | bytes 1572872 | tf_op jit(solution)/shard_map/ppermute | solution.py:467
  83.1 1.3 slot_products.8
  84.4 2.1 %collective-permute-start.29 = (f32[1024,128]{1,0:T(8,128)S(1)}, f32[1024,128]{1,0:T(8,128)S(1)}, u32[]{:S(2)}, u32[]{:S(2)}) collective-permute-start(f32[1024,128]{1,0:T(8,128)S(1)} %get-tuple-element.69.refs_2_), channel_id=1, source_target_pairs={{0,1},{1,0},{2,3},{3,2},{4,5},{5,4},{6,7},{7,6},{8,9},{9,8},{10,11... | collective-permute-start | bytes 1572872 | tf_op jit(solution)/shard_map/ppermute | solution.py:464
  86.5 1.2 slot_products.9
  87.8 2.5 %second_rest.1 = (f32[1024,128]{1,0:T(8,128)S(1)}, f32[1024,128]{1,0:T(8,128)S(1)}, f32[2,256]{1,0:T(2,128)S(1)}) custom-call(f32[1024,256]{1,0:T(8,128)S(1)} %copy-done, f32[1024,128]{1,0:T(8,128)S(1)} %get-tuple-element.58.refs_1_, f32[1024,128]{1,0:T(8,128)S(1)} %get-tuple-element.61.refs_2_.refs_1_, bf16[1024,128]{1,0:T(8,128)(2,1)S(1)} %strip_columns.3.refs_2_.refs_3_, ...), custom_call_target="tpu_custom_call" | custom-call | flops 1024 | bytes 1024 | tf_op jit(solution)/shard_map/second_rest/pallas_call | solution.py:39
  90.4 0.6 collective-permute-start.26
  90.9 0.8 collective-permute-done.26.refs_1_
  91.7 0.3 collective-permute-start.38
  92.1 3.0 %collective-permute-start.37 = (f32[1024,128]{1,0:T(8,128)S(1)}, f32[1024,128]{1,0:T(8,128)S(1)}, u32[]{:S(2)}, u32[]{:S(2)}) collective-permute-start(f32[1024,128]{1,0:T(8,128)S(1)} %pick.9.refs_2_.refs_1_), channel_id=1, source_target_pairs={{0,1},{1,0},{2,3},{3,2},{4,5},{5,4},{6,7},{7,6},{8,9},{9,8},{10,11... | collective-permute-start | bytes 1572872 | tf_op jit(solution)/shard_map/ppermute | solution.py:464
  95.2 4.1 %collective-permute-start.33 = (f32[1024,128]{1,0:T(8,128)S(1)}, f32[1024,128]{1,0:T(8,128)S(1)}, u32[]{:S(2)}, u32[]{:S(2)}) collective-permute-start(f32[1024,128]{1,0:T(8,128)S(1)} %payload.20.refs_2_), channel_id=1, source_target_pairs={{0,2},{3,5},{4,6},{2,0},{5,3},{6,4},{8,10},{11,13},{12,14},{10,8},... | collective-permute-start | bytes 1572872 | tf_op jit(solution)/shard_map/ppermute | solution.py:467
  99.4 1.9 %collective-permute-start.28 = (f32[1024,128]{1,0:T(8,128)S(1)}, f32[1024,128]{1,0:T(8,128)S(1)}, u32[]{:S(2)}, u32[]{:S(2)}) collective-permute-start(f32[1024,128]{1,0:T(8,128)S(1)} %payload.21.refs_2_), channel_id=1, source_target_pairs={{1,3},{2,4},{5,7},{3,1},{4,2},{7,5},{9,11},{10,12},{13,15},{11,9},... | collective-permute-start | bytes 1572872 | tf_op jit(solution)/shard_map/ppermute | solution.py:467
  101.6 0.3 collective-permute-start.36
  102.2 1.0 collective-permute-done.36.refs_3_
  103.2 2.5 %collective-permute-start.31 = (f32[2,256]{1,0:T(2,128)S(1)}, f32[2,256]{1,0:T(2,128)S(1)}, u32[]{:S(2)}, u32[]{:S(2)}) collective-permute-start(f32[2,256]{1,0:T(2,128)S(1)} %get-tuple-element.74.refs_0_), channel_id=1, source_target_pairs={{0,4},{1,5},{2,6},{3,7},{4,0},{5,1},{6,2},{7,3},{8,12},{9,13},{10,... | collective-permute-start | bytes 6152 | tf_op jit(solution)/shard_map/ppermute | solution.py:665
  105.8 1.3 %two_blocks.12.refs_3_ = f32[256,1024]{1,0:T(8,128)S(1)} custom-call(bf16[8192,1024]{1,0:T(8,128)(2,1)S(1)} %get-tuple-element.45.refs_2_.refs_0_, f32[1024,128]{1,0:T(8,128)S(1)} %pick.10.refs_1_, f32[512,128]{1,0:T(8,128)S(1)} %collective-permute-done.35.refs_2_, f32[512,128]{1,0:T(8,128)S(1)} %collective-permute-done.36.refs_3_, ...), custom_call_target="tpu_custom_call" | custom-call | flops 1024 | bytes 1024 | tf_op jit(solution)/shard_map/two_blocks/pallas_call | solution.py:39
  107.1 2.4 %collective-permute-done.33.refs_0_.refs_1_ = f32[1024,128]{1,0:T(8,128)S(1)} collective-permute-done((f32[1024,128]{1,0:T(8,128)S(1)}, f32[1024,128]{1,0:T(8,128)S(1)}, u32[]{:S(2)}, u32[]{:S(2)}) %collective-permute-start.33) | collective-permute-done | bytes 524320 | tf_op jit(solution)/shard_map/ppermute | solution.py:467
  109.6 1.9 %collective-permute-start.40 = (f32[1024,128]{1,0:T(8,128)S(1)}, f32[1024,128]{1,0:T(8,128)S(1)}, u32[]{:S(2)}, u32[]{:S(2)}) collective-permute-start(f32[1024,128]{1,0:T(8,128)S(1)} %payload.22.refs_4_), channel_id=1, source_target_pairs={{1,3},{2,4},{5,7},{3,1},{4,2},{7,5},{9,11},{10,12},{13,15},{11,9},... | collective-permute-start | bytes 1572872 | tf_op jit(solution)/shard_map/ppermute | solution.py:467
  111.5 1.7 %collective-permute-done.31.refs_2_ = f32[2,256]{1,0:T(2,128)S(1)} collective-permute-done((f32[2,256]{1,0:T(2,128)S(1)}, f32[2,256]{1,0:T(2,128)S(1)}, u32[]{:S(2)}, u32[]{:S(2)}) %collective-permute-start.31) | collective-permute-done | bytes 2080 | tf_op jit(solution)/shard_map/ppermute | solution.py:665
  113.3 2.4 %collective-permute-start.39 = (f32[1024,128]{1,0:T(8,128)S(1)}, f32[1024,128]{1,0:T(8,128)S(1)}, u32[]{:S(2)}, u32[]{:S(2)}) collective-permute-start(f32[1024,128]{1,0:T(8,128)S(1)} %payload.23.refs_4_), channel_id=1, source_target_pairs={{0,2},{3,5},{4,6},{2,0},{5,3},{6,4},{8,10},{11,13},{12,14},{10,8},... | collective-permute-start | bytes 1572872 | tf_op jit(solution)/shard_map/ppermute | solution.py:467
  115.8 1.3 %collective-permute-start.42 = (f32[512,128]{1,0:T(8,128)S(1)}, f32[512,128]{1,0:T(8,128)S(1)}, u32[]{:S(2)}, u32[]{:S(2)}) collective-permute-start(f32[512,128]{1,0:T(8,128)S(1)} %get-tuple-element.82), channel_id=1, source_target_pairs={{0,1},{1,0},{2,3},{3,2},{4,5},{5,4},{6,7},{7,6},{8,9},{9,8},{10,11... | collective-permute-start | bytes 786440 | tf_op jit(solution)/shard_map/ppermute | solution.py:464
  117.2 1.3 %two_blocks.13.refs_3_.refs_4_ = f32[256,1024]{1,0:T(8,128)S(1)} custom-call(bf16[8192,1024]{1,0:T(8,128)(2,1)S(1)} %get-tuple-element.45.refs_2_.refs_0_, f32[1024,128]{1,0:T(8,128)S(1)} %get-tuple-element.61.refs_2_.refs_1_, f32[1024,128]{1,0:T(8,128)S(1)} %pass_on.2.refs_1_.refs_2_, f32[256,1024]{1,0:T(8,128)S(1)} %two_blocks.12.refs_3_, ...), custom_call_target="tpu_custom_call" | custom-call | flops 1024 | bytes 1024 | tf_op jit(solution)/shard_map/two_blocks/pallas_call | solution.py:39
  118.5 1.3 %two_blocks.14.refs_4_.refs_6_ = f32[256,1024]{1,0:T(8,128)S(1)} custom-call(bf16[8192,1024]{1,0:T(8,128)(2,1)S(1)} %get-tuple-element.45.refs_2_.refs_0_, f32[1024,128]{1,0:T(8,128)S(1)} %pick.9.refs_2_.refs_1_, f32[1024,128]{1,0:T(8,128)S(1)} %pass_on.3.refs_4_.refs_2_, f32[256,1024]{1,0:T(8,128)S(1)} %two_blocks.13.refs_3_.refs_4_, ...), custom_call_target="tpu_custom_call" | custom-call | flops 1024 | bytes 1024 | tf_op jit(solution)/shard_map/two_blocks/pallas_call | solution.py:39
  119.8 1.4 %two_blocks.15.refs_3_.refs_2_ = f32[1024,128]{1,0:T(8,128)S(1)} custom-call(bf16[8192,1024]{1,0:T(8,128)(2,1)S(1)} %get-tuple-element.45.refs_2_.refs_0_, f32[1024,128]{1,0:T(8,128)S(1)} %pick.11.refs_4_.refs_1_, f32[512,128]{1,0:T(8,128)S(1)} %collective-permute-done.41.refs_2_, f32[512,128]{1,0:T(8,128)S(1)} %collective-permute-done.42.refs_3_, ...), custom_call_target="tpu_custom_call" | custom-call | flops 1024 | bytes 1024 | tf_op jit(solution)/shard_map/two_blocks/pallas_call | solution.py:39
  121.4 5.4 %collective-permute-done.39.refs_0_ = f32[1024,128]{1,0:T(8,128)S(1)} collective-permute-done((f32[1024,128]{1,0:T(8,128)S(1)}, f32[1024,128]{1,0:T(8,128)S(1)}, u32[]{:S(2)}, u32[]{:S(2)}) %collective-permute-start.39) | collective-permute-done | bytes 524320 | tf_op jit(solution)/shard_map/ppermute | solution.py:467
  126.7 1.0 last_sum.1
  (99 shorter events, 4.1 us)
Async XLA Ops:
  0.6 7.1 %copy-start = (f32[1024,256]{1,0:T(8,128)S(1)}, f32[1024,256]{1,0:T(8,128)}, u32[]{:S(2)}) copy-start(f32[1024,256]{1,0:T(8,128)} %refs_0_.9) | copy-start | bytes 3145732
  2.6 15.1 %collective-permute-start.2 = (f32[1040,128]{1,0:T(8,128)}, f32[1040,128]{1,0:T(8,128)S(1)}, u32[]{:S(2)}, u32[]{:S(2)}) collective-permute-start(f32[1040,128]{1,0:T(8,128)} %get-tuple-element.41.refs_1_), channel_id=1, source_target_pairs={{0,2},{3,5},{4,6},{2,0},{5,3},{6,4},{8,10},{11,13},{12,14},{10,8},... | collective-permute-start | bytes 1597448 | tf_op jit(solution)/shard_map/ppermute | solution.py:467
  5.8 13.9 %collective-permute-start = (f32[1040,128]{1,0:T(8,128)}, f32[1040,128]{1,0:T(8,128)S(1)}, u32[]{:S(2)}, u32[]{:S(2)}) collective-permute-start(f32[1040,128]{1,0:T(8,128)} %get-tuple-element.41.refs_1_), channel_id=1, source_target_pairs={{1,3},{2,4},{5,7},{3,1},{4,2},{7,5},{9,11},{10,12},{13,15},{11,9},... | collective-permute-start | bytes 1597448 | tf_op jit(solution)/shard_map/ppermute | solution.py:467
  7.8 0.7 copy-start.3
  8.5 9.3 %copy-start.2 = (f32[1040,128]{1,0:T(8,128)S(1)}, f32[1040,128]{1,0:T(8,128)}, u32[]{:S(2)}) copy-start(f32[1040,128]{1,0:T(8,128)} %get-tuple-element.41.refs_1_) | copy-start | bytes 1597444
  14.6 5.1 %collective-permute-start.1 = (f32[1024,128]{1,0:T(8,128)S(1)}, f32[1024,128]{1,0:T(8,128)S(1)}, u32[]{:S(2)}, u32[]{:S(2)}) collective-permute-start(f32[1024,128]{1,0:T(8,128)S(1)} %get-tuple-element.44), channel_id=1, source_target_pairs={{0,1},{1,0},{2,3},{3,2},{4,5},{5,4},{6,7},{7,6},{8,9},{9,8},{10,11... | collective-permute-start | bytes 1572872 | tf_op jit(solution)/shard_map/ppermute | solution.py:464
  17.2 9.5 %collective-permute-start.4 = (f32[1024,128]{1,0:T(8,128)S(1)}, f32[1024,128]{1,0:T(8,128)S(1)}, u32[]{:S(2)}, u32[]{:S(2)}) collective-permute-start(f32[1024,128]{1,0:T(8,128)S(1)} %get-tuple-element.47), channel_id=1, source_target_pairs={{0,1},{1,0},{2,3},{3,2},{4,5},{5,4},{6,7},{7,6},{8,9},{9,8},{10,11... | collective-permute-start | bytes 1572872 | tf_op jit(solution)/shard_map/ppermute | solution.py:464
  17.3 9.5 %collective-permute-start.5 = (f32[1024,128]{1,0:T(8,128)S(1)}, f32[1024,128]{1,0:T(8,128)S(1)}, u32[]{:S(2)}, u32[]{:S(2)}) collective-permute-start(f32[1024,128]{1,0:T(8,128)S(1)} %get-tuple-element.49), channel_id=1, source_target_pairs={{0,1},{1,0},{2,3},{3,2},{4,5},{5,4},{6,7},{7,6},{8,9},{9,8},{10,11... | collective-permute-start | bytes 1572872 | tf_op jit(solution)/shard_map/ppermute | solution.py:464
  17.7 12.9 %collective-permute-start.9 = (f32[1040,128]{1,0:T(8,128)S(1)}, f32[1040,128]{1,0:T(8,128)S(1)}, u32[]{:S(2)}, u32[]{:S(2)}) collective-permute-start(f32[1040,128]{1,0:T(8,128)S(1)} %copy-done.2), channel_id=1, source_target_pairs={{0,1},{1,0},{2,3},{3,2},{4,5},{5,4},{6,7},{7,6},{8,9},{9,8},{10,11... | collective-permute-start | bytes 1597448 | tf_op jit(solution)/shard_map/ppermute | solution.py:464
  19.9 12.2 %collective-permute-start.8 = (f32[1040,128]{1,0:T(8,128)S(1)}, f32[1040,128]{1,0:T(8,128)S(1)}, u32[]{:S(2)}, u32[]{:S(2)}) collective-permute-start(f32[1040,128]{1,0:T(8,128)S(1)} %payload.12.refs_2_), channel_id=1, source_target_pairs={{1,3},{2,4},{5,7},{3,1},{4,2},{7,5},{9,11},{10,12},{13,15},{11,9},... | collective-permute-start | bytes 1597448 | tf_op jit(solution)/shard_map/ppermute | solution.py:467
  22.0 15.5 %collective-permute-start.3 = (f32[1040,128]{1,0:T(8,128)S(1)}, f32[1040,128]{1,0:T(8,128)S(1)}, u32[]{:S(2)}, u32[]{:S(2)}) collective-permute-start(f32[1040,128]{1,0:T(8,128)S(1)} %payload.13.refs_2_), channel_id=1, source_target_pairs={{0,2},{3,5},{4,6},{2,0},{5,3},{6,4},{8,10},{11,13},{12,14},{10,8},... | collective-permute-start | bytes 1597448 | tf_op jit(solution)/shard_map/ppermute | solution.py:467
  27.3 10.1 %collective-permute-start.6 = (f32[32,1024]{1,0:T(8,128)S(1)}, f32[32,1024]{1,0:T(8,128)S(1)}, u32[]{:S(2)}, u32[]{:S(2)}) collective-permute-start(f32[32,1024]{1,0:T(8,128)S(1)} %get-tuple-element.52), channel_id=1, source_target_pairs={{0,8},{16,24},{8,0},{24,16},{1,9},{17,25},{9,1},{25,17},{2,10},{18... | collective-permute-start | bytes 393224 | tf_op jit(solution)/shard_map/ppermute | solution.py:378
  28.6 8.8 %collective-permute-start.7 = (f32[32,1024]{1,0:T(8,128)S(1)}, f32[32,1024]{1,0:T(8,128)S(1)}, u32[]{:S(2)}, u32[]{:S(2)}) collective-permute-start(f32[32,1024]{1,0:T(8,128)S(1)} %get-tuple-element.53.refs_3_), channel_id=1, source_target_pairs={{8,16},{16,8},{9,17},{17,9},{10,18},{18,10},{11,19},{19,11},{12,20... | collective-permute-start | bytes 393224 | tf_op jit(solution)/shard_map/ppermute | solution.py:378
  30.7 11.0 %collective-permute-start.12 = (f32[1040,128]{1,0:T(8,128)S(1)}, f32[1040,128]{1,0:T(8,128)S(1)}, u32[]{:S(2)}, u32[]{:S(2)}) collective-permute-start(f32[1040,128]{1,0:T(8,128)S(1)} %pick.6.refs_2_.refs_1_), channel_id=1, source_target_pairs={{0,1},{1,0},{2,3},{3,2},{4,5},{5,4},{6,7},{7,6},{8,9},{9,8},{10,11... | collective-permute-start | bytes 1597448 | tf_op jit(solution)/shard_map/ppermute | solution.py:464
  32.2 14.9 %collective-permute-start.11 = (f32[1040,128]{1,0:T(8,128)S(1)}, f32[1040,128]{1,0:T(8,128)S(1)}, u32[]{:S(2)}, u32[]{:S(2)}) collective-permute-start(f32[1040,128]{1,0:T(8,128)S(1)} %payload.14.refs_2_), channel_id=1, source_target_pairs={{0,2},{3,5},{4,6},{2,0},{5,3},{6,4},{8,10},{11,13},{12,14},{10,8},... | collective-permute-start | bytes 1597448 | tf_op jit(solution)/shard_map/ppermute | solution.py:467
  37.6 11.6 %collective-permute-start.10 = (f32[1040,128]{1,0:T(8,128)S(1)}, f32[1040,128]{1,0:T(8,128)S(1)}, u32[]{:S(2)}, u32[]{:S(2)}) collective-permute-start(f32[1040,128]{1,0:T(8,128)S(1)} %payload.15.refs_3_), channel_id=1, source_target_pairs={{1,3},{2,4},{5,7},{3,1},{4,2},{7,5},{9,11},{10,12},{13,15},{11,9},... | collective-permute-start | bytes 1597448 | tf_op jit(solution)/shard_map/ppermute | solution.py:467
  39.6 1.9 %copy-start.5 = (f32[2,1024]{1,0:T(2,128)S(1)}, f32[2,1024]{1,0:T(2,128)}, u32[]{:S(2)}) copy-start(f32[2,1024]{1,0:T(2,128)} %refs_1_.3) | copy-start | bytes 24580
  39.6 1.9 %copy-start.6 = (f32[1024]{0:T(1024)S(1)}, f32[1024]{0:T(1024)}, u32[]{:S(2)}) copy-start(f32[1024]{0:T(1024)} %param.9) | copy-start | bytes 12292
  40.9 12.3 %collective-permute-start.15 = (f32[1024,128]{1,0:T(8,128)S(1)}, f32[1024,128]{1,0:T(8,128)S(1)}, u32[]{:S(2)}, u32[]{:S(2)}) collective-permute-start(f32[1024,128]{1,0:T(8,128)S(1)} %get-tuple-element.54.refs_4_), channel_id=1, source_target_pairs={{0,1},{1,0},{2,3},{3,2},{4,5},{5,4},{6,7},{7,6},{8,9},{9,8},{10,11... | collective-permute-start | bytes 1572872 | tf_op jit(solution)/shard_map/ppermute | solution.py:464
  41.6 12.2 %collective-permute-start.18 = (f32[1040,128]{1,0:T(8,128)S(1)}, f32[1040,128]{1,0:T(8,128)S(1)}, u32[]{:S(2)}, u32[]{:S(2)}) collective-permute-start(f32[1040,128]{1,0:T(8,128)S(1)} %pick.7.refs_2_.refs_1_), channel_id=1, source_target_pairs={{0,1},{1,0},{2,3},{3,2},{4,5},{5,4},{6,7},{7,6},{8,9},{9,8},{10,11... | collective-permute-start | bytes 1597448 | tf_op jit(solution)/shard_map/ppermute | solution.py:464
  41.7 1.4 %copy-start.1 = (bf16[640,1024]{1,0:T(8,128)(2,1)S(1)}, bf16[640,1024]{1,0:T(8,128)(2,1)}, u32[]{:S(2)}) copy-start(bf16[640,1024]{1,0:T(8,128)(2,1)} %constant.4.clone.refs_2_.refs_4_) | copy-start | bytes 3932164
  41.7 1.4 %copy-start.4 = (s32[256]{0:T(256)S(1)}, s32[256]{0:T(256)}, u32[]{:S(2)}) copy-start(s32[256]{0:T(256)} %param.10) | copy-start | bytes 3076
  47.2 11.7 %collective-permute-start.14 = (f32[1024,128]{1,0:T(8,128)S(1)}, f32[1024,128]{1,0:T(8,128)S(1)}, u32[]{:S(2)}, u32[]{:S(2)}) collective-permute-start(f32[1024,128]{1,0:T(8,128)S(1)} %payload.16.refs_3_), channel_id=1, source_target_pairs={{1,3},{2,4},{5,7},{3,1},{4,2},{7,5},{9,11},{10,12},{13,15},{11,9},... | collective-permute-start | bytes 1572872 | tf_op jit(solution)/shard_map/ppermute | solution.py:467
  49.3 13.7 %collective-permute-start.13 = (f32[1024,128]{1,0:T(8,128)S(1)}, f32[1024,128]{1,0:T(8,128)S(1)}, u32[]{:S(2)}, u32[]{:S(2)}) collective-permute-start(f32[1024,128]{1,0:T(8,128)S(1)} %payload.17.refs_4_), channel_id=1, source_target_pairs={{0,2},{3,5},{4,6},{2,0},{5,3},{6,4},{8,10},{11,13},{12,14},{10,8},... | collective-permute-start | bytes 1572872 | tf_op jit(solution)/shard_map/ppermute | solution.py:467
  53.1 2.0 %collective-permute-start.17 = (f32[520,128]{1,0:T(8,128)S(1)}, f32[520,128]{1,0:T(8,128)S(1)}, u32[]{:S(2)}, u32[]{:S(2)}) collective-permute-start(f32[520,128]{1,0:T(8,128)S(1)} %get-tuple-element.80), channel_id=1, source_target_pairs={{0,1},{1,0},{2,3},{3,2},{4,5},{5,4},{6,7},{7,6},{8,9},{9,8},{10,11... | collective-permute-start | bytes 798728 | tf_op jit(solution)/shard_map/ppermute | solution.py:464
  53.2 2.0 %collective-permute-start.16 = (f32[520,128]{1,0:T(8,128)S(1)}, f32[520,128]{1,0:T(8,128)S(1)}, u32[]{:S(2)}, u32[]{:S(2)}) collective-permute-start(f32[520,128]{1,0:T(8,128)S(1)} %get-tuple-element.81), channel_id=1, source_target_pairs={{0,1},{1,0},{2,3},{3,2},{4,5},{5,4},{6,7},{7,6},{8,9},{9,8},{10,11... | collective-permute-start | bytes 798728 | tf_op jit(solution)/shard_map/ppermute | solution.py:464
  58.0 12.8 %collective-permute-start.20 = (f32[1024,128]{1,0:T(8,128)S(1)}, f32[1024,128]{1,0:T(8,128)S(1)}, u32[]{:S(2)}, u32[]{:S(2)}) collective-permute-start(f32[1024,128]{1,0:T(8,128)S(1)} %get-tuple-element.60.refs_3_), channel_id=1, source_target_pairs={{0,1},{1,0},{2,3},{3,2},{4,5},{5,4},{6,7},{7,6},{8,9},{9,8},{10,11... | collective-permute-start | bytes 1572872 | tf_op jit(solution)/shard_map/ppermute | solution.py:464
  63.2 12.7 %collective-permute-start.23 = (f32[1024,128]{1,0:T(8,128)S(1)}, f32[1024,128]{1,0:T(8,128)S(1)}, u32[]{:S(2)}, u32[]{:S(2)}) collective-permute-start(f32[1024,128]{1,0:T(8,128)S(1)} %get-tuple-element.61.refs_2_.refs_1_), channel_id=1, source_target_pairs={{0,2},{3,5},{4,6},{2,0},{5,3},{6,4},{8,10},{11,13},{12,14},{10,8},... | collective-permute-start | bytes 1572872 | tf_op jit(solution)/shard_map/ppermute | solution.py:467
  66.6 13.3 %collective-permute-start.19 = (f32[1024,128]{1,0:T(8,128)S(1)}, f32[1024,128]{1,0:T(8,128)S(1)}, u32[]{:S(2)}, u32[]{:S(2)}) collective-permute-start(f32[1024,128]{1,0:T(8,128)S(1)} %get-tuple-element.61.refs_2_.refs_1_), channel_id=1, source_target_pairs={{1,3},{2,4},{5,7},{3,1},{4,2},{7,5},{9,11},{10,12},{13,15},{11,9},... | collective-permute-start | bytes 1572872 | tf_op jit(solution)/shard_map/ppermute | solution.py:467
  69.8 13.2 %collective-permute-start.25 = (f32[1024,128]{1,0:T(8,128)S(1)}, f32[1024,128]{1,0:T(8,128)S(1)}, u32[]{:S(2)}, u32[]{:S(2)}) collective-permute-start(f32[1024,128]{1,0:T(8,128)S(1)} %get-tuple-element.64.refs_2_), channel_id=1, source_target_pairs={{0,1},{1,0},{2,3},{3,2},{4,5},{5,4},{6,7},{7,6},{8,9},{9,8},{10,11... | collective-permute-start | bytes 1572872 | tf_op jit(solution)/shard_map/ppermute | solution.py:464
  70.9 7.0 %collective-permute-start.21 = (f32[32,1024]{1,0:T(8,128)S(1)}, f32[32,1024]{1,0:T(8,128)S(1)}, u32[]{:S(2)}, u32[]{:S(2)}) collective-permute-start(f32[32,1024]{1,0:T(8,128)S(1)} %get-tuple-element.66), channel_id=1, source_target_pairs={{0,8},{16,24},{8,0},{24,16},{1,9},{17,25},{9,1},{25,17},{2,10},{18... | collective-permute-start | bytes 393224 | tf_op jit(solution)/shard_map/ppermute | solution.py:378
  72.2 7.6 %collective-permute-start.22 = (f32[32,1024]{1,0:T(8,128)S(1)}, f32[32,1024]{1,0:T(8,128)S(1)}, u32[]{:S(2)}, u32[]{:S(2)}) collective-permute-start(f32[32,1024]{1,0:T(8,128)S(1)} %get-tuple-element.67.refs_2_), channel_id=1, source_target_pairs={{8,16},{16,8},{9,17},{17,9},{10,18},{18,10},{11,19},{19,11},{12,20... | collective-permute-start | bytes 393224 | tf_op jit(solution)/shard_map/ppermute | solution.py:378
  76.0 16.1 %collective-permute-start.27 = (f32[1024,128]{1,0:T(8,128)S(1)}, f32[1024,128]{1,0:T(8,128)S(1)}, u32[]{:S(2)}, u32[]{:S(2)}) collective-permute-start(f32[1024,128]{1,0:T(8,128)S(1)} %payload.18.refs_2_), channel_id=1, source_target_pairs={{1,3},{2,4},{5,7},{3,1},{4,2},{7,5},{9,11},{10,12},{13,15},{11,9},... | collective-permute-start | bytes 1572872 | tf_op jit(solution)/shard_map/ppermute | solution.py:467
  80.0 15.2 %collective-permute-start.24 = (f32[1024,128]{1,0:T(8,128)S(1)}, f32[1024,128]{1,0:T(8,128)S(1)}, u32[]{:S(2)}, u32[]{:S(2)}) collective-permute-start(f32[1024,128]{1,0:T(8,128)S(1)} %payload.19.refs_2_), channel_id=1, source_target_pairs={{0,2},{3,5},{4,6},{2,0},{5,3},{6,4},{8,10},{11,13},{12,14},{10,8},... | collective-permute-start | bytes 1572872 | tf_op jit(solution)/shard_map/ppermute | solution.py:467
  84.4 15.0 %collective-permute-start.29 = (f32[1024,128]{1,0:T(8,128)S(1)}, f32[1024,128]{1,0:T(8,128)S(1)}, u32[]{:S(2)}, u32[]{:S(2)}) collective-permute-start(f32[1024,128]{1,0:T(8,128)S(1)} %get-tuple-element.69.refs_2_), channel_id=1, source_target_pairs={{0,1},{1,0},{2,3},{3,2},{4,5},{5,4},{6,7},{7,6},{8,9},{9,8},{10,11... | collective-permute-start | bytes 1572872 | tf_op jit(solution)/shard_map/ppermute | solution.py:464
  87.7 13.7 %collective-permute-start.34 = (f32[1024,128]{1,0:T(8,128)S(1)}, f32[1024,128]{1,0:T(8,128)S(1)}, u32[]{:S(2)}, u32[]{:S(2)}) collective-permute-start(f32[1024,128]{1,0:T(8,128)S(1)} %get-tuple-element.70.refs_8_), channel_id=1, source_target_pairs={{0,1},{1,0},{2,3},{3,2},{4,5},{5,4},{6,7},{7,6},{8,9},{9,8},{10,11... | collective-permute-start | bytes 1572872 | tf_op jit(solution)/shard_map/ppermute | solution.py:464
  90.4 1.4 %collective-permute-start.26 = (f32[2,256]{1,0:T(2,128)S(1)}, f32[2,256]{1,0:T(2,128)S(1)}, u32[]{:S(2)}, u32[]{:S(2)}) collective-permute-start(f32[2,256]{1,0:T(2,128)S(1)} %get-tuple-element.71.refs_3_.refs_0_), channel_id=1, source_target_pairs={{0,1},{1,0},{2,3},{3,2},{4,5},{5,4},{6,7},{7,6},{8,9},{9,8},{10,11... | collective-permute-start | bytes 6152 | tf_op jit(solution)/shard_map/ppermute | solution.py:665
  91.7 10.2 %collective-permute-start.38 = (f32[1024,128]{1,0:T(8,128)S(1)}, f32[1024,128]{1,0:T(8,128)S(1)}, u32[]{:S(2)}, u32[]{:S(2)}) collective-permute-start(f32[1024,128]{1,0:T(8,128)S(1)} %get-tuple-element.61.refs_2_.refs_1_), channel_id=1, source_target_pairs={{0,1},{1,0},{2,3},{3,2},{4,5},{5,4},{6,7},{7,6},{8,9},{9,8},{10,11... | collective-permute-start | bytes 1572872 | tf_op jit(solution)/shard_map/ppermute | solution.py:464
  92.1 10.1 %collective-permute-start.37 = (f32[1024,128]{1,0:T(8,128)S(1)}, f32[1024,128]{1,0:T(8,128)S(1)}, u32[]{:S(2)}, u32[]{:S(2)}) collective-permute-start(f32[1024,128]{1,0:T(8,128)S(1)} %pick.9.refs_2_.refs_1_), channel_id=1, source_target_pairs={{0,1},{1,0},{2,3},{3,2},{4,5},{5,4},{6,7},{7,6},{8,9},{9,8},{10,11... | collective-permute-start | bytes 1572872 | tf_op jit(solution)/shard_map/ppermute | solution.py:464
  95.2 14.3 %collective-permute-start.33 = (f32[1024,128]{1,0:T(8,128)S(1)}, f32[1024,128]{1,0:T(8,128)S(1)}, u32[]{:S(2)}, u32[]{:S(2)}) collective-permute-start(f32[1024,128]{1,0:T(8,128)S(1)} %payload.20.refs_2_), channel_id=1, source_target_pairs={{0,2},{3,5},{4,6},{2,0},{5,3},{6,4},{8,10},{11,13},{12,14},{10,8},... | collective-permute-start | bytes 1572872 | tf_op jit(solution)/shard_map/ppermute | solution.py:467
  99.4 13.8 %collective-permute-start.28 = (f32[1024,128]{1,0:T(8,128)S(1)}, f32[1024,128]{1,0:T(8,128)S(1)}, u32[]{:S(2)}, u32[]{:S(2)}) collective-permute-start(f32[1024,128]{1,0:T(8,128)S(1)} %payload.21.refs_2_), channel_id=1, source_target_pairs={{1,3},{2,4},{5,7},{3,1},{4,2},{7,5},{9,11},{10,12},{13,15},{11,9},... | collective-permute-start | bytes 1572872 | tf_op jit(solution)/shard_map/ppermute | solution.py:467
  101.6 1.6 %collective-permute-start.36 = (f32[512,128]{1,0:T(8,128)S(1)}, f32[512,128]{1,0:T(8,128)S(1)}, u32[]{:S(2)}, u32[]{:S(2)}) collective-permute-start(f32[512,128]{1,0:T(8,128)S(1)} %get-tuple-element.84), channel_id=1, source_target_pairs={{0,1},{1,0},{2,3},{3,2},{4,5},{5,4},{6,7},{7,6},{8,9},{9,8},{10,11... | collective-permute-start | bytes 786440 | tf_op jit(solution)/shard_map/ppermute | solution.py:464
  101.9 3.8 %collective-permute-start.35 = (f32[512,128]{1,0:T(8,128)S(1)}, f32[512,128]{1,0:T(8,128)S(1)}, u32[]{:S(2)}, u32[]{:S(2)}) collective-permute-start(f32[512,128]{1,0:T(8,128)S(1)} %get-tuple-element.85), channel_id=1, source_target_pairs={{0,1},{1,0},{2,3},{3,2},{4,5},{5,4},{6,7},{7,6},{8,9},{9,8},{10,11... | collective-permute-start | bytes 786440 | tf_op jit(solution)/shard_map/ppermute | solution.py:464
  102.2 9.3 %collective-permute-start.32 = (f32[2,256]{1,0:T(2,128)S(1)}, f32[2,256]{1,0:T(2,128)S(1)}, u32[]{:S(2)}, u32[]{:S(2)}) collective-permute-start(f32[2,256]{1,0:T(2,128)S(1)} %get-tuple-element.74.refs_0_), channel_id=1, source_target_pairs={{0,6},{1,7},{2,4},{3,5},{4,2},{5,3},{6,0},{7,1},{8,14},{9,15},{10,... | collective-permute-start | bytes 6152 | tf_op jit(solution)/shard_map/ppermute | solution.py:665
  103.2 10.0 %collective-permute-start.31 = (f32[2,256]{1,0:T(2,128)S(1)}, f32[2,256]{1,0:T(2,128)S(1)}, u32[]{:S(2)}, u32[]{:S(2)}) collective-permute-start(f32[2,256]{1,0:T(2,128)S(1)} %get-tuple-element.74.refs_0_), channel_id=1, source_target_pairs={{0,4},{1,5},{2,6},{3,7},{4,0},{5,1},{6,2},{7,3},{8,12},{9,13},{10,... | collective-permute-start | bytes 6152 | tf_op jit(solution)/shard_map/ppermute | solution.py:665
  105.7 7.5 %collective-permute-start.30 = (f32[2,256]{1,0:T(2,128)S(1)}, f32[2,256]{1,0:T(2,128)S(1)}, u32[]{:S(2)}, u32[]{:S(2)}) collective-permute-start(f32[2,256]{1,0:T(2,128)S(1)} %get-tuple-element.74.refs_0_), channel_id=1, source_target_pairs={{0,2},{1,3},{2,0},{3,1},{4,6},{5,7},{6,4},{7,5},{8,10},{9,11},{10,... | collective-permute-start | bytes 6152 | tf_op jit(solution)/shard_map/ppermute | solution.py:665
  109.6 11.7 %collective-permute-start.40 = (f32[1024,128]{1,0:T(8,128)S(1)}, f32[1024,128]{1,0:T(8,128)S(1)}, u32[]{:S(2)}, u32[]{:S(2)}) collective-permute-start(f32[1024,128]{1,0:T(8,128)S(1)} %payload.22.refs_4_), channel_id=1, source_target_pairs={{1,3},{2,4},{5,7},{3,1},{4,2},{7,5},{9,11},{10,12},{13,15},{11,9},... | collective-permute-start | bytes 1572872 | tf_op jit(solution)/shard_map/ppermute | solution.py:467
  113.3 13.4 %collective-permute-start.39 = (f32[1024,128]{1,0:T(8,128)S(1)}, f32[1024,128]{1,0:T(8,128)S(1)}, u32[]{:S(2)}, u32[]{:S(2)}) collective-permute-start(f32[1024,128]{1,0:T(8,128)S(1)} %payload.23.refs_4_), channel_id=1, source_target_pairs={{0,2},{3,5},{4,6},{2,0},{5,3},{6,4},{8,10},{11,13},{12,14},{10,8},... | collective-permute-start | bytes 1572872 | tf_op jit(solution)/shard_map/ppermute | solution.py:467
  115.8 4.0 %collective-permute-start.42 = (f32[512,128]{1,0:T(8,128)S(1)}, f32[512,128]{1,0:T(8,128)S(1)}, u32[]{:S(2)}, u32[]{:S(2)}) collective-permute-start(f32[512,128]{1,0:T(8,128)S(1)} %get-tuple-element.82), channel_id=1, source_target_pairs={{0,1},{1,0},{2,3},{3,2},{4,5},{5,4},{6,7},{7,6},{8,9},{9,8},{10,11... | collective-permute-start | bytes 786440 | tf_op jit(solution)/shard_map/ppermute | solution.py:464
  117.1 2.7 %collective-permute-start.41 = (f32[512,128]{1,0:T(8,128)S(1)}, f32[512,128]{1,0:T(8,128)S(1)}, u32[]{:S(2)}, u32[]{:S(2)}) collective-permute-start(f32[512,128]{1,0:T(8,128)S(1)} %get-tuple-element.83), channel_id=1, source_target_pairs={{0,1},{1,0},{2,3},{3,2},{4,5},{5,4},{6,7},{7,6},{8,9},{9,8},{10,11... | collective-permute-start | bytes 786440 | tf_op jit(solution)/shard_map/ppermute | solution.py:464

commit v18 on v17

--- a/solution.py
+++ b/solution.py
@@ -230,11 +230,13 @@
     out[...] = base[...] - scale * (arrived[:modes] + terms[...])
 
 
-def turn_sum(scale, arrived, base, out, strip):
+def turn_sum(scale, arrived, base, out):
     modes = base.shape[0]
-    value = base[...] - scale * arrived[:modes]
-    out[...] = value
-    strip[...] = value.T[-HALO:]
+    out[...] = base[...] - scale * arrived[:modes]
+
+
+def last_strip(field, strip):
+    strip[...] = field[:, field.shape[1] - LANES :].T[-HALO:]
 
 
 def last_sum(scale, arrived, base, other, flux, out, flux_out, value, sems):
@@ -245,9 +247,17 @@
     ]
     for copy in copies:
         copy.start()
-    value[...] = base[...] - scale * arrived[...]
-    copies.append(pltpu.make_async_copy(value, out.at[:, pl.ds(0, cells)], sems.at[2]))
-    copies[-1].start()
+    rows = base.shape[0] // 2
+    for k in range(2):
+        part = slice(k * rows, (k + 1) * rows)
+        value[part] = base[part] - scale * arrived[part]
+        at = pl.ds(k * rows, rows)
+        copies.append(
+            pltpu.make_async_copy(
+                value.at[at, :], out.at[at, pl.ds(0, cells)], sems.at[2 + k]
+            )
+        )
+        copies[-1].start()
     for copy in copies:
         copy.wait()
 
@@ -605,13 +615,12 @@
 
     two = Round(matrix, step_size, False)
     two.add_terms(mid_a)
+    two.add_terms(mid_a)
     one.first_end(base_b)
-    mid_b, last = call(
-        functools.partial(turn_sum, time_step), [part, (HALO, modes)], one.ends()
-    )
+    (mid_b,) = call(functools.partial(turn_sum, time_step), [part], one.ends())
     two.begin(mid_b)
-    two.add_terms(mid_a)
     two.join_terms(0)
+    (last,) = call(last_strip, [(HALO, modes)], [mid_b])
     strips = paired(*call(strip_pairs, [(HALO, modes)] * 2, [leading, last]))
     flux = None
     for step in range(1, chips):
@@ -650,7 +659,7 @@
         functools.partial(last_sum, step_size),
         [(modes, cells), (2, cells)],
         [*two.ends(), last_b, flux.value],
-        scratch=[pltpu.VMEM(part, jnp.float32), pltpu.SemaphoreType.DMA((3,))],
+        scratch=[pltpu.VMEM(part, jnp.float32), pltpu.SemaphoreType.DMA((4,))],
         out_specs=[HBM, HBM],
     )
     return (updated, heat_flux)

time: 129 us -> 129 us (level)
    pallas_call x56 -> x57, Pallas kernels: 33.9 us -> 33.9 us  [__call__(): pl.pallas_call(body, out_shape=[jax.ShapeDtypeStruct(shape, jnp.float32)...]
  transfers between devices with their start and end apart: 43 -> 43, of which waited for: 13 -> 12; matrix products, arithmetic and copies ran while one was open for 0% -> 0% of each run, Pallas kernels for 24% -> 24%
where the time goes in v18:
time: 129 us; the launch traced here: 128 us
  starting transfers between devices  68.6 us (53%)
  Pallas kernels  33.9 us (26%)
  waiting for transfers between devices  22.7 us (18%)
  between operations  1.62 us (1%)
    ppermute x16, starting transfers between devices, along(): return lax.ppermute(value, 'mode', plan.pairs[stream])  45.1 us
    pallas_call x57, Pallas kernels, __call__(): pl.pallas_call(body, out_shape=[jax.ShapeDtypeStruct(shape, jnp.float32)...  33.9 us
    ppermute x16, waiting for transfers between devices, along(): return lax.ppermute(value, 'mode', plan.pairs[stream])  18.4 us
    ppermute x19, starting transfers between devices, exchange(): lax.ppermute(value[i:j], 'mode', across)  13.6 us
    ppermute x4, starting transfers between devices, paired(): lax.ppermute(value, 'space', pairs + [(j, i) for i, j in pairs])  6.74 us
    ppermute x4, starting transfers between devices, over(): lax.ppermute(self.value, 'mode', [(i, i ^ bit) for i in range(self.device...  3.12 us
  transfers between devices with their start and end apart: 43, of which 12 were waited for; matrix products, arithmetic and copies ran while one was open for 0% of the time, Pallas kernels for 24%

profile of v18, /device:TPU:13, one launch (start us, length us, event | category | flops | bytes accessed | tf_op | source)
XLA Modules:
  0.0 127.8 jit_solution(17036057447554614581)
XLA Ops:
  0.6 2.0 %own_rows.1 = (f32[1040,128]{1,0:T(8,128)}, f32[8,128]{1,0:T(8,128)}) custom-call(f32[1024,256]{1,0:T(8,128)} %refs_0_.9, f32[2,1024]{1,0:T(2,128)} %refs_1_.3, f32[1,1024]{1,0:T(1,128)} %bitcast.4), custom_call_target="tpu_custom_call" | custom-call | flops 1024 | bytes 1024 | tf_op jit(solution)/shard_map/own_rows/pallas_call | solution.py:39
  2.6 3.2 %collective-permute-start.2 = (f32[1040,128]{1,0:T(8,128)}, f32[1040,128]{1,0:T(8,128)S(1)}, u32[]{:S(2)}, u32[]{:S(2)}) collective-permute-start(f32[1040,128]{1,0:T(8,128)} %get-tuple-element.39.refs_1_), channel_id=1, source_target_pairs={{0,2},{3,5},{4,6},{2,0},{5,3},{6,4},{8,10},{11,13},{12,14},{10,8},... | collective-permute-start | bytes 1597448 | tf_op jit(solution)/shard_map/ppermute | solution.py:477
  5.8 1.9 %collective-permute-start = (f32[1040,128]{1,0:T(8,128)}, f32[1040,128]{1,0:T(8,128)S(1)}, u32[]{:S(2)}, u32[]{:S(2)}) collective-permute-start(f32[1040,128]{1,0:T(8,128)} %get-tuple-element.39.refs_1_), channel_id=1, source_target_pairs={{1,3},{2,4},{5,7},{3,1},{4,2},{7,5},{9,11},{10,12},{13,15},{11,9},... | collective-permute-start | bytes 1597448 | tf_op jit(solution)/shard_map/ppermute | solution.py:477
  7.8 0.7 copy-done.3
  8.5 6.2 %load_and_products.1 = (f32[1024,128]{1,0:T(8,128)S(1)}, f32[1024,128]{1,0:T(8,128)S(1)}, f32[1024,128]{1,0:T(8,128)S(1)}, f32[1024,128]{1,0:T(8,128)S(1)}, f32[...) custom-call(bf16[8192,1024]{1,0:T(8,128)(2,1)} %refs_0_.6, f32[1024,256]{1,0:T(8,128)S(1)} %copy-done, ...), custom_call_target="tpu_custom_call" | custom-call | flops 1024 | bytes 1024 | tf_op jit(solution)/shard_map/load_and_products/pallas_call | solution.py:39
  14.6 2.6 %collective-permute-start.1 = (f32[1024,128]{1,0:T(8,128)S(1)}, f32[1024,128]{1,0:T(8,128)S(1)}, u32[]{:S(2)}, u32[]{:S(2)}) collective-permute-start(f32[1024,128]{1,0:T(8,128)S(1)} %get-tuple-element.42), channel_id=1, source_target_pairs={{0,1},{1,0},{2,3},{3,2},{4,5},{5,4},{6,7},{7,6},{8,9},{9,8},{10,11... | collective-permute-start | bytes 1572872 | tf_op jit(solution)/shard_map/ppermute | solution.py:474
  17.3 0.4 collective-permute-start.5
  17.7 0.5 collective-permute-start.9
  18.2 1.5 %collective-permute-done.refs_1_.refs_0_ = f32[1040,128]{1,0:T(8,128)S(1)} collective-permute-done((f32[1040,128]{1,0:T(8,128)}, f32[1040,128]{1,0:T(8,128)S(1)}, u32[]{:S(2)}, u32[]{:S(2)}) %collective-permute-start) | collective-permute-done | bytes 532512 | tf_op jit(solution)/shard_map/ppermute | solution.py:477
  19.9 2.1 %collective-permute-start.8 = (f32[1040,128]{1,0:T(8,128)S(1)}, f32[1040,128]{1,0:T(8,128)S(1)}, u32[]{:S(2)}, u32[]{:S(2)}) collective-permute-start(f32[1040,128]{1,0:T(8,128)S(1)} %payload.12.refs_2_), channel_id=1, source_target_pairs={{1,3},{2,4},{5,7},{3,1},{4,2},{7,5},{9,11},{10,12},{13,15},{11,9},... | collective-permute-start | bytes 1597448 | tf_op jit(solution)/shard_map/ppermute | solution.py:477
  22.0 4.7 %collective-permute-start.3 = (f32[1040,128]{1,0:T(8,128)S(1)}, f32[1040,128]{1,0:T(8,128)S(1)}, u32[]{:S(2)}, u32[]{:S(2)}) collective-permute-start(f32[1040,128]{1,0:T(8,128)S(1)} %payload.13.refs_2_), channel_id=1, source_target_pairs={{0,2},{3,5},{4,6},{2,0},{5,3},{6,4},{8,10},{11,13},{12,14},{10,8},... | collective-permute-start | bytes 1597448 | tf_op jit(solution)/shard_map/ppermute | solution.py:477
  26.9 0.3 strip_rows.1
  27.3 1.3 collective-permute-start.6
  28.6 2.1 %collective-permute-start.7 = (f32[32,1024]{1,0:T(8,128)S(1)}, f32[32,1024]{1,0:T(8,128)S(1)}, u32[]{:S(2)}, u32[]{:S(2)}) collective-permute-start(f32[32,1024]{1,0:T(8,128)S(1)} %get-tuple-element.51.refs_3_), channel_id=1, source_target_pairs={{8,16},{16,8},{9,17},{17,9},{10,18},{18,10},{11,19},{19,11},{12,20... | collective-permute-start | bytes 393224 | tf_op jit(solution)/shard_map/ppermute | solution.py:388
  30.7 1.4 %two_blocks.8.refs_3_ = f32[272,1024]{1,0:T(8,128)S(1)} custom-call(bf16[8192,1024]{1,0:T(8,128)(2,1)S(1)} %get-tuple-element.43.refs_2_.refs_0_, f32[1040,128]{1,0:T(8,128)S(1)} %copy-done.2, f32[1040,128]{1,0:T(8,128)S(1)} %collective-permute-done.9.refs_2_, f32[32,1024]{1,0:T(8,128)S(1)} %get-tuple-element.51.refs_3_), custom_call_target="tpu_custom_call" | custom-call | flops 1024 | bytes 1024 | tf_op jit(solution)/shard_map/two_blocks/pallas_call | solution.py:39
  32.2 5.1 %collective-permute-start.11 = (f32[1040,128]{1,0:T(8,128)S(1)}, f32[1040,128]{1,0:T(8,128)S(1)}, u32[]{:S(2)}, u32[]{:S(2)}) collective-permute-start(f32[1040,128]{1,0:T(8,128)S(1)} %payload.14.refs_2_), channel_id=1, source_target_pairs={{0,2},{3,5},{4,6},{2,0},{5,3},{6,4},{8,10},{11,13},{12,14},{10,8},... | collective-permute-start | bytes 1597448 | tf_op jit(solution)/shard_map/ppermute | solution.py:477
  37.6 1.9 %collective-permute-start.10 = (f32[1040,128]{1,0:T(8,128)S(1)}, f32[1040,128]{1,0:T(8,128)S(1)}, u32[]{:S(2)}, u32[]{:S(2)}) collective-permute-start(f32[1040,128]{1,0:T(8,128)S(1)} %payload.15.refs_3_), channel_id=1, source_target_pairs={{1,3},{2,4},{5,7},{3,1},{4,2},{7,5},{9,11},{10,12},{13,15},{11,9},... | collective-permute-start | bytes 1597448 | tf_op jit(solution)/shard_map/ppermute | solution.py:477
  39.6 1.3 slot_products.5
  40.9 0.6 collective-permute-start.15
  41.7 1.4 %two_blocks.9.refs_5_.refs_3_ = f32[272,1024]{1,0:T(8,128)S(1)} custom-call(bf16[8192,1024]{1,0:T(8,128)(2,1)S(1)} %get-tuple-element.43.refs_2_.refs_0_, f32[1040,128]{1,0:T(8,128)S(1)} %pick.6.refs_2_.refs_1_, f32[1040,128]{1,0:T(8,128)S(1)} %collective-permute-done.12.refs_2_, f32[272,1024]{1,0:T(8,128)S(1)} %two_blocks.8.refs_3_, ...), custom_call_target="tpu_custom_call" | custom-call | flops 1024 | bytes 1024 | tf_op jit(solution)/shard_map/two_blocks/pallas_call | solution.py:39
  43.1 2.0 %first_rest.1 = (f32[1024,128]{1,0:T(8,128)S(1)}, f32[1024,128]{1,0:T(8,128)S(1)}) custom-call(f32[1024,256]{1,0:T(8,128)S(1)} %copy-done, bf16[1024,128]{1,0:T(8,128)(2,1)S(1)} %strip_columns.2.refs_3_.refs_1_, bf16[640,1024]{1,0:T(8,128)(2,1)S(1)} %copy-done.1, f32[8,1024]{1,0:T(8,128)S(1)} %maximum_maximum_fusion.refs_3_.refs_5_, s32[1,256]{1,0:T(1,128)S(1)} %bitcast.2, ...), custom_call_target="tpu_custom_call" | custom-call | flops 1024 | bytes 1024 | tf_op jit(solution)/shard_map/first_rest/pallas_call | solution.py:39
  45.1 2.0 %collective-permute-done.11.refs_0_.refs_1_ = f32[1040,128]{1,0:T(8,128)S(1)} collective-permute-done((f32[1040,128]{1,0:T(8,128)S(1)}, f32[1040,128]{1,0:T(8,128)S(1)}, u32[]{:S(2)}, u32[]{:S(2)}) %collective-permute-start.11) | collective-permute-done | bytes 532512 | tf_op jit(solution)/shard_map/ppermute | solution.py:477
  47.2 1.9 %collective-permute-start.14 = (f32[1024,128]{1,0:T(8,128)S(1)}, f32[1024,128]{1,0:T(8,128)S(1)}, u32[]{:S(2)}, u32[]{:S(2)}) collective-permute-start(f32[1024,128]{1,0:T(8,128)S(1)} %payload.16.refs_3_), channel_id=1, source_target_pairs={{1,3},{2,4},{5,7},{3,1},{4,2},{7,5},{9,11},{10,12},{13,15},{11,9},... | collective-permute-start | bytes 1572872 | tf_op jit(solution)/shard_map/ppermute | solution.py:477
  49.3 3.5 %collective-permute-start.13 = (f32[1024,128]{1,0:T(8,128)S(1)}, f32[1024,128]{1,0:T(8,128)S(1)}, u32[]{:S(2)}, u32[]{:S(2)}) collective-permute-start(f32[1024,128]{1,0:T(8,128)S(1)} %payload.17.refs_4_), channel_id=1, source_target_pairs={{0,2},{3,5},{4,6},{2,0},{5,3},{6,4},{8,10},{11,13},{12,14},{10,8},... | collective-permute-start | bytes 1572872 | tf_op jit(solution)/shard_map/ppermute | solution.py:477
  53.2 0.5 collective-permute-start.16
  53.8 1.4 %two_blocks.10.refs_4_.refs_6_ = f32[272,1024]{1,0:T(8,128)S(1)} custom-call(bf16[8192,1024]{1,0:T(8,128)(2,1)S(1)} %get-tuple-element.43.refs_2_.refs_0_, f32[1040,128]{1,0:T(8,128)S(1)} %pick.7.refs_2_.refs_1_, f32[1040,128]{1,0:T(8,128)S(1)} %collective-permute-done.18.refs_2_, f32[272,1024]{1,0:T(8,128)S(1)} %two_blocks.9.refs_5_.refs_3_, ...), custom_call_target="tpu_custom_call" | custom-call | flops 1024 | bytes 1024 | tf_op jit(solution)/shard_map/two_blocks/pallas_call | solution.py:39
  55.2 1.5 %two_blocks.11 = (f32[1024,128]{1,0:T(8,128)S(1)}, f32[32,1024]{1,0:T(8,128)S(1)}, f32[8,1024]{1,0:T(8,128)S(1)}) custom-call(bf16[8192,1024]{1,0:T(8,128)(2,1)S(1)} %get-tuple-element.43.refs_2_.refs_0_, f32[1040,128]{1,0:T(8,128)S(1)} %pick.8.refs_2_.refs_1_, f32[520,128]{1,0:T(8,128)S(1)} %collective-permute-done.16.refs_2_, ...), custom_call_target="tpu_custom_call" | custom-call | flops 1024 | bytes 1024 | tf_op jit(solution)/shard_map/two_blocks/pallas_call | solution.py:39
  56.7 1.3 slot_products.6
  58.1 1.3 slot_products.7
  59.5 3.5 %collective-permute-done.13.refs_0_ = f32[1024,128]{1,0:T(8,128)S(1)} collective-permute-done((f32[1024,128]{1,0:T(8,128)S(1)}, f32[1024,128]{1,0:T(8,128)S(1)}, u32[]{:S(2)}, u32[]{:S(2)}) %collective-permute-start.13) | collective-permute-done | bytes 524320 | tf_op jit(solution)/shard_map/ppermute | solution.py:477
  63.1 3.3 %collective-permute-start.23 = (f32[1024,128]{1,0:T(8,128)S(1)}, f32[1024,128]{1,0:T(8,128)S(1)}, u32[]{:S(2)}, u32[]{:S(2)}) collective-permute-start(f32[1024,128]{1,0:T(8,128)S(1)} %turn_sum.1.refs_2_.refs_0_.refs_1_), channel_id=1, source_target_pairs={{0,2},{3,5},{4,6},{2,0},{5,3},{6,4},{8,10},{11,13},{12,14},{10,8},... | collective-permute-start | bytes 1572872 | tf_op jit(solution)/shard_map/ppermute | solution.py:477
  66.4 1.9 %collective-permute-start.19 = (f32[1024,128]{1,0:T(8,128)S(1)}, f32[1024,128]{1,0:T(8,128)S(1)}, u32[]{:S(2)}, u32[]{:S(2)}) collective-permute-start(f32[1024,128]{1,0:T(8,128)S(1)} %turn_sum.1.refs_2_.refs_0_.refs_1_), channel_id=1, source_target_pairs={{1,3},{2,4},{5,7},{3,1},{4,2},{7,5},{9,11},{10,12},{13,15},{11,9},... | collective-permute-start | bytes 1572872 | tf_op jit(solution)/shard_map/ppermute | solution.py:477
  68.4 1.0 collective-permute-start.25
  69.7 1.3 collective-permute-start.21
  70.9 2.1 %collective-permute-start.22 = (f32[32,1024]{1,0:T(8,128)S(1)}, f32[32,1024]{1,0:T(8,128)S(1)}, u32[]{:S(2)}, u32[]{:S(2)}) collective-permute-start(f32[32,1024]{1,0:T(8,128)S(1)} %get-tuple-element.63.refs_2_), channel_id=1, source_target_pairs={{8,16},{16,8},{9,17},{17,9},{10,18},{18,10},{11,19},{19,11},{12,20... | collective-permute-start | bytes 393224 | tf_op jit(solution)/shard_map/ppermute | solution.py:388
  73.0 2.7 %collective-permute-done.23.refs_0_ = f32[1024,128]{1,0:T(8,128)S(1)} collective-permute-done((f32[1024,128]{1,0:T(8,128)S(1)}, f32[1024,128]{1,0:T(8,128)S(1)}, u32[]{:S(2)}, u32[]{:S(2)}) %collective-permute-start.23) | collective-permute-done | bytes 524320 | tf_op jit(solution)/shard_map/ppermute | solution.py:477
  75.8 1.9 %collective-permute-start.27 = (f32[1024,128]{1,0:T(8,128)S(1)}, f32[1024,128]{1,0:T(8,128)S(1)}, u32[]{:S(2)}, u32[]{:S(2)}) collective-permute-start(f32[1024,128]{1,0:T(8,128)S(1)} %payload.18.refs_2_), channel_id=1, source_target_pairs={{1,3},{2,4},{5,7},{3,1},{4,2},{7,5},{9,11},{10,12},{13,15},{11,9},... | collective-permute-start | bytes 1572872 | tf_op jit(solution)/shard_map/ppermute | solution.py:477
  77.8 0.8 collective-permute-done.22.refs_1_
  78.7 0.8 collective-permute-done.19.refs_0_.refs_1_
  79.5 3.3 %collective-permute-start.24 = (f32[1024,128]{1,0:T(8,128)S(1)}, f32[1024,128]{1,0:T(8,128)S(1)}, u32[]{:S(2)}, u32[]{:S(2)}) collective-permute-start(f32[1024,128]{1,0:T(8,128)S(1)} %payload.19.refs_2_), channel_id=1, source_target_pairs={{0,2},{3,5},{4,6},{2,0},{5,3},{6,4},{8,10},{11,13},{12,14},{10,8},... | collective-permute-start | bytes 1572872 | tf_op jit(solution)/shard_map/ppermute | solution.py:477
  83.0 1.3 slot_products.8
  84.2 2.1 %collective-permute-start.29 = (f32[1024,128]{1,0:T(8,128)S(1)}, f32[1024,128]{1,0:T(8,128)S(1)}, u32[]{:S(2)}, u32[]{:S(2)}) collective-permute-start(f32[1024,128]{1,0:T(8,128)S(1)} %get-tuple-element.65.refs_2_), channel_id=1, source_target_pairs={{0,1},{1,0},{2,3},{3,2},{4,5},{5,4},{6,7},{7,6},{8,9},{9,8},{10,11... | collective-permute-start | bytes 1572872 | tf_op jit(solution)/shard_map/ppermute | solution.py:474
  86.3 1.2 slot_products.9
  87.6 2.5 %second_rest.1 = (f32[1024,128]{1,0:T(8,128)S(1)}, f32[1024,128]{1,0:T(8,128)S(1)}, f32[2,256]{1,0:T(2,128)S(1)}) custom-call(f32[1024,256]{1,0:T(8,128)S(1)} %copy-done, f32[1024,128]{1,0:T(8,128)S(1)} %get-tuple-element.56.refs_1_, f32[1024,128]{1,0:T(8,128)S(1)} %turn_sum.1.refs_2_.refs_0_.refs_1_, bf16[1024,128]{1,0:T(8,128)(2,1)S(1)} %strip_columns.3.refs_2_.refs_3_, ...), custom_call_target="tpu_custom_call" | custom-call | flops 1024 | bytes 1024 | tf_op jit(solution)/shard_map/second_rest/pallas_call | solution.py:39
  90.2 0.6 collective-permute-start.26
  90.7 0.8 collective-permute-done.26.refs_1_
  91.6 0.3 collective-permute-start.38
  91.9 3.2 %collective-permute-start.37 = (f32[1024,128]{1,0:T(8,128)S(1)}, f32[1024,128]{1,0:T(8,128)S(1)}, u32[]{:S(2)}, u32[]{:S(2)}) collective-permute-start(f32[1024,128]{1,0:T(8,128)S(1)} %pick.9.refs_2_.refs_1_), channel_id=1, source_target_pairs={{0,1},{1,0},{2,3},{3,2},{4,5},{5,4},{6,7},{7,6},{8,9},{9,8},{10,11... | collective-permute-start | bytes 1572872 | tf_op jit(solution)/shard_map/ppermute | solution.py:474
  95.2 4.0 %collective-permute-start.33 = (f32[1024,128]{1,0:T(8,128)S(1)}, f32[1024,128]{1,0:T(8,128)S(1)}, u32[]{:S(2)}, u32[]{:S(2)}) collective-permute-start(f32[1024,128]{1,0:T(8,128)S(1)} %payload.20.refs_2_), channel_id=1, source_target_pairs={{0,2},{3,5},{4,6},{2,0},{5,3},{6,4},{8,10},{11,13},{12,14},{10,8},... | collective-permute-start | bytes 1572872 | tf_op jit(solution)/shard_map/ppermute | solution.py:477
  99.2 1.9 %collective-permute-start.28 = (f32[1024,128]{1,0:T(8,128)S(1)}, f32[1024,128]{1,0:T(8,128)S(1)}, u32[]{:S(2)}, u32[]{:S(2)}) collective-permute-start(f32[1024,128]{1,0:T(8,128)S(1)} %payload.21.refs_2_), channel_id=1, source_target_pairs={{1,3},{2,4},{5,7},{3,1},{4,2},{7,5},{9,11},{10,12},{13,15},{11,9},... | collective-permute-start | bytes 1572872 | tf_op jit(solution)/shard_map/ppermute | solution.py:477
  101.4 0.3 collective-permute-start.36
  102.0 1.0 collective-permute-done.36.refs_3_
  103.0 2.5 %collective-permute-start.31 = (f32[2,256]{1,0:T(2,128)S(1)}, f32[2,256]{1,0:T(2,128)S(1)}, u32[]{:S(2)}, u32[]{:S(2)}) collective-permute-start(f32[2,256]{1,0:T(2,128)S(1)} %get-tuple-element.70.refs_0_), channel_id=1, source_target_pairs={{0,4},{1,5},{2,6},{3,7},{4,0},{5,1},{6,2},{7,3},{8,12},{9,13},{10,... | collective-permute-start | bytes 6152 | tf_op jit(solution)/shard_map/ppermute | solution.py:674
  105.7 1.3 %two_blocks.12.refs_3_ = f32[256,1024]{1,0:T(8,128)S(1)} custom-call(bf16[8192,1024]{1,0:T(8,128)(2,1)S(1)} %get-tuple-element.43.refs_2_.refs_0_, f32[1024,128]{1,0:T(8,128)S(1)} %pick.10.refs_1_, f32[512,128]{1,0:T(8,128)S(1)} %collective-permute-done.35.refs_2_, f32[512,128]{1,0:T(8,128)S(1)} %collective-permute-done.36.refs_3_, ...), custom_call_target="tpu_custom_call" | custom-call | flops 1024 | bytes 1024 | tf_op jit(solution)/shard_map/two_blocks/pallas_call | solution.py:39
  107.0 2.4 %collective-permute-done.33.refs_0_.refs_1_ = f32[1024,128]{1,0:T(8,128)S(1)} collective-permute-done((f32[1024,128]{1,0:T(8,128)S(1)}, f32[1024,128]{1,0:T(8,128)S(1)}, u32[]{:S(2)}, u32[]{:S(2)}) %collective-permute-start.33) | collective-permute-done | bytes 524320 | tf_op jit(solution)/shard_map/ppermute | solution.py:477
  109.4 1.9 %collective-permute-start.40 = (f32[1024,128]{1,0:T(8,128)S(1)}, f32[1024,128]{1,0:T(8,128)S(1)}, u32[]{:S(2)}, u32[]{:S(2)}) collective-permute-start(f32[1024,128]{1,0:T(8,128)S(1)} %payload.22.refs_4_), channel_id=1, source_target_pairs={{1,3},{2,4},{5,7},{3,1},{4,2},{7,5},{9,11},{10,12},{13,15},{11,9},... | collective-permute-start | bytes 1572872 | tf_op jit(solution)/shard_map/ppermute | solution.py:477
  111.4 1.7 %collective-permute-done.31.refs_2_ = f32[2,256]{1,0:T(2,128)S(1)} collective-permute-done((f32[2,256]{1,0:T(2,128)S(1)}, f32[2,256]{1,0:T(2,128)S(1)}, u32[]{:S(2)}, u32[]{:S(2)}) %collective-permute-start.31) | collective-permute-done | bytes 2080 | tf_op jit(solution)/shard_map/ppermute | solution.py:674
  113.1 2.4 %collective-permute-start.39 = (f32[1024,128]{1,0:T(8,128)S(1)}, f32[1024,128]{1,0:T(8,128)S(1)}, u32[]{:S(2)}, u32[]{:S(2)}) collective-permute-start(f32[1024,128]{1,0:T(8,128)S(1)} %payload.23.refs_4_), channel_id=1, source_target_pairs={{0,2},{3,5},{4,6},{2,0},{5,3},{6,4},{8,10},{11,13},{12,14},{10,8},... | collective-permute-start | bytes 1572872 | tf_op jit(solution)/shard_map/ppermute | solution.py:477
  115.7 1.3 %collective-permute-start.42 = (f32[512,128]{1,0:T(8,128)S(1)}, f32[512,128]{1,0:T(8,128)S(1)}, u32[]{:S(2)}, u32[]{:S(2)}) collective-permute-start(f32[512,128]{1,0:T(8,128)S(1)} %get-tuple-element.78), channel_id=1, source_target_pairs={{0,1},{1,0},{2,3},{3,2},{4,5},{5,4},{6,7},{7,6},{8,9},{9,8},{10,11... | collective-permute-start | bytes 786440 | tf_op jit(solution)/shard_map/ppermute | solution.py:474
  117.1 1.3 %two_blocks.13.refs_3_.refs_4_ = f32[256,1024]{1,0:T(8,128)S(1)} custom-call(bf16[8192,1024]{1,0:T(8,128)(2,1)S(1)} %get-tuple-element.43.refs_2_.refs_0_, f32[1024,128]{1,0:T(8,128)S(1)} %turn_sum.1.refs_2_.refs_0_.refs_1_, f32[1024,128]{1,0:T(8,128)S(1)} %pass_on.2.refs_1_.refs_2_, f32[256,1024]{1,0:T(8,128)S(1)} %two_blocks.12.refs_3_, ...), custom_call_target="tpu_custom_call" | custom-call | flops 1024 | bytes 1024 | tf_op jit(solution)/shard_map/two_blocks/pallas_call | solution.py:39
  118.3 1.3 %two_blocks.14.refs_4_.refs_6_ = f32[256,1024]{1,0:T(8,128)S(1)} custom-call(bf16[8192,1024]{1,0:T(8,128)(2,1)S(1)} %get-tuple-element.43.refs_2_.refs_0_, f32[1024,128]{1,0:T(8,128)S(1)} %pick.9.refs_2_.refs_1_, f32[1024,128]{1,0:T(8,128)S(1)} %pass_on.3.refs_4_.refs_2_, f32[256,1024]{1,0:T(8,128)S(1)} %two_blocks.13.refs_3_.refs_4_, ...), custom_call_target="tpu_custom_call" | custom-call | flops 1024 | bytes 1024 | tf_op jit(solution)/shard_map/two_blocks/pallas_call | solution.py:39
  119.7 1.4 %two_blocks.15.refs_3_.refs_2_ = f32[1024,128]{1,0:T(8,128)S(1)} custom-call(bf16[8192,1024]{1,0:T(8,128)(2,1)S(1)} %get-tuple-element.43.refs_2_.refs_0_, f32[1024,128]{1,0:T(8,128)S(1)} %pick.11.refs_4_.refs_1_, f32[512,128]{1,0:T(8,128)S(1)} %collective-permute-done.41.refs_2_, f32[512,128]{1,0:T(8,128)S(1)} %collective-permute-done.42.refs_3_, ...), custom_call_target="tpu_custom_call" | custom-call | flops 1024 | bytes 1024 | tf_op jit(solution)/shard_map/two_blocks/pallas_call | solution.py:39
  121.2 5.4 %collective-permute-done.39.refs_0_ = f32[1024,128]{1,0:T(8,128)S(1)} collective-permute-done((f32[1024,128]{1,0:T(8,128)S(1)}, f32[1024,128]{1,0:T(8,128)S(1)}, u32[]{:S(2)}, u32[]{:S(2)}) %collective-permute-start.39) | collective-permute-done | bytes 524320 | tf_op jit(solution)/shard_map/ppermute | solution.py:477
  126.6 1.0 last_sum.1
  (100 shorter events, 4.0 us)
Async XLA Ops:
  0.6 7.1 %copy-start = (f32[1024,256]{1,0:T(8,128)S(1)}, f32[1024,256]{1,0:T(8,128)}, u32[]{:S(2)}) copy-start(f32[1024,256]{1,0:T(8,128)} %refs_0_.9) | copy-start | bytes 3145732
  2.6 15.1 %collective-permute-start.2 = (f32[1040,128]{1,0:T(8,128)}, f32[1040,128]{1,0:T(8,128)S(1)}, u32[]{:S(2)}, u32[]{:S(2)}) collective-permute-start(f32[1040,128]{1,0:T(8,128)} %get-tuple-element.39.refs_1_), channel_id=1, source_target_pairs={{0,2},{3,5},{4,6},{2,0},{5,3},{6,4},{8,10},{11,13},{12,14},{10,8},... | collective-permute-start | bytes 1597448 | tf_op jit(solution)/shard_map/ppermute | solution.py:477
  5.8 13.9 %collective-permute-start = (f32[1040,128]{1,0:T(8,128)}, f32[1040,128]{1,0:T(8,128)S(1)}, u32[]{:S(2)}, u32[]{:S(2)}) collective-permute-start(f32[1040,128]{1,0:T(8,128)} %get-tuple-element.39.refs_1_), channel_id=1, source_target_pairs={{1,3},{2,4},{5,7},{3,1},{4,2},{7,5},{9,11},{10,12},{13,15},{11,9},... | collective-permute-start | bytes 1597448 | tf_op jit(solution)/shard_map/ppermute | solution.py:477
  7.8 0.7 copy-start.3
  8.5 9.3 %copy-start.2 = (f32[1040,128]{1,0:T(8,128)S(1)}, f32[1040,128]{1,0:T(8,128)}, u32[]{:S(2)}) copy-start(f32[1040,128]{1,0:T(8,128)} %get-tuple-element.39.refs_1_) | copy-start | bytes 1597444
  14.6 5.1 %collective-permute-start.1 = (f32[1024,128]{1,0:T(8,128)S(1)}, f32[1024,128]{1,0:T(8,128)S(1)}, u32[]{:S(2)}, u32[]{:S(2)}) collective-permute-start(f32[1024,128]{1,0:T(8,128)S(1)} %get-tuple-element.42), channel_id=1, source_target_pairs={{0,1},{1,0},{2,3},{3,2},{4,5},{5,4},{6,7},{7,6},{8,9},{9,8},{10,11... | collective-permute-start | bytes 1572872 | tf_op jit(solution)/shard_map/ppermute | solution.py:474
  17.2 9.5 %collective-permute-start.4 = (f32[1024,128]{1,0:T(8,128)S(1)}, f32[1024,128]{1,0:T(8,128)S(1)}, u32[]{:S(2)}, u32[]{:S(2)}) collective-permute-start(f32[1024,128]{1,0:T(8,128)S(1)} %get-tuple-element.45), channel_id=1, source_target_pairs={{0,1},{1,0},{2,3},{3,2},{4,5},{5,4},{6,7},{7,6},{8,9},{9,8},{10,11... | collective-permute-start | bytes 1572872 | tf_op jit(solution)/shard_map/ppermute | solution.py:474
  17.3 9.5 %collective-permute-start.5 = (f32[1024,128]{1,0:T(8,128)S(1)}, f32[1024,128]{1,0:T(8,128)S(1)}, u32[]{:S(2)}, u32[]{:S(2)}) collective-permute-start(f32[1024,128]{1,0:T(8,128)S(1)} %get-tuple-element.47), channel_id=1, source_target_pairs={{0,1},{1,0},{2,3},{3,2},{4,5},{5,4},{6,7},{7,6},{8,9},{9,8},{10,11... | collective-permute-start | bytes 1572872 | tf_op jit(solution)/shard_map/ppermute | solution.py:474
  17.7 12.9 %collective-permute-start.9 = (f32[1040,128]{1,0:T(8,128)S(1)}, f32[1040,128]{1,0:T(8,128)S(1)}, u32[]{:S(2)}, u32[]{:S(2)}) collective-permute-start(f32[1040,128]{1,0:T(8,128)S(1)} %copy-done.2), channel_id=1, source_target_pairs={{0,1},{1,0},{2,3},{3,2},{4,5},{5,4},{6,7},{7,6},{8,9},{9,8},{10,11... | collective-permute-start | bytes 1597448 | tf_op jit(solution)/shard_map/ppermute | solution.py:474
  19.9 12.2 %collective-permute-start.8 = (f32[1040,128]{1,0:T(8,128)S(1)}, f32[1040,128]{1,0:T(8,128)S(1)}, u32[]{:S(2)}, u32[]{:S(2)}) collective-permute-start(f32[1040,128]{1,0:T(8,128)S(1)} %payload.12.refs_2_), channel_id=1, source_target_pairs={{1,3},{2,4},{5,7},{3,1},{4,2},{7,5},{9,11},{10,12},{13,15},{11,9},... | collective-permute-start | bytes 1597448 | tf_op jit(solution)/shard_map/ppermute | solution.py:477
  22.0 15.5 %collective-permute-start.3 = (f32[1040,128]{1,0:T(8,128)S(1)}, f32[1040,128]{1,0:T(8,128)S(1)}, u32[]{:S(2)}, u32[]{:S(2)}) collective-permute-start(f32[1040,128]{1,0:T(8,128)S(1)} %payload.13.refs_2_), channel_id=1, source_target_pairs={{0,2},{3,5},{4,6},{2,0},{5,3},{6,4},{8,10},{11,13},{12,14},{10,8},... | collective-permute-start | bytes 1597448 | tf_op jit(solution)/shard_map/ppermute | solution.py:477
  27.3 10.1 %collective-permute-start.6 = (f32[32,1024]{1,0:T(8,128)S(1)}, f32[32,1024]{1,0:T(8,128)S(1)}, u32[]{:S(2)}, u32[]{:S(2)}) collective-permute-start(f32[32,1024]{1,0:T(8,128)S(1)} %get-tuple-element.50), channel_id=1, source_target_pairs={{0,8},{16,24},{8,0},{24,16},{1,9},{17,25},{9,1},{25,17},{2,10},{18... | collective-permute-start | bytes 393224 | tf_op jit(solution)/shard_map/ppermute | solution.py:388
  28.6 8.8 %collective-permute-start.7 = (f32[32,1024]{1,0:T(8,128)S(1)}, f32[32,1024]{1,0:T(8,128)S(1)}, u32[]{:S(2)}, u32[]{:S(2)}) collective-permute-start(f32[32,1024]{1,0:T(8,128)S(1)} %get-tuple-element.51.refs_3_), channel_id=1, source_target_pairs={{8,16},{16,8},{9,17},{17,9},{10,18},{18,10},{11,19},{19,11},{12,20... | collective-permute-start | bytes 393224 | tf_op jit(solution)/shard_map/ppermute | solution.py:388
  30.7 11.0 %collective-permute-start.12 = (f32[1040,128]{1,0:T(8,128)S(1)}, f32[1040,128]{1,0:T(8,128)S(1)}, u32[]{:S(2)}, u32[]{:S(2)}) collective-permute-start(f32[1040,128]{1,0:T(8,128)S(1)} %pick.6.refs_2_.refs_1_), channel_id=1, source_target_pairs={{0,1},{1,0},{2,3},{3,2},{4,5},{5,4},{6,7},{7,6},{8,9},{9,8},{10,11... | collective-permute-start | bytes 1597448 | tf_op jit(solution)/shard_map/ppermute | solution.py:474
  32.2 14.9 %collective-permute-start.11 = (f32[1040,128]{1,0:T(8,128)S(1)}, f32[1040,128]{1,0:T(8,128)S(1)}, u32[]{:S(2)}, u32[]{:S(2)}) collective-permute-start(f32[1040,128]{1,0:T(8,128)S(1)} %payload.14.refs_2_), channel_id=1, source_target_pairs={{0,2},{3,5},{4,6},{2,0},{5,3},{6,4},{8,10},{11,13},{12,14},{10,8},... | collective-permute-start | bytes 1597448 | tf_op jit(solution)/shard_map/ppermute | solution.py:477
  37.6 11.6 %collective-permute-start.10 = (f32[1040,128]{1,0:T(8,128)S(1)}, f32[1040,128]{1,0:T(8,128)S(1)}, u32[]{:S(2)}, u32[]{:S(2)}) collective-permute-start(f32[1040,128]{1,0:T(8,128)S(1)} %payload.15.refs_3_), channel_id=1, source_target_pairs={{1,3},{2,4},{5,7},{3,1},{4,2},{7,5},{9,11},{10,12},{13,15},{11,9},... | collective-permute-start | bytes 1597448 | tf_op jit(solution)/shard_map/ppermute | solution.py:477
  39.6 1.9 %copy-start.5 = (f32[2,1024]{1,0:T(2,128)S(1)}, f32[2,1024]{1,0:T(2,128)}, u32[]{:S(2)}) copy-start(f32[2,1024]{1,0:T(2,128)} %refs_1_.3) | copy-start | bytes 24580
  39.6 1.9 %copy-start.6 = (f32[1024]{0:T(1024)S(1)}, f32[1024]{0:T(1024)}, u32[]{:S(2)}) copy-start(f32[1024]{0:T(1024)} %param.9) | copy-start | bytes 12292
  40.9 12.3 %collective-permute-start.15 = (f32[1024,128]{1,0:T(8,128)S(1)}, f32[1024,128]{1,0:T(8,128)S(1)}, u32[]{:S(2)}, u32[]{:S(2)}) collective-permute-start(f32[1024,128]{1,0:T(8,128)S(1)} %get-tuple-element.52.refs_4_), channel_id=1, source_target_pairs={{0,1},{1,0},{2,3},{3,2},{4,5},{5,4},{6,7},{7,6},{8,9},{9,8},{10,11... | collective-permute-start | bytes 1572872 | tf_op jit(solution)/shard_map/ppermute | solution.py:474
  41.6 12.2 %collective-permute-start.18 = (f32[1040,128]{1,0:T(8,128)S(1)}, f32[1040,128]{1,0:T(8,128)S(1)}, u32[]{:S(2)}, u32[]{:S(2)}) collective-permute-start(f32[1040,128]{1,0:T(8,128)S(1)} %pick.7.refs_2_.refs_1_), channel_id=1, source_target_pairs={{0,1},{1,0},{2,3},{3,2},{4,5},{5,4},{6,7},{7,6},{8,9},{9,8},{10,11... | collective-permute-start | bytes 1597448 | tf_op jit(solution)/shard_map/ppermute | solution.py:474
  41.7 1.4 %copy-start.1 = (bf16[640,1024]{1,0:T(8,128)(2,1)S(1)}, bf16[640,1024]{1,0:T(8,128)(2,1)}, u32[]{:S(2)}) copy-start(bf16[640,1024]{1,0:T(8,128)(2,1)} %constant.4.clone.refs_2_.refs_4_) | copy-start | bytes 3932164
  41.7 1.4 %copy-start.4 = (s32[256]{0:T(256)S(1)}, s32[256]{0:T(256)}, u32[]{:S(2)}) copy-start(s32[256]{0:T(256)} %param.10) | copy-start | bytes 3076
  47.2 12.2 %collective-permute-start.14 = (f32[1024,128]{1,0:T(8,128)S(1)}, f32[1024,128]{1,0:T(8,128)S(1)}, u32[]{:S(2)}, u32[]{:S(2)}) collective-permute-start(f32[1024,128]{1,0:T(8,128)S(1)} %payload.16.refs_3_), channel_id=1, source_target_pairs={{1,3},{2,4},{5,7},{3,1},{4,2},{7,5},{9,11},{10,12},{13,15},{11,9},... | collective-permute-start | bytes 1572872 | tf_op jit(solution)/shard_map/ppermute | solution.py:477
  49.3 13.7 %collective-permute-start.13 = (f32[1024,128]{1,0:T(8,128)S(1)}, f32[1024,128]{1,0:T(8,128)S(1)}, u32[]{:S(2)}, u32[]{:S(2)}) collective-permute-start(f32[1024,128]{1,0:T(8,128)S(1)} %payload.17.refs_4_), channel_id=1, source_target_pairs={{0,2},{3,5},{4,6},{2,0},{5,3},{6,4},{8,10},{11,13},{12,14},{10,8},... | collective-permute-start | bytes 1572872 | tf_op jit(solution)/shard_map/ppermute | solution.py:477
  53.1 2.0 %collective-permute-start.17 = (f32[520,128]{1,0:T(8,128)S(1)}, f32[520,128]{1,0:T(8,128)S(1)}, u32[]{:S(2)}, u32[]{:S(2)}) collective-permute-start(f32[520,128]{1,0:T(8,128)S(1)} %get-tuple-element.76), channel_id=1, source_target_pairs={{0,1},{1,0},{2,3},{3,2},{4,5},{5,4},{6,7},{7,6},{8,9},{9,8},{10,11... | collective-permute-start | bytes 798728 | tf_op jit(solution)/shard_map/ppermute | solution.py:474
  53.2 2.0 %collective-permute-start.16 = (f32[520,128]{1,0:T(8,128)S(1)}, f32[520,128]{1,0:T(8,128)S(1)}, u32[]{:S(2)}, u32[]{:S(2)}) collective-permute-start(f32[520,128]{1,0:T(8,128)S(1)} %get-tuple-element.77), channel_id=1, source_target_pairs={{0,1},{1,0},{2,3},{3,2},{4,5},{5,4},{6,7},{7,6},{8,9},{9,8},{10,11... | collective-permute-start | bytes 798728 | tf_op jit(solution)/shard_map/ppermute | solution.py:474
  58.0 11.4 %collective-permute-start.20 = (f32[1024,128]{1,0:T(8,128)S(1)}, f32[1024,128]{1,0:T(8,128)S(1)}, u32[]{:S(2)}, u32[]{:S(2)}) collective-permute-start(f32[1024,128]{1,0:T(8,128)S(1)} %get-tuple-element.58.refs_2_), channel_id=1, source_target_pairs={{0,1},{1,0},{2,3},{3,2},{4,5},{5,4},{6,7},{7,6},{8,9},{9,8},{10,11... | collective-permute-start | bytes 1572872 | tf_op jit(solution)/shard_map/ppermute | solution.py:474
  63.1 12.7 %collective-permute-start.23 = (f32[1024,128]{1,0:T(8,128)S(1)}, f32[1024,128]{1,0:T(8,128)S(1)}, u32[]{:S(2)}, u32[]{:S(2)}) collective-permute-start(f32[1024,128]{1,0:T(8,128)S(1)} %turn_sum.1.refs_2_.refs_0_.refs_1_), channel_id=1, source_target_pairs={{0,2},{3,5},{4,6},{2,0},{5,3},{6,4},{8,10},{11,13},{12,14},{10,8},... | collective-permute-start | bytes 1572872 | tf_op jit(solution)/shard_map/ppermute | solution.py:477
  66.4 13.0 %collective-permute-start.19 = (f32[1024,128]{1,0:T(8,128)S(1)}, f32[1024,128]{1,0:T(8,128)S(1)}, u32[]{:S(2)}, u32[]{:S(2)}) collective-permute-start(f32[1024,128]{1,0:T(8,128)S(1)} %turn_sum.1.refs_2_.refs_0_.refs_1_), channel_id=1, source_target_pairs={{1,3},{2,4},{5,7},{3,1},{4,2},{7,5},{9,11},{10,12},{13,15},{11,9},... | collective-permute-start | bytes 1572872 | tf_op jit(solution)/shard_map/ppermute | solution.py:477
  68.4 14.5 %collective-permute-start.25 = (f32[1024,128]{1,0:T(8,128)S(1)}, f32[1024,128]{1,0:T(8,128)S(1)}, u32[]{:S(2)}, u32[]{:S(2)}) collective-permute-start(f32[1024,128]{1,0:T(8,128)S(1)} %get-tuple-element.59.refs_3_), channel_id=1, source_target_pairs={{0,1},{1,0},{2,3},{3,2},{4,5},{5,4},{6,7},{7,6},{8,9},{9,8},{10,11... | collective-permute-start | bytes 1572872 | tf_op jit(solution)/shard_map/ppermute | solution.py:474
  69.7 8.1 %collective-permute-start.21 = (f32[32,1024]{1,0:T(8,128)S(1)}, f32[32,1024]{1,0:T(8,128)S(1)}, u32[]{:S(2)}, u32[]{:S(2)}) collective-permute-start(f32[32,1024]{1,0:T(8,128)S(1)} %get-tuple-element.62), channel_id=1, source_target_pairs={{0,8},{16,24},{8,0},{24,16},{1,9},{17,25},{9,1},{25,17},{2,10},{18... | collective-permute-start | bytes 393224 | tf_op jit(solution)/shard_map/ppermute | solution.py:388
  70.9 7.6 %collective-permute-start.22 = (f32[32,1024]{1,0:T(8,128)S(1)}, f32[32,1024]{1,0:T(8,128)S(1)}, u32[]{:S(2)}, u32[]{:S(2)}) collective-permute-start(f32[32,1024]{1,0:T(8,128)S(1)} %get-tuple-element.63.refs_2_), channel_id=1, source_target_pairs={{8,16},{16,8},{9,17},{17,9},{10,18},{18,10},{11,19},{19,11},{12,20... | collective-permute-start | bytes 393224 | tf_op jit(solution)/shard_map/ppermute | solution.py:388
  75.8 16.1 %collective-permute-start.27 = (f32[1024,128]{1,0:T(8,128)S(1)}, f32[1024,128]{1,0:T(8,128)S(1)}, u32[]{:S(2)}, u32[]{:S(2)}) collective-permute-start(f32[1024,128]{1,0:T(8,128)S(1)} %payload.18.refs_2_), channel_id=1, source_target_pairs={{1,3},{2,4},{5,7},{3,1},{4,2},{7,5},{9,11},{10,12},{13,15},{11,9},... | collective-permute-start | bytes 1572872 | tf_op jit(solution)/shard_map/ppermute | solution.py:477
  79.5 15.6 %collective-permute-start.24 = (f32[1024,128]{1,0:T(8,128)S(1)}, f32[1024,128]{1,0:T(8,128)S(1)}, u32[]{:S(2)}, u32[]{:S(2)}) collective-permute-start(f32[1024,128]{1,0:T(8,128)S(1)} %payload.19.refs_2_), channel_id=1, source_target_pairs={{0,2},{3,5},{4,6},{2,0},{5,3},{6,4},{8,10},{11,13},{12,14},{10,8},... | collective-permute-start | bytes 1572872 | tf_op jit(solution)/shard_map/ppermute | solution.py:477
  84.2 15.0 %collective-permute-start.29 = (f32[1024,128]{1,0:T(8,128)S(1)}, f32[1024,128]{1,0:T(8,128)S(1)}, u32[]{:S(2)}, u32[]{:S(2)}) collective-permute-start(f32[1024,128]{1,0:T(8,128)S(1)} %get-tuple-element.65.refs_2_), channel_id=1, source_target_pairs={{0,1},{1,0},{2,3},{3,2},{4,5},{5,4},{6,7},{7,6},{8,9},{9,8},{10,11... | collective-permute-start | bytes 1572872 | tf_op jit(solution)/shard_map/ppermute | solution.py:474
  87.6 13.7 %collective-permute-start.34 = (f32[1024,128]{1,0:T(8,128)S(1)}, f32[1024,128]{1,0:T(8,128)S(1)}, u32[]{:S(2)}, u32[]{:S(2)}) collective-permute-start(f32[1024,128]{1,0:T(8,128)S(1)} %get-tuple-element.66.refs_8_), channel_id=1, source_target_pairs={{0,1},{1,0},{2,3},{3,2},{4,5},{5,4},{6,7},{7,6},{8,9},{9,8},{10,11... | collective-permute-start | bytes 1572872 | tf_op jit(solution)/shard_map/ppermute | solution.py:474
  90.2 1.4 %collective-permute-start.26 = (f32[2,256]{1,0:T(2,128)S(1)}, f32[2,256]{1,0:T(2,128)S(1)}, u32[]{:S(2)}, u32[]{:S(2)}) collective-permute-start(f32[2,256]{1,0:T(2,128)S(1)} %get-tuple-element.67.refs_3_.refs_0_), channel_id=1, source_target_pairs={{0,1},{1,0},{2,3},{3,2},{4,5},{5,4},{6,7},{7,6},{8,9},{9,8},{10,11... | collective-permute-start | bytes 6152 | tf_op jit(solution)/shard_map/ppermute | solution.py:674
  91.6 10.2 %collective-permute-start.38 = (f32[1024,128]{1,0:T(8,128)S(1)}, f32[1024,128]{1,0:T(8,128)S(1)}, u32[]{:S(2)}, u32[]{:S(2)}) collective-permute-start(f32[1024,128]{1,0:T(8,128)S(1)} %turn_sum.1.refs_2_.refs_0_.refs_1_), channel_id=1, source_target_pairs={{0,1},{1,0},{2,3},{3,2},{4,5},{5,4},{6,7},{7,6},{8,9},{9,8},{10,11... | collective-permute-start | bytes 1572872 | tf_op jit(solution)/shard_map/ppermute | solution.py:474
  91.9 10.1 %collective-permute-start.37 = (f32[1024,128]{1,0:T(8,128)S(1)}, f32[1024,128]{1,0:T(8,128)S(1)}, u32[]{:S(2)}, u32[]{:S(2)}) collective-permute-start(f32[1024,128]{1,0:T(8,128)S(1)} %pick.9.refs_2_.refs_1_), channel_id=1, source_target_pairs={{0,1},{1,0},{2,3},{3,2},{4,5},{5,4},{6,7},{7,6},{8,9},{9,8},{10,11... | collective-permute-start | bytes 1572872 | tf_op jit(solution)/shard_map/ppermute | solution.py:474
  95.2 14.2 %collective-permute-start.33 = (f32[1024,128]{1,0:T(8,128)S(1)}, f32[1024,128]{1,0:T(8,128)S(1)}, u32[]{:S(2)}, u32[]{:S(2)}) collective-permute-start(f32[1024,128]{1,0:T(8,128)S(1)} %payload.20.refs_2_), channel_id=1, source_target_pairs={{0,2},{3,5},{4,6},{2,0},{5,3},{6,4},{8,10},{11,13},{12,14},{10,8},... | collective-permute-start | bytes 1572872 | tf_op jit(solution)/shard_map/ppermute | solution.py:477
  99.2 13.8 %collective-permute-start.28 = (f32[1024,128]{1,0:T(8,128)S(1)}, f32[1024,128]{1,0:T(8,128)S(1)}, u32[]{:S(2)}, u32[]{:S(2)}) collective-permute-start(f32[1024,128]{1,0:T(8,128)S(1)} %payload.21.refs_2_), channel_id=1, source_target_pairs={{1,3},{2,4},{5,7},{3,1},{4,2},{7,5},{9,11},{10,12},{13,15},{11,9},... | collective-permute-start | bytes 1572872 | tf_op jit(solution)/shard_map/ppermute | solution.py:477
  101.4 1.6 %collective-permute-start.36 = (f32[512,128]{1,0:T(8,128)S(1)}, f32[512,128]{1,0:T(8,128)S(1)}, u32[]{:S(2)}, u32[]{:S(2)}) collective-permute-start(f32[512,128]{1,0:T(8,128)S(1)} %get-tuple-element.80), channel_id=1, source_target_pairs={{0,1},{1,0},{2,3},{3,2},{4,5},{5,4},{6,7},{7,6},{8,9},{9,8},{10,11... | collective-permute-start | bytes 786440 | tf_op jit(solution)/shard_map/ppermute | solution.py:474
  101.8 3.8 %collective-permute-start.35 = (f32[512,128]{1,0:T(8,128)S(1)}, f32[512,128]{1,0:T(8,128)S(1)}, u32[]{:S(2)}, u32[]{:S(2)}) collective-permute-start(f32[512,128]{1,0:T(8,128)S(1)} %get-tuple-element.81), channel_id=1, source_target_pairs={{0,1},{1,0},{2,3},{3,2},{4,5},{5,4},{6,7},{7,6},{8,9},{9,8},{10,11... | collective-permute-start | bytes 786440 | tf_op jit(solution)/shard_map/ppermute | solution.py:474
  102.0 9.3 %collective-permute-start.32 = (f32[2,256]{1,0:T(2,128)S(1)}, f32[2,256]{1,0:T(2,128)S(1)}, u32[]{:S(2)}, u32[]{:S(2)}) collective-permute-start(f32[2,256]{1,0:T(2,128)S(1)} %get-tuple-element.70.refs_0_), channel_id=1, source_target_pairs={{0,6},{1,7},{2,4},{3,5},{4,2},{5,3},{6,0},{7,1},{8,14},{9,15},{10,... | collective-permute-start | bytes 6152 | tf_op jit(solution)/shard_map/ppermute | solution.py:674
  103.0 10.0 %collective-permute-start.31 = (f32[2,256]{1,0:T(2,128)S(1)}, f32[2,256]{1,0:T(2,128)S(1)}, u32[]{:S(2)}, u32[]{:S(2)}) collective-permute-start(f32[2,256]{1,0:T(2,128)S(1)} %get-tuple-element.70.refs_0_), channel_id=1, source_target_pairs={{0,4},{1,5},{2,6},{3,7},{4,0},{5,1},{6,2},{7,3},{8,12},{9,13},{10,... | collective-permute-start | bytes 6152 | tf_op jit(solution)/shard_map/ppermute | solution.py:674
  105.6 7.5 %collective-permute-start.30 = (f32[2,256]{1,0:T(2,128)S(1)}, f32[2,256]{1,0:T(2,128)S(1)}, u32[]{:S(2)}, u32[]{:S(2)}) collective-permute-start(f32[2,256]{1,0:T(2,128)S(1)} %get-tuple-element.70.refs_0_), channel_id=1, source_target_pairs={{0,2},{1,3},{2,0},{3,1},{4,6},{5,7},{6,4},{7,5},{8,10},{9,11},{10,... | collective-permute-start | bytes 6152 | tf_op jit(solution)/shard_map/ppermute | solution.py:674
  109.4 11.7 %collective-permute-start.40 = (f32[1024,128]{1,0:T(8,128)S(1)}, f32[1024,128]{1,0:T(8,128)S(1)}, u32[]{:S(2)}, u32[]{:S(2)}) collective-permute-start(f32[1024,128]{1,0:T(8,128)S(1)} %payload.22.refs_4_), channel_id=1, source_target_pairs={{1,3},{2,4},{5,7},{3,1},{4,2},{7,5},{9,11},{10,12},{13,15},{11,9},... | collective-permute-start | bytes 1572872 | tf_op jit(solution)/shard_map/ppermute | solution.py:477
  113.1 13.4 %collective-permute-start.39 = (f32[1024,128]{1,0:T(8,128)S(1)}, f32[1024,128]{1,0:T(8,128)S(1)}, u32[]{:S(2)}, u32[]{:S(2)}) collective-permute-start(f32[1024,128]{1,0:T(8,128)S(1)} %payload.23.refs_4_), channel_id=1, source_target_pairs={{0,2},{3,5},{4,6},{2,0},{5,3},{6,4},{8,10},{11,13},{12,14},{10,8},... | collective-permute-start | bytes 1572872 | tf_op jit(solution)/shard_map/ppermute | solution.py:477
  115.7 4.0 %collective-permute-start.42 = (f32[512,128]{1,0:T(8,128)S(1)}, f32[512,128]{1,0:T(8,128)S(1)}, u32[]{:S(2)}, u32[]{:S(2)}) collective-permute-start(f32[512,128]{1,0:T(8,128)S(1)} %get-tuple-element.78), channel_id=1, source_target_pairs={{0,1},{1,0},{2,3},{3,2},{4,5},{5,4},{6,7},{7,6},{8,9},{9,8},{10,11... | collective-permute-start | bytes 786440 | tf_op jit(solution)/shard_map/ppermute | solution.py:474
  117.0 2.7 %collective-permute-start.41 = (f32[512,128]{1,0:T(8,128)S(1)}, f32[512,128]{1,0:T(8,128)S(1)}, u32[]{:S(2)}, u32[]{:S(2)}) collective-permute-start(f32[512,128]{1,0:T(8,128)S(1)} %get-tuple-element.79), channel_id=1, source_target_pairs={{0,1},{1,0},{2,3},{3,2},{4,5},{5,4},{6,7},{7,6},{8,9},{9,8},{10,11... | collective-permute-start | bytes 786440 | tf_op jit(solution)/shard_map/ppermute | solution.py:474

commit v19 on v18

--- a/solution.py
+++ b/solution.py
@@ -13,7 +13,7 @@
 NY = 16
 HALO = 2 * NY
 LANES = 128
-BLOCK = 512
+BLOCK = 1024
 
 
 relax_rate = 0.5

time: 129 us -> 129 us (level)
  no operation moved by 1% of the time
where the time goes in v19:
time: 129 us; the launch traced here: 128 us
  starting transfers between devices  68.5 us (53%)
  Pallas kernels  33.8 us (26%)
  waiting for transfers between devices  22.8 us (18%)
  between operations  1.62 us (1%)
    ppermute x16, starting transfers between devices, along(): return lax.ppermute(value, 'mode', plan.pairs[stream])  44.9 us
    pallas_call x57, Pallas kernels, __call__(): pl.pallas_call(body, out_shape=[jax.ShapeDtypeStruct(shape, jnp.float32)...  33.8 us
    ppermute x16, waiting for transfers between devices, along(): return lax.ppermute(value, 'mode', plan.pairs[stream])  18.5 us
    ppermute x19, starting transfers between devices, exchange(): lax.ppermute(value[i:j], 'mode', across)  13.7 us
    ppermute x4, starting transfers between devices, paired(): lax.ppermute(value, 'space', pairs + [(j, i) for i, j in pairs])  6.74 us
    ppermute x4, starting transfers between devices, over(): lax.ppermute(self.value, 'mode', [(i, i ^ bit) for i in range(self.device...  3.12 us
  transfers between devices with their start and end apart: 43, of which 12 were waited for; matrix products, arithmetic and copies ran while one was open for 0% of the time, Pallas kernels for 24%

profile of v19, /device:TPU:13, one launch (start us, length us, event | category | flops | bytes accessed | tf_op | source)
XLA Modules:
  0.0 127.8 jit_solution(18028896081939113300)
XLA Ops:
  0.6 2.0 %own_rows.1 = (f32[1040,128]{1,0:T(8,128)}, f32[8,128]{1,0:T(8,128)}) custom-call(f32[1024,256]{1,0:T(8,128)} %refs_0_.9, f32[2,1024]{1,0:T(2,128)} %refs_1_.3, f32[1,1024]{1,0:T(1,128)} %bitcast.4), custom_call_target="tpu_custom_call" | custom-call | flops 1024 | bytes 1024 | tf_op jit(solution)/shard_map/own_rows/pallas_call | solution.py:39
  2.6 3.2 %collective-permute-start.2 = (f32[1040,128]{1,0:T(8,128)}, f32[1040,128]{1,0:T(8,128)S(1)}, u32[]{:S(2)}, u32[]{:S(2)}) collective-permute-start(f32[1040,128]{1,0:T(8,128)} %get-tuple-element.39.refs_1_), channel_id=1, source_target_pairs={{0,2},{3,5},{4,6},{2,0},{5,3},{6,4},{8,10},{11,13},{12,14},{10,8},... | collective-permute-start | bytes 1597448 | tf_op jit(solution)/shard_map/ppermute | solution.py:477
  5.8 1.9 %collective-permute-start = (f32[1040,128]{1,0:T(8,128)}, f32[1040,128]{1,0:T(8,128)S(1)}, u32[]{:S(2)}, u32[]{:S(2)}) collective-permute-start(f32[1040,128]{1,0:T(8,128)} %get-tuple-element.39.refs_1_), channel_id=1, source_target_pairs={{1,3},{2,4},{5,7},{3,1},{4,2},{7,5},{9,11},{10,12},{13,15},{11,9},... | collective-permute-start | bytes 1597448 | tf_op jit(solution)/shard_map/ppermute | solution.py:477
  7.8 0.7 copy-done.3
  8.5 6.2 %load_and_products.1 = (f32[1024,128]{1,0:T(8,128)S(1)}, f32[1024,128]{1,0:T(8,128)S(1)}, f32[1024,128]{1,0:T(8,128)S(1)}, f32[1024,128]{1,0:T(8,128)S(1)}, f32[...) custom-call(bf16[8192,1024]{1,0:T(8,128)(2,1)} %refs_0_.6, f32[1024,256]{1,0:T(8,128)S(1)} %copy-done, ...), custom_call_target="tpu_custom_call" | custom-call | flops 1024 | bytes 1024 | tf_op jit(solution)/shard_map/load_and_products/pallas_call | solution.py:39
  14.6 2.6 %collective-permute-start.1 = (f32[1024,128]{1,0:T(8,128)S(1)}, f32[1024,128]{1,0:T(8,128)S(1)}, u32[]{:S(2)}, u32[]{:S(2)}) collective-permute-start(f32[1024,128]{1,0:T(8,128)S(1)} %get-tuple-element.42), channel_id=1, source_target_pairs={{0,1},{1,0},{2,3},{3,2},{4,5},{5,4},{6,7},{7,6},{8,9},{9,8},{10,11... | collective-permute-start | bytes 1572872 | tf_op jit(solution)/shard_map/ppermute | solution.py:474
  17.3 0.4 collective-permute-start.5
  17.7 0.5 collective-permute-start.9
  18.2 1.5 %collective-permute-done.refs_1_.refs_0_ = f32[1040,128]{1,0:T(8,128)S(1)} collective-permute-done((f32[1040,128]{1,0:T(8,128)}, f32[1040,128]{1,0:T(8,128)S(1)}, u32[]{:S(2)}, u32[]{:S(2)}) %collective-permute-start) | collective-permute-done | bytes 532512 | tf_op jit(solution)/shard_map/ppermute | solution.py:477
  19.9 2.1 %collective-permute-start.8 = (f32[1040,128]{1,0:T(8,128)S(1)}, f32[1040,128]{1,0:T(8,128)S(1)}, u32[]{:S(2)}, u32[]{:S(2)}) collective-permute-start(f32[1040,128]{1,0:T(8,128)S(1)} %payload.12.refs_2_), channel_id=1, source_target_pairs={{1,3},{2,4},{5,7},{3,1},{4,2},{7,5},{9,11},{10,12},{13,15},{11,9},... | collective-permute-start | bytes 1597448 | tf_op jit(solution)/shard_map/ppermute | solution.py:477
  22.0 4.7 %collective-permute-start.3 = (f32[1040,128]{1,0:T(8,128)S(1)}, f32[1040,128]{1,0:T(8,128)S(1)}, u32[]{:S(2)}, u32[]{:S(2)}) collective-permute-start(f32[1040,128]{1,0:T(8,128)S(1)} %payload.13.refs_2_), channel_id=1, source_target_pairs={{0,2},{3,5},{4,6},{2,0},{5,3},{6,4},{8,10},{11,13},{12,14},{10,8},... | collective-permute-start | bytes 1597448 | tf_op jit(solution)/shard_map/ppermute | solution.py:477
  26.9 0.3 strip_rows.1
  27.3 1.3 collective-permute-start.6
  28.6 2.1 %collective-permute-start.7 = (f32[32,1024]{1,0:T(8,128)S(1)}, f32[32,1024]{1,0:T(8,128)S(1)}, u32[]{:S(2)}, u32[]{:S(2)}) collective-permute-start(f32[32,1024]{1,0:T(8,128)S(1)} %get-tuple-element.51.refs_3_), channel_id=1, source_target_pairs={{8,16},{16,8},{9,17},{17,9},{10,18},{18,10},{11,19},{19,11},{12,20... | collective-permute-start | bytes 393224 | tf_op jit(solution)/shard_map/ppermute | solution.py:388
  30.7 1.4 %two_blocks.8.refs_3_ = f32[272,1024]{1,0:T(8,128)S(1)} custom-call(bf16[8192,1024]{1,0:T(8,128)(2,1)S(1)} %get-tuple-element.43.refs_2_.refs_0_, f32[1040,128]{1,0:T(8,128)S(1)} %copy-done.2, f32[1040,128]{1,0:T(8,128)S(1)} %collective-permute-done.9.refs_2_, f32[32,1024]{1,0:T(8,128)S(1)} %get-tuple-element.51.refs_3_), custom_call_target="tpu_custom_call" | custom-call | flops 1024 | bytes 1024 | tf_op jit(solution)/shard_map/two_blocks/pallas_call | solution.py:39
  32.2 5.1 %collective-permute-start.11 = (f32[1040,128]{1,0:T(8,128)S(1)}, f32[1040,128]{1,0:T(8,128)S(1)}, u32[]{:S(2)}, u32[]{:S(2)}) collective-permute-start(f32[1040,128]{1,0:T(8,128)S(1)} %payload.14.refs_2_), channel_id=1, source_target_pairs={{0,2},{3,5},{4,6},{2,0},{5,3},{6,4},{8,10},{11,13},{12,14},{10,8},... | collective-permute-start | bytes 1597448 | tf_op jit(solution)/shard_map/ppermute | solution.py:477
  37.6 1.9 %collective-permute-start.10 = (f32[1040,128]{1,0:T(8,128)S(1)}, f32[1040,128]{1,0:T(8,128)S(1)}, u32[]{:S(2)}, u32[]{:S(2)}) collective-permute-start(f32[1040,128]{1,0:T(8,128)S(1)} %payload.15.refs_3_), channel_id=1, source_target_pairs={{1,3},{2,4},{5,7},{3,1},{4,2},{7,5},{9,11},{10,12},{13,15},{11,9},... | collective-permute-start | bytes 1597448 | tf_op jit(solution)/shard_map/ppermute | solution.py:477
  39.6 1.3 slot_products.5
  40.9 0.6 collective-permute-start.15
  41.7 1.4 %two_blocks.9.refs_5_.refs_3_ = f32[272,1024]{1,0:T(8,128)S(1)} custom-call(bf16[8192,1024]{1,0:T(8,128)(2,1)S(1)} %get-tuple-element.43.refs_2_.refs_0_, f32[1040,128]{1,0:T(8,128)S(1)} %pick.6.refs_2_.refs_1_, f32[1040,128]{1,0:T(8,128)S(1)} %collective-permute-done.12.refs_2_, f32[272,1024]{1,0:T(8,128)S(1)} %two_blocks.8.refs_3_, ...), custom_call_target="tpu_custom_call" | custom-call | flops 1024 | bytes 1024 | tf_op jit(solution)/shard_map/two_blocks/pallas_call | solution.py:39
  43.1 1.8 %first_rest.1 = (f32[1024,128]{1,0:T(8,128)S(1)}, f32[1024,128]{1,0:T(8,128)S(1)}) custom-call(f32[1024,256]{1,0:T(8,128)S(1)} %copy-done, bf16[1024,128]{1,0:T(8,128)(2,1)S(1)} %strip_columns.2.refs_3_.refs_1_, bf16[640,1024]{1,0:T(8,128)(2,1)S(1)} %copy-done.1, f32[8,1024]{1,0:T(8,128)S(1)} %maximum_maximum_fusion.refs_3_.refs_5_, s32[1,256]{1,0:T(1,128)S(1)} %bitcast.2, ...), custom_call_target="tpu_custom_call" | custom-call | flops 1024 | bytes 1024 | tf_op jit(solution)/shard_map/first_rest/pallas_call | solution.py:39
  45.0 2.1 %collective-permute-done.11.refs_0_.refs_1_ = f32[1040,128]{1,0:T(8,128)S(1)} collective-permute-done((f32[1040,128]{1,0:T(8,128)S(1)}, f32[1040,128]{1,0:T(8,128)S(1)}, u32[]{:S(2)}, u32[]{:S(2)}) %collective-permute-start.11) | collective-permute-done | bytes 532512 | tf_op jit(solution)/shard_map/ppermute | solution.py:477
  47.2 1.9 %collective-permute-start.14 = (f32[1024,128]{1,0:T(8,128)S(1)}, f32[1024,128]{1,0:T(8,128)S(1)}, u32[]{:S(2)}, u32[]{:S(2)}) collective-permute-start(f32[1024,128]{1,0:T(8,128)S(1)} %payload.16.refs_3_), channel_id=1, source_target_pairs={{1,3},{2,4},{5,7},{3,1},{4,2},{7,5},{9,11},{10,12},{13,15},{11,9},... | collective-permute-start | bytes 1572872 | tf_op jit(solution)/shard_map/ppermute | solution.py:477
  49.3 3.5 %collective-permute-start.13 = (f32[1024,128]{1,0:T(8,128)S(1)}, f32[1024,128]{1,0:T(8,128)S(1)}, u32[]{:S(2)}, u32[]{:S(2)}) collective-permute-start(f32[1024,128]{1,0:T(8,128)S(1)} %payload.17.refs_4_), channel_id=1, source_target_pairs={{0,2},{3,5},{4,6},{2,0},{5,3},{6,4},{8,10},{11,13},{12,14},{10,8},... | collective-permute-start | bytes 1572872 | tf_op jit(solution)/shard_map/ppermute | solution.py:477
  53.2 0.5 collective-permute-start.16
  53.8 1.4 %two_blocks.10.refs_4_.refs_6_ = f32[272,1024]{1,0:T(8,128)S(1)} custom-call(bf16[8192,1024]{1,0:T(8,128)(2,1)S(1)} %get-tuple-element.43.refs_2_.refs_0_, f32[1040,128]{1,0:T(8,128)S(1)} %pick.7.refs_2_.refs_1_, f32[1040,128]{1,0:T(8,128)S(1)} %collective-permute-done.18.refs_2_, f32[272,1024]{1,0:T(8,128)S(1)} %two_blocks.9.refs_5_.refs_3_, ...), custom_call_target="tpu_custom_call" | custom-call | flops 1024 | bytes 1024 | tf_op jit(solution)/shard_map/two_blocks/pallas_call | solution.py:39
  55.2 1.5 %two_blocks.11 = (f32[1024,128]{1,0:T(8,128)S(1)}, f32[32,1024]{1,0:T(8,128)S(1)}, f32[8,1024]{1,0:T(8,128)S(1)}) custom-call(bf16[8192,1024]{1,0:T(8,128)(2,1)S(1)} %get-tuple-element.43.refs_2_.refs_0_, f32[1040,128]{1,0:T(8,128)S(1)} %pick.8.refs_2_.refs_1_, f32[520,128]{1,0:T(8,128)S(1)} %collective-permute-done.16.refs_2_, ...), custom_call_target="tpu_custom_call" | custom-call | flops 1024 | bytes 1024 | tf_op jit(solution)/shard_map/two_blocks/pallas_call | solution.py:39
  56.7 1.3 slot_products.6
  58.1 1.3 slot_products.7
  59.5 3.5 %collective-permute-done.13.refs_0_ = f32[1024,128]{1,0:T(8,128)S(1)} collective-permute-done((f32[1024,128]{1,0:T(8,128)S(1)}, f32[1024,128]{1,0:T(8,128)S(1)}, u32[]{:S(2)}, u32[]{:S(2)}) %collective-permute-start.13) | collective-permute-done | bytes 524320 | tf_op jit(solution)/shard_map/ppermute | solution.py:477
  63.1 3.3 %collective-permute-start.23 = (f32[1024,128]{1,0:T(8,128)S(1)}, f32[1024,128]{1,0:T(8,128)S(1)}, u32[]{:S(2)}, u32[]{:S(2)}) collective-permute-start(f32[1024,128]{1,0:T(8,128)S(1)} %turn_sum.1.refs_2_.refs_0_.refs_1_), channel_id=1, source_target_pairs={{0,2},{3,5},{4,6},{2,0},{5,3},{6,4},{8,10},{11,13},{12,14},{10,8},... | collective-permute-start | bytes 1572872 | tf_op jit(solution)/shard_map/ppermute | solution.py:477
  66.4 1.9 %collective-permute-start.19 = (f32[1024,128]{1,0:T(8,128)S(1)}, f32[1024,128]{1,0:T(8,128)S(1)}, u32[]{:S(2)}, u32[]{:S(2)}) collective-permute-start(f32[1024,128]{1,0:T(8,128)S(1)} %turn_sum.1.refs_2_.refs_0_.refs_1_), channel_id=1, source_target_pairs={{1,3},{2,4},{5,7},{3,1},{4,2},{7,5},{9,11},{10,12},{13,15},{11,9},... | collective-permute-start | bytes 1572872 | tf_op jit(solution)/shard_map/ppermute | solution.py:477
  68.4 1.0 collective-permute-start.25
  69.7 1.3 collective-permute-start.21
  70.9 2.1 %collective-permute-start.22 = (f32[32,1024]{1,0:T(8,128)S(1)}, f32[32,1024]{1,0:T(8,128)S(1)}, u32[]{:S(2)}, u32[]{:S(2)}) collective-permute-start(f32[32,1024]{1,0:T(8,128)S(1)} %get-tuple-element.63.refs_2_), channel_id=1, source_target_pairs={{8,16},{16,8},{9,17},{17,9},{10,18},{18,10},{11,19},{19,11},{12,20... | collective-permute-start | bytes 393224 | tf_op jit(solution)/shard_map/ppermute | solution.py:388
  73.0 2.7 %collective-permute-done.23.refs_0_ = f32[1024,128]{1,0:T(8,128)S(1)} collective-permute-done((f32[1024,128]{1,0:T(8,128)S(1)}, f32[1024,128]{1,0:T(8,128)S(1)}, u32[]{:S(2)}, u32[]{:S(2)}) %collective-permute-start.23) | collective-permute-done | bytes 524320 | tf_op jit(solution)/shard_map/ppermute | solution.py:477
  75.8 1.9 %collective-permute-start.27 = (f32[1024,128]{1,0:T(8,128)S(1)}, f32[1024,128]{1,0:T(8,128)S(1)}, u32[]{:S(2)}, u32[]{:S(2)}) collective-permute-start(f32[1024,128]{1,0:T(8,128)S(1)} %payload.18.refs_2_), channel_id=1, source_target_pairs={{1,3},{2,4},{5,7},{3,1},{4,2},{7,5},{9,11},{10,12},{13,15},{11,9},... | collective-permute-start | bytes 1572872 | tf_op jit(solution)/shard_map/ppermute | solution.py:477
  77.8 0.8 collective-permute-done.22.refs_1_
  78.7 0.8 collective-permute-done.19.refs_0_.refs_1_
  79.5 3.3 %collective-permute-start.24 = (f32[1024,128]{1,0:T(8,128)S(1)}, f32[1024,128]{1,0:T(8,128)S(1)}, u32[]{:S(2)}, u32[]{:S(2)}) collective-permute-start(f32[1024,128]{1,0:T(8,128)S(1)} %payload.19.refs_2_), channel_id=1, source_target_pairs={{0,2},{3,5},{4,6},{2,0},{5,3},{6,4},{8,10},{11,13},{12,14},{10,8},... | collective-permute-start | bytes 1572872 | tf_op jit(solution)/shard_map/ppermute | solution.py:477
  83.0 1.3 slot_products.8
  84.2 2.1 %collective-permute-start.29 = (f32[1024,128]{1,0:T(8,128)S(1)}, f32[1024,128]{1,0:T(8,128)S(1)}, u32[]{:S(2)}, u32[]{:S(2)}) collective-permute-start(f32[1024,128]{1,0:T(8,128)S(1)} %get-tuple-element.65.refs_2_), channel_id=1, source_target_pairs={{0,1},{1,0},{2,3},{3,2},{4,5},{5,4},{6,7},{7,6},{8,9},{9,8},{10,11... | collective-permute-start | bytes 1572872 | tf_op jit(solution)/shard_map/ppermute | solution.py:474
  86.3 1.2 slot_products.9
  87.6 2.4 %second_rest.1 = (f32[1024,128]{1,0:T(8,128)S(1)}, f32[1024,128]{1,0:T(8,128)S(1)}, f32[2,256]{1,0:T(2,128)S(1)}) custom-call(f32[1024,256]{1,0:T(8,128)S(1)} %copy-done, f32[1024,128]{1,0:T(8,128)S(1)} %get-tuple-element.56.refs_1_, f32[1024,128]{1,0:T(8,128)S(1)} %turn_sum.1.refs_2_.refs_0_.refs_1_, bf16[1024,128]{1,0:T(8,128)(2,1)S(1)} %strip_columns.3.refs_2_.refs_3_, ...), custom_call_target="tpu_custom_call" | custom-call | flops 1024 | bytes 1024 | tf_op jit(solution)/shard_map/second_rest/pallas_call | solution.py:39
  90.1 0.6 collective-permute-start.26
  90.6 0.8 collective-permute-done.26.refs_1_
  91.4 0.3 collective-permute-start.38
  91.8 3.3 %collective-permute-start.37 = (f32[1024,128]{1,0:T(8,128)S(1)}, f32[1024,128]{1,0:T(8,128)S(1)}, u32[]{:S(2)}, u32[]{:S(2)}) collective-permute-start(f32[1024,128]{1,0:T(8,128)S(1)} %pick.9.refs_2_.refs_1_), channel_id=1, source_target_pairs={{0,1},{1,0},{2,3},{3,2},{4,5},{5,4},{6,7},{7,6},{8,9},{9,8},{10,11... | collective-permute-start | bytes 1572872 | tf_op jit(solution)/shard_map/ppermute | solution.py:474
  95.2 4.0 %collective-permute-start.33 = (f32[1024,128]{1,0:T(8,128)S(1)}, f32[1024,128]{1,0:T(8,128)S(1)}, u32[]{:S(2)}, u32[]{:S(2)}) collective-permute-start(f32[1024,128]{1,0:T(8,128)S(1)} %payload.20.refs_2_), channel_id=1, source_target_pairs={{0,2},{3,5},{4,6},{2,0},{5,3},{6,4},{8,10},{11,13},{12,14},{10,8},... | collective-permute-start | bytes 1572872 | tf_op jit(solution)/shard_map/ppermute | solution.py:477
  99.2 1.9 %collective-permute-start.28 = (f32[1024,128]{1,0:T(8,128)S(1)}, f32[1024,128]{1,0:T(8,128)S(1)}, u32[]{:S(2)}, u32[]{:S(2)}) collective-permute-start(f32[1024,128]{1,0:T(8,128)S(1)} %payload.21.refs_2_), channel_id=1, source_target_pairs={{1,3},{2,4},{5,7},{3,1},{4,2},{7,5},{9,11},{10,12},{13,15},{11,9},... | collective-permute-start | bytes 1572872 | tf_op jit(solution)/shard_map/ppermute | solution.py:477
  101.7 0.3 collective-permute-start.36
  102.3 1.0 collective-permute-done.36.refs_3_
  103.3 2.5 %collective-permute-start.31 = (f32[2,256]{1,0:T(2,128)S(1)}, f32[2,256]{1,0:T(2,128)S(1)}, u32[]{:S(2)}, u32[]{:S(2)}) collective-permute-start(f32[2,256]{1,0:T(2,128)S(1)} %get-tuple-element.70.refs_0_), channel_id=1, source_target_pairs={{0,4},{1,5},{2,6},{3,7},{4,0},{5,1},{6,2},{7,3},{8,12},{9,13},{10,... | collective-permute-start | bytes 6152 | tf_op jit(solution)/shard_map/ppermute | solution.py:674
  105.9 1.3 %two_blocks.12.refs_3_ = f32[256,1024]{1,0:T(8,128)S(1)} custom-call(bf16[8192,1024]{1,0:T(8,128)(2,1)S(1)} %get-tuple-element.43.refs_2_.refs_0_, f32[1024,128]{1,0:T(8,128)S(1)} %pick.10.refs_1_, f32[512,128]{1,0:T(8,128)S(1)} %collective-permute-done.35.refs_2_, f32[512,128]{1,0:T(8,128)S(1)} %collective-permute-done.36.refs_3_, ...), custom_call_target="tpu_custom_call" | custom-call | flops 1024 | bytes 1024 | tf_op jit(solution)/shard_map/two_blocks/pallas_call | solution.py:39
  107.2 2.2 %collective-permute-done.33.refs_0_.refs_1_ = f32[1024,128]{1,0:T(8,128)S(1)} collective-permute-done((f32[1024,128]{1,0:T(8,128)S(1)}, f32[1024,128]{1,0:T(8,128)S(1)}, u32[]{:S(2)}, u32[]{:S(2)}) %collective-permute-start.33) | collective-permute-done | bytes 524320 | tf_op jit(solution)/shard_map/ppermute | solution.py:477
  109.4 1.9 %collective-permute-start.40 = (f32[1024,128]{1,0:T(8,128)S(1)}, f32[1024,128]{1,0:T(8,128)S(1)}, u32[]{:S(2)}, u32[]{:S(2)}) collective-permute-start(f32[1024,128]{1,0:T(8,128)S(1)} %payload.22.refs_4_), channel_id=1, source_target_pairs={{1,3},{2,4},{5,7},{3,1},{4,2},{7,5},{9,11},{10,12},{13,15},{11,9},... | collective-permute-start | bytes 1572872 | tf_op jit(solution)/shard_map/ppermute | solution.py:477
  111.4 1.7 %collective-permute-done.31.refs_2_ = f32[2,256]{1,0:T(2,128)S(1)} collective-permute-done((f32[2,256]{1,0:T(2,128)S(1)}, f32[2,256]{1,0:T(2,128)S(1)}, u32[]{:S(2)}, u32[]{:S(2)}) %collective-permute-start.31) | collective-permute-done | bytes 2080 | tf_op jit(solution)/shard_map/ppermute | solution.py:674
  113.1 2.2 %collective-permute-start.39 = (f32[1024,128]{1,0:T(8,128)S(1)}, f32[1024,128]{1,0:T(8,128)S(1)}, u32[]{:S(2)}, u32[]{:S(2)}) collective-permute-start(f32[1024,128]{1,0:T(8,128)S(1)} %payload.23.refs_4_), channel_id=1, source_target_pairs={{0,2},{3,5},{4,6},{2,0},{5,3},{6,4},{8,10},{11,13},{12,14},{10,8},... | collective-permute-start | bytes 1572872 | tf_op jit(solution)/shard_map/ppermute | solution.py:477
  115.5 1.3 %collective-permute-start.42 = (f32[512,128]{1,0:T(8,128)S(1)}, f32[512,128]{1,0:T(8,128)S(1)}, u32[]{:S(2)}, u32[]{:S(2)}) collective-permute-start(f32[512,128]{1,0:T(8,128)S(1)} %get-tuple-element.78), channel_id=1, source_target_pairs={{0,1},{1,0},{2,3},{3,2},{4,5},{5,4},{6,7},{7,6},{8,9},{9,8},{10,11... | collective-permute-start | bytes 786440 | tf_op jit(solution)/shard_map/ppermute | solution.py:474
  116.8 1.3 %two_blocks.13.refs_3_.refs_4_ = f32[256,1024]{1,0:T(8,128)S(1)} custom-call(bf16[8192,1024]{1,0:T(8,128)(2,1)S(1)} %get-tuple-element.43.refs_2_.refs_0_, f32[1024,128]{1,0:T(8,128)S(1)} %turn_sum.1.refs_2_.refs_0_.refs_1_, f32[1024,128]{1,0:T(8,128)S(1)} %pass_on.2.refs_1_.refs_2_, f32[256,1024]{1,0:T(8,128)S(1)} %two_blocks.12.refs_3_, ...), custom_call_target="tpu_custom_call" | custom-call | flops 1024 | bytes 1024 | tf_op jit(solution)/shard_map/two_blocks/pallas_call | solution.py:39
  118.1 1.3 %two_blocks.14.refs_4_.refs_6_ = f32[256,1024]{1,0:T(8,128)S(1)} custom-call(bf16[8192,1024]{1,0:T(8,128)(2,1)S(1)} %get-tuple-element.43.refs_2_.refs_0_, f32[1024,128]{1,0:T(8,128)S(1)} %pick.9.refs_2_.refs_1_, f32[1024,128]{1,0:T(8,128)S(1)} %pass_on.3.refs_4_.refs_2_, f32[256,1024]{1,0:T(8,128)S(1)} %two_blocks.13.refs_3_.refs_4_, ...), custom_call_target="tpu_custom_call" | custom-call | flops 1024 | bytes 1024 | tf_op jit(solution)/shard_map/two_blocks/pallas_call | solution.py:39
  119.5 1.4 %two_blocks.15.refs_3_.refs_2_ = f32[1024,128]{1,0:T(8,128)S(1)} custom-call(bf16[8192,1024]{1,0:T(8,128)(2,1)S(1)} %get-tuple-element.43.refs_2_.refs_0_, f32[1024,128]{1,0:T(8,128)S(1)} %pick.11.refs_4_.refs_1_, f32[512,128]{1,0:T(8,128)S(1)} %collective-permute-done.41.refs_2_, f32[512,128]{1,0:T(8,128)S(1)} %collective-permute-done.42.refs_3_, ...), custom_call_target="tpu_custom_call" | custom-call | flops 1024 | bytes 1024 | tf_op jit(solution)/shard_map/two_blocks/pallas_call | solution.py:39
  121.0 5.6 %collective-permute-done.39.refs_0_ = f32[1024,128]{1,0:T(8,128)S(1)} collective-permute-done((f32[1024,128]{1,0:T(8,128)S(1)}, f32[1024,128]{1,0:T(8,128)S(1)}, u32[]{:S(2)}, u32[]{:S(2)}) %collective-permute-start.39) | collective-permute-done | bytes 524320 | tf_op jit(solution)/shard_map/ppermute | solution.py:477
  126.6 1.0 last_sum.1
  (100 shorter events, 4.3 us)
Async XLA Ops:
  0.6 7.1 %copy-start = (f32[1024,256]{1,0:T(8,128)S(1)}, f32[1024,256]{1,0:T(8,128)}, u32[]{:S(2)}) copy-start(f32[1024,256]{1,0:T(8,128)} %refs_0_.9) | copy-start | bytes 3145732
  2.6 15.1 %collective-permute-start.2 = (f32[1040,128]{1,0:T(8,128)}, f32[1040,128]{1,0:T(8,128)S(1)}, u32[]{:S(2)}, u32[]{:S(2)}) collective-permute-start(f32[1040,128]{1,0:T(8,128)} %get-tuple-element.39.refs_1_), channel_id=1, source_target_pairs={{0,2},{3,5},{4,6},{2,0},{5,3},{6,4},{8,10},{11,13},{12,14},{10,8},... | collective-permute-start | bytes 1597448 | tf_op jit(solution)/shard_map/ppermute | solution.py:477
  5.8 13.9 %collective-permute-start = (f32[1040,128]{1,0:T(8,128)}, f32[1040,128]{1,0:T(8,128)S(1)}, u32[]{:S(2)}, u32[]{:S(2)}) collective-permute-start(f32[1040,128]{1,0:T(8,128)} %get-tuple-element.39.refs_1_), channel_id=1, source_target_pairs={{1,3},{2,4},{5,7},{3,1},{4,2},{7,5},{9,11},{10,12},{13,15},{11,9},... | collective-permute-start | bytes 1597448 | tf_op jit(solution)/shard_map/ppermute | solution.py:477
  7.8 0.7 copy-start.3
  8.5 9.3 %copy-start.2 = (f32[1040,128]{1,0:T(8,128)S(1)}, f32[1040,128]{1,0:T(8,128)}, u32[]{:S(2)}) copy-start(f32[1040,128]{1,0:T(8,128)} %get-tuple-element.39.refs_1_) | copy-start | bytes 1597444
  14.6 5.1 %collective-permute-start.1 = (f32[1024,128]{1,0:T(8,128)S(1)}, f32[1024,128]{1,0:T(8,128)S(1)}, u32[]{:S(2)}, u32[]{:S(2)}) collective-permute-start(f32[1024,128]{1,0:T(8,128)S(1)} %get-tuple-element.42), channel_id=1, source_target_pairs={{0,1},{1,0},{2,3},{3,2},{4,5},{5,4},{6,7},{7,6},{8,9},{9,8},{10,11... | collective-permute-start | bytes 1572872 | tf_op jit(solution)/shard_map/ppermute | solution.py:474
  17.2 9.5 %collective-permute-start.4 = (f32[1024,128]{1,0:T(8,128)S(1)}, f32[1024,128]{1,0:T(8,128)S(1)}, u32[]{:S(2)}, u32[]{:S(2)}) collective-permute-start(f32[1024,128]{1,0:T(8,128)S(1)} %get-tuple-element.45), channel_id=1, source_target_pairs={{0,1},{1,0},{2,3},{3,2},{4,5},{5,4},{6,7},{7,6},{8,9},{9,8},{10,11... | collective-permute-start | bytes 1572872 | tf_op jit(solution)/shard_map/ppermute | solution.py:474
  17.3 9.5 %collective-permute-start.5 = (f32[1024,128]{1,0:T(8,128)S(1)}, f32[1024,128]{1,0:T(8,128)S(1)}, u32[]{:S(2)}, u32[]{:S(2)}) collective-permute-start(f32[1024,128]{1,0:T(8,128)S(1)} %get-tuple-element.47), channel_id=1, source_target_pairs={{0,1},{1,0},{2,3},{3,2},{4,5},{5,4},{6,7},{7,6},{8,9},{9,8},{10,11... | collective-permute-start | bytes 1572872 | tf_op jit(solution)/shard_map/ppermute | solution.py:474
  17.7 12.9 %collective-permute-start.9 = (f32[1040,128]{1,0:T(8,128)S(1)}, f32[1040,128]{1,0:T(8,128)S(1)}, u32[]{:S(2)}, u32[]{:S(2)}) collective-permute-start(f32[1040,128]{1,0:T(8,128)S(1)} %copy-done.2), channel_id=1, source_target_pairs={{0,1},{1,0},{2,3},{3,2},{4,5},{5,4},{6,7},{7,6},{8,9},{9,8},{10,11... | collective-permute-start | bytes 1597448 | tf_op jit(solution)/shard_map/ppermute | solution.py:474
  19.9 12.2 %collective-permute-start.8 = (f32[1040,128]{1,0:T(8,128)S(1)}, f32[1040,128]{1,0:T(8,128)S(1)}, u32[]{:S(2)}, u32[]{:S(2)}) collective-permute-start(f32[1040,128]{1,0:T(8,128)S(1)} %payload.12.refs_2_), channel_id=1, source_target_pairs={{1,3},{2,4},{5,7},{3,1},{4,2},{7,5},{9,11},{10,12},{13,15},{11,9},... | collective-permute-start | bytes 1597448 | tf_op jit(solution)/shard_map/ppermute | solution.py:477
  22.0 15.5 %collective-permute-start.3 = (f32[1040,128]{1,0:T(8,128)S(1)}, f32[1040,128]{1,0:T(8,128)S(1)}, u32[]{:S(2)}, u32[]{:S(2)}) collective-permute-start(f32[1040,128]{1,0:T(8,128)S(1)} %payload.13.refs_2_), channel_id=1, source_target_pairs={{0,2},{3,5},{4,6},{2,0},{5,3},{6,4},{8,10},{11,13},{12,14},{10,8},... | collective-permute-start | bytes 1597448 | tf_op jit(solution)/shard_map/ppermute | solution.py:477
  27.3 10.1 %collective-permute-start.6 = (f32[32,1024]{1,0:T(8,128)S(1)}, f32[32,1024]{1,0:T(8,128)S(1)}, u32[]{:S(2)}, u32[]{:S(2)}) collective-permute-start(f32[32,1024]{1,0:T(8,128)S(1)} %get-tuple-element.50), channel_id=1, source_target_pairs={{0,8},{16,24},{8,0},{24,16},{1,9},{17,25},{9,1},{25,17},{2,10},{18... | collective-permute-start | bytes 393224 | tf_op jit(solution)/shard_map/ppermute | solution.py:388
  28.6 8.8 %collective-permute-start.7 = (f32[32,1024]{1,0:T(8,128)S(1)}, f32[32,1024]{1,0:T(8,128)S(1)}, u32[]{:S(2)}, u32[]{:S(2)}) collective-permute-start(f32[32,1024]{1,0:T(8,128)S(1)} %get-tuple-element.51.refs_3_), channel_id=1, source_target_pairs={{8,16},{16,8},{9,17},{17,9},{10,18},{18,10},{11,19},{19,11},{12,20... | collective-permute-start | bytes 393224 | tf_op jit(solution)/shard_map/ppermute | solution.py:388
  30.7 11.0 %collective-permute-start.12 = (f32[1040,128]{1,0:T(8,128)S(1)}, f32[1040,128]{1,0:T(8,128)S(1)}, u32[]{:S(2)}, u32[]{:S(2)}) collective-permute-start(f32[1040,128]{1,0:T(8,128)S(1)} %pick.6.refs_2_.refs_1_), channel_id=1, source_target_pairs={{0,1},{1,0},{2,3},{3,2},{4,5},{5,4},{6,7},{7,6},{8,9},{9,8},{10,11... | collective-permute-start | bytes 1597448 | tf_op jit(solution)/shard_map/ppermute | solution.py:474
  32.2 14.9 %collective-permute-start.11 = (f32[1040,128]{1,0:T(8,128)S(1)}, f32[1040,128]{1,0:T(8,128)S(1)}, u32[]{:S(2)}, u32[]{:S(2)}) collective-permute-start(f32[1040,128]{1,0:T(8,128)S(1)} %payload.14.refs_2_), channel_id=1, source_target_pairs={{0,2},{3,5},{4,6},{2,0},{5,3},{6,4},{8,10},{11,13},{12,14},{10,8},... | collective-permute-start | bytes 1597448 | tf_op jit(solution)/shard_map/ppermute | solution.py:477
  37.6 11.6 %collective-permute-start.10 = (f32[1040,128]{1,0:T(8,128)S(1)}, f32[1040,128]{1,0:T(8,128)S(1)}, u32[]{:S(2)}, u32[]{:S(2)}) collective-permute-start(f32[1040,128]{1,0:T(8,128)S(1)} %payload.15.refs_3_), channel_id=1, source_target_pairs={{1,3},{2,4},{5,7},{3,1},{4,2},{7,5},{9,11},{10,12},{13,15},{11,9},... | collective-permute-start | bytes 1597448 | tf_op jit(solution)/shard_map/ppermute | solution.py:477
  39.6 1.9 %copy-start.5 = (f32[2,1024]{1,0:T(2,128)S(1)}, f32[2,1024]{1,0:T(2,128)}, u32[]{:S(2)}) copy-start(f32[2,1024]{1,0:T(2,128)} %refs_1_.3) | copy-start | bytes 24580
  39.6 1.9 %copy-start.6 = (f32[1024]{0:T(1024)S(1)}, f32[1024]{0:T(1024)}, u32[]{:S(2)}) copy-start(f32[1024]{0:T(1024)} %param.9) | copy-start | bytes 12292
  40.9 12.3 %collective-permute-start.15 = (f32[1024,128]{1,0:T(8,128)S(1)}, f32[1024,128]{1,0:T(8,128)S(1)}, u32[]{:S(2)}, u32[]{:S(2)}) collective-permute-start(f32[1024,128]{1,0:T(8,128)S(1)} %get-tuple-element.52.refs_4_), channel_id=1, source_target_pairs={{0,1},{1,0},{2,3},{3,2},{4,5},{5,4},{6,7},{7,6},{8,9},{9,8},{10,11... | collective-permute-start | bytes 1572872 | tf_op jit(solution)/shard_map/ppermute | solution.py:474
  41.6 12.2 %collective-permute-start.18 = (f32[1040,128]{1,0:T(8,128)S(1)}, f32[1040,128]{1,0:T(8,128)S(1)}, u32[]{:S(2)}, u32[]{:S(2)}) collective-permute-start(f32[1040,128]{1,0:T(8,128)S(1)} %pick.7.refs_2_.refs_1_), channel_id=1, source_target_pairs={{0,1},{1,0},{2,3},{3,2},{4,5},{5,4},{6,7},{7,6},{8,9},{9,8},{10,11... | collective-permute-start | bytes 1597448 | tf_op jit(solution)/shard_map/ppermute | solution.py:474
  41.7 1.4 %copy-start.1 = (bf16[640,1024]{1,0:T(8,128)(2,1)S(1)}, bf16[640,1024]{1,0:T(8,128)(2,1)}, u32[]{:S(2)}) copy-start(bf16[640,1024]{1,0:T(8,128)(2,1)} %constant.4.clone.refs_2_.refs_4_) | copy-start | bytes 3932164
  41.7 1.4 %copy-start.4 = (s32[256]{0:T(256)S(1)}, s32[256]{0:T(256)}, u32[]{:S(2)}) copy-start(s32[256]{0:T(256)} %param.10) | copy-start | bytes 3076
  47.2 12.2 %collective-permute-start.14 = (f32[1024,128]{1,0:T(8,128)S(1)}, f32[1024,128]{1,0:T(8,128)S(1)}, u32[]{:S(2)}, u32[]{:S(2)}) collective-permute-start(f32[1024,128]{1,0:T(8,128)S(1)} %payload.16.refs_3_), channel_id=1, source_target_pairs={{1,3},{2,4},{5,7},{3,1},{4,2},{7,5},{9,11},{10,12},{13,15},{11,9},... | collective-permute-start | bytes 1572872 | tf_op jit(solution)/shard_map/ppermute | solution.py:477
  49.3 13.7 %collective-permute-start.13 = (f32[1024,128]{1,0:T(8,128)S(1)}, f32[1024,128]{1,0:T(8,128)S(1)}, u32[]{:S(2)}, u32[]{:S(2)}) collective-permute-start(f32[1024,128]{1,0:T(8,128)S(1)} %payload.17.refs_4_), channel_id=1, source_target_pairs={{0,2},{3,5},{4,6},{2,0},{5,3},{6,4},{8,10},{11,13},{12,14},{10,8},... | collective-permute-start | bytes 1572872 | tf_op jit(solution)/shard_map/ppermute | solution.py:477
  53.1 2.0 %collective-permute-start.17 = (f32[520,128]{1,0:T(8,128)S(1)}, f32[520,128]{1,0:T(8,128)S(1)}, u32[]{:S(2)}, u32[]{:S(2)}) collective-permute-start(f32[520,128]{1,0:T(8,128)S(1)} %get-tuple-element.76), channel_id=1, source_target_pairs={{0,1},{1,0},{2,3},{3,2},{4,5},{5,4},{6,7},{7,6},{8,9},{9,8},{10,11... | collective-permute-start | bytes 798728 | tf_op jit(solution)/shard_map/ppermute | solution.py:474
  53.2 2.0 %collective-permute-start.16 = (f32[520,128]{1,0:T(8,128)S(1)}, f32[520,128]{1,0:T(8,128)S(1)}, u32[]{:S(2)}, u32[]{:S(2)}) collective-permute-start(f32[520,128]{1,0:T(8,128)S(1)} %get-tuple-element.77), channel_id=1, source_target_pairs={{0,1},{1,0},{2,3},{3,2},{4,5},{5,4},{6,7},{7,6},{8,9},{9,8},{10,11... | collective-permute-start | bytes 798728 | tf_op jit(solution)/shard_map/ppermute | solution.py:474
  58.0 11.4 %collective-permute-start.20 = (f32[1024,128]{1,0:T(8,128)S(1)}, f32[1024,128]{1,0:T(8,128)S(1)}, u32[]{:S(2)}, u32[]{:S(2)}) collective-permute-start(f32[1024,128]{1,0:T(8,128)S(1)} %get-tuple-element.58.refs_2_), channel_id=1, source_target_pairs={{0,1},{1,0},{2,3},{3,2},{4,5},{5,4},{6,7},{7,6},{8,9},{9,8},{10,11... | collective-permute-start | bytes 1572872 | tf_op jit(solution)/shard_map/ppermute | solution.py:474
  63.1 12.7 %collective-permute-start.23 = (f32[1024,128]{1,0:T(8,128)S(1)}, f32[1024,128]{1,0:T(8,128)S(1)}, u32[]{:S(2)}, u32[]{:S(2)}) collective-permute-start(f32[1024,128]{1,0:T(8,128)S(1)} %turn_sum.1.refs_2_.refs_0_.refs_1_), channel_id=1, source_target_pairs={{0,2},{3,5},{4,6},{2,0},{5,3},{6,4},{8,10},{11,13},{12,14},{10,8},... | collective-permute-start | bytes 1572872 | tf_op jit(solution)/shard_map/ppermute | solution.py:477
  66.4 13.0 %collective-permute-start.19 = (f32[1024,128]{1,0:T(8,128)S(1)}, f32[1024,128]{1,0:T(8,128)S(1)}, u32[]{:S(2)}, u32[]{:S(2)}) collective-permute-start(f32[1024,128]{1,0:T(8,128)S(1)} %turn_sum.1.refs_2_.refs_0_.refs_1_), channel_id=1, source_target_pairs={{1,3},{2,4},{5,7},{3,1},{4,2},{7,5},{9,11},{10,12},{13,15},{11,9},... | collective-permute-start | bytes 1572872 | tf_op jit(solution)/shard_map/ppermute | solution.py:477
  68.4 14.5 %collective-permute-start.25 = (f32[1024,128]{1,0:T(8,128)S(1)}, f32[1024,128]{1,0:T(8,128)S(1)}, u32[]{:S(2)}, u32[]{:S(2)}) collective-permute-start(f32[1024,128]{1,0:T(8,128)S(1)} %get-tuple-element.59.refs_3_), channel_id=1, source_target_pairs={{0,1},{1,0},{2,3},{3,2},{4,5},{5,4},{6,7},{7,6},{8,9},{9,8},{10,11... | collective-permute-start | bytes 1572872 | tf_op jit(solution)/shard_map/ppermute | solution.py:474
  69.7 8.1 %collective-permute-start.21 = (f32[32,1024]{1,0:T(8,128)S(1)}, f32[32,1024]{1,0:T(8,128)S(1)}, u32[]{:S(2)}, u32[]{:S(2)}) collective-permute-start(f32[32,1024]{1,0:T(8,128)S(1)} %get-tuple-element.62), channel_id=1, source_target_pairs={{0,8},{16,24},{8,0},{24,16},{1,9},{17,25},{9,1},{25,17},{2,10},{18... | collective-permute-start | bytes 393224 | tf_op jit(solution)/shard_map/ppermute | solution.py:388
  70.9 7.6 %collective-permute-start.22 = (f32[32,1024]{1,0:T(8,128)S(1)}, f32[32,1024]{1,0:T(8,128)S(1)}, u32[]{:S(2)}, u32[]{:S(2)}) collective-permute-start(f32[32,1024]{1,0:T(8,128)S(1)} %get-tuple-element.63.refs_2_), channel_id=1, source_target_pairs={{8,16},{16,8},{9,17},{17,9},{10,18},{18,10},{11,19},{19,11},{12,20... | collective-permute-start | bytes 393224 | tf_op jit(solution)/shard_map/ppermute | solution.py:388
  75.8 16.0 %collective-permute-start.27 = (f32[1024,128]{1,0:T(8,128)S(1)}, f32[1024,128]{1,0:T(8,128)S(1)}, u32[]{:S(2)}, u32[]{:S(2)}) collective-permute-start(f32[1024,128]{1,0:T(8,128)S(1)} %payload.18.refs_2_), channel_id=1, source_target_pairs={{1,3},{2,4},{5,7},{3,1},{4,2},{7,5},{9,11},{10,12},{13,15},{11,9},... | collective-permute-start | bytes 1572872 | tf_op jit(solution)/shard_map/ppermute | solution.py:477
  79.5 15.6 %collective-permute-start.24 = (f32[1024,128]{1,0:T(8,128)S(1)}, f32[1024,128]{1,0:T(8,128)S(1)}, u32[]{:S(2)}, u32[]{:S(2)}) collective-permute-start(f32[1024,128]{1,0:T(8,128)S(1)} %payload.19.refs_2_), channel_id=1, source_target_pairs={{0,2},{3,5},{4,6},{2,0},{5,3},{6,4},{8,10},{11,13},{12,14},{10,8},... | collective-permute-start | bytes 1572872 | tf_op jit(solution)/shard_map/ppermute | solution.py:477
  84.2 15.0 %collective-permute-start.29 = (f32[1024,128]{1,0:T(8,128)S(1)}, f32[1024,128]{1,0:T(8,128)S(1)}, u32[]{:S(2)}, u32[]{:S(2)}) collective-permute-start(f32[1024,128]{1,0:T(8,128)S(1)} %get-tuple-element.65.refs_2_), channel_id=1, source_target_pairs={{0,1},{1,0},{2,3},{3,2},{4,5},{5,4},{6,7},{7,6},{8,9},{9,8},{10,11... | collective-permute-start | bytes 1572872 | tf_op jit(solution)/shard_map/ppermute | solution.py:474
  87.6 13.7 %collective-permute-start.34 = (f32[1024,128]{1,0:T(8,128)S(1)}, f32[1024,128]{1,0:T(8,128)S(1)}, u32[]{:S(2)}, u32[]{:S(2)}) collective-permute-start(f32[1024,128]{1,0:T(8,128)S(1)} %get-tuple-element.66.refs_8_), channel_id=1, source_target_pairs={{0,1},{1,0},{2,3},{3,2},{4,5},{5,4},{6,7},{7,6},{8,9},{9,8},{10,11... | collective-permute-start | bytes 1572872 | tf_op jit(solution)/shard_map/ppermute | solution.py:474
  90.1 1.4 %collective-permute-start.26 = (f32[2,256]{1,0:T(2,128)S(1)}, f32[2,256]{1,0:T(2,128)S(1)}, u32[]{:S(2)}, u32[]{:S(2)}) collective-permute-start(f32[2,256]{1,0:T(2,128)S(1)} %get-tuple-element.67.refs_3_.refs_0_), channel_id=1, source_target_pairs={{0,1},{1,0},{2,3},{3,2},{4,5},{5,4},{6,7},{7,6},{8,9},{9,8},{10,11... | collective-permute-start | bytes 6152 | tf_op jit(solution)/shard_map/ppermute | solution.py:674
  91.4 10.6 %collective-permute-start.38 = (f32[1024,128]{1,0:T(8,128)S(1)}, f32[1024,128]{1,0:T(8,128)S(1)}, u32[]{:S(2)}, u32[]{:S(2)}) collective-permute-start(f32[1024,128]{1,0:T(8,128)S(1)} %turn_sum.1.refs_2_.refs_0_.refs_1_), channel_id=1, source_target_pairs={{0,1},{1,0},{2,3},{3,2},{4,5},{5,4},{6,7},{7,6},{8,9},{9,8},{10,11... | collective-permute-start | bytes 1572872 | tf_op jit(solution)/shard_map/ppermute | solution.py:474
  91.8 10.5 %collective-permute-start.37 = (f32[1024,128]{1,0:T(8,128)S(1)}, f32[1024,128]{1,0:T(8,128)S(1)}, u32[]{:S(2)}, u32[]{:S(2)}) collective-permute-start(f32[1024,128]{1,0:T(8,128)S(1)} %pick.9.refs_2_.refs_1_), channel_id=1, source_target_pairs={{0,1},{1,0},{2,3},{3,2},{4,5},{5,4},{6,7},{7,6},{8,9},{9,8},{10,11... | collective-permute-start | bytes 1572872 | tf_op jit(solution)/shard_map/ppermute | solution.py:474
  95.2 14.2 %collective-permute-start.33 = (f32[1024,128]{1,0:T(8,128)S(1)}, f32[1024,128]{1,0:T(8,128)S(1)}, u32[]{:S(2)}, u32[]{:S(2)}) collective-permute-start(f32[1024,128]{1,0:T(8,128)S(1)} %payload.20.refs_2_), channel_id=1, source_target_pairs={{0,2},{3,5},{4,6},{2,0},{5,3},{6,4},{8,10},{11,13},{12,14},{10,8},... | collective-permute-start | bytes 1572872 | tf_op jit(solution)/shard_map/ppermute | solution.py:477
  99.2 13.8 %collective-permute-start.28 = (f32[1024,128]{1,0:T(8,128)S(1)}, f32[1024,128]{1,0:T(8,128)S(1)}, u32[]{:S(2)}, u32[]{:S(2)}) collective-permute-start(f32[1024,128]{1,0:T(8,128)S(1)} %payload.21.refs_2_), channel_id=1, source_target_pairs={{1,3},{2,4},{5,7},{3,1},{4,2},{7,5},{9,11},{10,12},{13,15},{11,9},... | collective-permute-start | bytes 1572872 | tf_op jit(solution)/shard_map/ppermute | solution.py:477
  101.7 1.6 %collective-permute-start.36 = (f32[512,128]{1,0:T(8,128)S(1)}, f32[512,128]{1,0:T(8,128)S(1)}, u32[]{:S(2)}, u32[]{:S(2)}) collective-permute-start(f32[512,128]{1,0:T(8,128)S(1)} %get-tuple-element.80), channel_id=1, source_target_pairs={{0,1},{1,0},{2,3},{3,2},{4,5},{5,4},{6,7},{7,6},{8,9},{9,8},{10,11... | collective-permute-start | bytes 786440 | tf_op jit(solution)/shard_map/ppermute | solution.py:474
  102.0 3.8 %collective-permute-start.35 = (f32[512,128]{1,0:T(8,128)S(1)}, f32[512,128]{1,0:T(8,128)S(1)}, u32[]{:S(2)}, u32[]{:S(2)}) collective-permute-start(f32[512,128]{1,0:T(8,128)S(1)} %get-tuple-element.81), channel_id=1, source_target_pairs={{0,1},{1,0},{2,3},{3,2},{4,5},{5,4},{6,7},{7,6},{8,9},{9,8},{10,11... | collective-permute-start | bytes 786440 | tf_op jit(solution)/shard_map/ppermute | solution.py:474
  102.2 9.1 %collective-permute-start.32 = (f32[2,256]{1,0:T(2,128)S(1)}, f32[2,256]{1,0:T(2,128)S(1)}, u32[]{:S(2)}, u32[]{:S(2)}) collective-permute-start(f32[2,256]{1,0:T(2,128)S(1)} %get-tuple-element.70.refs_0_), channel_id=1, source_target_pairs={{0,6},{1,7},{2,4},{3,5},{4,2},{5,3},{6,0},{7,1},{8,14},{9,15},{10,... | collective-permute-start | bytes 6152 | tf_op jit(solution)/shard_map/ppermute | solution.py:674
  103.3 9.8 %collective-permute-start.31 = (f32[2,256]{1,0:T(2,128)S(1)}, f32[2,256]{1,0:T(2,128)S(1)}, u32[]{:S(2)}, u32[]{:S(2)}) collective-permute-start(f32[2,256]{1,0:T(2,128)S(1)} %get-tuple-element.70.refs_0_), channel_id=1, source_target_pairs={{0,4},{1,5},{2,6},{3,7},{4,0},{5,1},{6,2},{7,3},{8,12},{9,13},{10,... | collective-permute-start | bytes 6152 | tf_op jit(solution)/shard_map/ppermute | solution.py:674
  105.8 7.2 %collective-permute-start.30 = (f32[2,256]{1,0:T(2,128)S(1)}, f32[2,256]{1,0:T(2,128)S(1)}, u32[]{:S(2)}, u32[]{:S(2)}) collective-permute-start(f32[2,256]{1,0:T(2,128)S(1)} %get-tuple-element.70.refs_0_), channel_id=1, source_target_pairs={{0,2},{1,3},{2,0},{3,1},{4,6},{5,7},{6,4},{7,5},{8,10},{9,11},{10,... | collective-permute-start | bytes 6152 | tf_op jit(solution)/shard_map/ppermute | solution.py:674
  109.4 11.5 %collective-permute-start.40 = (f32[1024,128]{1,0:T(8,128)S(1)}, f32[1024,128]{1,0:T(8,128)S(1)}, u32[]{:S(2)}, u32[]{:S(2)}) collective-permute-start(f32[1024,128]{1,0:T(8,128)S(1)} %payload.22.refs_4_), channel_id=1, source_target_pairs={{1,3},{2,4},{5,7},{3,1},{4,2},{7,5},{9,11},{10,12},{13,15},{11,9},... | collective-permute-start | bytes 1572872 | tf_op jit(solution)/shard_map/ppermute | solution.py:477
  113.1 13.4 %collective-permute-start.39 = (f32[1024,128]{1,0:T(8,128)S(1)}, f32[1024,128]{1,0:T(8,128)S(1)}, u32[]{:S(2)}, u32[]{:S(2)}) collective-permute-start(f32[1024,128]{1,0:T(8,128)S(1)} %payload.23.refs_4_), channel_id=1, source_target_pairs={{0,2},{3,5},{4,6},{2,0},{5,3},{6,4},{8,10},{11,13},{12,14},{10,8},... | collective-permute-start | bytes 1572872 | tf_op jit(solution)/shard_map/ppermute | solution.py:477
  115.5 4.0 %collective-permute-start.42 = (f32[512,128]{1,0:T(8,128)S(1)}, f32[512,128]{1,0:T(8,128)S(1)}, u32[]{:S(2)}, u32[]{:S(2)}) collective-permute-start(f32[512,128]{1,0:T(8,128)S(1)} %get-tuple-element.78), channel_id=1, source_target_pairs={{0,1},{1,0},{2,3},{3,2},{4,5},{5,4},{6,7},{7,6},{8,9},{9,8},{10,11... | collective-permute-start | bytes 786440 | tf_op jit(solution)/shard_map/ppermute | solution.py:474
  116.8 2.7 %collective-permute-start.41 = (f32[512,128]{1,0:T(8,128)S(1)}, f32[512,128]{1,0:T(8,128)S(1)}, u32[]{:S(2)}, u32[]{:S(2)}) collective-permute-start(f32[512,128]{1,0:T(8,128)S(1)} %get-tuple-element.79), channel_id=1, source_target_pairs={{0,1},{1,0},{2,3},{3,2},{4,5},{5,4},{6,7},{7,6},{8,9},{9,8},{10,11... | collective-permute-start | bytes 786440 | tf_op jit(solution)/shard_map/ppermute | solution.py:474
